TPU v7x, 32 devices: a whole 2x2x4 slice. The times are simulated.
32 devices in a mesh: groups: 2 (over x), slab: 16 (over z, y, core).
Axes of the slice: x: 2, y: 2, z: 4, core: 2. Of those that a mesh axis runs over, the one named last changes fastest.
Arguments:
- particles: bfloat16 [32, 1048576], P(('groups', 'slab')), parts along dimension 0, may hold values from -8 to 8
- observed: bfloat16 [2097152], P('groups'), parts along dimension 0, may hold values from -1 to 1
- precision: bfloat16 [2097152], P('groups'), parts along dimension 0, may hold values from 0.099609375 to 10
- spread: float32 [2], P('groups'), parts along dimension 0, may hold values from 1 to 4
- anneal: float32 [2], P('groups'), parts along dimension 0, may hold values from 0.06 to 0.6
- step_size: float32 [2], P('groups'), parts along dimension 0, may hold values from 2 to 8
Outputs:
- updated: bfloat16 [32, 1048576], P(('groups', 'slab')), parts along dimension 0
There are 2 independent parts, one for each index of `groups`. A program takes and returns all parts, laid end to end along the dimension named above; each array names one. Nothing has to cross between parts.
All inputs are finite; a program needn't handle non-finite values.
Results may differ from a plain program's by a relative error of at most 0.0014.
The roundings to bfloat16 on the way count: a program that leaves them out, or rounds other values in their place, can miss the bound.
Values may be sent and summed in bfloat16 or wider, within the bound.
No kernel may reach another device: no remote copies, remote signals or barrier semaphores. Data moves between devices by JAX's collectives and lax.ppermute only.
A program may use at most 128 MiB of HBM per device.

v0:
```python
import jax
import jax.numpy as jnp
from jax import lax
from jax.sharding import PartitionSpec as P

GRID_X = 1024
GRID_Y = 1024
NCELL = 1048576


prior_scale = 0.25
mass_term = 1.0


def with_halo(cells, sides, width):
    for axis, dim in sides:
        count = lax.axis_size(axis)
        ends = count - 1
        head = lax.slice_in_dim(cells, 0, width, axis=dim)
        tail = lax.slice_in_dim(cells, cells.shape[dim] - width, cells.shape[dim], axis=dim)
        cells = jnp.concatenate(
            [
                lax.ppermute(tail, axis, [(i, (i + 1) % count) for i in range(ends)]),
                cells,
                lax.ppermute(head, axis, [((i + 1) % count, i) for i in range(ends)]),
            ],
            axis=dim,
        )
    return cells


def gradient_block(padded, observed, precision):
    field = padded[:, 1:-1, 1:-1]
    beside_all = (
        padded[:, 2:, 1:-1] + padded[:, :-2, 1:-1] + padded[:, 1:-1, 2:] + padded[:, 1:-1, :-2]
    )
    laplace = (4.0 + mass_term) * field - beside_all
    squash = jnp.tanh(field)
    obs = observed.astype(jnp.float32).reshape(1, field.shape[1], field.shape[2])
    prec = precision.astype(jnp.float32).reshape(1, field.shape[1], field.shape[2])
    result = prec * (obs - squash) * (1.0 - squash * squash) - prior_scale * laplace
    return result.reshape(field.shape[0], -1).astype(jnp.bfloat16)


def on_device(particles, observed, precision, spread, anneal, step_size):
    slab_count = lax.axis_size("slab")
    owned = particles.shape[0]
    total = owned * slab_count
    states = lax.all_to_all(particles, "slab", split_axis=1, concat_axis=0, tiled=True)
    slab_rows = GRID_X // slab_count
    grid = states.reshape(total, slab_rows, GRID_Y)
    rimmed = with_halo(grid, (("slab", 1),), 1)
    padded = jnp.pad(rimmed.astype(jnp.float32), ((0, 0), (0, 0), (1, 1)))
    start = lax.axis_index("slab") * (slab_rows * GRID_Y)
    obs_rows = lax.dynamic_slice_in_dim(observed, start, slab_rows * GRID_Y)
    prec_rows = lax.dynamic_slice_in_dim(precision, start, slab_rows * GRID_Y)
    slab_grads = gradient_block(padded, obs_rows, prec_rows)
    local_gram = lax.dot_general(
        states, states, (((1,), (1,)), ((), ())), preferred_element_type=jnp.float32
    )
    scale = 1.0 / (spread[0] * NCELL)
    gram = lax.psum(local_gram, "slab")
    norms = jnp.diagonal(gram)
    kernel = jnp.exp(-(norms[:, None] + norms[None, :] - 2.0 * gram) * scale).astype(jnp.bfloat16)
    ksum = jnp.sum(kernel.astype(jnp.float32), axis=1)
    drive = jnp.dot(kernel, slab_grads, preferred_element_type=jnp.float32)
    pulled = jnp.dot(kernel, states, preferred_element_type=jnp.float32)
    values = states.astype(jnp.float32)
    repel = values * ksum[:, None] - pulled
    coeff = 2.0 * anneal[0] / spread[0]
    new_slab = (values + step_size[0] / total * (drive + coeff * repel)).astype(jnp.bfloat16)
    return lax.all_to_all(new_slab, "slab", split_axis=0, concat_axis=1, tiled=True)


def solution(mesh):
    in_specs = (
        P(("groups", "slab"), None),
        P("groups"),
        P("groups"),
        P("groups"),
        P("groups"),
        P("groups"),
    )
    out_specs = P(("groups", "slab"), None)
    return jax.shard_map(
        on_device, mesh=mesh, in_specs=in_specs, out_specs=out_specs, check_vma=False
    )
```

profile of v0, /device:TPU:9, one launch (start us, length us, event | category | flops | bytes accessed | tf_op | source)
XLA Modules:
  0.0 212.1 jit_solution(12481730594869660662)
XLA Ops:
  0.0 0.6 broadcast.27
  0.6 13.1 %reduce.2 = bf16[16,65536]{1,0:T(8,128)(2,1)S(1)} reduce(bf16[16,1,65536]{2,1,0:T(2,128)(2,1)} %bitcast.31, bf16[]{:T(256)} %broadcast.27), dimensions={1}, to_apply=%bitcast.18.reduce_sub_computation | reduce | bytes 4194306
  13.7 2.7 %reshape.45 = bf16[16,2,32768]{2,1,0:T(2,128)(2,1)} reshape(bf16[16,65536]{1,0:T(8,128)(2,1)S(1)} %reduce.2) | data formatting | bytes 4194304
  16.4 6.6 %all-to-all-start = ((bf16[16,2,32768]{2,1,0:T(2,128)(2,1)}), bf16[16,2,32768]{2,1,0:T(2,128)(2,1)S(1)}, u32[]{:S(2)}, u32[]{:S(2)}) async-start(bf16[16,2,32768]{2,1,0:T(2,128)(2,1)} %reshape.45), calls=%async_computation | async-start | bytes 4194304 | tf_op jit(solution)/shard_map/all_to_all | solution.py:49
  23.0 1.0 dynamic-slice_convert_fusion
  26.2 42.8 %all-to-all-done = bf16[16,2,32768]{2,1,0:T(2,128)(2,1)S(1)} async-done(((bf16[16,2,32768]{2,1,0:T(2,128)(2,1)}), bf16[16,2,32768]{2,1,0:T(2,128)(2,1)S(1)}, u32[]{:S(2)}, u32[]{:S(2)}) %all-to-all-start) | async-done | bytes 2097184 | tf_op jit(solution)/shard_map/all_to_all | solution.py:49
  69.0 6.7 %reshape.46 = bf16[16,1,65536]{2,1,0:T(2,128)(2,1)} reshape(bf16[16,2,32768]{2,1,0:T(2,128)(2,1)S(1)} %all-to-all-done) | data formatting | bytes 4194304
  75.7 0.0 copy-start
  75.7 13.3 %bitcast_reduce_fusion = bf16[16,65536]{1,0:T(8,128)(2,1)S(1)} fusion(bf16[16,1,65536]{2,1,0:T(2,128)(2,1)} %reshape.46), kind=kLoop, calls=%fused_computation.30 | loop fusion | bytes 4194304 | tf_op jit(solution)/shard_map/all_to_all | solution.py:49
  89.0 1.2 copy.10
  90.2 0.1 fusion.17
  90.3 4.6 %collective-permute-start = (bf16[16,1,1024]{2,1,0:T(2,128)(2,1)S(1)}, bf16[16,1,1024]{2,1,0:T(2,128)(2,1)S(1)}, u32[]{:S(2)}, u32[]{:S(2)}) collective-permute-start(bf16[16,1,1024]{2,1,0:T(2,128)(2,1)S(1)} %get-tuple-element.7), channel_id=1, source_target_pairs={{0,1},{1,2},{2,3},{3,4},{4,5},{5,6},{6,7},{7,8},{8,9},{9,10},{10,1... | collective-permute-start | bytes 98312 | tf_op jit(solution)/shard_map/ppermute | solution.py:23
  95.0 1.9 collective-permute-start.1
  96.9 0.0 copy-done
  96.9 2.3 %fusion.12 = f32[16,16]{1,0:T(8,128)S(1)} fusion(bf16[1,16,65536]{2,0,1:T(2,128)(2,1)S(1)} %bitcast.24), kind=kOutput, calls=%fused_computation.19 | convolution fusion | flops 33554432 | bytes 2098176 | tf_op jit(solution)/shard_map/dot_general | solution.py:58
  99.2 22.5 %psum.7 = f32[16,16]{1,0:T(8,128)S(1)} all-reduce(f32[16,16]{1,0:T(8,128)S(1)} %fusion.12), channel_id=1, replica_groups=mesh['groups'=2,'slab'=16] {'slab'}, use_global_device_ids=true, to_apply=%region_0.1 | all-reduce | flops 256 | bytes 2048 | tf_op jit(solution)/shard_map/psum | solution.py:62
  121.7 0.7 gather_fusion
  122.3 0.2 convert_reduce_fusion
  122.5 0.0 collective-permute-done
  122.5 0.0 collective-permute-done.1
  122.5 0.8 maximum_convert_fusion
  123.3 4.2 %fusion.11 = bf16[16,64,1024]{2,1,0:T(8,128)(2,1)S(1)} fusion(f32[16,66,1024]{2,1,0:T(8,128)S(1)} %maximum_convert_fusion, f32[64,1024]{1,0:T(8,128)S(1)} %reshape.37, f32[64,1024]{1,0:T(8,128)S(1)} %reshape.36), kind=kLoop, calls=%fused_computation.16 | loop fusion | flops 13631488 | bytes 19922944 | tf_op jit(solution)/shard_map/convert_element_type | solution.py:42
  127.5 1.2 copy.11
  128.7 0.0 copy-start.1
  128.7 0.7 fusion.18
  129.4 1.5 copy-done.1
  130.9 6.0 %fusion.5 = bf16[16,1,65536]{2,0,1:T(8,128)(2,1)} fusion(f32[16,65536]{1,0:T(8,128)S(1)} %fusion.18, bf16[16,16]{1,0:T(8,128)(2,1)S(1)} %get-tuple-element.6, f32[16]{0:T(128)S(1)} %get-tuple-element.5, f32[]{:T(128)} %bitcast.4, f32[]{:T(128)} %bitcast.1, bf16[1,16,65536]{2,0,1:T(2,128)(2,1)S(1)} %bitcast.25), kind=kOutput, calls=%fused_computation.7 | convolution fusion | flops 41943040 | bytes 8389192 | tf_op jit(solution)/shard_map/dot_general | solution.py:67
  136.9 3.9 %reduce.3 = bf16[16,65536]{1,0:T(8,128)(2,1)S(1)} reduce(bf16[16,1,65536]{2,0,1:T(8,128)(2,1)} %fusion.5, bf16[]{:T(256)} %broadcast.27), dimensions={1}, to_apply=%copy.8.reduce_sub_computation | reduce | bytes 4194306 | tf_op jit(solution)/shard_map/all_to_all | solution.py:72
  140.8 2.7 %reshape.47 = bf16[16,2,32768]{2,1,0:T(2,128)(2,1)} reshape(bf16[16,65536]{1,0:T(8,128)(2,1)S(1)} %reduce.3) | data formatting | bytes 4194304
  143.6 61.8 %all_to_all.32 = bf16[16,2,32768]{2,1,0:T(2,128)(2,1)S(1)} all-to-all(bf16[16,2,32768]{2,1,0:T(2,128)(2,1)} %reshape.47), channel_id=1, replica_groups=mesh['groups'=2,'slab'=16] {'slab'}, dimensions={0} | all-to-all | bytes 4194304 | tf_op jit(solution)/shard_map/all_to_all | solution.py:72
  205.4 6.7 %reshape.48 = bf16[16,1,65536]{2,1,0:T(2,128)(2,1)} reshape(bf16[16,2,32768]{2,1,0:T(2,128)(2,1)S(1)} %all_to_all.32) | data formatting | bytes 4194304
  (3 shorter events, 0.1 us)
Async XLA Ops:
  16.4 52.6 %all-to-all-start = ((bf16[16,2,32768]{2,1,0:T(2,128)(2,1)}), bf16[16,2,32768]{2,1,0:T(2,128)(2,1)S(1)}, u32[]{:S(2)}, u32[]{:S(2)}) async-start(bf16[16,2,32768]{2,1,0:T(2,128)(2,1)} %reshape.45), calls=%async_computation | async-start | bytes 4194304 | tf_op jit(solution)/shard_map/all_to_all | solution.py:49
  75.7 21.2 %copy-start = (bf16[16,1,65536]{2,1,0:T(2,128)(2,1)S(1)}, bf16[16,1,65536]{2,1,0:T(2,128)(2,1)}, u32[]{:S(2)}) copy-start(bf16[16,1,65536]{2,1,0:T(2,128)(2,1)} %reshape.46) | copy-start | bytes 6291460
  90.3 32.2 %collective-permute-start = (bf16[16,1,1024]{2,1,0:T(2,128)(2,1)S(1)}, bf16[16,1,1024]{2,1,0:T(2,128)(2,1)S(1)}, u32[]{:S(2)}, u32[]{:S(2)}) collective-permute-start(bf16[16,1,1024]{2,1,0:T(2,128)(2,1)S(1)} %get-tuple-element.7), channel_id=1, source_target_pairs={{0,1},{1,2},{2,3},{3,4},{4,5},{5,6},{6,7},{7,8},{8,9},{9,10},{10,1... | collective-permute-start | bytes 98312 | tf_op jit(solution)/shard_map/ppermute | solution.py:23
  95.0 27.6 %collective-permute-start.1 = (bf16[16,1,1024]{2,1,0:T(2,128)(2,1)S(1)}, bf16[16,1,1024]{2,1,0:T(2,128)(2,1)S(1)}, u32[]{:S(2)}, u32[]{:S(2)}) collective-permute-start(bf16[16,1,1024]{2,1,0:T(2,128)(2,1)S(1)} %get-tuple-element.8), channel_id=1, source_target_pairs={{1,0},{2,1},{3,2},{4,3},{5,4},{6,5},{7,6},{8,7},{9,8},{10,9},{11,1... | collective-permute-start | bytes 98312 | tf_op jit(solution)/shard_map/ppermute | solution.py:25
  128.7 2.2 %copy-start.1 = (bf16[16,1,65536]{2,1,0:T(2,128)(2,1)S(1)}, bf16[16,1,65536]{2,1,0:T(2,128)(2,1)}, u32[]{:S(2)}) copy-start(bf16[16,1,65536]{2,1,0:T(2,128)(2,1)} %reshape.46) | copy-start | bytes 6291460
where the time goes:
time: 213 us; the launch traced here: 212 us
  blocking collectives  84.3 us (40%)
  waiting for transfers between devices  42.8 us (20%)
  local copies, waits for them, and re-layouts  37.5 us (18%)
  other arithmetic  23.2 us (11%)
  starting transfers between devices  13.2 us (6%)
  matrix products  8.95 us (4%)
  between operations  2.17 us (1%)
    all_to_all x1, blocking collectives, on_device(): lax.all_to_all(new_slab, 'slab', split_axis=0, concat_axis=1, tiled=True)  61.8 us
    all_to_all x1, waiting for transfers between devices, on_device(): lax.all_to_all(particles, 'slab', split_axis=1, concat_axis=0, tiled=True)  42.8 us
    unnamed x11, local copies, waits for them, and re-layouts  23.3 us
    psum x1, blocking collectives, on_device(): gram = lax.psum(local_gram, 'slab')  22.5 us
    all_to_all x1, local copies, waits for them, and re-layouts, on_device(): lax.all_to_all(particles, 'slab', split_axis=1, concat_axis=0, tiled=True)  13.3 us
    unnamed x1, other arithmetic  13.1 us
    all_to_all x1, starting transfers between devices, on_device(): lax.all_to_all(particles, 'slab', split_axis=1, concat_axis=0, tiled=True)  6.61 us
    dot_general x1, matrix products, on_device(): pulled = jnp.dot(kernel, states, preferred_element_type=jnp.float32)  5.99 us
  transfers between devices with their start and end apart: 3, of which 1 were waited for; matrix products, arithmetic and copies ran while one was open for 2% of the time, Pallas kernels for 0%

commit v1 on v0

v1 whole, which is shorter than its diff:
```python
import functools

import jax
import jax.numpy as jnp
from jax import lax
from jax.experimental import pallas as pl
from jax.experimental.pallas import tpu as pltpu
from jax.sharding import PartitionSpec as P

GRID_X = 1024
GRID_Y = 1024
NCELL = 1048576
LANES = 128
LINE = GRID_Y // LANES
TILE = 16

prior_scale = 0.25
mass_term = 1.0

F32 = jnp.float32
BF16 = jnp.bfloat16
VMEM_LIMIT = 32 * 1024 * 1024


def call(body, name, flops=0, moved=0, **kwargs):
    return pl.pallas_call(
        body,
        name=name,
        compiler_params=pltpu.CompilerParams(vmem_limit_bytes=VMEM_LIMIT),
        cost_estimate=pl.CostEstimate(flops=flops, bytes_accessed=moved, transcendentals=0),
        **kwargs,
    )


def split_body(row_ref, above_ref, below_ref, out_ref):
    slab = pl.program_id(0)
    lines = out_ref.shape[1] - TILE
    out_ref[0, :lines, :] = row_ref[...].reshape(lines, LANES)
    below = below_ref[...].astype(F32).reshape(LINE, LANES)
    above = above_ref[...].astype(F32).reshape(LINE, LANES)
    below = jnp.where(slab == pl.num_programs(0) - 1, 0.0, below)
    above = jnp.where(slab == 0, 0.0, above)
    out_ref[0, lines:, :] = jnp.concatenate([below, above], axis=0).astype(BF16)


def split_row(row, slabs):
    cells = row.shape[1] // slabs
    rows = cells // GRID_Y
    lines = cells // LANES
    last = GRID_X - 1
    return call(
        split_body,
        "split_row",
        moved=6 * row.shape[1],
        grid=(slabs,),
        in_specs=[
            pl.BlockSpec((1, cells), lambda i: (0, i)),
            pl.BlockSpec((1, GRID_Y), lambda i: (0, jnp.maximum(i * rows - 1, 0))),
            pl.BlockSpec((1, GRID_Y), lambda i: (0, jnp.minimum(i * rows + rows, last))),
        ],
        out_specs=pl.BlockSpec((1, lines + TILE, LANES), lambda i: (i, 0, 0)),
        out_shape=jax.ShapeDtypeStruct((slabs, lines + TILE, LANES), BF16),
    )(row, row, row)


def join_body(slab_ref, row_ref):
    row_ref[...] = slab_ref[...].reshape(row_ref.shape)


def join_row(slabs):
    count, lines, _ = slabs.shape
    cells = lines * LANES
    return call(
        join_body,
        "join_row",
        moved=6 * count * cells,
        grid=(count,),
        in_specs=[pl.BlockSpec((1, lines, LANES), lambda i: (i, 0, 0))],
        out_specs=pl.BlockSpec((1, cells), lambda i: (0, i)),
        out_shape=jax.ShapeDtypeStruct((1, count * cells), BF16),
    )(slabs)


def same_line(total):
    wide = total * TILE
    row = lax.broadcasted_iota(jnp.int32, (wide, wide), 0)
    col = lax.broadcasted_iota(jnp.int32, (wide, wide), 1)
    return row % TILE == col % TILE


def members(total, dtype):
    wide = total * TILE
    row = lax.broadcasted_iota(jnp.int32, (wide, total), 0)
    col = lax.broadcasted_iota(jnp.int32, (wide, total), 1)
    return (row // TILE == col).astype(dtype)


def gram_body(states_ref, out_ref, pairs):
    total = states_ref.shape[0]
    wide = total * TILE
    tiles = 4
    steps = (states_ref.shape[1] - TILE) // (tiles * TILE)
    pairs[...] = jnp.zeros_like(pairs)

    def step(i, carry):
        parts = [
            states_ref[:, pl.ds(pl.multiple_of((i * tiles + t) * TILE, TILE), TILE), :].reshape(wide, LANES)
            for t in range(tiles)
        ]
        block = jnp.concatenate(parts, axis=1)
        pairs[...] += lax.dot_general(block, block, (((1,), (1,)), ((), ())), preferred_element_type=F32)
        return carry

    lax.fori_loop(0, steps, step, 0)
    equal = jnp.where(same_line(total), pairs[...], 0.0)
    rows = jnp.sum(equal.reshape(total, TILE, wide), axis=1)
    gram = jnp.dot(rows, members(total, F32), precision=lax.Precision.HIGHEST, preferred_element_type=F32)
    gram = jnp.concatenate([gram, jnp.zeros((total, LANES - total), F32)], axis=1)
    out_ref[...] = jnp.broadcast_to(gram[None], out_ref.shape)


def slab_gram(states, copies):
    total, lines, _ = states.shape
    wide = total * TILE
    return call(
        gram_body,
        "slab_gram",
        flops=2 * wide * wide * LANES * (lines // TILE),
        moved=2 * states.size,
        in_specs=[pl.BlockSpec(memory_space=pltpu.VMEM)],
        out_specs=pl.BlockSpec(memory_space=pltpu.VMEM),
        out_shape=jax.ShapeDtypeStruct((copies, total, LANES), F32),
        scratch_shapes=[pltpu.VMEM((wide, wide), F32)],
    )(states)


def gradient_body(states_ref, observed_ref, precision_ref, out_ref):
    total = states_ref.shape[0]
    tiles = (states_ref.shape[1] - TILE) // TILE
    lane = lax.broadcasted_iota(jnp.int32, (2, LINE, LANES), 2)
    line = lax.broadcasted_iota(jnp.int32, (2, LINE, LANES), 1)
    group = 4

    def load(particle, tile):
        start = pl.multiple_of(tile * TILE, TILE)
        return states_ref[particle, pl.ds(start, TILE), :].astype(F32)

    def step(i, carry):
        tile = i // (total // group)
        first = (i % (total // group)) * group
        start = pl.multiple_of(tile * TILE, TILE)
        obs = observed_ref[pl.ds(start, TILE), :].astype(F32).reshape(2, LINE, LANES)
        prec = precision_ref[pl.ds(start, TILE), :].astype(F32).reshape(2, LINE, LANES)
        for p in range(group):
            particle = first + p
            here = load(particle, tile)
            before = load(particle, jnp.where(tile == 0, tiles, tile - 1))
            after = load(particle, tile + 1)
            above = jnp.concatenate([before[LINE:], here[:LINE]], axis=0).reshape(2, LINE, LANES)
            below = jnp.concatenate([here[LINE:], after[:LINE]], axis=0).reshape(2, LINE, LANES)
            field = here.reshape(2, LINE, LANES)
            turned = pltpu.roll(field, 1, 2)
            carried = jnp.where(line == 0, 0.0, pltpu.roll(turned, 1, 1))
            left = jnp.where(lane == 0, carried, turned)
            turned = pltpu.roll(field, LANES - 1, 2)
            carried = jnp.where(line == LINE - 1, 0.0, pltpu.roll(turned, LINE - 1, 1))
            right = jnp.where(lane == LANES - 1, carried, turned)
            laplace = (4.0 + mass_term) * field - (below + above + right + left)
            squash = jnp.tanh(field)
            result = prec * (obs - squash) * (1.0 - squash * squash) - prior_scale * laplace
            out_ref[particle, pl.ds(start, TILE), :] = result.reshape(TILE, LANES).astype(BF16)
        return carry

    lax.fori_loop(0, tiles * (total // group), step, 0)


def slab_gradient(states, observed, precision):
    total, lines, _ = states.shape
    return call(
        gradient_body,
        "slab_gradient",
        flops=30 * states.size,
        moved=4 * states.size,
        in_specs=[pl.BlockSpec(memory_space=pltpu.VMEM)] * 3,
        out_specs=pl.BlockSpec(memory_space=pltpu.VMEM),
        out_shape=jax.ShapeDtypeStruct((total, lines - TILE, LANES), BF16),
    )(states, observed, precision)


def update_body(spread_ref, anneal_ref, step_ref, grams_ref, states_ref, grads_ref, out_ref, mixer, own):
    total = states_ref.shape[0]
    wide = total * TILE
    rate = step_ref[0] / total
    coeff = 2.0 * anneal_ref[0] / spread_ref[0]

    @pl.when(pl.program_id(0) == 0)
    def _():
        gram = jnp.sum(grams_ref[...], axis=0)[:, :total]
        row = lax.broadcasted_iota(jnp.int32, (total, total), 0)
        col = lax.broadcasted_iota(jnp.int32, (total, total), 1)
        diagonal = jnp.where(row == col, gram, 0.0)
        down = jnp.sum(diagonal, axis=1, keepdims=True)
        across = jnp.sum(diagonal, axis=0, keepdims=True)
        kernel = jnp.exp(-(down + across - 2.0 * gram) / (spread_ref[0] * NCELL)).astype(BF16)
        ksum = jnp.sum(kernel.astype(F32), axis=1, keepdims=True)
        member = members(total, BF16)
        half = jnp.dot(member, kernel, preferred_element_type=F32).astype(BF16)
        full = lax.dot_general(half, member, (((1,), (1,)), ((), ())), preferred_element_type=F32)
        mixer[...] = jnp.where(same_line(total), full, 0.0).astype(BF16)
        gain = 1.0 + rate * coeff * ksum
        own[...] = jnp.broadcast_to(gain[:, :, None], (total, TILE, LANES)).reshape(wide, LANES)

    for t in range(states_ref.shape[1] // TILE):
        lines = slice(t * TILE, (t + 1) * TILE)
        states = states_ref[:, lines, :].reshape(wide, LANES)
        grads = grads_ref[:, lines, :].reshape(wide, LANES)
        mixed = jnp.dot(mixer[...], jnp.concatenate([grads, states], axis=1), preferred_element_type=F32)
        drive, pulled = mixed[:, :LANES], mixed[:, LANES:]
        new = states.astype(F32) * own[...] + rate * (drive - coeff * pulled)
        out_ref[:, lines, :] = new.astype(BF16).reshape(total, TILE, LANES)


def slab_update(spread, anneal, step_size, grams, states, grads):
    total, lines, _ = grads.shape
    wide = total * TILE
    block = min(lines, 4 * TILE)
    return call(
        update_body,
        "slab_update",
        flops=4 * wide * wide * LANES * (lines // TILE),
        moved=6 * grads.size,
        grid=(lines // block,),
        in_specs=[pl.BlockSpec(memory_space=pltpu.SMEM)] * 3
        + [
            pl.BlockSpec(grams.shape, lambda i: (0, 0, 0)),
            pl.BlockSpec((total, block, LANES), lambda i: (0, i, 0)),
            pl.BlockSpec((total, block, LANES), lambda i: (0, i, 0)),
        ],
        out_specs=pl.BlockSpec((total, block, LANES), lambda i: (0, i, 0)),
        out_shape=jax.ShapeDtypeStruct(grads.shape, BF16),
        scratch_shapes=[pltpu.VMEM((wide, wide), BF16), pltpu.VMEM((wide, LANES), F32)],
    )(spread, anneal, step_size, grams, states, grads)


def plain_update(spread, anneal, step_size, states, grads):
    total, lines, _ = grads.shape
    flat = states[:, :lines].reshape(total, -1)
    gram = lax.dot_general(flat, flat, (((1,), (1,)), ((), ())), preferred_element_type=F32)
    gram = lax.psum(gram, "slab")
    norms = jnp.diagonal(gram)
    kernel = jnp.exp(-(norms[:, None] + norms[None, :] - 2.0 * gram) / (spread[0] * NCELL)).astype(BF16)
    ksum = jnp.sum(kernel.astype(F32), axis=1)
    drive = jnp.dot(kernel, grads.reshape(total, -1), preferred_element_type=F32)
    pulled = jnp.dot(kernel, flat, preferred_element_type=F32)
    values = flat.astype(F32)
    repel = values * ksum[:, None] - pulled
    coeff = 2.0 * anneal[0] / spread[0]
    new = values + step_size[0] / total * (drive + coeff * repel)
    return new.astype(BF16).reshape(grads.shape)


def on_device(particles, observed, precision, spread, anneal, step_size):
    slabs = lax.axis_size("slab")
    total = particles.shape[0] * slabs
    cells = NCELL // slabs
    lines = cells // LANES
    states = split_row(particles, slabs)
    states = lax.all_to_all(states, "slab", split_axis=0, concat_axis=0, tiled=True)
    start = lax.axis_index("slab") * lines
    obs = lax.dynamic_slice_in_dim(observed.reshape(-1, LANES), start, lines)
    prec = lax.dynamic_slice_in_dim(precision.reshape(-1, LANES), start, lines)
    if total * TILE <= 256:
        grams = slab_gram(states, slabs)
        grams = lax.all_to_all(grams, "slab", split_axis=0, concat_axis=0, tiled=True)
        grads = slab_gradient(states, obs, prec)
        new = slab_update(spread, anneal, step_size, grams, states, grads)
    else:
        grads = slab_gradient(states, obs, prec)
        new = plain_update(spread, anneal, step_size, states, grads)
    new = lax.all_to_all(new, "slab", split_axis=0, concat_axis=0, tiled=True)
    return join_row(new)


def solution(mesh):
    in_specs = (
        P(("groups", "slab"), None),
        P("groups"),
        P("groups"),
        P("groups"),
        P("groups"),
        P("groups"),
    )
    out_specs = P(("groups", "slab"), None)
    return jax.shard_map(
        on_device, mesh=mesh, in_specs=in_specs, out_specs=out_specs, check_vma=False
    )
```

time: 213 us -> 153 us (0.72)
  waiting for transfers between devices: 42.8 us -> 0.01 us
  local copies, waits for them, and re-layouts: 37.5 us -> 6.08 us
  Pallas kernels: 0 us -> 29.1 us
  blocking collectives: 84.3 us -> 110 us
  other arithmetic: 23.2 us -> 0 us
  matrix products: 8.95 us -> 0 us
  starting transfers between devices: 13.2 us -> 4.73 us
    all_to_all x1 -> x2, blocking collectives: 61.8 us -> 110 us  [the longest x1 56.1 us: on_device(): lax.all_to_all(states, 'slab', split_axis=0, concat_axis=0, tiled=True)]
    all_to_all x1, waiting for transfers between devices: 42.8 us -> 0.01 us  [on_device(): lax.all_to_all(grams, 'slab', split_axis=0, concat_axis=0, tiled=True)]
    pallas_call x0 -> x5, Pallas kernels: none -> 29.1 us  [the longest x1 12 us: slab_gradient(): call(gradient_body, 'slab_gradient', flops=30 * states.size, moved=4 * st...]
    psum x1 -> x0, blocking collectives: 22.5 us -> none  [on_device(): gram = lax.psum(local_gram, 'slab')]
    unnamed x11 -> x6, local copies, waits for them, and re-layouts: 23.3 us -> 5.09 us
    all_to_all x1 -> x0, local copies, waits for them, and re-layouts: 13.3 us -> none  [on_device(): lax.all_to_all(particles, 'slab', split_axis=1, concat_axis=0, tiled=True)]
    unnamed x1 -> x0, other arithmetic: 13.1 us -> none
    dot_general x3 -> x0, matrix products: 8.95 us -> none  [the longest x1 5.99 us: on_device(): pulled = jnp.dot(kernel, states, preferred_element_type=jnp.float32)]
  transfers between devices with their start and end apart: 3 -> 1, of which waited for: 1 -> 0; matrix products, arithmetic and copies ran while one was open for 2% -> 1% of each run, Pallas kernels for 0% -> 8%
where the time goes in v1:
time: 153 us; the launch traced here: 152 us
  blocking collectives  110 us (72%)
  Pallas kernels  29.1 us (19%)
  local copies, waits for them, and re-layouts  6.08 us (4%)
  starting transfers between devices  4.73 us (3%)
  between operations  1.98 us (1%)
    all_to_all x1, blocking collectives, on_device(): lax.all_to_all(states, 'slab', split_axis=0, concat_axis=0, tiled=True)  56.1 us
    all_to_all x1, blocking collectives, on_device(): new = lax.all_to_all(new, 'slab', split_axis=0, concat_axis=0, tiled=True)  53.7 us
    pallas_call x1, Pallas kernels, slab_gradient(): call(gradient_body, 'slab_gradient', flops=30 * states.size, moved=4 * st...  12 us
    pallas_call x1, Pallas kernels, join_row(): call(join_body, 'join_row', moved=6 * count * cells, grid=(count,), in_sp...  7.62 us
    unnamed x6, local copies, waits for them, and re-layouts  5.09 us
    all_to_all x1, starting transfers between devices, on_device(): lax.all_to_all(grams, 'slab', split_axis=0, concat_axis=0, tiled=True)  4.73 us
    pallas_call x1, Pallas kernels, slab_update(): call(update_body, 'slab_update', flops=4 * wide * wide * LANES * (lines /...  4 us
  transfers between devices with their start and end apart: 1, of which 0 were waited for; matrix products, arithmetic and copies ran while one was open for 1% of the time, Pallas kernels for 8%

profile of v1, /device:TPU:9, one launch (start us, length us, event | category | flops | bytes accessed | tf_op | source)
XLA Modules:
  0.0 151.8 jit_solution(14905781850924962719)
XLA Ops:
  0.0 0.0 copy-start
  0.0 2.2 %copy-done = bf16[1,1048576]{1,0:T(2,128)(2,1)S(1)} copy-done((bf16[1,1048576]{1,0:T(2,128)(2,1)S(1)}, bf16[1,1048576]{1,0:T(2,128)(2,1)}, u32[]{:S(2)}) %copy-start) | copy-done | bytes 2097176
  2.2 2.5 %split_row.1 = bf16[16,528,128]{2,1,0:T(8,128)(2,1)S(1)} custom-call(bf16[1,1048576]{1,0:T(2,128)(2,1)S(1)} %copy-done, bf16[1,1048576]{1,0:T(2,128)(2,1)S(1)} %copy-done, bf16[1,1048576]{1,0:T(2,128)(2,1)S(1)} %copy-done), custom_call_target="tpu_custom_call" | custom-call | bytes 6291456 | tf_op jit(solution)/shard_map/split_row/pallas_call | solution.py:51
  4.7 56.1 %all_to_all.15.states_ref = bf16[16,528,128]{2,1,0:T(8,128)(2,1)S(1)} all-to-all(bf16[16,528,128]{2,1,0:T(8,128)(2,1)S(1)} %split_row.1), channel_id=1, replica_groups=mesh['groups'=2,'slab'=16] {'slab'}, dimensions={0} | all-to-all | bytes 4325376 | tf_op jit(solution)/shard_map/all_to_all | solution.py:268
  60.7 3.1 %slab_gram.1 = f32[16,16,128]{2,1,0:T(8,128)} custom-call(bf16[16,528,128]{2,1,0:T(8,128)(2,1)S(1)} %all_to_all.15.states_ref), custom_call_target="tpu_custom_call" | custom-call | flops 553648128 | bytes 2162688 | tf_op jit(solution)/shard_map/slab_gram/pallas_call | solution.py:125
  63.8 4.7 %all-to-all-start.1 = ((f32[16,16,128]{2,1,0:T(8,128)}), f32[16,16,128]{2,1,0:T(8,128)S(1)}, u32[]{:S(2)}, u32[]{:S(2)}) async-start(f32[16,16,128]{2,1,0:T(8,128)} %slab_gram.1), calls=%async_computation.1 | async-start | bytes 262144 | tf_op jit(solution)/shard_map/all_to_all | solution.py:274
  70.5 1.0 constant_dynamic-slice_fusion
  71.5 12.0 %slab_gradient.1.grads_ref = bf16[16,512,128]{2,1,0:T(8,128)(2,1)S(1)} custom-call(bf16[16,528,128]{2,1,0:T(8,128)(2,1)S(1)} %all_to_all.15.states_ref, bf16[512,128]{1,0:T(8,128)(2,1)S(1)} %get-tuple-element.6.observed_ref, bf16[512,128]{1,0:T(8,128)(2,1)S(1)} %get-tuple-element.5.precision_ref), custom_call_target="tpu_custom_call" | custom-call | flops 32440320 | bytes 4325376 | tf_op jit(solution)/shard_map/slab_gradient/pallas_call | solution.py:179
  83.5 0.0 copy-start.1
  83.5 1.3 copy-done.1
  84.8 0.0 all-to-all-done.1.grams_ref
  84.8 0.0 copy-start.2
  84.8 1.6 %copy-done.2 = bf16[16,512,128]{2,1,0:T(8,128)(2,1)S(1)} copy-done((bf16[16,512,128]{2,1,0:T(8,128)(2,1)S(1)}, bf16[16,512,128]{2,1,0:T(8,128)(2,1)}, u32[]{:S(2)}) %copy-start.2) | copy-done | bytes 2097176
  86.4 4.0 %slab_update.1 = bf16[16,512,128]{2,1,0:T(8,128)(2,1)S(1)} custom-call(f32[1]{0:T(128)S(6)} %copy.7.spread_ref, f32[1]{0:T(128)S(6)} %copy.8.anneal_ref, f32[1]{0:T(128)S(6)} %copy.9.step_ref, f32[16,16,128]{2,1,0:T(8,128)S(1)} %all-to-all-done.1.grams_ref, bf16[16,528,128]{2,1,0:T(8,128)(2,1)S(1)} %all_to_all.15.states_ref, bf16[16,512,128]{2,1,0:T(8,128)(2,1)S(1)} %copy-done.2), custom_call_target="tpu_custom_call" | custom-call | flops 1073741824 | bytes 6291456 | tf_op jit(solution)/shard_map/slab_update/pallas_call | solution.py:227
  90.4 53.7 %all_to_all.16.slab_ref = bf16[16,512,128]{2,1,0:T(8,128)(2,1)S(1)} all-to-all(bf16[16,512,128]{2,1,0:T(8,128)(2,1)S(1)} %slab_update.1), channel_id=1, replica_groups=mesh['groups'=2,'slab'=16] {'slab'}, dimensions={0} | all-to-all | bytes 4194304 | tf_op jit(solution)/shard_map/all_to_all | solution.py:280
  144.1 7.6 %join_row.1 = bf16[1,1048576]{1,0:T(2,128)(2,1)} custom-call(bf16[16,512,128]{2,1,0:T(8,128)(2,1)S(1)} %all_to_all.16.slab_ref), custom_call_target="tpu_custom_call" | custom-call | bytes 6291456 | tf_op jit(solution)/shard_map/join_row/pallas_call | solution.py:73
Async XLA Ops:
  0.0 2.2 %copy-start = (bf16[1,1048576]{1,0:T(2,128)(2,1)S(1)}, bf16[1,1048576]{1,0:T(2,128)(2,1)}, u32[]{:S(2)}) copy-start(bf16[1,1048576]{1,0:T(2,128)(2,1)} %below_ref.1) | copy-start | bytes 6291460
  63.8 21.0 %all-to-all-start.1 = ((f32[16,16,128]{2,1,0:T(8,128)}), f32[16,16,128]{2,1,0:T(8,128)S(1)}, u32[]{:S(2)}, u32[]{:S(2)}) async-start(f32[16,16,128]{2,1,0:T(8,128)} %slab_gram.1), calls=%async_computation.1 | async-start | bytes 262144 | tf_op jit(solution)/shard_map/all_to_all | solution.py:274
  83.5 1.3 copy-start.1
  84.8 1.6 %copy-start.2 = (bf16[16,512,128]{2,1,0:T(8,128)(2,1)S(1)}, bf16[16,512,128]{2,1,0:T(8,128)(2,1)}, u32[]{:S(2)}) copy-start(bf16[16,512,128]{2,1,0:T(8,128)(2,1)} %copy-done.1) | copy-start | bytes 6291460

commit v2 on v1

--- a/solution.py
+++ b/solution.py
@@ -259,9 +259,302 @@
     return new.astype(BF16).reshape(grads.shape)
 
 
+def split_pieces_body(first, me_ref, row_ref, above_ref, below_ref, *out_refs):
+    step = pl.program_id(0)
+    slab = me_ref[0] ^ (first + step)
+    slabs = GRID_X * GRID_Y // row_ref.shape[1]
+    lines = out_refs[0].shape[0] - TILE
+    for k, out_ref in enumerate(out_refs):
+
+        @pl.when(step == k)
+        def _():
+            out_ref[:lines, :] = row_ref[...].reshape(lines, LANES)
+            below = below_ref[...].astype(F32).reshape(LINE, LANES)
+            above = above_ref[...].astype(F32).reshape(LINE, LANES)
+            below = jnp.where(slab == slabs - 1, 0.0, below)
+            above = jnp.where(slab == 0, 0.0, above)
+            out_ref[lines:, :] = jnp.concatenate([below, above], axis=0).astype(BF16)
+
+
+def split_pieces(me, row, slabs, first, count):
+    cells = row.shape[1] // slabs
+    rows = cells // GRID_Y
+    lines = cells // LANES
+    last = GRID_X - 1
+
+    def slab(i, me_ref):
+        return me_ref[0] ^ (first + i)
+
+    return call(
+        functools.partial(split_pieces_body, first),
+        "split_pieces",
+        moved=6 * cells * count,
+        grid_spec=pltpu.PrefetchScalarGridSpec(
+            num_scalar_prefetch=1,
+            grid=(count,),
+            in_specs=[
+                pl.BlockSpec((1, cells), lambda i, m: (0, slab(i, m))),
+                pl.BlockSpec((1, GRID_Y), lambda i, m: (0, jnp.maximum(slab(i, m) * rows - 1, 0))),
+                pl.BlockSpec((1, GRID_Y), lambda i, m: (0, jnp.minimum(slab(i, m) * rows + rows, last))),
+            ],
+            out_specs=[pl.BlockSpec((lines + TILE, LANES), lambda i, m: (0, 0))] * count,
+        ),
+        out_shape=[jax.ShapeDtypeStruct((lines + TILE, LANES), BF16)] * count,
+    )(me, row, row, row)
+
+
+def join_pieces_body(me_ref, *refs):
+    row_ref = refs[-1]
+    pieces = refs[:-1] if refs[0].shape[-1] == LANES else refs[1:-1]
+    for k, piece_ref in enumerate(pieces):
+
+        @pl.when(pl.program_id(0) == k)
+        def _():
+            row_ref[...] = piece_ref[...].reshape(row_ref.shape)
+
+
+def join_pieces(me, row, pieces, group):
+    count = len(pieces)
+    lines = pieces[0].shape[0]
+    cells = lines * LANES
+    whole = pl.BlockSpec((lines, LANES), lambda i, m: (0, 0))
+    begun = [] if row is None else [row]
+
+    def slab(i, me_ref):
+        k = jnp.int32(group[0])
+        for at in range(1, count):
+            k = jnp.where(i == at, group[at], k)
+        return me_ref[0] ^ k
+
+    return call(
+        join_pieces_body,
+        "join_pieces",
+        moved=6 * count * cells,
+        grid_spec=pltpu.PrefetchScalarGridSpec(
+            num_scalar_prefetch=1,
+            grid=(count,),
+            in_specs=[pl.BlockSpec(memory_space=pl.ANY)] * len(begun) + [whole] * count,
+            out_specs=pl.BlockSpec((1, cells), lambda i, m: (0, slab(i, m))),
+        ),
+        out_shape=jax.ShapeDtypeStruct((1, NCELL), BF16),
+        input_output_aliases={1: 0} if begun else {},
+    )(me, *begun, *pieces)
+
+
+def swap(me, total):
+    row = lax.broadcasted_iota(jnp.int32, (total, total), 0)
+    col = lax.broadcasted_iota(jnp.int32, (total, total), 1)
+    return (row == col ^ me).astype(F32)
+
+
+def reorder(me, gram):
+    order = swap(me, gram.shape[0])
+    half = jnp.dot(order, gram, precision=lax.Precision.HIGHEST, preferred_element_type=F32)
+    return jnp.dot(half, order, precision=lax.Precision.HIGHEST, preferred_element_type=F32)
+
+
+def gram_pieces_body(total, me_ref, *refs):
+    pieces, out_ref, pairs = refs[:total], refs[-2], refs[-1]
+    wide = total * TILE
+    tiles = 4
+    steps = (pieces[0].shape[0] - TILE) // (tiles * TILE)
+    pairs[...] = jnp.zeros_like(pairs)
+
+    def step(i, carry):
+        parts = []
+        for t in range(tiles):
+            lines = pl.ds(pl.multiple_of((i * tiles + t) * TILE, TILE), TILE)
+            parts.append(jnp.concatenate([piece[lines, :] for piece in pieces], axis=0))
+        block = jnp.concatenate(parts, axis=1)
+        pairs[...] += lax.dot_general(block, block, (((1,), (1,)), ((), ())), preferred_element_type=F32)
+        return carry
+
+    lax.fori_loop(0, steps, step, 0)
+    equal = jnp.where(same_line(total), pairs[...], 0.0)
+    rows = jnp.sum(equal.reshape(total, TILE, wide), axis=1)
+    gram = jnp.dot(rows, members(total, F32), precision=lax.Precision.HIGHEST, preferred_element_type=F32)
+    gram = reorder(me_ref[0], gram)
+    gram = jnp.concatenate([gram, jnp.zeros((total, LANES - total), F32)], axis=1)
+    out_ref[...] = jnp.broadcast_to(gram[None], out_ref.shape)
+
+
+def gram_pieces(me, pieces, earlier):
+    total = len(pieces)
+    wide = total * TILE
+    lines = pieces[0].shape[0]
+    return call(
+        functools.partial(gram_pieces_body, total),
+        "gram_pieces",
+        flops=2 * wide * wide * LANES * (lines // TILE),
+        moved=2 * total * pieces[0].size,
+        in_specs=[pl.BlockSpec(memory_space=pltpu.SMEM)]
+        + [pl.BlockSpec(memory_space=pltpu.VMEM)] * total
+        + [pl.BlockSpec(memory_space=pl.ANY)] * len(earlier),
+        out_specs=pl.BlockSpec(memory_space=pltpu.VMEM),
+        out_shape=jax.ShapeDtypeStruct((total, total, LANES), F32),
+        scratch_shapes=[pltpu.VMEM((wide, wide), F32)],
+    )(me, *pieces, *earlier)
+
+
+def gradient_pieces_body(count, observed_ref, precision_ref, *refs):
+    pieces, out_refs = refs[:count], refs[count:]
+    tiles = 4
+    block = tiles * TILE
+    rows = block // LINE
+    steps = (pieces[0].shape[0] - TILE) // block
+    shape = (rows, LINE, LANES)
+    lane = lax.broadcasted_iota(jnp.int32, (1, LINE, LANES), 2)
+    line = lax.broadcasted_iota(jnp.int32, (1, LINE, LANES), 1)
+
+    def step(i, carry):
+        start = pl.multiple_of(i * block, block)
+        before = pl.multiple_of(jnp.where(i == 0, steps * block, start - TILE), TILE)
+        after = pl.multiple_of(start + block, TILE)
+        obs = observed_ref[pl.ds(start, block), :].astype(F32).reshape(shape)
+        prec = precision_ref[pl.ds(start, block), :].astype(F32).reshape(shape)
+        for piece, out_ref in zip(pieces, out_refs):
+            here = piece[pl.ds(start, block), :].astype(F32)
+            first = piece[pl.ds(before, TILE), :].astype(F32)[LINE:]
+            last = piece[pl.ds(after, TILE), :].astype(F32)[:LINE]
+            above = jnp.concatenate([first, here[:-LINE]], axis=0).reshape(shape)
+            below = jnp.concatenate([here[LINE:], last], axis=0).reshape(shape)
+            field = here.reshape(shape)
+            turned = pltpu.roll(field, 1, 2)
+            carried = jnp.where(line == 0, 0.0, pltpu.roll(turned, 1, 1))
+            left = jnp.where(lane == 0, carried, turned)
+            turned = pltpu.roll(field, LANES - 1, 2)
+            carried = jnp.where(line == LINE - 1, 0.0, pltpu.roll(turned, LINE - 1, 1))
+            right = jnp.where(lane == LANES - 1, carried, turned)
+            laplace = (4.0 + mass_term) * field - (below + above + right + left)
+            squash = jnp.tanh(field)
+            result = prec * (obs - squash) * (1.0 - squash * squash) - prior_scale * laplace
+            out_ref[pl.ds(start, block), :] = result.reshape(block, LANES).astype(BF16)
+        return carry
+
+    lax.fori_loop(0, steps, step, 0)
+
+
+def gradient_pieces(pieces, observed, precision):
+    count = len(pieces)
+    lines = pieces[0].shape[0] - TILE
+    return call(
+        functools.partial(gradient_pieces_body, count),
+        "gradient_pieces",
+        flops=30 * count * lines * LANES,
+        moved=4 * count * lines * LANES,
+        in_specs=[pl.BlockSpec(memory_space=pltpu.VMEM)] * (2 + count),
+        out_specs=[pl.BlockSpec(memory_space=pltpu.VMEM)] * count,
+        out_shape=[jax.ShapeDtypeStruct((lines, LANES), BF16)] * count,
+    )(observed, precision, *pieces)
+
+
+def update_pieces_body(total, first, count, me_ref, spread_ref, anneal_ref, step_ref, grams_ref, *refs):
+    states_refs, grads_refs = refs[:total], refs[total : 2 * total]
+    out_refs, mixer, own = refs[2 * total : 2 * total + count], refs[-2], refs[-1]
+    wide = total * TILE
+    high = count * TILE
+    rate = step_ref[0] / total
+    coeff = 2.0 * anneal_ref[0] / spread_ref[0]
+
+    @pl.when(pl.program_id(0) == 0)
+    def _():
+        gram = reorder(me_ref[0], jnp.sum(grams_ref[...], axis=0)[:, :total])
+        row = lax.broadcasted_iota(jnp.int32, (total, total), 0)
+        col = lax.broadcasted_iota(jnp.int32, (total, total), 1)
+        diagonal = jnp.where(row == col, gram, 0.0)
+        down = jnp.sum(diagonal, axis=1, keepdims=True)
+        across = jnp.sum(diagonal, axis=0, keepdims=True)
+        kernel = jnp.exp(-(down + across - 2.0 * gram) / (spread_ref[0] * NCELL)).astype(BF16)
+        ksum = jnp.sum(kernel.astype(F32), axis=1, keepdims=True)[first : first + count]
+        member = members(total, BF16)
+        half = jnp.dot(member, kernel, preferred_element_type=F32).astype(BF16)
+        full = lax.dot_general(half, member, (((1,), (1,)), ((), ())), preferred_element_type=F32)
+        full = jnp.where(same_line(total), full, 0.0)
+        mixer[...] = full[first * TILE : first * TILE + high].astype(BF16)
+        gain = 1.0 + rate * coeff * ksum
+        own[...] = jnp.broadcast_to(gain[:, :, None], (count, TILE, LANES)).reshape(high, LANES)
+
+    for t in range(out_refs[0].shape[0] // TILE):
+        lines = slice(t * TILE, (t + 1) * TILE)
+        states = jnp.concatenate([ref[lines, :] for ref in states_refs], axis=0)
+        grads = jnp.concatenate([ref[lines, :] for ref in grads_refs], axis=0)
+        mixed = jnp.dot(mixer[...], jnp.concatenate([grads, states], axis=1), preferred_element_type=F32)
+        drive, pulled = mixed[:, :LANES], mixed[:, LANES:]
+        kept = states[first * TILE : first * TILE + high].astype(F32)
+        new = (kept * own[...] + rate * (drive - coeff * pulled)).astype(BF16)
+        for k, out_ref in enumerate(out_refs):
+            out_ref[lines, :] = new[k * TILE : (k + 1) * TILE]
+
+
+def update_pieces(me, spread, anneal, step_size, grams, states, grads, first, count):
+    total = len(states)
+    lines = grads[0].shape[0]
+    wide = total * TILE
+    block = min(lines, 4 * TILE)
+    part = pl.BlockSpec((block, LANES), lambda i: (i, 0))
+    return call(
+        functools.partial(update_pieces_body, total, first, count),
+        "update_pieces",
+        flops=4 * count * TILE * wide * LANES * (lines // TILE),
+        moved=2 * (2 * total + count) * grads[0].size,
+        grid=(lines // block,),
+        in_specs=[pl.BlockSpec(memory_space=pltpu.SMEM)] * 4
+        + [pl.BlockSpec(grams.shape, lambda i: (0, 0, 0))]
+        + [part] * (2 * total),
+        out_specs=[part] * count,
+        out_shape=[jax.ShapeDtypeStruct((lines, LANES), BF16)] * count,
+        scratch_shapes=[pltpu.VMEM((count * TILE, wide), BF16), pltpu.VMEM((count * TILE, LANES), F32)],
+    )(me, spread, anneal, step_size, grams, *states, *grads)
+
+
+def exchange(piece, k, slabs):
+    return lax.ppermute(piece, "slab", [(i, i ^ k) for i in range(slabs)])
+
+
+ORDER = (8, 9, 4, 10, 11, 5, 12, 13, 6, 14, 15, 7, 1, 2, 3)
+GROUPS = ((0, 8, 9, 4), (10, 11, 5, 12), (13, 6, 14, 15), (7, 1, 2, 3))
+
+
+def by_pieces(particles, observed, precision, spread, anneal, step_size):
+    slabs = lax.axis_size("slab")
+    half = slabs // 2
+    me = lax.axis_index("slab").astype(jnp.int32).reshape(1)
+    far = split_pieces(me, particles, slabs, half, half)
+    near = split_pieces(me, particles, slabs, 0, half)
+    mine = near + far
+    states = [mine[0]] + [None] * (slabs - 1)
+    for k in ORDER:
+        states[k] = exchange(mine[k], k, slabs)
+    lines = NCELL // slabs // LANES
+    start = me[0] * lines
+    obs = lax.dynamic_slice_in_dim(observed.reshape(-1, LANES), start, lines)
+    prec = lax.dynamic_slice_in_dim(precision.reshape(-1, LANES), start, lines)
+    grads = [None] * slabs
+    for group in GROUPS[:-1]:
+        for k, grad in zip(group, gradient_pieces([states[k] for k in group], obs, prec)):
+            grads[k] = grad
+    grams = gram_pieces(me, states, [grads[group[0]] for group in GROUPS[:-1]])
+    grams = lax.all_to_all(grams, "slab", split_axis=0, concat_axis=0, tiled=True)
+    for group in GROUPS[-1:]:
+        for k, grad in zip(group, gradient_pieces([states[k] for k in group], obs, prec)):
+            grads[k] = grad
+    far = update_pieces(me, spread, anneal, step_size, grams, states, grads, half, half)
+    near = update_pieces(me, spread, anneal, step_size, grams, states, grads, 0, half)
+    mine = near + far
+    new = [mine[0]] + [None] * (slabs - 1)
+    for k in ORDER:
+        new[k] = exchange(mine[k], k, slabs)
+    row = None
+    for group in GROUPS:
+        row = join_pieces(me, row, [new[k] for k in group], group)
+    return row
+
+
 def on_device(particles, observed, precision, spread, anneal, step_size):
     slabs = lax.axis_size("slab")
     total = particles.shape[0] * slabs
+    if slabs == 16:
+        return by_pieces(particles, observed, precision, spread, anneal, step_size)
     cells = NCELL // slabs
     lines = cells // LANES
     states = split_row(particles, slabs)

time: 153 us -> 153 us (level)
  blocking collectives: 110 us -> 0 us
  waiting for transfers between devices: 0.01 us -> 69.1 us
  starting transfers between devices: 4.73 us -> 42.4 us
  local copies, waits for them, and re-layouts: 6.08 us -> 17.1 us
  Pallas kernels: 29.1 us -> 21.7 us
    all_to_all x2 -> x0, blocking collectives: 110 us -> none  [the longest x1 56.1 us: on_device(): lax.all_to_all(states, 'slab', split_axis=0, concat_axis=0, tiled=True)]
    ppermute x0 -> x30, waiting for transfers between devices: none -> 68.9 us  [exchange(): return lax.ppermute(piece, 'slab', [(i, i ^ k) for i in range(slabs)])]
    ppermute x0 -> x30, starting transfers between devices: none -> 38.7 us  [exchange(): return lax.ppermute(piece, 'slab', [(i, i ^ k) for i in range(slabs)])]
    unnamed x6 -> x40, local copies, waits for them, and re-layouts: 5.09 us -> 16.1 us
    pallas_call x5 -> x13, Pallas kernels: 29.1 us -> 21.7 us  [the longest x4 6.29 us: join_pieces(): call(join_pieces_body, 'join_pieces', moved=6 * count * cells, grid_spec=...]
  transfers between devices with their start and end apart: 1 -> 31, of which waited for: 0 -> 20; matrix products, arithmetic and copies ran while one was open for 1% -> 1% of each run, Pallas kernels for 8% -> 9%
where the time goes in v2:
time: 153 us; the launch traced here: 152 us
  waiting for transfers between devices  69.1 us (45%)
  starting transfers between devices  42.4 us (28%)
  Pallas kernels  21.7 us (14%)
  local copies, waits for them, and re-layouts  17.1 us (11%)
  between operations  2.11 us (1%)
    ppermute x30, waiting for transfers between devices, exchange(): return lax.ppermute(piece, 'slab', [(i, i ^ k) for i in range(slabs)])  68.9 us
    ppermute x30, starting transfers between devices, exchange(): return lax.ppermute(piece, 'slab', [(i, i ^ k) for i in range(slabs)])  38.7 us
    unnamed x40, local copies, waits for them, and re-layouts  16.1 us
    pallas_call x4, Pallas kernels, join_pieces(): call(join_pieces_body, 'join_pieces', moved=6 * count * cells, grid_spec=...  6.29 us
    pallas_call x2, Pallas kernels, update_pieces(): call(functools.partial(update_pieces_body, total, first, count), 'update_...  6.21 us
    pallas_call x4, Pallas kernels, gradient_pieces(): call(functools.partial(gradient_pieces_body, count), 'gradient_pieces', f...  4.41 us
    all_to_all x1, starting transfers between devices, by_pieces(): lax.all_to_all(grams, 'slab', split_axis=0, concat_axis=0, tiled=True)  3.63 us
  transfers between devices with their start and end apart: 31, of which 20 were waited for; matrix products, arithmetic and copies ran while one was open for 1% of the time, Pallas kernels for 9%

profile of v2, /device:TPU:9, one launch (start us, length us, event | category | flops | bytes accessed | tf_op | source)
XLA Modules:
  0.0 152.4 jit_solution(1261337761310190435)
XLA Ops:
  0.0 2.2 %copy-done = bf16[1,1048576]{1,0:T(2,128)(2,1)S(1)} copy-done((bf16[1,1048576]{1,0:T(2,128)(2,1)S(1)}, bf16[1,1048576]{1,0:T(2,128)(2,1)}, u32[]{:S(2)}) %copy-start) | copy-done | bytes 2097176
  2.8 2.4 %collective-permute-start.7 = (bf16[528,128]{1,0:T(8,128)(2,1)S(1)}, bf16[528,128]{1,0:T(8,128)(2,1)S(1)}, u32[]{:S(2)}, u32[]{:S(2)}) collective-permute-start(bf16[528,128]{1,0:T(8,128)(2,1)S(1)} %get-tuple-element.61), channel_id=1, source_target_pairs={{0,8},{1,9},{2,10},{3,11},{4,12},{5,13},{6,14},{7,15},{8,0},{9,1},... | collective-permute-start | bytes 405512 | tf_op jit(solution)/shard_map/ppermute | solution.py:511
  6.1 3.3 %collective-permute-start.9 = (bf16[528,128]{1,0:T(8,128)(2,1)S(1)}, bf16[528,128]{1,0:T(8,128)(2,1)S(1)}, u32[]{:S(2)}, u32[]{:S(2)}) collective-permute-start(bf16[528,128]{1,0:T(8,128)(2,1)S(1)} %get-tuple-element.63), channel_id=1, source_target_pairs={{0,10},{1,11},{2,8},{3,9},{4,14},{5,15},{6,12},{7,13},{8,2},{9,3},... | collective-permute-start | bytes 405512 | tf_op jit(solution)/shard_map/ppermute | solution.py:511
  10.3 12.5 %collective-permute-done.7.refs_1_.refs_8_ = bf16[528,128]{1,0:T(8,128)(2,1)S(1)} collective-permute-done((bf16[528,128]{1,0:T(8,128)(2,1)S(1)}, bf16[528,128]{1,0:T(8,128)(2,1)S(1)}, u32[]{:S(2)}, u32[]{:S(2)}) %collective-permute-start.7) | collective-permute-done | bytes 135200 | tf_op jit(solution)/shard_map/ppermute | solution.py:511
  23.1 1.5 split_pieces.2
  24.6 1.1 collective-permute-done.8.refs_2_.refs_9_
  25.7 1.5 collective-permute-start.13
  27.2 4.2 %collective-permute-done.9.refs_0_.refs_10_ = bf16[528,128]{1,0:T(8,128)(2,1)S(1)} collective-permute-done((bf16[528,128]{1,0:T(8,128)(2,1)S(1)}, bf16[528,128]{1,0:T(8,128)(2,1)S(1)}, u32[]{:S(2)}, u32[]{:S(2)}) %collective-permute-start.9) | collective-permute-done | bytes 135200 | tf_op jit(solution)/shard_map/ppermute | solution.py:511
  31.4 1.7 %collective-permute-start.14 = (bf16[528,128]{1,0:T(8,128)(2,1)S(1)}, bf16[528,128]{1,0:T(8,128)(2,1)S(1)}, u32[]{:S(2)}, u32[]{:S(2)}) collective-permute-start(bf16[528,128]{1,0:T(8,128)(2,1)S(1)} %get-tuple-element.68), channel_id=1, source_target_pairs={{0,15},{1,14},{2,13},{3,12},{4,11},{5,10},{6,9},{7,8},{8,7},{9,6},... | collective-permute-start | bytes 405512 | tf_op jit(solution)/shard_map/ppermute | solution.py:511
  33.1 4.3 %collective-permute-done.10.refs_1_.refs_11_ = bf16[528,128]{1,0:T(8,128)(2,1)S(1)} collective-permute-done((bf16[528,128]{1,0:T(8,128)(2,1)S(1)}, bf16[528,128]{1,0:T(8,128)(2,1)S(1)}, u32[]{:S(2)}, u32[]{:S(2)}) %collective-permute-start.10) | collective-permute-done | bytes 135200 | tf_op jit(solution)/shard_map/ppermute | solution.py:511
  37.3 2.6 %collective-permute-start.4 = (bf16[528,128]{1,0:T(8,128)(2,1)S(1)}, bf16[528,128]{1,0:T(8,128)(2,1)S(1)}, u32[]{:S(2)}, u32[]{:S(2)}) collective-permute-start(bf16[528,128]{1,0:T(8,128)(2,1)S(1)} %get-tuple-element.58), channel_id=1, source_target_pairs={{0,5},{1,4},{2,7},{3,6},{4,1},{5,0},{6,3},{7,2},{8,13},{9,12},{10,... | collective-permute-start | bytes 405512 | tf_op jit(solution)/shard_map/ppermute | solution.py:511
  41.1 5.7 %collective-permute-done.12.refs_0_.refs_13_ = bf16[528,128]{1,0:T(8,128)(2,1)S(1)} collective-permute-done((bf16[528,128]{1,0:T(8,128)(2,1)S(1)}, bf16[528,128]{1,0:T(8,128)(2,1)S(1)}, u32[]{:S(2)}, u32[]{:S(2)}) %collective-permute-start.12) | collective-permute-done | bytes 135200 | tf_op jit(solution)/shard_map/ppermute | solution.py:511
  46.8 2.2 %collective-permute-done.13.refs_2_.refs_14_ = bf16[528,128]{1,0:T(8,128)(2,1)S(1)} collective-permute-done((bf16[528,128]{1,0:T(8,128)(2,1)S(1)}, bf16[528,128]{1,0:T(8,128)(2,1)S(1)}, u32[]{:S(2)}, u32[]{:S(2)}) %collective-permute-start.13) | collective-permute-done | bytes 135200 | tf_op jit(solution)/shard_map/ppermute | solution.py:511
  49.0 5.2 %collective-permute-start = (bf16[528,128]{1,0:T(8,128)(2,1)}, bf16[528,128]{1,0:T(8,128)(2,1)S(1)}, u32[]{:S(2)}, u32[]{:S(2)}) collective-permute-start(bf16[528,128]{1,0:T(8,128)(2,1)} %get-tuple-element.54), channel_id=1, source_target_pairs={{0,1},{1,0},{2,3},{3,2},{4,5},{5,4},{6,7},{7,6},{8,9},{9,8},{10,11... | collective-permute-start | bytes 405512 | tf_op jit(solution)/shard_map/ppermute | solution.py:511
  54.2 1.1 collective-permute-done.14.refs_3_.refs_15_
  55.5 1.0 collective-permute-start.2
  56.5 1.0 constant_dynamic-slice_fusion
  57.5 1.1 gradient_pieces.6
  58.6 1.1 gradient_pieces.5
  60.4 1.1 gradient_pieces.4
  64.0 2.9 %collective-permute-done.2.refs_3_ = bf16[528,128]{1,0:T(8,128)(2,1)S(1)} collective-permute-done((bf16[528,128]{1,0:T(8,128)(2,1)}, bf16[528,128]{1,0:T(8,128)(2,1)S(1)}, u32[]{:S(2)}, u32[]{:S(2)}) %collective-permute-start.2) | collective-permute-done | bytes 135200 | tf_op jit(solution)/shard_map/ppermute | solution.py:511
  66.9 2.7 %gram_pieces.1 = f32[16,16,128]{2,1,0:T(8,128)S(1)} custom-call(s32[1]{0:T(128)} %bitcast.me_ref, bf16[528,128]{1,0:T(8,128)(2,1)S(1)} %get-tuple-element.53.refs_0_, bf16[528,128]{1,0:T(8,128)(2,1)S(1)} %collective-permute-done.refs_1_, bf16[528,128]{1,0:T(8,128)(2,1)S(1)} %collective-permute-done.1.refs_2_, ...), custom_call_target="tpu_custom_call" | custom-call | flops 553648128 | bytes 2162688 | tf_op jit(solution)/shard_map/gram_pieces/pallas_call | solution.py:385
  70.3 3.6 %all-to-all-start = ((f32[16,16,128]{2,1,0:T(8,128)}), f32[16,16,128]{2,1,0:T(8,128)S(1)}, u32[]{:S(2)}, u32[]{:S(2)}) async-start(f32[16,16,128]{2,1,0:T(8,128)} %copy-done.19), calls=%async_computation | async-start | bytes 262144 | tf_op jit(solution)/shard_map/all_to_all | solution.py:537
  75.8 1.1 gradient_pieces.7
  79.8 0.9 copy-done.2
  83.4 0.9 copy-done.10
  87.9 3.1 %update_pieces.3 = (bf16[512,128]{1,0:T(8,128)(2,1)S(1)}, bf16[512,128]{1,0:T(8,128)(2,1)S(1)}, bf16[512,128]{1,0:T(8,128)(2,1)S(1)}, bf16[512,128]{1,0:T(8,128)...) custom-call(s32[1]{0:T(128)} %bitcast.me_ref, ...), custom_call_target="tpu_custom_call" | custom-call | flops 536870912 | bytes 5242880 | tf_op jit(solution)/shard_map/update_pieces/pallas_call | solution.py:495
  91.0 1.9 %collective-permute-start.15 = (bf16[512,128]{1,0:T(8,128)(2,1)S(1)}, bf16[512,128]{1,0:T(8,128)(2,1)S(1)}, u32[]{:S(2)}, u32[]{:S(2)}) collective-permute-start(bf16[512,128]{1,0:T(8,128)(2,1)S(1)} %get-tuple-element.86), channel_id=1, source_target_pairs={{0,8},{1,9},{2,10},{3,11},{4,12},{5,13},{6,14},{7,15},{8,0},{9,1},... | collective-permute-start | bytes 393224 | tf_op jit(solution)/shard_map/ppermute | solution.py:511
  93.8 3.0 %collective-permute-start.18 = (bf16[512,128]{1,0:T(8,128)(2,1)S(1)}, bf16[512,128]{1,0:T(8,128)(2,1)S(1)}, u32[]{:S(2)}, u32[]{:S(2)}) collective-permute-start(bf16[512,128]{1,0:T(8,128)(2,1)S(1)} %get-tuple-element.89), channel_id=1, source_target_pairs={{0,10},{1,11},{2,8},{3,9},{4,14},{5,15},{6,12},{7,13},{8,2},{9,3},... | collective-permute-start | bytes 393224 | tf_op jit(solution)/shard_map/ppermute | solution.py:511
  97.3 1.0 collective-permute-start.21
  98.3 3.1 %update_pieces.2 = (bf16[512,128]{1,0:T(8,128)(2,1)S(1)}, bf16[512,128]{1,0:T(8,128)(2,1)S(1)}, bf16[512,128]{1,0:T(8,128)(2,1)S(1)}, bf16[512,128]{1,0:T(8,128)...) custom-call(s32[1]{0:T(128)} %bitcast.me_ref, ...), custom_call_target="tpu_custom_call" | custom-call | flops 536870912 | bytes 5242880 | tf_op jit(solution)/shard_map/update_pieces/pallas_call | solution.py:495
  101.4 8.9 %collective-permute-done.15.refs_1_ = bf16[512,128]{1,0:T(8,128)(2,1)S(1)} collective-permute-done((bf16[512,128]{1,0:T(8,128)(2,1)S(1)}, bf16[512,128]{1,0:T(8,128)(2,1)S(1)}, u32[]{:S(2)}, u32[]{:S(2)}) %collective-permute-start.15) | collective-permute-done | bytes 131104 | tf_op jit(solution)/shard_map/ppermute | solution.py:511
  110.2 1.0 collective-permute-start.22
  111.2 1.8 %collective-permute-done.16.refs_2_ = bf16[512,128]{1,0:T(8,128)(2,1)S(1)} collective-permute-done((bf16[512,128]{1,0:T(8,128)(2,1)S(1)}, bf16[512,128]{1,0:T(8,128)(2,1)S(1)}, u32[]{:S(2)}, u32[]{:S(2)}) %collective-permute-start.16) | collective-permute-done | bytes 131104 | tf_op jit(solution)/shard_map/ppermute | solution.py:511
  113.1 5.4 %collective-permute-done.18.refs_1_ = bf16[512,128]{1,0:T(8,128)(2,1)S(1)} collective-permute-done((bf16[512,128]{1,0:T(8,128)(2,1)S(1)}, bf16[512,128]{1,0:T(8,128)(2,1)S(1)}, u32[]{:S(2)}, u32[]{:S(2)}) %collective-permute-start.18) | collective-permute-done | bytes 131104 | tf_op jit(solution)/shard_map/ppermute | solution.py:511
  118.5 4.4 %collective-permute-start.25 = (bf16[512,128]{1,0:T(8,128)(2,1)S(1)}, bf16[512,128]{1,0:T(8,128)(2,1)S(1)}, u32[]{:S(2)}, u32[]{:S(2)}) collective-permute-start(bf16[512,128]{1,0:T(8,128)(2,1)S(1)} %get-tuple-element.96), channel_id=1, source_target_pairs={{0,15},{1,14},{2,13},{3,12},{4,11},{5,10},{6,9},{7,8},{8,7},{9,6},... | collective-permute-start | bytes 393224 | tf_op jit(solution)/shard_map/ppermute | solution.py:511
  122.9 1.4 collective-permute-done.19.refs_2_
  124.3 2.8 %collective-permute-start.17 = (bf16[512,128]{1,0:T(8,128)(2,1)S(1)}, bf16[512,128]{1,0:T(8,128)(2,1)S(1)}, u32[]{:S(2)}, u32[]{:S(2)}) collective-permute-start(bf16[512,128]{1,0:T(8,128)(2,1)S(1)} %get-tuple-element.88), channel_id=1, source_target_pairs={{0,4},{1,5},{2,6},{3,7},{4,0},{5,1},{6,2},{7,3},{8,12},{9,13},{10,... | collective-permute-start | bytes 393224 | tf_op jit(solution)/shard_map/ppermute | solution.py:511
  127.1 1.0 collective-permute-done.21.refs_4_
  128.1 6.1 %collective-permute-done.22.refs_1_ = bf16[512,128]{1,0:T(8,128)(2,1)S(1)} collective-permute-done((bf16[512,128]{1,0:T(8,128)(2,1)S(1)}, bf16[512,128]{1,0:T(8,128)(2,1)S(1)}, u32[]{:S(2)}, u32[]{:S(2)}) %collective-permute-start.22) | collective-permute-done | bytes 131104 | tf_op jit(solution)/shard_map/ppermute | solution.py:511
  134.1 2.2 %collective-permute-done.24.refs_3_ = bf16[512,128]{1,0:T(8,128)(2,1)S(1)} collective-permute-done((bf16[512,128]{1,0:T(8,128)(2,1)S(1)}, bf16[512,128]{1,0:T(8,128)(2,1)S(1)}, u32[]{:S(2)}, u32[]{:S(2)}) %collective-permute-start.24) | collective-permute-done | bytes 131104 | tf_op jit(solution)/shard_map/ppermute | solution.py:511
  136.6 4.7 %collective-permute-done.25.refs_4_ = bf16[512,128]{1,0:T(8,128)(2,1)S(1)} collective-permute-done((bf16[512,128]{1,0:T(8,128)(2,1)S(1)}, bf16[512,128]{1,0:T(8,128)(2,1)S(1)}, u32[]{:S(2)}, u32[]{:S(2)}) %collective-permute-start.25) | collective-permute-done | bytes 131104 | tf_op jit(solution)/shard_map/ppermute | solution.py:511
  141.3 1.6 %collective-permute-start.28 = (bf16[512,128]{1,0:T(8,128)(2,1)S(1)}, bf16[512,128]{1,0:T(8,128)(2,1)S(1)}, u32[]{:S(2)}, u32[]{:S(2)}) collective-permute-start(bf16[512,128]{1,0:T(8,128)(2,1)S(1)} %get-tuple-element.99), channel_id=1, source_target_pairs={{0,2},{1,3},{2,0},{3,1},{4,6},{5,7},{6,4},{7,5},{8,10},{9,11},{10,... | collective-permute-start | bytes 393224 | tf_op jit(solution)/shard_map/ppermute | solution.py:511
  143.4 1.6 %join_pieces.4.refs_0_ = bf16[1,1048576]{1,0:T(2,128)(2,1)} custom-call(s32[1]{0:T(128)} %bitcast.me_ref, bf16[512,128]{1,0:T(8,128)(2,1)S(1)} %get-tuple-element.85.refs_0_, bf16[512,128]{1,0:T(8,128)(2,1)S(1)} %collective-permute-done.15.refs_1_, bf16[512,128]{1,0:T(8,128)(2,1)S(1)} %collective-permute-done.16.refs_2_, ...), custom_call_target="tpu_custom_call" | custom-call | bytes 1572864 | tf_op jit(solution)/shard_map/join_pieces/pallas_call | solution.py:329
  145.0 1.6 %join_pieces.5.refs_0_ = bf16[1,1048576]{1,0:T(2,128)(2,1)} custom-call(s32[1]{0:T(128)} %bitcast.me_ref, bf16[1,1048576]{1,0:T(2,128)(2,1)} %join_pieces.4.refs_0_, bf16[512,128]{1,0:T(8,128)(2,1)S(1)} %collective-permute-done.18.refs_1_, bf16[512,128]{1,0:T(8,128)(2,1)S(1)} %collective-permute-done.19.refs_2_, ...), custom_call_target="tpu_custom_call", output_to_operand_aliasing={{}: (1, {})} | custom-call | bytes 1572864 | tf_op jit(solution)/shard_map/join_pieces/pallas_call | solution.py:329
  146.6 1.6 %join_pieces.6.refs_0_ = bf16[1,1048576]{1,0:T(2,128)(2,1)} custom-call(s32[1]{0:T(128)} %bitcast.me_ref, bf16[1,1048576]{1,0:T(2,128)(2,1)} %join_pieces.5.refs_0_, bf16[512,128]{1,0:T(8,128)(2,1)S(1)} %collective-permute-done.22.refs_1_, bf16[512,128]{1,0:T(8,128)(2,1)S(1)} %collective-permute-done.23.refs_2_, ...), custom_call_target="tpu_custom_call", output_to_operand_aliasing={{}: (1, {})} | custom-call | bytes 1572864 | tf_op jit(solution)/shard_map/join_pieces/pallas_call | solution.py:329
  148.2 2.7 %collective-permute-done.29.refs_4_ = bf16[512,128]{1,0:T(8,128)(2,1)S(1)} collective-permute-done((bf16[512,128]{1,0:T(8,128)(2,1)S(1)}, bf16[512,128]{1,0:T(8,128)(2,1)S(1)}, u32[]{:S(2)}, u32[]{:S(2)}) %collective-permute-start.29) | collective-permute-done | bytes 131104 | tf_op jit(solution)/shard_map/ppermute | solution.py:511
  150.8 1.6 %join_pieces.7 = bf16[1,1048576]{1,0:T(2,128)(2,1)} custom-call(s32[1]{0:T(128)} %bitcast.me_ref, bf16[1,1048576]{1,0:T(2,128)(2,1)} %join_pieces.6.refs_0_, bf16[512,128]{1,0:T(8,128)(2,1)S(1)} %collective-permute-done.26.refs_1_, bf16[512,128]{1,0:T(8,128)(2,1)S(1)} %collective-permute-done.27.refs_2_, ...), custom_call_target="tpu_custom_call", output_to_operand_aliasing={{}: (1, {})} | custom-call | bytes 1572864 | tf_op jit(solution)/shard_map/join_pieces/pallas_call | solution.py:329
  (68 shorter events, 19.5 us)
Async XLA Ops:
  0.0 2.2 %copy-start = (bf16[1,1048576]{1,0:T(2,128)(2,1)S(1)}, bf16[1,1048576]{1,0:T(2,128)(2,1)}, u32[]{:S(2)}) copy-start(bf16[1,1048576]{1,0:T(2,128)(2,1)} %below_ref.3) | copy-start | bytes 6291460
  2.8 20.1 %collective-permute-start.7 = (bf16[528,128]{1,0:T(8,128)(2,1)S(1)}, bf16[528,128]{1,0:T(8,128)(2,1)S(1)}, u32[]{:S(2)}, u32[]{:S(2)}) collective-permute-start(bf16[528,128]{1,0:T(8,128)(2,1)S(1)} %get-tuple-element.61), channel_id=1, source_target_pairs={{0,8},{1,9},{2,10},{3,11},{4,12},{5,13},{6,14},{7,15},{8,0},{9,1},... | collective-permute-start | bytes 405512 | tf_op jit(solution)/shard_map/ppermute | solution.py:511
  5.2 20.6 %collective-permute-start.8 = (bf16[528,128]{1,0:T(8,128)(2,1)S(1)}, bf16[528,128]{1,0:T(8,128)(2,1)S(1)}, u32[]{:S(2)}, u32[]{:S(2)}) collective-permute-start(bf16[528,128]{1,0:T(8,128)(2,1)S(1)} %get-tuple-element.62), channel_id=1, source_target_pairs={{0,9},{1,8},{2,11},{3,10},{4,13},{5,12},{6,15},{7,14},{8,1},{9,0},... | collective-permute-start | bytes 405512 | tf_op jit(solution)/shard_map/ppermute | solution.py:511
  6.1 25.3 %collective-permute-start.9 = (bf16[528,128]{1,0:T(8,128)(2,1)S(1)}, bf16[528,128]{1,0:T(8,128)(2,1)S(1)}, u32[]{:S(2)}, u32[]{:S(2)}) collective-permute-start(bf16[528,128]{1,0:T(8,128)(2,1)S(1)} %get-tuple-element.63), channel_id=1, source_target_pairs={{0,10},{1,11},{2,8},{3,9},{4,14},{5,15},{6,12},{7,13},{8,2},{9,3},... | collective-permute-start | bytes 405512 | tf_op jit(solution)/shard_map/ppermute | solution.py:511
  9.3 28.0 %collective-permute-start.10 = (bf16[528,128]{1,0:T(8,128)(2,1)S(1)}, bf16[528,128]{1,0:T(8,128)(2,1)S(1)}, u32[]{:S(2)}, u32[]{:S(2)}) collective-permute-start(bf16[528,128]{1,0:T(8,128)(2,1)S(1)} %get-tuple-element.64), channel_id=1, source_target_pairs={{0,11},{1,10},{2,9},{3,8},{4,15},{5,14},{6,13},{7,12},{8,3},{9,2},... | collective-permute-start | bytes 405512 | tf_op jit(solution)/shard_map/ppermute | solution.py:511
  9.5 30.7 %collective-permute-start.11 = (bf16[528,128]{1,0:T(8,128)(2,1)S(1)}, bf16[528,128]{1,0:T(8,128)(2,1)S(1)}, u32[]{:S(2)}, u32[]{:S(2)}) collective-permute-start(bf16[528,128]{1,0:T(8,128)(2,1)S(1)} %get-tuple-element.65), channel_id=1, source_target_pairs={{0,12},{1,13},{2,14},{3,15},{4,8},{5,9},{6,10},{7,11},{8,4},{9,5},... | collective-permute-start | bytes 405512 | tf_op jit(solution)/shard_map/ppermute | solution.py:511
  22.8 23.9 %collective-permute-start.12 = (bf16[528,128]{1,0:T(8,128)(2,1)S(1)}, bf16[528,128]{1,0:T(8,128)(2,1)S(1)}, u32[]{:S(2)}, u32[]{:S(2)}) collective-permute-start(bf16[528,128]{1,0:T(8,128)(2,1)S(1)} %get-tuple-element.66), channel_id=1, source_target_pairs={{0,13},{1,12},{2,15},{3,14},{4,9},{5,8},{6,11},{7,10},{8,5},{9,4},... | collective-permute-start | bytes 405512 | tf_op jit(solution)/shard_map/ppermute | solution.py:511
  25.7 23.3 %collective-permute-start.13 = (bf16[528,128]{1,0:T(8,128)(2,1)S(1)}, bf16[528,128]{1,0:T(8,128)(2,1)S(1)}, u32[]{:S(2)}, u32[]{:S(2)}) collective-permute-start(bf16[528,128]{1,0:T(8,128)(2,1)S(1)} %get-tuple-element.67), channel_id=1, source_target_pairs={{0,14},{1,15},{2,12},{3,13},{4,10},{5,11},{6,8},{7,9},{8,6},{9,7},... | collective-permute-start | bytes 405512 | tf_op jit(solution)/shard_map/ppermute | solution.py:511
  31.4 23.9 %collective-permute-start.14 = (bf16[528,128]{1,0:T(8,128)(2,1)S(1)}, bf16[528,128]{1,0:T(8,128)(2,1)S(1)}, u32[]{:S(2)}, u32[]{:S(2)}) collective-permute-start(bf16[528,128]{1,0:T(8,128)(2,1)S(1)} %get-tuple-element.68), channel_id=1, source_target_pairs={{0,15},{1,14},{2,13},{3,12},{4,11},{5,10},{6,9},{7,8},{8,7},{9,6},... | collective-permute-start | bytes 405512 | tf_op jit(solution)/shard_map/ppermute | solution.py:511
  37.3 18.2 %collective-permute-start.4 = (bf16[528,128]{1,0:T(8,128)(2,1)S(1)}, bf16[528,128]{1,0:T(8,128)(2,1)S(1)}, u32[]{:S(2)}, u32[]{:S(2)}) collective-permute-start(bf16[528,128]{1,0:T(8,128)(2,1)S(1)} %get-tuple-element.58), channel_id=1, source_target_pairs={{0,5},{1,4},{2,7},{3,6},{4,1},{5,0},{6,3},{7,2},{8,13},{9,12},{10,... | collective-permute-start | bytes 405512 | tf_op jit(solution)/shard_map/ppermute | solution.py:511
  40.2 16.3 %collective-permute-start.5 = (bf16[528,128]{1,0:T(8,128)(2,1)S(1)}, bf16[528,128]{1,0:T(8,128)(2,1)S(1)}, u32[]{:S(2)}, u32[]{:S(2)}) collective-permute-start(bf16[528,128]{1,0:T(8,128)(2,1)S(1)} %get-tuple-element.59), channel_id=1, source_target_pairs={{0,6},{1,7},{2,4},{3,5},{4,2},{5,3},{6,0},{7,1},{8,14},{9,15},{10,... | collective-permute-start | bytes 405512 | tf_op jit(solution)/shard_map/ppermute | solution.py:511
  46.8 13.6 %collective-permute-start.3 = (bf16[528,128]{1,0:T(8,128)(2,1)}, bf16[528,128]{1,0:T(8,128)(2,1)S(1)}, u32[]{:S(2)}, u32[]{:S(2)}) collective-permute-start(bf16[528,128]{1,0:T(8,128)(2,1)} %get-tuple-element.57), channel_id=1, source_target_pairs={{0,4},{1,5},{2,6},{3,7},{4,0},{5,1},{6,2},{7,3},{8,12},{9,13},{10,... | collective-permute-start | bytes 405512 | tf_op jit(solution)/shard_map/ppermute | solution.py:511
  49.0 14.4 %collective-permute-start = (bf16[528,128]{1,0:T(8,128)(2,1)}, bf16[528,128]{1,0:T(8,128)(2,1)S(1)}, u32[]{:S(2)}, u32[]{:S(2)}) collective-permute-start(bf16[528,128]{1,0:T(8,128)(2,1)} %get-tuple-element.54), channel_id=1, source_target_pairs={{0,1},{1,0},{2,3},{3,2},{4,5},{5,4},{6,7},{7,6},{8,9},{9,8},{10,11... | collective-permute-start | bytes 405512 | tf_op jit(solution)/shard_map/ppermute | solution.py:511
  55.3 8.7 %collective-permute-start.1 = (bf16[528,128]{1,0:T(8,128)(2,1)}, bf16[528,128]{1,0:T(8,128)(2,1)S(1)}, u32[]{:S(2)}, u32[]{:S(2)}) collective-permute-start(bf16[528,128]{1,0:T(8,128)(2,1)} %get-tuple-element.55), channel_id=1, source_target_pairs={{0,2},{1,3},{2,0},{3,1},{4,6},{5,7},{6,4},{7,5},{8,10},{9,11},{10,... | collective-permute-start | bytes 405512 | tf_op jit(solution)/shard_map/ppermute | solution.py:511
  55.5 11.4 %collective-permute-start.2 = (bf16[528,128]{1,0:T(8,128)(2,1)}, bf16[528,128]{1,0:T(8,128)(2,1)S(1)}, u32[]{:S(2)}, u32[]{:S(2)}) collective-permute-start(bf16[528,128]{1,0:T(8,128)(2,1)} %get-tuple-element.56), channel_id=1, source_target_pairs={{0,3},{1,2},{2,1},{3,0},{4,7},{5,6},{6,5},{7,4},{8,11},{9,10},{10,... | collective-permute-start | bytes 405512 | tf_op jit(solution)/shard_map/ppermute | solution.py:511
  56.5 10.4 %collective-permute-start.6 = (bf16[528,128]{1,0:T(8,128)(2,1)}, bf16[528,128]{1,0:T(8,128)(2,1)S(1)}, u32[]{:S(2)}, u32[]{:S(2)}) collective-permute-start(bf16[528,128]{1,0:T(8,128)(2,1)} %get-tuple-element.60), channel_id=1, source_target_pairs={{0,7},{1,6},{2,5},{3,4},{4,3},{5,2},{6,1},{7,0},{8,15},{9,14},{10,... | collective-permute-start | bytes 405512 | tf_op jit(solution)/shard_map/ppermute | solution.py:511
  59.7 0.7 copy-start.1
  60.4 9.9 %copy-start.3 = (bf16[512,128]{1,0:T(8,128)(2,1)}, bf16[512,128]{1,0:T(8,128)(2,1)S(1)}, u32[]{:S(2)}) copy-start(bf16[512,128]{1,0:T(8,128)(2,1)S(1)} %get-tuple-element.82.refs_28_) | copy-start | bytes 393220
  61.5 0.7 copy-start.5
  69.6 0.7 copy-start.19
  70.3 9.5 %all-to-all-start = ((f32[16,16,128]{2,1,0:T(8,128)}), f32[16,16,128]{2,1,0:T(8,128)S(1)}, u32[]{:S(2)}, u32[]{:S(2)}) async-start(f32[16,16,128]{2,1,0:T(8,128)} %copy-done.19), calls=%async_computation | async-start | bytes 262144 | tf_op jit(solution)/shard_map/all_to_all | solution.py:537
  76.9 0.7 copy-start.11
  77.6 0.6 copy-start.13
  78.9 0.7 copy-start.17
  79.8 0.9 copy-start.2
  80.7 0.9 copy-start.4
  81.6 0.9 copy-start.6
  82.5 0.9 copy-start.8
  83.4 0.9 copy-start.10
  84.3 0.9 copy-start.12
  85.2 0.9 copy-start.14
  86.1 0.9 copy-start.16
  87.0 0.9 copy-start.18
  91.0 19.2 %collective-permute-start.15 = (bf16[512,128]{1,0:T(8,128)(2,1)S(1)}, bf16[512,128]{1,0:T(8,128)(2,1)S(1)}, u32[]{:S(2)}, u32[]{:S(2)}) collective-permute-start(bf16[512,128]{1,0:T(8,128)(2,1)S(1)} %get-tuple-element.86), channel_id=1, source_target_pairs={{0,8},{1,9},{2,10},{3,11},{4,12},{5,13},{6,14},{7,15},{8,0},{9,1},... | collective-permute-start | bytes 393224 | tf_op jit(solution)/shard_map/ppermute | solution.py:511
  93.0 20.1 %collective-permute-start.16 = (bf16[512,128]{1,0:T(8,128)(2,1)S(1)}, bf16[512,128]{1,0:T(8,128)(2,1)S(1)}, u32[]{:S(2)}, u32[]{:S(2)}) collective-permute-start(bf16[512,128]{1,0:T(8,128)(2,1)S(1)} %get-tuple-element.87), channel_id=1, source_target_pairs={{0,9},{1,8},{2,11},{3,10},{4,13},{5,12},{6,15},{7,14},{8,1},{9,0},... | collective-permute-start | bytes 393224 | tf_op jit(solution)/shard_map/ppermute | solution.py:511
  93.8 24.7 %collective-permute-start.18 = (bf16[512,128]{1,0:T(8,128)(2,1)S(1)}, bf16[512,128]{1,0:T(8,128)(2,1)S(1)}, u32[]{:S(2)}, u32[]{:S(2)}) collective-permute-start(bf16[512,128]{1,0:T(8,128)(2,1)S(1)} %get-tuple-element.89), channel_id=1, source_target_pairs={{0,10},{1,11},{2,8},{3,9},{4,14},{5,15},{6,12},{7,13},{8,2},{9,3},... | collective-permute-start | bytes 393224 | tf_op jit(solution)/shard_map/ppermute | solution.py:511
  96.7 27.5 %collective-permute-start.19 = (bf16[512,128]{1,0:T(8,128)(2,1)S(1)}, bf16[512,128]{1,0:T(8,128)(2,1)S(1)}, u32[]{:S(2)}, u32[]{:S(2)}) collective-permute-start(bf16[512,128]{1,0:T(8,128)(2,1)S(1)} %get-tuple-element.90), channel_id=1, source_target_pairs={{0,11},{1,10},{2,9},{3,8},{4,15},{5,14},{6,13},{7,12},{8,3},{9,2},... | collective-permute-start | bytes 393224 | tf_op jit(solution)/shard_map/ppermute | solution.py:511
  97.3 30.8 %collective-permute-start.21 = (bf16[512,128]{1,0:T(8,128)(2,1)S(1)}, bf16[512,128]{1,0:T(8,128)(2,1)S(1)}, u32[]{:S(2)}, u32[]{:S(2)}) collective-permute-start(bf16[512,128]{1,0:T(8,128)(2,1)S(1)} %get-tuple-element.92), channel_id=1, source_target_pairs={{0,12},{1,13},{2,14},{3,15},{4,8},{5,9},{6,10},{7,11},{8,4},{9,5},... | collective-permute-start | bytes 393224 | tf_op jit(solution)/shard_map/ppermute | solution.py:511
  110.2 23.9 %collective-permute-start.22 = (bf16[512,128]{1,0:T(8,128)(2,1)S(1)}, bf16[512,128]{1,0:T(8,128)(2,1)S(1)}, u32[]{:S(2)}, u32[]{:S(2)}) collective-permute-start(bf16[512,128]{1,0:T(8,128)(2,1)S(1)} %get-tuple-element.93), channel_id=1, source_target_pairs={{0,13},{1,12},{2,15},{3,14},{4,9},{5,8},{6,11},{7,10},{8,5},{9,4},... | collective-permute-start | bytes 393224 | tf_op jit(solution)/shard_map/ppermute | solution.py:511
  113.0 23.2 %collective-permute-start.24 = (bf16[512,128]{1,0:T(8,128)(2,1)S(1)}, bf16[512,128]{1,0:T(8,128)(2,1)S(1)}, u32[]{:S(2)}, u32[]{:S(2)}) collective-permute-start(bf16[512,128]{1,0:T(8,128)(2,1)S(1)} %get-tuple-element.95), channel_id=1, source_target_pairs={{0,14},{1,15},{2,12},{3,13},{4,10},{5,11},{6,8},{7,9},{8,6},{9,7},... | collective-permute-start | bytes 393224 | tf_op jit(solution)/shard_map/ppermute | solution.py:511
  118.5 22.7 %collective-permute-start.25 = (bf16[512,128]{1,0:T(8,128)(2,1)S(1)}, bf16[512,128]{1,0:T(8,128)(2,1)S(1)}, u32[]{:S(2)}, u32[]{:S(2)}) collective-permute-start(bf16[512,128]{1,0:T(8,128)(2,1)S(1)} %get-tuple-element.96), channel_id=1, source_target_pairs={{0,15},{1,14},{2,13},{3,12},{4,11},{5,10},{6,9},{7,8},{8,7},{9,6},... | collective-permute-start | bytes 393224 | tf_op jit(solution)/shard_map/ppermute | solution.py:511
  124.3 17.0 %collective-permute-start.17 = (bf16[512,128]{1,0:T(8,128)(2,1)S(1)}, bf16[512,128]{1,0:T(8,128)(2,1)S(1)}, u32[]{:S(2)}, u32[]{:S(2)}) collective-permute-start(bf16[512,128]{1,0:T(8,128)(2,1)S(1)} %get-tuple-element.88), channel_id=1, source_target_pairs={{0,4},{1,5},{2,6},{3,7},{4,0},{5,1},{6,2},{7,3},{8,12},{9,13},{10,... | collective-permute-start | bytes 393224 | tf_op jit(solution)/shard_map/ppermute | solution.py:511
  128.1 14.8 %collective-permute-start.20 = (bf16[512,128]{1,0:T(8,128)(2,1)S(1)}, bf16[512,128]{1,0:T(8,128)(2,1)S(1)}, u32[]{:S(2)}, u32[]{:S(2)}) collective-permute-start(bf16[512,128]{1,0:T(8,128)(2,1)S(1)} %get-tuple-element.91), channel_id=1, source_target_pairs={{0,5},{1,4},{2,7},{3,6},{4,1},{5,0},{6,3},{7,2},{8,13},{9,12},{10,... | collective-permute-start | bytes 393224 | tf_op jit(solution)/shard_map/ppermute | solution.py:511
  134.1 12.4 %collective-permute-start.23 = (bf16[512,128]{1,0:T(8,128)(2,1)S(1)}, bf16[512,128]{1,0:T(8,128)(2,1)S(1)}, u32[]{:S(2)}, u32[]{:S(2)}) collective-permute-start(bf16[512,128]{1,0:T(8,128)(2,1)S(1)} %get-tuple-element.94), channel_id=1, source_target_pairs={{0,6},{1,7},{2,4},{3,5},{4,2},{5,3},{6,0},{7,1},{8,14},{9,15},{10,... | collective-permute-start | bytes 393224 | tf_op jit(solution)/shard_map/ppermute | solution.py:511
  136.3 11.9 %collective-permute-start.26 = (bf16[512,128]{1,0:T(8,128)(2,1)S(1)}, bf16[512,128]{1,0:T(8,128)(2,1)S(1)}, u32[]{:S(2)}, u32[]{:S(2)}) collective-permute-start(bf16[512,128]{1,0:T(8,128)(2,1)S(1)} %get-tuple-element.97), channel_id=1, source_target_pairs={{0,7},{1,6},{2,5},{3,4},{4,3},{5,2},{6,1},{7,0},{8,15},{9,14},{10,... | collective-permute-start | bytes 393224 | tf_op jit(solution)/shard_map/ppermute | solution.py:511
  141.3 6.9 %collective-permute-start.27 = (bf16[512,128]{1,0:T(8,128)(2,1)S(1)}, bf16[512,128]{1,0:T(8,128)(2,1)S(1)}, u32[]{:S(2)}, u32[]{:S(2)}) collective-permute-start(bf16[512,128]{1,0:T(8,128)(2,1)S(1)} %get-tuple-element.98), channel_id=1, source_target_pairs={{0,1},{1,0},{2,3},{3,2},{4,5},{5,4},{6,7},{7,6},{8,9},{9,8},{10,11... | collective-permute-start | bytes 393224 | tf_op jit(solution)/shard_map/ppermute | solution.py:511
  141.3 6.9 %collective-permute-start.28 = (bf16[512,128]{1,0:T(8,128)(2,1)S(1)}, bf16[512,128]{1,0:T(8,128)(2,1)S(1)}, u32[]{:S(2)}, u32[]{:S(2)}) collective-permute-start(bf16[512,128]{1,0:T(8,128)(2,1)S(1)} %get-tuple-element.99), channel_id=1, source_target_pairs={{0,2},{1,3},{2,0},{3,1},{4,6},{5,7},{6,4},{7,5},{8,10},{9,11},{10,... | collective-permute-start | bytes 393224 | tf_op jit(solution)/shard_map/ppermute | solution.py:511
  142.9 7.9 %collective-permute-start.29 = (bf16[512,128]{1,0:T(8,128)(2,1)S(1)}, bf16[512,128]{1,0:T(8,128)(2,1)S(1)}, u32[]{:S(2)}, u32[]{:S(2)}) collective-permute-start(bf16[512,128]{1,0:T(8,128)(2,1)S(1)} %get-tuple-element.100), channel_id=1, source_target_pairs={{0,3},{1,2},{2,1},{3,0},{4,7},{5,6},{6,5},{7,4},{8,11},{9,10},{10,... | collective-permute-start | bytes 393224 | tf_op jit(solution)/shard_map/ppermute | solution.py:511
  (3 other events, 1.9 us)

commit v3 on v1

v3 whole, which is shorter than its diff:
```python
import jax
import jax.numpy as jnp
from jax import lax
from jax.experimental import pallas as pl
from jax.experimental.pallas import tpu as pltpu
from jax.sharding import PartitionSpec as P

GRID_X = 1024
GRID_Y = 1024
NCELL = 1048576
LANES = 128
LINE = GRID_Y // LANES
TILE = 16

prior_scale = 0.25
mass_term = 1.0

F32 = jnp.float32
BF16 = jnp.bfloat16
MIB = 1024 * 1024


def call(body, name, flops=0, moved=0, limit=16, **kwargs):
    return pl.pallas_call(
        body,
        name=name,
        compiler_params=pltpu.CompilerParams(vmem_limit_bytes=limit * MIB),
        cost_estimate=pl.CostEstimate(flops=flops, bytes_accessed=moved, transcendentals=0),
        **kwargs,
    )


IN_VMEM = pl.BlockSpec(memory_space=pltpu.VMEM)
ANYWHERE = pl.BlockSpec(memory_space=pl.ANY)


def split_body(row_ref, out_ref, held, sems):
    slabs, lines, _ = out_ref.shape
    lines -= TILE
    cells = lines * LANES

    def part(slab):
        at = pl.ds(slab * cells, cells)
        return pltpu.make_async_copy(row_ref.at[:, at], held.at[:, at], sems.at[slab])

    def edge(start):
        return held[:, pl.ds(start, GRID_Y)].astype(F32).reshape(LINE, LANES)

    for slab in range(slabs):
        part(slab).start()
    part(0).wait()
    outside = jnp.zeros((LINE, LANES), F32)
    for slab in range(slabs):
        if slab + 1 < slabs:
            part(slab + 1).wait()
        out_ref[slab, :lines, :] = held[:, pl.ds(slab * cells, cells)].reshape(lines, LANES)
        below = edge((slab + 1) * cells) if slab + 1 < slabs else outside
        above = edge(slab * cells - GRID_Y) if slab else outside
        out_ref[slab, lines:, :] = jnp.concatenate([below, above], axis=0).astype(BF16)


def split_row(row, slabs):
    lines = row.shape[1] // slabs // LANES
    return call(
        split_body,
        "split_row",
        moved=6 * row.shape[1],
        limit=60,
        in_specs=[ANYWHERE],
        out_specs=IN_VMEM,
        out_shape=jax.ShapeDtypeStruct((slabs, lines + TILE, LANES), BF16),
        scratch_shapes=[pltpu.VMEM(row.shape, BF16), pltpu.SemaphoreType.DMA((slabs,))],
    )(row)


def join_body(slabs_ref, row_ref, held, sems):
    slabs, lines, _ = slabs_ref.shape
    cells = lines * LANES
    copies = []
    for slab in range(slabs):
        at = pl.ds(slab * cells, cells)
        held[:, at] = slabs_ref[slab].reshape(1, cells)
        copies.append(pltpu.make_async_copy(held.at[:, at], row_ref.at[:, at], sems.at[slab]))
        copies[-1].start()
    for copy in copies:
        copy.wait()


def join_row(slabs):
    count, lines, _ = slabs.shape
    row = jax.ShapeDtypeStruct((1, count * lines * LANES), BF16)
    return call(
        join_body,
        "join_row",
        moved=6 * row.size,
        in_specs=[IN_VMEM],
        out_specs=ANYWHERE,
        out_shape=row,
        scratch_shapes=[pltpu.VMEM(row.shape, BF16), pltpu.SemaphoreType.DMA((count,))],
    )(slabs)


def same_line(total):
    wide = total * TILE
    row = lax.broadcasted_iota(jnp.int32, (wide, wide), 0)
    col = lax.broadcasted_iota(jnp.int32, (wide, wide), 1)
    return row % TILE == col % TILE


def members(total, dtype):
    wide = total * TILE
    row = lax.broadcasted_iota(jnp.int32, (wide, total), 0)
    col = lax.broadcasted_iota(jnp.int32, (wide, total), 1)
    return (row // TILE == col).astype(dtype)


def gram_body(states_ref, out_ref, pairs):
    total = states_ref.shape[0]
    wide = total * TILE
    tiles = min(8, states_ref.shape[1] // TILE - 1)
    steps = (states_ref.shape[1] - TILE) // (tiles * TILE)
    pairs[...] = jnp.zeros_like(pairs)

    def step(i, carry):
        parts = [
            states_ref[:, pl.ds(pl.multiple_of((i * tiles + t) * TILE, TILE), TILE), :].reshape(wide, LANES)
            for t in range(tiles)
        ]
        block = jnp.concatenate(parts, axis=1)
        pairs[...] += lax.dot_general(block, block, (((1,), (1,)), ((), ())), preferred_element_type=F32)
        return carry

    lax.fori_loop(0, steps, step, 0)
    equal = jnp.where(same_line(total), pairs[...], 0.0)
    rows = jnp.sum(equal.reshape(total, TILE, wide), axis=1)
    gram = jnp.dot(rows, members(total, F32), precision=lax.Precision.HIGHEST, preferred_element_type=F32)
    gram = jnp.concatenate([gram, jnp.zeros((total, LANES - total), F32)], axis=1)
    out_ref[...] = jnp.broadcast_to(gram[None], out_ref.shape)


def slab_gram(states, copies):
    total, lines, _ = states.shape
    wide = total * TILE
    return call(
        gram_body,
        "slab_gram",
        flops=2 * wide * wide * LANES * (lines // TILE),
        moved=2 * states.size,
        in_specs=[IN_VMEM],
        out_specs=IN_VMEM,
        out_shape=jax.ShapeDtypeStruct((copies, total, LANES), F32),
        scratch_shapes=[pltpu.VMEM((wide, wide), F32)],
    )(states)


def gradient_body(states_ref, observed_ref, precision_ref, out_ref, observed, precision, sems):
    total, lines, _ = out_ref.shape
    tiles = min(4, lines // TILE)
    block = tiles * TILE
    rows = block // LINE
    steps = lines // block
    group = 4
    shape = (rows, LINE, LANES)
    lane = lax.broadcasted_iota(jnp.int32, (1, LINE, LANES), 2)
    line = lax.broadcasted_iota(jnp.int32, (1, LINE, LANES), 1)
    slab = pl.ds(pl.multiple_of(lax.axis_index("slab") * lines, TILE), lines)
    fetches = [
        pltpu.make_async_copy(observed_ref.at[slab, :], observed, sems.at[0]),
        pltpu.make_async_copy(precision_ref.at[slab, :], precision, sems.at[1]),
    ]
    for fetch in fetches:
        fetch.start()
    for fetch in fetches:
        fetch.wait()

    def step(i, carry):
        at = i // (total // group)
        start = pl.multiple_of(at * block, block)
        before = pl.multiple_of(jnp.where(at == 0, lines, start - TILE), TILE)
        after = pl.multiple_of(start + block, TILE)
        obs = observed[pl.ds(start, block), :].astype(F32).reshape(shape)
        prec = precision[pl.ds(start, block), :].astype(F32).reshape(shape)
        for p in range(group):
            particle = (i % (total // group)) * group + p
            here = states_ref[particle, pl.ds(start, block), :].astype(F32)
            first = states_ref[particle, pl.ds(before, TILE), :].astype(F32)[LINE:]
            last = states_ref[particle, pl.ds(after, TILE), :].astype(F32)[:LINE]
            above = jnp.concatenate([first, here[:-LINE]], axis=0).reshape(shape)
            below = jnp.concatenate([here[LINE:], last], axis=0).reshape(shape)
            field = here.reshape(shape)
            turned = pltpu.roll(field, 1, 2)
            carried = jnp.where(line == 0, 0.0, pltpu.roll(turned, 1, 1))
            left = jnp.where(lane == 0, carried, turned)
            turned = pltpu.roll(field, LANES - 1, 2)
            carried = jnp.where(line == LINE - 1, 0.0, pltpu.roll(turned, LINE - 1, 1))
            right = jnp.where(lane == LANES - 1, carried, turned)
            laplace = (4.0 + mass_term) * field - (below + above + right + left)
            squash = jnp.tanh(field)
            result = prec * (obs - squash) * (1.0 - squash * squash) - prior_scale * laplace
            out_ref[particle, pl.ds(start, block), :] = result.reshape(block, LANES).astype(BF16)
        return carry

    lax.fori_loop(0, steps * (total // group), step, 0)


def slab_gradient(states, observed, precision):
    total, lines, _ = states.shape
    lines -= TILE
    return call(
        gradient_body,
        "slab_gradient",
        flops=30 * states.size,
        moved=4 * states.size,
        in_specs=[IN_VMEM, ANYWHERE, ANYWHERE],
        out_specs=IN_VMEM,
        out_shape=jax.ShapeDtypeStruct((total, lines, LANES), BF16),
        scratch_shapes=[pltpu.VMEM((lines, LANES), BF16)] * 2 + [pltpu.SemaphoreType.DMA((2,))],
    )(states, observed, precision)


def update_body(spread_ref, anneal_ref, step_ref, grams_ref, states_ref, grads_ref, out_ref, mixer, own):
    total, lines, _ = grads_ref.shape
    wide = total * TILE
    spread = spread_ref[...]
    rate = step_ref[...] / total
    coeff = 2.0 * anneal_ref[...] / spread

    gram = jnp.sum(grams_ref[...], axis=0)[:, :total]
    row = lax.broadcasted_iota(jnp.int32, (total, total), 0)
    col = lax.broadcasted_iota(jnp.int32, (total, total), 1)
    diagonal = jnp.where(row == col, gram, 0.0)
    down = jnp.sum(diagonal, axis=1, keepdims=True)
    across = jnp.sum(diagonal, axis=0, keepdims=True)
    kernel = jnp.exp(-(down + across - 2.0 * gram) / (spread * NCELL)).astype(BF16)
    ksum = jnp.sum(kernel.astype(F32), axis=1, keepdims=True)
    member = members(total, BF16)
    half = jnp.dot(member, kernel, preferred_element_type=F32).astype(BF16)
    full = lax.dot_general(half, member, (((1,), (1,)), ((), ())), preferred_element_type=F32)
    mixer[...] = jnp.where(same_line(total), full, 0.0).astype(BF16)
    gain = 1.0 + rate * coeff * ksum
    own[...] = jnp.broadcast_to(gain[:, :, None], (total, TILE, LANES)).reshape(wide, LANES)
    tiles = min(4, lines // TILE)

    def step(i, carry):
        for t in range(tiles):
            at = pl.ds(pl.multiple_of((i * tiles + t) * TILE, TILE), TILE)
            states = states_ref[:, at, :].reshape(wide, LANES)
            grads = grads_ref[:, at, :].reshape(wide, LANES)
            mixed = jnp.dot(mixer[...], jnp.concatenate([grads, states], axis=1), preferred_element_type=F32)
            drive, pulled = mixed[:, :LANES], mixed[:, LANES:]
            new = states.astype(F32) * own[...] + rate * (drive - coeff * pulled)
            out_ref[:, at, :] = new.astype(BF16).reshape(total, TILE, LANES)
        return carry

    lax.fori_loop(0, lines // TILE // tiles, step, 0)


def slab_update(spread, anneal, step_size, grams, states, grads):
    total, lines, _ = grads.shape
    wide = total * TILE
    return call(
        update_body,
        "slab_update",
        flops=4 * wide * wide * LANES * (lines // TILE),
        moved=6 * grads.size,
        in_specs=[IN_VMEM] * 6,
        out_specs=IN_VMEM,
        out_shape=jax.ShapeDtypeStruct(grads.shape, BF16),
        scratch_shapes=[pltpu.VMEM((wide, wide), BF16), pltpu.VMEM((wide, LANES), F32)],
    )(spread.reshape(1, 1), anneal.reshape(1, 1), step_size.reshape(1, 1), grams, states, grads)


def plain_update(spread, anneal, step_size, states, grads):
    total, lines, _ = grads.shape
    flat = states[:, :lines].reshape(total, -1)
    gram = lax.dot_general(flat, flat, (((1,), (1,)), ((), ())), preferred_element_type=F32)
    gram = lax.psum(gram, "slab")
    norms = jnp.diagonal(gram)
    kernel = jnp.exp(-(norms[:, None] + norms[None, :] - 2.0 * gram) / (spread[0] * NCELL)).astype(BF16)
    ksum = jnp.sum(kernel.astype(F32), axis=1)
    drive = jnp.dot(kernel, grads.reshape(total, -1), preferred_element_type=F32)
    pulled = jnp.dot(kernel, flat, preferred_element_type=F32)
    values = flat.astype(F32)
    repel = values * ksum[:, None] - pulled
    coeff = 2.0 * anneal[0] / spread[0]
    new = values + step_size[0] / total * (drive + coeff * repel)
    return new.astype(BF16).reshape(grads.shape)


def on_device(particles, observed, precision, spread, anneal, step_size):
    slabs = lax.axis_size("slab")
    total = particles.shape[0] * slabs
    states = split_row(particles, slabs)
    states = lax.all_to_all(states, "slab", split_axis=0, concat_axis=0, tiled=True)
    obs = observed.reshape(-1, LANES)
    prec = precision.reshape(-1, LANES)
    if total * TILE <= 256:
        grams = slab_gram(states, slabs)
        grams = lax.all_to_all(grams, "slab", split_axis=0, concat_axis=0, tiled=True)
        grads = slab_gradient(states, obs, prec)
        new = slab_update(spread, anneal, step_size, grams, states, grads)
    else:
        grads = slab_gradient(states, obs, prec)
        new = plain_update(spread, anneal, step_size, states, grads)
    new = lax.all_to_all(new, "slab", split_axis=0, concat_axis=0, tiled=True)
    return join_row(new)


def solution(mesh):
    in_specs = (
        P(("groups", "slab"), None),
        P("groups"),
        P("groups"),
        P("groups"),
        P("groups"),
        P("groups"),
    )
    out_specs = P(("groups", "slab"), None)
    return jax.shard_map(
        on_device, mesh=mesh, in_specs=in_specs, out_specs=out_specs, check_vma=False
    )
```

time: 153 us -> 143 us (0.935)
  Pallas kernels: 29.1 us -> 19.1 us
    pallas_call x1, Pallas kernels: 12 us -> 4.86 us  [slab_gradient(): call(gradient_body, 'slab_gradient', flops=30 * states.size, moved=4 * st...]
    unnamed x6 -> x8, local copies, waits for them, and re-layouts: 5.09 us -> 6.08 us
  transfers between devices with their start and end apart: 1 -> 1, of which waited for: 0 -> 0; matrix products, arithmetic and copies ran while one was open for 1% -> 0% of each run, Pallas kernels for 8% -> 3%
where the time goes in v3:
time: 143 us; the launch traced here: 142 us
  blocking collectives  110 us (77%)
  Pallas kernels  19.1 us (13%)
  local copies, waits for them, and re-layouts  6.08 us (4%)
  starting transfers between devices  4.73 us (3%)
  between operations  1.99 us (1%)
    all_to_all x1, blocking collectives, on_device(): lax.all_to_all(states, 'slab', split_axis=0, concat_axis=0, tiled=True)  56.3 us
    all_to_all x1, blocking collectives, on_device(): new = lax.all_to_all(new, 'slab', split_axis=0, concat_axis=0, tiled=True)  53.7 us
    unnamed x8, local copies, waits for them, and re-layouts  6.08 us
    pallas_call x1, Pallas kernels, slab_gradient(): call(gradient_body, 'slab_gradient', flops=30 * states.size, moved=4 * st...  4.86 us
    pallas_call x1, Pallas kernels, split_row(): call(split_body, 'split_row', moved=6 * row.shape[1], limit=60, in_specs=...  4.76 us
    all_to_all x1, starting transfers between devices, on_device(): lax.all_to_all(grams, 'slab', split_axis=0, concat_axis=0, tiled=True)  4.73 us
    pallas_call x1, Pallas kernels, join_row(): call(join_body, 'join_row', moved=6 * row.size, in_specs=[IN_VMEM], out_s...  4.22 us
    pallas_call x1, Pallas kernels, slab_update(): call(update_body, 'slab_update', flops=4 * wide * wide * LANES * (lines /...  3.03 us
  transfers between devices with their start and end apart: 1, of which 0 were waited for; matrix products, arithmetic and copies ran while one was open for 0% of the time, Pallas kernels for 3%

profile of v3, /device:TPU:9, one launch (start us, length us, event | category | flops | bytes accessed | tf_op | source)
XLA Modules:
  0.0 142.0 jit_solution(8472555126279367950)
XLA Ops:
  0.0 4.8 %split_row.1 = bf16[16,528,128]{2,1,0:T(8,128)(2,1)} custom-call(bf16[1,1048576]{1,0:T(2,128)(2,1)} %row_ref.1), custom_call_target="tpu_custom_call" | custom-call | bytes 6291456 | tf_op jit(solution)/shard_map/split_row/pallas_call | solution.py:64
  4.8 56.3 %all_to_all.15.states_ref = bf16[16,528,128]{2,1,0:T(8,128)(2,1)S(1)} all-to-all(bf16[16,528,128]{2,1,0:T(8,128)(2,1)} %split_row.1), channel_id=1, replica_groups=mesh['groups'=2,'slab'=16] {'slab'}, dimensions={0} | all-to-all | bytes 4325376 | tf_op jit(solution)/shard_map/all_to_all | solution.py:294
  61.1 2.3 %slab_gram.1 = f32[16,16,128]{2,1,0:T(8,128)} custom-call(bf16[16,528,128]{2,1,0:T(8,128)(2,1)S(1)} %all_to_all.15.states_ref), custom_call_target="tpu_custom_call" | custom-call | flops 553648128 | bytes 2162688 | tf_op jit(solution)/shard_map/slab_gram/pallas_call | solution.py:144
  63.3 4.7 %all-to-all-start.1 = ((f32[16,16,128]{2,1,0:T(8,128)}), f32[16,16,128]{2,1,0:T(8,128)S(1)}, u32[]{:S(2)}, u32[]{:S(2)}) async-start(f32[16,16,128]{2,1,0:T(8,128)} %slab_gram.1), calls=%async_computation.1 | async-start | bytes 262144 | tf_op jit(solution)/shard_map/all_to_all | solution.py:299
  70.0 0.0 copy-start.2
  70.0 1.6 %copy-done.2 = bf16[1048576]{0:T(1024)(128)(2,1)S(1)} copy-done((bf16[1048576]{0:T(1024)(128)(2,1)S(1)}, bf16[1048576]{0:T(1024)(128)(2,1)}, u32[]{:S(2)}) %copy-start.2) | copy-done | bytes 2097176
  71.6 0.0 copy-start.3
  71.6 1.6 %copy-done.3 = bf16[1048576]{0:T(1024)(128)(2,1)S(1)} copy-done((bf16[1048576]{0:T(1024)(128)(2,1)S(1)}, bf16[1048576]{0:T(1024)(128)(2,1)}, u32[]{:S(2)}) %copy-start.3) | copy-done | bytes 2097176
  73.2 4.9 %slab_gradient.1.grads_ref = bf16[16,512,128]{2,1,0:T(8,128)(2,1)S(1)} custom-call(bf16[16,528,128]{2,1,0:T(8,128)(2,1)S(1)} %all_to_all.15.states_ref, bf16[8192,128]{1,0:T(8,128)(2,1)S(1)} %bitcast.8, bf16[8192,128]{1,0:T(8,128)(2,1)S(1)} %bitcast.9), custom_call_target="tpu_custom_call" | custom-call | flops 32440320 | bytes 4325376 | tf_op jit(solution)/shard_map/slab_gradient/pallas_call | solution.py:209
  78.1 0.0 copy-start
  78.1 1.3 copy-done
  79.4 0.0 all-to-all-done.1.grams_ref
  79.4 0.0 copy-start.1
  79.4 1.6 %copy-done.1 = bf16[16,512,128]{2,1,0:T(8,128)(2,1)S(1)} copy-done((bf16[16,512,128]{2,1,0:T(8,128)(2,1)S(1)}, bf16[16,512,128]{2,1,0:T(8,128)(2,1)}, u32[]{:S(2)}) %copy-start.1) | copy-done | bytes 2097176
  81.0 3.0 %slab_update.1 = bf16[16,512,128]{2,1,0:T(8,128)(2,1)S(1)} custom-call(f32[1,1]{1,0:T(1,128)} %bitcast.5.spread_ref, f32[1,1]{1,0:T(1,128)} %bitcast.6.anneal_ref, f32[1,1]{1,0:T(1,128)} %bitcast.7.step_ref, f32[16,16,128]{2,1,0:T(8,128)S(1)} %all-to-all-done.1.grams_ref, bf16[16,528,128]{2,1,0:T(8,128)(2,1)S(1)} %all_to_all.15.states_ref, ...), custom_call_target="tpu_custom_call" | custom-call | flops 1073741824 | bytes 6291456 | tf_op jit(solution)/shard_map/slab_update/pallas_call | solution.py:261
  84.0 53.7 %all_to_all.16.slabs_ref = bf16[16,512,128]{2,1,0:T(8,128)(2,1)S(1)} all-to-all(bf16[16,512,128]{2,1,0:T(8,128)(2,1)S(1)} %slab_update.1), channel_id=1, replica_groups=mesh['groups'=2,'slab'=16] {'slab'}, dimensions={0} | all-to-all | bytes 4194304 | tf_op jit(solution)/shard_map/all_to_all | solution.py:305
  137.7 4.2 %join_row.1 = bf16[1,1048576]{1,0:T(2,128)(2,1)} custom-call(bf16[16,512,128]{2,1,0:T(8,128)(2,1)S(1)} %all_to_all.16.slabs_ref), custom_call_target="tpu_custom_call" | custom-call | bytes 6291456 | tf_op jit(solution)/shard_map/join_row/pallas_call | solution.py:92
Async XLA Ops:
  63.3 16.1 %all-to-all-start.1 = ((f32[16,16,128]{2,1,0:T(8,128)}), f32[16,16,128]{2,1,0:T(8,128)S(1)}, u32[]{:S(2)}, u32[]{:S(2)}) async-start(f32[16,16,128]{2,1,0:T(8,128)} %slab_gram.1), calls=%async_computation.1 | async-start | bytes 262144 | tf_op jit(solution)/shard_map/all_to_all | solution.py:299
  70.0 1.6 %copy-start.2 = (bf16[1048576]{0:T(1024)(128)(2,1)S(1)}, bf16[1048576]{0:T(1024)(128)(2,1)}, u32[]{:S(2)}) copy-start(bf16[1048576]{0:T(1024)(128)(2,1)} %param.7) | copy-start | bytes 6291460
  71.6 1.6 %copy-start.3 = (bf16[1048576]{0:T(1024)(128)(2,1)S(1)}, bf16[1048576]{0:T(1024)(128)(2,1)}, u32[]{:S(2)}) copy-start(bf16[1048576]{0:T(1024)(128)(2,1)} %param.8) | copy-start | bytes 6291460
  78.1 1.3 copy-start
  79.4 1.6 %copy-start.1 = (bf16[16,512,128]{2,1,0:T(8,128)(2,1)S(1)}, bf16[16,512,128]{2,1,0:T(8,128)(2,1)}, u32[]{:S(2)}) copy-start(bf16[16,512,128]{2,1,0:T(8,128)(2,1)} %copy-done) | copy-start | bytes 6291460

commit v4 on v3

v4 whole, which is shorter than its diff:
```python
import functools

import jax
import jax.numpy as jnp
from jax import lax
from jax.experimental import pallas as pl
from jax.experimental.pallas import tpu as pltpu
from jax.sharding import PartitionSpec as P

GRID_X = 1024
GRID_Y = 1024
NCELL = 1048576
LANES = 128
LINE = GRID_Y // LANES
TILE = 16

prior_scale = 0.25
mass_term = 1.0

F32 = jnp.float32
BF16 = jnp.bfloat16
MIB = 1024 * 1024


def call(body, name, flops=0, moved=0, limit=16, **kwargs):
    return pl.pallas_call(
        body,
        name=name,
        compiler_params=pltpu.CompilerParams(vmem_limit_bytes=limit * MIB),
        cost_estimate=pl.CostEstimate(flops=flops, bytes_accessed=moved, transcendentals=0),
        **kwargs,
    )


IN_VMEM = pl.BlockSpec(memory_space=pltpu.VMEM)
IN_HBM = pl.BlockSpec(memory_space=pltpu.HBM)
BLOCK = 4 * TILE


def cuts(lines):
    if lines % (8 * BLOCK):
        return lines, lines
    return lines * 3 // 4, lines * 3 // 4 - BLOCK


def split_body(lines, begin, rim, fields, numbers, row_ref, *refs):
    field_refs, number_refs = refs[:fields], refs[fields : fields + numbers]
    out_ref, *slab_refs, rows_ref = refs[-7 - fields : -5]
    held, edges, sems, edge_sems, field_sems = refs[-5:]
    for k, number_ref in enumerate(number_refs):
        rows_ref[k : k + 1, :] = jnp.broadcast_to(number_ref[...].reshape(1, 1), (1, LANES))
    slabs, count, _ = out_ref.shape
    count -= TILE * rim
    size = count * LANES
    cells = lines * LANES

    def part(slab):
        source = row_ref.at[:, pl.ds(slab * cells + begin * LANES, size)]
        return pltpu.make_async_copy(source, held.at[:, pl.ds(slab * size, size)], sems.at[slab])

    def edge(slab):
        source = row_ref.at[:, pl.ds(slab * cells - GRID_Y, GRID_Y)]
        return pltpu.make_async_copy(source, edges.at[:, pl.ds(slab * GRID_Y, GRID_Y)], edge_sems.at[slab])

    def grid_row(ref, start):
        return ref[:, pl.ds(start, GRID_Y)].astype(F32).reshape(LINE, LANES)

    for slab in range(slabs):
        part(slab).start()
        if rim and slab:
            edge(slab).start()
    mine = pl.ds(pl.multiple_of(lax.axis_index("slab") * lines, TILE), lines)
    fetches = [
        pltpu.make_async_copy(source.at[mine, :], target, field_sems.at[k])
        for k, (source, target) in enumerate(zip(field_refs, slab_refs))
    ]
    for fetch in fetches:
        fetch.start()
    part(0).wait()
    outside = jnp.zeros((LINE, LANES), F32)
    for slab in range(slabs):
        if slab + 1 < slabs:
            part(slab + 1).wait()
        out_ref[slab, :count, :] = held[:, pl.ds(slab * size, size)].reshape(count, LANES)
        if rim:
            if slab:
                edge(slab).wait()
            below = grid_row(held, (slab + 1) * size) if slab + 1 < slabs else outside
            above = grid_row(edges, slab * GRID_Y) if slab else outside
            out_ref[slab, count:, :] = jnp.concatenate([below, above], axis=0).astype(BF16)
    for fetch in fetches:
        fetch.wait()


def split_row(row, slabs, begin, end, rim, fields, numbers, earlier):
    lines = row.shape[1] // slabs // LANES
    count = end - begin
    return call(
        functools.partial(split_body, lines, begin, rim, len(fields), len(numbers)),
        "split_row",
        moved=6 * slabs * count * LANES,
        limit=60,
        in_specs=[IN_HBM] * (1 + len(fields)) + [IN_VMEM] * len(numbers) + [IN_HBM] * len(earlier),
        out_specs=[IN_VMEM] * (2 + len(fields)),
        out_shape=[jax.ShapeDtypeStruct((slabs, count + TILE * rim, LANES), BF16)]
        + [jax.ShapeDtypeStruct((lines, LANES), BF16)] * len(fields)
        + [jax.ShapeDtypeStruct((8, LANES), F32)],
        scratch_shapes=[
            pltpu.VMEM((1, slabs * count * LANES), BF16),
            pltpu.VMEM((1, slabs * GRID_Y), BF16),
            pltpu.SemaphoreType.DMA((slabs,)),
            pltpu.SemaphoreType.DMA((slabs,)),
            pltpu.SemaphoreType.DMA((2,)),
        ],
    )(row, *fields, *numbers, *earlier)


def join_body(lines, begin, slabs_ref, *refs):
    row_ref, held, sems = refs[-3:]
    slabs, count, _ = slabs_ref.shape
    size = count * LANES
    copies = []
    for slab in range(slabs):
        at = pl.ds(slab * size, size)
        held[:, at] = slabs_ref[slab].reshape(1, size)
        target = row_ref.at[:, pl.ds((slab * lines + begin) * LANES, size)]
        copies.append(pltpu.make_async_copy(held.at[:, at], target, sems.at[slab]))
        copies[-1].start()
    for copy in copies:
        copy.wait()


def join_row(slabs, lines, begin, row):
    total, count, _ = slabs.shape
    begun = [] if row is None else [row]
    return call(
        functools.partial(join_body, lines, begin),
        "join_row",
        moved=6 * slabs.size,
        in_specs=[IN_VMEM] + [IN_HBM] * len(begun),
        out_specs=IN_HBM,
        out_shape=jax.ShapeDtypeStruct((1, total * lines * LANES), BF16),
        input_output_aliases={1: 0} if begun else {},
        scratch_shapes=[pltpu.VMEM((1, slabs.size), BF16), pltpu.SemaphoreType.DMA((total,))],
    )(slabs, *begun)


def same_line(total):
    wide = total * TILE
    row = lax.broadcasted_iota(jnp.int32, (wide, wide), 0)
    col = lax.broadcasted_iota(jnp.int32, (wide, wide), 1)
    return row % TILE == col % TILE


def members(total, dtype):
    wide = total * TILE
    row = lax.broadcasted_iota(jnp.int32, (wide, total), 0)
    col = lax.broadcasted_iota(jnp.int32, (wide, total), 1)
    return (row // TILE == col).astype(dtype)


def gram_body(steps, tiles, parts, states_ref, *refs):
    out_ref, pairs = refs[-2:]
    total = states_ref.shape[0]
    wide = total * TILE
    pairs[...] = jnp.zeros_like(pairs)

    def step(i, carry):
        parts = [
            states_ref[:, pl.ds(pl.multiple_of((i * tiles + t) * TILE, TILE), TILE), :].reshape(wide, LANES)
            for t in range(tiles)
        ]
        block = jnp.concatenate(parts, axis=1)
        pairs[...] += lax.dot_general(block, block, (((1,), (1,)), ((), ())), preferred_element_type=F32)
        return carry

    lax.fori_loop(0, steps, step, 0)
    equal = jnp.where(same_line(total), pairs[...], 0.0)
    rows = jnp.sum(equal.reshape(total, TILE, wide), axis=1)
    gram = jnp.dot(rows, members(total, F32), precision=lax.Precision.HIGHEST, preferred_element_type=F32)
    gram = jnp.concatenate([gram, jnp.zeros((total, LANES - total), F32)], axis=1)
    for part_ref in refs[:parts]:
        gram += part_ref[0]
    out_ref[...] = jnp.broadcast_to(gram[None], out_ref.shape)


def slab_gram(states, lines, copies, parts, earlier):
    total = states.shape[0]
    wide = total * TILE
    tiles = min(8, lines // TILE)
    return call(
        functools.partial(gram_body, lines // TILE // tiles, tiles, len(parts)),
        "slab_gram",
        flops=2 * wide * wide * LANES * (lines // TILE),
        moved=2 * states.size,
        in_specs=[IN_VMEM] * (1 + len(parts)) + [IN_HBM] * len(earlier),
        out_specs=IN_VMEM,
        out_shape=jax.ShapeDtypeStruct((copies, total, LANES), F32),
        scratch_shapes=[pltpu.VMEM((wide, wide), F32)],
    )(states, *parts, *earlier)


def gradient_body(lines, begin, end, parts, *refs):
    observed, precision, out_ref, grads, sems = refs[parts:]
    total = grads.shape[0]
    first = refs[0].shape[1] - TILE
    rows = BLOCK // LINE
    group = 4
    shape = (rows, LINE, LANES)
    lane = lax.broadcasted_iota(jnp.int32, (1, LINE, LANES), 2)
    line = lax.broadcasted_iota(jnp.int32, (1, LINE, LANES), 1)

    def load(particle, at, count):
        ref, at = (refs[0], at) if at < first else (refs[1], at - first)
        return ref[particle, at : at + count, :].astype(F32)

    def rim(particle):
        return refs[0][particle, first:, :].astype(F32)

    stores = []
    for k, at in enumerate(range(begin, end, BLOCK)):
        mine = slice(at - begin, at - begin + BLOCK)
        obs = observed[at : at + BLOCK, :].astype(F32).reshape(shape)
        prec = precision[at : at + BLOCK, :].astype(F32).reshape(shape)

        def step(i, carry):
            for p in range(group):
                particle = i * group + p
                here = load(particle, at, BLOCK)
                before = load(particle, at - TILE, TILE) if at else rim(particle)
                after = load(particle, at + BLOCK, TILE) if at + BLOCK < lines else rim(particle)
                above = jnp.concatenate([before[LINE:], here[:-LINE]], axis=0).reshape(shape)
                below = jnp.concatenate([here[LINE:], after[:LINE]], axis=0).reshape(shape)
                field = here.reshape(shape)
                turned = pltpu.roll(field, 1, 2)
                carried = jnp.where(line == 0, 0.0, pltpu.roll(turned, 1, 1))
                left = jnp.where(lane == 0, carried, turned)
                turned = pltpu.roll(field, LANES - 1, 2)
                carried = jnp.where(line == LINE - 1, 0.0, pltpu.roll(turned, LINE - 1, 1))
                right = jnp.where(lane == LANES - 1, carried, turned)
                laplace = (4.0 + mass_term) * field - (below + above + right + left)
                squash = jnp.tanh(field)
                result = prec * (obs - squash) * (1.0 - squash * squash) - prior_scale * laplace
                grads[particle, mine, :] = result.reshape(BLOCK, LANES).astype(BF16)
            return carry

        lax.fori_loop(0, total // group, step, 0)
        stores.append(pltpu.make_async_copy(grads.at[:, mine, :], out_ref.at[:, mine, :], sems.at[k]))
        stores[-1].start()
    for store in stores:
        store.wait()


def slab_gradient(parts, observed, precision, lines, begin, end):
    total = parts[0].shape[0]
    count = end - begin
    out = jax.ShapeDtypeStruct((total, count, LANES), BF16)
    return call(
        functools.partial(gradient_body, lines, begin, end, len(parts)),
        "slab_gradient",
        flops=30 * out.size,
        moved=8 * out.size,
        in_specs=[IN_VMEM] * (len(parts) + 2),
        out_specs=IN_HBM,
        out_shape=out,
        scratch_shapes=[pltpu.VMEM(out.shape, BF16), pltpu.SemaphoreType.DMA((count // BLOCK,))],
    )(*parts, observed, precision)


def update_body(begin, end, parts, *refs):
    states_refs, refs = refs[:parts], refs[parts:]
    scalars_ref, grams_ref, grads_ref = refs[:3]
    out_ref, grads, mixer, own, sem = refs[-5:]
    total = out_ref.shape[0]
    wide = total * TILE
    fetch = pltpu.make_async_copy(grads_ref, grads, sem)
    fetch.start()
    gram = jnp.sum(grams_ref[...], axis=0)[:, :total]
    row = lax.broadcasted_iota(jnp.int32, (total, total), 0)
    col = lax.broadcasted_iota(jnp.int32, (total, total), 1)
    diagonal = jnp.where(row == col, gram, 0.0)
    down = jnp.sum(diagonal, axis=1, keepdims=True)
    across = jnp.sum(diagonal, axis=0, keepdims=True)
    member = members(total, BF16)
    spread, anneal, step_size = (scalars_ref[k : k + 1, :1] for k in range(3))
    rate = step_size / total
    coeff = 2.0 * anneal / spread
    kernel = jnp.exp(-(down + across - 2.0 * gram) / (spread * NCELL)).astype(BF16)
    ksum = jnp.sum(kernel.astype(F32), axis=1, keepdims=True)
    half = jnp.dot(member, kernel, preferred_element_type=F32).astype(BF16)
    full = lax.dot_general(half, member, (((1,), (1,)), ((), ())), preferred_element_type=F32)
    mixer[...] = jnp.where(same_line(total), full, 0.0).astype(BF16)
    gain = 1.0 + rate * coeff * ksum
    own[...] = jnp.broadcast_to(gain[:, :, None], (total, TILE, LANES)).reshape(wide, LANES)
    fetch.wait()

    done = 0
    for part, states_ref in enumerate(states_refs):
        have = states_ref.shape[1] - (0 if part else TILE)
        low = max(begin - done, 0)
        high = min(end - done, have)
        into = done - begin
        done += have

        def step(i, carry):
            for t in range(BLOCK // TILE):
                at = pl.multiple_of(i * BLOCK + t * TILE, TILE)
                there = pl.ds(pl.multiple_of(at + into, TILE), TILE)
                states = states_ref[:, pl.ds(at, TILE), :].reshape(wide, LANES)
                both = jnp.concatenate([grads[:, there, :].reshape(wide, LANES), states], axis=1)
                mixed = jnp.dot(mixer[...], both, preferred_element_type=F32)
                drive, pulled = mixed[:, :LANES], mixed[:, LANES:]
                new = states.astype(F32) * own[...] + rate * (drive - coeff * pulled)
                out_ref[:, there, :] = new.astype(BF16).reshape(total, TILE, LANES)
            return carry

        lax.fori_loop(low // BLOCK, high // BLOCK, step, 0)


def slab_update(scalars, grams, parts, grads, begin, end, earlier):
    total, count, _ = grads.shape
    wide = total * TILE
    return call(
        functools.partial(update_body, begin, end, len(parts)),
        "slab_update",
        flops=4 * wide * wide * LANES * (count // TILE),
        moved=6 * grads.size,
        in_specs=[IN_VMEM] * len(parts)
        + [IN_VMEM, IN_VMEM, IN_HBM]
        + [IN_HBM] * len(earlier),
        out_specs=IN_VMEM,
        out_shape=jax.ShapeDtypeStruct(grads.shape, BF16),
        scratch_shapes=[
            pltpu.VMEM(grads.shape, BF16),
            pltpu.VMEM((wide, wide), BF16),
            pltpu.VMEM((wide, LANES), F32),
            pltpu.SemaphoreType.DMA,
        ],
    )(*parts, scalars, grams, grads, *earlier)


def plain_update(spread, anneal, step_size, states, grads):
    total, lines, _ = grads.shape
    flat = states[:, :lines].reshape(total, -1)
    gram = lax.dot_general(flat, flat, (((1,), (1,)), ((), ())), preferred_element_type=F32)
    gram = lax.psum(gram, "slab")
    norms = jnp.diagonal(gram)
    kernel = jnp.exp(-(norms[:, None] + norms[None, :] - 2.0 * gram) / (spread[0] * NCELL)).astype(BF16)
    ksum = jnp.sum(kernel.astype(F32), axis=1)
    drive = jnp.dot(kernel, grads.reshape(total, -1), preferred_element_type=F32)
    pulled = jnp.dot(kernel, flat, preferred_element_type=F32)
    values = flat.astype(F32)
    repel = values * ksum[:, None] - pulled
    coeff = 2.0 * anneal[0] / spread[0]
    new = values + step_size[0] / total * (drive + coeff * repel)
    return new.astype(BF16).reshape(grads.shape)


def swap(slabs):
    return lax.all_to_all(slabs, "slab", split_axis=0, concat_axis=0, tiled=True)


def on_device(particles, observed, precision, spread, anneal, step_size):
    slabs = lax.axis_size("slab")
    total = particles.shape[0] * slabs
    lines = NCELL // slabs // LANES
    sent, begun = cuts(lines)
    fields = [observed.reshape(-1, LANES), precision.reshape(-1, LANES)]
    numbers = [spread, anneal, step_size]
    first, obs, prec, scalars = split_row(particles, slabs, 0, sent, True, fields, numbers, [])
    parts = [swap(first)]
    if sent < lines:
        parts += [swap(split_row(particles, slabs, sent, lines, False, [], [], [scalars])[0])]
    if total * TILE > 256:
        grads = slab_gradient(parts, obs, prec, lines, 0, lines)
        states = jnp.concatenate([parts[0][:, :sent]] + parts[1:], axis=1)
        new = plain_update(spread, anneal, step_size, states, grads)
        return join_row(swap(new), lines, 0, None)
    if sent == lines:
        grads = slab_gradient(parts, obs, prec, lines, 0, lines)
        grams = swap(slab_gram(parts[0], lines, slabs, [], []))
        new = slab_update(scalars, grams, parts, grads, 0, lines, [])
        return join_row(swap(new), lines, 0, None)
    gram = slab_gram(parts[0], sent, 1, [], [])
    early = slab_gradient(parts[:1], obs, prec, lines, 0, begun)
    grams = swap(slab_gram(parts[1], lines - sent, slabs, [gram], [early]))
    late = slab_gradient(parts, obs, prec, lines, begun, lines)
    new = slab_update(scalars, grams, parts[:1], early, 0, begun, [])
    rest = slab_update(scalars, grams, parts, late, begun, lines, [new])
    row = join_row(swap(new), lines, 0, None)
    return join_row(swap(rest), lines, begun, row)


def solution(mesh):
    in_specs = (
        P(("groups", "slab"), None),
        P("groups"),
        P("groups"),
        P("groups"),
        P("groups"),
        P("groups"),
    )
    out_specs = P(("groups", "slab"), None)
    return jax.shard_map(
        on_device, mesh=mesh, in_specs=in_specs, out_specs=out_specs, check_vma=False
    )
```

time: 143 us -> 148 us (1.035)
  blocking collectives: 110 us -> 10.1 us
  waiting for transfers between devices: 0.01 us -> 83.7 us
  starting transfers between devices: 4.73 us -> 24 us
  Pallas kernels: 19.1 us -> 24.3 us
  local copies, waits for them, and re-layouts: 6.08 us -> 3.53 us
    all_to_all x2 -> x1, blocking collectives: 110 us -> 10.1 us  [swap(): lax.all_to_all(slabs, 'slab', split_axis=0, concat_axis=0, tiled=True)]
    all_to_all x1 -> x4, waiting for transfers between devices: 0.01 us -> 83.7 us  [swap(): lax.all_to_all(slabs, 'slab', split_axis=0, concat_axis=0, tiled=True)]
    all_to_all x1 -> x4, starting transfers between devices: 4.73 us -> 24 us  [swap(): lax.all_to_all(slabs, 'slab', split_axis=0, concat_axis=0, tiled=True)]
    pallas_call x5 -> x10, Pallas kernels: 19.1 us -> 24.3 us  [the longest x2 6.98 us: split_row(): call(functools.partial(split_body, lines, begin, rim, len(fields), len(nu...]
    unnamed x8 -> x18, local copies, waits for them, and re-layouts: 6.08 us -> 3.53 us
  transfers between devices with their start and end apart: 1 -> 4, of which waited for: 0 -> 4; matrix products, arithmetic and copies ran while one was open for 0% -> 0% of each run, Pallas kernels for 3% -> 10%
where the time goes in v4:
time: 148 us
  waiting for transfers between devices  83.7 us (57%)
  Pallas kernels  24.3 us (16%)
  starting transfers between devices  24 us (16%)
  blocking collectives  10.1 us (7%)
  local copies, waits for them, and re-layouts  3.53 us (2%)
  between operations  2.08 us (1%)
    all_to_all x4, waiting for transfers between devices, swap(): lax.all_to_all(slabs, 'slab', split_axis=0, concat_axis=0, tiled=True)  83.7 us
    all_to_all x4, starting transfers between devices, swap(): lax.all_to_all(slabs, 'slab', split_axis=0, concat_axis=0, tiled=True)  24 us
    all_to_all x1, blocking collectives, swap(): lax.all_to_all(slabs, 'slab', split_axis=0, concat_axis=0, tiled=True)  10.1 us
    pallas_call x2, Pallas kernels, split_row(): call(functools.partial(split_body, lines, begin, rim, len(fields), len(nu...  6.98 us
    pallas_call x2, Pallas kernels, join_row(): call(functools.partial(join_body, lines, begin), 'join_row', moved=6 * sl...  6.29 us
    pallas_call x2, Pallas kernels, slab_gradient(): call(functools.partial(gradient_body, lines, begin, end, len(parts)), 'sl...  4.72 us
    pallas_call x2, Pallas kernels, slab_update(): call(functools.partial(update_body, begin, end, len(parts)), 'slab_update...  4.49 us
    unnamed x18, local copies, waits for them, and re-layouts  3.53 us
  transfers between devices with their start and end apart: 4, of which 4 were waited for; matrix products, arithmetic and copies ran while one was open for 0% of the time, Pallas kernels for 10%

profile of v4, /device:TPU:9, one launch (start us, length us, event | category | flops | bytes accessed | tf_op | source)
XLA Modules:
  0.0 147.8 jit_solution(1612250417091454306)
XLA Ops:
  1.9 4.4 %split_row.2 = (bf16[16,400,128]{2,1,0:T(8,128)(2,1)}, bf16[512,128]{1,0:T(8,128)(2,1)}, bf16[512,128]{1,0:T(8,128)(2,1)}, f32[8,128]{1,0:T(8,128)}) custom-call(bf16[1,1048576]{1,0:T(2,128)(2,1)} %row_ref.3, bf16[8192,128]{1,0:T(8,128)(2,1)} %bitcast.2, bf16[8192,128]{1,0:T(8,128)(2,1)} %bitcast.3, f32[1]{0:T(128)S(6)} %copy.9.refs_2_, f32[1]{0:T(128)S(6)} %copy.10.refs_3_, ...), custom_call_target="tpu_custom_call" | custom-call | bytes 4718592 | tf_op jit(solution)/shard_map/split_row/pallas_call | solution.py:98
  6.3 6.6 %all-to-all-start = ((bf16[16,400,128]{2,1,0:T(8,128)(2,1)}), bf16[16,400,128]{2,1,0:T(8,128)(2,1)S(1)}, u32[]{:S(2)}, u32[]{:S(2)}) async-start(bf16[16,400,128]{2,1,0:T(8,128)(2,1)} %get-tuple-element.10), calls=%async_computation | async-start | bytes 3276800 | tf_op jit(solution)/shard_map/all_to_all | solution.py:360
  13.0 2.6 %split_row.3 = (bf16[16,128,128]{2,1,0:T(8,128)(2,1)}, f32[8,128]{1,0:T(8,128)}) custom-call(bf16[1,1048576]{1,0:T(2,128)(2,1)} %row_ref.3, f32[8,128]{1,0:T(8,128)} %get-tuple-element.11.refs_0_.refs_1_.refs_2_), custom_call_target="tpu_custom_call" | custom-call | bytes 1572864 | tf_op jit(solution)/shard_map/split_row/pallas_call | solution.py:98
  15.6 34.2 %all-to-all-done.states_ref.refs_0_ = bf16[16,400,128]{2,1,0:T(8,128)(2,1)S(1)} async-done(((bf16[16,400,128]{2,1,0:T(8,128)(2,1)}), bf16[16,400,128]{2,1,0:T(8,128)(2,1)S(1)}, u32[]{:S(2)}, u32[]{:S(2)}) %all-to-all-start) | async-done | bytes 1638432 | tf_op jit(solution)/shard_map/all_to_all | solution.py:360
  49.7 5.7 %all-to-all-start.1 = ((bf16[16,128,128]{2,1,0:T(8,128)(2,1)}), bf16[16,128,128]{2,1,0:T(8,128)(2,1)S(1)}, u32[]{:S(2)}, u32[]{:S(2)}) async-start(bf16[16,128,128]{2,1,0:T(8,128)(2,1)} %get-tuple-element.12), calls=%async_computation.1 | async-start | bytes 1048576 | tf_op jit(solution)/shard_map/all_to_all | solution.py:360
  55.4 0.0 copy-start.4
  55.5 0.9 copy-done.4
  56.4 0.0 copy-start.6
  56.4 0.9 copy-done.6
  57.3 2.9 %slab_gradient.2.refs_1_.refs_3_ = bf16[16,320,128]{2,1,0:T(8,128)(2,1)S(1)} custom-call(bf16[16,400,128]{2,1,0:T(8,128)(2,1)S(1)} %all-to-all-done.states_ref.refs_0_, bf16[512,128]{1,0:T(8,128)(2,1)S(1)} %copy-done.4, bf16[512,128]{1,0:T(8,128)(2,1)S(1)} %copy-done.6), custom_call_target="tpu_custom_call" | custom-call | flops 19660800 | bytes 5242880 | tf_op jit(solution)/shard_map/slab_gradient/pallas_call | solution.py:258
  60.2 0.0 copy-start.8
  60.2 1.3 slab_gram.2.refs_0_
  61.5 8.1 %all-to-all-done.1.states_ref.refs_1_ = bf16[16,128,128]{2,1,0:T(8,128)(2,1)S(1)} async-done(((bf16[16,128,128]{2,1,0:T(8,128)(2,1)}), bf16[16,128,128]{2,1,0:T(8,128)(2,1)S(1)}, u32[]{:S(2)}, u32[]{:S(2)}) %all-to-all-start.1) | async-done | bytes 524320 | tf_op jit(solution)/shard_map/all_to_all | solution.py:360
  69.6 0.6 slab_gram.3
  70.2 10.1 %all_to_all.25.refs_2_.refs_3_ = f32[16,16,128]{2,1,0:T(8,128)S(1)} all-to-all(f32[16,16,128]{2,1,0:T(8,128)S(1)} %slab_gram.3), channel_id=1, replica_groups=mesh['groups'=2,'slab'=16] {'slab'}, dimensions={0} | all-to-all | bytes 262144 | tf_op jit(solution)/shard_map/all_to_all | solution.py:360
  80.3 0.0 copy-done.8
  80.3 2.2 %slab_update.2.refs_5_ = bf16[16,320,128]{2,1,0:T(8,128)(2,1)S(1)} custom-call(bf16[16,400,128]{2,1,0:T(8,128)(2,1)S(1)} %all-to-all-done.states_ref.refs_0_, f32[8,128]{1,0:T(8,128)S(1)} %copy-done.8, f32[16,16,128]{2,1,0:T(8,128)S(1)} %all_to_all.25.refs_2_.refs_3_, bf16[16,320,128]{2,1,0:T(8,128)(2,1)S(1)} %slab_gradient.2.refs_1_.refs_3_), custom_call_target="tpu_custom_call" | custom-call | flops 671088640 | bytes 3932160 | tf_op jit(solution)/shard_map/slab_update/pallas_call | solution.py:323
  82.5 0.0 copy-start
  82.5 1.0 copy-done
  83.5 0.0 copy-start.2
  83.5 0.7 copy-done.2
  84.2 0.0 copy-start.5
  84.2 0.0 copy-start.7
  84.2 6.4 %all-to-all-start.4 = ((bf16[16,320,128]{2,1,0:T(8,128)(2,1)}), bf16[16,320,128]{2,1,0:T(8,128)(2,1)}, u32[]{:S(2)}, u32[]{:S(2)}) async-start(bf16[16,320,128]{2,1,0:T(8,128)(2,1)} %copy-done), calls=%async_computation.4 | async-start | bytes 2621440 | tf_op jit(solution)/shard_map/all_to_all | solution.py:360
  90.6 0.0 copy-done.5
  90.6 0.0 copy-done.7
  90.6 0.0 copy-start.1
  90.7 0.0 copy-start.3
  90.7 1.8 %slab_gradient.3.refs_4_ = bf16[16,192,128]{2,1,0:T(8,128)(2,1)S(1)} custom-call(bf16[16,400,128]{2,1,0:T(8,128)(2,1)S(1)} %all-to-all-done.states_ref.refs_0_, bf16[16,128,128]{2,1,0:T(8,128)(2,1)S(1)} %all-to-all-done.1.states_ref.refs_1_, bf16[512,128]{1,0:T(8,128)(2,1)S(1)} %copy-done.5, bf16[512,128]{1,0:T(8,128)(2,1)S(1)} %copy-done.7), custom_call_target="tpu_custom_call" | custom-call | flops 11796480 | bytes 3145728 | tf_op jit(solution)/shard_map/slab_gradient/pallas_call | solution.py:258
  92.4 0.0 copy-done.1
  92.5 0.0 copy-done.3
  92.5 2.3 %slab_update.3 = bf16[16,192,128]{2,1,0:T(8,128)(2,1)} custom-call(bf16[16,400,128]{2,1,0:T(8,128)(2,1)S(1)} %all-to-all-done.states_ref.refs_0_, bf16[16,128,128]{2,1,0:T(8,128)(2,1)S(1)} %all-to-all-done.1.states_ref.refs_1_, f32[8,128]{1,0:T(8,128)S(1)} %copy-done.8, f32[16,16,128]{2,1,0:T(8,128)S(1)} %copy-done.3, ...), custom_call_target="tpu_custom_call" | custom-call | flops 402653184 | bytes 2359296 | tf_op jit(solution)/shard_map/slab_update/pallas_call | solution.py:323
  94.8 26.1 %all-to-all-done.4.slabs_ref = bf16[16,320,128]{2,1,0:T(8,128)(2,1)} async-done(((bf16[16,320,128]{2,1,0:T(8,128)(2,1)}), bf16[16,320,128]{2,1,0:T(8,128)(2,1)}, u32[]{:S(2)}, u32[]{:S(2)}) %all-to-all-start.4) | async-done | bytes 1310752 | tf_op jit(solution)/shard_map/all_to_all | solution.py:360
  121.0 5.2 %all-to-all-start.3 = ((bf16[16,192,128]{2,1,0:T(8,128)(2,1)}), bf16[16,192,128]{2,1,0:T(8,128)(2,1)S(1)}, u32[]{:S(2)}, u32[]{:S(2)}) async-start(bf16[16,192,128]{2,1,0:T(8,128)(2,1)} %slab_update.3), calls=%async_computation.3 | async-start | bytes 1572864 | tf_op jit(solution)/shard_map/all_to_all | solution.py:360
  126.2 4.2 %join_row.2.refs_0_ = bf16[1,1048576]{1,0:T(2,128)(2,1)} custom-call(bf16[16,320,128]{2,1,0:T(8,128)(2,1)} %all-to-all-done.4.slabs_ref), custom_call_target="tpu_custom_call" | custom-call | bytes 3932160 | tf_op jit(solution)/shard_map/join_row/pallas_call | solution.py:136
  130.4 15.3 %all-to-all-done.3.slabs_ref = bf16[16,192,128]{2,1,0:T(8,128)(2,1)S(1)} async-done(((bf16[16,192,128]{2,1,0:T(8,128)(2,1)}), bf16[16,192,128]{2,1,0:T(8,128)(2,1)S(1)}, u32[]{:S(2)}, u32[]{:S(2)}) %all-to-all-start.3) | async-done | bytes 786464 | tf_op jit(solution)/shard_map/all_to_all | solution.py:360
  145.7 2.1 %join_row.3 = bf16[1,1048576]{1,0:T(2,128)(2,1)} custom-call(bf16[16,192,128]{2,1,0:T(8,128)(2,1)S(1)} %all-to-all-done.3.slabs_ref, bf16[1,1048576]{1,0:T(2,128)(2,1)} %join_row.2.refs_0_), custom_call_target="tpu_custom_call", output_to_operand_aliasing={{}: (1, {})} | custom-call | bytes 2359296 | tf_op jit(solution)/shard_map/join_row/pallas_call | solution.py:136
Async XLA Ops:
  6.3 43.4 %all-to-all-start = ((bf16[16,400,128]{2,1,0:T(8,128)(2,1)}), bf16[16,400,128]{2,1,0:T(8,128)(2,1)S(1)}, u32[]{:S(2)}, u32[]{:S(2)}) async-start(bf16[16,400,128]{2,1,0:T(8,128)(2,1)} %get-tuple-element.10), calls=%async_computation | async-start | bytes 3276800 | tf_op jit(solution)/shard_map/all_to_all | solution.py:360
  49.7 19.9 %all-to-all-start.1 = ((bf16[16,128,128]{2,1,0:T(8,128)(2,1)}), bf16[16,128,128]{2,1,0:T(8,128)(2,1)S(1)}, u32[]{:S(2)}, u32[]{:S(2)}) async-start(bf16[16,128,128]{2,1,0:T(8,128)(2,1)} %get-tuple-element.12), calls=%async_computation.1 | async-start | bytes 1048576 | tf_op jit(solution)/shard_map/all_to_all | solution.py:360
  55.4 0.9 copy-start.4
  56.4 0.9 copy-start.6
  60.2 20.1 %copy-start.8 = (f32[8,128]{1,0:T(8,128)S(1)}, f32[8,128]{1,0:T(8,128)}, u32[]{:S(2)}) copy-start(f32[8,128]{1,0:T(8,128)} %get-tuple-element.11.refs_0_.refs_1_.refs_2_) | copy-start | bytes 12292
  82.5 1.1 copy-start
  83.5 0.7 copy-start.2
  84.2 6.4 %copy-start.5 = (bf16[512,128]{1,0:T(8,128)(2,1)S(1)}, bf16[512,128]{1,0:T(8,128)(2,1)}, u32[]{:S(2)}) copy-start(bf16[512,128]{1,0:T(8,128)(2,1)} %get-tuple-element.13.refs_1_.refs_2_) | copy-start | bytes 393220
  84.2 6.4 %copy-start.7 = (bf16[512,128]{1,0:T(8,128)(2,1)S(1)}, bf16[512,128]{1,0:T(8,128)(2,1)}, u32[]{:S(2)}) copy-start(bf16[512,128]{1,0:T(8,128)(2,1)} %get-tuple-element.14.refs_2_.refs_3_) | copy-start | bytes 393220
  84.2 36.8 %all-to-all-start.4 = ((bf16[16,320,128]{2,1,0:T(8,128)(2,1)}), bf16[16,320,128]{2,1,0:T(8,128)(2,1)}, u32[]{:S(2)}, u32[]{:S(2)}) async-start(bf16[16,320,128]{2,1,0:T(8,128)(2,1)} %copy-done), calls=%async_computation.4 | async-start | bytes 2621440 | tf_op jit(solution)/shard_map/all_to_all | solution.py:360
  90.6 1.8 %copy-start.1 = (bf16[16,320,128]{2,1,0:T(8,128)(2,1)S(1)}, bf16[16,320,128]{2,1,0:T(8,128)(2,1)}, u32[]{:S(2)}) copy-start(bf16[16,320,128]{2,1,0:T(8,128)(2,1)} %copy-done) | copy-start | bytes 3932164
  90.7 1.8 %copy-start.3 = (f32[16,16,128]{2,1,0:T(8,128)S(1)}, f32[16,16,128]{2,1,0:T(8,128)}, u32[]{:S(2)}) copy-start(f32[16,16,128]{2,1,0:T(8,128)} %copy-done.2) | copy-start | bytes 393220
  121.0 24.8 %all-to-all-start.3 = ((bf16[16,192,128]{2,1,0:T(8,128)(2,1)}), bf16[16,192,128]{2,1,0:T(8,128)(2,1)S(1)}, u32[]{:S(2)}, u32[]{:S(2)}) async-start(bf16[16,192,128]{2,1,0:T(8,128)(2,1)} %slab_update.3), calls=%async_computation.3 | async-start | bytes 1572864 | tf_op jit(solution)/shard_map/all_to_all | solution.py:360

commit v5 on v4

--- a/solution.py
+++ b/solution.py
@@ -360,10 +360,432 @@
     return lax.all_to_all(slabs, "slab", split_axis=0, concat_axis=0, tiled=True)
 
 
+def partner(k):
+    return lax.axis_index("slab").astype(jnp.int32) ^ k
+
+
+def lines_of(start, count):
+    return pl.ds(pl.multiple_of(start, TILE), count)
+
+
+def split_pieces_body(ks, half, raw, lines, gates, row_ref, *refs):
+    refs = refs[gates:]
+    count = len(ks)
+    out_refs, helds, sems = refs[:count], refs[count : 2 * count], refs[2 * count]
+    cells = lines * LANES
+    end = row_ref.shape[1]
+    copies = []
+    for k, held in zip(ks, helds):
+        mine = []
+
+        def fetch(start, size, to):
+            source = row_ref.at[:, pl.ds(pl.multiple_of(start, GRID_Y), size)]
+            at = sems.at[len(copies) * 5 + len(mine)]
+            mine.append(pltpu.make_async_copy(source, held.at[:, pl.ds(to, size)], at))
+            mine[-1].start()
+
+        slab = partner(k)
+        fetch(slab * cells, cells, 0)
+        fetch(jnp.minimum((slab + 1) * cells, end - GRID_Y), GRID_Y, cells)
+        fetch(jnp.maximum(slab * cells - GRID_Y, 0), GRID_Y, cells + GRID_Y)
+        if raw and k < half:
+            other = partner(k ^ half)
+            fetch(other * cells, raw * LANES + GRID_Y, cells + 2 * GRID_Y)
+            fetch(jnp.maximum(other * cells - GRID_Y, 0), GRID_Y, cells + 3 * GRID_Y + raw * LANES)
+        copies.append(mine)
+
+    def grid_row(held, at):
+        return held[:, pl.ds(at, GRID_Y)].astype(F32).reshape(LINE, LANES)
+
+    for k, held, out_ref, mine in zip(ks, helds, out_refs, copies):
+        for copy in mine:
+            copy.wait()
+        slab = partner(k)
+        out_ref[:lines, :] = held[:, :cells].reshape(lines, LANES)
+        below = jnp.where(slab == end // cells - 1, 0.0, grid_row(held, cells))
+        above = jnp.where(slab == 0, 0.0, grid_row(held, cells + GRID_Y))
+        out_ref[lines : lines + TILE, :] = jnp.concatenate([below, above], axis=0).astype(BF16)
+        if raw and k < half:
+            at = cells + 2 * GRID_Y
+            to = lines + TILE
+            out_ref[to : to + raw, :] = held[:, at : at + raw * LANES].reshape(raw, LANES)
+            below = grid_row(held, at + raw * LANES)
+            above = jnp.where(partner(k ^ half) == 0, 0.0, grid_row(held, at + raw * LANES + GRID_Y))
+            out_ref[to + raw :, :] = jnp.concatenate([below, above], axis=0).astype(BF16)
+
+
+def split_pieces(row, slabs, raw, ks, gates):
+    lines = row.shape[1] // slabs // LANES
+    half = slabs // 2
+    extra = [raw if k < half else 0 for k in ks]
+    sizes = [lines + TILE + (more + TILE if more else 0) for more in extra]
+    return call(
+        functools.partial(split_pieces_body, ks, half, raw, lines, len(gates)),
+        "split_pieces",
+        moved=6 * sum(sizes) * LANES,
+        limit=16 if gates else 60,
+        in_specs=[IN_HBM] + [IN_VMEM] * len(gates),
+        out_specs=[IN_VMEM] * len(ks),
+        out_shape=[jax.ShapeDtypeStruct((size, LANES), BF16) for size in sizes],
+        scratch_shapes=[pltpu.VMEM((1, (size + TILE) * LANES), BF16) for size in sizes]
+        + [pltpu.SemaphoreType.DMA((5 * len(ks),))],
+    )(row, *gates)
+
+
+def join_pieces_body(ks, half, raw, lines, row_ref, *refs):
+    count = len(ks)
+    pieces = refs[:count]
+    row_ref, token_ref, *helds, sems = refs[count:]
+    cells = lines * LANES
+    skip = raw * LANES
+    copies = []
+    for k, piece, held in zip(ks, pieces, helds):
+        near = k < half
+        held[...] = piece[...].reshape(held.shape)
+
+        def store(at, size, start):
+            target = row_ref.at[:, pl.ds(pl.multiple_of(start, GRID_Y), size)]
+            copies.append(pltpu.make_async_copy(held.at[:, pl.ds(at, size)], target, sems.at[len(copies)]))
+            copies[-1].start()
+
+        if near:
+            store(0, cells, partner(k) * cells)
+            if raw:
+                store(cells, skip, partner(k ^ half) * cells)
+        else:
+            store(0, cells - skip, partner(k) * cells + skip)
+    for copy in copies:
+        copy.wait()
+    token_ref[...] = jnp.zeros_like(token_ref)
+
+
+def join_pieces(row, slabs, raw, pieces, ks):
+    cells = NCELL // slabs
+    out = jax.ShapeDtypeStruct((1, NCELL), BF16)
+    token = jax.ShapeDtypeStruct((8, LANES), F32)
+    body = functools.partial(join_pieces_body, ks, slabs // 2, raw, cells // LANES)
+    return call(
+        body if row is not None else functools.partial(body, None),
+        "join_pieces",
+        moved=6 * sum(piece.size for piece in pieces),
+        in_specs=([] if row is None else [IN_HBM]) + [IN_VMEM] * len(ks),
+        out_specs=[IN_HBM, IN_VMEM],
+        out_shape=[out, token],
+        input_output_aliases={} if row is None else {0: 0},
+        scratch_shapes=[pltpu.VMEM((1, piece.size), BF16) for piece in pieces]
+        + [pltpu.SemaphoreType.DMA((2 * len(ks),))],
+    )(*([] if row is None else [row]), *pieces)
+
+
+def swap_order(total):
+    row = lax.broadcasted_iota(jnp.int32, (total, total), 0)
+    col = lax.broadcasted_iota(jnp.int32, (total, total), 1)
+    return (row == partner(col)).astype(F32)
+
+
+def reorder(gram):
+    order = swap_order(gram.shape[0])
+    half = jnp.dot(order, gram, precision=lax.Precision.HIGHEST, preferred_element_type=F32)
+    return jnp.dot(half, order, precision=lax.Precision.HIGHEST, preferred_element_type=F32)
+
+
+def gram_pieces_body(lines, *refs):
+    pieces, out_ref, pairs = refs[:-2], refs[-2], refs[-1]
+    total = len(pieces)
+    wide = total * TILE
+    tiles = 4
+    pairs[...] = jnp.zeros_like(pairs)
+
+    def step(i, carry):
+        parts = []
+        for t in range(tiles):
+            at = lines_of((i * tiles + t) * TILE, TILE)
+            parts.append(jnp.concatenate([piece[at, :] for piece in pieces], axis=0))
+        block = jnp.concatenate(parts, axis=1)
+        pairs[...] += lax.dot_general(block, block, (((1,), (1,)), ((), ())), preferred_element_type=F32)
+        return carry
+
+    lax.fori_loop(0, lines // TILE // tiles, step, 0)
+    equal = jnp.where(same_line(total), pairs[...], 0.0)
+    rows = jnp.sum(equal.reshape(total, TILE, wide), axis=1)
+    gram = jnp.dot(rows, members(total, F32), precision=lax.Precision.HIGHEST, preferred_element_type=F32)
+    gram = jnp.concatenate([reorder(gram), jnp.zeros((total, LANES - total), F32)], axis=1)
+    out_ref[...] = jnp.broadcast_to(gram[None], out_ref.shape)
+
+
+def gram_pieces(pieces, lines):
+    total = len(pieces)
+    wide = total * TILE
+    return call(
+        functools.partial(gram_pieces_body, lines),
+        "gram_pieces",
+        flops=2 * wide * wide * LANES * (lines // TILE),
+        moved=2 * total * lines * LANES,
+        in_specs=[IN_VMEM] * total,
+        out_specs=IN_VMEM,
+        out_shape=jax.ShapeDtypeStruct((total, total, LANES), F32),
+        scratch_shapes=[pltpu.VMEM((wide, wide), F32)],
+    )(*pieces)
+
+
+def gradient_pieces_body(k, lines, count, views, arrays, *refs):
+    observed_ref, precision_ref, out_ref, observed, precision, grads, sems = refs[arrays:]
+    rows = BLOCK // LINE
+    shape = (rows, LINE, LANES)
+    lane = lax.broadcasted_iota(jnp.int32, (1, LINE, LANES), 2)
+    line = lax.broadcasted_iota(jnp.int32, (1, LINE, LANES), 1)
+    steps = count // BLOCK
+    mine = lines_of(partner(k) * lines, count)
+    fetches = [
+        pltpu.make_async_copy(observed_ref.at[mine, :], observed, sems.at[steps]),
+        pltpu.make_async_copy(precision_ref.at[mine, :], precision, sems.at[steps + 1]),
+    ]
+    for fetch in fetches:
+        fetch.start()
+    for fetch in fetches:
+        fetch.wait()
+
+    def store(i):
+        at = lines_of(i * BLOCK, BLOCK)
+        return pltpu.make_async_copy(grads.at[:, at, :], out_ref.at[:, at, :], sems.at[i])
+
+    def step(i, carry):
+        start = i * BLOCK
+        at = lines_of(start, BLOCK)
+        obs = observed[at, :].astype(F32).reshape(shape)
+        prec = precision[at, :].astype(F32).reshape(shape)
+        for p, (array, lead, base) in enumerate(views):
+
+            def load(begin, size):
+                part = lines_of(base + begin, size)
+                value = refs[array][part, :] if lead is None else refs[array][lead, part, :]
+                return value.astype(F32)
+
+            here = load(start, BLOCK)
+            before = load(jnp.where(i == 0, count, start - TILE), TILE)
+            after = load(start + BLOCK, TILE)
+            above = jnp.concatenate([before[LINE:], here[:-LINE]], axis=0).reshape(shape)
+            below = jnp.concatenate([here[LINE:], after[:LINE]], axis=0).reshape(shape)
+            field = here.reshape(shape)
+            turned = pltpu.roll(field, 1, 2)
+            carried = jnp.where(line == 0, 0.0, pltpu.roll(turned, 1, 1))
+            left = jnp.where(lane == 0, carried, turned)
+            turned = pltpu.roll(field, LANES - 1, 2)
+            carried = jnp.where(line == LINE - 1, 0.0, pltpu.roll(turned, LINE - 1, 1))
+            right = jnp.where(lane == LANES - 1, carried, turned)
+            laplace = (4.0 + mass_term) * field - (below + above + right + left)
+            squash = jnp.tanh(field)
+            result = prec * (obs - squash) * (1.0 - squash * squash) - prior_scale * laplace
+            grads[p, at, :] = result.reshape(BLOCK, LANES).astype(BF16)
+        store(i).start()
+        return carry
+
+    def finish(i, carry):
+        store(i).wait()
+        return carry
+
+    lax.fori_loop(0, steps, step, 0)
+    lax.fori_loop(0, steps, finish, 0)
+
+
+def gradient_pieces(arrays, views, observed, precision, lines, count, k):
+    out = jax.ShapeDtypeStruct((len(views), count, LANES), BF16)
+    return call(
+        functools.partial(gradient_pieces_body, k, lines, count, views, len(arrays)),
+        "gradient_pieces",
+        flops=30 * out.size,
+        moved=8 * out.size,
+        in_specs=[IN_VMEM] * len(arrays) + [IN_HBM, IN_HBM],
+        out_specs=IN_HBM,
+        out_shape=out,
+        scratch_shapes=[
+            pltpu.VMEM((count, LANES), BF16),
+            pltpu.VMEM((count, LANES), BF16),
+            pltpu.VMEM(out.shape, BF16),
+            pltpu.SemaphoreType.DMA((count // BLOCK + 2,)),
+        ],
+    )(*arrays, observed, precision)
+
+
+def raw_body(raw, lines, *refs):
+    out_ref = refs[-1]
+    for k, piece in enumerate(refs[:-1]):
+        out_ref[k, :raw, :] = piece[:raw, :]
+        below = piece[raw : raw + TILE, :].astype(F32)[:LINE]
+        above = piece[lines : lines + TILE, :].astype(F32)[LINE:]
+        out_ref[k, raw:, :] = jnp.concatenate([below, above], axis=0).astype(BF16)
+
+
+def raw_states(pieces, raw, lines):
+    out = jax.ShapeDtypeStruct((len(pieces), raw + TILE, LANES), BF16)
+    return call(
+        functools.partial(raw_body, raw, lines),
+        "raw_states",
+        moved=4 * out.size,
+        in_specs=[IN_VMEM] * len(pieces),
+        out_specs=IN_VMEM,
+        out_shape=out,
+    )(*pieces)
+
+
+def update_pieces_body(ks, half, raw, lines, groups, extra, *refs):
+    total = 2 * half
+    pieces, refs = refs[:total], refs[total:]
+    scalars_ref, grams_ref, *refs = refs
+    group_refs, refs = refs[: len(groups)], refs[len(groups) :]
+    raw_refs, refs = refs[:extra], refs[extra:]
+    out_refs = refs[-len(ks) - 5 : -5]
+    grads, raw_grads, mixer, own, sems = refs[-5:]
+    wide = total * TILE
+    high = len(ks) * TILE
+    fetches = []
+    for group, group_ref in zip(groups, group_refs):
+        for j, k in enumerate(group):
+            fetches.append(pltpu.make_async_copy(group_ref.at[j], grads.at[k], sems.at[len(fetches)]))
+    if extra:
+        fetches.append(pltpu.make_async_copy(raw_refs[1], raw_grads, sems.at[len(fetches)]))
+    for fetch in fetches:
+        fetch.start()
+    spread, anneal, step_size = (scalars_ref[k : k + 1, :1] for k in range(3))
+    rate = step_size / total
+    coeff = 2.0 * anneal / spread
+    gram = reorder(jnp.sum(grams_ref[...], axis=0)[:, :total])
+    row = lax.broadcasted_iota(jnp.int32, (total, total), 0)
+    col = lax.broadcasted_iota(jnp.int32, (total, total), 1)
+    diagonal = jnp.where(row == col, gram, 0.0)
+    down = jnp.sum(diagonal, axis=1, keepdims=True)
+    across = jnp.sum(diagonal, axis=0, keepdims=True)
+    kernel = jnp.exp(-(down + across - 2.0 * gram) / (spread * NCELL)).astype(BF16)
+    ksum = jnp.sum(kernel.astype(F32), axis=1, keepdims=True)
+    member = members(total, BF16)
+    half_way = jnp.dot(member, kernel, preferred_element_type=F32).astype(BF16)
+    full = lax.dot_general(half_way, member, (((1,), (1,)), ((), ())), preferred_element_type=F32)
+    full = jnp.where(same_line(total), full, 0.0)
+    gain = jnp.broadcast_to((1.0 + rate * coeff * ksum)[:, :, None], (total, TILE, LANES)).reshape(wide, LANES)
+    for j, k in enumerate(ks):
+        mixer[j * TILE : (j + 1) * TILE, :] = full[k * TILE : (k + 1) * TILE].astype(BF16)
+        own[j * TILE : (j + 1) * TILE, :] = gain[k * TILE : (k + 1) * TILE]
+    for fetch in fetches:
+        fetch.wait()
+
+    def mix(states, slopes, who, stores):
+        size = len(who) * TILE
+        states = jnp.concatenate(states, axis=0)
+        both = jnp.concatenate([slopes.reshape(wide, LANES), states], axis=1)
+        mixed = jnp.dot(mixer[:size, :], both, preferred_element_type=F32)
+        drive, pulled = mixed[:, :LANES], mixed[:, LANES:]
+        kept = jnp.concatenate([states[k * TILE : (k + 1) * TILE] for k in who], axis=0).astype(F32)
+        new = (kept * own[:size, :] + rate * (drive - coeff * pulled)).astype(BF16)
+        for j, (out_ref, to) in enumerate(stores):
+            out_ref[lines_of(to, TILE), :] = new[j * TILE : (j + 1) * TILE]
+
+    near = [k for k in ks if k < half]
+
+    def slab_step(who, i, carry):
+        for t in range(BLOCK // TILE):
+            at = i * BLOCK + t * TILE
+            stores = [(out_ref, at if k < half else at - raw) for k, out_ref in zip(who, out_refs)]
+            mix([ref[lines_of(at, TILE), :] for ref in pieces], grads[:, lines_of(at, TILE), :], who, stores)
+        return carry
+
+    def raw_step(i, carry):
+        for t in range(BLOCK // TILE):
+            at = i * BLOCK + t * TILE
+            states = [ref[lines_of(lines + TILE + at, TILE), :] for ref in pieces[:half]]
+            states += [raw_refs[0][j, lines_of(at, TILE), :] for j in range(half)]
+            stores = [(out_ref, lines + at) for out_ref in out_refs[: len(near)]]
+            mix(states, raw_grads[:, lines_of(at, TILE), :], near, stores)
+        return carry
+
+    if near and raw:
+        lax.fori_loop(0, raw // BLOCK, functools.partial(slab_step, near), 0)
+    lax.fori_loop(raw // BLOCK, lines // BLOCK, functools.partial(slab_step, ks), 0)
+    if near and raw:
+        lax.fori_loop(0, raw // BLOCK, raw_step, 0)
+
+
+def update_pieces(scalars, grams, pieces, grads, groups, raw_parts, gates, raw, lines, ks):
+    total = len(pieces)
+    half = total // 2
+    wide = total * TILE
+    ks = tuple(sorted(ks))
+    sizes = [lines + raw if k < half else lines - raw for k in ks]
+    results = call(
+        functools.partial(update_pieces_body, ks, half, raw, lines, groups, len(raw_parts)),
+        "update_pieces",
+        flops=4 * len(ks) * TILE * wide * LANES * (lines // TILE),
+        moved=2 * (2 * total + len(ks)) * lines * LANES,
+        in_specs=[IN_VMEM] * (total + 2)
+        + [IN_HBM] * len(groups)
+        + [IN_VMEM, IN_HBM][: len(raw_parts)]
+        + [IN_VMEM] * len(gates),
+        out_specs=[IN_VMEM] * len(ks),
+        out_shape=[jax.ShapeDtypeStruct((size, LANES), BF16) for size in sizes],
+        scratch_shapes=[
+            pltpu.VMEM((total, lines, LANES), BF16),
+            pltpu.VMEM((total, max(raw, TILE), LANES), BF16),
+            pltpu.VMEM((len(ks) * TILE, wide), BF16),
+            pltpu.VMEM((len(ks) * TILE, LANES), F32),
+            pltpu.SemaphoreType.DMA((total + 1,)),
+        ],
+    )(*pieces, scalars, grams, *grads, *raw_parts, *gates)
+    return dict(zip(ks, results))
+
+
+def exchange(piece, k, slabs):
+    return lax.ppermute(piece, "slab", [(i, i ^ k) for i in range(slabs)])
+
+
+RAW = 0
+SENDS = ((8, 9, 10, 4, 11), (5, 12, 6, 13, 7), (14, 1, 15, 2, 3, 0))
+GROUPS = ((8, 9, 10, 4), (11, 5, 12, 6), (13, 7, 14, 0), (1, 15, 2, 3))
+
+
+def by_pieces(particles, observed, precision, spread, anneal, step_size):
+    slabs = lax.axis_size("slab")
+    half = slabs // 2
+    lines = NCELL // slabs // LANES
+    obs = observed.reshape(-1, LANES)
+    prec = precision.reshape(-1, LANES)
+    states = [None] * slabs
+    for n, ks in enumerate(SENDS):
+        gates = [states[SENDS[n - 1][0]]] if n else []
+        for k, piece in zip(ks, split_pieces(particles, slabs, RAW, ks, gates)):
+            states[k] = exchange(piece, k, slabs) if k else piece
+    grads = []
+    for group in GROUPS:
+        arrays = [states[k] for k in group]
+        views = tuple((j, None, 0) for j in range(len(group)))
+        grads.append(gradient_pieces(arrays, views, obs, prec, lines, lines, 0))
+    grams = swap(gram_pieces(states, lines))
+    scalars = jnp.concatenate([spread, anneal, step_size])
+    scalars = jnp.broadcast_to(scalars[:, None], (3, LANES))
+    extra = []
+    if RAW:
+        far = exchange(raw_states(states[:half], RAW, lines), half, slabs)
+        views = [(k, None, lines + TILE) for k in range(half)] + [(half, k, 0) for k in range(half)]
+        slopes = gradient_pieces(states[:half] + [far], tuple(views), obs, prec, lines, RAW, half)
+        extra = [far, slopes]
+    new = [None] * slabs
+    row = None
+    gates = []
+    for n, ks in enumerate(SENDS):
+        more = extra if min(ks) < half else []
+        results = update_pieces(scalars, grams, states, grads, GROUPS, more, gates, RAW, lines, ks)
+        for k in ks:
+            new[k] = exchange(results[k], k, slabs) if k else results[k]
+        gates = [new[ks[0]]]
+    for group in GROUPS:
+        row, _ = join_pieces(row, slabs, RAW, [new[k] for k in group], group)
+    return row
+
+
 def on_device(particles, observed, precision, spread, anneal, step_size):
     slabs = lax.axis_size("slab")
     total = particles.shape[0] * slabs
     lines = NCELL // slabs // LANES
+    if slabs == 16:
+        return by_pieces(particles, observed, precision, spread, anneal, step_size)
     sent, begun = cuts(lines)
     fields = [observed.reshape(-1, LANES), precision.reshape(-1, LANES)]
     numbers = [spread, anneal, step_size]

time: 148 us -> 165 us (1.11)
  waiting for transfers between devices: 83.7 us -> 44.8 us
  starting transfers between devices: 24 us -> 52.2 us
  local copies, waits for them, and re-layouts: 3.53 us -> 25.5 us
  Pallas kernels: 24.3 us -> 38.9 us
  blocking collectives: 10.1 us -> 0 us
    all_to_all x4 -> x1, waiting for transfers between devices: 83.7 us -> 0.01 us  [swap(): lax.all_to_all(slabs, 'slab', split_axis=0, concat_axis=0, tiled=True)]
    ppermute x0 -> x30, starting transfers between devices: none -> 47.1 us  [exchange(): return lax.ppermute(piece, 'slab', [(i, i ^ k) for i in range(slabs)])]
    ppermute x0 -> x30, waiting for transfers between devices: none -> 44.8 us  [exchange(): return lax.ppermute(piece, 'slab', [(i, i ^ k) for i in range(slabs)])]
    unnamed x18 -> x92, local copies, waits for them, and re-layouts: 3.53 us -> 25.4 us
    all_to_all x4 -> x1, starting transfers between devices: 24 us -> 5.14 us  [swap(): lax.all_to_all(slabs, 'slab', split_axis=0, concat_axis=0, tiled=True)]
    pallas_call x10 -> x15, Pallas kernels: 24.3 us -> 38.9 us  [the longest x3 18.8 us: update_pieces(): call(functools.partial(update_pieces_body, ks, half, raw, lines, groups,...]
    all_to_all x1 -> x0, blocking collectives: 10.1 us -> none  [swap(): lax.all_to_all(slabs, 'slab', split_axis=0, concat_axis=0, tiled=True)]
  transfers between devices with their start and end apart: 4 -> 31, of which waited for: 4 -> 11; matrix products, arithmetic and copies ran while one was open for 0% -> 0% of each run, Pallas kernels for 10% -> 16%
where the time goes in v5:
time: 165 us; the launch traced here: 164 us
  starting transfers between devices  52.2 us (32%)
  waiting for transfers between devices  44.8 us (27%)
  Pallas kernels  38.9 us (24%)
  local copies, waits for them, and re-layouts  25.5 us (15%)
  between operations  2.33 us (1%)
    ppermute x30, starting transfers between devices, exchange(): return lax.ppermute(piece, 'slab', [(i, i ^ k) for i in range(slabs)])  47.1 us
    ppermute x30, waiting for transfers between devices, exchange(): return lax.ppermute(piece, 'slab', [(i, i ^ k) for i in range(slabs)])  44.8 us
    unnamed x92, local copies, waits for them, and re-layouts  25.4 us
    pallas_call x3, Pallas kernels, update_pieces(): call(functools.partial(update_pieces_body, ks, half, raw, lines, groups,...  18.8 us
    pallas_call x4, Pallas kernels, gradient_pieces(): call(functools.partial(gradient_pieces_body, k, lines, count, views, len(...  7.22 us
    pallas_call x4, Pallas kernels, join_pieces(): call(body if row is not None else functools.partial(body, None), 'join_pi...  6.63 us
    all_to_all x1, starting transfers between devices, swap(): lax.all_to_all(slabs, 'slab', split_axis=0, concat_axis=0, tiled=True)  5.14 us
    pallas_call x3, Pallas kernels, split_pieces(): call(functools.partial(split_pieces_body, ks, half, raw, lines, len(gates...  3.58 us
  transfers between devices with their start and end apart: 31, of which 11 were waited for; matrix products, arithmetic and copies ran while one was open for 0% of the time, Pallas kernels for 16%

profile of v5, /device:TPU:9, one launch (start us, length us, event | category | flops | bytes accessed | tf_op | source)
XLA Modules:
  0.0 163.8 jit_solution(4621501130981614954)
XLA Ops:
  0.0 2.4 %split_pieces.3 = (bf16[528,128]{1,0:T(8,128)(2,1)}, bf16[528,128]{1,0:T(8,128)(2,1)}, bf16[528,128]{1,0:T(8,128)(2,1)}, bf16[528,128]{1,0:T(8,128)(2,1)}, bf16[528,128]{1,0:T(8,128)(2,1)}) custom-call(bf16[1,1048576]{1,0:T(2,128)(2,1)} %row_ref.5), custom_call_target="tpu_custom_call" | custom-call | bytes 2027520 | tf_op jit(solution)/shard_map/split_pieces/pallas_call | solution.py:422
  2.4 2.4 %collective-permute-start = (bf16[528,128]{1,0:T(8,128)(2,1)}, bf16[528,128]{1,0:T(8,128)(2,1)S(1)}, u32[]{:S(2)}, u32[]{:S(2)}) collective-permute-start(bf16[528,128]{1,0:T(8,128)(2,1)} %get-tuple-element.41), channel_id=1, source_target_pairs={{0,8},{1,9},{2,10},{3,11},{4,12},{5,13},{6,14},{7,15},{8,0},{9,1},... | collective-permute-start | bytes 405512 | tf_op jit(solution)/shard_map/ppermute | solution.py:736
  5.0 0.9 collective-permute-start.8
  5.9 3.5 %collective-permute-start.9 = (bf16[528,128]{1,0:T(8,128)(2,1)}, bf16[528,128]{1,0:T(8,128)(2,1)S(1)}, u32[]{:S(2)}, u32[]{:S(2)}) collective-permute-start(bf16[528,128]{1,0:T(8,128)(2,1)} %get-tuple-element.51), channel_id=1, source_target_pairs={{0,10},{1,11},{2,8},{3,9},{4,14},{5,15},{6,12},{7,13},{8,2},{9,3},... | collective-permute-start | bytes 405512 | tf_op jit(solution)/shard_map/ppermute | solution.py:736
  9.4 2.3 %collective-permute-done.refs_0_.refs_8_ = bf16[528,128]{1,0:T(8,128)(2,1)S(1)} collective-permute-done((bf16[528,128]{1,0:T(8,128)(2,1)}, bf16[528,128]{1,0:T(8,128)(2,1)S(1)}, u32[]{:S(2)}, u32[]{:S(2)}) %collective-permute-start) | collective-permute-done | bytes 135200 | tf_op jit(solution)/shard_map/ppermute | solution.py:736
  11.7 2.2 %copy-done = bf16[1,1048576]{1,0:T(2,128)(2,1)S(1)} copy-done((bf16[1,1048576]{1,0:T(2,128)(2,1)S(1)}, bf16[1,1048576]{1,0:T(2,128)(2,1)}, u32[]{:S(2)}) %copy-start) | copy-done | bytes 2097176
  14.5 2.5 %collective-permute-start.1 = (bf16[528,128]{1,0:T(8,128)(2,1)S(1)}, bf16[528,128]{1,0:T(8,128)(2,1)S(1)}, u32[]{:S(2)}, u32[]{:S(2)}) collective-permute-start(bf16[528,128]{1,0:T(8,128)(2,1)S(1)} %get-tuple-element.42), channel_id=1, source_target_pairs={{0,5},{1,4},{2,7},{3,6},{4,1},{5,0},{6,3},{7,2},{8,13},{9,12},{10,... | collective-permute-start | bytes 405512 | tf_op jit(solution)/shard_map/ppermute | solution.py:736
  17.0 2.9 %collective-permute-start.10 = (bf16[528,128]{1,0:T(8,128)(2,1)S(1)}, bf16[528,128]{1,0:T(8,128)(2,1)S(1)}, u32[]{:S(2)}, u32[]{:S(2)}) collective-permute-start(bf16[528,128]{1,0:T(8,128)(2,1)S(1)} %copy-done.45), channel_id=1, source_target_pairs={{0,11},{1,10},{2,9},{3,8},{4,15},{5,14},{6,13},{7,12},{8,3},{9,2},... | collective-permute-start | bytes 405512 | tf_op jit(solution)/shard_map/ppermute | solution.py:736
  20.7 1.5 collective-permute-start.7
  22.2 3.5 %collective-permute-done.9.refs_10_.refs_2_ = bf16[528,128]{1,0:T(8,128)(2,1)S(1)} collective-permute-done((bf16[528,128]{1,0:T(8,128)(2,1)}, bf16[528,128]{1,0:T(8,128)(2,1)S(1)}, u32[]{:S(2)}, u32[]{:S(2)}) %collective-permute-start.9) | collective-permute-done | bytes 135200 | tf_op jit(solution)/shard_map/ppermute | solution.py:736
  25.7 2.3 %collective-permute-start.12 = (bf16[528,128]{1,0:T(8,128)(2,1)S(1)}, bf16[528,128]{1,0:T(8,128)(2,1)S(1)}, u32[]{:S(2)}, u32[]{:S(2)}) collective-permute-start(bf16[528,128]{1,0:T(8,128)(2,1)S(1)} %get-tuple-element.54), channel_id=1, source_target_pairs={{0,13},{1,12},{2,15},{3,14},{4,9},{5,8},{6,11},{7,10},{8,5},{9,4},... | collective-permute-start | bytes 405512 | tf_op jit(solution)/shard_map/ppermute | solution.py:736
  29.2 1.1 collective-permute-done.6.refs_6_.refs_3_
  30.2 2.1 %collective-permute-start.3 = (bf16[528,128]{1,0:T(8,128)(2,1)S(1)}, bf16[528,128]{1,0:T(8,128)(2,1)S(1)}, u32[]{:S(2)}, u32[]{:S(2)}) collective-permute-start(bf16[528,128]{1,0:T(8,128)(2,1)S(1)} %get-tuple-element.45), channel_id=1, source_target_pairs={{0,2},{1,3},{2,0},{3,1},{4,6},{5,7},{6,4},{7,5},{8,10},{9,11},{10,... | collective-permute-start | bytes 405512 | tf_op jit(solution)/shard_map/ppermute | solution.py:736
  32.3 5.8 %collective-permute-done.7.refs_7_.refs_1_ = bf16[528,128]{1,0:T(8,128)(2,1)S(1)} collective-permute-done((bf16[528,128]{1,0:T(8,128)(2,1)S(1)}, bf16[528,128]{1,0:T(8,128)(2,1)S(1)}, u32[]{:S(2)}, u32[]{:S(2)}) %collective-permute-start.7) | collective-permute-done | bytes 135200 | tf_op jit(solution)/shard_map/ppermute | solution.py:736
  38.9 3.9 %collective-permute-start.13 = (bf16[528,128]{1,0:T(8,128)(2,1)S(1)}, bf16[528,128]{1,0:T(8,128)(2,1)S(1)}, u32[]{:S(2)}, u32[]{:S(2)}) collective-permute-start(bf16[528,128]{1,0:T(8,128)(2,1)S(1)} %get-tuple-element.55), channel_id=1, source_target_pairs={{0,14},{1,15},{2,12},{3,13},{4,10},{5,11},{6,8},{7,9},{8,6},{9,7},... | collective-permute-start | bytes 405512 | tf_op jit(solution)/shard_map/ppermute | solution.py:736
  43.6 3.1 %collective-permute-done.13.refs_14_.refs_2_ = bf16[528,128]{1,0:T(8,128)(2,1)S(1)} collective-permute-done((bf16[528,128]{1,0:T(8,128)(2,1)S(1)}, bf16[528,128]{1,0:T(8,128)(2,1)S(1)}, u32[]{:S(2)}, u32[]{:S(2)}) %collective-permute-start.13) | collective-permute-done | bytes 135200 | tf_op jit(solution)/shard_map/ppermute | solution.py:736
  46.7 8.8 %collective-permute-done.14.refs_15_.refs_1_ = bf16[528,128]{1,0:T(8,128)(2,1)S(1)} collective-permute-done((bf16[528,128]{1,0:T(8,128)(2,1)S(1)}, bf16[528,128]{1,0:T(8,128)(2,1)S(1)}, u32[]{:S(2)}, u32[]{:S(2)}) %collective-permute-start.14) | collective-permute-done | bytes 135200 | tf_op jit(solution)/shard_map/ppermute | solution.py:736
  55.5 2.7 %gram_pieces.1 = f32[16,16,128]{2,1,0:T(8,128)S(1)} custom-call(bf16[528,128]{1,0:T(8,128)(2,1)S(1)} %get-tuple-element.43.refs_0_.refs_3_, bf16[528,128]{1,0:T(8,128)(2,1)S(1)} %collective-permute-done.2.refs_1_.refs_0_, bf16[528,128]{1,0:T(8,128)(2,1)S(1)} %collective-permute-done.3.refs_2_, bf16[528,128]{1,0:T(8,128)(2,1)S(1)} %collective-permute-done.4.refs_3_, ...), custom_call_target="tpu_custom_call" | custom-call | flops 536870912 | bytes 2097152 | tf_op jit(solution)/shard_map/gram_pieces/pallas_call | solution.py:519
  63.4 5.1 %all-to-all-start = ((f32[16,16,128]{2,1,0:T(8,128)}), f32[16,16,128]{2,1,0:T(8,128)}, u32[]{:S(2)}, u32[]{:S(2)}) async-start(f32[16,16,128]{2,1,0:T(8,128)} %copy-done.44), calls=%async_computation | async-start | bytes 262144 | tf_op jit(solution)/shard_map/all_to_all | solution.py:360
  70.7 1.6 copy-done.2
  72.3 1.8 %gradient_pieces.4.refs_18_ = bf16[4,512,128]{2,1,0:T(8,128)(2,1)S(1)} custom-call(bf16[528,128]{1,0:T(8,128)(2,1)S(1)} %collective-permute-done.refs_0_.refs_8_, bf16[528,128]{1,0:T(8,128)(2,1)S(1)} %collective-permute-done.8.refs_9_.refs_1_, bf16[528,128]{1,0:T(8,128)(2,1)S(1)} %collective-permute-done.9.refs_10_.refs_2_, ...), custom_call_target="tpu_custom_call" | custom-call | flops 7864320 | bytes 2097152 | tf_op jit(solution)/shard_map/gradient_pieces/pallas_call | solution.py:593
  75.0 1.8 %gradient_pieces.5.refs_19_ = bf16[4,512,128]{2,1,0:T(8,128)(2,1)S(1)} custom-call(bf16[528,128]{1,0:T(8,128)(2,1)S(1)} %copy-done.12, bf16[528,128]{1,0:T(8,128)(2,1)S(1)} %collective-permute-done.1.refs_0_.refs_5_.refs_1_, bf16[528,128]{1,0:T(8,128)(2,1)S(1)} %copy-done.21, bf16[528,128]{1,0:T(8,128)(2,1)S(1)} %copy-done.15, ...), custom_call_target="tpu_custom_call" | custom-call | flops 7864320 | bytes 2097152 | tf_op jit(solution)/shard_map/gradient_pieces/pallas_call | solution.py:593
  76.9 1.8 %gradient_pieces.7.refs_21_ = bf16[4,512,128]{2,1,0:T(8,128)(2,1)S(1)} custom-call(bf16[528,128]{1,0:T(8,128)(2,1)S(1)} %copy-done.30, bf16[528,128]{1,0:T(8,128)(2,1)S(1)} %copy-done.42, bf16[528,128]{1,0:T(8,128)(2,1)S(1)} %copy-done.33, bf16[528,128]{1,0:T(8,128)(2,1)S(1)} %copy-done.36, bf16[8192,128]{1,0:T(8,128)(2,1)S(1)} %bitcast.4, ...), custom_call_target="tpu_custom_call" | custom-call | flops 7864320 | bytes 2097152 | tf_op jit(solution)/shard_map/gradient_pieces/pallas_call | solution.py:593
  79.5 1.8 %gradient_pieces.6.refs_20_ = bf16[4,512,128]{2,1,0:T(8,128)(2,1)S(1)} custom-call(bf16[528,128]{1,0:T(8,128)(2,1)S(1)} %copy-done.24, bf16[528,128]{1,0:T(8,128)(2,1)S(1)} %copy-done.18, bf16[528,128]{1,0:T(8,128)(2,1)S(1)} %copy-done.39, bf16[528,128]{1,0:T(8,128)(2,1)S(1)} %copy-done.27, bf16[8192,128]{1,0:T(8,128)(2,1)S(1)} %bitcast.5, ...), custom_call_target="tpu_custom_call" | custom-call | flops 7864320 | bytes 2097152 | tf_op jit(solution)/shard_map/gradient_pieces/pallas_call | solution.py:593
  82.2 1.0 copy-done.4
  83.2 1.0 copy-done.6
  87.9 0.9 copy-done.19
  96.1 6.3 %update_pieces.3 = (bf16[512,128]{1,0:T(8,128)(2,1)S(1)}, bf16[512,128]{1,0:T(8,128)(2,1)S(1)}, bf16[512,128]{1,0:T(8,128)(2,1)S(1)}, bf16[512,128]{1,0:T(8,128)(2,1)S(1)}, bf16[512,128]{1,0:T(8,128)(2,1)S(1)}) custom-call(bf16[528,128]{1,0:T(8,128)(2,1)S(1)} %copy-done.28, bf16[528,128]{1,0:T(8,128)(2,1)S(1)} %copy-done.31, ...), custom_call_target="tpu_custom_call" | custom-call | flops 335544320 | bytes 4849664 | tf_op jit(solution)/shard_map/update_pieces/pallas_call | solution.py:713
  102.3 2.2 %collective-permute-start.15 = (bf16[512,128]{1,0:T(8,128)(2,1)S(1)}, bf16[512,128]{1,0:T(8,128)(2,1)S(1)}, u32[]{:S(2)}, u32[]{:S(2)}) collective-permute-start(bf16[512,128]{1,0:T(8,128)(2,1)S(1)} %get-tuple-element.57), channel_id=1, source_target_pairs={{0,8},{1,9},{2,10},{3,11},{4,12},{5,13},{6,14},{7,15},{8,0},{9,1},... | collective-permute-start | bytes 393224 | tf_op jit(solution)/shard_map/ppermute | solution.py:736
  105.3 3.0 %collective-permute-start.17 = (bf16[512,128]{1,0:T(8,128)(2,1)S(1)}, bf16[512,128]{1,0:T(8,128)(2,1)S(1)}, u32[]{:S(2)}, u32[]{:S(2)}) collective-permute-start(bf16[512,128]{1,0:T(8,128)(2,1)S(1)} %get-tuple-element.59), channel_id=1, source_target_pairs={{0,10},{1,11},{2,8},{3,9},{4,14},{5,15},{6,12},{7,13},{8,2},{9,3},... | collective-permute-start | bytes 393224 | tf_op jit(solution)/shard_map/ppermute | solution.py:736
  108.5 7.5 %collective-permute-done.15.refs_0_.refs_22_ = bf16[512,128]{1,0:T(8,128)(2,1)S(1)} collective-permute-done((bf16[512,128]{1,0:T(8,128)(2,1)S(1)}, bf16[512,128]{1,0:T(8,128)(2,1)S(1)}, u32[]{:S(2)}, u32[]{:S(2)}) %collective-permute-start.15) | collective-permute-done | bytes 131104 | tf_op jit(solution)/shard_map/ppermute | solution.py:736
  116.1 6.2 %update_pieces.4 = (bf16[512,128]{1,0:T(8,128)(2,1)S(1)}, bf16[512,128]{1,0:T(8,128)(2,1)S(1)}, bf16[512,128]{1,0:T(8,128)(2,1)S(1)}, bf16[512,128]{1,0:T(8,128)(2,1)S(1)}, bf16[512,128]{1,0:T(8,128)(2,1)S(1)}) custom-call(bf16[528,128]{1,0:T(8,128)(2,1)S(1)} %copy-done.28, bf16[528,128]{1,0:T(8,128)(2,1)S(1)} %copy-done.31, ...), custom_call_target="tpu_custom_call" | custom-call | flops 335544320 | bytes 4849664 | tf_op jit(solution)/shard_map/update_pieces/pallas_call | solution.py:713
  122.3 2.1 %collective-permute-start.20 = (bf16[512,128]{1,0:T(8,128)(2,1)S(1)}, bf16[512,128]{1,0:T(8,128)(2,1)S(1)}, u32[]{:S(2)}, u32[]{:S(2)}) collective-permute-start(bf16[512,128]{1,0:T(8,128)(2,1)S(1)} %get-tuple-element.63), channel_id=1, source_target_pairs={{0,5},{1,4},{2,7},{3,6},{4,1},{5,0},{6,3},{7,2},{8,13},{9,12},{10,... | collective-permute-start | bytes 393224 | tf_op jit(solution)/shard_map/ppermute | solution.py:736
  124.5 2.5 %collective-permute-start.19 = (bf16[512,128]{1,0:T(8,128)(2,1)S(1)}, bf16[512,128]{1,0:T(8,128)(2,1)S(1)}, u32[]{:S(2)}, u32[]{:S(2)}) collective-permute-start(bf16[512,128]{1,0:T(8,128)(2,1)S(1)} %get-tuple-element.62), channel_id=1, source_target_pairs={{0,11},{1,10},{2,9},{3,8},{4,15},{5,14},{6,13},{7,12},{8,3},{9,2},... | collective-permute-start | bytes 393224 | tf_op jit(solution)/shard_map/ppermute | solution.py:736
  127.1 1.1 collective-permute-start.22
  128.2 3.4 %collective-permute-start.23 = (bf16[512,128]{1,0:T(8,128)(2,1)S(1)}, bf16[512,128]{1,0:T(8,128)(2,1)S(1)}, u32[]{:S(2)}, u32[]{:S(2)}) collective-permute-start(bf16[512,128]{1,0:T(8,128)(2,1)S(1)} %get-tuple-element.67), channel_id=1, source_target_pairs={{0,13},{1,12},{2,15},{3,14},{4,9},{5,8},{6,11},{7,10},{8,5},{9,4},... | collective-permute-start | bytes 393224 | tf_op jit(solution)/shard_map/ppermute | solution.py:736
  132.1 6.3 %update_pieces.5 = (bf16[512,128]{1,0:T(8,128)(2,1)S(1)}, bf16[512,128]{1,0:T(8,128)(2,1)S(1)}, bf16[512,128]{1,0:T(8,128)(2,1)S(1)}, bf16[512,128]{1,0:T(8,128)...) custom-call(bf16[528,128]{1,0:T(8,128)(2,1)S(1)} %copy-done.28, bf16[528,128]{1,0:T(8,128)(2,1)S(1)} %copy-done.31, ...), custom_call_target="tpu_custom_call" | custom-call | flops 402653184 | bytes 4980736 | tf_op jit(solution)/shard_map/update_pieces/pallas_call | solution.py:713
  138.4 2.1 %collective-permute-start.25 = (bf16[512,128]{1,0:T(8,128)(2,1)S(1)}, bf16[512,128]{1,0:T(8,128)(2,1)S(1)}, u32[]{:S(2)}, u32[]{:S(2)}) collective-permute-start(bf16[512,128]{1,0:T(8,128)(2,1)S(1)} %get-tuple-element.69), channel_id=1, source_target_pairs={{0,14},{1,15},{2,12},{3,13},{4,10},{5,11},{6,8},{7,9},{8,6},{9,7},... | collective-permute-start | bytes 393224 | tf_op jit(solution)/shard_map/ppermute | solution.py:736
  140.5 1.9 %collective-permute-done.21.refs_2_ = bf16[512,128]{1,0:T(8,128)(2,1)S(1)} collective-permute-done((bf16[512,128]{1,0:T(8,128)(2,1)S(1)}, bf16[512,128]{1,0:T(8,128)(2,1)S(1)}, u32[]{:S(2)}, u32[]{:S(2)}) %collective-permute-start.21) | collective-permute-done | bytes 131104 | tf_op jit(solution)/shard_map/ppermute | solution.py:736
  142.7 1.6 collective-permute-start.27
  144.2 6.4 %collective-permute-done.23.refs_0_ = bf16[512,128]{1,0:T(8,128)(2,1)S(1)} collective-permute-done((bf16[512,128]{1,0:T(8,128)(2,1)S(1)}, bf16[512,128]{1,0:T(8,128)(2,1)S(1)}, u32[]{:S(2)}, u32[]{:S(2)}) %collective-permute-start.23) | collective-permute-done | bytes 131104 | tf_op jit(solution)/shard_map/ppermute | solution.py:736
  151.1 1.7 %collective-permute-start.29 = (bf16[512,128]{1,0:T(8,128)(2,1)S(1)}, bf16[512,128]{1,0:T(8,128)(2,1)S(1)}, u32[]{:S(2)}, u32[]{:S(2)}) collective-permute-start(bf16[512,128]{1,0:T(8,128)(2,1)S(1)} %get-tuple-element.75), channel_id=1, source_target_pairs={{0,3},{1,2},{2,1},{3,0},{4,7},{5,6},{6,5},{7,4},{8,11},{9,10},{10,... | collective-permute-start | bytes 393224 | tf_op jit(solution)/shard_map/ppermute | solution.py:736
  152.8 1.7 %join_pieces.4 = (bf16[1,1048576]{1,0:T(2,128)(2,1)}, f32[8,128]{1,0:T(8,128)}) custom-call(bf16[512,128]{1,0:T(8,128)(2,1)S(1)} %collective-permute-done.15.refs_0_.refs_22_, bf16[512,128]{1,0:T(8,128)(2,1)S(1)} %collective-permute-done.16.refs_1_, bf16[512,128]{1,0:T(8,128)(2,1)S(1)} %collective-permute-done.17.refs_2_, ...), custom_call_target="tpu_custom_call" | custom-call | bytes 1572864 | tf_op jit(solution)/shard_map/join_pieces/pallas_call | solution.py:467
  154.5 1.7 %join_pieces.5 = (bf16[1,1048576]{1,0:T(2,128)(2,1)}, f32[8,128]{1,0:T(8,128)}) custom-call(bf16[1,1048576]{1,0:T(2,128)(2,1)} %get-tuple-element.61.row_ref, bf16[512,128]{1,0:T(8,128)(2,1)S(1)} %collective-permute-done.19.refs_0_, bf16[512,128]{1,0:T(8,128)(2,1)S(1)} %collective-permute-done.20.refs_1_.refs_22_, ...), custom_call_target="tpu_custom_call", output_to_operand_aliasing={{0}: (0, {})} | custom-call | bytes 1572864 | tf_op jit(solution)/shard_map/join_pieces/pallas_call | solution.py:467
  156.2 1.7 %join_pieces.6 = (bf16[1,1048576]{1,0:T(2,128)(2,1)}, f32[8,128]{1,0:T(8,128)}) custom-call(bf16[1,1048576]{1,0:T(2,128)(2,1)} %get-tuple-element.66.row_ref, bf16[512,128]{1,0:T(8,128)(2,1)S(1)} %collective-permute-done.23.refs_0_, bf16[512,128]{1,0:T(8,128)(2,1)S(1)} %collective-permute-done.24.refs_1_, ...), custom_call_target="tpu_custom_call", output_to_operand_aliasing={{0}: (0, {})} | custom-call | bytes 1572864 | tf_op jit(solution)/shard_map/join_pieces/pallas_call | solution.py:467
  157.9 1.4 collective-permute-done.28.refs_2_
  159.3 2.8 %collective-permute-done.29.refs_3_ = bf16[512,128]{1,0:T(8,128)(2,1)S(1)} collective-permute-done((bf16[512,128]{1,0:T(8,128)(2,1)S(1)}, bf16[512,128]{1,0:T(8,128)(2,1)S(1)}, u32[]{:S(2)}, u32[]{:S(2)}) %collective-permute-start.29) | collective-permute-done | bytes 131104 | tf_op jit(solution)/shard_map/ppermute | solution.py:736
  162.1 1.7 %join_pieces.7 = (bf16[1,1048576]{1,0:T(2,128)(2,1)}, f32[8,128]{1,0:T(8,128)}) custom-call(bf16[1,1048576]{1,0:T(2,128)(2,1)} %get-tuple-element.71.row_ref, bf16[512,128]{1,0:T(8,128)(2,1)S(1)} %collective-permute-done.26.refs_0_, bf16[512,128]{1,0:T(8,128)(2,1)S(1)} %collective-permute-done.27.refs_1_, ...), custom_call_target="tpu_custom_call", output_to_operand_aliasing={{0}: (0, {})} | custom-call | bytes 1572864 | tf_op jit(solution)/shard_map/join_pieces/pallas_call | solution.py:467
  (123 shorter events, 25.3 us)
Async XLA Ops:
  2.4 9.3 %collective-permute-start = (bf16[528,128]{1,0:T(8,128)(2,1)}, bf16[528,128]{1,0:T(8,128)(2,1)S(1)}, u32[]{:S(2)}, u32[]{:S(2)}) collective-permute-start(bf16[528,128]{1,0:T(8,128)(2,1)} %get-tuple-element.41), channel_id=1, source_target_pairs={{0,8},{1,9},{2,10},{3,11},{4,12},{5,13},{6,14},{7,15},{8,0},{9,1},... | collective-permute-start | bytes 405512 | tf_op jit(solution)/shard_map/ppermute | solution.py:736
  4.8 15.1 %collective-permute-start.5 = (bf16[528,128]{1,0:T(8,128)(2,1)}, bf16[528,128]{1,0:T(8,128)(2,1)S(1)}, u32[]{:S(2)}, u32[]{:S(2)}) collective-permute-start(bf16[528,128]{1,0:T(8,128)(2,1)} %get-tuple-element.47), channel_id=1, source_target_pairs={{0,4},{1,5},{2,6},{3,7},{4,0},{5,1},{6,2},{7,3},{8,12},{9,13},{10,... | collective-permute-start | bytes 405512 | tf_op jit(solution)/shard_map/ppermute | solution.py:736
  5.0 15.7 %collective-permute-start.8 = (bf16[528,128]{1,0:T(8,128)(2,1)}, bf16[528,128]{1,0:T(8,128)(2,1)S(1)}, u32[]{:S(2)}, u32[]{:S(2)}) collective-permute-start(bf16[528,128]{1,0:T(8,128)(2,1)} %get-tuple-element.50), channel_id=1, source_target_pairs={{0,9},{1,8},{2,11},{3,10},{4,13},{5,12},{6,15},{7,14},{8,1},{9,0},... | collective-permute-start | bytes 405512 | tf_op jit(solution)/shard_map/ppermute | solution.py:736
  5.9 19.8 %collective-permute-start.9 = (bf16[528,128]{1,0:T(8,128)(2,1)}, bf16[528,128]{1,0:T(8,128)(2,1)S(1)}, u32[]{:S(2)}, u32[]{:S(2)}) collective-permute-start(bf16[528,128]{1,0:T(8,128)(2,1)} %get-tuple-element.51), channel_id=1, source_target_pairs={{0,10},{1,11},{2,8},{3,9},{4,14},{5,15},{6,12},{7,13},{8,2},{9,3},... | collective-permute-start | bytes 405512 | tf_op jit(solution)/shard_map/ppermute | solution.py:736
  11.7 2.2 %copy-start = (bf16[1,1048576]{1,0:T(2,128)(2,1)S(1)}, bf16[1,1048576]{1,0:T(2,128)(2,1)}, u32[]{:S(2)}) copy-start(bf16[1,1048576]{1,0:T(2,128)(2,1)} %row_ref.5) | copy-start | bytes 6291460
  13.9 3.0 %copy-start.45 = (bf16[528,128]{1,0:T(8,128)(2,1)S(1)}, bf16[528,128]{1,0:T(8,128)(2,1)}, u32[]{:S(2)}) copy-start(bf16[528,128]{1,0:T(8,128)(2,1)} %get-tuple-element.52) | copy-start | bytes 405508
  14.5 56.2 %copy-start.1 = (bf16[1048576]{0:T(1024)(128)(2,1)S(1)}, bf16[1048576]{0:T(1024)(128)(2,1)}, u32[]{:S(2)}) copy-start(bf16[1048576]{0:T(1024)(128)(2,1)} %param.7) | copy-start | bytes 6291460
  14.5 11.3 %collective-permute-start.1 = (bf16[528,128]{1,0:T(8,128)(2,1)S(1)}, bf16[528,128]{1,0:T(8,128)(2,1)S(1)}, u32[]{:S(2)}, u32[]{:S(2)}) collective-permute-start(bf16[528,128]{1,0:T(8,128)(2,1)S(1)} %get-tuple-element.42), channel_id=1, source_target_pairs={{0,5},{1,4},{2,7},{3,6},{4,1},{5,0},{6,3},{7,2},{8,13},{9,12},{10,... | collective-permute-start | bytes 405512 | tf_op jit(solution)/shard_map/ppermute | solution.py:736
  17.0 11.7 %collective-permute-start.10 = (bf16[528,128]{1,0:T(8,128)(2,1)S(1)}, bf16[528,128]{1,0:T(8,128)(2,1)S(1)}, u32[]{:S(2)}, u32[]{:S(2)}) collective-permute-start(bf16[528,128]{1,0:T(8,128)(2,1)S(1)} %copy-done.45), channel_id=1, source_target_pairs={{0,11},{1,10},{2,9},{3,8},{4,15},{5,14},{6,13},{7,12},{8,3},{9,2},... | collective-permute-start | bytes 405512 | tf_op jit(solution)/shard_map/ppermute | solution.py:736
  19.9 10.3 %collective-permute-start.6 = (bf16[528,128]{1,0:T(8,128)(2,1)S(1)}, bf16[528,128]{1,0:T(8,128)(2,1)S(1)}, u32[]{:S(2)}, u32[]{:S(2)}) collective-permute-start(bf16[528,128]{1,0:T(8,128)(2,1)S(1)} %get-tuple-element.48), channel_id=1, source_target_pairs={{0,6},{1,7},{2,4},{3,5},{4,2},{5,3},{6,0},{7,1},{8,14},{9,15},{10,... | collective-permute-start | bytes 405512 | tf_op jit(solution)/shard_map/ppermute | solution.py:736
  20.7 49.9 %copy-start.7 = (bf16[528,128]{1,0:T(8,128)(2,1)}, bf16[528,128]{1,0:T(8,128)(2,1)S(1)}, u32[]{:S(2)}) copy-start(bf16[528,128]{1,0:T(8,128)(2,1)S(1)} %collective-permute-done.8.refs_9_.refs_1_) | copy-start | bytes 405508
  20.7 17.5 %collective-permute-start.7 = (bf16[528,128]{1,0:T(8,128)(2,1)S(1)}, bf16[528,128]{1,0:T(8,128)(2,1)S(1)}, u32[]{:S(2)}, u32[]{:S(2)}) collective-permute-start(bf16[528,128]{1,0:T(8,128)(2,1)S(1)} %get-tuple-element.49), channel_id=1, source_target_pairs={{0,7},{1,6},{2,5},{3,4},{4,3},{5,2},{6,1},{7,0},{8,15},{9,14},{10,... | collective-permute-start | bytes 405512 | tf_op jit(solution)/shard_map/ppermute | solution.py:736
  25.7 44.9 %copy-start.9 = (bf16[528,128]{1,0:T(8,128)(2,1)}, bf16[528,128]{1,0:T(8,128)(2,1)S(1)}, u32[]{:S(2)}) copy-start(bf16[528,128]{1,0:T(8,128)(2,1)S(1)} %collective-permute-done.9.refs_10_.refs_2_) | copy-start | bytes 405508
  25.7 13.1 %collective-permute-start.11 = (bf16[528,128]{1,0:T(8,128)(2,1)S(1)}, bf16[528,128]{1,0:T(8,128)(2,1)S(1)}, u32[]{:S(2)}, u32[]{:S(2)}) collective-permute-start(bf16[528,128]{1,0:T(8,128)(2,1)S(1)} %get-tuple-element.53), channel_id=1, source_target_pairs={{0,12},{1,13},{2,14},{3,15},{4,8},{5,9},{6,10},{7,11},{8,4},{9,5},... | collective-permute-start | bytes 405512 | tf_op jit(solution)/shard_map/ppermute | solution.py:736
  25.7 17.1 %collective-permute-start.12 = (bf16[528,128]{1,0:T(8,128)(2,1)S(1)}, bf16[528,128]{1,0:T(8,128)(2,1)S(1)}, u32[]{:S(2)}, u32[]{:S(2)}) collective-permute-start(bf16[528,128]{1,0:T(8,128)(2,1)S(1)} %get-tuple-element.54), channel_id=1, source_target_pairs={{0,13},{1,12},{2,15},{3,14},{4,9},{5,8},{6,11},{7,10},{8,5},{9,4},... | collective-permute-start | bytes 405512 | tf_op jit(solution)/shard_map/ppermute | solution.py:736
  28.7 14.9 %collective-permute-start.2 = (bf16[528,128]{1,0:T(8,128)(2,1)S(1)}, bf16[528,128]{1,0:T(8,128)(2,1)S(1)}, u32[]{:S(2)}, u32[]{:S(2)}) collective-permute-start(bf16[528,128]{1,0:T(8,128)(2,1)S(1)} %get-tuple-element.44), channel_id=1, source_target_pairs={{0,1},{1,0},{2,3},{3,2},{4,5},{5,4},{6,7},{7,6},{8,9},{9,8},{10,11... | collective-permute-start | bytes 405512 | tf_op jit(solution)/shard_map/ppermute | solution.py:736
  30.2 40.4 %copy-start.14 = (bf16[528,128]{1,0:T(8,128)(2,1)}, bf16[528,128]{1,0:T(8,128)(2,1)S(1)}, u32[]{:S(2)}) copy-start(bf16[528,128]{1,0:T(8,128)(2,1)S(1)} %collective-permute-done.6.refs_6_.refs_3_) | copy-start | bytes 405508
  30.2 13.4 %collective-permute-start.3 = (bf16[528,128]{1,0:T(8,128)(2,1)S(1)}, bf16[528,128]{1,0:T(8,128)(2,1)S(1)}, u32[]{:S(2)}, u32[]{:S(2)}) collective-permute-start(bf16[528,128]{1,0:T(8,128)(2,1)S(1)} %get-tuple-element.45), channel_id=1, source_target_pairs={{0,2},{1,3},{2,0},{3,1},{4,6},{5,7},{6,4},{7,5},{8,10},{9,11},{10,... | collective-permute-start | bytes 405512 | tf_op jit(solution)/shard_map/ppermute | solution.py:736
  38.2 32.5 %copy-start.17 = (bf16[528,128]{1,0:T(8,128)(2,1)}, bf16[528,128]{1,0:T(8,128)(2,1)S(1)}, u32[]{:S(2)}) copy-start(bf16[528,128]{1,0:T(8,128)(2,1)S(1)} %collective-permute-done.7.refs_7_.refs_1_) | copy-start | bytes 405508
  38.2 5.4 %collective-permute-start.4 = (bf16[528,128]{1,0:T(8,128)(2,1)S(1)}, bf16[528,128]{1,0:T(8,128)(2,1)S(1)}, u32[]{:S(2)}, u32[]{:S(2)}) collective-permute-start(bf16[528,128]{1,0:T(8,128)(2,1)S(1)} %get-tuple-element.46), channel_id=1, source_target_pairs={{0,3},{1,2},{2,1},{3,0},{4,7},{5,6},{6,5},{7,4},{8,11},{9,10},{10,... | collective-permute-start | bytes 405512 | tf_op jit(solution)/shard_map/ppermute | solution.py:736
  38.9 31.7 %copy-start.20 = (bf16[528,128]{1,0:T(8,128)(2,1)}, bf16[528,128]{1,0:T(8,128)(2,1)S(1)}, u32[]{:S(2)}) copy-start(bf16[528,128]{1,0:T(8,128)(2,1)S(1)} %collective-permute-done.11.refs_12_.refs_2_) | copy-start | bytes 405508
  38.9 7.8 %collective-permute-start.13 = (bf16[528,128]{1,0:T(8,128)(2,1)S(1)}, bf16[528,128]{1,0:T(8,128)(2,1)S(1)}, u32[]{:S(2)}, u32[]{:S(2)}) collective-permute-start(bf16[528,128]{1,0:T(8,128)(2,1)S(1)} %get-tuple-element.55), channel_id=1, source_target_pairs={{0,14},{1,15},{2,12},{3,13},{4,10},{5,11},{6,8},{7,9},{8,6},{9,7},... | collective-permute-start | bytes 405512 | tf_op jit(solution)/shard_map/ppermute | solution.py:736
  42.8 27.8 %copy-start.23 = (bf16[528,128]{1,0:T(8,128)(2,1)}, bf16[528,128]{1,0:T(8,128)(2,1)S(1)}, u32[]{:S(2)}) copy-start(bf16[528,128]{1,0:T(8,128)(2,1)S(1)} %collective-permute-done.12.refs_13_.refs_0_) | copy-start | bytes 405508
  42.8 12.7 %collective-permute-start.14 = (bf16[528,128]{1,0:T(8,128)(2,1)S(1)}, bf16[528,128]{1,0:T(8,128)(2,1)S(1)}, u32[]{:S(2)}, u32[]{:S(2)}) collective-permute-start(bf16[528,128]{1,0:T(8,128)(2,1)S(1)} %get-tuple-element.56), channel_id=1, source_target_pairs={{0,15},{1,14},{2,13},{3,12},{4,11},{5,10},{6,9},{7,8},{8,7},{9,6},... | collective-permute-start | bytes 405512 | tf_op jit(solution)/shard_map/ppermute | solution.py:736
  63.4 18.7 %all-to-all-start = ((f32[16,16,128]{2,1,0:T(8,128)}), f32[16,16,128]{2,1,0:T(8,128)}, u32[]{:S(2)}, u32[]{:S(2)}) async-start(f32[16,16,128]{2,1,0:T(8,128)} %copy-done.44), calls=%async_computation | async-start | bytes 262144 | tf_op jit(solution)/shard_map/all_to_all | solution.py:360
  72.3 4.6 %copy-start.30 = (bf16[528,128]{1,0:T(8,128)(2,1)S(1)}, bf16[528,128]{1,0:T(8,128)(2,1)}, u32[]{:S(2)}) copy-start(bf16[528,128]{1,0:T(8,128)(2,1)} %copy-done.29) | copy-start | bytes 405508
  72.3 4.6 %copy-start.33 = (bf16[528,128]{1,0:T(8,128)(2,1)S(1)}, bf16[528,128]{1,0:T(8,128)(2,1)}, u32[]{:S(2)}) copy-start(bf16[528,128]{1,0:T(8,128)(2,1)} %copy-done.32) | copy-start | bytes 405508
  72.3 4.6 %copy-start.36 = (bf16[528,128]{1,0:T(8,128)(2,1)S(1)}, bf16[528,128]{1,0:T(8,128)(2,1)}, u32[]{:S(2)}) copy-start(bf16[528,128]{1,0:T(8,128)(2,1)} %copy-done.35) | copy-start | bytes 405508
  72.3 4.6 %copy-start.42 = (bf16[528,128]{1,0:T(8,128)(2,1)S(1)}, bf16[528,128]{1,0:T(8,128)(2,1)}, u32[]{:S(2)}) copy-start(bf16[528,128]{1,0:T(8,128)(2,1)} %copy-done.41) | copy-start | bytes 405508
  75.0 4.5 %copy-start.18 = (bf16[528,128]{1,0:T(8,128)(2,1)S(1)}, bf16[528,128]{1,0:T(8,128)(2,1)}, u32[]{:S(2)}) copy-start(bf16[528,128]{1,0:T(8,128)(2,1)} %copy-done.17) | copy-start | bytes 405508
  75.0 4.5 %copy-start.24 = (bf16[528,128]{1,0:T(8,128)(2,1)S(1)}, bf16[528,128]{1,0:T(8,128)(2,1)}, u32[]{:S(2)}) copy-start(bf16[528,128]{1,0:T(8,128)(2,1)} %copy-done.23) | copy-start | bytes 405508
  75.0 4.5 %copy-start.27 = (bf16[528,128]{1,0:T(8,128)(2,1)S(1)}, bf16[528,128]{1,0:T(8,128)(2,1)}, u32[]{:S(2)}) copy-start(bf16[528,128]{1,0:T(8,128)(2,1)} %copy-done.26) | copy-start | bytes 405508
  75.0 4.5 %copy-start.39 = (bf16[528,128]{1,0:T(8,128)(2,1)S(1)}, bf16[528,128]{1,0:T(8,128)(2,1)}, u32[]{:S(2)}) copy-start(bf16[528,128]{1,0:T(8,128)(2,1)} %copy-done.38) | copy-start | bytes 405508
  102.3 13.7 %collective-permute-start.15 = (bf16[512,128]{1,0:T(8,128)(2,1)S(1)}, bf16[512,128]{1,0:T(8,128)(2,1)S(1)}, u32[]{:S(2)}, u32[]{:S(2)}) collective-permute-start(bf16[512,128]{1,0:T(8,128)(2,1)S(1)} %get-tuple-element.57), channel_id=1, source_target_pairs={{0,8},{1,9},{2,10},{3,11},{4,12},{5,13},{6,14},{7,15},{8,0},{9,1},... | collective-permute-start | bytes 393224 | tf_op jit(solution)/shard_map/ppermute | solution.py:736
  104.5 22.5 %collective-permute-start.16 = (bf16[512,128]{1,0:T(8,128)(2,1)S(1)}, bf16[512,128]{1,0:T(8,128)(2,1)S(1)}, u32[]{:S(2)}, u32[]{:S(2)}) collective-permute-start(bf16[512,128]{1,0:T(8,128)(2,1)S(1)} %get-tuple-element.58), channel_id=1, source_target_pairs={{0,9},{1,8},{2,11},{3,10},{4,13},{5,12},{6,15},{7,14},{8,1},{9,0},... | collective-permute-start | bytes 393224 | tf_op jit(solution)/shard_map/ppermute | solution.py:736
  105.3 21.8 %collective-permute-start.17 = (bf16[512,128]{1,0:T(8,128)(2,1)S(1)}, bf16[512,128]{1,0:T(8,128)(2,1)S(1)}, u32[]{:S(2)}, u32[]{:S(2)}) collective-permute-start(bf16[512,128]{1,0:T(8,128)(2,1)S(1)} %get-tuple-element.59), channel_id=1, source_target_pairs={{0,10},{1,11},{2,8},{3,9},{4,14},{5,15},{6,12},{7,13},{8,2},{9,3},... | collective-permute-start | bytes 393224 | tf_op jit(solution)/shard_map/ppermute | solution.py:736
  108.3 19.9 %collective-permute-start.18 = (bf16[512,128]{1,0:T(8,128)(2,1)S(1)}, bf16[512,128]{1,0:T(8,128)(2,1)S(1)}, u32[]{:S(2)}, u32[]{:S(2)}) collective-permute-start(bf16[512,128]{1,0:T(8,128)(2,1)S(1)} %get-tuple-element.60), channel_id=1, source_target_pairs={{0,4},{1,5},{2,6},{3,7},{4,0},{5,1},{6,2},{7,3},{8,12},{9,13},{10,... | collective-permute-start | bytes 393224 | tf_op jit(solution)/shard_map/ppermute | solution.py:736
  122.3 9.3 %collective-permute-start.20 = (bf16[512,128]{1,0:T(8,128)(2,1)S(1)}, bf16[512,128]{1,0:T(8,128)(2,1)S(1)}, u32[]{:S(2)}, u32[]{:S(2)}) collective-permute-start(bf16[512,128]{1,0:T(8,128)(2,1)S(1)} %get-tuple-element.63), channel_id=1, source_target_pairs={{0,5},{1,4},{2,7},{3,6},{4,1},{5,0},{6,3},{7,2},{8,13},{9,12},{10,... | collective-permute-start | bytes 393224 | tf_op jit(solution)/shard_map/ppermute | solution.py:736
  124.5 13.9 %collective-permute-start.19 = (bf16[512,128]{1,0:T(8,128)(2,1)S(1)}, bf16[512,128]{1,0:T(8,128)(2,1)S(1)}, u32[]{:S(2)}, u32[]{:S(2)}) collective-permute-start(bf16[512,128]{1,0:T(8,128)(2,1)S(1)} %get-tuple-element.62), channel_id=1, source_target_pairs={{0,11},{1,10},{2,9},{3,8},{4,15},{5,14},{6,13},{7,12},{8,3},{9,2},... | collective-permute-start | bytes 393224 | tf_op jit(solution)/shard_map/ppermute | solution.py:736
  127.0 15.4 %collective-permute-start.21 = (bf16[512,128]{1,0:T(8,128)(2,1)S(1)}, bf16[512,128]{1,0:T(8,128)(2,1)S(1)}, u32[]{:S(2)}, u32[]{:S(2)}) collective-permute-start(bf16[512,128]{1,0:T(8,128)(2,1)S(1)} %get-tuple-element.64), channel_id=1, source_target_pairs={{0,12},{1,13},{2,14},{3,15},{4,8},{5,9},{6,10},{7,11},{8,4},{9,5},... | collective-permute-start | bytes 393224 | tf_op jit(solution)/shard_map/ppermute | solution.py:736
  127.1 15.6 %collective-permute-start.22 = (bf16[512,128]{1,0:T(8,128)(2,1)S(1)}, bf16[512,128]{1,0:T(8,128)(2,1)S(1)}, u32[]{:S(2)}, u32[]{:S(2)}) collective-permute-start(bf16[512,128]{1,0:T(8,128)(2,1)S(1)} %get-tuple-element.65), channel_id=1, source_target_pairs={{0,6},{1,7},{2,4},{3,5},{4,2},{5,3},{6,0},{7,1},{8,14},{9,15},{10,... | collective-permute-start | bytes 393224 | tf_op jit(solution)/shard_map/ppermute | solution.py:736
  128.2 22.5 %collective-permute-start.23 = (bf16[512,128]{1,0:T(8,128)(2,1)S(1)}, bf16[512,128]{1,0:T(8,128)(2,1)S(1)}, u32[]{:S(2)}, u32[]{:S(2)}) collective-permute-start(bf16[512,128]{1,0:T(8,128)(2,1)S(1)} %get-tuple-element.67), channel_id=1, source_target_pairs={{0,13},{1,12},{2,15},{3,14},{4,9},{5,8},{6,11},{7,10},{8,5},{9,4},... | collective-permute-start | bytes 393224 | tf_op jit(solution)/shard_map/ppermute | solution.py:736
  131.6 19.5 %collective-permute-start.24 = (bf16[512,128]{1,0:T(8,128)(2,1)S(1)}, bf16[512,128]{1,0:T(8,128)(2,1)S(1)}, u32[]{:S(2)}, u32[]{:S(2)}) collective-permute-start(bf16[512,128]{1,0:T(8,128)(2,1)S(1)} %get-tuple-element.68), channel_id=1, source_target_pairs={{0,7},{1,6},{2,5},{3,4},{4,3},{5,2},{6,1},{7,0},{8,15},{9,14},{10,... | collective-permute-start | bytes 393224 | tf_op jit(solution)/shard_map/ppermute | solution.py:736
  138.4 17.8 %collective-permute-start.25 = (bf16[512,128]{1,0:T(8,128)(2,1)S(1)}, bf16[512,128]{1,0:T(8,128)(2,1)S(1)}, u32[]{:S(2)}, u32[]{:S(2)}) collective-permute-start(bf16[512,128]{1,0:T(8,128)(2,1)S(1)} %get-tuple-element.69), channel_id=1, source_target_pairs={{0,14},{1,15},{2,12},{3,13},{4,10},{5,11},{6,8},{7,9},{8,6},{9,7},... | collective-permute-start | bytes 393224 | tf_op jit(solution)/shard_map/ppermute | solution.py:736
  142.4 15.5 %collective-permute-start.26 = (bf16[512,128]{1,0:T(8,128)(2,1)S(1)}, bf16[512,128]{1,0:T(8,128)(2,1)S(1)}, u32[]{:S(2)}, u32[]{:S(2)}) collective-permute-start(bf16[512,128]{1,0:T(8,128)(2,1)S(1)} %get-tuple-element.72), channel_id=1, source_target_pairs={{0,1},{1,0},{2,3},{3,2},{4,5},{5,4},{6,7},{7,6},{8,9},{9,8},{10,11... | collective-permute-start | bytes 393224 | tf_op jit(solution)/shard_map/ppermute | solution.py:736
  142.7 15.2 %collective-permute-start.27 = (bf16[512,128]{1,0:T(8,128)(2,1)S(1)}, bf16[512,128]{1,0:T(8,128)(2,1)S(1)}, u32[]{:S(2)}, u32[]{:S(2)}) collective-permute-start(bf16[512,128]{1,0:T(8,128)(2,1)S(1)} %get-tuple-element.73), channel_id=1, source_target_pairs={{0,15},{1,14},{2,13},{3,12},{4,11},{5,10},{6,9},{7,8},{8,7},{9,6},... | collective-permute-start | bytes 393224 | tf_op jit(solution)/shard_map/ppermute | solution.py:736
  150.7 8.6 %collective-permute-start.28 = (bf16[512,128]{1,0:T(8,128)(2,1)S(1)}, bf16[512,128]{1,0:T(8,128)(2,1)S(1)}, u32[]{:S(2)}, u32[]{:S(2)}) collective-permute-start(bf16[512,128]{1,0:T(8,128)(2,1)S(1)} %get-tuple-element.74), channel_id=1, source_target_pairs={{0,2},{1,3},{2,0},{3,1},{4,6},{5,7},{6,4},{7,5},{8,10},{9,11},{10,... | collective-permute-start | bytes 393224 | tf_op jit(solution)/shard_map/ppermute | solution.py:736
  151.1 11.0 %collective-permute-start.29 = (bf16[512,128]{1,0:T(8,128)(2,1)S(1)}, bf16[512,128]{1,0:T(8,128)(2,1)S(1)}, u32[]{:S(2)}, u32[]{:S(2)}) collective-permute-start(bf16[512,128]{1,0:T(8,128)(2,1)S(1)} %get-tuple-element.75), channel_id=1, source_target_pairs={{0,3},{1,2},{2,1},{3,0},{4,7},{5,6},{6,5},{7,4},{8,11},{9,10},{10,... | collective-permute-start | bytes 393224 | tf_op jit(solution)/shard_map/ppermute | solution.py:736
  (29 other events, 26.9 us)

commit v6 on v5

--- a/solution.py
+++ b/solution.py
@@ -34,6 +34,12 @@
 
 IN_VMEM = pl.BlockSpec(memory_space=pltpu.VMEM)
 IN_HBM = pl.BlockSpec(memory_space=pltpu.HBM)
+
+
+def in_hbm(array):
+    return pltpu.with_memory_space_constraint(array, pltpu.HBM)
+
+
 BLOCK = 4 * TILE
 
 
@@ -99,7 +105,6 @@
         functools.partial(split_body, lines, begin, rim, len(fields), len(numbers)),
         "split_row",
         moved=6 * slabs * count * LANES,
-        limit=60,
         in_specs=[IN_HBM] * (1 + len(fields)) + [IN_VMEM] * len(numbers) + [IN_HBM] * len(earlier),
         out_specs=[IN_VMEM] * (2 + len(fields)),
         out_shape=[jax.ShapeDtypeStruct((slabs, count + TILE * rim, LANES), BF16)]
@@ -360,36 +365,37 @@
     return lax.all_to_all(slabs, "slab", split_axis=0, concat_axis=0, tiled=True)
 
 
-def partner(k):
-    return lax.axis_index("slab").astype(jnp.int32) ^ k
+def device_at(at, half):
+    me = lax.axis_index("slab").astype(jnp.int32)
+    return jnp.where(at < half, me - me % half + at, me ^ at)
 
 
 def lines_of(start, count):
     return pl.ds(pl.multiple_of(start, TILE), count)
 
 
-def split_pieces_body(ks, half, raw, lines, gates, row_ref, *refs):
+def split_pieces_body(positions, half, raw, lines, gates, row_ref, *refs):
     refs = refs[gates:]
-    count = len(ks)
-    out_refs, helds, sems = refs[:count], refs[count : 2 * count], refs[2 * count]
+    count = len(positions)
+    out_refs, helds, sems = refs[: -count - 1], refs[-count - 1 : -1], refs[-1]
     cells = lines * LANES
     end = row_ref.shape[1]
     copies = []
-    for k, held in zip(ks, helds):
+    for at, held in zip(positions, helds):
         mine = []
 
         def fetch(start, size, to):
             source = row_ref.at[:, pl.ds(pl.multiple_of(start, GRID_Y), size)]
-            at = sems.at[len(copies) * 5 + len(mine)]
-            mine.append(pltpu.make_async_copy(source, held.at[:, pl.ds(to, size)], at))
+            sem = sems.at[len(copies) * 5 + len(mine)]
+            mine.append(pltpu.make_async_copy(source, held.at[:, pl.ds(to, size)], sem))
             mine[-1].start()
 
-        slab = partner(k)
+        slab = device_at(at, half)
         fetch(slab * cells, cells, 0)
         fetch(jnp.minimum((slab + 1) * cells, end - GRID_Y), GRID_Y, cells)
         fetch(jnp.maximum(slab * cells - GRID_Y, 0), GRID_Y, cells + GRID_Y)
-        if raw and k < half:
-            other = partner(k ^ half)
+        if raw and at < half:
+            other = slab ^ half
             fetch(other * cells, raw * LANES + GRID_Y, cells + 2 * GRID_Y)
             fetch(jnp.maximum(other * cells - GRID_Y, 0), GRID_Y, cells + 3 * GRID_Y + raw * LANES)
         copies.append(mine)
@@ -397,101 +403,101 @@
     def grid_row(held, at):
         return held[:, pl.ds(at, GRID_Y)].astype(F32).reshape(LINE, LANES)
 
-    for k, held, out_ref, mine in zip(ks, helds, out_refs, copies):
+    for n, (at, held, mine) in enumerate(zip(positions, helds, copies)):
+        out_ref = out_refs[n] if at >= half else out_refs[0].at[n]
         for copy in mine:
             copy.wait()
-        slab = partner(k)
+        slab = device_at(at, half)
         out_ref[:lines, :] = held[:, :cells].reshape(lines, LANES)
         below = jnp.where(slab == end // cells - 1, 0.0, grid_row(held, cells))
         above = jnp.where(slab == 0, 0.0, grid_row(held, cells + GRID_Y))
         out_ref[lines : lines + TILE, :] = jnp.concatenate([below, above], axis=0).astype(BF16)
-        if raw and k < half:
-            at = cells + 2 * GRID_Y
+        if raw and at < half:
+            start = cells + 2 * GRID_Y
             to = lines + TILE
-            out_ref[to : to + raw, :] = held[:, at : at + raw * LANES].reshape(raw, LANES)
-            below = grid_row(held, at + raw * LANES)
-            above = jnp.where(partner(k ^ half) == 0, 0.0, grid_row(held, at + raw * LANES + GRID_Y))
+            out_ref[to : to + raw, :] = held[:, start : start + raw * LANES].reshape(raw, LANES)
+            below = grid_row(held, start + raw * LANES)
+            above = jnp.where(slab ^ half == 0, 0.0, grid_row(held, start + raw * LANES + GRID_Y))
             out_ref[to + raw :, :] = jnp.concatenate([below, above], axis=0).astype(BF16)
 
 
-def split_pieces(row, slabs, raw, ks, gates):
+def split_pieces(row, slabs, raw, near, gates):
     lines = row.shape[1] // slabs // LANES
     half = slabs // 2
-    extra = [raw if k < half else 0 for k in ks]
-    sizes = [lines + TILE + (more + TILE if more else 0) for more in extra]
-    return call(
-        functools.partial(split_pieces_body, ks, half, raw, lines, len(gates)),
+    count = half
+    size = lines + TILE + (raw + TILE if near and raw else 0)
+    if near:
+        out_shape = [jax.ShapeDtypeStruct((count, size, LANES), BF16)]
+    else:
+        out_shape = [jax.ShapeDtypeStruct((size, LANES), BF16)] * count
+    positions = range(half) if near else range(half, slabs)
+    return call(
+        functools.partial(split_pieces_body, positions, half, raw, lines, len(gates)),
         "split_pieces",
-        moved=6 * sum(sizes) * LANES,
-        limit=16 if gates else 60,
+        moved=6 * count * size * LANES,
         in_specs=[IN_HBM] + [IN_VMEM] * len(gates),
-        out_specs=[IN_VMEM] * len(ks),
-        out_shape=[jax.ShapeDtypeStruct((size, LANES), BF16) for size in sizes],
-        scratch_shapes=[pltpu.VMEM((1, (size + TILE) * LANES), BF16) for size in sizes]
-        + [pltpu.SemaphoreType.DMA((5 * len(ks),))],
+        out_specs=[IN_VMEM] * len(out_shape),
+        out_shape=out_shape,
+        scratch_shapes=[pltpu.VMEM((1, (size + TILE) * LANES), BF16)] * count + [pltpu.SemaphoreType.DMA((5 * count,))],
     )(row, *gates)
 
 
-def join_pieces_body(ks, half, raw, lines, row_ref, *refs):
-    count = len(ks)
-    pieces = refs[:count]
-    row_ref, token_ref, *helds, sems = refs[count:]
+def join_pieces_body(positions, half, raw, lines, begun, *refs):
+    count = len(positions)
+    pieces, row_ref, helds, sems = refs[begun : -count - 2], refs[-count - 2], refs[-count - 1 : -1], refs[-1]
     cells = lines * LANES
     skip = raw * LANES
     copies = []
-    for k, piece, held in zip(ks, pieces, helds):
-        near = k < half
-        held[...] = piece[...].reshape(held.shape)
-
-        def store(at, size, start):
+    for n, (at, held) in enumerate(zip(positions, helds)):
+        piece = pieces[n][...] if at >= half else pieces[0][n]
+        held[...] = piece.reshape(held.shape)
+
+        def store(begin, size, start):
             target = row_ref.at[:, pl.ds(pl.multiple_of(start, GRID_Y), size)]
-            copies.append(pltpu.make_async_copy(held.at[:, pl.ds(at, size)], target, sems.at[len(copies)]))
+            copies.append(pltpu.make_async_copy(held.at[:, pl.ds(begin, size)], target, sems.at[len(copies)]))
             copies[-1].start()
 
-        if near:
-            store(0, cells, partner(k) * cells)
+        slab = device_at(at, half)
+        if at >= half:
+            store(0, cells - skip, slab * cells + skip)
+        else:
+            store(0, cells, slab * cells)
             if raw:
-                store(cells, skip, partner(k ^ half) * cells)
-        else:
-            store(0, cells - skip, partner(k) * cells + skip)
+                store(cells, skip, (slab ^ half) * cells)
     for copy in copies:
         copy.wait()
-    token_ref[...] = jnp.zeros_like(token_ref)
-
-
-def join_pieces(row, slabs, raw, pieces, ks):
+
+
+def join_pieces(row, slabs, raw, pieces, positions):
     cells = NCELL // slabs
-    out = jax.ShapeDtypeStruct((1, NCELL), BF16)
-    token = jax.ShapeDtypeStruct((8, LANES), F32)
-    body = functools.partial(join_pieces_body, ks, slabs // 2, raw, cells // LANES)
-    return call(
-        body if row is not None else functools.partial(body, None),
+    size = pieces[0].shape[-2] * LANES
+    begun = [] if row is None else [row]
+    return call(
+        functools.partial(join_pieces_body, positions, slabs // 2, raw, cells // LANES, len(begun)),
         "join_pieces",
-        moved=6 * sum(piece.size for piece in pieces),
-        in_specs=([] if row is None else [IN_HBM]) + [IN_VMEM] * len(ks),
-        out_specs=[IN_HBM, IN_VMEM],
-        out_shape=[out, token],
-        input_output_aliases={} if row is None else {0: 0},
-        scratch_shapes=[pltpu.VMEM((1, piece.size), BF16) for piece in pieces]
-        + [pltpu.SemaphoreType.DMA((2 * len(ks),))],
-    )(*([] if row is None else [row]), *pieces)
-
-
-def swap_order(total):
+        moved=6 * size * len(positions),
+        in_specs=[IN_HBM] * len(begun) + [IN_VMEM] * len(pieces),
+        out_specs=IN_HBM,
+        out_shape=jax.ShapeDtypeStruct((1, NCELL), BF16),
+        input_output_aliases={0: 0} if begun else {},
+        scratch_shapes=[pltpu.VMEM((1, size), BF16)] * len(positions)
+        + [pltpu.SemaphoreType.DMA((2 * len(positions),))],
+    )(*begun, *pieces)
+
+
+def reorder(gram, back):
+    total = gram.shape[0]
     row = lax.broadcasted_iota(jnp.int32, (total, total), 0)
     col = lax.broadcasted_iota(jnp.int32, (total, total), 1)
-    return (row == partner(col)).astype(F32)
-
-
-def reorder(gram):
-    order = swap_order(gram.shape[0])
-    half = jnp.dot(order, gram, precision=lax.Precision.HIGHEST, preferred_element_type=F32)
-    return jnp.dot(half, order, precision=lax.Precision.HIGHEST, preferred_element_type=F32)
-
-
-def gram_pieces_body(lines, *refs):
-    pieces, out_ref, pairs = refs[:-2], refs[-2], refs[-1]
-    total = len(pieces)
+    left = (col == device_at(row, total // 2) if back else row == device_at(col, total // 2)).astype(F32)
+    right = (row == device_at(col, total // 2) if back else col == device_at(row, total // 2)).astype(F32)
+    exact = {"precision": lax.Precision.HIGHEST, "preferred_element_type": F32}
+    return jnp.dot(jnp.dot(left, gram, **exact), right, **exact)
+
+
+def gram_pieces_body(lines, total, near_ref, *refs):
+    half = total // 2
+    pieces, out_ref, pairs = refs[:half], refs[-2], refs[-1]
     wide = total * TILE
     tiles = 4
     pairs[...] = jnp.zeros_like(pairs)
@@ -500,7 +506,8 @@
         parts = []
         for t in range(tiles):
             at = lines_of((i * tiles + t) * TILE, TILE)
-            parts.append(jnp.concatenate([piece[at, :] for piece in pieces], axis=0))
+            near = near_ref[:, at, :].reshape(wide // 2, LANES)
+            parts.append(jnp.concatenate([near] + [piece[at, :] for piece in pieces], axis=0))
         block = jnp.concatenate(parts, axis=1)
         pairs[...] += lax.dot_general(block, block, (((1,), (1,)), ((), ())), preferred_element_type=F32)
         return carry
@@ -509,33 +516,36 @@
     equal = jnp.where(same_line(total), pairs[...], 0.0)
     rows = jnp.sum(equal.reshape(total, TILE, wide), axis=1)
     gram = jnp.dot(rows, members(total, F32), precision=lax.Precision.HIGHEST, preferred_element_type=F32)
-    gram = jnp.concatenate([reorder(gram), jnp.zeros((total, LANES - total), F32)], axis=1)
+    gram = jnp.concatenate([reorder(gram, False), jnp.zeros((total, LANES - total), F32)], axis=1)
     out_ref[...] = jnp.broadcast_to(gram[None], out_ref.shape)
 
 
-def gram_pieces(pieces, lines):
-    total = len(pieces)
-    wide = total * TILE
-    return call(
-        functools.partial(gram_pieces_body, lines),
+def gram_pieces(near, far, lines, gates):
+    total = 2 * len(far)
+    wide = total * TILE
+    return call(
+        functools.partial(gram_pieces_body, lines, total),
         "gram_pieces",
         flops=2 * wide * wide * LANES * (lines // TILE),
         moved=2 * total * lines * LANES,
-        in_specs=[IN_VMEM] * total,
+        in_specs=[IN_VMEM] * (1 + len(far)) + [IN_HBM] * len(gates),
         out_specs=IN_VMEM,
         out_shape=jax.ShapeDtypeStruct((total, total, LANES), F32),
         scratch_shapes=[pltpu.VMEM((wide, wide), F32)],
-    )(*pieces)
-
-
-def gradient_pieces_body(k, lines, count, views, arrays, *refs):
-    observed_ref, precision_ref, out_ref, observed, precision, grads, sems = refs[arrays:]
+    )(near, *far, *gates)
+
+
+def gradient_pieces_body(k, lines, count, views, arrays, numbers, *refs):
+    observed_ref, precision_ref, *number_refs = refs[arrays : arrays + 2 + numbers]
+    out_ref, rows_ref, observed, precision, grads, sems = refs[-6:]
+    for n, number_ref in enumerate(number_refs):
+        rows_ref[n : n + 1, :] = jnp.full((1, LANES), number_ref[0], F32)
     rows = BLOCK // LINE
     shape = (rows, LINE, LANES)
     lane = lax.broadcasted_iota(jnp.int32, (1, LINE, LANES), 2)
     line = lax.broadcasted_iota(jnp.int32, (1, LINE, LANES), 1)
     steps = count // BLOCK
-    mine = lines_of(partner(k) * lines, count)
+    mine = lines_of((lax.axis_index("slab").astype(jnp.int32) ^ k) * lines, count)
     fetches = [
         pltpu.make_async_copy(observed_ref.at[mine, :], observed, sems.at[steps]),
         pltpu.make_async_copy(precision_ref.at[mine, :], precision, sems.at[steps + 1]),
@@ -588,68 +598,68 @@
     lax.fori_loop(0, steps, finish, 0)
 
 
-def gradient_pieces(arrays, views, observed, precision, lines, count, k):
-    out = jax.ShapeDtypeStruct((len(views), count, LANES), BF16)
-    return call(
-        functools.partial(gradient_pieces_body, k, lines, count, views, len(arrays)),
+def gradient_pieces(arrays, views, observed, precision, lines, count, k, numbers):
+    out = pltpu.HBM((len(views), count, LANES), BF16)
+    size = len(views) * count * LANES
+    return call(
+        functools.partial(gradient_pieces_body, k, lines, count, views, len(arrays), len(numbers)),
         "gradient_pieces",
-        flops=30 * out.size,
-        moved=8 * out.size,
-        in_specs=[IN_VMEM] * len(arrays) + [IN_HBM, IN_HBM],
-        out_specs=IN_HBM,
-        out_shape=out,
+        flops=30 * size,
+        moved=8 * size,
+        in_specs=[IN_VMEM] * len(arrays)
+        + [IN_HBM, IN_HBM]
+        + [pl.BlockSpec(memory_space=pltpu.SMEM)] * len(numbers),
+        out_specs=[IN_HBM, IN_VMEM],
+        out_shape=[out, jax.ShapeDtypeStruct((8, LANES), F32)],
         scratch_shapes=[
             pltpu.VMEM((count, LANES), BF16),
             pltpu.VMEM((count, LANES), BF16),
             pltpu.VMEM(out.shape, BF16),
             pltpu.SemaphoreType.DMA((count // BLOCK + 2,)),
         ],
-    )(*arrays, observed, precision)
-
-
-def raw_body(raw, lines, *refs):
-    out_ref = refs[-1]
-    for k, piece in enumerate(refs[:-1]):
-        out_ref[k, :raw, :] = piece[:raw, :]
-        below = piece[raw : raw + TILE, :].astype(F32)[:LINE]
-        above = piece[lines : lines + TILE, :].astype(F32)[LINE:]
+    )(*arrays, observed, precision, *numbers)
+
+
+def raw_body(raw, lines, near_ref, out_ref):
+    for k in range(near_ref.shape[0]):
+        out_ref[k, :raw, :] = near_ref[k, :raw, :]
+        below = near_ref[k, raw : raw + TILE, :].astype(F32)[:LINE]
+        above = near_ref[k, lines : lines + TILE, :].astype(F32)[LINE:]
         out_ref[k, raw:, :] = jnp.concatenate([below, above], axis=0).astype(BF16)
 
 
-def raw_states(pieces, raw, lines):
-    out = jax.ShapeDtypeStruct((len(pieces), raw + TILE, LANES), BF16)
+def raw_states(near, raw, lines):
+    out = jax.ShapeDtypeStruct((near.shape[0], raw + TILE, LANES), BF16)
     return call(
         functools.partial(raw_body, raw, lines),
         "raw_states",
         moved=4 * out.size,
-        in_specs=[IN_VMEM] * len(pieces),
+        in_specs=[IN_VMEM],
         out_specs=IN_VMEM,
         out_shape=out,
-    )(*pieces)
-
-
-def update_pieces_body(ks, half, raw, lines, groups, extra, *refs):
+    )(near)
+
+
+def update_pieces_body(near, half, raw, lines, groups, extra, near_ref, *refs):
     total = 2 * half
-    pieces, refs = refs[:total], refs[total:]
-    scalars_ref, grams_ref, *refs = refs
+    far_refs, numbers_ref, grams_ref, refs = refs[:half], refs[half], refs[half + 1], refs[half + 2 :]
     group_refs, refs = refs[: len(groups)], refs[len(groups) :]
-    raw_refs, refs = refs[:extra], refs[extra:]
-    out_refs = refs[-len(ks) - 5 : -5]
-    grads, raw_grads, mixer, own, sems = refs[-5:]
-    wide = total * TILE
-    high = len(ks) * TILE
+    raw_refs, out_refs, (grads, raw_grads, mixer, own, sems) = refs[:extra], refs[extra:-5], refs[-5:]
+    wide = total * TILE
+    high = half * TILE
+    first = 0 if near else high
     fetches = []
     for group, group_ref in zip(groups, group_refs):
-        for j, k in enumerate(group):
-            fetches.append(pltpu.make_async_copy(group_ref.at[j], grads.at[k], sems.at[len(fetches)]))
+        for j, at in enumerate(group):
+            fetches.append(pltpu.make_async_copy(group_ref.at[j], grads.at[at], sems.at[len(fetches)]))
     if extra:
         fetches.append(pltpu.make_async_copy(raw_refs[1], raw_grads, sems.at[len(fetches)]))
     for fetch in fetches:
         fetch.start()
-    spread, anneal, step_size = (scalars_ref[k : k + 1, :1] for k in range(3))
+    gram = reorder(jnp.sum(grams_ref[...], axis=0)[:, :total], True)
+    spread, anneal, step_size = (numbers_ref[k : k + 1, :1] for k in range(3))
     rate = step_size / total
     coeff = 2.0 * anneal / spread
-    gram = reorder(jnp.sum(grams_ref[...], axis=0)[:, :total])
     row = lax.broadcasted_iota(jnp.int32, (total, total), 0)
     col = lax.broadcasted_iota(jnp.int32, (total, total), 1)
     diagonal = jnp.where(row == col, gram, 0.0)
@@ -662,121 +672,129 @@
     full = lax.dot_general(half_way, member, (((1,), (1,)), ((), ())), preferred_element_type=F32)
     full = jnp.where(same_line(total), full, 0.0)
     gain = jnp.broadcast_to((1.0 + rate * coeff * ksum)[:, :, None], (total, TILE, LANES)).reshape(wide, LANES)
-    for j, k in enumerate(ks):
-        mixer[j * TILE : (j + 1) * TILE, :] = full[k * TILE : (k + 1) * TILE].astype(BF16)
-        own[j * TILE : (j + 1) * TILE, :] = gain[k * TILE : (k + 1) * TILE]
+    mixer[...] = full[first : first + high].astype(BF16)
+    own[...] = gain[first : first + high]
     for fetch in fetches:
         fetch.wait()
 
-    def mix(states, slopes, who, stores):
-        size = len(who) * TILE
-        states = jnp.concatenate(states, axis=0)
-        both = jnp.concatenate([slopes.reshape(wide, LANES), states], axis=1)
-        mixed = jnp.dot(mixer[:size, :], both, preferred_element_type=F32)
+    def mix(states, slopes):
+        both = jnp.concatenate([slopes, states], axis=1)
+        mixed = jnp.dot(mixer[...], both, preferred_element_type=F32)
         drive, pulled = mixed[:, :LANES], mixed[:, LANES:]
-        kept = jnp.concatenate([states[k * TILE : (k + 1) * TILE] for k in who], axis=0).astype(F32)
-        new = (kept * own[:size, :] + rate * (drive - coeff * pulled)).astype(BF16)
-        for j, (out_ref, to) in enumerate(stores):
-            out_ref[lines_of(to, TILE), :] = new[j * TILE : (j + 1) * TILE]
-
-    near = [k for k in ks if k < half]
-
-    def slab_step(who, i, carry):
+        kept = states[first : first + high].astype(F32)
+        return (kept * own[...] + rate * (drive - coeff * pulled)).astype(BF16)
+
+    def put(to, new):
+        if near:
+            out_refs[0][:, lines_of(to, TILE), :] = new.reshape(half, TILE, LANES)
+        else:
+            for j, out_ref in enumerate(out_refs):
+                out_ref[lines_of(to, TILE), :] = new[j * TILE : (j + 1) * TILE]
+
+    def slab_step(i, carry):
         for t in range(BLOCK // TILE):
             at = i * BLOCK + t * TILE
-            stores = [(out_ref, at if k < half else at - raw) for k, out_ref in zip(who, out_refs)]
-            mix([ref[lines_of(at, TILE), :] for ref in pieces], grads[:, lines_of(at, TILE), :], who, stores)
+            states = [near_ref[:, lines_of(at, TILE), :].reshape(high, LANES)]
+            states += [ref[lines_of(at, TILE), :] for ref in far_refs]
+            slopes = grads[:, lines_of(at, TILE), :].reshape(wide, LANES)
+            put(at if near else at - raw, mix(jnp.concatenate(states, axis=0), slopes))
         return carry
 
     def raw_step(i, carry):
+        here = lax.axis_index("slab").astype(jnp.int32) % half
         for t in range(BLOCK // TILE):
             at = i * BLOCK + t * TILE
-            states = [ref[lines_of(lines + TILE + at, TILE), :] for ref in pieces[:half]]
-            states += [raw_refs[0][j, lines_of(at, TILE), :] for j in range(half)]
-            stores = [(out_ref, lines + at) for out_ref in out_refs[: len(near)]]
-            mix(states, raw_grads[:, lines_of(at, TILE), :], near, stores)
+            part = lines_of(at, TILE)
+            states = [near_ref[:, lines_of(lines + TILE + at, TILE), :].reshape(high, LANES)]
+            slopes = [raw_grads[:half, part, :].reshape(high, LANES)]
+            for x in range(half):
+                states += [raw_refs[0][here ^ x, part, :]]
+                slopes += [raw_grads[half + (here ^ x), part, :]]
+            put(lines + at, mix(jnp.concatenate(states, axis=0), jnp.concatenate(slopes, axis=0)))
         return carry
 
-    if near and raw:
-        lax.fori_loop(0, raw // BLOCK, functools.partial(slab_step, near), 0)
-    lax.fori_loop(raw // BLOCK, lines // BLOCK, functools.partial(slab_step, ks), 0)
+    lax.fori_loop(0 if near else raw // BLOCK, lines // BLOCK, slab_step, 0)
     if near and raw:
         lax.fori_loop(0, raw // BLOCK, raw_step, 0)
 
 
-def update_pieces(scalars, grams, pieces, grads, groups, raw_parts, gates, raw, lines, ks):
-    total = len(pieces)
-    half = total // 2
-    wide = total * TILE
-    ks = tuple(sorted(ks))
-    sizes = [lines + raw if k < half else lines - raw for k in ks]
-    results = call(
-        functools.partial(update_pieces_body, ks, half, raw, lines, groups, len(raw_parts)),
+def update_pieces(numbers, grams, near_states, far_states, grads, groups, raw_parts, raw, lines, near):
+    half = len(far_states)
+    total = 2 * half
+    wide = total * TILE
+    if near:
+        out_shape = [jax.ShapeDtypeStruct((half, lines + raw, LANES), BF16)]
+    else:
+        out_shape = [jax.ShapeDtypeStruct((lines - raw, LANES), BF16)] * half
+    return call(
+        functools.partial(update_pieces_body, near, half, raw, lines, groups, len(raw_parts)),
         "update_pieces",
-        flops=4 * len(ks) * TILE * wide * LANES * (lines // TILE),
-        moved=2 * (2 * total + len(ks)) * lines * LANES,
-        in_specs=[IN_VMEM] * (total + 2)
-        + [IN_HBM] * len(groups)
-        + [IN_VMEM, IN_HBM][: len(raw_parts)]
-        + [IN_VMEM] * len(gates),
-        out_specs=[IN_VMEM] * len(ks),
-        out_shape=[jax.ShapeDtypeStruct((size, LANES), BF16) for size in sizes],
+        flops=4 * half * TILE * wide * LANES * (lines // TILE),
+        moved=2 * (2 * total + half) * lines * LANES,
+        in_specs=[IN_VMEM] * (half + 3) + [IN_HBM] * len(groups) + [IN_VMEM, IN_HBM][: len(raw_parts)],
+        out_specs=[IN_VMEM] * len(out_shape),
+        out_shape=out_shape,
         scratch_shapes=[
             pltpu.VMEM((total, lines, LANES), BF16),
             pltpu.VMEM((total, max(raw, TILE), LANES), BF16),
-            pltpu.VMEM((len(ks) * TILE, wide), BF16),
-            pltpu.VMEM((len(ks) * TILE, LANES), F32),
+            pltpu.VMEM((half * TILE, wide), BF16),
+            pltpu.VMEM((half * TILE, LANES), F32),
             pltpu.SemaphoreType.DMA((total + 1,)),
         ],
-    )(*pieces, scalars, grams, *grads, *raw_parts, *gates)
-    return dict(zip(ks, results))
+    )(near_states, *far_states, numbers, grams, *grads, *raw_parts)
 
 
 def exchange(piece, k, slabs):
     return lax.ppermute(piece, "slab", [(i, i ^ k) for i in range(slabs)])
 
 
+def swap_near(pieces, slabs):
+    groups = [list(range(slabs // 2)), list(range(slabs // 2, slabs))]
+    return lax.all_to_all(pieces, "slab", 0, 0, axis_index_groups=groups, tiled=True)
+
+
 RAW = 0
-SENDS = ((8, 9, 10, 4, 11), (5, 12, 6, 13, 7), (14, 1, 15, 2, 3, 0))
-GROUPS = ((8, 9, 10, 4), (11, 5, 12, 6), (13, 7, 14, 0), (1, 15, 2, 3))
-
-
-def by_pieces(particles, observed, precision, spread, anneal, step_size):
+GRADIENTS = ((8, 9, 10, 11), (0, 1, 2, 3), (4, 5, 6, 7), (12, 13), (14, 15))
+JOINS = ((0, 1, 2, 3, 4, 5, 6, 7), (8, 9, 10, 11), (12, 13), (14, 15))
+
+
+def by_halves(particles, observed, precision, spread, anneal, step_size):
     slabs = lax.axis_size("slab")
     half = slabs // 2
     lines = NCELL // slabs // LANES
-    obs = observed.reshape(-1, LANES)
-    prec = precision.reshape(-1, LANES)
-    states = [None] * slabs
-    for n, ks in enumerate(SENDS):
-        gates = [states[SENDS[n - 1][0]]] if n else []
-        for k, piece in zip(ks, split_pieces(particles, slabs, RAW, ks, gates)):
-            states[k] = exchange(piece, k, slabs) if k else piece
-    grads = []
-    for group in GROUPS:
-        arrays = [states[k] for k in group]
-        views = tuple((j, None, 0) for j in range(len(group)))
-        grads.append(gradient_pieces(arrays, views, obs, prec, lines, lines, 0))
-    grams = swap(gram_pieces(states, lines))
-    scalars = jnp.concatenate([spread, anneal, step_size])
-    scalars = jnp.broadcast_to(scalars[:, None], (3, LANES))
+    row = in_hbm(particles)
+    obs = in_hbm(observed.reshape(-1, LANES))
+    prec = in_hbm(precision.reshape(-1, LANES))
+    far = split_pieces(row, slabs, RAW, False, [])
+    near = split_pieces(row, slabs, RAW, True, far[:1])[0]
+    near = swap_near(near, slabs)
+    far = [exchange(piece, half + x, slabs) for x, piece in enumerate(far)]
     extra = []
     if RAW:
-        far = exchange(raw_states(states[:half], RAW, lines), half, slabs)
-        views = [(k, None, lines + TILE) for k in range(half)] + [(half, k, 0) for k in range(half)]
-        slopes = gradient_pieces(states[:half] + [far], tuple(views), obs, prec, lines, RAW, half)
-        extra = [far, slopes]
-    new = [None] * slabs
+        extra = [exchange(raw_states(near, RAW, lines), half, slabs)]
+    grads = []
+    numbers = [spread, anneal, step_size]
+    for group in GRADIENTS:
+        if group[0] < half:
+            arrays, views = [near], [(0, k, 0) for k in group]
+        else:
+            arrays, views = [far[k - half] for k in group], [(j, None, 0) for j in range(len(group))]
+        slopes, rows = gradient_pieces(arrays, tuple(views), obs, prec, lines, lines, 0, [] if grads else numbers)
+        grads.append(in_hbm(slopes))
+        numbers = numbers if len(grads) > 1 else rows
+    grams = swap(gram_pieces(near, far, lines, grads[:-1]))
+    if RAW:
+        views = [(0, k, lines + TILE) for k in range(half)] + [(1, k, 0) for k in range(half)]
+        slopes, _ = gradient_pieces([near] + extra, tuple(views), obs, prec, lines, RAW, half, [])
+        extra += [in_hbm(slopes)]
+    new_far = update_pieces(numbers, grams, near, far, grads, GRADIENTS, [], RAW, lines, False)
+    new_near = update_pieces(numbers, grams, near, far, grads, GRADIENTS, extra, RAW, lines, True)[0]
+    new_near = swap_near(new_near, slabs)
+    new_far = [exchange(piece, half + x, slabs) for x, piece in enumerate(new_far)]
     row = None
-    gates = []
-    for n, ks in enumerate(SENDS):
-        more = extra if min(ks) < half else []
-        results = update_pieces(scalars, grams, states, grads, GROUPS, more, gates, RAW, lines, ks)
-        for k in ks:
-            new[k] = exchange(results[k], k, slabs) if k else results[k]
-        gates = [new[ks[0]]]
-    for group in GROUPS:
-        row, _ = join_pieces(row, slabs, RAW, [new[k] for k in group], group)
+    for group in JOINS:
+        pieces = [new_near] if group[0] < half else [new_far[k - half] for k in group]
+        row = join_pieces(row, slabs, RAW, pieces, group)
     return row
 
 
@@ -785,7 +803,7 @@
     total = particles.shape[0] * slabs
     lines = NCELL // slabs // LANES
     if slabs == 16:
-        return by_pieces(particles, observed, precision, spread, anneal, step_size)
+        return by_halves(particles, observed, precision, spread, anneal, step_size)
     sent, begun = cuts(lines)
     fields = [observed.reshape(-1, LANES), precision.reshape(-1, LANES)]
     numbers = [spread, anneal, step_size]

time: 165 us -> 145 us (0.88)
  local copies, waits for them, and re-layouts: 25.5 us -> 0 us
  waiting for transfers between devices: 44.8 us -> 60.2 us
  starting transfers between devices: 52.2 us -> 42.7 us
    unnamed x92 -> x0, local copies, waits for them, and re-layouts: 25.4 us -> none
    ppermute x30 -> x16, starting transfers between devices: 47.1 us -> 24.8 us  [exchange(): return lax.ppermute(piece, 'slab', [(i, i ^ k) for i in range(slabs)])]
    ppermute x30 -> x16, waiting for transfers between devices: 44.8 us -> 57.4 us  [exchange(): return lax.ppermute(piece, 'slab', [(i, i ^ k) for i in range(slabs)])]
    all_to_all x0 -> x2, starting transfers between devices: none -> 10.2 us  [swap_near(): lax.all_to_all(pieces, 'slab', 0, 0, axis_index_groups=groups, tiled=True)]
    pallas_call x4 -> x5, Pallas kernels: 7.22 us -> 15.8 us  [gradient_pieces(): call(functools.partial(gradient_pieces_body, k, lines, count, views, len(...]
    pallas_call x11 -> x9, Pallas kernels: 31.7 us -> 23.8 us  [the longest x2 10.1 us: update_pieces(): call(functools.partial(update_pieces_body, near, half, raw, lines, groups...]
    all_to_all x1, waiting for transfers between devices: 0.01 us -> 2.77 us  [swap(): lax.all_to_all(slabs, 'slab', split_axis=0, concat_axis=0, tiled=True)]
    all_to_all x1, starting transfers between devices: 5.14 us -> 7.75 us  [swap(): lax.all_to_all(slabs, 'slab', split_axis=0, concat_axis=0, tiled=True)]
  transfers between devices with their start and end apart: 31 -> 19, of which waited for: 11 -> 12; matrix products, arithmetic and copies ran while one was open for 0% -> 0% of each run, Pallas kernels for 16% -> 17%
where the time goes in v6:
time: 145 us
  waiting for transfers between devices  60.2 us (42%)
  starting transfers between devices  42.7 us (29%)
  Pallas kernels  39.5 us (27%)
  between operations  2.09 us (1%)
    ppermute x16, waiting for transfers between devices, exchange(): return lax.ppermute(piece, 'slab', [(i, i ^ k) for i in range(slabs)])  57.4 us
    ppermute x16, starting transfers between devices, exchange(): return lax.ppermute(piece, 'slab', [(i, i ^ k) for i in range(slabs)])  24.8 us
    pallas_call x5, Pallas kernels, gradient_pieces(): call(functools.partial(gradient_pieces_body, k, lines, count, views, len(...  15.8 us
    all_to_all x2, starting transfers between devices, swap_near(): lax.all_to_all(pieces, 'slab', 0, 0, axis_index_groups=groups, tiled=True)  10.2 us
    pallas_call x2, Pallas kernels, update_pieces(): call(functools.partial(update_pieces_body, near, half, raw, lines, groups...  10.1 us
    all_to_all x1, starting transfers between devices, swap(): lax.all_to_all(slabs, 'slab', split_axis=0, concat_axis=0, tiled=True)  7.75 us
    pallas_call x4, Pallas kernels, join_pieces(): call(functools.partial(join_pieces_body, positions, slabs // 2, raw, cell...  5.31 us
    pallas_call x2, Pallas kernels, split_pieces(): call(functools.partial(split_pieces_body, positions, half, raw, lines, le...  5 us
  transfers between devices with their start and end apart: 19, of which 12 were waited for; matrix products, arithmetic and copies ran while one was open for 0% of the time, Pallas kernels for 17%

profile of v6, /device:TPU:9, one launch (start us, length us, event | category | flops | bytes accessed | tf_op | source)
XLA Modules:
  0.0 144.5 jit_solution(9058612555209621269)
XLA Ops:
  0.0 2.0 %split_pieces.2 = (bf16[528,128]{1,0:T(8,128)(2,1)S(1)}, bf16[528,128]{1,0:T(8,128)(2,1)S(1)}, bf16[528,128]{1,0:T(8,128)(2,1)S(1)}, bf16[528,128]{1,0:T(8,128)(...) custom-call(bf16[1,1048576]{1,0:T(2,128)(2,1)} %row_ref.3), custom_call_target="tpu_custom_call" | custom-call | bytes 3244032 | tf_op jit(solution)/shard_map/split_pieces/pallas_call | solution.py:434
  2.0 3.0 %split_pieces.3 = bf16[8,528,128]{2,1,0:T(8,128)(2,1)} custom-call(bf16[1,1048576]{1,0:T(2,128)(2,1)} %row_ref.3, bf16[528,128]{1,0:T(8,128)(2,1)S(1)} %get-tuple-element.27.refs_0_), custom_call_target="tpu_custom_call" | custom-call | bytes 3244032 | tf_op jit(solution)/shard_map/split_pieces/pallas_call | solution.py:434
  5.0 4.6 %all-to-all-start = ((bf16[8,528,128]{2,1,0:T(8,128)(2,1)}), bf16[8,528,128]{2,1,0:T(8,128)(2,1)S(1)}, u32[]{:S(2)}, u32[]{:S(2)}) async-start(bf16[8,528,128]{2,1,0:T(8,128)(2,1)} %split_pieces.3), calls=%async_computation | async-start | bytes 2162688 | tf_op jit(solution)/shard_map/all_to_all | solution.py:753
  9.6 2.6 %collective-permute-start.1 = (bf16[528,128]{1,0:T(8,128)(2,1)S(1)}, bf16[528,128]{1,0:T(8,128)(2,1)S(1)}, u32[]{:S(2)}, u32[]{:S(2)}) collective-permute-start(bf16[528,128]{1,0:T(8,128)(2,1)S(1)} %get-tuple-element.28), channel_id=1, source_target_pairs={{0,9},{1,8},{2,11},{3,10},{4,13},{5,12},{6,15},{7,14},{8,1},{9,0},... | collective-permute-start | bytes 405512 | tf_op jit(solution)/shard_map/ppermute | solution.py:748
  12.2 0.0 collective-permute-start.4
  12.2 1.8 %collective-permute-start.5 = (bf16[528,128]{1,0:T(8,128)(2,1)S(1)}, bf16[528,128]{1,0:T(8,128)(2,1)S(1)}, u32[]{:S(2)}, u32[]{:S(2)}) collective-permute-start(bf16[528,128]{1,0:T(8,128)(2,1)S(1)} %get-tuple-element.32), channel_id=1, source_target_pairs={{0,13},{1,12},{2,15},{3,14},{4,9},{5,8},{6,11},{7,10},{8,5},{9,4},... | collective-permute-start | bytes 405512 | tf_op jit(solution)/shard_map/ppermute | solution.py:748
  14.0 2.7 %collective-permute-start.2 = (bf16[528,128]{1,0:T(8,128)(2,1)S(1)}, bf16[528,128]{1,0:T(8,128)(2,1)S(1)}, u32[]{:S(2)}, u32[]{:S(2)}) collective-permute-start(bf16[528,128]{1,0:T(8,128)(2,1)S(1)} %get-tuple-element.29), channel_id=1, source_target_pairs={{0,10},{1,11},{2,8},{3,9},{4,14},{5,15},{6,12},{7,13},{8,2},{9,3},... | collective-permute-start | bytes 405512 | tf_op jit(solution)/shard_map/ppermute | solution.py:748
  16.7 0.7 collective-permute-start.3
  17.4 10.7 %collective-permute-done.1.refs_1_ = bf16[528,128]{1,0:T(8,128)(2,1)S(1)} collective-permute-done((bf16[528,128]{1,0:T(8,128)(2,1)S(1)}, bf16[528,128]{1,0:T(8,128)(2,1)S(1)}, u32[]{:S(2)}, u32[]{:S(2)}) %collective-permute-start.1) | collective-permute-done | bytes 135200 | tf_op jit(solution)/shard_map/ppermute | solution.py:748
  28.1 0.0 collective-permute-start
  28.1 0.0 collective-permute-done.4.refs_0_.refs_4_
  28.1 0.1 collective-permute-start.6
  28.2 0.0 collective-permute-done.5.refs_1_.refs_5_
  28.2 2.7 %collective-permute-start.7 = (bf16[528,128]{1,0:T(8,128)(2,1)S(1)}, bf16[528,128]{1,0:T(8,128)(2,1)S(1)}, u32[]{:S(2)}, u32[]{:S(2)}) collective-permute-start(bf16[528,128]{1,0:T(8,128)(2,1)S(1)} %get-tuple-element.34), channel_id=1, source_target_pairs={{0,15},{1,14},{2,13},{3,12},{4,11},{5,10},{6,9},{7,8},{8,7},{9,6},... | collective-permute-start | bytes 405512 | tf_op jit(solution)/shard_map/ppermute | solution.py:748
  32.8 3.1 %gradient_pieces.8 = (bf16[2,512,128]{2,1,0:T(8,128)(2,1)}, f32[8,128]{1,0:T(8,128)}) custom-call(bf16[528,128]{1,0:T(8,128)(2,1)S(1)} %collective-permute-done.4.refs_0_.refs_4_, bf16[528,128]{1,0:T(8,128)(2,1)S(1)} %collective-permute-done.5.refs_1_.refs_5_, bf16[8192,128]{1,0:T(8,128)(2,1)} %bitcast.2, bf16[8192,128]{1,0:T(8,128)(2,1)} %bitcast.7), custom_call_target="tpu_custom_call" | custom-call | flops 3932160 | bytes 1048576 | tf_op jit(solution)/shard_map/gradient_pieces/pallas_call | solution.py:604
  35.9 11.3 %collective-permute-done.2.refs_2_ = bf16[528,128]{1,0:T(8,128)(2,1)S(1)} collective-permute-done((bf16[528,128]{1,0:T(8,128)(2,1)S(1)}, bf16[528,128]{1,0:T(8,128)(2,1)S(1)}, u32[]{:S(2)}, u32[]{:S(2)}) %collective-permute-start.2) | collective-permute-done | bytes 135200 | tf_op jit(solution)/shard_map/ppermute | solution.py:748
  47.2 2.9 %collective-permute-done.3.refs_3_ = bf16[528,128]{1,0:T(8,128)(2,1)S(1)} collective-permute-done((bf16[528,128]{1,0:T(8,128)(2,1)S(1)}, bf16[528,128]{1,0:T(8,128)(2,1)S(1)}, u32[]{:S(2)}, u32[]{:S(2)}) %collective-permute-start.3) | collective-permute-done | bytes 135200 | tf_op jit(solution)/shard_map/ppermute | solution.py:748
  50.1 2.9 %collective-permute-done.refs_0_ = bf16[528,128]{1,0:T(8,128)(2,1)S(1)} collective-permute-done((bf16[528,128]{1,0:T(8,128)(2,1)S(1)}, bf16[528,128]{1,0:T(8,128)(2,1)S(1)}, u32[]{:S(2)}, u32[]{:S(2)}) %collective-permute-start) | collective-permute-done | bytes 135200 | tf_op jit(solution)/shard_map/ppermute | solution.py:748
  53.0 2.8 %gradient_pieces.5 = (bf16[4,512,128]{2,1,0:T(8,128)(2,1)}, f32[8,128]{1,0:T(8,128)S(1)}) custom-call(bf16[528,128]{1,0:T(8,128)(2,1)S(1)} %collective-permute-done.refs_0_, bf16[528,128]{1,0:T(8,128)(2,1)S(1)} %collective-permute-done.1.refs_1_, bf16[528,128]{1,0:T(8,128)(2,1)S(1)} %collective-permute-done.2.refs_2_, ...), custom_call_target="tpu_custom_call" | custom-call | flops 7864320 | bytes 2097152 | tf_op jit(solution)/shard_map/gradient_pieces/pallas_call | solution.py:604
  55.8 0.0 all-to-all-done.refs_0_.near_ref
  55.8 3.4 %gradient_pieces.7 = (bf16[4,512,128]{2,1,0:T(8,128)(2,1)}, f32[8,128]{1,0:T(8,128)}) custom-call(bf16[8,528,128]{2,1,0:T(8,128)(2,1)S(1)} %all-to-all-done.refs_0_.near_ref, bf16[8192,128]{1,0:T(8,128)(2,1)} %bitcast.4, bf16[8192,128]{1,0:T(8,128)(2,1)} %bitcast.9), custom_call_target="tpu_custom_call" | custom-call | flops 7864320 | bytes 2097152 | tf_op jit(solution)/shard_map/gradient_pieces/pallas_call | solution.py:604
  59.2 3.4 %gradient_pieces.6 = (bf16[4,512,128]{2,1,0:T(8,128)(2,1)}, f32[8,128]{1,0:T(8,128)}) custom-call(bf16[8,528,128]{2,1,0:T(8,128)(2,1)S(1)} %all-to-all-done.refs_0_.near_ref, bf16[8192,128]{1,0:T(8,128)(2,1)} %bitcast.5, bf16[8192,128]{1,0:T(8,128)(2,1)} %bitcast.10), custom_call_target="tpu_custom_call" | custom-call | flops 7864320 | bytes 2097152 | tf_op jit(solution)/shard_map/gradient_pieces/pallas_call | solution.py:604
  62.6 0.0 collective-permute-done.6.refs_6_.refs_0_
  62.6 3.3 %gram_pieces.1 = f32[16,16,128]{2,1,0:T(8,128)} custom-call(bf16[8,528,128]{2,1,0:T(8,128)(2,1)S(1)} %all-to-all-done.refs_0_.near_ref, bf16[528,128]{1,0:T(8,128)(2,1)S(1)} %collective-permute-done.refs_0_, bf16[528,128]{1,0:T(8,128)(2,1)S(1)} %collective-permute-done.1.refs_1_, bf16[528,128]{1,0:T(8,128)(2,1)S(1)} %collective-permute-done.2.refs_2_, ...), custom_call_target="tpu_custom_call" | custom-call | flops 536870912 | bytes 2097152 | tf_op jit(solution)/shard_map/gram_pieces/pallas_call | solution.py:526
  65.9 7.7 %all-to-all-start.1 = ((f32[16,16,128]{2,1,0:T(8,128)}), f32[16,16,128]{2,1,0:T(8,128)S(1)}, u32[]{:S(2)}, u32[]{:S(2)}) async-start(f32[16,16,128]{2,1,0:T(8,128)} %gram_pieces.1), calls=%async_computation.1 | async-start | bytes 262144 | tf_op jit(solution)/shard_map/all_to_all | solution.py:365
  73.7 3.1 %gradient_pieces.9 = (bf16[2,512,128]{2,1,0:T(8,128)(2,1)}, f32[8,128]{1,0:T(8,128)}) custom-call(bf16[528,128]{1,0:T(8,128)(2,1)S(1)} %collective-permute-done.6.refs_6_.refs_0_, bf16[528,128]{1,0:T(8,128)(2,1)S(1)} %collective-permute-done.7.refs_7_.refs_1_, bf16[8192,128]{1,0:T(8,128)(2,1)} %bitcast.6, bf16[8192,128]{1,0:T(8,128)(2,1)} %bitcast.11), custom_call_target="tpu_custom_call" | custom-call | flops 3932160 | bytes 1048576 | tf_op jit(solution)/shard_map/gradient_pieces/pallas_call | solution.py:604
  76.8 2.8 %all-to-all-done.1.refs_9_ = f32[16,16,128]{2,1,0:T(8,128)S(1)} async-done(((f32[16,16,128]{2,1,0:T(8,128)}), f32[16,16,128]{2,1,0:T(8,128)S(1)}, u32[]{:S(2)}, u32[]{:S(2)}) %all-to-all-start.1) | async-done | bytes 131104 | tf_op jit(solution)/shard_map/all_to_all | solution.py:365
  79.6 5.1 %update_pieces.2 = bf16[8,512,128]{2,1,0:T(8,128)(2,1)} custom-call(bf16[8,528,128]{2,1,0:T(8,128)(2,1)S(1)} %all-to-all-done.refs_0_.near_ref, bf16[528,128]{1,0:T(8,128)(2,1)S(1)} %collective-permute-done.refs_0_, bf16[528,128]{1,0:T(8,128)(2,1)S(1)} %collective-permute-done.1.refs_1_, bf16[528,128]{1,0:T(8,128)(2,1)S(1)} %collective-permute-done.2.refs_2_, ...), custom_call_target="tpu_custom_call" | custom-call | flops 536870912 | bytes 5242880 | tf_op jit(solution)/shard_map/update_pieces/pallas_call | solution.py:729
  84.7 5.6 %all-to-all-start.2 = ((bf16[8,512,128]{2,1,0:T(8,128)(2,1)}), bf16[8,512,128]{2,1,0:T(8,128)(2,1)S(1)}, u32[]{:S(2)}, u32[]{:S(2)}) async-start(bf16[8,512,128]{2,1,0:T(8,128)(2,1)} %update_pieces.2), calls=%async_computation.2 | async-start | bytes 2097152 | tf_op jit(solution)/shard_map/all_to_all | solution.py:753
  90.3 5.0 %update_pieces.3 = (bf16[512,128]{1,0:T(8,128)(2,1)S(1)}, bf16[512,128]{1,0:T(8,128)(2,1)S(1)}, bf16[512,128]{1,0:T(8,128)(2,1)S(1)}, bf16[512,128]{1,0:T(8,128)...) custom-call(bf16[8,528,128]{2,1,0:T(8,128)(2,1)S(1)} %all-to-all-don, ...), custom_call_target="tpu_custom_call" | custom-call | flops 536870912 | bytes 5242880 | tf_op jit(solution)/shard_map/update_pieces/pallas_call | solution.py:729
  95.3 0.2 collective-permute-start.8
  95.5 2.7 %collective-permute-start.9 = (bf16[512,128]{1,0:T(8,128)(2,1)S(1)}, bf16[512,128]{1,0:T(8,128)(2,1)S(1)}, u32[]{:S(2)}, u32[]{:S(2)}) collective-permute-start(bf16[512,128]{1,0:T(8,128)(2,1)S(1)} %get-tuple-element.42), channel_id=1, source_target_pairs={{0,9},{1,8},{2,11},{3,10},{4,13},{5,12},{6,15},{7,14},{8,1},{9,0},... | collective-permute-start | bytes 393224 | tf_op jit(solution)/shard_map/ppermute | solution.py:748
  98.3 1.1 collective-permute-start.10
  99.4 2.3 %collective-permute-start.11 = (bf16[512,128]{1,0:T(8,128)(2,1)}, bf16[512,128]{1,0:T(8,128)(2,1)S(1)}, u32[]{:S(2)}, u32[]{:S(2)}) collective-permute-start(bf16[512,128]{1,0:T(8,128)(2,1)} %get-tuple-element.44), channel_id=1, source_target_pairs={{0,11},{1,10},{2,9},{3,8},{4,15},{5,14},{6,13},{7,12},{8,3},{9,2},... | collective-permute-start | bytes 393224 | tf_op jit(solution)/shard_map/ppermute | solution.py:748
  101.6 3.9 %collective-permute-done.8.refs_1_ = bf16[512,128]{1,0:T(8,128)(2,1)S(1)} collective-permute-done((bf16[512,128]{1,0:T(8,128)(2,1)S(1)}, bf16[512,128]{1,0:T(8,128)(2,1)S(1)}, u32[]{:S(2)}, u32[]{:S(2)}) %collective-permute-start.8) | collective-permute-done | bytes 131104 | tf_op jit(solution)/shard_map/ppermute | solution.py:748
  105.5 2.2 %collective-permute-start.13 = (bf16[512,128]{1,0:T(8,128)(2,1)}, bf16[512,128]{1,0:T(8,128)(2,1)S(1)}, u32[]{:S(2)}, u32[]{:S(2)}) collective-permute-start(bf16[512,128]{1,0:T(8,128)(2,1)} %get-tuple-element.46), channel_id=1, source_target_pairs={{0,13},{1,12},{2,15},{3,14},{4,9},{5,8},{6,11},{7,10},{8,5},{9,4},... | collective-permute-start | bytes 393224 | tf_op jit(solution)/shard_map/ppermute | solution.py:748
  107.7 1.3 collective-permute-done.9.refs_2_
  109.1 2.4 %collective-permute-start.14 = (bf16[512,128]{1,0:T(8,128)(2,1)}, bf16[512,128]{1,0:T(8,128)(2,1)S(1)}, u32[]{:S(2)}, u32[]{:S(2)}) collective-permute-start(bf16[512,128]{1,0:T(8,128)(2,1)} %get-tuple-element.47), channel_id=1, source_target_pairs={{0,14},{1,15},{2,12},{3,13},{4,10},{5,11},{6,8},{7,9},{8,6},{9,7},... | collective-permute-start | bytes 393224 | tf_op jit(solution)/shard_map/ppermute | solution.py:748
  111.5 11.2 %collective-permute-done.10.refs_3_ = bf16[512,128]{1,0:T(8,128)(2,1)S(1)} collective-permute-done((bf16[512,128]{1,0:T(8,128)(2,1)S(1)}, bf16[512,128]{1,0:T(8,128)(2,1)S(1)}, u32[]{:S(2)}, u32[]{:S(2)}) %collective-permute-start.10) | collective-permute-done | bytes 131104 | tf_op jit(solution)/shard_map/ppermute | solution.py:748
  122.7 3.3 %collective-permute-start.15 = (bf16[512,128]{1,0:T(8,128)(2,1)S(1)}, bf16[512,128]{1,0:T(8,128)(2,1)S(1)}, u32[]{:S(2)}, u32[]{:S(2)}) collective-permute-start(bf16[512,128]{1,0:T(8,128)(2,1)S(1)} %get-tuple-element.48), channel_id=1, source_target_pairs={{0,15},{1,14},{2,13},{3,12},{4,11},{5,10},{6,9},{7,8},{8,7},{9,6},... | collective-permute-start | bytes 393224 | tf_op jit(solution)/shard_map/ppermute | solution.py:748
  126.1 2.5 %join_pieces.4.refs_0_ = bf16[1,1048576]{1,0:T(2,128)(2,1)} custom-call(bf16[8,512,128]{2,1,0:T(8,128)(2,1)S(1)} %all-to-all-done.2.refs_0_), custom_call_target="tpu_custom_call" | custom-call | bytes 3145728 | tf_op jit(solution)/shard_map/join_pieces/pallas_call | solution.py:475
  128.6 1.1 join_pieces.5.refs_0_
  129.7 4.2 %collective-permute-done.12.refs_1_ = bf16[512,128]{1,0:T(8,128)(2,1)S(1)} collective-permute-done((bf16[512,128]{1,0:T(8,128)(2,1)}, bf16[512,128]{1,0:T(8,128)(2,1)S(1)}, u32[]{:S(2)}, u32[]{:S(2)}) %collective-permute-start.12) | collective-permute-done | bytes 131104 | tf_op jit(solution)/shard_map/ppermute | solution.py:748
  133.9 3.6 %collective-permute-done.13.refs_2_ = bf16[512,128]{1,0:T(8,128)(2,1)S(1)} collective-permute-done((bf16[512,128]{1,0:T(8,128)(2,1)}, bf16[512,128]{1,0:T(8,128)(2,1)S(1)}, u32[]{:S(2)}, u32[]{:S(2)}) %collective-permute-start.13) | collective-permute-done | bytes 131104 | tf_op jit(solution)/shard_map/ppermute | solution.py:748
  137.5 0.9 join_pieces.6.refs_0_
  138.4 2.0 %collective-permute-done.14.refs_1_ = bf16[512,128]{1,0:T(8,128)(2,1)S(1)} collective-permute-done((bf16[512,128]{1,0:T(8,128)(2,1)}, bf16[512,128]{1,0:T(8,128)(2,1)S(1)}, u32[]{:S(2)}, u32[]{:S(2)}) %collective-permute-start.14) | collective-permute-done | bytes 131104 | tf_op jit(solution)/shard_map/ppermute | solution.py:748
  140.4 3.3 %collective-permute-done.15.refs_2_ = bf16[512,128]{1,0:T(8,128)(2,1)S(1)} collective-permute-done((bf16[512,128]{1,0:T(8,128)(2,1)S(1)}, bf16[512,128]{1,0:T(8,128)(2,1)S(1)}, u32[]{:S(2)}, u32[]{:S(2)}) %collective-permute-start.15) | collective-permute-done | bytes 131104 | tf_op jit(solution)/shard_map/ppermute | solution.py:748
  143.7 0.9 join_pieces.7
  (4 shorter events, 0.0 us)
Async XLA Ops:
  5.0 50.8 %all-to-all-start = ((bf16[8,528,128]{2,1,0:T(8,128)(2,1)}), bf16[8,528,128]{2,1,0:T(8,128)(2,1)S(1)}, u32[]{:S(2)}, u32[]{:S(2)}) async-start(bf16[8,528,128]{2,1,0:T(8,128)(2,1)} %split_pieces.3), calls=%async_computation | async-start | bytes 2162688 | tf_op jit(solution)/shard_map/all_to_all | solution.py:753
  9.6 18.5 %collective-permute-start.1 = (bf16[528,128]{1,0:T(8,128)(2,1)S(1)}, bf16[528,128]{1,0:T(8,128)(2,1)S(1)}, u32[]{:S(2)}, u32[]{:S(2)}) collective-permute-start(bf16[528,128]{1,0:T(8,128)(2,1)S(1)} %get-tuple-element.28), channel_id=1, source_target_pairs={{0,9},{1,8},{2,11},{3,10},{4,13},{5,12},{6,15},{7,14},{8,1},{9,0},... | collective-permute-start | bytes 405512 | tf_op jit(solution)/shard_map/ppermute | solution.py:748
  12.2 16.0 %collective-permute-start.4 = (bf16[528,128]{1,0:T(8,128)(2,1)S(1)}, bf16[528,128]{1,0:T(8,128)(2,1)S(1)}, u32[]{:S(2)}, u32[]{:S(2)}) collective-permute-start(bf16[528,128]{1,0:T(8,128)(2,1)S(1)} %get-tuple-element.31), channel_id=1, source_target_pairs={{0,12},{1,13},{2,14},{3,15},{4,8},{5,9},{6,10},{7,11},{8,4},{9,5},... | collective-permute-start | bytes 405512 | tf_op jit(solution)/shard_map/ppermute | solution.py:748
  12.2 16.0 %collective-permute-start.5 = (bf16[528,128]{1,0:T(8,128)(2,1)S(1)}, bf16[528,128]{1,0:T(8,128)(2,1)S(1)}, u32[]{:S(2)}, u32[]{:S(2)}) collective-permute-start(bf16[528,128]{1,0:T(8,128)(2,1)S(1)} %get-tuple-element.32), channel_id=1, source_target_pairs={{0,13},{1,12},{2,15},{3,14},{4,9},{5,8},{6,11},{7,10},{8,5},{9,4},... | collective-permute-start | bytes 405512 | tf_op jit(solution)/shard_map/ppermute | solution.py:748
  14.0 33.2 %collective-permute-start.2 = (bf16[528,128]{1,0:T(8,128)(2,1)S(1)}, bf16[528,128]{1,0:T(8,128)(2,1)S(1)}, u32[]{:S(2)}, u32[]{:S(2)}) collective-permute-start(bf16[528,128]{1,0:T(8,128)(2,1)S(1)} %get-tuple-element.29), channel_id=1, source_target_pairs={{0,10},{1,11},{2,8},{3,9},{4,14},{5,15},{6,12},{7,13},{8,2},{9,3},... | collective-permute-start | bytes 405512 | tf_op jit(solution)/shard_map/ppermute | solution.py:748
  16.7 33.4 %collective-permute-start.3 = (bf16[528,128]{1,0:T(8,128)(2,1)S(1)}, bf16[528,128]{1,0:T(8,128)(2,1)S(1)}, u32[]{:S(2)}, u32[]{:S(2)}) collective-permute-start(bf16[528,128]{1,0:T(8,128)(2,1)S(1)} %get-tuple-element.30), channel_id=1, source_target_pairs={{0,11},{1,10},{2,9},{3,8},{4,15},{5,14},{6,13},{7,12},{8,3},{9,2},... | collective-permute-start | bytes 405512 | tf_op jit(solution)/shard_map/ppermute | solution.py:748
  28.1 24.9 %collective-permute-start = (bf16[528,128]{1,0:T(8,128)(2,1)S(1)}, bf16[528,128]{1,0:T(8,128)(2,1)S(1)}, u32[]{:S(2)}, u32[]{:S(2)}) collective-permute-start(bf16[528,128]{1,0:T(8,128)(2,1)S(1)} %get-tuple-element.27.refs_0_), channel_id=1, source_target_pairs={{0,8},{1,9},{2,10},{3,11},{4,12},{5,13},{6,14},{7,15},{8,0},{9,1},... | collective-permute-start | bytes 405512 | tf_op jit(solution)/shard_map/ppermute | solution.py:748
  28.1 34.4 %collective-permute-start.6 = (bf16[528,128]{1,0:T(8,128)(2,1)S(1)}, bf16[528,128]{1,0:T(8,128)(2,1)S(1)}, u32[]{:S(2)}, u32[]{:S(2)}) collective-permute-start(bf16[528,128]{1,0:T(8,128)(2,1)S(1)} %get-tuple-element.33), channel_id=1, source_target_pairs={{0,14},{1,15},{2,12},{3,13},{4,10},{5,11},{6,8},{7,9},{8,6},{9,7},... | collective-permute-start | bytes 405512 | tf_op jit(solution)/shard_map/ppermute | solution.py:748
  28.2 34.4 %collective-permute-start.7 = (bf16[528,128]{1,0:T(8,128)(2,1)S(1)}, bf16[528,128]{1,0:T(8,128)(2,1)S(1)}, u32[]{:S(2)}, u32[]{:S(2)}) collective-permute-start(bf16[528,128]{1,0:T(8,128)(2,1)S(1)} %get-tuple-element.34), channel_id=1, source_target_pairs={{0,15},{1,14},{2,13},{3,12},{4,11},{5,10},{6,9},{7,8},{8,7},{9,6},... | collective-permute-start | bytes 405512 | tf_op jit(solution)/shard_map/ppermute | solution.py:748
  65.9 13.6 %all-to-all-start.1 = ((f32[16,16,128]{2,1,0:T(8,128)}), f32[16,16,128]{2,1,0:T(8,128)S(1)}, u32[]{:S(2)}, u32[]{:S(2)}) async-start(f32[16,16,128]{2,1,0:T(8,128)} %gram_pieces.1), calls=%async_computation.1 | async-start | bytes 262144 | tf_op jit(solution)/shard_map/all_to_all | solution.py:365
  84.7 41.4 %all-to-all-start.2 = ((bf16[8,512,128]{2,1,0:T(8,128)(2,1)}), bf16[8,512,128]{2,1,0:T(8,128)(2,1)S(1)}, u32[]{:S(2)}, u32[]{:S(2)}) async-start(bf16[8,512,128]{2,1,0:T(8,128)(2,1)} %update_pieces.2), calls=%async_computation.2 | async-start | bytes 2097152 | tf_op jit(solution)/shard_map/all_to_all | solution.py:753
  95.3 10.2 %collective-permute-start.8 = (bf16[512,128]{1,0:T(8,128)(2,1)S(1)}, bf16[512,128]{1,0:T(8,128)(2,1)S(1)}, u32[]{:S(2)}, u32[]{:S(2)}) collective-permute-start(bf16[512,128]{1,0:T(8,128)(2,1)S(1)} %get-tuple-element.41), channel_id=1, source_target_pairs={{0,8},{1,9},{2,10},{3,11},{4,12},{5,13},{6,14},{7,15},{8,0},{9,1},... | collective-permute-start | bytes 393224 | tf_op jit(solution)/shard_map/ppermute | solution.py:748
  95.5 13.5 %collective-permute-start.9 = (bf16[512,128]{1,0:T(8,128)(2,1)S(1)}, bf16[512,128]{1,0:T(8,128)(2,1)S(1)}, u32[]{:S(2)}, u32[]{:S(2)}) collective-permute-start(bf16[512,128]{1,0:T(8,128)(2,1)S(1)} %get-tuple-element.42), channel_id=1, source_target_pairs={{0,9},{1,8},{2,11},{3,10},{4,13},{5,12},{6,15},{7,14},{8,1},{9,0},... | collective-permute-start | bytes 393224 | tf_op jit(solution)/shard_map/ppermute | solution.py:748
  98.3 24.4 %collective-permute-start.10 = (bf16[512,128]{1,0:T(8,128)(2,1)S(1)}, bf16[512,128]{1,0:T(8,128)(2,1)S(1)}, u32[]{:S(2)}, u32[]{:S(2)}) collective-permute-start(bf16[512,128]{1,0:T(8,128)(2,1)S(1)} %get-tuple-element.43), channel_id=1, source_target_pairs={{0,10},{1,11},{2,8},{3,9},{4,14},{5,15},{6,12},{7,13},{8,2},{9,3},... | collective-permute-start | bytes 393224 | tf_op jit(solution)/shard_map/ppermute | solution.py:748
  99.4 29.3 %collective-permute-start.11 = (bf16[512,128]{1,0:T(8,128)(2,1)}, bf16[512,128]{1,0:T(8,128)(2,1)S(1)}, u32[]{:S(2)}, u32[]{:S(2)}) collective-permute-start(bf16[512,128]{1,0:T(8,128)(2,1)} %get-tuple-element.44), channel_id=1, source_target_pairs={{0,11},{1,10},{2,9},{3,8},{4,15},{5,14},{6,13},{7,12},{8,3},{9,2},... | collective-permute-start | bytes 393224 | tf_op jit(solution)/shard_map/ppermute | solution.py:748
  101.6 32.3 %collective-permute-start.12 = (bf16[512,128]{1,0:T(8,128)(2,1)}, bf16[512,128]{1,0:T(8,128)(2,1)S(1)}, u32[]{:S(2)}, u32[]{:S(2)}) collective-permute-start(bf16[512,128]{1,0:T(8,128)(2,1)} %get-tuple-element.45), channel_id=1, source_target_pairs={{0,12},{1,13},{2,14},{3,15},{4,8},{5,9},{6,10},{7,11},{8,4},{9,5},... | collective-permute-start | bytes 393224 | tf_op jit(solution)/shard_map/ppermute | solution.py:748
  105.5 32.0 %collective-permute-start.13 = (bf16[512,128]{1,0:T(8,128)(2,1)}, bf16[512,128]{1,0:T(8,128)(2,1)S(1)}, u32[]{:S(2)}, u32[]{:S(2)}) collective-permute-start(bf16[512,128]{1,0:T(8,128)(2,1)} %get-tuple-element.46), channel_id=1, source_target_pairs={{0,13},{1,12},{2,15},{3,14},{4,9},{5,8},{6,11},{7,10},{8,5},{9,4},... | collective-permute-start | bytes 393224 | tf_op jit(solution)/shard_map/ppermute | solution.py:748
  109.1 31.3 %collective-permute-start.14 = (bf16[512,128]{1,0:T(8,128)(2,1)}, bf16[512,128]{1,0:T(8,128)(2,1)S(1)}, u32[]{:S(2)}, u32[]{:S(2)}) collective-permute-start(bf16[512,128]{1,0:T(8,128)(2,1)} %get-tuple-element.47), channel_id=1, source_target_pairs={{0,14},{1,15},{2,12},{3,13},{4,10},{5,11},{6,8},{7,9},{8,6},{9,7},... | collective-permute-start | bytes 393224 | tf_op jit(solution)/shard_map/ppermute | solution.py:748
  122.7 20.9 %collective-permute-start.15 = (bf16[512,128]{1,0:T(8,128)(2,1)S(1)}, bf16[512,128]{1,0:T(8,128)(2,1)S(1)}, u32[]{:S(2)}, u32[]{:S(2)}) collective-permute-start(bf16[512,128]{1,0:T(8,128)(2,1)S(1)} %get-tuple-element.48), channel_id=1, source_target_pairs={{0,15},{1,14},{2,13},{3,12},{4,11},{5,10},{6,9},{7,8},{8,7},{9,6},... | collective-permute-start | bytes 393224 | tf_op jit(solution)/shard_map/ppermute | solution.py:748

commit v7 on v6

--- a/solution.py
+++ b/solution.py
@@ -374,10 +374,17 @@
     return pl.ds(pl.multiple_of(start, TILE), count)
 
 
-def split_pieces_body(positions, half, raw, lines, gates, row_ref, *refs):
-    refs = refs[gates:]
+def split_pieces_body(positions, half, raw, lines, gates, fields, row_ref, *refs):
+    field_refs, refs = refs[:fields], refs[fields + gates :]
     count = len(positions)
     out_refs, helds, sems = refs[: -count - 1], refs[-count - 1 : -1], refs[-1]
+    me = lax.axis_index("slab").astype(jnp.int32)
+    slab_refs = out_refs[len(out_refs) - 2 * fields :]
+    fetches = []
+    for n, target in enumerate(slab_refs):
+        start = (me if n < fields else me ^ half) * lines
+        source = field_refs[n % fields].at[lines_of(start, target.shape[0]), :]
+        fetches.append(pltpu.make_async_copy(source, target, sems.at[5 * count + n]))
     cells = lines * LANES
     end = row_ref.shape[1]
     copies = []
@@ -403,6 +410,8 @@
     def grid_row(held, at):
         return held[:, pl.ds(at, GRID_Y)].astype(F32).reshape(LINE, LANES)
 
+    for fetch in fetches:
+        fetch.start()
     for n, (at, held, mine) in enumerate(zip(positions, helds, copies)):
         out_ref = out_refs[n] if at >= half else out_refs[0].at[n]
         for copy in mine:
@@ -419,9 +428,11 @@
             below = grid_row(held, start + raw * LANES)
             above = jnp.where(slab ^ half == 0, 0.0, grid_row(held, start + raw * LANES + GRID_Y))
             out_ref[to + raw :, :] = jnp.concatenate([below, above], axis=0).astype(BF16)
-
-
-def split_pieces(row, slabs, raw, near, gates):
+    for fetch in fetches:
+        fetch.wait()
+
+
+def split_pieces(row, slabs, raw, near, gates, fields):
     lines = row.shape[1] // slabs // LANES
     half = slabs // 2
     count = half
@@ -430,16 +441,19 @@
         out_shape = [jax.ShapeDtypeStruct((count, size, LANES), BF16)]
     else:
         out_shape = [jax.ShapeDtypeStruct((size, LANES), BF16)] * count
+    out_shape += [jax.ShapeDtypeStruct((lines, LANES), BF16)] * len(fields)
+    out_shape += [jax.ShapeDtypeStruct((max(raw, TILE), LANES), BF16)] * len(fields)
     positions = range(half) if near else range(half, slabs)
     return call(
-        functools.partial(split_pieces_body, positions, half, raw, lines, len(gates)),
+        functools.partial(split_pieces_body, positions, half, raw, lines, len(gates), len(fields)),
         "split_pieces",
         moved=6 * count * size * LANES,
-        in_specs=[IN_HBM] + [IN_VMEM] * len(gates),
+        in_specs=[IN_HBM] * (1 + len(fields)) + [IN_VMEM] * len(gates),
         out_specs=[IN_VMEM] * len(out_shape),
         out_shape=out_shape,
-        scratch_shapes=[pltpu.VMEM((1, (size + TILE) * LANES), BF16)] * count + [pltpu.SemaphoreType.DMA((5 * count,))],
-    )(row, *gates)
+        scratch_shapes=[pltpu.VMEM((1, (size + TILE) * LANES), BF16)] * count
+        + [pltpu.SemaphoreType.DMA((5 * count + 2 * len(fields),))],
+    )(row, *fields, *gates)
 
 
 def join_pieces_body(positions, half, raw, lines, begun, *refs):
@@ -485,14 +499,11 @@
     )(*begun, *pieces)
 
 
-def reorder(gram, back):
-    total = gram.shape[0]
-    row = lax.broadcasted_iota(jnp.int32, (total, total), 0)
-    col = lax.broadcasted_iota(jnp.int32, (total, total), 1)
-    left = (col == device_at(row, total // 2) if back else row == device_at(col, total // 2)).astype(F32)
-    right = (row == device_at(col, total // 2) if back else col == device_at(row, total // 2)).astype(F32)
-    exact = {"precision": lax.Precision.HIGHEST, "preferred_element_type": F32}
-    return jnp.dot(jnp.dot(left, gram, **exact), right, **exact)
+def owners(total, dtype):
+    wide = total * TILE
+    row = lax.broadcasted_iota(jnp.int32, (wide, total), 0)
+    col = lax.broadcasted_iota(jnp.int32, (wide, total), 1)
+    return (device_at(row // TILE, total // 2) == col).astype(dtype)
 
 
 def gram_pieces_body(lines, total, near_ref, *refs):
@@ -514,10 +525,11 @@
 
     lax.fori_loop(0, lines // TILE // tiles, step, 0)
     equal = jnp.where(same_line(total), pairs[...], 0.0)
-    rows = jnp.sum(equal.reshape(total, TILE, wide), axis=1)
-    gram = jnp.dot(rows, members(total, F32), precision=lax.Precision.HIGHEST, preferred_element_type=F32)
-    gram = jnp.concatenate([reorder(gram, False), jnp.zeros((total, LANES - total), F32)], axis=1)
-    out_ref[...] = jnp.broadcast_to(gram[None], out_ref.shape)
+    exact = {"precision": lax.Precision.HIGHEST, "preferred_element_type": F32}
+    owner = owners(total, F32)
+    half_way = jnp.dot(equal, owner, **exact)
+    gram = lax.dot_general(owner, half_way, (((0,), (0,)), ((), ())), **exact)
+    out_ref[...] = jnp.concatenate([gram, jnp.zeros((total, LANES - total), F32)], axis=1)
 
 
 def gram_pieces(near, far, lines, gates):
@@ -530,30 +542,22 @@
         moved=2 * total * lines * LANES,
         in_specs=[IN_VMEM] * (1 + len(far)) + [IN_HBM] * len(gates),
         out_specs=IN_VMEM,
-        out_shape=jax.ShapeDtypeStruct((total, total, LANES), F32),
+        out_shape=jax.ShapeDtypeStruct((total, LANES), F32),
         scratch_shapes=[pltpu.VMEM((wide, wide), F32)],
     )(near, *far, *gates)
 
 
-def gradient_pieces_body(k, lines, count, views, arrays, numbers, *refs):
-    observed_ref, precision_ref, *number_refs = refs[arrays : arrays + 2 + numbers]
-    out_ref, rows_ref, observed, precision, grads, sems = refs[-6:]
+def gradient_pieces_body(views, arrays, numbers, *refs):
+    observed, precision, *number_refs = refs[arrays : arrays + 2 + numbers]
+    out_ref, rows_ref, grads, sems = refs[-4:]
     for n, number_ref in enumerate(number_refs):
         rows_ref[n : n + 1, :] = jnp.full((1, LANES), number_ref[0], F32)
+    count = observed.shape[0]
     rows = BLOCK // LINE
     shape = (rows, LINE, LANES)
     lane = lax.broadcasted_iota(jnp.int32, (1, LINE, LANES), 2)
     line = lax.broadcasted_iota(jnp.int32, (1, LINE, LANES), 1)
     steps = count // BLOCK
-    mine = lines_of((lax.axis_index("slab").astype(jnp.int32) ^ k) * lines, count)
-    fetches = [
-        pltpu.make_async_copy(observed_ref.at[mine, :], observed, sems.at[steps]),
-        pltpu.make_async_copy(precision_ref.at[mine, :], precision, sems.at[steps + 1]),
-    ]
-    for fetch in fetches:
-        fetch.start()
-    for fetch in fetches:
-        fetch.wait()
 
     def store(i):
         at = lines_of(i * BLOCK, BLOCK)
@@ -598,25 +602,20 @@
     lax.fori_loop(0, steps, finish, 0)
 
 
-def gradient_pieces(arrays, views, observed, precision, lines, count, k, numbers):
+def gradient_pieces(arrays, views, observed, precision, numbers):
+    count = observed.shape[0]
     out = pltpu.HBM((len(views), count, LANES), BF16)
     size = len(views) * count * LANES
     return call(
-        functools.partial(gradient_pieces_body, k, lines, count, views, len(arrays), len(numbers)),
+        functools.partial(gradient_pieces_body, views, len(arrays), len(numbers)),
         "gradient_pieces",
         flops=30 * size,
         moved=8 * size,
-        in_specs=[IN_VMEM] * len(arrays)
-        + [IN_HBM, IN_HBM]
+        in_specs=[IN_VMEM] * (len(arrays) + 2)
         + [pl.BlockSpec(memory_space=pltpu.SMEM)] * len(numbers),
         out_specs=[IN_HBM, IN_VMEM],
         out_shape=[out, jax.ShapeDtypeStruct((8, LANES), F32)],
-        scratch_shapes=[
-            pltpu.VMEM((count, LANES), BF16),
-            pltpu.VMEM((count, LANES), BF16),
-            pltpu.VMEM(out.shape, BF16),
-            pltpu.SemaphoreType.DMA((count // BLOCK + 2,)),
-        ],
+        scratch_shapes=[pltpu.VMEM(out.shape, BF16), pltpu.SemaphoreType.DMA((count // BLOCK,))],
     )(*arrays, observed, precision, *numbers)
 
 
@@ -640,8 +639,9 @@
     )(near)
 
 
-def update_pieces_body(near, half, raw, lines, groups, extra, near_ref, *refs):
+def update_pieces_body(near, half, raw, lines, groups, extra, gates, near_ref, *refs):
     total = 2 * half
+    refs = refs[gates:]
     far_refs, numbers_ref, grams_ref, refs = refs[:half], refs[half], refs[half + 1], refs[half + 2 :]
     group_refs, refs = refs[: len(groups)], refs[len(groups) :]
     raw_refs, out_refs, (grads, raw_grads, mixer, own, sems) = refs[:extra], refs[extra:-5], refs[-5:]
@@ -656,7 +656,7 @@
         fetches.append(pltpu.make_async_copy(raw_refs[1], raw_grads, sems.at[len(fetches)]))
     for fetch in fetches:
         fetch.start()
-    gram = reorder(jnp.sum(grams_ref[...], axis=0)[:, :total], True)
+    gram = jnp.sum(grams_ref[...], axis=0)[:, :total]
     spread, anneal, step_size = (numbers_ref[k : k + 1, :1] for k in range(3))
     rate = step_size / total
     coeff = 2.0 * anneal / spread
@@ -666,14 +666,13 @@
     down = jnp.sum(diagonal, axis=1, keepdims=True)
     across = jnp.sum(diagonal, axis=0, keepdims=True)
     kernel = jnp.exp(-(down + across - 2.0 * gram) / (spread * NCELL)).astype(BF16)
-    ksum = jnp.sum(kernel.astype(F32), axis=1, keepdims=True)
-    member = members(total, BF16)
-    half_way = jnp.dot(member, kernel, preferred_element_type=F32).astype(BF16)
-    full = lax.dot_general(half_way, member, (((1,), (1,)), ((), ())), preferred_element_type=F32)
-    full = jnp.where(same_line(total), full, 0.0)
-    gain = jnp.broadcast_to((1.0 + rate * coeff * ksum)[:, :, None], (total, TILE, LANES)).reshape(wide, LANES)
-    mixer[...] = full[first : first + high].astype(BF16)
-    own[...] = gain[first : first + high]
+    owner = owners(total, BF16)
+    half_way = jnp.dot(owner[first : first + high], kernel, preferred_element_type=F32).astype(BF16)
+    full = lax.dot_general(half_way, owner, (((1,), (1,)), ((), ())), preferred_element_type=F32)
+    full = jnp.where(same_line(total)[first : first + high], full, 0.0)
+    mixer[...] = full.astype(BF16)
+    ksum = jnp.sum(full, axis=1, keepdims=True)
+    own[...] = jnp.broadcast_to(1.0 + rate * coeff * ksum, (high, LANES))
     for fetch in fetches:
         fetch.wait()
 
@@ -718,7 +717,7 @@
         lax.fori_loop(0, raw // BLOCK, raw_step, 0)
 
 
-def update_pieces(numbers, grams, near_states, far_states, grads, groups, raw_parts, raw, lines, near):
+def update_pieces(numbers, grams, near_states, far_states, grads, groups, raw_parts, gates, raw, lines, near):
     half = len(far_states)
     total = 2 * half
     wide = total * TILE
@@ -727,11 +726,11 @@
     else:
         out_shape = [jax.ShapeDtypeStruct((lines - raw, LANES), BF16)] * half
     return call(
-        functools.partial(update_pieces_body, near, half, raw, lines, groups, len(raw_parts)),
+        functools.partial(update_pieces_body, near, half, raw, lines, groups, len(raw_parts), len(gates)),
         "update_pieces",
         flops=4 * half * TILE * wide * LANES * (lines // TILE),
         moved=2 * (2 * total + half) * lines * LANES,
-        in_specs=[IN_VMEM] * (half + 3) + [IN_HBM] * len(groups) + [IN_VMEM, IN_HBM][: len(raw_parts)],
+        in_specs=[IN_VMEM] * (half + 3 + len(gates)) + [IN_HBM] * len(groups) + [IN_VMEM, IN_HBM][: len(raw_parts)],
         out_specs=[IN_VMEM] * len(out_shape),
         out_shape=out_shape,
         scratch_shapes=[
@@ -741,7 +740,7 @@
             pltpu.VMEM((half * TILE, LANES), F32),
             pltpu.SemaphoreType.DMA((total + 1,)),
         ],
-    )(near_states, *far_states, numbers, grams, *grads, *raw_parts)
+    )(near_states, *gates, *far_states, numbers, grams, *grads, *raw_parts)
 
 
 def exchange(piece, k, slabs):
@@ -754,7 +753,7 @@
 
 
 RAW = 0
-GRADIENTS = ((8, 9, 10, 11), (0, 1, 2, 3), (4, 5, 6, 7), (12, 13), (14, 15))
+GRADIENTS = ((8, 9, 10, 11), (0, 1, 2, 3, 4, 5, 6, 7), (12, 13, 14, 15))
 JOINS = ((0, 1, 2, 3, 4, 5, 6, 7), (8, 9, 10, 11), (12, 13), (14, 15))
 
 
@@ -763,12 +762,10 @@
     half = slabs // 2
     lines = NCELL // slabs // LANES
     row = in_hbm(particles)
-    obs = in_hbm(observed.reshape(-1, LANES))
-    prec = in_hbm(precision.reshape(-1, LANES))
-    far = split_pieces(row, slabs, RAW, False, [])
-    near = split_pieces(row, slabs, RAW, True, far[:1])[0]
-    near = swap_near(near, slabs)
+    fields = [in_hbm(field.reshape(-1, LANES)) for field in (observed, precision)]
+    *far, obs, prec, raw_obs, raw_prec = split_pieces(row, slabs, RAW, False, [], fields)
     far = [exchange(piece, half + x, slabs) for x, piece in enumerate(far)]
+    near = swap_near(split_pieces(row, slabs, RAW, True, far[:1], [])[0], slabs)
     extra = []
     if RAW:
         extra = [exchange(raw_states(near, RAW, lines), half, slabs)]
@@ -779,18 +776,19 @@
             arrays, views = [near], [(0, k, 0) for k in group]
         else:
             arrays, views = [far[k - half] for k in group], [(j, None, 0) for j in range(len(group))]
-        slopes, rows = gradient_pieces(arrays, tuple(views), obs, prec, lines, lines, 0, [] if grads else numbers)
+        slopes, rows = gradient_pieces(arrays, tuple(views), obs, prec, [] if grads else numbers)
         grads.append(in_hbm(slopes))
         numbers = numbers if len(grads) > 1 else rows
-    grams = swap(gram_pieces(near, far, lines, grads[:-1]))
+    grams = lax.all_gather(gram_pieces(near, far, lines, grads[:1]), "slab")
     if RAW:
         views = [(0, k, lines + TILE) for k in range(half)] + [(1, k, 0) for k in range(half)]
-        slopes, _ = gradient_pieces([near] + extra, tuple(views), obs, prec, lines, RAW, half, [])
+        slopes, _ = gradient_pieces([near] + extra, tuple(views), raw_obs, raw_prec, [])
         extra += [in_hbm(slopes)]
-    new_far = update_pieces(numbers, grams, near, far, grads, GRADIENTS, [], RAW, lines, False)
-    new_near = update_pieces(numbers, grams, near, far, grads, GRADIENTS, extra, RAW, lines, True)[0]
+    new_far = update_pieces(numbers, grams, near, far, grads, GRADIENTS, [], [], RAW, lines, False)
+    new_far = [exchange(piece, half + x, slabs) for x, piece in enumerate(new_far)]
+    gates = new_far[:1]
+    new_near = update_pieces(numbers, grams, near, far, grads, GRADIENTS, extra, gates, RAW, lines, True)[0]
     new_near = swap_near(new_near, slabs)
-    new_far = [exchange(piece, half + x, slabs) for x, piece in enumerate(new_far)]
     row = None
     for group in JOINS:
         pieces = [new_near] if group[0] < half else [new_far[k - half] for k in group]

time: 145 us -> 158 us (1.090)
  blocking collectives: 0 us -> 20.2 us
  Pallas kernels: 39.5 us -> 29.9 us
  starting transfers between devices: 42.7 us -> 50.1 us
  waiting for transfers between devices: 60.2 us -> 55.3 us
    all_gather x0 -> x1, blocking collectives: none -> 20.2 us  [by_halves(): grams = lax.all_gather(gram_pieces(near, far, lines, grads[:1]), 'slab')]
    ppermute x16, waiting for transfers between devices: 57.4 us -> 45.2 us  [exchange(): return lax.ppermute(piece, 'slab', [(i, i ^ k) for i in range(slabs)])]
    ppermute x16, starting transfers between devices: 24.8 us -> 36.8 us  [exchange(): return lax.ppermute(piece, 'slab', [(i, i ^ k) for i in range(slabs)])]
    all_to_all x2, waiting for transfers between devices: 0.01 us -> 10 us  [swap_near(): lax.all_to_all(pieces, 'slab', 0, 0, axis_index_groups=groups, tiled=True)]
    pallas_call x5 -> x3, Pallas kernels: 15.8 us -> 7.32 us  [gradient_pieces(): call(functools.partial(gradient_pieces_body, views, len(arrays), len(numb...]
    all_to_all x1 -> x0, starting transfers between devices: 7.75 us -> none  [swap(): lax.all_to_all(slabs, 'slab', split_axis=0, concat_axis=0, tiled=True)]
    all_to_all x2, starting transfers between devices: 10.2 us -> 13.3 us  [swap_near(): lax.all_to_all(pieces, 'slab', 0, 0, axis_index_groups=groups, tiled=True)]
    all_to_all x1 -> x0, waiting for transfers between devices: 2.77 us -> none  [swap(): lax.all_to_all(slabs, 'slab', split_axis=0, concat_axis=0, tiled=True)]
  transfers between devices with their start and end apart: 19 -> 18, of which waited for: 12 -> 11; matrix products, arithmetic and copies ran while one was open for 0% -> 0% of each run, Pallas kernels for 17% -> 5%
where the time goes in v7:
time: 158 us
  waiting for transfers between devices  55.3 us (35%)
  starting transfers between devices  50.1 us (32%)
  Pallas kernels  29.9 us (19%)
  blocking collectives  20.2 us (13%)
  between operations  2.08 us (1%)
    ppermute x16, waiting for transfers between devices, exchange(): return lax.ppermute(piece, 'slab', [(i, i ^ k) for i in range(slabs)])  45.2 us
    ppermute x16, starting transfers between devices, exchange(): return lax.ppermute(piece, 'slab', [(i, i ^ k) for i in range(slabs)])  36.8 us
    all_gather x1, blocking collectives, by_halves(): grams = lax.all_gather(gram_pieces(near, far, lines, grads[:1]), 'slab')  20.2 us
    all_to_all x2, starting transfers between devices, swap_near(): lax.all_to_all(pieces, 'slab', 0, 0, axis_index_groups=groups, tiled=True)  13.3 us
    all_to_all x2, waiting for transfers between devices, swap_near(): lax.all_to_all(pieces, 'slab', 0, 0, axis_index_groups=groups, tiled=True)  10 us
    pallas_call x2, Pallas kernels, update_pieces(): call(functools.partial(update_pieces_body, near, half, raw, lines, groups...  8.86 us
    pallas_call x3, Pallas kernels, gradient_pieces(): call(functools.partial(gradient_pieces_body, views, len(arrays), len(numb...  7.32 us
    pallas_call x2, Pallas kernels, split_pieces(): call(functools.partial(split_pieces_body, positions, half, raw, lines, le...  5.67 us
  transfers between devices with their start and end apart: 18, of which 11 were waited for; matrix products, arithmetic and copies ran while one was open for 0% of the time, Pallas kernels for 5%

profile of v7, /device:TPU:9, one launch (start us, length us, event | category | flops | bytes accessed | tf_op | source)
XLA Modules:
  0.0 157.5 jit_solution(11465473535132779101)
XLA Ops:
  0.0 2.7 %split_pieces.2 = (bf16[528,128]{1,0:T(8,128)(2,1)S(1)}, bf16[528,128]{1,0:T(8,128)(2,1)S(1)}, bf16[528,128]{1,0:T(8,128)(2,1)S(1)}, bf16[528,128]{1,0:T(8,128)(...) custom-call(bf16[1,1048576]{1,0:T(2,128)(2,1)} %row_ref.3, ...), custom_call_target="tpu_custom_call" | custom-call | bytes 3244032 | tf_op jit(solution)/shard_map/split_pieces/pallas_call | solution.py:447
  2.7 2.4 %collective-permute-start = (bf16[528,128]{1,0:T(8,128)(2,1)S(1)}, bf16[528,128]{1,0:T(8,128)(2,1)S(1)}, u32[]{:S(2)}, u32[]{:S(2)}) collective-permute-start(bf16[528,128]{1,0:T(8,128)(2,1)S(1)} %get-tuple-element.27), channel_id=1, source_target_pairs={{0,8},{1,9},{2,10},{3,11},{4,12},{5,13},{6,14},{7,15},{8,0},{9,1},... | collective-permute-start | bytes 405512 | tf_op jit(solution)/shard_map/ppermute | solution.py:747
  5.1 6.1 %collective-permute-done.refs_0_.refs_1_ = bf16[528,128]{1,0:T(8,128)(2,1)S(1)} collective-permute-done((bf16[528,128]{1,0:T(8,128)(2,1)S(1)}, bf16[528,128]{1,0:T(8,128)(2,1)S(1)}, u32[]{:S(2)}, u32[]{:S(2)}) %collective-permute-start) | collective-permute-done | bytes 135200 | tf_op jit(solution)/shard_map/ppermute | solution.py:747
  11.2 3.0 %split_pieces.3 = bf16[8,528,128]{2,1,0:T(8,128)(2,1)} custom-call(bf16[1,1048576]{1,0:T(2,128)(2,1)} %row_ref.3, bf16[528,128]{1,0:T(8,128)(2,1)S(1)} %collective-permute-done.refs_0_.refs_1_), custom_call_target="tpu_custom_call" | custom-call | bytes 3244032 | tf_op jit(solution)/shard_map/split_pieces/pallas_call | solution.py:447
  14.2 4.9 %all-to-all-start = ((bf16[8,528,128]{2,1,0:T(8,128)(2,1)}), bf16[8,528,128]{2,1,0:T(8,128)(2,1)S(1)}, u32[]{:S(2)}, u32[]{:S(2)}) async-start(bf16[8,528,128]{2,1,0:T(8,128)(2,1)} %split_pieces.3), calls=%async_computation | async-start | bytes 2162688 | tf_op jit(solution)/shard_map/all_to_all | solution.py:752
  19.1 1.5 collective-permute-start.4
  20.6 0.5 collective-permute-start.5
  21.1 2.6 %collective-permute-start.6 = (bf16[528,128]{1,0:T(8,128)(2,1)S(1)}, bf16[528,128]{1,0:T(8,128)(2,1)S(1)}, u32[]{:S(2)}, u32[]{:S(2)}) collective-permute-start(bf16[528,128]{1,0:T(8,128)(2,1)S(1)} %get-tuple-element.33), channel_id=1, source_target_pairs={{0,14},{1,15},{2,12},{3,13},{4,10},{5,11},{6,8},{7,9},{8,6},{9,7},... | collective-permute-start | bytes 405512 | tf_op jit(solution)/shard_map/ppermute | solution.py:747
  23.6 0.0 collective-permute-start.7
  23.6 6.2 %collective-permute-start.1 = (bf16[528,128]{1,0:T(8,128)(2,1)S(1)}, bf16[528,128]{1,0:T(8,128)(2,1)S(1)}, u32[]{:S(2)}, u32[]{:S(2)}) collective-permute-start(bf16[528,128]{1,0:T(8,128)(2,1)S(1)} %get-tuple-element.28), channel_id=1, source_target_pairs={{0,9},{1,8},{2,11},{3,10},{4,13},{5,12},{6,15},{7,14},{8,1},{9,0},... | collective-permute-start | bytes 405512 | tf_op jit(solution)/shard_map/ppermute | solution.py:747
  29.9 0.0 collective-permute-done.4.refs_4_.refs_0_.refs_5_
  29.9 7.9 %collective-permute-start.2 = (bf16[528,128]{1,0:T(8,128)(2,1)S(1)}, bf16[528,128]{1,0:T(8,128)(2,1)S(1)}, u32[]{:S(2)}, u32[]{:S(2)}) collective-permute-start(bf16[528,128]{1,0:T(8,128)(2,1)S(1)} %get-tuple-element.29), channel_id=1, source_target_pairs={{0,10},{1,11},{2,8},{3,9},{4,14},{5,15},{6,12},{7,13},{8,2},{9,3},... | collective-permute-start | bytes 405512 | tf_op jit(solution)/shard_map/ppermute | solution.py:747
  37.8 0.0 collective-permute-done.5.refs_5_.refs_1_.refs_6_
  37.8 3.7 %collective-permute-start.3 = (bf16[528,128]{1,0:T(8,128)(2,1)S(1)}, bf16[528,128]{1,0:T(8,128)(2,1)S(1)}, u32[]{:S(2)}, u32[]{:S(2)}) collective-permute-start(bf16[528,128]{1,0:T(8,128)(2,1)S(1)} %get-tuple-element.30), channel_id=1, source_target_pairs={{0,11},{1,10},{2,9},{3,8},{4,15},{5,14},{6,13},{7,12},{8,3},{9,2},... | collective-permute-start | bytes 405512 | tf_op jit(solution)/shard_map/ppermute | solution.py:747
  43.5 0.0 collective-permute-done.6.refs_6_.refs_2_.refs_7_
  43.5 10.5 %collective-permute-done.7.refs_7_.refs_3_.refs_8_ = bf16[528,128]{1,0:T(8,128)(2,1)S(1)} collective-permute-done((bf16[528,128]{1,0:T(8,128)(2,1)S(1)}, bf16[528,128]{1,0:T(8,128)(2,1)S(1)}, u32[]{:S(2)}, u32[]{:S(2)}) %collective-permute-start.7) | collective-permute-done | bytes 135200 | tf_op jit(solution)/shard_map/ppermute | solution.py:747
  54.0 2.4 %gradient_pieces.5 = (bf16[4,512,128]{2,1,0:T(8,128)(2,1)}, f32[8,128]{1,0:T(8,128)}) custom-call(bf16[528,128]{1,0:T(8,128)(2,1)S(1)} %collective-permute-done.4.refs_4_.refs_0_.refs_5_, bf16[528,128]{1,0:T(8,128)(2,1)S(1)} %collective-permute-done.5.refs_5_.refs_1_.refs_6_, bf16[528,128]{1,0:T(8,128)(2,1)S(1)} %collective-permute-done.6.refs_6_.refs_2_.refs_7_, ...), custom_call_target="tpu_custom_call" | custom-call | flops 7864320 | bytes 2097152 | tf_op jit(solution)/shard_map/gradient_pieces/pallas_call | solution.py:609
  56.4 0.5 collective-permute-done.1.refs_1_.refs_2_
  56.9 2.9 %collective-permute-done.2.refs_2_.refs_3_ = bf16[528,128]{1,0:T(8,128)(2,1)S(1)} collective-permute-done((bf16[528,128]{1,0:T(8,128)(2,1)S(1)}, bf16[528,128]{1,0:T(8,128)(2,1)S(1)}, u32[]{:S(2)}, u32[]{:S(2)}) %collective-permute-start.2) | collective-permute-done | bytes 135200 | tf_op jit(solution)/shard_map/ppermute | solution.py:747
  59.8 2.9 %collective-permute-done.3.refs_3_.refs_4_ = bf16[528,128]{1,0:T(8,128)(2,1)S(1)} collective-permute-done((bf16[528,128]{1,0:T(8,128)(2,1)S(1)}, bf16[528,128]{1,0:T(8,128)(2,1)S(1)}, u32[]{:S(2)}, u32[]{:S(2)}) %collective-permute-start.3) | collective-permute-done | bytes 135200 | tf_op jit(solution)/shard_map/ppermute | solution.py:747
  62.7 1.8 %gradient_pieces.3 = (bf16[4,512,128]{2,1,0:T(8,128)(2,1)}, f32[8,128]{1,0:T(8,128)S(1)}) custom-call(bf16[528,128]{1,0:T(8,128)(2,1)S(1)} %collective-permute-done.refs_0_.refs_1_, bf16[528,128]{1,0:T(8,128)(2,1)S(1)} %collective-permute-done.1.refs_1_.refs_2_, bf16[528,128]{1,0:T(8,128)(2,1)S(1)} %collective-permute-done.2.refs_2_.refs_3_, ...), custom_call_target="tpu_custom_call" | custom-call | flops 7864320 | bytes 2097152 | tf_op jit(solution)/shard_map/gradient_pieces/pallas_call | solution.py:609
  64.5 0.0 all-to-all-done.near_ref.refs_0_
  64.5 2.8 %gram_pieces.1 = f32[16,128]{1,0:T(8,128)S(1)} custom-call(bf16[8,528,128]{2,1,0:T(8,128)(2,1)S(1)} %all-to-all-done.near_ref.refs_0_, bf16[528,128]{1,0:T(8,128)(2,1)S(1)} %collective-permute-done.refs_0_.refs_1_, bf16[528,128]{1,0:T(8,128)(2,1)S(1)} %collective-permute-done.1.refs_1_.refs_2_, bf16[528,128]{1,0:T(8,128)(2,1)S(1)} %collective-permute-done.2.refs_2_.refs_3_, ...), custom_call_target="tpu_custom_call" | custom-call | flops 536870912 | bytes 2097152 | tf_op jit(solution)/shard_map/gram_pieces/pallas_call | solution.py:538
  67.3 20.2 %all-gather = f32[256,128]{1,0:T(8,128)S(1)} all-gather(f32[16,128]{1,0:T(8,128)S(1)} %gram_pieces.1), channel_id=2, replica_groups=mesh['groups'=2,'slab'=16] {'slab'}, dimensions={0}, use_global_device_ids=true | all-gather | bytes 139264 | tf_op jit(solution)/shard_map/all_gather | solution.py:782
  87.5 3.1 %gradient_pieces.4 = (bf16[8,512,128]{2,1,0:T(8,128)(2,1)}, f32[8,128]{1,0:T(8,128)}) custom-call(bf16[8,528,128]{2,1,0:T(8,128)(2,1)S(1)} %all-to-all-done.near_ref.refs_0_, bf16[512,128]{1,0:T(8,128)(2,1)S(1)} %get-tuple-element.35.refs_4_.refs_1_, bf16[512,128]{1,0:T(8,128)(2,1)S(1)} %get-tuple-element.36.refs_5_.refs_2_), custom_call_target="tpu_custom_call" | custom-call | flops 15728640 | bytes 4194304 | tf_op jit(solution)/shard_map/gradient_pieces/pallas_call | solution.py:609
  90.6 3.8 %update_pieces.2 = (bf16[512,128]{1,0:T(8,128)(2,1)S(1)}, bf16[512,128]{1,0:T(8,128)(2,1)S(1)}, bf16[512,128]{1,0:T(8,128)(2,1)S(1)}, bf16[512,128]{1,0:T(8,128)...) custom-call(bf16[8,528,128]{2,1,0:T(8,128)(2,1)S(1)} %all-to-all-don, ...), custom_call_target="tpu_custom_call" | custom-call | flops 536870912 | bytes 5242880 | tf_op jit(solution)/shard_map/update_pieces/pallas_call | solution.py:728
  94.4 0.3 collective-permute-start.8
  94.7 5.6 %collective-permute-done.8.refs_0_.refs_1_ = bf16[512,128]{1,0:T(8,128)(2,1)S(1)} collective-permute-done((bf16[512,128]{1,0:T(8,128)(2,1)S(1)}, bf16[512,128]{1,0:T(8,128)(2,1)S(1)}, u32[]{:S(2)}, u32[]{:S(2)}) %collective-permute-start.8) | collective-permute-done | bytes 131104 | tf_op jit(solution)/shard_map/ppermute | solution.py:747
  100.3 5.1 %update_pieces.3 = bf16[8,512,128]{2,1,0:T(8,128)(2,1)} custom-call(bf16[8,528,128]{2,1,0:T(8,128)(2,1)S(1)} %all-to-all-done.near_ref.refs_0_, bf16[512,128]{1,0:T(8,128)(2,1)S(1)} %collective-permute-done.8.refs_0_.refs_1_, bf16[528,128]{1,0:T(8,128)(2,1)S(1)} %collective-permute-done.refs_0_.refs_1_, ...), custom_call_target="tpu_custom_call" | custom-call | flops 536870912 | bytes 5242880 | tf_op jit(solution)/shard_map/update_pieces/pallas_call | solution.py:728
  105.4 8.4 %all-to-all-start.1 = ((bf16[8,512,128]{2,1,0:T(8,128)(2,1)}), bf16[8,512,128]{2,1,0:T(8,128)(2,1)S(1)}, u32[]{:S(2)}, u32[]{:S(2)}) async-start(bf16[8,512,128]{2,1,0:T(8,128)(2,1)} %update_pieces.3), calls=%async_computation.1 | async-start | bytes 2097152 | tf_op jit(solution)/shard_map/all_to_all | solution.py:752
  113.7 0.0 collective-permute-start.9
  113.7 3.5 %collective-permute-start.10 = (bf16[512,128]{1,0:T(8,128)(2,1)S(1)}, bf16[512,128]{1,0:T(8,128)(2,1)S(1)}, u32[]{:S(2)}, u32[]{:S(2)}) collective-permute-start(bf16[512,128]{1,0:T(8,128)(2,1)S(1)} %get-tuple-element.43), channel_id=1, source_target_pairs={{0,10},{1,11},{2,8},{3,9},{4,14},{5,15},{6,12},{7,13},{8,2},{9,3},... | collective-permute-start | bytes 393224 | tf_op jit(solution)/shard_map/ppermute | solution.py:747
  117.3 0.3 collective-permute-start.11
  117.5 1.3 collective-permute-start.12
  118.8 0.5 collective-permute-start.13
  119.3 9.5 %collective-permute-done.9.refs_2_ = bf16[512,128]{1,0:T(8,128)(2,1)S(1)} collective-permute-done((bf16[512,128]{1,0:T(8,128)(2,1)S(1)}, bf16[512,128]{1,0:T(8,128)(2,1)S(1)}, u32[]{:S(2)}, u32[]{:S(2)}) %collective-permute-start.9) | collective-permute-done | bytes 131104 | tf_op jit(solution)/shard_map/ppermute | solution.py:747
  128.8 3.3 %collective-permute-start.14 = (bf16[512,128]{1,0:T(8,128)(2,1)S(1)}, bf16[512,128]{1,0:T(8,128)(2,1)S(1)}, u32[]{:S(2)}, u32[]{:S(2)}) collective-permute-start(bf16[512,128]{1,0:T(8,128)(2,1)S(1)} %get-tuple-element.47), channel_id=1, source_target_pairs={{0,14},{1,15},{2,12},{3,13},{4,10},{5,11},{6,8},{7,9},{8,6},{9,7},... | collective-permute-start | bytes 393224 | tf_op jit(solution)/shard_map/ppermute | solution.py:747
  132.1 0.0 collective-permute-done.10.refs_3_
  132.1 2.7 %collective-permute-start.15 = (bf16[512,128]{1,0:T(8,128)(2,1)S(1)}, bf16[512,128]{1,0:T(8,128)(2,1)S(1)}, u32[]{:S(2)}, u32[]{:S(2)}) collective-permute-start(bf16[512,128]{1,0:T(8,128)(2,1)S(1)} %get-tuple-element.48), channel_id=1, source_target_pairs={{0,15},{1,14},{2,13},{3,12},{4,11},{5,10},{6,9},{7,8},{8,7},{9,6},... | collective-permute-start | bytes 393224 | tf_op jit(solution)/shard_map/ppermute | solution.py:747
  134.8 10.0 %all-to-all-done.1.refs_0_ = bf16[8,512,128]{2,1,0:T(8,128)(2,1)S(1)} async-done(((bf16[8,512,128]{2,1,0:T(8,128)(2,1)}), bf16[8,512,128]{2,1,0:T(8,128)(2,1)S(1)}, u32[]{:S(2)}, u32[]{:S(2)}) %all-to-all-start.1) | async-done | bytes 1048608 | tf_op jit(solution)/shard_map/all_to_all | solution.py:752
  144.9 2.5 %join_pieces.4.refs_0_ = bf16[1,1048576]{1,0:T(2,128)(2,1)} custom-call(bf16[8,512,128]{2,1,0:T(8,128)(2,1)S(1)} %all-to-all-done.1.refs_0_), custom_call_target="tpu_custom_call" | custom-call | bytes 3145728 | tf_op jit(solution)/shard_map/join_pieces/pallas_call | solution.py:489
  147.4 0.0 collective-permute-done.11.refs_4_
  147.4 1.1 join_pieces.5.refs_0_
  148.5 1.7 %collective-permute-done.13.refs_2_ = bf16[512,128]{1,0:T(8,128)(2,1)S(1)} collective-permute-done((bf16[512,128]{1,0:T(8,128)(2,1)S(1)}, bf16[512,128]{1,0:T(8,128)(2,1)S(1)}, u32[]{:S(2)}, u32[]{:S(2)}) %collective-permute-start.13) | collective-permute-done | bytes 131104 | tf_op jit(solution)/shard_map/ppermute | solution.py:747
  150.2 0.9 join_pieces.6.refs_0_
  151.1 2.8 %collective-permute-done.14.refs_1_ = bf16[512,128]{1,0:T(8,128)(2,1)S(1)} collective-permute-done((bf16[512,128]{1,0:T(8,128)(2,1)S(1)}, bf16[512,128]{1,0:T(8,128)(2,1)S(1)}, u32[]{:S(2)}, u32[]{:S(2)}) %collective-permute-start.14) | collective-permute-done | bytes 131104 | tf_op jit(solution)/shard_map/ppermute | solution.py:747
  153.9 2.8 %collective-permute-done.15.refs_2_ = bf16[512,128]{1,0:T(8,128)(2,1)S(1)} collective-permute-done((bf16[512,128]{1,0:T(8,128)(2,1)S(1)}, bf16[512,128]{1,0:T(8,128)(2,1)S(1)}, u32[]{:S(2)}, u32[]{:S(2)}) %collective-permute-start.15) | collective-permute-done | bytes 131104 | tf_op jit(solution)/shard_map/ppermute | solution.py:747
  156.7 0.9 join_pieces.7
  (1 shorter events, 0.0 us)
Async XLA Ops:
  2.7 8.5 %collective-permute-start = (bf16[528,128]{1,0:T(8,128)(2,1)S(1)}, bf16[528,128]{1,0:T(8,128)(2,1)S(1)}, u32[]{:S(2)}, u32[]{:S(2)}) collective-permute-start(bf16[528,128]{1,0:T(8,128)(2,1)S(1)} %get-tuple-element.27), channel_id=1, source_target_pairs={{0,8},{1,9},{2,10},{3,11},{4,12},{5,13},{6,14},{7,15},{8,0},{9,1},... | collective-permute-start | bytes 405512 | tf_op jit(solution)/shard_map/ppermute | solution.py:747
  14.2 50.4 %all-to-all-start = ((bf16[8,528,128]{2,1,0:T(8,128)(2,1)}), bf16[8,528,128]{2,1,0:T(8,128)(2,1)S(1)}, u32[]{:S(2)}, u32[]{:S(2)}) async-start(bf16[8,528,128]{2,1,0:T(8,128)(2,1)} %split_pieces.3), calls=%async_computation | async-start | bytes 2162688 | tf_op jit(solution)/shard_map/all_to_all | solution.py:752
  19.1 10.8 %collective-permute-start.4 = (bf16[528,128]{1,0:T(8,128)(2,1)S(1)}, bf16[528,128]{1,0:T(8,128)(2,1)S(1)}, u32[]{:S(2)}, u32[]{:S(2)}) collective-permute-start(bf16[528,128]{1,0:T(8,128)(2,1)S(1)} %get-tuple-element.31), channel_id=1, source_target_pairs={{0,12},{1,13},{2,14},{3,15},{4,8},{5,9},{6,10},{7,11},{8,4},{9,5},... | collective-permute-start | bytes 405512 | tf_op jit(solution)/shard_map/ppermute | solution.py:747
  20.6 17.3 %collective-permute-start.5 = (bf16[528,128]{1,0:T(8,128)(2,1)S(1)}, bf16[528,128]{1,0:T(8,128)(2,1)S(1)}, u32[]{:S(2)}, u32[]{:S(2)}) collective-permute-start(bf16[528,128]{1,0:T(8,128)(2,1)S(1)} %get-tuple-element.32), channel_id=1, source_target_pairs={{0,13},{1,12},{2,15},{3,14},{4,9},{5,8},{6,11},{7,10},{8,5},{9,4},... | collective-permute-start | bytes 405512 | tf_op jit(solution)/shard_map/ppermute | solution.py:747
  21.1 22.4 %collective-permute-start.6 = (bf16[528,128]{1,0:T(8,128)(2,1)S(1)}, bf16[528,128]{1,0:T(8,128)(2,1)S(1)}, u32[]{:S(2)}, u32[]{:S(2)}) collective-permute-start(bf16[528,128]{1,0:T(8,128)(2,1)S(1)} %get-tuple-element.33), channel_id=1, source_target_pairs={{0,14},{1,15},{2,12},{3,13},{4,10},{5,11},{6,8},{7,9},{8,6},{9,7},... | collective-permute-start | bytes 405512 | tf_op jit(solution)/shard_map/ppermute | solution.py:747
  23.6 30.4 %collective-permute-start.7 = (bf16[528,128]{1,0:T(8,128)(2,1)S(1)}, bf16[528,128]{1,0:T(8,128)(2,1)S(1)}, u32[]{:S(2)}, u32[]{:S(2)}) collective-permute-start(bf16[528,128]{1,0:T(8,128)(2,1)S(1)} %get-tuple-element.34), channel_id=1, source_target_pairs={{0,15},{1,14},{2,13},{3,12},{4,11},{5,10},{6,9},{7,8},{8,7},{9,6},... | collective-permute-start | bytes 405512 | tf_op jit(solution)/shard_map/ppermute | solution.py:747
  23.6 33.3 %collective-permute-start.1 = (bf16[528,128]{1,0:T(8,128)(2,1)S(1)}, bf16[528,128]{1,0:T(8,128)(2,1)S(1)}, u32[]{:S(2)}, u32[]{:S(2)}) collective-permute-start(bf16[528,128]{1,0:T(8,128)(2,1)S(1)} %get-tuple-element.28), channel_id=1, source_target_pairs={{0,9},{1,8},{2,11},{3,10},{4,13},{5,12},{6,15},{7,14},{8,1},{9,0},... | collective-permute-start | bytes 405512 | tf_op jit(solution)/shard_map/ppermute | solution.py:747
  29.9 29.9 %collective-permute-start.2 = (bf16[528,128]{1,0:T(8,128)(2,1)S(1)}, bf16[528,128]{1,0:T(8,128)(2,1)S(1)}, u32[]{:S(2)}, u32[]{:S(2)}) collective-permute-start(bf16[528,128]{1,0:T(8,128)(2,1)S(1)} %get-tuple-element.29), channel_id=1, source_target_pairs={{0,10},{1,11},{2,8},{3,9},{4,14},{5,15},{6,12},{7,13},{8,2},{9,3},... | collective-permute-start | bytes 405512 | tf_op jit(solution)/shard_map/ppermute | solution.py:747
  37.8 24.9 %collective-permute-start.3 = (bf16[528,128]{1,0:T(8,128)(2,1)S(1)}, bf16[528,128]{1,0:T(8,128)(2,1)S(1)}, u32[]{:S(2)}, u32[]{:S(2)}) collective-permute-start(bf16[528,128]{1,0:T(8,128)(2,1)S(1)} %get-tuple-element.30), channel_id=1, source_target_pairs={{0,11},{1,10},{2,9},{3,8},{4,15},{5,14},{6,13},{7,12},{8,3},{9,2},... | collective-permute-start | bytes 405512 | tf_op jit(solution)/shard_map/ppermute | solution.py:747
  94.4 5.9 %collective-permute-start.8 = (bf16[512,128]{1,0:T(8,128)(2,1)S(1)}, bf16[512,128]{1,0:T(8,128)(2,1)S(1)}, u32[]{:S(2)}, u32[]{:S(2)}) collective-permute-start(bf16[512,128]{1,0:T(8,128)(2,1)S(1)} %get-tuple-element.41), channel_id=1, source_target_pairs={{0,8},{1,9},{2,10},{3,11},{4,12},{5,13},{6,14},{7,15},{8,0},{9,1},... | collective-permute-start | bytes 393224 | tf_op jit(solution)/shard_map/ppermute | solution.py:747
  105.4 39.5 %all-to-all-start.1 = ((bf16[8,512,128]{2,1,0:T(8,128)(2,1)}), bf16[8,512,128]{2,1,0:T(8,128)(2,1)S(1)}, u32[]{:S(2)}, u32[]{:S(2)}) async-start(bf16[8,512,128]{2,1,0:T(8,128)(2,1)} %update_pieces.3), calls=%async_computation.1 | async-start | bytes 2097152 | tf_op jit(solution)/shard_map/all_to_all | solution.py:752
  113.7 15.1 %collective-permute-start.9 = (bf16[512,128]{1,0:T(8,128)(2,1)S(1)}, bf16[512,128]{1,0:T(8,128)(2,1)S(1)}, u32[]{:S(2)}, u32[]{:S(2)}) collective-permute-start(bf16[512,128]{1,0:T(8,128)(2,1)S(1)} %get-tuple-element.42), channel_id=1, source_target_pairs={{0,9},{1,8},{2,11},{3,10},{4,13},{5,12},{6,15},{7,14},{8,1},{9,0},... | collective-permute-start | bytes 393224 | tf_op jit(solution)/shard_map/ppermute | solution.py:747
  113.7 18.4 %collective-permute-start.10 = (bf16[512,128]{1,0:T(8,128)(2,1)S(1)}, bf16[512,128]{1,0:T(8,128)(2,1)S(1)}, u32[]{:S(2)}, u32[]{:S(2)}) collective-permute-start(bf16[512,128]{1,0:T(8,128)(2,1)S(1)} %get-tuple-element.43), channel_id=1, source_target_pairs={{0,10},{1,11},{2,8},{3,9},{4,14},{5,15},{6,12},{7,13},{8,2},{9,3},... | collective-permute-start | bytes 393224 | tf_op jit(solution)/shard_map/ppermute | solution.py:747
  117.3 30.2 %collective-permute-start.11 = (bf16[512,128]{1,0:T(8,128)(2,1)S(1)}, bf16[512,128]{1,0:T(8,128)(2,1)S(1)}, u32[]{:S(2)}, u32[]{:S(2)}) collective-permute-start(bf16[512,128]{1,0:T(8,128)(2,1)S(1)} %get-tuple-element.44), channel_id=1, source_target_pairs={{0,11},{1,10},{2,9},{3,8},{4,15},{5,14},{6,13},{7,12},{8,3},{9,2},... | collective-permute-start | bytes 393224 | tf_op jit(solution)/shard_map/ppermute | solution.py:747
  117.5 31.0 %collective-permute-start.12 = (bf16[512,128]{1,0:T(8,128)(2,1)S(1)}, bf16[512,128]{1,0:T(8,128)(2,1)S(1)}, u32[]{:S(2)}, u32[]{:S(2)}) collective-permute-start(bf16[512,128]{1,0:T(8,128)(2,1)S(1)} %get-tuple-element.45), channel_id=1, source_target_pairs={{0,12},{1,13},{2,14},{3,15},{4,8},{5,9},{6,10},{7,11},{8,4},{9,5},... | collective-permute-start | bytes 393224 | tf_op jit(solution)/shard_map/ppermute | solution.py:747
  118.8 31.4 %collective-permute-start.13 = (bf16[512,128]{1,0:T(8,128)(2,1)S(1)}, bf16[512,128]{1,0:T(8,128)(2,1)S(1)}, u32[]{:S(2)}, u32[]{:S(2)}) collective-permute-start(bf16[512,128]{1,0:T(8,128)(2,1)S(1)} %get-tuple-element.46), channel_id=1, source_target_pairs={{0,13},{1,12},{2,15},{3,14},{4,9},{5,8},{6,11},{7,10},{8,5},{9,4},... | collective-permute-start | bytes 393224 | tf_op jit(solution)/shard_map/ppermute | solution.py:747
  128.8 25.1 %collective-permute-start.14 = (bf16[512,128]{1,0:T(8,128)(2,1)S(1)}, bf16[512,128]{1,0:T(8,128)(2,1)S(1)}, u32[]{:S(2)}, u32[]{:S(2)}) collective-permute-start(bf16[512,128]{1,0:T(8,128)(2,1)S(1)} %get-tuple-element.47), channel_id=1, source_target_pairs={{0,14},{1,15},{2,12},{3,13},{4,10},{5,11},{6,8},{7,9},{8,6},{9,7},... | collective-permute-start | bytes 393224 | tf_op jit(solution)/shard_map/ppermute | solution.py:747
  132.1 24.6 %collective-permute-start.15 = (bf16[512,128]{1,0:T(8,128)(2,1)S(1)}, bf16[512,128]{1,0:T(8,128)(2,1)S(1)}, u32[]{:S(2)}, u32[]{:S(2)}) collective-permute-start(bf16[512,128]{1,0:T(8,128)(2,1)S(1)} %get-tuple-element.48), channel_id=1, source_target_pairs={{0,15},{1,14},{2,13},{3,12},{4,11},{5,10},{6,9},{7,8},{8,7},{9,6},... | collective-permute-start | bytes 393224 | tf_op jit(solution)/shard_map/ppermute | solution.py:747

commit v8 on v7

--- a/solution.py
+++ b/solution.py
@@ -413,7 +413,7 @@
     for fetch in fetches:
         fetch.start()
     for n, (at, held, mine) in enumerate(zip(positions, helds, copies)):
-        out_ref = out_refs[n] if at >= half else out_refs[0].at[n]
+        out_ref = out_refs[1 + at - half] if at >= half else out_refs[0].at[at]
         for copy in mine:
             copy.wait()
         slab = device_at(at, half)
@@ -432,71 +432,57 @@
         fetch.wait()
 
 
-def split_pieces(row, slabs, raw, near, gates, fields):
+def split_pieces(row, slabs, raw, fields):
     lines = row.shape[1] // slabs // LANES
     half = slabs // 2
-    count = half
-    size = lines + TILE + (raw + TILE if near and raw else 0)
-    if near:
-        out_shape = [jax.ShapeDtypeStruct((count, size, LANES), BF16)]
-    else:
-        out_shape = [jax.ShapeDtypeStruct((size, LANES), BF16)] * count
+    rim = lines + TILE
+    size = rim + (raw + TILE if raw else 0)
+    out_shape = [jax.ShapeDtypeStruct((half, size, LANES), BF16)]
+    out_shape += [jax.ShapeDtypeStruct((rim, LANES), BF16)] * half
     out_shape += [jax.ShapeDtypeStruct((lines, LANES), BF16)] * len(fields)
     out_shape += [jax.ShapeDtypeStruct((max(raw, TILE), LANES), BF16)] * len(fields)
-    positions = range(half) if near else range(half, slabs)
-    return call(
-        functools.partial(split_pieces_body, positions, half, raw, lines, len(gates), len(fields)),
+    return call(
+        functools.partial(split_pieces_body, range(slabs), half, raw, lines, 0, len(fields)),
         "split_pieces",
-        moved=6 * count * size * LANES,
-        in_specs=[IN_HBM] * (1 + len(fields)) + [IN_VMEM] * len(gates),
+        moved=6 * half * (size + rim) * LANES,
+        in_specs=[IN_HBM] * (1 + len(fields)),
         out_specs=[IN_VMEM] * len(out_shape),
         out_shape=out_shape,
-        scratch_shapes=[pltpu.VMEM((1, (size + TILE) * LANES), BF16)] * count
-        + [pltpu.SemaphoreType.DMA((5 * count + 2 * len(fields),))],
-    )(row, *fields, *gates)
-
-
-def join_pieces_body(positions, half, raw, lines, begun, *refs):
-    count = len(positions)
-    pieces, row_ref, helds, sems = refs[begun : -count - 2], refs[-count - 2], refs[-count - 1 : -1], refs[-1]
-    cells = lines * LANES
-    skip = raw * LANES
+        scratch_shapes=[pltpu.VMEM((1, (size + TILE) * LANES), BF16)] * half
+        + [pltpu.VMEM((1, (rim + TILE) * LANES), BF16)] * half
+        + [pltpu.SemaphoreType.DMA((5 * slabs + 2 * len(fields),))],
+    )(row, *fields)
+
+
+def join_pieces_body(pieces, half, lines, begun, arrays, *refs):
+    row_ref, helds, sems = refs[begun + arrays], refs[begun + arrays + 1 : -1], refs[-1]
     copies = []
-    for n, (at, held) in enumerate(zip(positions, helds)):
-        piece = pieces[n][...] if at >= half else pieces[0][n]
+    for (array, lead, at, across, begin), held in zip(pieces, helds):
+        ref = refs[begun + array]
+        piece = ref[...] if lead is None else ref[lead]
         held[...] = piece.reshape(held.shape)
-
-        def store(begin, size, start):
-            target = row_ref.at[:, pl.ds(pl.multiple_of(start, GRID_Y), size)]
-            copies.append(pltpu.make_async_copy(held.at[:, pl.ds(begin, size)], target, sems.at[len(copies)]))
-            copies[-1].start()
-
         slab = device_at(at, half)
-        if at >= half:
-            store(0, cells - skip, slab * cells + skip)
-        else:
-            store(0, cells, slab * cells)
-            if raw:
-                store(cells, skip, (slab ^ half) * cells)
+        start = ((slab ^ half if across else slab) * lines + begin) * LANES
+        target = row_ref.at[:, pl.ds(pl.multiple_of(start, GRID_Y), held.shape[1])]
+        copies.append(pltpu.make_async_copy(held, target, sems.at[len(copies)]))
+        copies[-1].start()
     for copy in copies:
         copy.wait()
 
 
-def join_pieces(row, slabs, raw, pieces, positions):
-    cells = NCELL // slabs
-    size = pieces[0].shape[-2] * LANES
+def join_pieces(row, slabs, arrays, pieces):
+    sizes = [arrays[piece[0]].shape[-2] * LANES for piece in pieces]
     begun = [] if row is None else [row]
     return call(
-        functools.partial(join_pieces_body, positions, slabs // 2, raw, cells // LANES, len(begun)),
+        functools.partial(join_pieces_body, pieces, slabs // 2, NCELL // slabs // LANES, len(begun), len(arrays)),
         "join_pieces",
-        moved=6 * size * len(positions),
-        in_specs=[IN_HBM] * len(begun) + [IN_VMEM] * len(pieces),
+        moved=6 * sum(sizes),
+        in_specs=[IN_HBM] * len(begun) + [IN_VMEM] * len(arrays),
         out_specs=IN_HBM,
         out_shape=jax.ShapeDtypeStruct((1, NCELL), BF16),
         input_output_aliases={0: 0} if begun else {},
-        scratch_shapes=[pltpu.VMEM((1, size), BF16)] * len(positions)
-        + [pltpu.SemaphoreType.DMA((2 * len(positions),))],
-    )(*begun, *pieces)
+        scratch_shapes=[pltpu.VMEM((1, size), BF16) for size in sizes] + [pltpu.SemaphoreType.DMA((len(sizes),))],
+    )(*begun, *arrays)
 
 
 def owners(total, dtype):
@@ -529,10 +515,11 @@
     owner = owners(total, F32)
     half_way = jnp.dot(equal, owner, **exact)
     gram = lax.dot_general(owner, half_way, (((0,), (0,)), ((), ())), **exact)
-    out_ref[...] = jnp.concatenate([gram, jnp.zeros((total, LANES - total), F32)], axis=1)
-
-
-def gram_pieces(near, far, lines, gates):
+    gram = jnp.concatenate([gram, jnp.zeros((total, LANES - total), F32)], axis=1)
+    out_ref[...] = jnp.broadcast_to(gram[None], out_ref.shape)
+
+
+def gram_pieces(near, far, lines, gates, early):
     total = 2 * len(far)
     wide = total * TILE
     return call(
@@ -540,11 +527,11 @@
         "gram_pieces",
         flops=2 * wide * wide * LANES * (lines // TILE),
         moved=2 * total * lines * LANES,
-        in_specs=[IN_VMEM] * (1 + len(far)) + [IN_HBM] * len(gates),
+        in_specs=[IN_VMEM] * (1 + len(far)) + [IN_HBM] * len(gates) + [IN_VMEM] * len(early),
         out_specs=IN_VMEM,
-        out_shape=jax.ShapeDtypeStruct((total, LANES), F32),
+        out_shape=jax.ShapeDtypeStruct((total, total, LANES), F32),
         scratch_shapes=[pltpu.VMEM((wide, wide), F32)],
-    )(near, *far, *gates)
+    )(near, *far, *gates, *early)
 
 
 def gradient_pieces_body(views, arrays, numbers, *refs):
@@ -639,21 +626,27 @@
     )(near)
 
 
-def update_pieces_body(near, half, raw, lines, groups, extra, gates, near_ref, *refs):
+def mix(mixer, own, numbers_ref, total, states, slopes):
+    high = mixer.shape[0]
+    rate = numbers_ref[2:3, :1] / total
+    coeff = 2.0 * numbers_ref[1:2, :1] / numbers_ref[:1, :1]
+    both = jnp.concatenate([slopes, states], axis=1)
+    mixed = jnp.dot(mixer[...], both, preferred_element_type=F32)
+    drive, pulled = mixed[:, :LANES], mixed[:, LANES:]
+    return (states[:high].astype(F32) * own[...] + rate * (drive - coeff * pulled)).astype(BF16)
+
+
+def update_pieces_body(half, raw, lines, groups, near_ref, *refs):
     total = 2 * half
-    refs = refs[gates:]
     far_refs, numbers_ref, grams_ref, refs = refs[:half], refs[half], refs[half + 1], refs[half + 2 :]
-    group_refs, refs = refs[: len(groups)], refs[len(groups) :]
-    raw_refs, out_refs, (grads, raw_grads, mixer, own, sems) = refs[:extra], refs[extra:-5], refs[-5:]
+    group_refs, near_out, far_outs = refs[: len(groups)], refs[-5 - half], refs[-4 - half : -4]
+    mixer, own, grads, sems = refs[-4:]
     wide = total * TILE
     high = half * TILE
-    first = 0 if near else high
     fetches = []
     for group, group_ref in zip(groups, group_refs):
         for j, at in enumerate(group):
             fetches.append(pltpu.make_async_copy(group_ref.at[j], grads.at[at], sems.at[len(fetches)]))
-    if extra:
-        fetches.append(pltpu.make_async_copy(raw_refs[1], raw_grads, sems.at[len(fetches)]))
     for fetch in fetches:
         fetch.start()
     gram = jnp.sum(grams_ref[...], axis=0)[:, :total]
@@ -667,80 +660,88 @@
     across = jnp.sum(diagonal, axis=0, keepdims=True)
     kernel = jnp.exp(-(down + across - 2.0 * gram) / (spread * NCELL)).astype(BF16)
     owner = owners(total, BF16)
-    half_way = jnp.dot(owner[first : first + high], kernel, preferred_element_type=F32).astype(BF16)
+    half_way = jnp.dot(owner, kernel, preferred_element_type=F32).astype(BF16)
     full = lax.dot_general(half_way, owner, (((1,), (1,)), ((), ())), preferred_element_type=F32)
-    full = jnp.where(same_line(total)[first : first + high], full, 0.0)
+    full = jnp.where(same_line(total), full, 0.0)
     mixer[...] = full.astype(BF16)
     ksum = jnp.sum(full, axis=1, keepdims=True)
-    own[...] = jnp.broadcast_to(1.0 + rate * coeff * ksum, (high, LANES))
+    own[...] = jnp.broadcast_to(1.0 + rate * coeff * ksum, (wide, LANES))
     for fetch in fetches:
         fetch.wait()
 
-    def mix(states, slopes):
-        both = jnp.concatenate([slopes, states], axis=1)
-        mixed = jnp.dot(mixer[...], both, preferred_element_type=F32)
-        drive, pulled = mixed[:, :LANES], mixed[:, LANES:]
-        kept = states[first : first + high].astype(F32)
-        return (kept * own[...] + rate * (drive - coeff * pulled)).astype(BF16)
-
-    def put(to, new):
-        if near:
-            out_refs[0][:, lines_of(to, TILE), :] = new.reshape(half, TILE, LANES)
-        else:
-            for j, out_ref in enumerate(out_refs):
-                out_ref[lines_of(to, TILE), :] = new[j * TILE : (j + 1) * TILE]
-
-    def slab_step(i, carry):
+    def step(with_far, i, carry):
         for t in range(BLOCK // TILE):
             at = i * BLOCK + t * TILE
-            states = [near_ref[:, lines_of(at, TILE), :].reshape(high, LANES)]
-            states += [ref[lines_of(at, TILE), :] for ref in far_refs]
-            slopes = grads[:, lines_of(at, TILE), :].reshape(wide, LANES)
-            put(at if near else at - raw, mix(jnp.concatenate(states, axis=0), slopes))
+            part = lines_of(at, TILE)
+            states = [near_ref[:, part, :].reshape(high, LANES)] + [ref[part, :] for ref in far_refs]
+            slopes = grads[:, part, :].reshape(wide, LANES)
+            new = mix(mixer, own, numbers_ref, total, jnp.concatenate(states, axis=0), slopes)
+            near_out[:, part, :] = new[:high].reshape(half, TILE, LANES)
+            if with_far:
+                for x, far_out in enumerate(far_outs):
+                    far_out[lines_of(at - raw, TILE), :] = new[high + x * TILE : high + (x + 1) * TILE]
         return carry
 
-    def raw_step(i, carry):
-        here = lax.axis_index("slab").astype(jnp.int32) % half
+    lax.fori_loop(0, raw // BLOCK, functools.partial(step, False), 0)
+    lax.fori_loop(raw // BLOCK, lines // BLOCK, functools.partial(step, True), 0)
+
+
+def update_pieces(numbers, grams, near, far, grads, groups, gates, raw, lines):
+    half = len(far)
+    total = 2 * half
+    wide = total * TILE
+    out_shape = [jax.ShapeDtypeStruct((half, lines, LANES), BF16)]
+    out_shape += [jax.ShapeDtypeStruct((lines - raw, LANES), BF16)] * half
+    out_shape += [jax.ShapeDtypeStruct((wide, wide), BF16), jax.ShapeDtypeStruct((wide, LANES), F32)]
+    return call(
+        functools.partial(update_pieces_body, half, raw, lines, groups),
+        "update_pieces",
+        flops=4 * wide * wide * LANES * (lines // TILE),
+        moved=6 * total * lines * LANES,
+        in_specs=[IN_VMEM] * (half + 3) + [IN_HBM] * len(groups) + [IN_VMEM] * len(gates),
+        out_specs=[IN_VMEM] * len(out_shape),
+        out_shape=out_shape,
+        scratch_shapes=[pltpu.VMEM((total, lines, LANES), BF16), pltpu.SemaphoreType.DMA((total,))],
+    )(near, *far, numbers, grams, *grads, *gates)
+
+
+def update_raw_body(lines, near_ref, across_ref, mixer, own, numbers_ref, grads_ref, out_ref, grads, sem):
+    half, raw, _ = out_ref.shape
+    high = half * TILE
+    fetch = pltpu.make_async_copy(grads_ref, grads, sem)
+    fetch.start()
+    fetch.wait()
+    here = lax.axis_index("slab").astype(jnp.int32) % half
+
+    def step(i, carry):
         for t in range(BLOCK // TILE):
             at = i * BLOCK + t * TILE
             part = lines_of(at, TILE)
             states = [near_ref[:, lines_of(lines + TILE + at, TILE), :].reshape(high, LANES)]
-            slopes = [raw_grads[:half, part, :].reshape(high, LANES)]
+            slopes = [grads[:half, part, :].reshape(high, LANES)]
             for x in range(half):
-                states += [raw_refs[0][here ^ x, part, :]]
-                slopes += [raw_grads[half + (here ^ x), part, :]]
-            put(lines + at, mix(jnp.concatenate(states, axis=0), jnp.concatenate(slopes, axis=0)))
+                states += [across_ref[here ^ x, part, :]]
+                slopes += [grads[half + (here ^ x), part, :]]
+            states, slopes = jnp.concatenate(states, axis=0), jnp.concatenate(slopes, axis=0)
+            new = mix(mixer.at[:high, :], own.at[:high, :], numbers_ref, 2 * half, states, slopes)
+            out_ref[:, part, :] = new.reshape(half, TILE, LANES)
         return carry
 
-    lax.fori_loop(0 if near else raw // BLOCK, lines // BLOCK, slab_step, 0)
-    if near and raw:
-        lax.fori_loop(0, raw // BLOCK, raw_step, 0)
-
-
-def update_pieces(numbers, grams, near_states, far_states, grads, groups, raw_parts, gates, raw, lines, near):
-    half = len(far_states)
-    total = 2 * half
-    wide = total * TILE
-    if near:
-        out_shape = [jax.ShapeDtypeStruct((half, lines + raw, LANES), BF16)]
-    else:
-        out_shape = [jax.ShapeDtypeStruct((lines - raw, LANES), BF16)] * half
-    return call(
-        functools.partial(update_pieces_body, near, half, raw, lines, groups, len(raw_parts), len(gates)),
-        "update_pieces",
-        flops=4 * half * TILE * wide * LANES * (lines // TILE),
-        moved=2 * (2 * total + half) * lines * LANES,
-        in_specs=[IN_VMEM] * (half + 3 + len(gates)) + [IN_HBM] * len(groups) + [IN_VMEM, IN_HBM][: len(raw_parts)],
-        out_specs=[IN_VMEM] * len(out_shape),
-        out_shape=out_shape,
-        scratch_shapes=[
-            pltpu.VMEM((total, lines, LANES), BF16),
-            pltpu.VMEM((total, max(raw, TILE), LANES), BF16),
-            pltpu.VMEM((half * TILE, wide), BF16),
-            pltpu.VMEM((half * TILE, LANES), F32),
-            pltpu.SemaphoreType.DMA((total + 1,)),
-        ],
-    )(near_states, *gates, *far_states, numbers, grams, *grads, *raw_parts)
+    lax.fori_loop(0, raw // BLOCK, step, 0)
+
+
+def update_raw(near, across, mixer, own, numbers, grads, raw, lines):
+    half = near.shape[0]
+    return call(
+        functools.partial(update_raw_body, lines),
+        "update_raw",
+        flops=2 * mixer.size * LANES * (raw // TILE),
+        moved=12 * half * raw * LANES,
+        in_specs=[IN_VMEM] * 5 + [IN_HBM],
+        out_specs=IN_VMEM,
+        out_shape=jax.ShapeDtypeStruct((half, raw, LANES), BF16),
+        scratch_shapes=[pltpu.VMEM((2 * half, raw, LANES), BF16), pltpu.SemaphoreType.DMA],
+    )(near, across, mixer, own, numbers, grads)
 
 
 def exchange(piece, k, slabs):
@@ -752,9 +753,8 @@
     return lax.all_to_all(pieces, "slab", 0, 0, axis_index_groups=groups, tiled=True)
 
 
-RAW = 0
-GRADIENTS = ((8, 9, 10, 11), (0, 1, 2, 3, 4, 5, 6, 7), (12, 13, 14, 15))
-JOINS = ((0, 1, 2, 3, 4, 5, 6, 7), (8, 9, 10, 11), (12, 13), (14, 15))
+RAW = 128
+GRADIENTS = ((8, 9, 10, 11), (12, 13, 14, 15), (0, 1, 2, 3, 4, 5, 6, 7))
 
 
 def by_halves(particles, observed, precision, spread, anneal, step_size):
@@ -763,12 +763,14 @@
     lines = NCELL // slabs // LANES
     row = in_hbm(particles)
     fields = [in_hbm(field.reshape(-1, LANES)) for field in (observed, precision)]
-    *far, obs, prec, raw_obs, raw_prec = split_pieces(row, slabs, RAW, False, [], fields)
+    near, *far = split_pieces(row, slabs, RAW, fields)
+    far, (obs, prec, raw_obs, raw_prec) = far[:half], far[half:]
+    near = swap_near(near, slabs)
     far = [exchange(piece, half + x, slabs) for x, piece in enumerate(far)]
-    near = swap_near(split_pieces(row, slabs, RAW, True, far[:1], [])[0], slabs)
-    extra = []
+    early, gates = [], []
     if RAW:
-        extra = [exchange(raw_states(near, RAW, lines), half, slabs)]
+        early = [raw_states(near, RAW, lines)]
+        gates = [exchange(early[0], half, slabs)]
     grads = []
     numbers = [spread, anneal, step_size]
     for group in GRADIENTS:
@@ -779,21 +781,22 @@
         slopes, rows = gradient_pieces(arrays, tuple(views), obs, prec, [] if grads else numbers)
         grads.append(in_hbm(slopes))
         numbers = numbers if len(grads) > 1 else rows
-    grams = lax.all_gather(gram_pieces(near, far, lines, grads[:1]), "slab")
+    grams = swap(gram_pieces(near, far, lines, grads[:1], early))
+    new_near, *new_far = update_pieces(numbers, grams, near, far, grads, GRADIENTS, gates, RAW, lines)
+    new_far, (mixer, own) = new_far[:half], new_far[half:]
+    new_near = swap_near(new_near, slabs)
+    new_far = [exchange(piece, half + x, slabs) for x, piece in enumerate(new_far)]
     if RAW:
         views = [(0, k, lines + TILE) for k in range(half)] + [(1, k, 0) for k in range(half)]
-        slopes, _ = gradient_pieces([near] + extra, tuple(views), raw_obs, raw_prec, [])
-        extra += [in_hbm(slopes)]
-    new_far = update_pieces(numbers, grams, near, far, grads, GRADIENTS, [], [], RAW, lines, False)
-    new_far = [exchange(piece, half + x, slabs) for x, piece in enumerate(new_far)]
-    gates = new_far[:1]
-    new_near = update_pieces(numbers, grams, near, far, grads, GRADIENTS, extra, gates, RAW, lines, True)[0]
-    new_near = swap_near(new_near, slabs)
-    row = None
-    for group in JOINS:
-        pieces = [new_near] if group[0] < half else [new_far[k - half] for k in group]
-        row = join_pieces(row, slabs, RAW, pieces, group)
-    return row
+        slopes, _ = gradient_pieces([near] + gates, tuple(views), raw_obs, raw_prec, [])
+        new_raw = swap_near(update_raw(near, gates[0], mixer, own, numbers, in_hbm(slopes), RAW, lines), slabs)
+    row = join_pieces(None, slabs, [new_near], [(0, k, k, False, 0) for k in range(half)])
+    for group in ((0, 1, 2, 3), (4, 5)):
+        pieces = [(n, None, half + x, False, RAW) for n, x in enumerate(group)]
+        row = join_pieces(row, slabs, [new_far[x] for x in group], pieces)
+    if RAW:
+        row = join_pieces(row, slabs, [new_raw], [(0, k, k, True, 0) for k in range(half)])
+    return join_pieces(row, slabs, new_far[6:], [(n, None, half + 6 + n, False, RAW) for n in range(half - 6)])
 
 
 def on_device(particles, observed, precision, spread, anneal, step_size):

time: 158 us -> 155 us (0.981)
  blocking collectives: 20.2 us -> 0 us
  local copies, waits for them, and re-layouts: 0 us -> 9.8 us
  waiting for transfers between devices: 55.3 us -> 64 us
  starting transfers between devices: 50.1 us -> 48.4 us
    all_gather x1 -> x0, blocking collectives: 20.2 us -> none  [by_halves(): grams = lax.all_gather(gram_pieces(near, far, lines, grads[:1]), 'slab')]
    ppermute x16 -> x17, waiting for transfers between devices: 45.2 us -> 57.3 us  [exchange(): return lax.ppermute(piece, 'slab', [(i, i ^ k) for i in range(slabs)])]
    unnamed x0 -> x38, local copies, waits for them, and re-layouts: none -> 9.8 us
    ppermute x16 -> x17, starting transfers between devices: 36.8 us -> 28.3 us  [exchange(): return lax.ppermute(piece, 'slab', [(i, i ^ k) for i in range(slabs)])]
    all_to_all x0 -> x1, starting transfers between devices: none -> 4.47 us  [swap(): lax.all_to_all(slabs, 'slab', split_axis=0, concat_axis=0, tiled=True)]
    all_to_all x2 -> x3, waiting for transfers between devices: 10 us -> 6.32 us  [swap_near(): lax.all_to_all(pieces, 'slab', 0, 0, axis_index_groups=groups, tiled=True)]
    all_to_all x2 -> x3, starting transfers between devices: 13.3 us -> 15.6 us  [swap_near(): lax.all_to_all(pieces, 'slab', 0, 0, axis_index_groups=groups, tiled=True)]
    pallas_call x8 -> x9, Pallas kernels: 19.8 us -> 17.7 us  [the longest x5 6.09 us: join_pieces(): call(functools.partial(join_pieces_body, pieces, slabs // 2, NCELL // sla...]
  transfers between devices with their start and end apart: 18 -> 21, of which waited for: 11 -> 16; matrix products, arithmetic and copies ran while one was open for 0% -> 0% of each run, Pallas kernels for 5% -> 13%
where the time goes in v8:
time: 155 us; the launch traced here: 154 us
  waiting for transfers between devices  64 us (41%)
  starting transfers between devices  48.4 us (31%)
  Pallas kernels  29.9 us (19%)
  local copies, waits for them, and re-layouts  9.8 us (6%)
  between operations  2.15 us (1%)
    ppermute x17, waiting for transfers between devices, exchange(): return lax.ppermute(piece, 'slab', [(i, i ^ k) for i in range(slabs)])  57.3 us
    ppermute x17, starting transfers between devices, exchange(): return lax.ppermute(piece, 'slab', [(i, i ^ k) for i in range(slabs)])  28.3 us
    all_to_all x3, starting transfers between devices, swap_near(): lax.all_to_all(pieces, 'slab', 0, 0, axis_index_groups=groups, tiled=True)  15.6 us
    unnamed x38, local copies, waits for them, and re-layouts  9.8 us
    pallas_call x4, Pallas kernels, gradient_pieces(): call(functools.partial(gradient_pieces_body, views, len(arrays), len(numb...  9.45 us
    all_to_all x3, waiting for transfers between devices, swap_near(): lax.all_to_all(pieces, 'slab', 0, 0, axis_index_groups=groups, tiled=True)  6.32 us
    pallas_call x5, Pallas kernels, join_pieces(): call(functools.partial(join_pieces_body, pieces, slabs // 2, NCELL // sla...  6.09 us
    pallas_call x1, Pallas kernels, update_pieces(): call(functools.partial(update_pieces_body, half, raw, lines, groups), 'up...  4.65 us
  transfers between devices with their start and end apart: 21, of which 16 were waited for; matrix products, arithmetic and copies ran while one was open for 0% of the time, Pallas kernels for 13%

profile of v8, /device:TPU:9, one launch (start us, length us, event | category | flops | bytes accessed | tf_op | source)
XLA Modules:
  0.0 154.1 jit_solution(3702929665187845314)
XLA Ops:
  0.0 4.6 %split_pieces.1 = (bf16[8,672,128]{2,1,0:T(8,128)(2,1)}, bf16[528,128]{1,0:T(8,128)(2,1)S(1)}, bf16[528,128]{1,0:T(8,128)(2,1)S(1)}, bf16[528,128]{1,0:T(8,128)(...) custom-call(bf16[1,1048576]{1,0:T(2,128)(2,1)} %row_ref.1, ...), custom_call_target="tpu_custom_call" | custom-call | bytes 7372800 | tf_op jit(solution)/shard_map/split_pieces/pallas_call | solution.py:444
  4.6 4.6 %all-to-all-start = ((bf16[8,672,128]{2,1,0:T(8,128)(2,1)}), bf16[8,672,128]{2,1,0:T(8,128)(2,1)S(1)}, u32[]{:S(2)}, u32[]{:S(2)}) async-start(bf16[8,672,128]{2,1,0:T(8,128)(2,1)} %get-tuple-element.34), calls=%async_computation | async-start | bytes 2752512 | tf_op jit(solution)/shard_map/all_to_all | solution.py:753
  9.2 2.3 %collective-permute-start = (bf16[528,128]{1,0:T(8,128)(2,1)S(1)}, bf16[528,128]{1,0:T(8,128)(2,1)S(1)}, u32[]{:S(2)}, u32[]{:S(2)}) collective-permute-start(bf16[528,128]{1,0:T(8,128)(2,1)S(1)} %get-tuple-element.35), channel_id=1, source_target_pairs={{0,8},{1,9},{2,10},{3,11},{4,12},{5,13},{6,14},{7,15},{8,0},{9,1},... | collective-permute-start | bytes 405512 | tf_op jit(solution)/shard_map/ppermute | solution.py:748
  12.1 3.2 %collective-permute-start.2 = (bf16[528,128]{1,0:T(8,128)(2,1)S(1)}, bf16[528,128]{1,0:T(8,128)(2,1)S(1)}, u32[]{:S(2)}, u32[]{:S(2)}) collective-permute-start(bf16[528,128]{1,0:T(8,128)(2,1)S(1)} %get-tuple-element.37), channel_id=1, source_target_pairs={{0,10},{1,11},{2,8},{3,9},{4,14},{5,15},{6,12},{7,13},{8,2},{9,3},... | collective-permute-start | bytes 405512 | tf_op jit(solution)/shard_map/ppermute | solution.py:748
  15.6 1.0 collective-permute-start.4
  16.6 13.5 %collective-permute-done.refs_0_ = bf16[528,128]{1,0:T(8,128)(2,1)S(1)} collective-permute-done((bf16[528,128]{1,0:T(8,128)(2,1)S(1)}, bf16[528,128]{1,0:T(8,128)(2,1)S(1)}, u32[]{:S(2)}, u32[]{:S(2)}) %collective-permute-start) | collective-permute-done | bytes 135200 | tf_op jit(solution)/shard_map/ppermute | solution.py:748
  30.2 3.5 %collective-permute-done.1.refs_1_ = bf16[528,128]{1,0:T(8,128)(2,1)S(1)} collective-permute-done((bf16[528,128]{1,0:T(8,128)(2,1)S(1)}, bf16[528,128]{1,0:T(8,128)(2,1)S(1)}, u32[]{:S(2)}, u32[]{:S(2)}) %collective-permute-start.1) | collective-permute-done | bytes 135200 | tf_op jit(solution)/shard_map/ppermute | solution.py:748
  34.1 2.8 %collective-permute-done.2.refs_2_ = bf16[528,128]{1,0:T(8,128)(2,1)S(1)} collective-permute-done((bf16[528,128]{1,0:T(8,128)(2,1)S(1)}, bf16[528,128]{1,0:T(8,128)(2,1)S(1)}, u32[]{:S(2)}, u32[]{:S(2)}) %collective-permute-start.2) | collective-permute-done | bytes 135200 | tf_op jit(solution)/shard_map/ppermute | solution.py:748
  38.8 1.7 %collective-permute-done.3.refs_3_ = bf16[528,128]{1,0:T(8,128)(2,1)S(1)} collective-permute-done((bf16[528,128]{1,0:T(8,128)(2,1)S(1)}, bf16[528,128]{1,0:T(8,128)(2,1)S(1)}, u32[]{:S(2)}, u32[]{:S(2)}) %collective-permute-start.3) | collective-permute-done | bytes 135200 | tf_op jit(solution)/shard_map/ppermute | solution.py:748
  40.5 1.8 %gradient_pieces.4 = (bf16[4,512,128]{2,1,0:T(8,128)(2,1)}, f32[8,128]{1,0:T(8,128)S(1)}) custom-call(bf16[528,128]{1,0:T(8,128)(2,1)S(1)} %collective-permute-done.refs_0_, bf16[528,128]{1,0:T(8,128)(2,1)S(1)} %collective-permute-done.1.refs_1_, bf16[528,128]{1,0:T(8,128)(2,1)S(1)} %collective-permute-done.2.refs_2_, ...), custom_call_target="tpu_custom_call" | custom-call | flops 7864320 | bytes 2097152 | tf_op jit(solution)/shard_map/gradient_pieces/pallas_call | solution.py:596
  42.4 13.0 %collective-permute-done.4.refs_4_.refs_0_ = bf16[528,128]{1,0:T(8,128)(2,1)S(1)} collective-permute-done((bf16[528,128]{1,0:T(8,128)(2,1)}, bf16[528,128]{1,0:T(8,128)(2,1)S(1)}, u32[]{:S(2)}, u32[]{:S(2)}) %collective-permute-start.4) | collective-permute-done | bytes 135200 | tf_op jit(solution)/shard_map/ppermute | solution.py:748
  55.4 4.6 %collective-permute-done.5.refs_5_.refs_1_ = bf16[528,128]{1,0:T(8,128)(2,1)S(1)} collective-permute-done((bf16[528,128]{1,0:T(8,128)(2,1)}, bf16[528,128]{1,0:T(8,128)(2,1)S(1)}, u32[]{:S(2)}, u32[]{:S(2)}) %collective-permute-start.5) | collective-permute-done | bytes 135200 | tf_op jit(solution)/shard_map/ppermute | solution.py:748
  60.0 3.8 %collective-permute-done.6.refs_6_.refs_2_ = bf16[528,128]{1,0:T(8,128)(2,1)S(1)} collective-permute-done((bf16[528,128]{1,0:T(8,128)(2,1)}, bf16[528,128]{1,0:T(8,128)(2,1)S(1)}, u32[]{:S(2)}, u32[]{:S(2)}) %collective-permute-start.6) | collective-permute-done | bytes 135200 | tf_op jit(solution)/shard_map/ppermute | solution.py:748
  63.8 2.9 %collective-permute-done.7.refs_7_.refs_3_ = bf16[528,128]{1,0:T(8,128)(2,1)S(1)} collective-permute-done((bf16[528,128]{1,0:T(8,128)(2,1)}, bf16[528,128]{1,0:T(8,128)(2,1)S(1)}, u32[]{:S(2)}, u32[]{:S(2)}) %collective-permute-start.7) | collective-permute-done | bytes 135200 | tf_op jit(solution)/shard_map/ppermute | solution.py:748
  66.7 2.7 %gram_pieces.1 = f32[16,16,128]{2,1,0:T(8,128)S(1)} custom-call(bf16[8,672,128]{2,1,0:T(8,128)(2,1)S(1)} %all-to-all-done.near_ref.refs_0_, bf16[528,128]{1,0:T(8,128)(2,1)S(1)} %collective-permute-done.refs_0_, bf16[528,128]{1,0:T(8,128)(2,1)S(1)} %collective-permute-done.1.refs_1_, bf16[528,128]{1,0:T(8,128)(2,1)S(1)} %collective-permute-done.2.refs_2_, ...), custom_call_target="tpu_custom_call" | custom-call | flops 536870912 | bytes 2097152 | tf_op jit(solution)/shard_map/gram_pieces/pallas_call | solution.py:525
  69.5 0.6 copy-done.1
  70.1 4.5 %all-to-all-start.1 = ((f32[16,16,128]{2,1,0:T(8,128)}), f32[16,16,128]{2,1,0:T(8,128)S(1)}, u32[]{:S(2)}, u32[]{:S(2)}) async-start(f32[16,16,128]{2,1,0:T(8,128)} %copy-done.1), calls=%async_computation.1 | async-start | bytes 262144 | tf_op jit(solution)/shard_map/all_to_all | solution.py:365
  74.6 2.4 %gradient_pieces.5 = (bf16[4,512,128]{2,1,0:T(8,128)(2,1)}, f32[8,128]{1,0:T(8,128)}) custom-call(bf16[528,128]{1,0:T(8,128)(2,1)S(1)} %collective-permute-done.4.refs_4_.refs_0_, bf16[528,128]{1,0:T(8,128)(2,1)S(1)} %collective-permute-done.5.refs_5_.refs_1_, bf16[528,128]{1,0:T(8,128)(2,1)S(1)} %collective-permute-done.6.refs_6_.refs_2_, ...), custom_call_target="tpu_custom_call" | custom-call | flops 7864320 | bytes 2097152 | tf_op jit(solution)/shard_map/gradient_pieces/pallas_call | solution.py:596
  77.0 3.1 %gradient_pieces.6 = (bf16[8,512,128]{2,1,0:T(8,128)(2,1)}, f32[8,128]{1,0:T(8,128)}) custom-call(bf16[8,672,128]{2,1,0:T(8,128)(2,1)S(1)} %all-to-all-done.near_ref.refs_0_, bf16[512,128]{1,0:T(8,128)(2,1)S(1)} %get-tuple-element.43.refs_4_.refs_1_, bf16[512,128]{1,0:T(8,128)(2,1)S(1)} %get-tuple-element.44.refs_5_.refs_2_), custom_call_target="tpu_custom_call" | custom-call | flops 15728640 | bytes 4194304 | tf_op jit(solution)/shard_map/gradient_pieces/pallas_call | solution.py:596
  80.5 4.7 %update_pieces.1 = (bf16[8,512,128]{2,1,0:T(8,128)(2,1)S(1)}, bf16[384,128]{1,0:T(8,128)(2,1)S(1)}, bf16[384,128]{1,0:T(8,128)(2,1)S(1)}, bf16[384,128]{1,0:T(8,...) custom-call(bf16[8,672,128]{2,1,0:T(8,128)(2,1)S(1)} %all-to-all-don, ...), custom_call_target="tpu_custom_call" | custom-call | flops 1073741824 | bytes 6291456 | tf_op jit(solution)/shard_map/update_pieces/pallas_call | solution.py:696
  85.2 1.0 copy-done
  86.1 0.6 copy-done.2
  86.8 0.6 copy-done.4
  89.3 0.6 copy-done.12
  90.6 0.6 copy-done.16
  91.9 0.6 copy-done.18
  92.5 5.8 %all-to-all-start.2 = ((bf16[8,512,128]{2,1,0:T(8,128)(2,1)}), bf16[8,512,128]{2,1,0:T(8,128)(2,1)S(1)}, u32[]{:S(2)}, u32[]{:S(2)}) async-start(bf16[8,512,128]{2,1,0:T(8,128)(2,1)} %copy-done), calls=%async_computation.2 | async-start | bytes 2097152 | tf_op jit(solution)/shard_map/all_to_all | solution.py:753
  98.3 2.1 %gradient_pieces.7 = (bf16[16,128,128]{2,1,0:T(8,128)(2,1)}, f32[8,128]{1,0:T(8,128)}) custom-call(bf16[8,672,128]{2,1,0:T(8,128)(2,1)S(1)} %all-to-all-done.near_ref.refs_0_, bf16[8,144,128]{2,1,0:T(8,128)(2,1)S(1)} %collective-permute-done.8.refs_13_.refs_1_.across_ref, bf16[128,128]{1,0:T(8,128)(2,1)S(1)} %get-tuple-element.58.refs_2_, ...), custom_call_target="tpu_custom_call" | custom-call | flops 7864320 | bytes 2097152 | tf_op jit(solution)/shard_map/gradient_pieces/pallas_call | solution.py:596
  100.5 0.9 copy-done.3
  101.4 0.9 copy-done.5
  102.3 2.3 %update_raw.1 = bf16[8,128,128]{2,1,0:T(8,128)(2,1)} custom-call(bf16[8,672,128]{2,1,0:T(8,128)(2,1)S(1)} %all-to-all-done.near_ref.refs_0_, bf16[8,144,128]{2,1,0:T(8,128)(2,1)S(1)} %collective-permute-done.8.refs_13_.refs_1_.across_ref, bf16[256,256]{1,0:T(8,128)(2,1)S(1)} %copy-done.3, f32[256,128]{1,0:T(8,128)S(1)} %copy-done.5, ...), custom_call_target="tpu_custom_call" | custom-call | flops 134217728 | bytes 1572864 | tf_op jit(solution)/shard_map/update_raw/pallas_call | solution.py:735
  104.5 6.3 %all-to-all-done.2.refs_0_ = bf16[8,512,128]{2,1,0:T(8,128)(2,1)S(1)} async-done(((bf16[8,512,128]{2,1,0:T(8,128)(2,1)}), bf16[8,512,128]{2,1,0:T(8,128)(2,1)S(1)}, u32[]{:S(2)}, u32[]{:S(2)}) %all-to-all-start.2) | async-done | bytes 1048608 | tf_op jit(solution)/shard_map/all_to_all | solution.py:753
  110.9 5.2 %all-to-all-start.3 = ((bf16[8,128,128]{2,1,0:T(8,128)(2,1)}), bf16[8,128,128]{2,1,0:T(8,128)(2,1)S(1)}, u32[]{:S(2)}, u32[]{:S(2)}) async-start(bf16[8,128,128]{2,1,0:T(8,128)(2,1)} %update_raw.1), calls=%async_computation.3 | async-start | bytes 524288 | tf_op jit(solution)/shard_map/all_to_all | solution.py:753
  116.4 2.6 %collective-permute-start.10 = (bf16[384,128]{1,0:T(8,128)(2,1)}, bf16[384,128]{1,0:T(8,128)(2,1)S(1)}, u32[]{:S(2)}, u32[]{:S(2)}) collective-permute-start(bf16[384,128]{1,0:T(8,128)(2,1)} %copy-done.17), channel_id=1, source_target_pairs={{0,9},{1,8},{2,11},{3,10},{4,13},{5,12},{6,15},{7,14},{8,1},{9,0},... | collective-permute-start | bytes 294920 | tf_op jit(solution)/shard_map/ppermute | solution.py:748
  119.0 1.2 collective-permute-start.11
  120.2 2.1 %collective-permute-start.12 = (bf16[384,128]{1,0:T(8,128)(2,1)S(1)}, bf16[384,128]{1,0:T(8,128)(2,1)S(1)}, u32[]{:S(2)}, u32[]{:S(2)}) collective-permute-start(bf16[384,128]{1,0:T(8,128)(2,1)S(1)} %copy-done.15), channel_id=1, source_target_pairs={{0,11},{1,10},{2,9},{3,8},{4,15},{5,14},{6,13},{7,12},{8,3},{9,2},... | collective-permute-start | bytes 294920 | tf_op jit(solution)/shard_map/ppermute | solution.py:748
  122.4 10.3 %collective-permute-start.14 = (bf16[384,128]{1,0:T(8,128)(2,1)S(1)}, bf16[384,128]{1,0:T(8,128)(2,1)S(1)}, u32[]{:S(2)}, u32[]{:S(2)}) collective-permute-start(bf16[384,128]{1,0:T(8,128)(2,1)S(1)} %copy-done.11), channel_id=1, source_target_pairs={{0,13},{1,12},{2,15},{3,14},{4,9},{5,8},{6,11},{7,10},{8,5},{9,4},... | collective-permute-start | bytes 294920 | tf_op jit(solution)/shard_map/ppermute | solution.py:748
  133.3 1.1 collective-permute-start.15
  134.3 1.1 collective-permute-done.11.refs_3_
  135.4 2.9 %collective-permute-start.16 = (bf16[384,128]{1,0:T(8,128)(2,1)S(1)}, bf16[384,128]{1,0:T(8,128)(2,1)S(1)}, u32[]{:S(2)}, u32[]{:S(2)}) collective-permute-start(bf16[384,128]{1,0:T(8,128)(2,1)S(1)} %copy-done.7), channel_id=1, source_target_pairs={{0,15},{1,14},{2,13},{3,12},{4,11},{5,10},{6,9},{7,8},{8,7},{9,6},... | collective-permute-start | bytes 294920 | tf_op jit(solution)/shard_map/ppermute | solution.py:748
  138.3 2.5 %join_pieces.5.refs_0_ = bf16[1,1048576]{1,0:T(2,128)(2,1)} custom-call(bf16[8,512,128]{2,1,0:T(8,128)(2,1)S(1)} %all-to-all-done.2.refs_0_), custom_call_target="tpu_custom_call" | custom-call | bytes 3145728 | tf_op jit(solution)/shard_map/join_pieces/pallas_call | solution.py:476
  140.8 0.9 join_pieces.6.refs_0_
  141.7 3.9 %collective-permute-done.13.refs_1_ = bf16[384,128]{1,0:T(8,128)(2,1)S(1)} collective-permute-done((bf16[384,128]{1,0:T(8,128)(2,1)S(1)}, bf16[384,128]{1,0:T(8,128)(2,1)S(1)}, u32[]{:S(2)}, u32[]{:S(2)}) %collective-permute-start.13) | collective-permute-done | bytes 98336 | tf_op jit(solution)/shard_map/ppermute | solution.py:748
  145.7 3.0 %collective-permute-done.14.refs_2_ = bf16[384,128]{1,0:T(8,128)(2,1)S(1)} collective-permute-done((bf16[384,128]{1,0:T(8,128)(2,1)S(1)}, bf16[384,128]{1,0:T(8,128)(2,1)S(1)}, u32[]{:S(2)}, u32[]{:S(2)}) %collective-permute-start.14) | collective-permute-done | bytes 98336 | tf_op jit(solution)/shard_map/ppermute | solution.py:748
  148.6 0.8 join_pieces.7.refs_0_
  149.4 1.1 join_pieces.8.refs_0_
  150.8 2.6 %collective-permute-done.16.refs_2_ = bf16[384,128]{1,0:T(8,128)(2,1)S(1)} collective-permute-done((bf16[384,128]{1,0:T(8,128)(2,1)S(1)}, bf16[384,128]{1,0:T(8,128)(2,1)S(1)}, u32[]{:S(2)}, u32[]{:S(2)}) %collective-permute-start.16) | collective-permute-done | bytes 98336 | tf_op jit(solution)/shard_map/ppermute | solution.py:748
  153.4 0.8 join_pieces.9
  (46 shorter events, 6.1 us)
Async XLA Ops:
  4.6 37.7 %all-to-all-start = ((bf16[8,672,128]{2,1,0:T(8,128)(2,1)}), bf16[8,672,128]{2,1,0:T(8,128)(2,1)S(1)}, u32[]{:S(2)}, u32[]{:S(2)}) async-start(bf16[8,672,128]{2,1,0:T(8,128)(2,1)} %get-tuple-element.34), calls=%async_computation | async-start | bytes 2752512 | tf_op jit(solution)/shard_map/all_to_all | solution.py:753
  9.2 20.9 %collective-permute-start = (bf16[528,128]{1,0:T(8,128)(2,1)S(1)}, bf16[528,128]{1,0:T(8,128)(2,1)S(1)}, u32[]{:S(2)}, u32[]{:S(2)}) collective-permute-start(bf16[528,128]{1,0:T(8,128)(2,1)S(1)} %get-tuple-element.35), channel_id=1, source_target_pairs={{0,8},{1,9},{2,10},{3,11},{4,12},{5,13},{6,14},{7,15},{8,0},{9,1},... | collective-permute-start | bytes 405512 | tf_op jit(solution)/shard_map/ppermute | solution.py:748
  11.5 22.2 %collective-permute-start.1 = (bf16[528,128]{1,0:T(8,128)(2,1)S(1)}, bf16[528,128]{1,0:T(8,128)(2,1)S(1)}, u32[]{:S(2)}, u32[]{:S(2)}) collective-permute-start(bf16[528,128]{1,0:T(8,128)(2,1)S(1)} %get-tuple-element.36), channel_id=1, source_target_pairs={{0,9},{1,8},{2,11},{3,10},{4,13},{5,12},{6,15},{7,14},{8,1},{9,0},... | collective-permute-start | bytes 405512 | tf_op jit(solution)/shard_map/ppermute | solution.py:748
  12.1 24.8 %collective-permute-start.2 = (bf16[528,128]{1,0:T(8,128)(2,1)S(1)}, bf16[528,128]{1,0:T(8,128)(2,1)S(1)}, u32[]{:S(2)}, u32[]{:S(2)}) collective-permute-start(bf16[528,128]{1,0:T(8,128)(2,1)S(1)} %get-tuple-element.37), channel_id=1, source_target_pairs={{0,10},{1,11},{2,8},{3,9},{4,14},{5,15},{6,12},{7,13},{8,2},{9,3},... | collective-permute-start | bytes 405512 | tf_op jit(solution)/shard_map/ppermute | solution.py:748
  15.3 25.2 %collective-permute-start.3 = (bf16[528,128]{1,0:T(8,128)(2,1)S(1)}, bf16[528,128]{1,0:T(8,128)(2,1)S(1)}, u32[]{:S(2)}, u32[]{:S(2)}) collective-permute-start(bf16[528,128]{1,0:T(8,128)(2,1)S(1)} %get-tuple-element.38), channel_id=1, source_target_pairs={{0,11},{1,10},{2,9},{3,8},{4,15},{5,14},{6,13},{7,12},{8,3},{9,2},... | collective-permute-start | bytes 405512 | tf_op jit(solution)/shard_map/ppermute | solution.py:748
  15.6 39.8 %collective-permute-start.4 = (bf16[528,128]{1,0:T(8,128)(2,1)}, bf16[528,128]{1,0:T(8,128)(2,1)S(1)}, u32[]{:S(2)}, u32[]{:S(2)}) collective-permute-start(bf16[528,128]{1,0:T(8,128)(2,1)} %get-tuple-element.39), channel_id=1, source_target_pairs={{0,12},{1,13},{2,14},{3,15},{4,8},{5,9},{6,10},{7,11},{8,4},{9,5},... | collective-permute-start | bytes 405512 | tf_op jit(solution)/shard_map/ppermute | solution.py:748
  30.1 29.9 %collective-permute-start.5 = (bf16[528,128]{1,0:T(8,128)(2,1)}, bf16[528,128]{1,0:T(8,128)(2,1)S(1)}, u32[]{:S(2)}, u32[]{:S(2)}) collective-permute-start(bf16[528,128]{1,0:T(8,128)(2,1)} %get-tuple-element.40), channel_id=1, source_target_pairs={{0,13},{1,12},{2,15},{3,14},{4,9},{5,8},{6,11},{7,10},{8,5},{9,4},... | collective-permute-start | bytes 405512 | tf_op jit(solution)/shard_map/ppermute | solution.py:748
  33.7 30.1 %collective-permute-start.6 = (bf16[528,128]{1,0:T(8,128)(2,1)}, bf16[528,128]{1,0:T(8,128)(2,1)S(1)}, u32[]{:S(2)}, u32[]{:S(2)}) collective-permute-start(bf16[528,128]{1,0:T(8,128)(2,1)} %get-tuple-element.41), channel_id=1, source_target_pairs={{0,14},{1,15},{2,12},{3,13},{4,10},{5,11},{6,8},{7,9},{8,6},{9,7},... | collective-permute-start | bytes 405512 | tf_op jit(solution)/shard_map/ppermute | solution.py:748
  36.9 29.9 %collective-permute-start.7 = (bf16[528,128]{1,0:T(8,128)(2,1)}, bf16[528,128]{1,0:T(8,128)(2,1)S(1)}, u32[]{:S(2)}, u32[]{:S(2)}) collective-permute-start(bf16[528,128]{1,0:T(8,128)(2,1)} %get-tuple-element.42), channel_id=1, source_target_pairs={{0,15},{1,14},{2,13},{3,12},{4,11},{5,10},{6,9},{7,8},{8,7},{9,6},... | collective-permute-start | bytes 405512 | tf_op jit(solution)/shard_map/ppermute | solution.py:748
  42.3 38.2 %collective-permute-start.8 = (bf16[8,144,128]{2,1,0:T(8,128)(2,1)S(1)}, bf16[8,144,128]{2,1,0:T(8,128)(2,1)S(1)}, u32[]{:S(2)}, u32[]{:S(2)}) collective-permute-start(bf16[8,144,128]{2,1,0:T(8,128)(2,1)S(1)} %raw_states.1.refs_9_), channel_id=1, source_target_pairs={{0,8},{1,9},{2,10},{3,11},{4,12},{5,13},{6,14},{7,15},{8,0},{9,1},... | collective-permute-start | bytes 884744 | tf_op jit(solution)/shard_map/ppermute | solution.py:748
  69.5 0.6 copy-start.1
  70.1 10.4 %all-to-all-start.1 = ((f32[16,16,128]{2,1,0:T(8,128)}), f32[16,16,128]{2,1,0:T(8,128)S(1)}, u32[]{:S(2)}, u32[]{:S(2)}) async-start(f32[16,16,128]{2,1,0:T(8,128)} %copy-done.1), calls=%async_computation.1 | async-start | bytes 262144 | tf_op jit(solution)/shard_map/all_to_all | solution.py:365
  85.1 1.0 copy-start
  86.1 0.7 copy-start.2
  86.8 0.6 copy-start.4
  87.4 0.6 copy-start.6
  88.1 0.6 copy-start.8
  88.7 0.6 copy-start.10
  89.3 0.6 copy-start.12
  90.0 0.6 copy-start.14
  90.6 0.6 copy-start.16
  91.2 0.6 copy-start.17
  91.9 0.6 copy-start.18
  92.5 27.7 %copy-start.15 = (bf16[384,128]{1,0:T(8,128)(2,1)S(1)}, bf16[384,128]{1,0:T(8,128)(2,1)}, u32[]{:S(2)}) copy-start(bf16[384,128]{1,0:T(8,128)(2,1)} %copy-done.14) | copy-start | bytes 294916
  92.5 29.8 %copy-start.13 = (bf16[384,128]{1,0:T(8,128)(2,1)S(1)}, bf16[384,128]{1,0:T(8,128)(2,1)}, u32[]{:S(2)}) copy-start(bf16[384,128]{1,0:T(8,128)(2,1)} %copy-done.12) | copy-start | bytes 294916
  92.5 29.8 %copy-start.11 = (bf16[384,128]{1,0:T(8,128)(2,1)S(1)}, bf16[384,128]{1,0:T(8,128)(2,1)}, u32[]{:S(2)}) copy-start(bf16[384,128]{1,0:T(8,128)(2,1)} %copy-done.10) | copy-start | bytes 294916
  92.5 40.7 %copy-start.9 = (bf16[384,128]{1,0:T(8,128)(2,1)S(1)}, bf16[384,128]{1,0:T(8,128)(2,1)}, u32[]{:S(2)}) copy-start(bf16[384,128]{1,0:T(8,128)(2,1)} %copy-done.8) | copy-start | bytes 294916
  92.5 42.9 %copy-start.7 = (bf16[384,128]{1,0:T(8,128)(2,1)S(1)}, bf16[384,128]{1,0:T(8,128)(2,1)}, u32[]{:S(2)}) copy-start(bf16[384,128]{1,0:T(8,128)(2,1)} %copy-done.6) | copy-start | bytes 294916
  92.5 18.3 %all-to-all-start.2 = ((bf16[8,512,128]{2,1,0:T(8,128)(2,1)}), bf16[8,512,128]{2,1,0:T(8,128)(2,1)S(1)}, u32[]{:S(2)}, u32[]{:S(2)}) async-start(bf16[8,512,128]{2,1,0:T(8,128)(2,1)} %copy-done), calls=%async_computation.2 | async-start | bytes 2097152 | tf_op jit(solution)/shard_map/all_to_all | solution.py:753
  100.5 0.9 copy-start.3
  101.4 0.9 copy-start.5
  110.9 38.5 %all-to-all-start.3 = ((bf16[8,128,128]{2,1,0:T(8,128)(2,1)}), bf16[8,128,128]{2,1,0:T(8,128)(2,1)S(1)}, u32[]{:S(2)}, u32[]{:S(2)}) async-start(bf16[8,128,128]{2,1,0:T(8,128)(2,1)} %update_raw.1), calls=%async_computation.3 | async-start | bytes 524288 | tf_op jit(solution)/shard_map/all_to_all | solution.py:753
  116.1 6.2 %collective-permute-start.9 = (bf16[384,128]{1,0:T(8,128)(2,1)}, bf16[384,128]{1,0:T(8,128)(2,1)S(1)}, u32[]{:S(2)}, u32[]{:S(2)}) collective-permute-start(bf16[384,128]{1,0:T(8,128)(2,1)} %copy-done.18), channel_id=1, source_target_pairs={{0,8},{1,9},{2,10},{3,11},{4,12},{5,13},{6,14},{7,15},{8,0},{9,1},... | collective-permute-start | bytes 294920 | tf_op jit(solution)/shard_map/ppermute | solution.py:748
  116.4 16.8 %collective-permute-start.10 = (bf16[384,128]{1,0:T(8,128)(2,1)}, bf16[384,128]{1,0:T(8,128)(2,1)S(1)}, u32[]{:S(2)}, u32[]{:S(2)}) collective-permute-start(bf16[384,128]{1,0:T(8,128)(2,1)} %copy-done.17), channel_id=1, source_target_pairs={{0,9},{1,8},{2,11},{3,10},{4,13},{5,12},{6,15},{7,14},{8,1},{9,0},... | collective-permute-start | bytes 294920 | tf_op jit(solution)/shard_map/ppermute | solution.py:748
  119.0 16.4 %collective-permute-start.11 = (bf16[384,128]{1,0:T(8,128)(2,1)}, bf16[384,128]{1,0:T(8,128)(2,1)S(1)}, u32[]{:S(2)}, u32[]{:S(2)}) collective-permute-start(bf16[384,128]{1,0:T(8,128)(2,1)} %copy-done.16), channel_id=1, source_target_pairs={{0,10},{1,11},{2,8},{3,9},{4,14},{5,15},{6,12},{7,13},{8,2},{9,3},... | collective-permute-start | bytes 294920 | tf_op jit(solution)/shard_map/ppermute | solution.py:748
  120.2 20.6 %collective-permute-start.12 = (bf16[384,128]{1,0:T(8,128)(2,1)S(1)}, bf16[384,128]{1,0:T(8,128)(2,1)S(1)}, u32[]{:S(2)}, u32[]{:S(2)}) collective-permute-start(bf16[384,128]{1,0:T(8,128)(2,1)S(1)} %copy-done.15), channel_id=1, source_target_pairs={{0,11},{1,10},{2,9},{3,8},{4,15},{5,14},{6,13},{7,12},{8,3},{9,2},... | collective-permute-start | bytes 294920 | tf_op jit(solution)/shard_map/ppermute | solution.py:748
  122.3 23.3 %collective-permute-start.13 = (bf16[384,128]{1,0:T(8,128)(2,1)S(1)}, bf16[384,128]{1,0:T(8,128)(2,1)S(1)}, u32[]{:S(2)}, u32[]{:S(2)}) collective-permute-start(bf16[384,128]{1,0:T(8,128)(2,1)S(1)} %copy-done.13), channel_id=1, source_target_pairs={{0,12},{1,13},{2,14},{3,15},{4,8},{5,9},{6,10},{7,11},{8,4},{9,5},... | collective-permute-start | bytes 294920 | tf_op jit(solution)/shard_map/ppermute | solution.py:748
  122.4 26.3 %collective-permute-start.14 = (bf16[384,128]{1,0:T(8,128)(2,1)S(1)}, bf16[384,128]{1,0:T(8,128)(2,1)S(1)}, u32[]{:S(2)}, u32[]{:S(2)}) collective-permute-start(bf16[384,128]{1,0:T(8,128)(2,1)S(1)} %copy-done.11), channel_id=1, source_target_pairs={{0,13},{1,12},{2,15},{3,14},{4,9},{5,8},{6,11},{7,10},{8,5},{9,4},... | collective-permute-start | bytes 294920 | tf_op jit(solution)/shard_map/ppermute | solution.py:748
  133.3 17.5 %collective-permute-start.15 = (bf16[384,128]{1,0:T(8,128)(2,1)S(1)}, bf16[384,128]{1,0:T(8,128)(2,1)S(1)}, u32[]{:S(2)}, u32[]{:S(2)}) collective-permute-start(bf16[384,128]{1,0:T(8,128)(2,1)S(1)} %copy-done.9), channel_id=1, source_target_pairs={{0,14},{1,15},{2,12},{3,13},{4,10},{5,11},{6,8},{7,9},{8,6},{9,7},... | collective-permute-start | bytes 294920 | tf_op jit(solution)/shard_map/ppermute | solution.py:748
  135.4 17.9 %collective-permute-start.16 = (bf16[384,128]{1,0:T(8,128)(2,1)S(1)}, bf16[384,128]{1,0:T(8,128)(2,1)S(1)}, u32[]{:S(2)}, u32[]{:S(2)}) collective-permute-start(bf16[384,128]{1,0:T(8,128)(2,1)S(1)} %copy-done.7), channel_id=1, source_target_pairs={{0,15},{1,14},{2,13},{3,12},{4,11},{5,10},{6,9},{7,8},{8,7},{9,6},... | collective-permute-start | bytes 294920 | tf_op jit(solution)/shard_map/ppermute | solution.py:748

commit v9 on v8

--- a/solution.py
+++ b/solution.py
@@ -374,95 +374,71 @@
     return pl.ds(pl.multiple_of(start, TILE), count)
 
 
-def split_pieces_body(positions, half, raw, lines, gates, fields, row_ref, *refs):
-    field_refs, refs = refs[:fields], refs[fields + gates :]
-    count = len(positions)
-    out_refs, helds, sems = refs[: -count - 1], refs[-count - 1 : -1], refs[-1]
-    me = lax.axis_index("slab").astype(jnp.int32)
-    slab_refs = out_refs[len(out_refs) - 2 * fields :]
-    fetches = []
-    for n, target in enumerate(slab_refs):
-        start = (me if n < fields else me ^ half) * lines
-        source = field_refs[n % fields].at[lines_of(start, target.shape[0]), :]
-        fetches.append(pltpu.make_async_copy(source, target, sems.at[5 * count + n]))
+def split_pieces_body(slabs, lines, fields, row_ref, *refs):
+    half = slabs // 2
+    field_refs, near_out, far_outs = refs[:fields], refs[fields], refs[fields + 1 : fields + 1 + half]
+    slab_refs, helds, sems = refs[fields + 1 + half : -slabs - 1], refs[-slabs - 1 : -1], refs[-1]
     cells = lines * LANES
     end = row_ref.shape[1]
     copies = []
-    for at, held in zip(positions, helds):
-        mine = []
-
-        def fetch(start, size, to):
+    for at, held in enumerate(helds):
+        slab = device_at(at, half)
+        parts = (
+            (slab * cells, cells, 0),
+            (jnp.minimum((slab + 1) * cells, end - GRID_Y), GRID_Y, cells),
+            (jnp.maximum(slab * cells - GRID_Y, 0), GRID_Y, cells + GRID_Y),
+        )
+        for n, (start, size, to) in enumerate(parts):
             source = row_ref.at[:, pl.ds(pl.multiple_of(start, GRID_Y), size)]
-            sem = sems.at[len(copies) * 5 + len(mine)]
-            mine.append(pltpu.make_async_copy(source, held.at[:, pl.ds(to, size)], sem))
-            mine[-1].start()
-
-        slab = device_at(at, half)
-        fetch(slab * cells, cells, 0)
-        fetch(jnp.minimum((slab + 1) * cells, end - GRID_Y), GRID_Y, cells)
-        fetch(jnp.maximum(slab * cells - GRID_Y, 0), GRID_Y, cells + GRID_Y)
-        if raw and at < half:
-            other = slab ^ half
-            fetch(other * cells, raw * LANES + GRID_Y, cells + 2 * GRID_Y)
-            fetch(jnp.maximum(other * cells - GRID_Y, 0), GRID_Y, cells + 3 * GRID_Y + raw * LANES)
-        copies.append(mine)
-
-    def grid_row(held, at):
-        return held[:, pl.ds(at, GRID_Y)].astype(F32).reshape(LINE, LANES)
-
-    for fetch in fetches:
-        fetch.start()
-    for n, (at, held, mine) in enumerate(zip(positions, helds, copies)):
-        out_ref = out_refs[1 + at - half] if at >= half else out_refs[0].at[at]
-        for copy in mine:
+            copies.append(pltpu.make_async_copy(source, held.at[:, pl.ds(to, size)], sems.at[3 * at + n]))
+            copies[-1].start()
+    start = lax.axis_index("slab").astype(jnp.int32) * lines
+    for n, (field_ref, slab_ref) in enumerate(zip(field_refs, slab_refs)):
+        copies.append(pltpu.make_async_copy(field_ref.at[lines_of(start, lines), :], slab_ref, sems.at[3 * slabs + n]))
+        copies[-1].start()
+
+    for at, held in enumerate(helds):
+        out_ref = near_out.at[at] if at < half else far_outs[at - half]
+        for copy in copies[3 * at : 3 * at + 3]:
             copy.wait()
         slab = device_at(at, half)
         out_ref[:lines, :] = held[:, :cells].reshape(lines, LANES)
-        below = jnp.where(slab == end // cells - 1, 0.0, grid_row(held, cells))
-        above = jnp.where(slab == 0, 0.0, grid_row(held, cells + GRID_Y))
-        out_ref[lines : lines + TILE, :] = jnp.concatenate([below, above], axis=0).astype(BF16)
-        if raw and at < half:
-            start = cells + 2 * GRID_Y
-            to = lines + TILE
-            out_ref[to : to + raw, :] = held[:, start : start + raw * LANES].reshape(raw, LANES)
-            below = grid_row(held, start + raw * LANES)
-            above = jnp.where(slab ^ half == 0, 0.0, grid_row(held, start + raw * LANES + GRID_Y))
-            out_ref[to + raw :, :] = jnp.concatenate([below, above], axis=0).astype(BF16)
-    for fetch in fetches:
-        fetch.wait()
-
-
-def split_pieces(row, slabs, raw, fields):
+        below = held[:, cells : cells + GRID_Y].astype(F32).reshape(LINE, LANES)
+        above = held[:, cells + GRID_Y :].astype(F32).reshape(LINE, LANES)
+        below = jnp.where(slab == slabs - 1, 0.0, below)
+        above = jnp.where(slab == 0, 0.0, above)
+        out_ref[lines:, :] = jnp.concatenate([below, above], axis=0).astype(BF16)
+    for copy in copies[3 * slabs :]:
+        copy.wait()
+
+
+def split_pieces(row, slabs, fields):
     lines = row.shape[1] // slabs // LANES
     half = slabs // 2
     rim = lines + TILE
-    size = rim + (raw + TILE if raw else 0)
-    out_shape = [jax.ShapeDtypeStruct((half, size, LANES), BF16)]
+    out_shape = [jax.ShapeDtypeStruct((half, rim, LANES), BF16)]
     out_shape += [jax.ShapeDtypeStruct((rim, LANES), BF16)] * half
     out_shape += [jax.ShapeDtypeStruct((lines, LANES), BF16)] * len(fields)
-    out_shape += [jax.ShapeDtypeStruct((max(raw, TILE), LANES), BF16)] * len(fields)
-    return call(
-        functools.partial(split_pieces_body, range(slabs), half, raw, lines, 0, len(fields)),
+    return call(
+        functools.partial(split_pieces_body, slabs, lines, len(fields)),
         "split_pieces",
-        moved=6 * half * (size + rim) * LANES,
+        moved=6 * slabs * rim * LANES,
         in_specs=[IN_HBM] * (1 + len(fields)),
         out_specs=[IN_VMEM] * len(out_shape),
         out_shape=out_shape,
-        scratch_shapes=[pltpu.VMEM((1, (size + TILE) * LANES), BF16)] * half
-        + [pltpu.VMEM((1, (rim + TILE) * LANES), BF16)] * half
-        + [pltpu.SemaphoreType.DMA((5 * slabs + 2 * len(fields),))],
+        scratch_shapes=[pltpu.VMEM((1, rim * LANES), BF16)] * slabs
+        + [pltpu.SemaphoreType.DMA((3 * slabs + len(fields),))],
     )(row, *fields)
 
 
 def join_pieces_body(pieces, half, lines, begun, arrays, *refs):
     row_ref, helds, sems = refs[begun + arrays], refs[begun + arrays + 1 : -1], refs[-1]
     copies = []
-    for (array, lead, at, across, begin), held in zip(pieces, helds):
+    for (array, lead, at), held in zip(pieces, helds):
         ref = refs[begun + array]
         piece = ref[...] if lead is None else ref[lead]
         held[...] = piece.reshape(held.shape)
-        slab = device_at(at, half)
-        start = ((slab ^ half if across else slab) * lines + begin) * LANES
+        start = device_at(at, half) * lines * LANES
         target = row_ref.at[:, pl.ds(pl.multiple_of(start, GRID_Y), held.shape[1])]
         copies.append(pltpu.make_async_copy(held, target, sems.at[len(copies)]))
         copies[-1].start()
@@ -519,7 +495,7 @@
     out_ref[...] = jnp.broadcast_to(gram[None], out_ref.shape)
 
 
-def gram_pieces(near, far, lines, gates, early):
+def gram_pieces(near, far, lines, gates):
     total = 2 * len(far)
     wide = total * TILE
     return call(
@@ -527,11 +503,11 @@
         "gram_pieces",
         flops=2 * wide * wide * LANES * (lines // TILE),
         moved=2 * total * lines * LANES,
-        in_specs=[IN_VMEM] * (1 + len(far)) + [IN_HBM] * len(gates) + [IN_VMEM] * len(early),
+        in_specs=[IN_VMEM] * (1 + len(far)) + [IN_HBM] * len(gates),
         out_specs=IN_VMEM,
         out_shape=jax.ShapeDtypeStruct((total, total, LANES), F32),
         scratch_shapes=[pltpu.VMEM((wide, wide), F32)],
-    )(near, *far, *gates, *early)
+    )(near, *far, *gates)
 
 
 def gradient_pieces_body(views, arrays, numbers, *refs):
@@ -606,26 +582,6 @@
     )(*arrays, observed, precision, *numbers)
 
 
-def raw_body(raw, lines, near_ref, out_ref):
-    for k in range(near_ref.shape[0]):
-        out_ref[k, :raw, :] = near_ref[k, :raw, :]
-        below = near_ref[k, raw : raw + TILE, :].astype(F32)[:LINE]
-        above = near_ref[k, lines : lines + TILE, :].astype(F32)[LINE:]
-        out_ref[k, raw:, :] = jnp.concatenate([below, above], axis=0).astype(BF16)
-
-
-def raw_states(near, raw, lines):
-    out = jax.ShapeDtypeStruct((near.shape[0], raw + TILE, LANES), BF16)
-    return call(
-        functools.partial(raw_body, raw, lines),
-        "raw_states",
-        moved=4 * out.size,
-        in_specs=[IN_VMEM],
-        out_specs=IN_VMEM,
-        out_shape=out,
-    )(near)
-
-
 def mix(mixer, own, numbers_ref, total, states, slopes):
     high = mixer.shape[0]
     rate = numbers_ref[2:3, :1] / total
@@ -636,7 +592,7 @@
     return (states[:high].astype(F32) * own[...] + rate * (drive - coeff * pulled)).astype(BF16)
 
 
-def update_pieces_body(half, raw, lines, groups, near_ref, *refs):
+def update_pieces_body(half, lines, groups, near_ref, *refs):
     total = 2 * half
     far_refs, numbers_ref, grams_ref, refs = refs[:half], refs[half], refs[half + 1], refs[half + 2 :]
     group_refs, near_out, far_outs = refs[: len(groups)], refs[-5 - half], refs[-4 - half : -4]
@@ -669,7 +625,7 @@
     for fetch in fetches:
         fetch.wait()
 
-    def step(with_far, i, carry):
+    def step(i, carry):
         for t in range(BLOCK // TILE):
             at = i * BLOCK + t * TILE
             part = lines_of(at, TILE)
@@ -677,71 +633,34 @@
             slopes = grads[:, part, :].reshape(wide, LANES)
             new = mix(mixer, own, numbers_ref, total, jnp.concatenate(states, axis=0), slopes)
             near_out[:, part, :] = new[:high].reshape(half, TILE, LANES)
-            if with_far:
-                for x, far_out in enumerate(far_outs):
-                    far_out[lines_of(at - raw, TILE), :] = new[high + x * TILE : high + (x + 1) * TILE]
+            for x, far_out in enumerate(far_outs):
+                far_out[part, :] = new[high + x * TILE : high + (x + 1) * TILE]
         return carry
 
-    lax.fori_loop(0, raw // BLOCK, functools.partial(step, False), 0)
-    lax.fori_loop(raw // BLOCK, lines // BLOCK, functools.partial(step, True), 0)
-
-
-def update_pieces(numbers, grams, near, far, grads, groups, gates, raw, lines):
+    lax.fori_loop(0, lines // BLOCK, step, 0)
+
+
+def update_pieces(numbers, grams, near, far, grads, groups, lines):
     half = len(far)
     total = 2 * half
     wide = total * TILE
     out_shape = [jax.ShapeDtypeStruct((half, lines, LANES), BF16)]
-    out_shape += [jax.ShapeDtypeStruct((lines - raw, LANES), BF16)] * half
-    out_shape += [jax.ShapeDtypeStruct((wide, wide), BF16), jax.ShapeDtypeStruct((wide, LANES), F32)]
-    return call(
-        functools.partial(update_pieces_body, half, raw, lines, groups),
+    out_shape += [jax.ShapeDtypeStruct((lines, LANES), BF16)] * half
+    return call(
+        functools.partial(update_pieces_body, half, lines, groups),
         "update_pieces",
         flops=4 * wide * wide * LANES * (lines // TILE),
         moved=6 * total * lines * LANES,
-        in_specs=[IN_VMEM] * (half + 3) + [IN_HBM] * len(groups) + [IN_VMEM] * len(gates),
+        in_specs=[IN_VMEM] * (half + 3) + [IN_HBM] * len(groups),
         out_specs=[IN_VMEM] * len(out_shape),
         out_shape=out_shape,
-        scratch_shapes=[pltpu.VMEM((total, lines, LANES), BF16), pltpu.SemaphoreType.DMA((total,))],
-    )(near, *far, numbers, grams, *grads, *gates)
-
-
-def update_raw_body(lines, near_ref, across_ref, mixer, own, numbers_ref, grads_ref, out_ref, grads, sem):
-    half, raw, _ = out_ref.shape
-    high = half * TILE
-    fetch = pltpu.make_async_copy(grads_ref, grads, sem)
-    fetch.start()
-    fetch.wait()
-    here = lax.axis_index("slab").astype(jnp.int32) % half
-
-    def step(i, carry):
-        for t in range(BLOCK // TILE):
-            at = i * BLOCK + t * TILE
-            part = lines_of(at, TILE)
-            states = [near_ref[:, lines_of(lines + TILE + at, TILE), :].reshape(high, LANES)]
-            slopes = [grads[:half, part, :].reshape(high, LANES)]
-            for x in range(half):
-                states += [across_ref[here ^ x, part, :]]
-                slopes += [grads[half + (here ^ x), part, :]]
-            states, slopes = jnp.concatenate(states, axis=0), jnp.concatenate(slopes, axis=0)
-            new = mix(mixer.at[:high, :], own.at[:high, :], numbers_ref, 2 * half, states, slopes)
-            out_ref[:, part, :] = new.reshape(half, TILE, LANES)
-        return carry
-
-    lax.fori_loop(0, raw // BLOCK, step, 0)
-
-
-def update_raw(near, across, mixer, own, numbers, grads, raw, lines):
-    half = near.shape[0]
-    return call(
-        functools.partial(update_raw_body, lines),
-        "update_raw",
-        flops=2 * mixer.size * LANES * (raw // TILE),
-        moved=12 * half * raw * LANES,
-        in_specs=[IN_VMEM] * 5 + [IN_HBM],
-        out_specs=IN_VMEM,
-        out_shape=jax.ShapeDtypeStruct((half, raw, LANES), BF16),
-        scratch_shapes=[pltpu.VMEM((2 * half, raw, LANES), BF16), pltpu.SemaphoreType.DMA],
-    )(near, across, mixer, own, numbers, grads)
+        scratch_shapes=[
+            pltpu.VMEM((wide, wide), BF16),
+            pltpu.VMEM((wide, LANES), F32),
+            pltpu.VMEM((total, lines, LANES), BF16),
+            pltpu.SemaphoreType.DMA((total,)),
+        ],
+    )(near, *far, numbers, grams, *grads)
 
 
 def exchange(piece, k, slabs):
@@ -753,7 +672,6 @@
     return lax.all_to_all(pieces, "slab", 0, 0, axis_index_groups=groups, tiled=True)
 
 
-RAW = 128
 GRADIENTS = ((8, 9, 10, 11), (12, 13, 14, 15), (0, 1, 2, 3, 4, 5, 6, 7))
 
 
@@ -763,14 +681,10 @@
     lines = NCELL // slabs // LANES
     row = in_hbm(particles)
     fields = [in_hbm(field.reshape(-1, LANES)) for field in (observed, precision)]
-    near, *far = split_pieces(row, slabs, RAW, fields)
-    far, (obs, prec, raw_obs, raw_prec) = far[:half], far[half:]
+    near, *far = split_pieces(row, slabs, fields)
+    far, (obs, prec) = far[:half], far[half:]
     near = swap_near(near, slabs)
     far = [exchange(piece, half + x, slabs) for x, piece in enumerate(far)]
-    early, gates = [], []
-    if RAW:
-        early = [raw_states(near, RAW, lines)]
-        gates = [exchange(early[0], half, slabs)]
     grads = []
     numbers = [spread, anneal, step_size]
     for group in GRADIENTS:
@@ -781,22 +695,15 @@
         slopes, rows = gradient_pieces(arrays, tuple(views), obs, prec, [] if grads else numbers)
         grads.append(in_hbm(slopes))
         numbers = numbers if len(grads) > 1 else rows
-    grams = swap(gram_pieces(near, far, lines, grads[:1], early))
-    new_near, *new_far = update_pieces(numbers, grams, near, far, grads, GRADIENTS, gates, RAW, lines)
-    new_far, (mixer, own) = new_far[:half], new_far[half:]
+    grams = swap(gram_pieces(near, far, lines, grads[:1]))
+    new_near, *new_far = update_pieces(numbers, grams, near, far, grads, GRADIENTS, lines)
     new_near = swap_near(new_near, slabs)
     new_far = [exchange(piece, half + x, slabs) for x, piece in enumerate(new_far)]
-    if RAW:
-        views = [(0, k, lines + TILE) for k in range(half)] + [(1, k, 0) for k in range(half)]
-        slopes, _ = gradient_pieces([near] + gates, tuple(views), raw_obs, raw_prec, [])
-        new_raw = swap_near(update_raw(near, gates[0], mixer, own, numbers, in_hbm(slopes), RAW, lines), slabs)
-    row = join_pieces(None, slabs, [new_near], [(0, k, k, False, 0) for k in range(half)])
+    row = join_pieces(None, slabs, [new_near], [(0, k, k) for k in range(half)])
     for group in ((0, 1, 2, 3), (4, 5)):
-        pieces = [(n, None, half + x, False, RAW) for n, x in enumerate(group)]
+        pieces = [(n, None, half + x) for n, x in enumerate(group)]
         row = join_pieces(row, slabs, [new_far[x] for x in group], pieces)
-    if RAW:
-        row = join_pieces(row, slabs, [new_raw], [(0, k, k, True, 0) for k in range(half)])
-    return join_pieces(row, slabs, new_far[6:], [(n, None, half + 6 + n, False, RAW) for n in range(half - 6)])
+    return join_pieces(row, slabs, new_far[6:], [(n, None, half + 6 + n) for n in range(half - 6)])
 
 
 def on_device(particles, observed, precision, spread, anneal, step_size):

time: 155 us -> 133 us (0.86)
  starting transfers between devices: 48.4 us -> 35.2 us
  local copies, waits for them, and re-layouts: 9.8 us -> 0 us
  waiting for transfers between devices: 64 us -> 70.3 us
  Pallas kernels: 29.9 us -> 25.1 us
    ppermute x17 -> x16, waiting for transfers between devices: 57.3 us -> 70 us  [exchange(): return lax.ppermute(piece, 'slab', [(i, i ^ k) for i in range(slabs)])]
    unnamed x38 -> x0, local copies, waits for them, and re-layouts: 9.8 us -> none
    ppermute x17 -> x16, starting transfers between devices: 28.3 us -> 20.1 us  [exchange(): return lax.ppermute(piece, 'slab', [(i, i ^ k) for i in range(slabs)])]
    all_to_all x3 -> x2, waiting for transfers between devices: 6.32 us -> 0.01 us  [swap_near(): lax.all_to_all(pieces, 'slab', 0, 0, axis_index_groups=groups, tiled=True)]
    all_to_all x3 -> x2, starting transfers between devices: 15.6 us -> 10.2 us  [swap_near(): lax.all_to_all(pieces, 'slab', 0, 0, axis_index_groups=groups, tiled=True)]
    pallas_call x4 -> x2, Pallas kernels: 11.6 us -> 9.13 us  [the longest x1 5.3 us: update_pieces(): call(functools.partial(update_pieces_body, half, lines, groups), 'update_...]
    pallas_call x4 -> x3, Pallas kernels: 9.45 us -> 7.33 us  [gradient_pieces(): call(functools.partial(gradient_pieces_body, views, len(arrays), len(numb...]
    pallas_call x5 -> x4, Pallas kernels: 6.09 us -> 5.16 us  [join_pieces(): call(functools.partial(join_pieces_body, pieces, slabs // 2, NCELL // sla...]
  transfers between devices with their start and end apart: 21 -> 19, of which waited for: 16 -> 16; matrix products, arithmetic and copies ran while one was open for 0% -> 0% of each run, Pallas kernels for 13% -> 9%
where the time goes in v9:
time: 133 us
  waiting for transfers between devices  70.3 us (53%)
  starting transfers between devices  35.2 us (26%)
  Pallas kernels  25.1 us (19%)
  between operations  2.04 us (2%)
    ppermute x16, waiting for transfers between devices, exchange(): return lax.ppermute(piece, 'slab', [(i, i ^ k) for i in range(slabs)])  70 us
    ppermute x16, starting transfers between devices, exchange(): return lax.ppermute(piece, 'slab', [(i, i ^ k) for i in range(slabs)])  20.1 us
    all_to_all x2, starting transfers between devices, swap_near(): lax.all_to_all(pieces, 'slab', 0, 0, axis_index_groups=groups, tiled=True)  10.2 us
    pallas_call x3, Pallas kernels, gradient_pieces(): call(functools.partial(gradient_pieces_body, views, len(arrays), len(numb...  7.33 us
    pallas_call x1, Pallas kernels, update_pieces(): call(functools.partial(update_pieces_body, half, lines, groups), 'update_...  5.3 us
    pallas_call x4, Pallas kernels, join_pieces(): call(functools.partial(join_pieces_body, pieces, slabs // 2, NCELL // sla...  5.16 us
    all_to_all x1, starting transfers between devices, swap(): lax.all_to_all(slabs, 'slab', split_axis=0, concat_axis=0, tiled=True)  4.85 us
    pallas_call x1, Pallas kernels, split_pieces(): call(functools.partial(split_pieces_body, slabs, lines, len(fields)), 'sp...  3.83 us
  transfers between devices with their start and end apart: 19, of which 16 were waited for; matrix products, arithmetic and copies ran while one was open for 0% of the time, Pallas kernels for 9%

profile of v9, /device:TPU:9, one launch (start us, length us, event | category | flops | bytes accessed | tf_op | source)
XLA Modules:
  0.0 132.6 jit_solution(17901651137943959223)
XLA Ops:
  0.0 3.8 %split_pieces.1 = (bf16[8,528,128]{2,1,0:T(8,128)(2,1)}, bf16[528,128]{1,0:T(8,128)(2,1)S(1)}, bf16[528,128]{1,0:T(8,128)(2,1)S(1)}, bf16[528,128]{1,0:T(8,128)(...) custom-call(bf16[1,1048576]{1,0:T(2,128)(2,1)} %row_ref.1, ...), custom_call_target="tpu_custom_call" | custom-call | bytes 6488064 | tf_op jit(solution)/shard_map/split_pieces/pallas_call | solution.py:422
  3.8 4.6 %all-to-all-start = ((bf16[8,528,128]{2,1,0:T(8,128)(2,1)}), bf16[8,528,128]{2,1,0:T(8,128)(2,1)S(1)}, u32[]{:S(2)}, u32[]{:S(2)}) async-start(bf16[8,528,128]{2,1,0:T(8,128)(2,1)} %get-tuple-element.29), calls=%async_computation | async-start | bytes 2162688 | tf_op jit(solution)/shard_map/all_to_all | solution.py:672
  8.4 2.3 %collective-permute-start = (bf16[528,128]{1,0:T(8,128)(2,1)S(1)}, bf16[528,128]{1,0:T(8,128)(2,1)S(1)}, u32[]{:S(2)}, u32[]{:S(2)}) collective-permute-start(bf16[528,128]{1,0:T(8,128)(2,1)S(1)} %get-tuple-element.30), channel_id=1, source_target_pairs={{0,8},{1,9},{2,10},{3,11},{4,12},{5,13},{6,14},{7,15},{8,0},{9,1},... | collective-permute-start | bytes 405512 | tf_op jit(solution)/shard_map/ppermute | solution.py:667
  10.7 0.6 collective-permute-start.1
  11.3 3.2 %collective-permute-start.2 = (bf16[528,128]{1,0:T(8,128)(2,1)S(1)}, bf16[528,128]{1,0:T(8,128)(2,1)S(1)}, u32[]{:S(2)}, u32[]{:S(2)}) collective-permute-start(bf16[528,128]{1,0:T(8,128)(2,1)S(1)} %get-tuple-element.32), channel_id=1, source_target_pairs={{0,10},{1,11},{2,8},{3,9},{4,14},{5,15},{6,12},{7,13},{8,2},{9,3},... | collective-permute-start | bytes 405512 | tf_op jit(solution)/shard_map/ppermute | solution.py:667
  14.5 0.3 collective-permute-start.3
  14.8 1.0 collective-permute-start.4
  15.8 10.4 %collective-permute-done.refs_0_ = bf16[528,128]{1,0:T(8,128)(2,1)S(1)} collective-permute-done((bf16[528,128]{1,0:T(8,128)(2,1)S(1)}, bf16[528,128]{1,0:T(8,128)(2,1)S(1)}, u32[]{:S(2)}, u32[]{:S(2)}) %collective-permute-start) | collective-permute-done | bytes 135200 | tf_op jit(solution)/shard_map/ppermute | solution.py:667
  26.2 0.0 collective-permute-start.5
  26.2 3.6 %collective-permute-done.1.refs_1_ = bf16[528,128]{1,0:T(8,128)(2,1)S(1)} collective-permute-done((bf16[528,128]{1,0:T(8,128)(2,1)S(1)}, bf16[528,128]{1,0:T(8,128)(2,1)S(1)}, u32[]{:S(2)}, u32[]{:S(2)}) %collective-permute-start.1) | collective-permute-done | bytes 135200 | tf_op jit(solution)/shard_map/ppermute | solution.py:667
  29.8 0.3 collective-permute-start.6
  30.1 2.8 %collective-permute-done.2.refs_2_ = bf16[528,128]{1,0:T(8,128)(2,1)S(1)} collective-permute-done((bf16[528,128]{1,0:T(8,128)(2,1)S(1)}, bf16[528,128]{1,0:T(8,128)(2,1)S(1)}, u32[]{:S(2)}, u32[]{:S(2)}) %collective-permute-start.2) | collective-permute-done | bytes 135200 | tf_op jit(solution)/shard_map/ppermute | solution.py:667
  32.9 0.0 collective-permute-start.7
  34.9 8.9 %collective-permute-done.3.refs_3_ = bf16[528,128]{1,0:T(8,128)(2,1)S(1)} collective-permute-done((bf16[528,128]{1,0:T(8,128)(2,1)S(1)}, bf16[528,128]{1,0:T(8,128)(2,1)S(1)}, u32[]{:S(2)}, u32[]{:S(2)}) %collective-permute-start.3) | collective-permute-done | bytes 135200 | tf_op jit(solution)/shard_map/ppermute | solution.py:667
  43.8 1.8 %gradient_pieces.3 = (bf16[4,512,128]{2,1,0:T(8,128)(2,1)}, f32[8,128]{1,0:T(8,128)S(1)}) custom-call(bf16[528,128]{1,0:T(8,128)(2,1)S(1)} %collective-permute-done.refs_0_, bf16[528,128]{1,0:T(8,128)(2,1)S(1)} %collective-permute-done.1.refs_1_, bf16[528,128]{1,0:T(8,128)(2,1)S(1)} %collective-permute-done.2.refs_2_, ...), custom_call_target="tpu_custom_call" | custom-call | flops 7864320 | bytes 2097152 | tf_op jit(solution)/shard_map/gradient_pieces/pallas_call | solution.py:572
  45.6 2.6 %collective-permute-done.4.refs_4_.refs_0_ = bf16[528,128]{1,0:T(8,128)(2,1)S(1)} collective-permute-done((bf16[528,128]{1,0:T(8,128)(2,1)S(1)}, bf16[528,128]{1,0:T(8,128)(2,1)S(1)}, u32[]{:S(2)}, u32[]{:S(2)}) %collective-permute-start.4) | collective-permute-done | bytes 135200 | tf_op jit(solution)/shard_map/ppermute | solution.py:667
  48.2 3.4 %collective-permute-done.5.refs_5_.refs_1_ = bf16[528,128]{1,0:T(8,128)(2,1)S(1)} collective-permute-done((bf16[528,128]{1,0:T(8,128)(2,1)S(1)}, bf16[528,128]{1,0:T(8,128)(2,1)S(1)}, u32[]{:S(2)}, u32[]{:S(2)}) %collective-permute-start.5) | collective-permute-done | bytes 135200 | tf_op jit(solution)/shard_map/ppermute | solution.py:667
  51.6 3.9 %collective-permute-done.6.refs_6_.refs_2_ = bf16[528,128]{1,0:T(8,128)(2,1)S(1)} collective-permute-done((bf16[528,128]{1,0:T(8,128)(2,1)S(1)}, bf16[528,128]{1,0:T(8,128)(2,1)S(1)}, u32[]{:S(2)}, u32[]{:S(2)}) %collective-permute-start.6) | collective-permute-done | bytes 135200 | tf_op jit(solution)/shard_map/ppermute | solution.py:667
  55.5 2.9 %collective-permute-done.7.refs_7_.refs_3_ = bf16[528,128]{1,0:T(8,128)(2,1)S(1)} collective-permute-done((bf16[528,128]{1,0:T(8,128)(2,1)S(1)}, bf16[528,128]{1,0:T(8,128)(2,1)S(1)}, u32[]{:S(2)}, u32[]{:S(2)}) %collective-permute-start.7) | collective-permute-done | bytes 135200 | tf_op jit(solution)/shard_map/ppermute | solution.py:667
  58.4 0.0 all-to-all-done.near_ref.refs_0_
  58.4 3.4 %gram_pieces.1 = f32[16,16,128]{2,1,0:T(8,128)} custom-call(bf16[8,528,128]{2,1,0:T(8,128)(2,1)S(1)} %all-to-all-done.near_ref.refs_0_, bf16[528,128]{1,0:T(8,128)(2,1)S(1)} %collective-permute-done.refs_0_, bf16[528,128]{1,0:T(8,128)(2,1)S(1)} %collective-permute-done.1.refs_1_, bf16[528,128]{1,0:T(8,128)(2,1)S(1)} %collective-permute-done.2.refs_2_, ...), custom_call_target="tpu_custom_call" | custom-call | flops 536870912 | bytes 2097152 | tf_op jit(solution)/shard_map/gram_pieces/pallas_call | solution.py:501
  61.8 4.8 %all-to-all-start.1 = ((f32[16,16,128]{2,1,0:T(8,128)}), f32[16,16,128]{2,1,0:T(8,128)S(1)}, u32[]{:S(2)}, u32[]{:S(2)}) async-start(f32[16,16,128]{2,1,0:T(8,128)} %gram_pieces.1), calls=%async_computation.1 | async-start | bytes 262144 | tf_op jit(solution)/shard_map/all_to_all | solution.py:365
  66.7 2.4 %gradient_pieces.4 = (bf16[4,512,128]{2,1,0:T(8,128)(2,1)}, f32[8,128]{1,0:T(8,128)}) custom-call(bf16[528,128]{1,0:T(8,128)(2,1)S(1)} %collective-permute-done.4.refs_4_.refs_0_, bf16[528,128]{1,0:T(8,128)(2,1)S(1)} %collective-permute-done.5.refs_5_.refs_1_, bf16[528,128]{1,0:T(8,128)(2,1)S(1)} %collective-permute-done.6.refs_6_.refs_2_, ...), custom_call_target="tpu_custom_call" | custom-call | flops 7864320 | bytes 2097152 | tf_op jit(solution)/shard_map/gradient_pieces/pallas_call | solution.py:572
  69.1 3.1 %gradient_pieces.5 = (bf16[8,512,128]{2,1,0:T(8,128)(2,1)}, f32[8,128]{1,0:T(8,128)}) custom-call(bf16[8,528,128]{2,1,0:T(8,128)(2,1)S(1)} %all-to-all-done.near_ref.refs_0_, bf16[512,128]{1,0:T(8,128)(2,1)S(1)} %get-tuple-element.38.refs_4_.refs_1_, bf16[512,128]{1,0:T(8,128)(2,1)S(1)} %get-tuple-element.39.refs_5_.refs_2_), custom_call_target="tpu_custom_call" | custom-call | flops 15728640 | bytes 4194304 | tf_op jit(solution)/shard_map/gradient_pieces/pallas_call | solution.py:572
  72.2 0.4 all-to-all-done.1.refs_9_
  72.6 5.3 %update_pieces.1 = (bf16[8,512,128]{2,1,0:T(8,128)(2,1)}, bf16[512,128]{1,0:T(8,128)(2,1)S(1)}, bf16[512,128]{1,0:T(8,128)(2,1)S(1)}, bf16[512,128]{1,0:T(8,128)...) custom-call(bf16[8,528,128]{2,1,0:T(8,128)(2,1)S(1)} %all-to-all-don, ...), custom_call_target="tpu_custom_call" | custom-call | flops 1073741824 | bytes 6291456 | tf_op jit(solution)/shard_map/update_pieces/pallas_call | solution.py:649
  77.9 5.6 %all-to-all-start.2 = ((bf16[8,512,128]{2,1,0:T(8,128)(2,1)}), bf16[8,512,128]{2,1,0:T(8,128)(2,1)S(1)}, u32[]{:S(2)}, u32[]{:S(2)}) async-start(bf16[8,512,128]{2,1,0:T(8,128)(2,1)} %get-tuple-element.44), calls=%async_computation.2 | async-start | bytes 2097152 | tf_op jit(solution)/shard_map/all_to_all | solution.py:672
  83.5 0.3 collective-permute-start.8
  83.8 2.6 %collective-permute-start.9 = (bf16[512,128]{1,0:T(8,128)(2,1)S(1)}, bf16[512,128]{1,0:T(8,128)(2,1)S(1)}, u32[]{:S(2)}, u32[]{:S(2)}) collective-permute-start(bf16[512,128]{1,0:T(8,128)(2,1)S(1)} %get-tuple-element.46), channel_id=1, source_target_pairs={{0,9},{1,8},{2,11},{3,10},{4,13},{5,12},{6,15},{7,14},{8,1},{9,0},... | collective-permute-start | bytes 393224 | tf_op jit(solution)/shard_map/ppermute | solution.py:667
  86.4 1.2 collective-permute-start.10
  87.6 2.1 %collective-permute-start.11 = (bf16[512,128]{1,0:T(8,128)(2,1)S(1)}, bf16[512,128]{1,0:T(8,128)(2,1)S(1)}, u32[]{:S(2)}, u32[]{:S(2)}) collective-permute-start(bf16[512,128]{1,0:T(8,128)(2,1)S(1)} %get-tuple-element.48), channel_id=1, source_target_pairs={{0,11},{1,10},{2,9},{3,8},{4,15},{5,14},{6,13},{7,12},{8,3},{9,2},... | collective-permute-start | bytes 393224 | tf_op jit(solution)/shard_map/ppermute | solution.py:667
  89.7 0.0 collective-permute-start.12
  89.7 9.2 %collective-permute-done.8.refs_1_ = bf16[512,128]{1,0:T(8,128)(2,1)S(1)} collective-permute-done((bf16[512,128]{1,0:T(8,128)(2,1)S(1)}, bf16[512,128]{1,0:T(8,128)(2,1)S(1)}, u32[]{:S(2)}, u32[]{:S(2)}) %collective-permute-start.8) | collective-permute-done | bytes 131104 | tf_op jit(solution)/shard_map/ppermute | solution.py:667
  98.9 2.0 %collective-permute-start.13 = (bf16[512,128]{1,0:T(8,128)(2,1)S(1)}, bf16[512,128]{1,0:T(8,128)(2,1)S(1)}, u32[]{:S(2)}, u32[]{:S(2)}) collective-permute-start(bf16[512,128]{1,0:T(8,128)(2,1)S(1)} %get-tuple-element.50), channel_id=1, source_target_pairs={{0,13},{1,12},{2,15},{3,14},{4,9},{5,8},{6,11},{7,10},{8,5},{9,4},... | collective-permute-start | bytes 393224 | tf_op jit(solution)/shard_map/ppermute | solution.py:667
  100.9 1.5 %collective-permute-done.9.refs_2_ = bf16[512,128]{1,0:T(8,128)(2,1)S(1)} collective-permute-done((bf16[512,128]{1,0:T(8,128)(2,1)S(1)}, bf16[512,128]{1,0:T(8,128)(2,1)S(1)}, u32[]{:S(2)}, u32[]{:S(2)}) %collective-permute-start.9) | collective-permute-done | bytes 131104 | tf_op jit(solution)/shard_map/ppermute | solution.py:667
  102.4 2.2 %collective-permute-start.14 = (bf16[512,128]{1,0:T(8,128)(2,1)S(1)}, bf16[512,128]{1,0:T(8,128)(2,1)S(1)}, u32[]{:S(2)}, u32[]{:S(2)}) collective-permute-start(bf16[512,128]{1,0:T(8,128)(2,1)S(1)} %get-tuple-element.51), channel_id=1, source_target_pairs={{0,14},{1,15},{2,12},{3,13},{4,10},{5,11},{6,8},{7,9},{8,6},{9,7},... | collective-permute-start | bytes 393224 | tf_op jit(solution)/shard_map/ppermute | solution.py:667
  104.7 0.7 collective-permute-done.10.refs_3_
  105.4 2.0 %collective-permute-start.15 = (bf16[512,128]{1,0:T(8,128)(2,1)S(1)}, bf16[512,128]{1,0:T(8,128)(2,1)S(1)}, u32[]{:S(2)}, u32[]{:S(2)}) collective-permute-start(bf16[512,128]{1,0:T(8,128)(2,1)S(1)} %get-tuple-element.52), channel_id=1, source_target_pairs={{0,15},{1,14},{2,13},{3,12},{4,11},{5,10},{6,9},{7,8},{8,7},{9,6},... | collective-permute-start | bytes 393224 | tf_op jit(solution)/shard_map/ppermute | solution.py:667
  107.4 0.0 all-to-all-done.2.refs_0_
  107.4 2.5 %join_pieces.4.refs_0_ = bf16[1,1048576]{1,0:T(2,128)(2,1)} custom-call(bf16[8,512,128]{2,1,0:T(8,128)(2,1)S(1)} %all-to-all-done.2.refs_0_), custom_call_target="tpu_custom_call" | custom-call | bytes 3145728 | tf_op jit(solution)/shard_map/join_pieces/pallas_call | solution.py:452
  109.9 0.0 collective-permute-done.11.refs_4_
  109.9 1.0 join_pieces.5.refs_0_
  110.9 11.0 %collective-permute-done.12.refs_1_ = bf16[512,128]{1,0:T(8,128)(2,1)S(1)} collective-permute-done((bf16[512,128]{1,0:T(8,128)(2,1)S(1)}, bf16[512,128]{1,0:T(8,128)(2,1)S(1)}, u32[]{:S(2)}, u32[]{:S(2)}) %collective-permute-start.12) | collective-permute-done | bytes 131104 | tf_op jit(solution)/shard_map/ppermute | solution.py:667
  122.0 3.7 %collective-permute-done.13.refs_2_ = bf16[512,128]{1,0:T(8,128)(2,1)S(1)} collective-permute-done((bf16[512,128]{1,0:T(8,128)(2,1)S(1)}, bf16[512,128]{1,0:T(8,128)(2,1)S(1)}, u32[]{:S(2)}, u32[]{:S(2)}) %collective-permute-start.13) | collective-permute-done | bytes 131104 | tf_op jit(solution)/shard_map/ppermute | solution.py:667
  125.6 0.8 join_pieces.6.refs_0_
  126.5 2.0 %collective-permute-done.14.refs_1_ = bf16[512,128]{1,0:T(8,128)(2,1)S(1)} collective-permute-done((bf16[512,128]{1,0:T(8,128)(2,1)S(1)}, bf16[512,128]{1,0:T(8,128)(2,1)S(1)}, u32[]{:S(2)}, u32[]{:S(2)}) %collective-permute-start.14) | collective-permute-done | bytes 131104 | tf_op jit(solution)/shard_map/ppermute | solution.py:667
  128.5 3.3 %collective-permute-done.15.refs_2_ = bf16[512,128]{1,0:T(8,128)(2,1)S(1)} collective-permute-done((bf16[512,128]{1,0:T(8,128)(2,1)S(1)}, bf16[512,128]{1,0:T(8,128)(2,1)S(1)}, u32[]{:S(2)}, u32[]{:S(2)}) %collective-permute-start.15) | collective-permute-done | bytes 131104 | tf_op jit(solution)/shard_map/ppermute | solution.py:667
  131.8 0.8 join_pieces.7
Async XLA Ops:
  3.8 54.5 %all-to-all-start = ((bf16[8,528,128]{2,1,0:T(8,128)(2,1)}), bf16[8,528,128]{2,1,0:T(8,128)(2,1)S(1)}, u32[]{:S(2)}, u32[]{:S(2)}) async-start(bf16[8,528,128]{2,1,0:T(8,128)(2,1)} %get-tuple-element.29), calls=%async_computation | async-start | bytes 2162688 | tf_op jit(solution)/shard_map/all_to_all | solution.py:672
  8.4 17.8 %collective-permute-start = (bf16[528,128]{1,0:T(8,128)(2,1)S(1)}, bf16[528,128]{1,0:T(8,128)(2,1)S(1)}, u32[]{:S(2)}, u32[]{:S(2)}) collective-permute-start(bf16[528,128]{1,0:T(8,128)(2,1)S(1)} %get-tuple-element.30), channel_id=1, source_target_pairs={{0,8},{1,9},{2,10},{3,11},{4,12},{5,13},{6,14},{7,15},{8,0},{9,1},... | collective-permute-start | bytes 405512 | tf_op jit(solution)/shard_map/ppermute | solution.py:667
  10.7 19.1 %collective-permute-start.1 = (bf16[528,128]{1,0:T(8,128)(2,1)S(1)}, bf16[528,128]{1,0:T(8,128)(2,1)S(1)}, u32[]{:S(2)}, u32[]{:S(2)}) collective-permute-start(bf16[528,128]{1,0:T(8,128)(2,1)S(1)} %get-tuple-element.31), channel_id=1, source_target_pairs={{0,9},{1,8},{2,11},{3,10},{4,13},{5,12},{6,15},{7,14},{8,1},{9,0},... | collective-permute-start | bytes 405512 | tf_op jit(solution)/shard_map/ppermute | solution.py:667
  11.3 21.6 %collective-permute-start.2 = (bf16[528,128]{1,0:T(8,128)(2,1)S(1)}, bf16[528,128]{1,0:T(8,128)(2,1)S(1)}, u32[]{:S(2)}, u32[]{:S(2)}) collective-permute-start(bf16[528,128]{1,0:T(8,128)(2,1)S(1)} %get-tuple-element.32), channel_id=1, source_target_pairs={{0,10},{1,11},{2,8},{3,9},{4,14},{5,15},{6,12},{7,13},{8,2},{9,3},... | collective-permute-start | bytes 405512 | tf_op jit(solution)/shard_map/ppermute | solution.py:667
  14.5 29.3 %collective-permute-start.3 = (bf16[528,128]{1,0:T(8,128)(2,1)S(1)}, bf16[528,128]{1,0:T(8,128)(2,1)S(1)}, u32[]{:S(2)}, u32[]{:S(2)}) collective-permute-start(bf16[528,128]{1,0:T(8,128)(2,1)S(1)} %get-tuple-element.33), channel_id=1, source_target_pairs={{0,11},{1,10},{2,9},{3,8},{4,15},{5,14},{6,13},{7,12},{8,3},{9,2},... | collective-permute-start | bytes 405512 | tf_op jit(solution)/shard_map/ppermute | solution.py:667
  14.8 33.4 %collective-permute-start.4 = (bf16[528,128]{1,0:T(8,128)(2,1)S(1)}, bf16[528,128]{1,0:T(8,128)(2,1)S(1)}, u32[]{:S(2)}, u32[]{:S(2)}) collective-permute-start(bf16[528,128]{1,0:T(8,128)(2,1)S(1)} %get-tuple-element.34), channel_id=1, source_target_pairs={{0,12},{1,13},{2,14},{3,15},{4,8},{5,9},{6,10},{7,11},{8,4},{9,5},... | collective-permute-start | bytes 405512 | tf_op jit(solution)/shard_map/ppermute | solution.py:667
  26.2 25.4 %collective-permute-start.5 = (bf16[528,128]{1,0:T(8,128)(2,1)S(1)}, bf16[528,128]{1,0:T(8,128)(2,1)S(1)}, u32[]{:S(2)}, u32[]{:S(2)}) collective-permute-start(bf16[528,128]{1,0:T(8,128)(2,1)S(1)} %get-tuple-element.35), channel_id=1, source_target_pairs={{0,13},{1,12},{2,15},{3,14},{4,9},{5,8},{6,11},{7,10},{8,5},{9,4},... | collective-permute-start | bytes 405512 | tf_op jit(solution)/shard_map/ppermute | solution.py:667
  29.8 25.6 %collective-permute-start.6 = (bf16[528,128]{1,0:T(8,128)(2,1)S(1)}, bf16[528,128]{1,0:T(8,128)(2,1)S(1)}, u32[]{:S(2)}, u32[]{:S(2)}) collective-permute-start(bf16[528,128]{1,0:T(8,128)(2,1)S(1)} %get-tuple-element.36), channel_id=1, source_target_pairs={{0,14},{1,15},{2,12},{3,13},{4,10},{5,11},{6,8},{7,9},{8,6},{9,7},... | collective-permute-start | bytes 405512 | tf_op jit(solution)/shard_map/ppermute | solution.py:667
  32.9 25.4 %collective-permute-start.7 = (bf16[528,128]{1,0:T(8,128)(2,1)S(1)}, bf16[528,128]{1,0:T(8,128)(2,1)S(1)}, u32[]{:S(2)}, u32[]{:S(2)}) collective-permute-start(bf16[528,128]{1,0:T(8,128)(2,1)S(1)} %get-tuple-element.37), channel_id=1, source_target_pairs={{0,15},{1,14},{2,13},{3,12},{4,11},{5,10},{6,9},{7,8},{8,7},{9,6},... | collective-permute-start | bytes 405512 | tf_op jit(solution)/shard_map/ppermute | solution.py:667
  61.8 10.7 %all-to-all-start.1 = ((f32[16,16,128]{2,1,0:T(8,128)}), f32[16,16,128]{2,1,0:T(8,128)S(1)}, u32[]{:S(2)}, u32[]{:S(2)}) async-start(f32[16,16,128]{2,1,0:T(8,128)} %gram_pieces.1), calls=%async_computation.1 | async-start | bytes 262144 | tf_op jit(solution)/shard_map/all_to_all | solution.py:365
  77.9 29.5 %all-to-all-start.2 = ((bf16[8,512,128]{2,1,0:T(8,128)(2,1)}), bf16[8,512,128]{2,1,0:T(8,128)(2,1)S(1)}, u32[]{:S(2)}, u32[]{:S(2)}) async-start(bf16[8,512,128]{2,1,0:T(8,128)(2,1)} %get-tuple-element.44), calls=%async_computation.2 | async-start | bytes 2097152 | tf_op jit(solution)/shard_map/all_to_all | solution.py:672
  83.5 15.4 %collective-permute-start.8 = (bf16[512,128]{1,0:T(8,128)(2,1)S(1)}, bf16[512,128]{1,0:T(8,128)(2,1)S(1)}, u32[]{:S(2)}, u32[]{:S(2)}) collective-permute-start(bf16[512,128]{1,0:T(8,128)(2,1)S(1)} %get-tuple-element.45), channel_id=1, source_target_pairs={{0,8},{1,9},{2,10},{3,11},{4,12},{5,13},{6,14},{7,15},{8,0},{9,1},... | collective-permute-start | bytes 393224 | tf_op jit(solution)/shard_map/ppermute | solution.py:667
  83.8 18.6 %collective-permute-start.9 = (bf16[512,128]{1,0:T(8,128)(2,1)S(1)}, bf16[512,128]{1,0:T(8,128)(2,1)S(1)}, u32[]{:S(2)}, u32[]{:S(2)}) collective-permute-start(bf16[512,128]{1,0:T(8,128)(2,1)S(1)} %get-tuple-element.46), channel_id=1, source_target_pairs={{0,9},{1,8},{2,11},{3,10},{4,13},{5,12},{6,15},{7,14},{8,1},{9,0},... | collective-permute-start | bytes 393224 | tf_op jit(solution)/shard_map/ppermute | solution.py:667
  86.4 19.0 %collective-permute-start.10 = (bf16[512,128]{1,0:T(8,128)(2,1)S(1)}, bf16[512,128]{1,0:T(8,128)(2,1)S(1)}, u32[]{:S(2)}, u32[]{:S(2)}) collective-permute-start(bf16[512,128]{1,0:T(8,128)(2,1)S(1)} %get-tuple-element.47), channel_id=1, source_target_pairs={{0,10},{1,11},{2,8},{3,9},{4,14},{5,15},{6,12},{7,13},{8,2},{9,3},... | collective-permute-start | bytes 393224 | tf_op jit(solution)/shard_map/ppermute | solution.py:667
  87.6 22.3 %collective-permute-start.11 = (bf16[512,128]{1,0:T(8,128)(2,1)S(1)}, bf16[512,128]{1,0:T(8,128)(2,1)S(1)}, u32[]{:S(2)}, u32[]{:S(2)}) collective-permute-start(bf16[512,128]{1,0:T(8,128)(2,1)S(1)} %get-tuple-element.48), channel_id=1, source_target_pairs={{0,11},{1,10},{2,9},{3,8},{4,15},{5,14},{6,13},{7,12},{8,3},{9,2},... | collective-permute-start | bytes 393224 | tf_op jit(solution)/shard_map/ppermute | solution.py:667
  89.7 32.3 %collective-permute-start.12 = (bf16[512,128]{1,0:T(8,128)(2,1)S(1)}, bf16[512,128]{1,0:T(8,128)(2,1)S(1)}, u32[]{:S(2)}, u32[]{:S(2)}) collective-permute-start(bf16[512,128]{1,0:T(8,128)(2,1)S(1)} %get-tuple-element.49), channel_id=1, source_target_pairs={{0,12},{1,13},{2,14},{3,15},{4,8},{5,9},{6,10},{7,11},{8,4},{9,5},... | collective-permute-start | bytes 393224 | tf_op jit(solution)/shard_map/ppermute | solution.py:667
  98.9 26.7 %collective-permute-start.13 = (bf16[512,128]{1,0:T(8,128)(2,1)S(1)}, bf16[512,128]{1,0:T(8,128)(2,1)S(1)}, u32[]{:S(2)}, u32[]{:S(2)}) collective-permute-start(bf16[512,128]{1,0:T(8,128)(2,1)S(1)} %get-tuple-element.50), channel_id=1, source_target_pairs={{0,13},{1,12},{2,15},{3,14},{4,9},{5,8},{6,11},{7,10},{8,5},{9,4},... | collective-permute-start | bytes 393224 | tf_op jit(solution)/shard_map/ppermute | solution.py:667
  102.4 26.1 %collective-permute-start.14 = (bf16[512,128]{1,0:T(8,128)(2,1)S(1)}, bf16[512,128]{1,0:T(8,128)(2,1)S(1)}, u32[]{:S(2)}, u32[]{:S(2)}) collective-permute-start(bf16[512,128]{1,0:T(8,128)(2,1)S(1)} %get-tuple-element.51), channel_id=1, source_target_pairs={{0,14},{1,15},{2,12},{3,13},{4,10},{5,11},{6,8},{7,9},{8,6},{9,7},... | collective-permute-start | bytes 393224 | tf_op jit(solution)/shard_map/ppermute | solution.py:667
  105.4 26.4 %collective-permute-start.15 = (bf16[512,128]{1,0:T(8,128)(2,1)S(1)}, bf16[512,128]{1,0:T(8,128)(2,1)S(1)}, u32[]{:S(2)}, u32[]{:S(2)}) collective-permute-start(bf16[512,128]{1,0:T(8,128)(2,1)S(1)} %get-tuple-element.52), channel_id=1, source_target_pairs={{0,15},{1,14},{2,13},{3,12},{4,11},{5,10},{6,9},{7,8},{8,7},{9,6},... | collective-permute-start | bytes 393224 | tf_op jit(solution)/shard_map/ppermute | solution.py:667

commit v10 on v8

--- a/solution.py
+++ b/solution.py
@@ -461,8 +461,9 @@
         ref = refs[begun + array]
         piece = ref[...] if lead is None else ref[lead]
         held[...] = piece.reshape(held.shape)
-        slab = device_at(at, half)
-        start = ((slab ^ half if across else slab) * lines + begin) * LANES
+        me = lax.axis_index("slab").astype(jnp.int32)
+        slab = me ^ half ^ at if across else device_at(at, half)
+        start = (slab * lines + begin) * LANES
         target = row_ref.at[:, pl.ds(pl.multiple_of(start, GRID_Y), held.shape[1])]
         copies.append(pltpu.make_async_copy(held, target, sems.at[len(copies)]))
         copies[-1].start()
@@ -606,24 +607,26 @@
     )(*arrays, observed, precision, *numbers)
 
 
-def raw_body(raw, lines, near_ref, out_ref):
+def raw_body(raw, lines, near_ref, *refs):
+    out_ref, here_ref = refs[-2:]
     for k in range(near_ref.shape[0]):
         out_ref[k, :raw, :] = near_ref[k, :raw, :]
         below = near_ref[k, raw : raw + TILE, :].astype(F32)[:LINE]
         above = near_ref[k, lines : lines + TILE, :].astype(F32)[LINE:]
         out_ref[k, raw:, :] = jnp.concatenate([below, above], axis=0).astype(BF16)
-
-
-def raw_states(near, raw, lines):
+        here_ref[k, :, :] = near_ref[k, lines + TILE :, :]
+
+
+def raw_states(near, raw, lines, gates):
     out = jax.ShapeDtypeStruct((near.shape[0], raw + TILE, LANES), BF16)
     return call(
         functools.partial(raw_body, raw, lines),
         "raw_states",
-        moved=4 * out.size,
-        in_specs=[IN_VMEM],
-        out_specs=IN_VMEM,
-        out_shape=out,
-    )(near)
+        moved=8 * out.size,
+        in_specs=[IN_VMEM] * (1 + len(gates)),
+        out_specs=[IN_VMEM] * 2,
+        out_shape=[out] * 2,
+    )(near, *gates)
 
 
 def mix(mixer, own, numbers_ref, total, states, slopes):
@@ -639,8 +642,9 @@
 def update_pieces_body(half, raw, lines, groups, near_ref, *refs):
     total = 2 * half
     far_refs, numbers_ref, grams_ref, refs = refs[:half], refs[half], refs[half + 1], refs[half + 2 :]
-    group_refs, near_out, far_outs = refs[: len(groups)], refs[-5 - half], refs[-4 - half : -4]
-    mixer, own, grads, sems = refs[-4:]
+    group_refs, refs = refs[: len(groups)], refs[-half - 11 :]
+    near_to, far_tos, mixer_to, own_to = refs[0], refs[1 : 1 + half], refs[1 + half], refs[2 + half]
+    near_out, far_out, mixer, own, grads, sems, out_sems, last_sems = refs[3 + half :]
     wide = total * TILE
     high = half * TILE
     fetches = []
@@ -666,8 +670,23 @@
     mixer[...] = full.astype(BF16)
     ksum = jnp.sum(full, axis=1, keepdims=True)
     own[...] = jnp.broadcast_to(1.0 + rate * coeff * ksum, (wide, LANES))
+    stores = [
+        pltpu.make_async_copy(mixer, mixer_to, last_sems.at[0]),
+        pltpu.make_async_copy(own, own_to, last_sems.at[1]),
+    ]
+    for store in stores:
+        store.start()
     for fetch in fetches:
         fetch.wait()
+
+    def sent(i, with_far):
+        here = lines_of(i * BLOCK, BLOCK)
+        copies = [pltpu.make_async_copy(near_out.at[:, here, :], near_to.at[:, here, :], out_sems.at[i, 0])]
+        if with_far:
+            there = lines_of(i * BLOCK - raw, BLOCK)
+            for x, far_to in enumerate(far_tos):
+                copies.append(pltpu.make_async_copy(far_out.at[x, there, :], far_to.at[there, :], out_sems.at[i, 1 + x]))
+        return copies
 
     def step(with_far, i, carry):
         for t in range(BLOCK // TILE):
@@ -678,12 +697,23 @@
             new = mix(mixer, own, numbers_ref, total, jnp.concatenate(states, axis=0), slopes)
             near_out[:, part, :] = new[:high].reshape(half, TILE, LANES)
             if with_far:
-                for x, far_out in enumerate(far_outs):
-                    far_out[lines_of(at - raw, TILE), :] = new[high + x * TILE : high + (x + 1) * TILE]
+                far_out[:, lines_of(at - raw, TILE), :] = new[high:].reshape(half, TILE, LANES)
+        for copy in sent(i, with_far):
+            copy.start()
         return carry
 
-    lax.fori_loop(0, raw // BLOCK, functools.partial(step, False), 0)
-    lax.fori_loop(raw // BLOCK, lines // BLOCK, functools.partial(step, True), 0)
+    def finish(with_far, i, carry):
+        for copy in sent(i, with_far):
+            copy.wait()
+        return carry
+
+    first, last = raw // BLOCK, lines // BLOCK
+    lax.fori_loop(0, first, functools.partial(step, False), 0)
+    lax.fori_loop(first, last, functools.partial(step, True), 0)
+    lax.fori_loop(0, first, functools.partial(finish, False), 0)
+    lax.fori_loop(first, last, functools.partial(finish, True), 0)
+    for store in stores:
+        store.wait()
 
 
 def update_pieces(numbers, grams, near, far, grads, groups, gates, raw, lines):
@@ -699,49 +729,73 @@
         flops=4 * wide * wide * LANES * (lines // TILE),
         moved=6 * total * lines * LANES,
         in_specs=[IN_VMEM] * (half + 3) + [IN_HBM] * len(groups) + [IN_VMEM] * len(gates),
-        out_specs=[IN_VMEM] * len(out_shape),
+        out_specs=[IN_HBM] * len(out_shape),
         out_shape=out_shape,
-        scratch_shapes=[pltpu.VMEM((total, lines, LANES), BF16), pltpu.SemaphoreType.DMA((total,))],
+        scratch_shapes=[
+            pltpu.VMEM((half, lines, LANES), BF16),
+            pltpu.VMEM((half, lines - raw, LANES), BF16),
+            pltpu.VMEM((wide, wide), BF16),
+            pltpu.VMEM((wide, LANES), F32),
+            pltpu.VMEM((total, lines, LANES), BF16),
+            pltpu.SemaphoreType.DMA((total,)),
+            pltpu.SemaphoreType.DMA((lines // BLOCK, 1 + half)),
+            pltpu.SemaphoreType.DMA((2,)),
+        ],
     )(near, *far, numbers, grams, *grads, *gates)
 
 
-def update_raw_body(lines, near_ref, across_ref, mixer, own, numbers_ref, grads_ref, out_ref, grads, sem):
-    half, raw, _ = out_ref.shape
+def update_raw_body(here_ref, across_ref, numbers_ref, mixer_ref, own_ref, grads_ref, *refs):
+    out_refs, (news, mixer, own, grads, sems) = refs[:-5], refs[-5:]
+    half, raw, _ = news.shape
     high = half * TILE
-    fetch = pltpu.make_async_copy(grads_ref, grads, sem)
-    fetch.start()
-    fetch.wait()
-    here = lax.axis_index("slab").astype(jnp.int32) % half
+    fetches = [
+        pltpu.make_async_copy(mixer_ref.at[pl.ds(0, high), :], mixer, sems.at[0]),
+        pltpu.make_async_copy(own_ref.at[pl.ds(0, high), :], own, sems.at[1]),
+        pltpu.make_async_copy(grads_ref, grads, sems.at[2]),
+    ]
+    for fetch in fetches:
+        fetch.start()
+    for fetch in fetches:
+        fetch.wait()
+    me = lax.axis_index("slab").astype(jnp.int32) % half
 
     def step(i, carry):
         for t in range(BLOCK // TILE):
-            at = i * BLOCK + t * TILE
-            part = lines_of(at, TILE)
-            states = [near_ref[:, lines_of(lines + TILE + at, TILE), :].reshape(high, LANES)]
+            part = lines_of(i * BLOCK + t * TILE, TILE)
+            states = [here_ref[:, part, :].reshape(high, LANES)]
             slopes = [grads[:half, part, :].reshape(high, LANES)]
             for x in range(half):
-                states += [across_ref[here ^ x, part, :]]
-                slopes += [grads[half + (here ^ x), part, :]]
+                states += [across_ref[me ^ x, part, :]]
+                slopes += [grads[half + (me ^ x), part, :]]
             states, slopes = jnp.concatenate(states, axis=0), jnp.concatenate(slopes, axis=0)
-            new = mix(mixer.at[:high, :], own.at[:high, :], numbers_ref, 2 * half, states, slopes)
-            out_ref[:, part, :] = new.reshape(half, TILE, LANES)
+            new = mix(mixer, own, numbers_ref, 2 * half, states, slopes)
+            news[:, part, :] = new.reshape(half, TILE, LANES)
         return carry
 
     lax.fori_loop(0, raw // BLOCK, step, 0)
-
-
-def update_raw(near, across, mixer, own, numbers, grads, raw, lines):
-    half = near.shape[0]
-    return call(
-        functools.partial(update_raw_body, lines),
+    for k, out_ref in enumerate(out_refs):
+        out_ref[...] = news[me ^ k]
+
+
+def update_raw(here, across, mixer, own, numbers, grads, raw):
+    half = here.shape[0]
+    wide = mixer.shape[0]
+    return call(
+        update_raw_body,
         "update_raw",
         flops=2 * mixer.size * LANES * (raw // TILE),
         moved=12 * half * raw * LANES,
-        in_specs=[IN_VMEM] * 5 + [IN_HBM],
-        out_specs=IN_VMEM,
-        out_shape=jax.ShapeDtypeStruct((half, raw, LANES), BF16),
-        scratch_shapes=[pltpu.VMEM((2 * half, raw, LANES), BF16), pltpu.SemaphoreType.DMA],
-    )(near, across, mixer, own, numbers, grads)
+        in_specs=[IN_VMEM] * 3 + [IN_HBM] * 3,
+        out_specs=[IN_VMEM] * half,
+        out_shape=[jax.ShapeDtypeStruct((raw, LANES), BF16)] * half,
+        scratch_shapes=[
+            pltpu.VMEM((half, raw, LANES), BF16),
+            pltpu.VMEM((half * TILE, wide), BF16),
+            pltpu.VMEM((half * TILE, LANES), F32),
+            pltpu.VMEM((2 * half, raw, LANES), BF16),
+            pltpu.SemaphoreType.DMA((3,)),
+        ],
+    )(here, across, numbers, mixer, own, grads)
 
 
 def exchange(piece, k, slabs):
@@ -767,10 +821,8 @@
     far, (obs, prec, raw_obs, raw_prec) = far[:half], far[half:]
     near = swap_near(near, slabs)
     far = [exchange(piece, half + x, slabs) for x, piece in enumerate(far)]
-    early, gates = [], []
-    if RAW:
-        early = [raw_states(near, RAW, lines)]
-        gates = [exchange(early[0], half, slabs)]
+    raw_near, here = raw_states(near, RAW, lines, far)
+    across = exchange(raw_near, half, slabs)
     grads = []
     numbers = [spread, anneal, step_size]
     for group in GRADIENTS:
@@ -781,21 +833,20 @@
         slopes, rows = gradient_pieces(arrays, tuple(views), obs, prec, [] if grads else numbers)
         grads.append(in_hbm(slopes))
         numbers = numbers if len(grads) > 1 else rows
-    grams = swap(gram_pieces(near, far, lines, grads[:1], early))
-    new_near, *new_far = update_pieces(numbers, grams, near, far, grads, GRADIENTS, gates, RAW, lines)
+    grams = swap(gram_pieces(near, far, lines, grads[:1], [here]))
+    new_near, *new_far = update_pieces(numbers, grams, near, far, grads, GRADIENTS, [across], RAW, lines)
     new_far, (mixer, own) = new_far[:half], new_far[half:]
     new_near = swap_near(new_near, slabs)
     new_far = [exchange(piece, half + x, slabs) for x, piece in enumerate(new_far)]
-    if RAW:
-        views = [(0, k, lines + TILE) for k in range(half)] + [(1, k, 0) for k in range(half)]
-        slopes, _ = gradient_pieces([near] + gates, tuple(views), raw_obs, raw_prec, [])
-        new_raw = swap_near(update_raw(near, gates[0], mixer, own, numbers, in_hbm(slopes), RAW, lines), slabs)
+    views = [(0, k, 0) for k in range(half)] + [(1, k, 0) for k in range(half)]
+    slopes, _ = gradient_pieces([here, across, new_far[2]], tuple(views), raw_obs, raw_prec, [])
+    new_raw = update_raw(here, across, in_hbm(mixer), in_hbm(own), numbers, in_hbm(slopes), RAW)
+    new_raw = [exchange(piece, k, slabs) if k else piece for k, piece in enumerate(new_raw)]
     row = join_pieces(None, slabs, [new_near], [(0, k, k, False, 0) for k in range(half)])
     for group in ((0, 1, 2, 3), (4, 5)):
         pieces = [(n, None, half + x, False, RAW) for n, x in enumerate(group)]
         row = join_pieces(row, slabs, [new_far[x] for x in group], pieces)
-    if RAW:
-        row = join_pieces(row, slabs, [new_raw], [(0, k, k, True, 0) for k in range(half)])
+    row = join_pieces(row, slabs, new_raw, [(k, None, k, True, 0) for k in range(half)])
     return join_pieces(row, slabs, new_far[6:], [(n, None, half + 6 + n, False, RAW) for n in range(half - 6)])
 
 

time: 155 us -> 146 us (0.942); the launches traced: 154 us -> 143 us
  starting transfers between devices: 48.4 us -> 39.5 us
  local copies, waits for them, and re-layouts: 9.8 us -> 6.69 us
  Pallas kernels: 29.9 us -> 31.5 us
    all_to_all x3 -> x2, waiting for transfers between devices: 6.32 us -> 0.01 us  [swap_near(): lax.all_to_all(pieces, 'slab', 0, 0, axis_index_groups=groups, tiled=True)]
    all_to_all x3 -> x2, starting transfers between devices: 15.6 us -> 9.35 us  [swap_near(): lax.all_to_all(pieces, 'slab', 0, 0, axis_index_groups=groups, tiled=True)]
    ppermute x17 -> x24, starting transfers between devices: 28.3 us -> 24.4 us  [exchange(): return lax.ppermute(piece, 'slab', [(i, i ^ k) for i in range(slabs)])]
    ppermute x17 -> x24, waiting for transfers between devices: 57.3 us -> 60.8 us  [exchange(): return lax.ppermute(piece, 'slab', [(i, i ^ k) for i in range(slabs)])]
    unnamed x38 -> x28, local copies, waits for them, and re-layouts: 9.8 us -> 6.69 us
    all_to_all x1, waiting for transfers between devices: 0.36 us -> 2.79 us  [swap(): lax.all_to_all(slabs, 'slab', split_axis=0, concat_axis=0, tiled=True)]
    pallas_call x1, Pallas kernels: 4.65 us -> 6.47 us  [update_pieces(): call(functools.partial(update_pieces_body, half, raw, lines, groups), 'up...]
  transfers between devices with their start and end apart: 21 -> 27, of which waited for: 16 -> 14; matrix products, arithmetic and copies ran while one was open for 0% -> 0% of each run, Pallas kernels for 13% -> 13%
where the time goes in v10:
time: 146 us; the launch traced here: 143 us
  waiting for transfers between devices  63.6 us (44%)
  starting transfers between devices  39.5 us (27%)
  Pallas kernels  31.5 us (22%)
  local copies, waits for them, and re-layouts  6.69 us (5%)
  between operations  2.18 us (1%)
    ppermute x24, waiting for transfers between devices, exchange(): return lax.ppermute(piece, 'slab', [(i, i ^ k) for i in range(slabs)])  60.8 us
    ppermute x24, starting transfers between devices, exchange(): return lax.ppermute(piece, 'slab', [(i, i ^ k) for i in range(slabs)])  24.4 us
    pallas_call x4, Pallas kernels, gradient_pieces(): call(functools.partial(gradient_pieces_body, views, len(arrays), len(numb...  9.49 us
    all_to_all x2, starting transfers between devices, swap_near(): lax.all_to_all(pieces, 'slab', 0, 0, axis_index_groups=groups, tiled=True)  9.35 us
    unnamed x28, local copies, waits for them, and re-layouts  6.69 us
    pallas_call x1, Pallas kernels, update_pieces(): call(functools.partial(update_pieces_body, half, raw, lines, groups), 'up...  6.47 us
    pallas_call x5, Pallas kernels, join_pieces(): call(functools.partial(join_pieces_body, pieces, slabs // 2, NCELL // sla...  5.84 us
    all_to_all x1, starting transfers between devices, swap(): lax.all_to_all(slabs, 'slab', split_axis=0, concat_axis=0, tiled=True)  5.77 us
  transfers between devices with their start and end apart: 27, of which 14 were waited for; matrix products, arithmetic and copies ran while one was open for 0% of the time, Pallas kernels for 13%

profile of v10, /device:TPU:9, one launch (start us, length us, event | category | flops | bytes accessed | tf_op | source)
XLA Modules:
  0.0 143.4 jit_solution(8020231141239689081)
XLA Ops:
  0.0 4.5 %split_pieces.1 = (bf16[8,672,128]{2,1,0:T(8,128)(2,1)}, bf16[528,128]{1,0:T(8,128)(2,1)S(1)}, bf16[528,128]{1,0:T(8,128)(2,1)S(1)}, bf16[528,128]{1,0:T(8,128)(...) custom-call(bf16[1,1048576]{1,0:T(2,128)(2,1)} %row_ref.1, ...), custom_call_target="tpu_custom_call" | custom-call | bytes 7372800 | tf_op jit(solution)/shard_map/split_pieces/pallas_call | solution.py:444
  4.5 4.6 %all-to-all-start = ((bf16[8,672,128]{2,1,0:T(8,128)(2,1)}), bf16[8,672,128]{2,1,0:T(8,128)(2,1)S(1)}, u32[]{:S(2)}, u32[]{:S(2)}) async-start(bf16[8,672,128]{2,1,0:T(8,128)(2,1)} %get-tuple-element.44), calls=%async_computation | async-start | bytes 2752512 | tf_op jit(solution)/shard_map/all_to_all | solution.py:807
  9.1 2.3 %collective-permute-start = (bf16[528,128]{1,0:T(8,128)(2,1)S(1)}, bf16[528,128]{1,0:T(8,128)(2,1)S(1)}, u32[]{:S(2)}, u32[]{:S(2)}) collective-permute-start(bf16[528,128]{1,0:T(8,128)(2,1)S(1)} %get-tuple-element.45), channel_id=1, source_target_pairs={{0,8},{1,9},{2,10},{3,11},{4,12},{5,13},{6,14},{7,15},{8,0},{9,1},... | collective-permute-start | bytes 405512 | tf_op jit(solution)/shard_map/ppermute | solution.py:802
  12.0 3.2 %collective-permute-start.2 = (bf16[528,128]{1,0:T(8,128)(2,1)S(1)}, bf16[528,128]{1,0:T(8,128)(2,1)S(1)}, u32[]{:S(2)}, u32[]{:S(2)}) collective-permute-start(bf16[528,128]{1,0:T(8,128)(2,1)S(1)} %get-tuple-element.47), channel_id=1, source_target_pairs={{0,10},{1,11},{2,8},{3,9},{4,14},{5,15},{6,12},{7,13},{8,2},{9,3},... | collective-permute-start | bytes 405512 | tf_op jit(solution)/shard_map/ppermute | solution.py:802
  15.5 1.0 collective-permute-start.4
  16.5 13.5 %collective-permute-done.refs_0_ = bf16[528,128]{1,0:T(8,128)(2,1)S(1)} collective-permute-done((bf16[528,128]{1,0:T(8,128)(2,1)S(1)}, bf16[528,128]{1,0:T(8,128)(2,1)S(1)}, u32[]{:S(2)}, u32[]{:S(2)}) %collective-permute-start) | collective-permute-done | bytes 135200 | tf_op jit(solution)/shard_map/ppermute | solution.py:802
  30.0 3.6 %collective-permute-done.1.refs_1_ = bf16[528,128]{1,0:T(8,128)(2,1)S(1)} collective-permute-done((bf16[528,128]{1,0:T(8,128)(2,1)S(1)}, bf16[528,128]{1,0:T(8,128)(2,1)S(1)}, u32[]{:S(2)}, u32[]{:S(2)}) %collective-permute-start.1) | collective-permute-done | bytes 135200 | tf_op jit(solution)/shard_map/ppermute | solution.py:802
  33.9 2.8 %collective-permute-done.2.refs_2_ = bf16[528,128]{1,0:T(8,128)(2,1)S(1)} collective-permute-done((bf16[528,128]{1,0:T(8,128)(2,1)S(1)}, bf16[528,128]{1,0:T(8,128)(2,1)S(1)}, u32[]{:S(2)}, u32[]{:S(2)}) %collective-permute-start.2) | collective-permute-done | bytes 135200 | tf_op jit(solution)/shard_map/ppermute | solution.py:802
  38.7 1.7 %collective-permute-done.3.refs_3_ = bf16[528,128]{1,0:T(8,128)(2,1)S(1)} collective-permute-done((bf16[528,128]{1,0:T(8,128)(2,1)}, bf16[528,128]{1,0:T(8,128)(2,1)S(1)}, u32[]{:S(2)}, u32[]{:S(2)}) %collective-permute-start.3) | collective-permute-done | bytes 135200 | tf_op jit(solution)/shard_map/ppermute | solution.py:802
  40.3 1.8 %gradient_pieces.4 = (bf16[4,512,128]{2,1,0:T(8,128)(2,1)}, f32[8,128]{1,0:T(8,128)S(1)}) custom-call(bf16[528,128]{1,0:T(8,128)(2,1)S(1)} %collective-permute-done.refs_0_, bf16[528,128]{1,0:T(8,128)(2,1)S(1)} %collective-permute-done.1.refs_1_, bf16[528,128]{1,0:T(8,128)(2,1)S(1)} %collective-permute-done.2.refs_2_, ...), custom_call_target="tpu_custom_call" | custom-call | flops 7864320 | bytes 2097152 | tf_op jit(solution)/shard_map/gradient_pieces/pallas_call | solution.py:597
  42.2 6.7 %collective-permute-done.4.refs_4_.refs_0_ = bf16[528,128]{1,0:T(8,128)(2,1)S(1)} collective-permute-done((bf16[528,128]{1,0:T(8,128)(2,1)S(1)}, bf16[528,128]{1,0:T(8,128)(2,1)S(1)}, u32[]{:S(2)}, u32[]{:S(2)}) %collective-permute-start.4) | collective-permute-done | bytes 135200 | tf_op jit(solution)/shard_map/ppermute | solution.py:802
  48.8 4.7 %collective-permute-done.5.refs_5_.refs_1_ = bf16[528,128]{1,0:T(8,128)(2,1)S(1)} collective-permute-done((bf16[528,128]{1,0:T(8,128)(2,1)S(1)}, bf16[528,128]{1,0:T(8,128)(2,1)S(1)}, u32[]{:S(2)}, u32[]{:S(2)}) %collective-permute-start.5) | collective-permute-done | bytes 135200 | tf_op jit(solution)/shard_map/ppermute | solution.py:802
  53.6 3.8 %collective-permute-done.6.refs_6_.refs_2_ = bf16[528,128]{1,0:T(8,128)(2,1)S(1)} collective-permute-done((bf16[528,128]{1,0:T(8,128)(2,1)S(1)}, bf16[528,128]{1,0:T(8,128)(2,1)S(1)}, u32[]{:S(2)}, u32[]{:S(2)}) %collective-permute-start.6) | collective-permute-done | bytes 135200 | tf_op jit(solution)/shard_map/ppermute | solution.py:802
  57.4 2.9 %collective-permute-done.7.refs_7_.refs_3_ = bf16[528,128]{1,0:T(8,128)(2,1)S(1)} collective-permute-done((bf16[528,128]{1,0:T(8,128)(2,1)S(1)}, bf16[528,128]{1,0:T(8,128)(2,1)S(1)}, u32[]{:S(2)}, u32[]{:S(2)}) %collective-permute-start.7) | collective-permute-done | bytes 135200 | tf_op jit(solution)/shard_map/ppermute | solution.py:802
  60.3 0.7 raw_states.1
  61.0 2.8 %gram_pieces.1 = f32[16,16,128]{2,1,0:T(8,128)S(1)} custom-call(bf16[8,672,128]{2,1,0:T(8,128)(2,1)S(1)} %all-to-all-done.near_ref.refs_0_, bf16[528,128]{1,0:T(8,128)(2,1)S(1)} %collective-permute-done.refs_0_, bf16[528,128]{1,0:T(8,128)(2,1)S(1)} %collective-permute-done.1.refs_1_, bf16[528,128]{1,0:T(8,128)(2,1)S(1)} %collective-permute-done.2.refs_2_, ...), custom_call_target="tpu_custom_call" | custom-call | flops 536870912 | bytes 2097152 | tf_op jit(solution)/shard_map/gram_pieces/pallas_call | solution.py:526
  63.8 0.6 copy-done.1
  64.5 5.8 %all-to-all-start.1 = ((f32[16,16,128]{2,1,0:T(8,128)}), f32[16,16,128]{2,1,0:T(8,128)S(1)}, u32[]{:S(2)}, u32[]{:S(2)}) async-start(f32[16,16,128]{2,1,0:T(8,128)} %copy-done.1), calls=%async_computation.1 | async-start | bytes 262144 | tf_op jit(solution)/shard_map/all_to_all | solution.py:365
  70.2 2.4 %gradient_pieces.5 = (bf16[4,512,128]{2,1,0:T(8,128)(2,1)}, f32[8,128]{1,0:T(8,128)}) custom-call(bf16[528,128]{1,0:T(8,128)(2,1)S(1)} %collective-permute-done.4.refs_4_.refs_0_, bf16[528,128]{1,0:T(8,128)(2,1)S(1)} %collective-permute-done.5.refs_5_.refs_1_, bf16[528,128]{1,0:T(8,128)(2,1)S(1)} %collective-permute-done.6.refs_6_.refs_2_, ...), custom_call_target="tpu_custom_call" | custom-call | flops 7864320 | bytes 2097152 | tf_op jit(solution)/shard_map/gradient_pieces/pallas_call | solution.py:597
  72.7 3.1 %gradient_pieces.6 = (bf16[8,512,128]{2,1,0:T(8,128)(2,1)}, f32[8,128]{1,0:T(8,128)}) custom-call(bf16[8,672,128]{2,1,0:T(8,128)(2,1)S(1)} %all-to-all-done.near_ref.refs_0_, bf16[512,128]{1,0:T(8,128)(2,1)S(1)} %get-tuple-element.53.refs_4_.refs_1_, bf16[512,128]{1,0:T(8,128)(2,1)S(1)} %get-tuple-element.54.refs_5_.refs_2_), custom_call_target="tpu_custom_call" | custom-call | flops 15728640 | bytes 4194304 | tf_op jit(solution)/shard_map/gradient_pieces/pallas_call | solution.py:597
  75.8 2.8 %all-to-all-done.1.refs_9_ = f32[16,16,128]{2,1,0:T(8,128)S(1)} async-done(((f32[16,16,128]{2,1,0:T(8,128)}), f32[16,16,128]{2,1,0:T(8,128)S(1)}, u32[]{:S(2)}, u32[]{:S(2)}) %all-to-all-start.1) | async-done | bytes 131104 | tf_op jit(solution)/shard_map/all_to_all | solution.py:365
  78.6 6.5 %update_pieces.1 = (bf16[8,512,128]{2,1,0:T(8,128)(2,1)S(1)}, bf16[384,128]{1,0:T(8,128)(2,1)S(1)}, bf16[384,128]{1,0:T(8,128)(2,1)S(1)}, bf16[384,128]{1,0:T(8,...) custom-call(bf16[8,672,128]{2,1,0:T(8,128)(2,1)S(1)} %all-to-all-don, ...), custom_call_target="tpu_custom_call" | custom-call | flops 1073741824 | bytes 6291456 | tf_op jit(solution)/shard_map/update_pieces/pallas_call | solution.py:726
  85.1 1.0 copy-done
  86.0 0.6 copy-done.4
  89.2 0.6 copy-done.11
  91.1 4.8 %all-to-all-start.2 = ((bf16[8,512,128]{2,1,0:T(8,128)(2,1)}), bf16[8,512,128]{2,1,0:T(8,128)(2,1)S(1)}, u32[]{:S(2)}, u32[]{:S(2)}) async-start(bf16[8,512,128]{2,1,0:T(8,128)(2,1)} %copy-done), calls=%async_computation.2 | async-start | bytes 2097152 | tf_op jit(solution)/shard_map/all_to_all | solution.py:807
  95.9 2.1 %collective-permute-start.11 = (bf16[384,128]{1,0:T(8,128)(2,1)}, bf16[384,128]{1,0:T(8,128)(2,1)S(1)}, u32[]{:S(2)}, u32[]{:S(2)}) collective-permute-start(bf16[384,128]{1,0:T(8,128)(2,1)} %copy-done.13), channel_id=1, source_target_pairs={{0,10},{1,11},{2,8},{3,9},{4,14},{5,15},{6,12},{7,13},{8,2},{9,3},... | collective-permute-start | bytes 294920 | tf_op jit(solution)/shard_map/ppermute | solution.py:802
  98.0 1.2 collective-permute-start.9
  99.2 2.0 %collective-permute-start.10 = (bf16[384,128]{1,0:T(8,128)(2,1)}, bf16[384,128]{1,0:T(8,128)(2,1)S(1)}, u32[]{:S(2)}, u32[]{:S(2)}) collective-permute-start(bf16[384,128]{1,0:T(8,128)(2,1)} %copy-done.11), channel_id=1, source_target_pairs={{0,9},{1,8},{2,11},{3,10},{4,13},{5,12},{6,15},{7,14},{8,1},{9,0},... | collective-permute-start | bytes 294920 | tf_op jit(solution)/shard_map/ppermute | solution.py:802
  101.1 0.7 collective-permute-start.12
  101.8 10.4 %collective-permute-done.11.refs_3_.refs_2_ = bf16[384,128]{1,0:T(8,128)(2,1)S(1)} collective-permute-done((bf16[384,128]{1,0:T(8,128)(2,1)}, bf16[384,128]{1,0:T(8,128)(2,1)S(1)}, u32[]{:S(2)}, u32[]{:S(2)}) %collective-permute-start.11) | collective-permute-done | bytes 98336 | tf_op jit(solution)/shard_map/ppermute | solution.py:802
  112.3 1.6 %collective-permute-start.14 = (bf16[384,128]{1,0:T(8,128)(2,1)}, bf16[384,128]{1,0:T(8,128)(2,1)S(1)}, u32[]{:S(2)}, u32[]{:S(2)}) collective-permute-start(bf16[384,128]{1,0:T(8,128)(2,1)} %copy-done.8), channel_id=1, source_target_pairs={{0,13},{1,12},{2,15},{3,14},{4,9},{5,8},{6,11},{7,10},{8,5},{9,4},... | collective-permute-start | bytes 294920 | tf_op jit(solution)/shard_map/ppermute | solution.py:802
  113.9 2.1 %gradient_pieces.7 = (bf16[16,128,128]{2,1,0:T(8,128)(2,1)}, f32[8,128]{1,0:T(8,128)}) custom-call(bf16[8,144,128]{2,1,0:T(8,128)(2,1)S(1)} %get-tuple-element.57.refs_9_.refs_0_.here_ref, bf16[8,144,128]{2,1,0:T(8,128)(2,1)S(1)} %collective-permute-done.8.refs_13_.refs_1_.across_ref, bf16[384,128]{1,0:T(8,128)(2,1)S(1)} %collective-permute-done.11.refs_3_.refs_2_, ...), custom_call_target="tpu_custom_call" | custom-call | flops 7864320 | bytes 2097152 | tf_op jit(solution)/shard_map/gradient_pieces/pallas_call | solution.py:597
  116.0 1.7 %update_raw.1 = (bf16[128,128]{1,0:T(8,128)(2,1)S(1)}, bf16[128,128]{1,0:T(8,128)(2,1)S(1)}, bf16[128,128]{1,0:T(8,128)(2,1)S(1)}, bf16[128,128]{1,0:T(8,128)(2,...) custom-call(bf16[8,144,128]{2,1,0:T(8,128)(2,1)S(1)} %get-tuple-elem, ...), custom_call_target="tpu_custom_call" | custom-call | flops 134217728 | bytes 1572864 | tf_op jit(solution)/shard_map/update_raw/pallas_call | solution.py:783
  117.8 1.2 collective-permute-start.22
  119.4 1.5 %collective-permute-start.23 = (bf16[384,128]{1,0:T(8,128)(2,1)S(1)}, bf16[384,128]{1,0:T(8,128)(2,1)S(1)}, u32[]{:S(2)}, u32[]{:S(2)}) collective-permute-start(bf16[384,128]{1,0:T(8,128)(2,1)S(1)} %copy-done.5), channel_id=1, source_target_pairs={{0,15},{1,14},{2,13},{3,12},{4,11},{5,10},{6,9},{7,8},{8,7},{9,6},... | collective-permute-start | bytes 294920 | tf_op jit(solution)/shard_map/ppermute | solution.py:802
  120.9 3.4 %collective-permute-done.13.refs_1_ = bf16[384,128]{1,0:T(8,128)(2,1)S(1)} collective-permute-done((bf16[384,128]{1,0:T(8,128)(2,1)}, bf16[384,128]{1,0:T(8,128)(2,1)S(1)}, u32[]{:S(2)}, u32[]{:S(2)}) %collective-permute-start.13) | collective-permute-done | bytes 98336 | tf_op jit(solution)/shard_map/ppermute | solution.py:802
  124.3 5.3 %collective-permute-done.14.refs_2_ = bf16[384,128]{1,0:T(8,128)(2,1)S(1)} collective-permute-done((bf16[384,128]{1,0:T(8,128)(2,1)}, bf16[384,128]{1,0:T(8,128)(2,1)S(1)}, u32[]{:S(2)}, u32[]{:S(2)}) %collective-permute-start.14) | collective-permute-done | bytes 98336 | tf_op jit(solution)/shard_map/ppermute | solution.py:802
  129.6 1.1 collective-permute-start.18
  130.7 2.2 %collective-permute-start.19 = (bf16[128,128]{1,0:T(8,128)(2,1)S(1)}, bf16[128,128]{1,0:T(8,128)(2,1)S(1)}, u32[]{:S(2)}, u32[]{:S(2)}) collective-permute-start(bf16[128,128]{1,0:T(8,128)(2,1)S(1)} %get-tuple-element.78), channel_id=1, source_target_pairs={{0,5},{1,4},{2,7},{3,6},{4,1},{5,0},{6,3},{7,2},{8,13},{9,12},{10,... | collective-permute-start | bytes 98312 | tf_op jit(solution)/shard_map/ppermute | solution.py:802
  132.9 1.7 %collective-permute-done.17.refs_4_ = bf16[128,128]{1,0:T(8,128)(2,1)S(1)} collective-permute-done((bf16[128,128]{1,0:T(8,128)(2,1)S(1)}, bf16[128,128]{1,0:T(8,128)(2,1)S(1)}, u32[]{:S(2)}, u32[]{:S(2)}) %collective-permute-start.17) | collective-permute-done | bytes 32800 | tf_op jit(solution)/shard_map/ppermute | solution.py:802
  134.6 2.1 %collective-permute-start.20 = (bf16[128,128]{1,0:T(8,128)(2,1)S(1)}, bf16[128,128]{1,0:T(8,128)(2,1)S(1)}, u32[]{:S(2)}, u32[]{:S(2)}) collective-permute-start(bf16[128,128]{1,0:T(8,128)(2,1)S(1)} %get-tuple-element.79), channel_id=1, source_target_pairs={{0,6},{1,7},{2,4},{3,5},{4,2},{5,3},{6,0},{7,1},{8,14},{9,15},{10,... | collective-permute-start | bytes 98312 | tf_op jit(solution)/shard_map/ppermute | solution.py:802
  136.7 0.8 collective-permute-start.21
  137.5 2.5 %join_pieces.5.refs_0_ = bf16[1,1048576]{1,0:T(2,128)(2,1)} custom-call(bf16[8,512,128]{2,1,0:T(8,128)(2,1)S(1)} %all-to-all-done.2.refs_0_), custom_call_target="tpu_custom_call" | custom-call | bytes 3145728 | tf_op jit(solution)/shard_map/join_pieces/pallas_call | solution.py:477
  140.0 0.9 join_pieces.6.refs_0_
  140.9 0.8 join_pieces.7.refs_0_
  141.8 0.9 join_pieces.8.refs_0_
  142.7 0.8 join_pieces.9
  (48 shorter events, 5.5 us)
Async XLA Ops:
  4.5 55.8 %all-to-all-start = ((bf16[8,672,128]{2,1,0:T(8,128)(2,1)}), bf16[8,672,128]{2,1,0:T(8,128)(2,1)S(1)}, u32[]{:S(2)}, u32[]{:S(2)}) async-start(bf16[8,672,128]{2,1,0:T(8,128)(2,1)} %get-tuple-element.44), calls=%async_computation | async-start | bytes 2752512 | tf_op jit(solution)/shard_map/all_to_all | solution.py:807
  9.1 20.9 %collective-permute-start = (bf16[528,128]{1,0:T(8,128)(2,1)S(1)}, bf16[528,128]{1,0:T(8,128)(2,1)S(1)}, u32[]{:S(2)}, u32[]{:S(2)}) collective-permute-start(bf16[528,128]{1,0:T(8,128)(2,1)S(1)} %get-tuple-element.45), channel_id=1, source_target_pairs={{0,8},{1,9},{2,10},{3,11},{4,12},{5,13},{6,14},{7,15},{8,0},{9,1},... | collective-permute-start | bytes 405512 | tf_op jit(solution)/shard_map/ppermute | solution.py:802
  11.4 22.2 %collective-permute-start.1 = (bf16[528,128]{1,0:T(8,128)(2,1)S(1)}, bf16[528,128]{1,0:T(8,128)(2,1)S(1)}, u32[]{:S(2)}, u32[]{:S(2)}) collective-permute-start(bf16[528,128]{1,0:T(8,128)(2,1)S(1)} %get-tuple-element.46), channel_id=1, source_target_pairs={{0,9},{1,8},{2,11},{3,10},{4,13},{5,12},{6,15},{7,14},{8,1},{9,0},... | collective-permute-start | bytes 405512 | tf_op jit(solution)/shard_map/ppermute | solution.py:802
  12.0 24.8 %collective-permute-start.2 = (bf16[528,128]{1,0:T(8,128)(2,1)S(1)}, bf16[528,128]{1,0:T(8,128)(2,1)S(1)}, u32[]{:S(2)}, u32[]{:S(2)}) collective-permute-start(bf16[528,128]{1,0:T(8,128)(2,1)S(1)} %get-tuple-element.47), channel_id=1, source_target_pairs={{0,10},{1,11},{2,8},{3,9},{4,14},{5,15},{6,12},{7,13},{8,2},{9,3},... | collective-permute-start | bytes 405512 | tf_op jit(solution)/shard_map/ppermute | solution.py:802
  15.2 25.2 %collective-permute-start.3 = (bf16[528,128]{1,0:T(8,128)(2,1)}, bf16[528,128]{1,0:T(8,128)(2,1)S(1)}, u32[]{:S(2)}, u32[]{:S(2)}) collective-permute-start(bf16[528,128]{1,0:T(8,128)(2,1)} %get-tuple-element.48), channel_id=1, source_target_pairs={{0,11},{1,10},{2,9},{3,8},{4,15},{5,14},{6,13},{7,12},{8,3},{9,2},... | collective-permute-start | bytes 405512 | tf_op jit(solution)/shard_map/ppermute | solution.py:802
  15.5 33.4 %collective-permute-start.4 = (bf16[528,128]{1,0:T(8,128)(2,1)S(1)}, bf16[528,128]{1,0:T(8,128)(2,1)S(1)}, u32[]{:S(2)}, u32[]{:S(2)}) collective-permute-start(bf16[528,128]{1,0:T(8,128)(2,1)S(1)} %get-tuple-element.49), channel_id=1, source_target_pairs={{0,12},{1,13},{2,14},{3,15},{4,8},{5,9},{6,10},{7,11},{8,4},{9,5},... | collective-permute-start | bytes 405512 | tf_op jit(solution)/shard_map/ppermute | solution.py:802
  30.0 23.6 %collective-permute-start.5 = (bf16[528,128]{1,0:T(8,128)(2,1)S(1)}, bf16[528,128]{1,0:T(8,128)(2,1)S(1)}, u32[]{:S(2)}, u32[]{:S(2)}) collective-permute-start(bf16[528,128]{1,0:T(8,128)(2,1)S(1)} %get-tuple-element.50), channel_id=1, source_target_pairs={{0,13},{1,12},{2,15},{3,14},{4,9},{5,8},{6,11},{7,10},{8,5},{9,4},... | collective-permute-start | bytes 405512 | tf_op jit(solution)/shard_map/ppermute | solution.py:802
  33.6 23.8 %collective-permute-start.6 = (bf16[528,128]{1,0:T(8,128)(2,1)S(1)}, bf16[528,128]{1,0:T(8,128)(2,1)S(1)}, u32[]{:S(2)}, u32[]{:S(2)}) collective-permute-start(bf16[528,128]{1,0:T(8,128)(2,1)S(1)} %get-tuple-element.51), channel_id=1, source_target_pairs={{0,14},{1,15},{2,12},{3,13},{4,10},{5,11},{6,8},{7,9},{8,6},{9,7},... | collective-permute-start | bytes 405512 | tf_op jit(solution)/shard_map/ppermute | solution.py:802
  36.7 23.5 %collective-permute-start.7 = (bf16[528,128]{1,0:T(8,128)(2,1)S(1)}, bf16[528,128]{1,0:T(8,128)(2,1)S(1)}, u32[]{:S(2)}, u32[]{:S(2)}) collective-permute-start(bf16[528,128]{1,0:T(8,128)(2,1)S(1)} %get-tuple-element.52), channel_id=1, source_target_pairs={{0,15},{1,14},{2,13},{3,12},{4,11},{5,10},{6,9},{7,8},{8,7},{9,6},... | collective-permute-start | bytes 405512 | tf_op jit(solution)/shard_map/ppermute | solution.py:802
  61.0 17.6 %collective-permute-start.8 = (bf16[8,144,128]{2,1,0:T(8,128)(2,1)}, bf16[8,144,128]{2,1,0:T(8,128)(2,1)S(1)}, u32[]{:S(2)}, u32[]{:S(2)}) collective-permute-start(bf16[8,144,128]{2,1,0:T(8,128)(2,1)} %get-tuple-element.60), channel_id=1, source_target_pairs={{0,8},{1,9},{2,10},{3,11},{4,12},{5,13},{6,14},{7,15},{8,0},{9,1},... | collective-permute-start | bytes 884744 | tf_op jit(solution)/shard_map/ppermute | solution.py:802
  63.8 0.7 copy-start.1
  64.5 14.1 %all-to-all-start.1 = ((f32[16,16,128]{2,1,0:T(8,128)}), f32[16,16,128]{2,1,0:T(8,128)S(1)}, u32[]{:S(2)}, u32[]{:S(2)}) async-start(f32[16,16,128]{2,1,0:T(8,128)} %copy-done.1), calls=%async_computation.1 | async-start | bytes 262144 | tf_op jit(solution)/shard_map/all_to_all | solution.py:365
  85.1 1.0 copy-start
  86.0 0.6 copy-start.4
  86.7 0.6 copy-start.6
  87.3 0.6 copy-start.8
  87.9 0.6 copy-start.9
  88.6 0.6 copy-start.10
  89.2 0.6 copy-start.11
  89.8 0.6 copy-start.12
  90.5 0.6 copy-start.13
  91.1 24.9 %copy-start.2 = (bf16[256,256]{1,0:T(8,128)(2,1)}, bf16[256,256]{1,0:T(8,128)(2,1)S(1)}, u32[]{:S(2)}) copy-start(bf16[256,256]{1,0:T(8,128)(2,1)S(1)} %get-tuple-element.68.mixer_ref) | copy-start | bytes 393220
  91.1 24.9 %copy-start.3 = (f32[256,128]{1,0:T(8,128)}, f32[256,128]{1,0:T(8,128)S(1)}, u32[]{:S(2)}) copy-start(f32[256,128]{1,0:T(8,128)S(1)} %get-tuple-element.69.own_ref) | copy-start | bytes 393220
  91.1 26.7 %copy-start.7 = (bf16[384,128]{1,0:T(8,128)(2,1)S(1)}, bf16[384,128]{1,0:T(8,128)(2,1)}, u32[]{:S(2)}) copy-start(bf16[384,128]{1,0:T(8,128)(2,1)} %copy-done.6) | copy-start | bytes 294916
  91.1 28.2 %copy-start.5 = (bf16[384,128]{1,0:T(8,128)(2,1)S(1)}, bf16[384,128]{1,0:T(8,128)(2,1)}, u32[]{:S(2)}) copy-start(bf16[384,128]{1,0:T(8,128)(2,1)} %copy-done.4) | copy-start | bytes 294916
  91.1 46.4 %all-to-all-start.2 = ((bf16[8,512,128]{2,1,0:T(8,128)(2,1)}), bf16[8,512,128]{2,1,0:T(8,128)(2,1)S(1)}, u32[]{:S(2)}, u32[]{:S(2)}) async-start(bf16[8,512,128]{2,1,0:T(8,128)(2,1)} %copy-done), calls=%async_computation.2 | async-start | bytes 2097152 | tf_op jit(solution)/shard_map/all_to_all | solution.py:807
  95.9 16.4 %collective-permute-start.11 = (bf16[384,128]{1,0:T(8,128)(2,1)}, bf16[384,128]{1,0:T(8,128)(2,1)S(1)}, u32[]{:S(2)}, u32[]{:S(2)}) collective-permute-start(bf16[384,128]{1,0:T(8,128)(2,1)} %copy-done.13), channel_id=1, source_target_pairs={{0,10},{1,11},{2,8},{3,9},{4,14},{5,15},{6,12},{7,13},{8,2},{9,3},... | collective-permute-start | bytes 294920 | tf_op jit(solution)/shard_map/ppermute | solution.py:802
  98.0 19.8 %collective-permute-start.9 = (bf16[384,128]{1,0:T(8,128)(2,1)}, bf16[384,128]{1,0:T(8,128)(2,1)S(1)}, u32[]{:S(2)}, u32[]{:S(2)}) collective-permute-start(bf16[384,128]{1,0:T(8,128)(2,1)} %copy-done.12), channel_id=1, source_target_pairs={{0,8},{1,9},{2,10},{3,11},{4,12},{5,13},{6,14},{7,15},{8,0},{9,1},... | collective-permute-start | bytes 294920 | tf_op jit(solution)/shard_map/ppermute | solution.py:802
  99.2 18.7 %collective-permute-start.10 = (bf16[384,128]{1,0:T(8,128)(2,1)}, bf16[384,128]{1,0:T(8,128)(2,1)S(1)}, u32[]{:S(2)}, u32[]{:S(2)}) collective-permute-start(bf16[384,128]{1,0:T(8,128)(2,1)} %copy-done.11), channel_id=1, source_target_pairs={{0,9},{1,8},{2,11},{3,10},{4,13},{5,12},{6,15},{7,14},{8,1},{9,0},... | collective-permute-start | bytes 294920 | tf_op jit(solution)/shard_map/ppermute | solution.py:802
  101.1 18.2 %collective-permute-start.12 = (bf16[384,128]{1,0:T(8,128)(2,1)}, bf16[384,128]{1,0:T(8,128)(2,1)S(1)}, u32[]{:S(2)}, u32[]{:S(2)}) collective-permute-start(bf16[384,128]{1,0:T(8,128)(2,1)} %copy-done.10), channel_id=1, source_target_pairs={{0,11},{1,10},{2,9},{3,8},{4,15},{5,14},{6,13},{7,12},{8,3},{9,2},... | collective-permute-start | bytes 294920 | tf_op jit(solution)/shard_map/ppermute | solution.py:802
  101.8 22.5 %collective-permute-start.13 = (bf16[384,128]{1,0:T(8,128)(2,1)}, bf16[384,128]{1,0:T(8,128)(2,1)S(1)}, u32[]{:S(2)}, u32[]{:S(2)}) collective-permute-start(bf16[384,128]{1,0:T(8,128)(2,1)} %copy-done.9), channel_id=1, source_target_pairs={{0,12},{1,13},{2,14},{3,15},{4,8},{5,9},{6,10},{7,11},{8,4},{9,5},... | collective-permute-start | bytes 294920 | tf_op jit(solution)/shard_map/ppermute | solution.py:802
  112.3 17.3 %collective-permute-start.14 = (bf16[384,128]{1,0:T(8,128)(2,1)}, bf16[384,128]{1,0:T(8,128)(2,1)S(1)}, u32[]{:S(2)}, u32[]{:S(2)}) collective-permute-start(bf16[384,128]{1,0:T(8,128)(2,1)} %copy-done.8), channel_id=1, source_target_pairs={{0,13},{1,12},{2,15},{3,14},{4,9},{5,8},{6,11},{7,10},{8,5},{9,4},... | collective-permute-start | bytes 294920 | tf_op jit(solution)/shard_map/ppermute | solution.py:802
  117.8 11.9 %collective-permute-start.15 = (bf16[128,128]{1,0:T(8,128)(2,1)S(1)}, bf16[128,128]{1,0:T(8,128)(2,1)S(1)}, u32[]{:S(2)}, u32[]{:S(2)}) collective-permute-start(bf16[128,128]{1,0:T(8,128)(2,1)S(1)} %get-tuple-element.74), channel_id=1, source_target_pairs={{0,1},{1,0},{2,3},{3,2},{4,5},{5,4},{6,7},{7,6},{8,9},{9,8},{10,11... | collective-permute-start | bytes 98312 | tf_op jit(solution)/shard_map/ppermute | solution.py:802
  117.8 24.8 %collective-permute-start.22 = (bf16[384,128]{1,0:T(8,128)(2,1)S(1)}, bf16[384,128]{1,0:T(8,128)(2,1)S(1)}, u32[]{:S(2)}, u32[]{:S(2)}) collective-permute-start(bf16[384,128]{1,0:T(8,128)(2,1)S(1)} %copy-done.7), channel_id=1, source_target_pairs={{0,14},{1,15},{2,12},{3,13},{4,10},{5,11},{6,8},{7,9},{8,6},{9,7},... | collective-permute-start | bytes 294920 | tf_op jit(solution)/shard_map/ppermute | solution.py:802
  119.4 23.3 %collective-permute-start.23 = (bf16[384,128]{1,0:T(8,128)(2,1)S(1)}, bf16[384,128]{1,0:T(8,128)(2,1)S(1)}, u32[]{:S(2)}, u32[]{:S(2)}) collective-permute-start(bf16[384,128]{1,0:T(8,128)(2,1)S(1)} %copy-done.5), channel_id=1, source_target_pairs={{0,15},{1,14},{2,13},{3,12},{4,11},{5,10},{6,9},{7,8},{8,7},{9,6},... | collective-permute-start | bytes 294920 | tf_op jit(solution)/shard_map/ppermute | solution.py:802
  124.3 6.5 %collective-permute-start.16 = (bf16[128,128]{1,0:T(8,128)(2,1)S(1)}, bf16[128,128]{1,0:T(8,128)(2,1)S(1)}, u32[]{:S(2)}, u32[]{:S(2)}) collective-permute-start(bf16[128,128]{1,0:T(8,128)(2,1)S(1)} %get-tuple-element.75), channel_id=1, source_target_pairs={{0,2},{1,3},{2,0},{3,1},{4,6},{5,7},{6,4},{7,5},{8,10},{9,11},{10,... | collective-permute-start | bytes 98312 | tf_op jit(solution)/shard_map/ppermute | solution.py:802
  129.6 5.0 %collective-permute-start.17 = (bf16[128,128]{1,0:T(8,128)(2,1)S(1)}, bf16[128,128]{1,0:T(8,128)(2,1)S(1)}, u32[]{:S(2)}, u32[]{:S(2)}) collective-permute-start(bf16[128,128]{1,0:T(8,128)(2,1)S(1)} %get-tuple-element.76), channel_id=1, source_target_pairs={{0,3},{1,2},{2,1},{3,0},{4,7},{5,6},{6,5},{7,4},{8,11},{9,10},{10,... | collective-permute-start | bytes 98312 | tf_op jit(solution)/shard_map/ppermute | solution.py:802
  129.6 7.1 %collective-permute-start.18 = (bf16[128,128]{1,0:T(8,128)(2,1)S(1)}, bf16[128,128]{1,0:T(8,128)(2,1)S(1)}, u32[]{:S(2)}, u32[]{:S(2)}) collective-permute-start(bf16[128,128]{1,0:T(8,128)(2,1)S(1)} %get-tuple-element.77), channel_id=1, source_target_pairs={{0,4},{1,5},{2,6},{3,7},{4,0},{5,1},{6,2},{7,3},{8,12},{9,13},{10,... | collective-permute-start | bytes 98312 | tf_op jit(solution)/shard_map/ppermute | solution.py:802
  130.7 11.0 %collective-permute-start.19 = (bf16[128,128]{1,0:T(8,128)(2,1)S(1)}, bf16[128,128]{1,0:T(8,128)(2,1)S(1)}, u32[]{:S(2)}, u32[]{:S(2)}) collective-permute-start(bf16[128,128]{1,0:T(8,128)(2,1)S(1)} %get-tuple-element.78), channel_id=1, source_target_pairs={{0,5},{1,4},{2,7},{3,6},{4,1},{5,0},{6,3},{7,2},{8,13},{9,12},{10,... | collective-permute-start | bytes 98312 | tf_op jit(solution)/shard_map/ppermute | solution.py:802
  134.6 7.2 %collective-permute-start.20 = (bf16[128,128]{1,0:T(8,128)(2,1)S(1)}, bf16[128,128]{1,0:T(8,128)(2,1)S(1)}, u32[]{:S(2)}, u32[]{:S(2)}) collective-permute-start(bf16[128,128]{1,0:T(8,128)(2,1)S(1)} %get-tuple-element.79), channel_id=1, source_target_pairs={{0,6},{1,7},{2,4},{3,5},{4,2},{5,3},{6,0},{7,1},{8,14},{9,15},{10,... | collective-permute-start | bytes 98312 | tf_op jit(solution)/shard_map/ppermute | solution.py:802
  136.7 5.1 %collective-permute-start.21 = (bf16[128,128]{1,0:T(8,128)(2,1)S(1)}, bf16[128,128]{1,0:T(8,128)(2,1)S(1)}, u32[]{:S(2)}, u32[]{:S(2)}) collective-permute-start(bf16[128,128]{1,0:T(8,128)(2,1)S(1)} %get-tuple-element.80), channel_id=1, source_target_pairs={{0,7},{1,6},{2,5},{3,4},{4,3},{5,2},{6,1},{7,0},{8,15},{9,14},{10,... | collective-permute-start | bytes 98312 | tf_op jit(solution)/shard_map/ppermute | solution.py:802

commit v11 on v9

--- a/solution.py
+++ b/solution.py
@@ -365,112 +365,135 @@
     return lax.all_to_all(slabs, "slab", split_axis=0, concat_axis=0, tiled=True)
 
 
-def device_at(at, half):
-    me = lax.axis_index("slab").astype(jnp.int32)
-    return jnp.where(at < half, me - me % half + at, me ^ at)
+def partner(k):
+    return lax.axis_index("slab").astype(jnp.int32) ^ k
 
 
 def lines_of(start, count):
     return pl.ds(pl.multiple_of(start, TILE), count)
 
 
-def split_pieces_body(slabs, lines, fields, row_ref, *refs):
-    half = slabs // 2
-    field_refs, near_out, far_outs = refs[:fields], refs[fields], refs[fields + 1 : fields + 1 + half]
-    slab_refs, helds, sems = refs[fields + 1 + half : -slabs - 1], refs[-slabs - 1 : -1], refs[-1]
+def split_pieces_body(ks, half, raw, lines, gates, fields, row_ref, *refs):
+    field_refs, refs = refs[:fields], refs[fields + gates :]
+    count = len(ks)
+    out_refs, slab_refs, helds, sems = refs[:count], refs[count : -count - 1], refs[-count - 1 : -1], refs[-1]
     cells = lines * LANES
     end = row_ref.shape[1]
+    started = []
+
+    def fetch(source, target):
+        started.append(pltpu.make_async_copy(source, target, sems.at[len(started)]))
+        started[-1].start()
+        return started[-1]
+
+    def part(start, size):
+        return row_ref.at[:, pl.ds(pl.multiple_of(start, GRID_Y), size)]
+
     copies = []
-    for at, held in enumerate(helds):
-        slab = device_at(at, half)
-        parts = (
-            (slab * cells, cells, 0),
-            (jnp.minimum((slab + 1) * cells, end - GRID_Y), GRID_Y, cells),
-            (jnp.maximum(slab * cells - GRID_Y, 0), GRID_Y, cells + GRID_Y),
-        )
-        for n, (start, size, to) in enumerate(parts):
-            source = row_ref.at[:, pl.ds(pl.multiple_of(start, GRID_Y), size)]
-            copies.append(pltpu.make_async_copy(source, held.at[:, pl.ds(to, size)], sems.at[3 * at + n]))
-            copies[-1].start()
-    start = lax.axis_index("slab").astype(jnp.int32) * lines
-    for n, (field_ref, slab_ref) in enumerate(zip(field_refs, slab_refs)):
-        copies.append(pltpu.make_async_copy(field_ref.at[lines_of(start, lines), :], slab_ref, sems.at[3 * slabs + n]))
-        copies[-1].start()
-
-    for at, held in enumerate(helds):
-        out_ref = near_out.at[at] if at < half else far_outs[at - half]
-        for copy in copies[3 * at : 3 * at + 3]:
+    for k, held in zip(ks, helds):
+        slab = partner(k)
+        mine = [
+            fetch(part(slab * cells, cells), held.at[:, pl.ds(0, cells)]),
+            fetch(part(jnp.minimum((slab + 1) * cells, end - GRID_Y), GRID_Y), held.at[:, pl.ds(cells, GRID_Y)]),
+            fetch(part(jnp.maximum(slab * cells - GRID_Y, 0), GRID_Y), held.at[:, pl.ds(cells + GRID_Y, GRID_Y)]),
+        ]
+        if k < half:
+            other = partner(k ^ half)
+            at = cells + 2 * GRID_Y
+            size = raw * LANES + GRID_Y
+            mine += [
+                fetch(part(other * cells, size), held.at[:, pl.ds(at, size)]),
+                fetch(part(jnp.maximum(other * cells - GRID_Y, 0), GRID_Y), held.at[:, pl.ds(at + size, GRID_Y)]),
+            ]
+        copies.append(mine)
+    fetches = []
+    for n, target in enumerate(slab_refs):
+        start = partner(0 if n < fields else half) * lines
+        fetches.append(fetch(field_refs[n % fields].at[lines_of(start, target.shape[0]), :], target))
+
+    def grid_row(held, at):
+        return held[:, pl.ds(at, GRID_Y)].astype(F32).reshape(LINE, LANES)
+
+    for k, held, out_ref, mine in zip(ks, helds, out_refs, copies):
+        for copy in mine:
             copy.wait()
-        slab = device_at(at, half)
+        slab = partner(k)
         out_ref[:lines, :] = held[:, :cells].reshape(lines, LANES)
-        below = held[:, cells : cells + GRID_Y].astype(F32).reshape(LINE, LANES)
-        above = held[:, cells + GRID_Y :].astype(F32).reshape(LINE, LANES)
-        below = jnp.where(slab == slabs - 1, 0.0, below)
-        above = jnp.where(slab == 0, 0.0, above)
-        out_ref[lines:, :] = jnp.concatenate([below, above], axis=0).astype(BF16)
-    for copy in copies[3 * slabs :]:
+        below = jnp.where(slab == end // cells - 1, 0.0, grid_row(held, cells))
+        above = jnp.where(slab == 0, 0.0, grid_row(held, cells + GRID_Y))
+        out_ref[lines : lines + TILE, :] = jnp.concatenate([below, above], axis=0).astype(BF16)
+        if k < half:
+            at = cells + 2 * GRID_Y
+            to = lines + TILE
+            out_ref[to : to + raw, :] = held[:, at : at + raw * LANES].reshape(raw, LANES)
+            below = grid_row(held, at + raw * LANES)
+            above = jnp.where(partner(k ^ half) == 0, 0.0, grid_row(held, at + raw * LANES + GRID_Y))
+            out_ref[to + raw :, :] = jnp.concatenate([below, above], axis=0).astype(BF16)
+    for copy in fetches:
         copy.wait()
 
 
-def split_pieces(row, slabs, fields):
+def split_pieces(row, slabs, raw, ks, gates, fields):
     lines = row.shape[1] // slabs // LANES
     half = slabs // 2
-    rim = lines + TILE
-    out_shape = [jax.ShapeDtypeStruct((half, rim, LANES), BF16)]
-    out_shape += [jax.ShapeDtypeStruct((rim, LANES), BF16)] * half
-    out_shape += [jax.ShapeDtypeStruct((lines, LANES), BF16)] * len(fields)
-    return call(
-        functools.partial(split_pieces_body, slabs, lines, len(fields)),
+    sizes = [lines + TILE + (raw + TILE if k < half else 0) for k in ks]
+    shapes = sizes + [lines] * len(fields) + [raw] * len(fields)
+    return call(
+        functools.partial(split_pieces_body, ks, half, raw, lines, len(gates), len(fields)),
         "split_pieces",
-        moved=6 * slabs * rim * LANES,
-        in_specs=[IN_HBM] * (1 + len(fields)),
-        out_specs=[IN_VMEM] * len(out_shape),
-        out_shape=out_shape,
-        scratch_shapes=[pltpu.VMEM((1, rim * LANES), BF16)] * slabs
-        + [pltpu.SemaphoreType.DMA((3 * slabs + len(fields),))],
-    )(row, *fields)
-
-
-def join_pieces_body(pieces, half, lines, begun, arrays, *refs):
-    row_ref, helds, sems = refs[begun + arrays], refs[begun + arrays + 1 : -1], refs[-1]
+        moved=6 * sum(sizes) * LANES,
+        in_specs=[IN_HBM] * (1 + len(fields)) + [IN_VMEM] * len(gates),
+        out_specs=[IN_VMEM] * len(shapes),
+        out_shape=[jax.ShapeDtypeStruct((size, LANES), BF16) for size in shapes],
+        scratch_shapes=[pltpu.VMEM((1, size * LANES), BF16) for size in sizes]
+        + [pltpu.SemaphoreType.DMA((5 * len(ks) + 2 * len(fields),))],
+    )(row, *fields, *gates)
+
+
+def join_pieces_body(ks, half, raw, lines, begun, *refs):
+    count = len(ks)
+    pieces, row_ref, helds, sems = refs[begun : begun + count], refs[begun + count], refs[begun + count + 1 : -1], refs[-1]
+    cells = lines * LANES
+    skip = raw * LANES
     copies = []
-    for (array, lead, at), held in zip(pieces, helds):
-        ref = refs[begun + array]
-        piece = ref[...] if lead is None else ref[lead]
-        held[...] = piece.reshape(held.shape)
-        start = device_at(at, half) * lines * LANES
-        target = row_ref.at[:, pl.ds(pl.multiple_of(start, GRID_Y), held.shape[1])]
-        copies.append(pltpu.make_async_copy(held, target, sems.at[len(copies)]))
-        copies[-1].start()
+    for k, piece, held in zip(ks, pieces, helds):
+        held[...] = piece[...].reshape(held.shape)
+        if k < half:
+            parts = [(0, cells, partner(k) * cells), (cells, skip, partner(k ^ half) * cells)]
+        else:
+            parts = [(0, cells - skip, partner(k) * cells + skip)]
+        for at, size, start in parts:
+            target = row_ref.at[:, pl.ds(pl.multiple_of(start, GRID_Y), size)]
+            copies.append(pltpu.make_async_copy(held.at[:, pl.ds(at, size)], target, sems.at[len(copies)]))
+            copies[-1].start()
     for copy in copies:
         copy.wait()
 
 
-def join_pieces(row, slabs, arrays, pieces):
-    sizes = [arrays[piece[0]].shape[-2] * LANES for piece in pieces]
+def join_pieces(row, slabs, raw, pieces, ks):
+    sizes = [piece.size for piece in pieces]
     begun = [] if row is None else [row]
     return call(
-        functools.partial(join_pieces_body, pieces, slabs // 2, NCELL // slabs // LANES, len(begun), len(arrays)),
+        functools.partial(join_pieces_body, ks, slabs // 2, raw, NCELL // slabs // LANES, len(begun)),
         "join_pieces",
         moved=6 * sum(sizes),
-        in_specs=[IN_HBM] * len(begun) + [IN_VMEM] * len(arrays),
+        in_specs=[IN_HBM] * len(begun) + [IN_VMEM] * len(pieces),
         out_specs=IN_HBM,
         out_shape=jax.ShapeDtypeStruct((1, NCELL), BF16),
         input_output_aliases={0: 0} if begun else {},
-        scratch_shapes=[pltpu.VMEM((1, size), BF16) for size in sizes] + [pltpu.SemaphoreType.DMA((len(sizes),))],
-    )(*begun, *arrays)
+        scratch_shapes=[pltpu.VMEM((1, size), BF16) for size in sizes] + [pltpu.SemaphoreType.DMA((2 * len(sizes),))],
+    )(*begun, *pieces)
 
 
 def owners(total, dtype):
     wide = total * TILE
     row = lax.broadcasted_iota(jnp.int32, (wide, total), 0)
     col = lax.broadcasted_iota(jnp.int32, (wide, total), 1)
-    return (device_at(row // TILE, total // 2) == col).astype(dtype)
-
-
-def gram_pieces_body(lines, total, near_ref, *refs):
-    half = total // 2
-    pieces, out_ref, pairs = refs[:half], refs[-2], refs[-1]
+    return (partner(row // TILE) == col).astype(dtype)
+
+
+def gram_pieces_body(lines, total, *refs):
+    pieces, out_ref, pairs = refs[:total], refs[-2], refs[-1]
     wide = total * TILE
     tiles = 4
     pairs[...] = jnp.zeros_like(pairs)
@@ -479,35 +502,36 @@
         parts = []
         for t in range(tiles):
             at = lines_of((i * tiles + t) * TILE, TILE)
-            near = near_ref[:, at, :].reshape(wide // 2, LANES)
-            parts.append(jnp.concatenate([near] + [piece[at, :] for piece in pieces], axis=0))
+            parts.append(jnp.concatenate([piece[at, :] for piece in pieces], axis=0))
         block = jnp.concatenate(parts, axis=1)
         pairs[...] += lax.dot_general(block, block, (((1,), (1,)), ((), ())), preferred_element_type=F32)
         return carry
 
     lax.fori_loop(0, lines // TILE // tiles, step, 0)
+    exact = {"precision": lax.Precision.HIGHEST, "preferred_element_type": F32}
     equal = jnp.where(same_line(total), pairs[...], 0.0)
-    exact = {"precision": lax.Precision.HIGHEST, "preferred_element_type": F32}
-    owner = owners(total, F32)
-    half_way = jnp.dot(equal, owner, **exact)
-    gram = lax.dot_general(owner, half_way, (((0,), (0,)), ((), ())), **exact)
+    rows = jnp.sum(equal.reshape(total, TILE, wide), axis=1)
+    gram = jnp.dot(rows, owners(total, F32), **exact)
+    row = lax.broadcasted_iota(jnp.int32, (total, total), 0)
+    col = lax.broadcasted_iota(jnp.int32, (total, total), 1)
+    gram = jnp.dot((row == partner(col)).astype(F32), gram, **exact)
     gram = jnp.concatenate([gram, jnp.zeros((total, LANES - total), F32)], axis=1)
     out_ref[...] = jnp.broadcast_to(gram[None], out_ref.shape)
 
 
-def gram_pieces(near, far, lines, gates):
-    total = 2 * len(far)
+def gram_pieces(pieces, lines, gates):
+    total = len(pieces)
     wide = total * TILE
     return call(
         functools.partial(gram_pieces_body, lines, total),
         "gram_pieces",
         flops=2 * wide * wide * LANES * (lines // TILE),
         moved=2 * total * lines * LANES,
-        in_specs=[IN_VMEM] * (1 + len(far)) + [IN_HBM] * len(gates),
+        in_specs=[IN_VMEM] * total + [IN_HBM] * len(gates),
         out_specs=IN_VMEM,
         out_shape=jax.ShapeDtypeStruct((total, total, LANES), F32),
         scratch_shapes=[pltpu.VMEM((wide, wide), F32)],
-    )(near, *far, *gates)
+    )(*pieces, *gates)
 
 
 def gradient_pieces_body(views, arrays, numbers, *refs):
@@ -565,9 +589,8 @@
     lax.fori_loop(0, steps, finish, 0)
 
 
-def gradient_pieces(arrays, views, observed, precision, numbers):
+def gradient_pieces(arrays, views, observed, precision, numbers, gates):
     count = observed.shape[0]
-    out = pltpu.HBM((len(views), count, LANES), BF16)
     size = len(views) * count * LANES
     return call(
         functools.partial(gradient_pieces_body, views, len(arrays), len(numbers)),
@@ -575,34 +598,53 @@
         flops=30 * size,
         moved=8 * size,
         in_specs=[IN_VMEM] * (len(arrays) + 2)
-        + [pl.BlockSpec(memory_space=pltpu.SMEM)] * len(numbers),
+        + [pl.BlockSpec(memory_space=pltpu.SMEM)] * len(numbers)
+        + [IN_VMEM] * len(gates),
         out_specs=[IN_HBM, IN_VMEM],
-        out_shape=[out, jax.ShapeDtypeStruct((8, LANES), F32)],
-        scratch_shapes=[pltpu.VMEM(out.shape, BF16), pltpu.SemaphoreType.DMA((count // BLOCK,))],
-    )(*arrays, observed, precision, *numbers)
-
-
-def mix(mixer, own, numbers_ref, total, states, slopes):
-    high = mixer.shape[0]
-    rate = numbers_ref[2:3, :1] / total
-    coeff = 2.0 * numbers_ref[1:2, :1] / numbers_ref[:1, :1]
-    both = jnp.concatenate([slopes, states], axis=1)
-    mixed = jnp.dot(mixer[...], both, preferred_element_type=F32)
-    drive, pulled = mixed[:, :LANES], mixed[:, LANES:]
-    return (states[:high].astype(F32) * own[...] + rate * (drive - coeff * pulled)).astype(BF16)
-
-
-def update_pieces_body(half, lines, groups, near_ref, *refs):
+        out_shape=[pltpu.HBM((len(views), count, LANES), BF16), jax.ShapeDtypeStruct((8, LANES), F32)],
+        scratch_shapes=[
+            pltpu.VMEM((len(views), count, LANES), BF16),
+            pltpu.SemaphoreType.DMA((count // BLOCK,)),
+        ],
+    )(*arrays, observed, precision, *numbers, *gates)
+
+
+def raw_body(raw, lines, half, *refs):
+    out_ref = refs[-1]
+    for k, piece in enumerate(refs[:half]):
+        out_ref[k, :raw, :] = piece[:raw, :]
+        below = piece[raw : raw + TILE, :].astype(F32)[:LINE]
+        above = piece[lines : lines + TILE, :].astype(F32)[LINE:]
+        out_ref[k, raw:, :] = jnp.concatenate([below, above], axis=0).astype(BF16)
+
+
+def raw_states(near, raw, lines, gates):
+    half = len(near)
+    return call(
+        functools.partial(raw_body, raw, lines, half),
+        "raw_states",
+        moved=4 * half * raw * LANES,
+        in_specs=[IN_VMEM] * (half + len(gates)),
+        out_specs=IN_VMEM,
+        out_shape=jax.ShapeDtypeStruct((half, raw + TILE, LANES), BF16),
+    )(*near, *gates)
+
+
+def update_pieces_body(near, half, raw, lines, groups, extra, gates, *refs):
     total = 2 * half
-    far_refs, numbers_ref, grams_ref, refs = refs[:half], refs[half], refs[half + 1], refs[half + 2 :]
-    group_refs, near_out, far_outs = refs[: len(groups)], refs[-5 - half], refs[-4 - half : -4]
-    mixer, own, grads, sems = refs[-4:]
+    pieces, numbers_ref, grams_ref, refs = refs[:total], refs[total], refs[total + 1], refs[total + 2 :]
+    group_refs, refs = refs[: len(groups)], refs[len(groups) :]
+    raw_refs, refs = refs[:extra], refs[extra + gates :]
+    targets, (news, grads, raw_grads, mixer, own, sems, out_sems) = refs[:half], refs[half:]
     wide = total * TILE
     high = half * TILE
+    first = 0 if near else high
     fetches = []
     for group, group_ref in zip(groups, group_refs):
-        for j, at in enumerate(group):
-            fetches.append(pltpu.make_async_copy(group_ref.at[j], grads.at[at], sems.at[len(fetches)]))
+        for j, k in enumerate(group):
+            fetches.append(pltpu.make_async_copy(group_ref.at[j], grads.at[k], sems.at[len(fetches)]))
+    if extra:
+        fetches.append(pltpu.make_async_copy(raw_refs[1], raw_grads, sems.at[len(fetches)]))
     for fetch in fetches:
         fetch.start()
     gram = jnp.sum(grams_ref[...], axis=0)[:, :total]
@@ -616,94 +658,140 @@
     across = jnp.sum(diagonal, axis=0, keepdims=True)
     kernel = jnp.exp(-(down + across - 2.0 * gram) / (spread * NCELL)).astype(BF16)
     owner = owners(total, BF16)
-    half_way = jnp.dot(owner, kernel, preferred_element_type=F32).astype(BF16)
+    half_way = jnp.dot(owner[first : first + high], kernel, preferred_element_type=F32).astype(BF16)
     full = lax.dot_general(half_way, owner, (((1,), (1,)), ((), ())), preferred_element_type=F32)
-    full = jnp.where(same_line(total), full, 0.0)
+    full = jnp.where(same_line(total)[first : first + high], full, 0.0)
     mixer[...] = full.astype(BF16)
     ksum = jnp.sum(full, axis=1, keepdims=True)
-    own[...] = jnp.broadcast_to(1.0 + rate * coeff * ksum, (wide, LANES))
+    own[...] = jnp.broadcast_to(1.0 + rate * coeff * ksum, (high, LANES))
     for fetch in fetches:
         fetch.wait()
 
-    def step(i, carry):
+    def mix(to, states, slopes):
+        states = jnp.concatenate(states, axis=0)
+        both = jnp.concatenate([slopes.reshape(wide, LANES), states], axis=1)
+        mixed = jnp.dot(mixer[...], both, preferred_element_type=F32)
+        drive, pulled = mixed[:, :LANES], mixed[:, LANES:]
+        new = states[first : first + high].astype(F32) * own[...] + rate * (drive - coeff * pulled)
+        news[:, lines_of(to, TILE), :] = new.astype(BF16).reshape(half, TILE, LANES)
+
+    def sent(i):
+        part = lines_of(i * BLOCK, BLOCK)
+        return [
+            pltpu.make_async_copy(news.at[k, part, :], target.at[part, :], out_sems.at[i, k])
+            for k, target in enumerate(targets)
+        ]
+
+    begin = 0 if near else raw // BLOCK
+    steps = lines // BLOCK - begin
+
+    def slab_step(i, carry):
         for t in range(BLOCK // TILE):
-            at = i * BLOCK + t * TILE
-            part = lines_of(at, TILE)
-            states = [near_ref[:, part, :].reshape(high, LANES)] + [ref[part, :] for ref in far_refs]
-            slopes = grads[:, part, :].reshape(wide, LANES)
-            new = mix(mixer, own, numbers_ref, total, jnp.concatenate(states, axis=0), slopes)
-            near_out[:, part, :] = new[:high].reshape(half, TILE, LANES)
-            for x, far_out in enumerate(far_outs):
-                far_out[part, :] = new[high + x * TILE : high + (x + 1) * TILE]
+            to = i * BLOCK + t * TILE
+            at = lines_of(begin * BLOCK + to, TILE)
+            mix(to, [piece[at, :] for piece in pieces], grads[:, at, :])
+        for copy in sent(i):
+            copy.start()
         return carry
 
-    lax.fori_loop(0, lines // BLOCK, step, 0)
-
-
-def update_pieces(numbers, grams, near, far, grads, groups, lines):
-    half = len(far)
-    total = 2 * half
-    wide = total * TILE
-    out_shape = [jax.ShapeDtypeStruct((half, lines, LANES), BF16)]
-    out_shape += [jax.ShapeDtypeStruct((lines, LANES), BF16)] * half
-    return call(
-        functools.partial(update_pieces_body, half, lines, groups),
+    def raw_step(i, carry):
+        for t in range(BLOCK // TILE):
+            to = i * BLOCK + t * TILE
+            at = lines_of(to - lines, TILE)
+            states = [piece[lines_of(to + TILE, TILE), :] for piece in pieces[:half]]
+            states += [raw_refs[0][k, at, :] for k in range(half)]
+            mix(to, states, raw_grads[:, at, :])
+        for copy in sent(i):
+            copy.start()
+        return carry
+
+    def finish(i, carry):
+        for copy in sent(i):
+            copy.wait()
+        return carry
+
+    lax.fori_loop(0, steps, slab_step, 0)
+    if near:
+        lax.fori_loop(steps, steps + raw // BLOCK, raw_step, 0)
+        steps += raw // BLOCK
+    lax.fori_loop(0, steps, finish, 0)
+
+
+def update_pieces(numbers, grams, pieces, grads, groups, raw_parts, gates, raw, lines, near):
+    total = len(pieces)
+    half = total // 2
+    wide = total * TILE
+    size = lines + raw if near else lines - raw
+    return call(
+        functools.partial(update_pieces_body, near, half, raw, lines, groups, len(raw_parts), len(gates)),
         "update_pieces",
-        flops=4 * wide * wide * LANES * (lines // TILE),
+        flops=4 * half * TILE * wide * LANES * (lines // TILE),
         moved=6 * total * lines * LANES,
-        in_specs=[IN_VMEM] * (half + 3) + [IN_HBM] * len(groups),
-        out_specs=[IN_VMEM] * len(out_shape),
-        out_shape=out_shape,
+        in_specs=[IN_VMEM] * (total + 2)
+        + [IN_HBM] * len(groups)
+        + [IN_VMEM, IN_HBM][: len(raw_parts)]
+        + [IN_VMEM] * len(gates),
+        out_specs=[IN_HBM] * half,
+        out_shape=[pltpu.HBM((size, LANES), BF16)] * half,
         scratch_shapes=[
-            pltpu.VMEM((wide, wide), BF16),
-            pltpu.VMEM((wide, LANES), F32),
+            pltpu.VMEM((half, size, LANES), BF16),
             pltpu.VMEM((total, lines, LANES), BF16),
-            pltpu.SemaphoreType.DMA((total,)),
+            pltpu.VMEM((total, raw, LANES), BF16),
+            pltpu.VMEM((half * TILE, wide), BF16),
+            pltpu.VMEM((half * TILE, LANES), F32),
+            pltpu.SemaphoreType.DMA((total + 1,)),
+            pltpu.SemaphoreType.DMA((size // BLOCK, half)),
         ],
-    )(near, *far, numbers, grams, *grads)
+    )(*pieces, numbers, grams, *grads, *raw_parts, *gates)
 
 
 def exchange(piece, k, slabs):
-    return lax.ppermute(piece, "slab", [(i, i ^ k) for i in range(slabs)])
-
-
-def swap_near(pieces, slabs):
-    groups = [list(range(slabs // 2)), list(range(slabs // 2, slabs))]
-    return lax.all_to_all(pieces, "slab", 0, 0, axis_index_groups=groups, tiled=True)
-
-
-GRADIENTS = ((8, 9, 10, 11), (12, 13, 14, 15), (0, 1, 2, 3, 4, 5, 6, 7))
-
-
-def by_halves(particles, observed, precision, spread, anneal, step_size):
+    return lax.ppermute(piece, "slab", [(i, i ^ k) for i in range(slabs)]) if k else piece
+
+
+def swap(slabs):
+    return lax.all_to_all(slabs, "slab", split_axis=0, concat_axis=0, tiled=True)
+
+
+RAW = 128
+GRADIENTS = ((8, 9, 10, 11), (0, 1, 2, 3), (4, 5, 6, 7), (12, 13, 14, 15))
+JOINS = ((8, 9, 10, 11), (4, 5, 6, 7), (12, 13), (0, 1, 2, 3), (14, 15))
+
+
+def by_pieces(particles, observed, precision, spread, anneal, step_size):
     slabs = lax.axis_size("slab")
     half = slabs // 2
     lines = NCELL // slabs // LANES
     row = in_hbm(particles)
     fields = [in_hbm(field.reshape(-1, LANES)) for field in (observed, precision)]
-    near, *far = split_pieces(row, slabs, fields)
-    far, (obs, prec) = far[:half], far[half:]
-    near = swap_near(near, slabs)
-    far = [exchange(piece, half + x, slabs) for x, piece in enumerate(far)]
+    nears, fars = tuple(range(half)), tuple(range(half, slabs))
+    *pieces, obs, prec, raw_obs, raw_prec = split_pieces(row, slabs, RAW, fars, [], fields)
+    far = [exchange(piece, k, slabs) for k, piece in zip(fars, pieces)]
+    pieces = split_pieces(row, slabs, RAW, nears, far[:1], [])
+    near = [exchange(piece, k, slabs) for k, piece in zip(nears, pieces)]
+    states = near + far
+    raw_near = raw_states(near, RAW, lines, far)
+    across = exchange(raw_near, half, slabs)
     grads = []
     numbers = [spread, anneal, step_size]
     for group in GRADIENTS:
-        if group[0] < half:
-            arrays, views = [near], [(0, k, 0) for k in group]
-        else:
-            arrays, views = [far[k - half] for k in group], [(j, None, 0) for j in range(len(group))]
-        slopes, rows = gradient_pieces(arrays, tuple(views), obs, prec, [] if grads else numbers)
+        views = tuple((j, None, 0) for j in range(len(group)))
+        arrays = [states[k] for k in group]
+        slopes, rows = gradient_pieces(arrays, views, obs, prec, [] if grads else numbers, [])
         grads.append(in_hbm(slopes))
         numbers = numbers if len(grads) > 1 else rows
-    grams = swap(gram_pieces(near, far, lines, grads[:1]))
-    new_near, *new_far = update_pieces(numbers, grams, near, far, grads, GRADIENTS, lines)
-    new_near = swap_near(new_near, slabs)
-    new_far = [exchange(piece, half + x, slabs) for x, piece in enumerate(new_far)]
-    row = join_pieces(None, slabs, [new_near], [(0, k, k) for k in range(half)])
-    for group in ((0, 1, 2, 3), (4, 5)):
-        pieces = [(n, None, half + x) for n, x in enumerate(group)]
-        row = join_pieces(row, slabs, [new_far[x] for x in group], pieces)
-    return join_pieces(row, slabs, new_far[6:], [(n, None, half + 6 + n) for n in range(half - 6)])
+    grams = swap(gram_pieces(states, lines, grads[:-1]))
+    pieces = update_pieces(numbers, grams, states, grads, GRADIENTS, [], [], RAW, lines, False)
+    new_far = [exchange(piece, k, slabs) for k, piece in zip(fars, pieces)]
+    views = [(k, None, lines + TILE) for k in range(half)] + [(half, k, 0) for k in range(half)]
+    slopes, _ = gradient_pieces(near + [across], tuple(views), raw_obs, raw_prec, [], new_far[:1])
+    raw_parts = [across, in_hbm(slopes)]
+    pieces = update_pieces(numbers, grams, states, grads, GRADIENTS, raw_parts, new_far[1:2], RAW, lines, True)
+    new = [exchange(piece, k, slabs) for k, piece in zip(nears, pieces)] + new_far
+    row = None
+    for group in JOINS:
+        row = join_pieces(row, slabs, RAW, [new[k] for k in group], group)
+    return row
 
 
 def on_device(particles, observed, precision, spread, anneal, step_size):
@@ -711,7 +799,7 @@
     total = particles.shape[0] * slabs
     lines = NCELL // slabs // LANES
     if slabs == 16:
-        return by_halves(particles, observed, precision, spread, anneal, step_size)
+        return by_pieces(particles, observed, precision, spread, anneal, step_size)
     sent, begun = cuts(lines)
     fields = [observed.reshape(-1, LANES), precision.reshape(-1, LANES)]
     numbers = [spread, anneal, step_size]

time: 133 us -> 152 us (1.14)
  the two profiles are of different devices: /device:TPU:9 before, /device:TPU:0 now
where the time goes in v11:
time: 152 us
  waiting for transfers between devices  63.4 us (42%)
  starting transfers between devices  52.2 us (34%)
  Pallas kernels  33.9 us (22%)
  between operations  2.23 us (1%)
    ppermute x31, waiting for transfers between devices, exchange(): lax.ppermute(piece, 'slab', [(i, i ^ k) for i in range(slabs)])  60.3 us
    ppermute x31, starting transfers between devices, exchange(): lax.ppermute(piece, 'slab', [(i, i ^ k) for i in range(slabs)])  47.1 us
    pallas_call x5, Pallas kernels, gradient_pieces(): call(functools.partial(gradient_pieces_body, views, len(arrays), len(numb...  11.1 us
    pallas_call x2, Pallas kernels, update_pieces(): call(functools.partial(update_pieces_body, near, half, raw, lines, groups...  10.4 us
    all_to_all x1, starting transfers between devices, swap(): lax.all_to_all(slabs, 'slab', split_axis=0, concat_axis=0, tiled=True)  5.08 us
    pallas_call x5, Pallas kernels, join_pieces(): call(functools.partial(join_pieces_body, ks, slabs // 2, raw, NCELL // sl...  4.86 us
    pallas_call x2, Pallas kernels, split_pieces(): call(functools.partial(split_pieces_body, ks, half, raw, lines, len(gates...  4.31 us
    pallas_call x1, Pallas kernels, gram_pieces(): call(functools.partial(gram_pieces_body, lines, total), 'gram_pieces', fl...  3.21 us
  transfers between devices with their start and end apart: 32, of which 12 were waited for; matrix products, arithmetic and copies ran while one was open for 0% of the time, Pallas kernels for 17%

profile of v11, /device:TPU:0, one launch (start us, length us, event | category | flops | bytes accessed | tf_op | source)
XLA Modules:
  0.0 151.8 jit_solution(18048781836809125053)
XLA Ops:
  0.0 2.1 %split_pieces.2 = (bf16[528,128]{1,0:T(8,128)(2,1)S(1)}, bf16[528,128]{1,0:T(8,128)(2,1)S(1)}, bf16[528,128]{1,0:T(8,128)(2,1)S(1)}, bf16[528,128]{1,0:T(8,128)(...) custom-call(bf16[1,1048576]{1,0:T(2,128)(2,1)} %row_ref.3, ...), custom_call_target="tpu_custom_call" | custom-call | bytes 3244032 | tf_op jit(solution)/shard_map/split_pieces/pallas_call | solution.py:441
  2.1 4.1 %collective-permute-start = (bf16[528,128]{1,0:T(8,128)(2,1)S(1)}, bf16[528,128]{1,0:T(8,128)(2,1)S(1)}, u32[]{:S(2)}, u32[]{:S(2)}) collective-permute-start(bf16[528,128]{1,0:T(8,128)(2,1)S(1)} %get-tuple-element.47), channel_id=1, source_target_pairs={{0,8},{1,9},{2,10},{3,11},{4,12},{5,13},{6,14},{7,15},{8,0},{9,1},... | collective-permute-start | bytes 405512 | tf_op jit(solution)/shard_map/ppermute | solution.py:749
  6.2 6.5 %collective-permute-done.refs_0_.refs_8_ = bf16[528,128]{1,0:T(8,128)(2,1)S(1)} collective-permute-done((bf16[528,128]{1,0:T(8,128)(2,1)S(1)}, bf16[528,128]{1,0:T(8,128)(2,1)S(1)}, u32[]{:S(2)}, u32[]{:S(2)}) %collective-permute-start) | collective-permute-done | bytes 135200 | tf_op jit(solution)/shard_map/ppermute | solution.py:749
  12.7 2.2 %split_pieces.3 = (bf16[672,128]{1,0:T(8,128)(2,1)S(1)}, bf16[672,128]{1,0:T(8,128)(2,1)S(1)}, bf16[672,128]{1,0:T(8,128)(2,1)S(1)}, bf16[672,128]{1,0:T(8,128)(...) custom-call(bf16[1,1048576]{1,0:T(2,128)(2,1)} %row_ref.3, ...), custom_call_target="tpu_custom_call" | custom-call | bytes 4128768 | tf_op jit(solution)/shard_map/split_pieces/pallas_call | solution.py:441
  15.1 4.0 %collective-permute-start.9 = (bf16[528,128]{1,0:T(8,128)(2,1)S(1)}, bf16[528,128]{1,0:T(8,128)(2,1)S(1)}, u32[]{:S(2)}, u32[]{:S(2)}) collective-permute-start(bf16[528,128]{1,0:T(8,128)(2,1)S(1)} %get-tuple-element.57), channel_id=1, source_target_pairs={{0,10},{1,11},{2,8},{3,9},{4,14},{5,15},{6,12},{7,13},{8,2},{9,3},... | collective-permute-start | bytes 405512 | tf_op jit(solution)/shard_map/ppermute | solution.py:749
  19.0 1.2 collective-permute-start.2
  20.2 9.7 %collective-permute-done.8.refs_1_.refs_9_ = bf16[528,128]{1,0:T(8,128)(2,1)S(1)} collective-permute-done((bf16[528,128]{1,0:T(8,128)(2,1)S(1)}, bf16[528,128]{1,0:T(8,128)(2,1)S(1)}, u32[]{:S(2)}, u32[]{:S(2)}) %collective-permute-start.8) | collective-permute-done | bytes 135200 | tf_op jit(solution)/shard_map/ppermute | solution.py:749
  30.0 5.1 %collective-permute-done.9.refs_2_.refs_10_ = bf16[528,128]{1,0:T(8,128)(2,1)S(1)} collective-permute-done((bf16[528,128]{1,0:T(8,128)(2,1)S(1)}, bf16[528,128]{1,0:T(8,128)(2,1)S(1)}, u32[]{:S(2)}, u32[]{:S(2)}) %collective-permute-start.9) | collective-permute-done | bytes 135200 | tf_op jit(solution)/shard_map/ppermute | solution.py:749
  35.1 1.8 %collective-permute-done.10.refs_3_.refs_11_ = bf16[528,128]{1,0:T(8,128)(2,1)S(1)} collective-permute-done((bf16[528,128]{1,0:T(8,128)(2,1)S(1)}, bf16[528,128]{1,0:T(8,128)(2,1)S(1)}, u32[]{:S(2)}, u32[]{:S(2)}) %collective-permute-start.10) | collective-permute-done | bytes 135200 | tf_op jit(solution)/shard_map/ppermute | solution.py:749
  36.9 2.7 %collective-permute-start.7 = (bf16[672,128]{1,0:T(8,128)(2,1)S(1)}, bf16[672,128]{1,0:T(8,128)(2,1)S(1)}, u32[]{:S(2)}, u32[]{:S(2)}) collective-permute-start(bf16[672,128]{1,0:T(8,128)(2,1)S(1)} %get-tuple-element.55), channel_id=1, source_target_pairs={{0,7},{1,6},{2,5},{3,4},{4,3},{5,2},{6,1},{7,0},{8,15},{9,14},{10,... | collective-permute-start | bytes 516104 | tf_op jit(solution)/shard_map/ppermute | solution.py:749
  40.0 1.7 %collective-permute-start.11 = (bf16[528,128]{1,0:T(8,128)(2,1)S(1)}, bf16[528,128]{1,0:T(8,128)(2,1)S(1)}, u32[]{:S(2)}, u32[]{:S(2)}) collective-permute-start(bf16[528,128]{1,0:T(8,128)(2,1)S(1)} %get-tuple-element.59), channel_id=1, source_target_pairs={{0,12},{1,13},{2,14},{3,15},{4,8},{5,9},{6,10},{7,11},{8,4},{9,5},... | collective-permute-start | bytes 405512 | tf_op jit(solution)/shard_map/ppermute | solution.py:749
  41.7 2.0 %collective-permute-done.5.refs_1_.refs_5_ = bf16[672,128]{1,0:T(8,128)(2,1)S(1)} collective-permute-done((bf16[672,128]{1,0:T(8,128)(2,1)S(1)}, bf16[672,128]{1,0:T(8,128)(2,1)S(1)}, u32[]{:S(2)}, u32[]{:S(2)}) %collective-permute-start.5) | collective-permute-done | bytes 172064 | tf_op jit(solution)/shard_map/ppermute | solution.py:749
  43.7 1.0 collective-permute-start.12
  44.7 4.0 %collective-permute-done.6.refs_2_.refs_6_ = bf16[672,128]{1,0:T(8,128)(2,1)S(1)} collective-permute-done((bf16[672,128]{1,0:T(8,128)(2,1)S(1)}, bf16[672,128]{1,0:T(8,128)(2,1)S(1)}, u32[]{:S(2)}, u32[]{:S(2)}) %collective-permute-start.6) | collective-permute-done | bytes 172064 | tf_op jit(solution)/shard_map/ppermute | solution.py:749
  48.7 1.0 collective-permute-start.13
  49.7 11.1 %collective-permute-done.7.refs_3_.refs_7_ = bf16[672,128]{1,0:T(8,128)(2,1)S(1)} collective-permute-done((bf16[672,128]{1,0:T(8,128)(2,1)S(1)}, bf16[672,128]{1,0:T(8,128)(2,1)S(1)}, u32[]{:S(2)}, u32[]{:S(2)}) %collective-permute-start.7) | collective-permute-done | bytes 172064 | tf_op jit(solution)/shard_map/ppermute | solution.py:749
  60.8 0.8 collective-permute-start.14
  63.5 1.8 %gradient_pieces.5 = (bf16[4,512,128]{2,1,0:T(8,128)(2,1)}, f32[8,128]{1,0:T(8,128)S(1)}) custom-call(bf16[528,128]{1,0:T(8,128)(2,1)S(1)} %collective-permute-done.refs_0_.refs_8_, bf16[528,128]{1,0:T(8,128)(2,1)S(1)} %collective-permute-done.8.refs_1_.refs_9_, bf16[528,128]{1,0:T(8,128)(2,1)S(1)} %collective-permute-done.9.refs_2_.refs_10_, ...), custom_call_target="tpu_custom_call" | custom-call | flops 7864320 | bytes 2097152 | tf_op jit(solution)/shard_map/gradient_pieces/pallas_call | solution.py:595
  65.3 2.4 %gradient_pieces.7 = (bf16[4,512,128]{2,1,0:T(8,128)(2,1)}, f32[8,128]{1,0:T(8,128)}) custom-call(bf16[672,128]{1,0:T(8,128)(2,1)S(1)} %collective-permute-done.4.refs_0_.refs_4_, bf16[672,128]{1,0:T(8,128)(2,1)S(1)} %collective-permute-done.5.refs_1_.refs_5_, bf16[672,128]{1,0:T(8,128)(2,1)S(1)} %collective-permute-done.6.refs_2_.refs_6_, ...), custom_call_target="tpu_custom_call" | custom-call | flops 7864320 | bytes 2097152 | tf_op jit(solution)/shard_map/gradient_pieces/pallas_call | solution.py:595
  67.7 2.4 %gradient_pieces.6 = (bf16[4,512,128]{2,1,0:T(8,128)(2,1)}, f32[8,128]{1,0:T(8,128)}) custom-call(bf16[672,128]{1,0:T(8,128)(2,1)S(1)} %get-tuple-element.48.refs_0_, bf16[672,128]{1,0:T(8,128)(2,1)S(1)} %collective-permute-done.1.refs_1_, bf16[672,128]{1,0:T(8,128)(2,1)S(1)} %collective-permute-done.2.refs_2_, ...), custom_call_target="tpu_custom_call" | custom-call | flops 7864320 | bytes 2097152 | tf_op jit(solution)/shard_map/gradient_pieces/pallas_call | solution.py:595
  70.2 3.2 %gram_pieces.1 = f32[16,16,128]{2,1,0:T(8,128)} custom-call(bf16[672,128]{1,0:T(8,128)(2,1)S(1)} %get-tuple-element.48.refs_0_, bf16[672,128]{1,0:T(8,128)(2,1)S(1)} %collective-permute-done.1.refs_1_, bf16[672,128]{1,0:T(8,128)(2,1)S(1)} %collective-permute-done.2.refs_2_, bf16[672,128]{1,0:T(8,128)(2,1)S(1)} %collective-permute-done.3.refs_3_, ...), custom_call_target="tpu_custom_call" | custom-call | flops 536870912 | bytes 2097152 | tf_op jit(solution)/shard_map/gram_pieces/pallas_call | solution.py:525
  73.4 5.1 %all-to-all-start = ((f32[16,16,128]{2,1,0:T(8,128)}), f32[16,16,128]{2,1,0:T(8,128)S(1)}, u32[]{:S(2)}, u32[]{:S(2)}) async-start(f32[16,16,128]{2,1,0:T(8,128)} %gram_pieces.1), calls=%async_computation | async-start | bytes 262144 | tf_op jit(solution)/shard_map/all_to_all | solution.py:753
  78.5 2.9 %collective-permute-start.19 = (bf16[8,144,128]{2,1,0:T(8,128)(2,1)S(1)}, bf16[8,144,128]{2,1,0:T(8,128)(2,1)S(1)}, u32[]{:S(2)}, u32[]{:S(2)}) collective-permute-start(bf16[8,144,128]{2,1,0:T(8,128)(2,1)S(1)} %raw_states.1), channel_id=1, source_target_pairs={{0,8},{1,9},{2,10},{3,11},{4,12},{5,13},{6,14},{7,15},{8,0},{9,1},... | collective-permute-start | bytes 884744 | tf_op jit(solution)/shard_map/ppermute | solution.py:749
  81.4 2.4 %gradient_pieces.8 = (bf16[4,512,128]{2,1,0:T(8,128)(2,1)}, f32[8,128]{1,0:T(8,128)}) custom-call(bf16[528,128]{1,0:T(8,128)(2,1)S(1)} %collective-permute-done.11.refs_12_.refs_0_, bf16[528,128]{1,0:T(8,128)(2,1)S(1)} %collective-permute-done.12.refs_13_.refs_1_, bf16[528,128]{1,0:T(8,128)(2,1)S(1)} %collective-permute-done.13.refs_14_.refs_2_, ...), custom_call_target="tpu_custom_call" | custom-call | flops 7864320 | bytes 2097152 | tf_op jit(solution)/shard_map/gradient_pieces/pallas_call | solution.py:595
  83.8 3.1 %all-to-all-done.refs_17_ = f32[16,16,128]{2,1,0:T(8,128)S(1)} async-done(((f32[16,16,128]{2,1,0:T(8,128)}), f32[16,16,128]{2,1,0:T(8,128)S(1)}, u32[]{:S(2)}, u32[]{:S(2)}) %all-to-all-start) | async-done | bytes 131104 | tf_op jit(solution)/shard_map/all_to_all | solution.py:753
  86.9 4.5 %update_pieces.2 = (bf16[384,128]{1,0:T(8,128)(2,1)}, bf16[384,128]{1,0:T(8,128)(2,1)}, bf16[384,128]{1,0:T(8,128)(2,1)}, bf16[384,128]{1,0:T(8,128)(2,1)}, bf16...) custom-call(bf16[672,128]{1,0:T(8,128)(2,1)S(1)} %get-tuple-element.48.ref, ...), custom_call_target="tpu_custom_call" | custom-call | flops 536870912 | bytes 6291456 | tf_op jit(solution)/shard_map/update_pieces/pallas_call | solution.py:725
  91.4 6.5 %collective-permute-start.15 = (bf16[384,128]{1,0:T(8,128)(2,1)}, bf16[384,128]{1,0:T(8,128)(2,1)S(1)}, u32[]{:S(2)}, u32[]{:S(2)}) collective-permute-start(bf16[384,128]{1,0:T(8,128)(2,1)} %get-tuple-element.70), channel_id=1, source_target_pairs={{0,8},{1,9},{2,10},{3,11},{4,12},{5,13},{6,14},{7,15},{8,0},{9,1},... | collective-permute-start | bytes 294920 | tf_op jit(solution)/shard_map/ppermute | solution.py:749
  97.9 1.8 %collective-permute-start.17 = (bf16[384,128]{1,0:T(8,128)(2,1)}, bf16[384,128]{1,0:T(8,128)(2,1)S(1)}, u32[]{:S(2)}, u32[]{:S(2)}) collective-permute-start(bf16[384,128]{1,0:T(8,128)(2,1)} %get-tuple-element.72), channel_id=1, source_target_pairs={{0,10},{1,11},{2,8},{3,9},{4,14},{5,15},{6,12},{7,13},{8,2},{9,3},... | collective-permute-start | bytes 294920 | tf_op jit(solution)/shard_map/ppermute | solution.py:749
  99.6 1.6 %collective-permute-start.18 = (bf16[384,128]{1,0:T(8,128)(2,1)}, bf16[384,128]{1,0:T(8,128)(2,1)S(1)}, u32[]{:S(2)}, u32[]{:S(2)}) collective-permute-start(bf16[384,128]{1,0:T(8,128)(2,1)} %get-tuple-element.73), channel_id=1, source_target_pairs={{0,11},{1,10},{2,9},{3,8},{4,15},{5,14},{6,13},{7,12},{8,3},{9,2},... | collective-permute-start | bytes 294920 | tf_op jit(solution)/shard_map/ppermute | solution.py:749
  101.2 3.0 %collective-permute-start.24 = (bf16[384,128]{1,0:T(8,128)(2,1)}, bf16[384,128]{1,0:T(8,128)(2,1)S(1)}, u32[]{:S(2)}, u32[]{:S(2)}) collective-permute-start(bf16[384,128]{1,0:T(8,128)(2,1)} %get-tuple-element.81), channel_id=1, source_target_pairs={{0,12},{1,13},{2,14},{3,15},{4,8},{5,9},{6,10},{7,11},{8,4},{9,5},... | collective-permute-start | bytes 294920 | tf_op jit(solution)/shard_map/ppermute | solution.py:749
  104.2 7.8 %collective-permute-done.15.refs_0_.refs_11_ = bf16[384,128]{1,0:T(8,128)(2,1)S(1)} collective-permute-done((bf16[384,128]{1,0:T(8,128)(2,1)}, bf16[384,128]{1,0:T(8,128)(2,1)S(1)}, u32[]{:S(2)}, u32[]{:S(2)}) %collective-permute-start.15) | collective-permute-done | bytes 98336 | tf_op jit(solution)/shard_map/ppermute | solution.py:749
  112.0 2.2 %gradient_pieces.9 = (bf16[16,128,128]{2,1,0:T(8,128)(2,1)}, f32[8,128]{1,0:T(8,128)}) custom-call(bf16[672,128]{1,0:T(8,128)(2,1)S(1)} %get-tuple-element.48.refs_0_, bf16[672,128]{1,0:T(8,128)(2,1)S(1)} %collective-permute-done.1.refs_1_, bf16[672,128]{1,0:T(8,128)(2,1)S(1)} %collective-permute-done.2.refs_2_, ...), custom_call_target="tpu_custom_call" | custom-call | flops 7864320 | bytes 2097152 | tf_op jit(solution)/shard_map/gradient_pieces/pallas_call | solution.py:595
  114.2 5.9 %update_pieces.3 = (bf16[640,128]{1,0:T(8,128)(2,1)}, bf16[640,128]{1,0:T(8,128)(2,1)}, bf16[640,128]{1,0:T(8,128)(2,1)}, bf16[640,128]{1,0:T(8,128)(2,1)}, bf16...) custom-call(bf16[672,128]{1,0:T(8,128)(2,1)S(1)} %get-tuple-element.48.ref, ...), custom_call_target="tpu_custom_call" | custom-call | flops 536870912 | bytes 6291456 | tf_op jit(solution)/shard_map/update_pieces/pallas_call | solution.py:725
  120.2 1.4 collective-permute-start.21
  121.5 3.0 %collective-permute-start.25 = (bf16[384,128]{1,0:T(8,128)(2,1)S(1)}, bf16[384,128]{1,0:T(8,128)(2,1)S(1)}, u32[]{:S(2)}, u32[]{:S(2)}) collective-permute-start(bf16[384,128]{1,0:T(8,128)(2,1)S(1)} %copy-done.3), channel_id=1, source_target_pairs={{0,13},{1,12},{2,15},{3,14},{4,9},{5,8},{6,11},{7,10},{8,5},{9,4},... | collective-permute-start | bytes 294920 | tf_op jit(solution)/shard_map/ppermute | solution.py:749
  124.6 1.9 %collective-permute-start.23 = (bf16[640,128]{1,0:T(8,128)(2,1)}, bf16[640,128]{1,0:T(8,128)(2,1)S(1)}, u32[]{:S(2)}, u32[]{:S(2)}) collective-permute-start(bf16[640,128]{1,0:T(8,128)(2,1)} %get-tuple-element.80), channel_id=1, source_target_pairs={{0,7},{1,6},{2,5},{3,4},{4,3},{5,2},{6,1},{7,0},{8,15},{9,14},{10,... | collective-permute-start | bytes 491528 | tf_op jit(solution)/shard_map/ppermute | solution.py:749
  126.5 5.9 %collective-permute-done.25.refs_2_ = bf16[384,128]{1,0:T(8,128)(2,1)S(1)} collective-permute-done((bf16[384,128]{1,0:T(8,128)(2,1)S(1)}, bf16[384,128]{1,0:T(8,128)(2,1)S(1)}, u32[]{:S(2)}, u32[]{:S(2)}) %collective-permute-start.25) | collective-permute-done | bytes 98336 | tf_op jit(solution)/shard_map/ppermute | solution.py:749
  132.4 1.1 collective-permute-start.26
  134.1 0.7 collective-permute-start.28
  134.8 1.6 %collective-permute-done.22.refs_3_ = bf16[640,128]{1,0:T(8,128)(2,1)S(1)} collective-permute-done((bf16[640,128]{1,0:T(8,128)(2,1)}, bf16[640,128]{1,0:T(8,128)(2,1)S(1)}, u32[]{:S(2)}, u32[]{:S(2)}) %collective-permute-start.22) | collective-permute-done | bytes 163872 | tf_op jit(solution)/shard_map/ppermute | solution.py:749
  136.5 3.7 %collective-permute-start.29 = (bf16[384,128]{1,0:T(8,128)(2,1)S(1)}, bf16[384,128]{1,0:T(8,128)(2,1)S(1)}, u32[]{:S(2)}, u32[]{:S(2)}) collective-permute-start(bf16[384,128]{1,0:T(8,128)(2,1)S(1)} %copy-done.2), channel_id=1, source_target_pairs={{0,14},{1,15},{2,12},{3,13},{4,10},{5,11},{6,8},{7,9},{8,6},{9,7},... | collective-permute-start | bytes 294920 | tf_op jit(solution)/shard_map/ppermute | solution.py:749
  140.2 1.9 %collective-permute-start.30 = (bf16[384,128]{1,0:T(8,128)(2,1)S(1)}, bf16[384,128]{1,0:T(8,128)(2,1)S(1)}, u32[]{:S(2)}, u32[]{:S(2)}) collective-permute-start(bf16[384,128]{1,0:T(8,128)(2,1)S(1)} %copy-done.1), channel_id=1, source_target_pairs={{0,15},{1,14},{2,13},{3,12},{4,11},{5,10},{6,9},{7,8},{8,7},{9,6},... | collective-permute-start | bytes 294920 | tf_op jit(solution)/shard_map/ppermute | solution.py:749
  142.1 1.0 join_pieces.5.refs_0_
  143.1 1.1 join_pieces.6.refs_0_
  144.3 0.8 join_pieces.7.refs_0_
  145.1 4.7 %collective-permute-done.28.refs_4_ = bf16[640,128]{1,0:T(8,128)(2,1)S(1)} collective-permute-done((bf16[640,128]{1,0:T(8,128)(2,1)}, bf16[640,128]{1,0:T(8,128)(2,1)S(1)}, u32[]{:S(2)}, u32[]{:S(2)}) %collective-permute-start.28) | collective-permute-done | bytes 163872 | tf_op jit(solution)/shard_map/ppermute | solution.py:749
  149.9 1.1 join_pieces.8.refs_0_
  151.0 0.8 join_pieces.9
  (40 shorter events, 1.4 us)
Async XLA Ops:
  2.1 10.6 %collective-permute-start = (bf16[528,128]{1,0:T(8,128)(2,1)S(1)}, bf16[528,128]{1,0:T(8,128)(2,1)S(1)}, u32[]{:S(2)}, u32[]{:S(2)}) collective-permute-start(bf16[528,128]{1,0:T(8,128)(2,1)S(1)} %get-tuple-element.47), channel_id=1, source_target_pairs={{0,8},{1,9},{2,10},{3,11},{4,12},{5,13},{6,14},{7,15},{8,0},{9,1},... | collective-permute-start | bytes 405512 | tf_op jit(solution)/shard_map/ppermute | solution.py:749
  14.9 22.0 %collective-permute-start.1 = (bf16[672,128]{1,0:T(8,128)(2,1)S(1)}, bf16[672,128]{1,0:T(8,128)(2,1)S(1)}, u32[]{:S(2)}, u32[]{:S(2)}) collective-permute-start(bf16[672,128]{1,0:T(8,128)(2,1)S(1)} %get-tuple-element.49), channel_id=1, source_target_pairs={{0,1},{1,0},{2,3},{3,2},{4,5},{5,4},{6,7},{7,6},{8,9},{9,8},{10,11... | collective-permute-start | bytes 516104 | tf_op jit(solution)/shard_map/ppermute | solution.py:749
  15.0 15.0 %collective-permute-start.8 = (bf16[528,128]{1,0:T(8,128)(2,1)S(1)}, bf16[528,128]{1,0:T(8,128)(2,1)S(1)}, u32[]{:S(2)}, u32[]{:S(2)}) collective-permute-start(bf16[528,128]{1,0:T(8,128)(2,1)S(1)} %get-tuple-element.56), channel_id=1, source_target_pairs={{0,9},{1,8},{2,11},{3,10},{4,13},{5,12},{6,15},{7,14},{8,1},{9,0},... | collective-permute-start | bytes 405512 | tf_op jit(solution)/shard_map/ppermute | solution.py:749
  15.1 20.0 %collective-permute-start.9 = (bf16[528,128]{1,0:T(8,128)(2,1)S(1)}, bf16[528,128]{1,0:T(8,128)(2,1)S(1)}, u32[]{:S(2)}, u32[]{:S(2)}) collective-permute-start(bf16[528,128]{1,0:T(8,128)(2,1)S(1)} %get-tuple-element.57), channel_id=1, source_target_pairs={{0,10},{1,11},{2,8},{3,9},{4,14},{5,15},{6,12},{7,13},{8,2},{9,3},... | collective-permute-start | bytes 405512 | tf_op jit(solution)/shard_map/ppermute | solution.py:749
  19.0 17.8 %collective-permute-start.10 = (bf16[528,128]{1,0:T(8,128)(2,1)S(1)}, bf16[528,128]{1,0:T(8,128)(2,1)S(1)}, u32[]{:S(2)}, u32[]{:S(2)}) collective-permute-start(bf16[528,128]{1,0:T(8,128)(2,1)S(1)} %get-tuple-element.58), channel_id=1, source_target_pairs={{0,11},{1,10},{2,9},{3,8},{4,15},{5,14},{6,13},{7,12},{8,3},{9,2},... | collective-permute-start | bytes 405512 | tf_op jit(solution)/shard_map/ppermute | solution.py:749
  19.0 20.5 %collective-permute-start.2 = (bf16[672,128]{1,0:T(8,128)(2,1)S(1)}, bf16[672,128]{1,0:T(8,128)(2,1)S(1)}, u32[]{:S(2)}, u32[]{:S(2)}) collective-permute-start(bf16[672,128]{1,0:T(8,128)(2,1)S(1)} %get-tuple-element.50), channel_id=1, source_target_pairs={{0,2},{1,3},{2,0},{3,1},{4,6},{5,7},{6,4},{7,5},{8,10},{9,11},{10,... | collective-permute-start | bytes 516104 | tf_op jit(solution)/shard_map/ppermute | solution.py:749
  30.0 10.0 %collective-permute-start.4 = (bf16[672,128]{1,0:T(8,128)(2,1)S(1)}, bf16[672,128]{1,0:T(8,128)(2,1)S(1)}, u32[]{:S(2)}, u32[]{:S(2)}) collective-permute-start(bf16[672,128]{1,0:T(8,128)(2,1)S(1)} %get-tuple-element.52), channel_id=1, source_target_pairs={{0,4},{1,5},{2,6},{3,7},{4,0},{5,1},{6,2},{7,3},{8,12},{9,13},{10,... | collective-permute-start | bytes 516104 | tf_op jit(solution)/shard_map/ppermute | solution.py:749
  35.0 8.6 %collective-permute-start.5 = (bf16[672,128]{1,0:T(8,128)(2,1)S(1)}, bf16[672,128]{1,0:T(8,128)(2,1)S(1)}, u32[]{:S(2)}, u32[]{:S(2)}) collective-permute-start(bf16[672,128]{1,0:T(8,128)(2,1)S(1)} %get-tuple-element.53), channel_id=1, source_target_pairs={{0,5},{1,4},{2,7},{3,6},{4,1},{5,0},{6,3},{7,2},{8,13},{9,12},{10,... | collective-permute-start | bytes 516104 | tf_op jit(solution)/shard_map/ppermute | solution.py:749
  36.9 11.8 %collective-permute-start.6 = (bf16[672,128]{1,0:T(8,128)(2,1)S(1)}, bf16[672,128]{1,0:T(8,128)(2,1)S(1)}, u32[]{:S(2)}, u32[]{:S(2)}) collective-permute-start(bf16[672,128]{1,0:T(8,128)(2,1)S(1)} %get-tuple-element.54), channel_id=1, source_target_pairs={{0,6},{1,7},{2,4},{3,5},{4,2},{5,3},{6,0},{7,1},{8,14},{9,15},{10,... | collective-permute-start | bytes 516104 | tf_op jit(solution)/shard_map/ppermute | solution.py:749
  36.9 23.9 %collective-permute-start.7 = (bf16[672,128]{1,0:T(8,128)(2,1)S(1)}, bf16[672,128]{1,0:T(8,128)(2,1)S(1)}, u32[]{:S(2)}, u32[]{:S(2)}) collective-permute-start(bf16[672,128]{1,0:T(8,128)(2,1)S(1)} %get-tuple-element.55), channel_id=1, source_target_pairs={{0,7},{1,6},{2,5},{3,4},{4,3},{5,2},{6,1},{7,0},{8,15},{9,14},{10,... | collective-permute-start | bytes 516104 | tf_op jit(solution)/shard_map/ppermute | solution.py:749
  39.5 28.2 %collective-permute-start.3 = (bf16[672,128]{1,0:T(8,128)(2,1)S(1)}, bf16[672,128]{1,0:T(8,128)(2,1)S(1)}, u32[]{:S(2)}, u32[]{:S(2)}) collective-permute-start(bf16[672,128]{1,0:T(8,128)(2,1)S(1)} %get-tuple-element.51), channel_id=1, source_target_pairs={{0,3},{1,2},{2,1},{3,0},{4,7},{5,6},{6,5},{7,4},{8,11},{9,10},{10,... | collective-permute-start | bytes 516104 | tf_op jit(solution)/shard_map/ppermute | solution.py:749
  40.0 30.1 %collective-permute-start.11 = (bf16[528,128]{1,0:T(8,128)(2,1)S(1)}, bf16[528,128]{1,0:T(8,128)(2,1)S(1)}, u32[]{:S(2)}, u32[]{:S(2)}) collective-permute-start(bf16[528,128]{1,0:T(8,128)(2,1)S(1)} %get-tuple-element.59), channel_id=1, source_target_pairs={{0,12},{1,13},{2,14},{3,15},{4,8},{5,9},{6,10},{7,11},{8,4},{9,5},... | collective-permute-start | bytes 405512 | tf_op jit(solution)/shard_map/ppermute | solution.py:749
  43.7 26.5 %collective-permute-start.12 = (bf16[528,128]{1,0:T(8,128)(2,1)S(1)}, bf16[528,128]{1,0:T(8,128)(2,1)S(1)}, u32[]{:S(2)}, u32[]{:S(2)}) collective-permute-start(bf16[528,128]{1,0:T(8,128)(2,1)S(1)} %get-tuple-element.60), channel_id=1, source_target_pairs={{0,13},{1,12},{2,15},{3,14},{4,9},{5,8},{6,11},{7,10},{8,5},{9,4},... | collective-permute-start | bytes 405512 | tf_op jit(solution)/shard_map/ppermute | solution.py:749
  48.7 21.5 %collective-permute-start.13 = (bf16[528,128]{1,0:T(8,128)(2,1)S(1)}, bf16[528,128]{1,0:T(8,128)(2,1)S(1)}, u32[]{:S(2)}, u32[]{:S(2)}) collective-permute-start(bf16[528,128]{1,0:T(8,128)(2,1)S(1)} %get-tuple-element.61), channel_id=1, source_target_pairs={{0,14},{1,15},{2,12},{3,13},{4,10},{5,11},{6,8},{7,9},{8,6},{9,7},... | collective-permute-start | bytes 405512 | tf_op jit(solution)/shard_map/ppermute | solution.py:749
  60.8 9.4 %collective-permute-start.14 = (bf16[528,128]{1,0:T(8,128)(2,1)S(1)}, bf16[528,128]{1,0:T(8,128)(2,1)S(1)}, u32[]{:S(2)}, u32[]{:S(2)}) collective-permute-start(bf16[528,128]{1,0:T(8,128)(2,1)S(1)} %get-tuple-element.62), channel_id=1, source_target_pairs={{0,15},{1,14},{2,13},{3,12},{4,11},{5,10},{6,9},{7,8},{8,7},{9,6},... | collective-permute-start | bytes 405512 | tf_op jit(solution)/shard_map/ppermute | solution.py:749
  73.4 13.5 %all-to-all-start = ((f32[16,16,128]{2,1,0:T(8,128)}), f32[16,16,128]{2,1,0:T(8,128)S(1)}, u32[]{:S(2)}, u32[]{:S(2)}) async-start(f32[16,16,128]{2,1,0:T(8,128)} %gram_pieces.1), calls=%async_computation | async-start | bytes 262144 | tf_op jit(solution)/shard_map/all_to_all | solution.py:753
  78.5 22.7 %collective-permute-start.19 = (bf16[8,144,128]{2,1,0:T(8,128)(2,1)S(1)}, bf16[8,144,128]{2,1,0:T(8,128)(2,1)S(1)}, u32[]{:S(2)}, u32[]{:S(2)}) collective-permute-start(bf16[8,144,128]{2,1,0:T(8,128)(2,1)S(1)} %raw_states.1), channel_id=1, source_target_pairs={{0,8},{1,9},{2,10},{3,11},{4,12},{5,13},{6,14},{7,15},{8,0},{9,1},... | collective-permute-start | bytes 884744 | tf_op jit(solution)/shard_map/ppermute | solution.py:749
  91.4 30.2 %copy-start.3 = (bf16[384,128]{1,0:T(8,128)(2,1)S(1)}, bf16[384,128]{1,0:T(8,128)(2,1)}, u32[]{:S(2)}) copy-start(bf16[384,128]{1,0:T(8,128)(2,1)} %get-tuple-element.82) | copy-start | bytes 294916
  91.4 45.1 %copy-start.2 = (bf16[384,128]{1,0:T(8,128)(2,1)S(1)}, bf16[384,128]{1,0:T(8,128)(2,1)}, u32[]{:S(2)}) copy-start(bf16[384,128]{1,0:T(8,128)(2,1)} %get-tuple-element.87) | copy-start | bytes 294916
  91.4 48.8 %copy-start.1 = (bf16[384,128]{1,0:T(8,128)(2,1)S(1)}, bf16[384,128]{1,0:T(8,128)(2,1)}, u32[]{:S(2)}) copy-start(bf16[384,128]{1,0:T(8,128)(2,1)} %get-tuple-element.88) | copy-start | bytes 294916
  91.4 20.6 %collective-permute-start.15 = (bf16[384,128]{1,0:T(8,128)(2,1)}, bf16[384,128]{1,0:T(8,128)(2,1)S(1)}, u32[]{:S(2)}, u32[]{:S(2)}) collective-permute-start(bf16[384,128]{1,0:T(8,128)(2,1)} %get-tuple-element.70), channel_id=1, source_target_pairs={{0,8},{1,9},{2,10},{3,11},{4,12},{5,13},{6,14},{7,15},{8,0},{9,1},... | collective-permute-start | bytes 294920 | tf_op jit(solution)/shard_map/ppermute | solution.py:749
  97.9 16.3 %collective-permute-start.16 = (bf16[384,128]{1,0:T(8,128)(2,1)}, bf16[384,128]{1,0:T(8,128)(2,1)S(1)}, u32[]{:S(2)}, u32[]{:S(2)}) collective-permute-start(bf16[384,128]{1,0:T(8,128)(2,1)} %get-tuple-element.71), channel_id=1, source_target_pairs={{0,9},{1,8},{2,11},{3,10},{4,13},{5,12},{6,15},{7,14},{8,1},{9,0},... | collective-permute-start | bytes 294920 | tf_op jit(solution)/shard_map/ppermute | solution.py:749
  97.9 23.7 %collective-permute-start.17 = (bf16[384,128]{1,0:T(8,128)(2,1)}, bf16[384,128]{1,0:T(8,128)(2,1)S(1)}, u32[]{:S(2)}, u32[]{:S(2)}) collective-permute-start(bf16[384,128]{1,0:T(8,128)(2,1)} %get-tuple-element.72), channel_id=1, source_target_pairs={{0,10},{1,11},{2,8},{3,9},{4,14},{5,15},{6,12},{7,13},{8,2},{9,3},... | collective-permute-start | bytes 294920 | tf_op jit(solution)/shard_map/ppermute | solution.py:749
  99.6 24.9 %collective-permute-start.18 = (bf16[384,128]{1,0:T(8,128)(2,1)}, bf16[384,128]{1,0:T(8,128)(2,1)S(1)}, u32[]{:S(2)}, u32[]{:S(2)}) collective-permute-start(bf16[384,128]{1,0:T(8,128)(2,1)} %get-tuple-element.73), channel_id=1, source_target_pairs={{0,11},{1,10},{2,9},{3,8},{4,15},{5,14},{6,13},{7,12},{8,3},{9,2},... | collective-permute-start | bytes 294920 | tf_op jit(solution)/shard_map/ppermute | solution.py:749
  101.2 23.3 %collective-permute-start.24 = (bf16[384,128]{1,0:T(8,128)(2,1)}, bf16[384,128]{1,0:T(8,128)(2,1)S(1)}, u32[]{:S(2)}, u32[]{:S(2)}) collective-permute-start(bf16[384,128]{1,0:T(8,128)(2,1)} %get-tuple-element.81), channel_id=1, source_target_pairs={{0,12},{1,13},{2,14},{3,15},{4,8},{5,9},{6,10},{7,11},{8,4},{9,5},... | collective-permute-start | bytes 294920 | tf_op jit(solution)/shard_map/ppermute | solution.py:749
  120.1 13.4 %collective-permute-start.20 = (bf16[640,128]{1,0:T(8,128)(2,1)}, bf16[640,128]{1,0:T(8,128)(2,1)S(1)}, u32[]{:S(2)}, u32[]{:S(2)}) collective-permute-start(bf16[640,128]{1,0:T(8,128)(2,1)} %get-tuple-element.77), channel_id=1, source_target_pairs={{0,4},{1,5},{2,6},{3,7},{4,0},{5,1},{6,2},{7,3},{8,12},{9,13},{10,... | collective-permute-start | bytes 491528 | tf_op jit(solution)/shard_map/ppermute | solution.py:749
  120.2 13.9 %collective-permute-start.21 = (bf16[640,128]{1,0:T(8,128)(2,1)}, bf16[640,128]{1,0:T(8,128)(2,1)S(1)}, u32[]{:S(2)}, u32[]{:S(2)}) collective-permute-start(bf16[640,128]{1,0:T(8,128)(2,1)} %get-tuple-element.78), channel_id=1, source_target_pairs={{0,5},{1,4},{2,7},{3,6},{4,1},{5,0},{6,3},{7,2},{8,13},{9,12},{10,... | collective-permute-start | bytes 491528 | tf_op jit(solution)/shard_map/ppermute | solution.py:749
  121.5 10.8 %collective-permute-start.25 = (bf16[384,128]{1,0:T(8,128)(2,1)S(1)}, bf16[384,128]{1,0:T(8,128)(2,1)S(1)}, u32[]{:S(2)}, u32[]{:S(2)}) collective-permute-start(bf16[384,128]{1,0:T(8,128)(2,1)S(1)} %copy-done.3), channel_id=1, source_target_pairs={{0,13},{1,12},{2,15},{3,14},{4,9},{5,8},{6,11},{7,10},{8,5},{9,4},... | collective-permute-start | bytes 294920 | tf_op jit(solution)/shard_map/ppermute | solution.py:749
  124.5 11.9 %collective-permute-start.22 = (bf16[640,128]{1,0:T(8,128)(2,1)}, bf16[640,128]{1,0:T(8,128)(2,1)S(1)}, u32[]{:S(2)}, u32[]{:S(2)}) collective-permute-start(bf16[640,128]{1,0:T(8,128)(2,1)} %get-tuple-element.79), channel_id=1, source_target_pairs={{0,6},{1,7},{2,4},{3,5},{4,2},{5,3},{6,0},{7,1},{8,14},{9,15},{10,... | collective-permute-start | bytes 491528 | tf_op jit(solution)/shard_map/ppermute | solution.py:749
  124.6 15.6 %collective-permute-start.23 = (bf16[640,128]{1,0:T(8,128)(2,1)}, bf16[640,128]{1,0:T(8,128)(2,1)S(1)}, u32[]{:S(2)}, u32[]{:S(2)}) collective-permute-start(bf16[640,128]{1,0:T(8,128)(2,1)} %get-tuple-element.80), channel_id=1, source_target_pairs={{0,7},{1,6},{2,5},{3,4},{4,3},{5,2},{6,1},{7,0},{8,15},{9,14},{10,... | collective-permute-start | bytes 491528 | tf_op jit(solution)/shard_map/ppermute | solution.py:749
  132.4 12.7 %collective-permute-start.26 = (bf16[640,128]{1,0:T(8,128)(2,1)}, bf16[640,128]{1,0:T(8,128)(2,1)S(1)}, u32[]{:S(2)}, u32[]{:S(2)}) collective-permute-start(bf16[640,128]{1,0:T(8,128)(2,1)} %get-tuple-element.84), channel_id=1, source_target_pairs={{0,1},{1,0},{2,3},{3,2},{4,5},{5,4},{6,7},{7,6},{8,9},{9,8},{10,11... | collective-permute-start | bytes 491528 | tf_op jit(solution)/shard_map/ppermute | solution.py:749
  133.4 11.7 %collective-permute-start.27 = (bf16[640,128]{1,0:T(8,128)(2,1)}, bf16[640,128]{1,0:T(8,128)(2,1)S(1)}, u32[]{:S(2)}, u32[]{:S(2)}) collective-permute-start(bf16[640,128]{1,0:T(8,128)(2,1)} %get-tuple-element.85), channel_id=1, source_target_pairs={{0,2},{1,3},{2,0},{3,1},{4,6},{5,7},{6,4},{7,5},{8,10},{9,11},{10,... | collective-permute-start | bytes 491528 | tf_op jit(solution)/shard_map/ppermute | solution.py:749
  134.1 15.8 %collective-permute-start.28 = (bf16[640,128]{1,0:T(8,128)(2,1)}, bf16[640,128]{1,0:T(8,128)(2,1)S(1)}, u32[]{:S(2)}, u32[]{:S(2)}) collective-permute-start(bf16[640,128]{1,0:T(8,128)(2,1)} %get-tuple-element.86), channel_id=1, source_target_pairs={{0,3},{1,2},{2,1},{3,0},{4,7},{5,6},{6,5},{7,4},{8,11},{9,10},{10,... | collective-permute-start | bytes 491528 | tf_op jit(solution)/shard_map/ppermute | solution.py:749
  136.5 14.6 %collective-permute-start.29 = (bf16[384,128]{1,0:T(8,128)(2,1)S(1)}, bf16[384,128]{1,0:T(8,128)(2,1)S(1)}, u32[]{:S(2)}, u32[]{:S(2)}) collective-permute-start(bf16[384,128]{1,0:T(8,128)(2,1)S(1)} %copy-done.2), channel_id=1, source_target_pairs={{0,14},{1,15},{2,12},{3,13},{4,10},{5,11},{6,8},{7,9},{8,6},{9,7},... | collective-permute-start | bytes 294920 | tf_op jit(solution)/shard_map/ppermute | solution.py:749
  140.2 10.8 %collective-permute-start.30 = (bf16[384,128]{1,0:T(8,128)(2,1)S(1)}, bf16[384,128]{1,0:T(8,128)(2,1)S(1)}, u32[]{:S(2)}, u32[]{:S(2)}) collective-permute-start(bf16[384,128]{1,0:T(8,128)(2,1)S(1)} %copy-done.1), channel_id=1, source_target_pairs={{0,15},{1,14},{2,13},{3,12},{4,11},{5,10},{6,9},{7,8},{8,7},{9,6},... | collective-permute-start | bytes 294920 | tf_op jit(solution)/shard_map/ppermute | solution.py:749
  144.3 5.6 %copy-start = (bf16[640,128]{1,0:T(8,128)(2,1)S(1)}, bf16[640,128]{1,0:T(8,128)(2,1)}, u32[]{:S(2)}) copy-start(bf16[640,128]{1,0:T(8,128)(2,1)} %get-tuple-element.83.refs_1_) | copy-start | bytes 491524

commit v12 on v9

--- a/solution.py
+++ b/solution.py
@@ -20,6 +20,9 @@
 F32 = jnp.float32
 BF16 = jnp.bfloat16
 MIB = 1024 * 1024
+
+
+LATE = 400 * 1000 * 1000
 
 
 def call(body, name, flops=0, moved=0, limit=16, **kwargs):
@@ -374,14 +377,16 @@
     return pl.ds(pl.multiple_of(start, TILE), count)
 
 
-def split_pieces_body(slabs, lines, fields, row_ref, *refs):
-    half = slabs // 2
-    field_refs, near_out, far_outs = refs[:fields], refs[fields], refs[fields + 1 : fields + 1 + half]
-    slab_refs, helds, sems = refs[fields + 1 + half : -slabs - 1], refs[-slabs - 1 : -1], refs[-1]
+def split_pieces_body(positions, half, lines, fields, row_ref, *refs):
+    slabs = 2 * half
+    count = len(positions)
+    field_refs, out_refs = refs[:fields], refs[fields : -count - 1]
+    helds, sems = refs[-count - 1 : -1], refs[-1]
+    slab_refs = out_refs[len(out_refs) - fields :]
     cells = lines * LANES
     end = row_ref.shape[1]
     copies = []
-    for at, held in enumerate(helds):
+    for at, held in zip(positions, helds):
         slab = device_at(at, half)
         parts = (
             (slab * cells, cells, 0),
@@ -390,16 +395,16 @@
         )
         for n, (start, size, to) in enumerate(parts):
             source = row_ref.at[:, pl.ds(pl.multiple_of(start, GRID_Y), size)]
-            copies.append(pltpu.make_async_copy(source, held.at[:, pl.ds(to, size)], sems.at[3 * at + n]))
+            copies.append(pltpu.make_async_copy(source, held.at[:, pl.ds(to, size)], sems.at[len(copies)]))
             copies[-1].start()
     start = lax.axis_index("slab").astype(jnp.int32) * lines
-    for n, (field_ref, slab_ref) in enumerate(zip(field_refs, slab_refs)):
-        copies.append(pltpu.make_async_copy(field_ref.at[lines_of(start, lines), :], slab_ref, sems.at[3 * slabs + n]))
+    for field_ref, slab_ref in zip(field_refs, slab_refs):
+        copies.append(pltpu.make_async_copy(field_ref.at[lines_of(start, lines), :], slab_ref, sems.at[len(copies)]))
         copies[-1].start()
 
-    for at, held in enumerate(helds):
-        out_ref = near_out.at[at] if at < half else far_outs[at - half]
-        for copy in copies[3 * at : 3 * at + 3]:
+    for n, (at, held) in enumerate(zip(positions, helds)):
+        out_ref = out_refs[0].at[n] if at < half else out_refs[n]
+        for copy in copies[3 * n : 3 * n + 3]:
             copy.wait()
         slab = device_at(at, half)
         out_ref[:lines, :] = held[:, :cells].reshape(lines, LANES)
@@ -408,26 +413,27 @@
         below = jnp.where(slab == slabs - 1, 0.0, below)
         above = jnp.where(slab == 0, 0.0, above)
         out_ref[lines:, :] = jnp.concatenate([below, above], axis=0).astype(BF16)
-    for copy in copies[3 * slabs :]:
+    for copy in copies[3 * count :]:
         copy.wait()
 
 
-def split_pieces(row, slabs, fields):
+def split_pieces(row, slabs, near, fields):
     lines = row.shape[1] // slabs // LANES
     half = slabs // 2
     rim = lines + TILE
-    out_shape = [jax.ShapeDtypeStruct((half, rim, LANES), BF16)]
-    out_shape += [jax.ShapeDtypeStruct((rim, LANES), BF16)] * half
+    out_shape = [jax.ShapeDtypeStruct((half, rim, LANES), BF16)] if near else []
+    out_shape += [] if near else [jax.ShapeDtypeStruct((rim, LANES), BF16)] * half
     out_shape += [jax.ShapeDtypeStruct((lines, LANES), BF16)] * len(fields)
-    return call(
-        functools.partial(split_pieces_body, slabs, lines, len(fields)),
+    positions = range(half) if near else range(half, slabs)
+    return call(
+        functools.partial(split_pieces_body, positions, half, lines, len(fields)),
         "split_pieces",
-        moved=6 * slabs * rim * LANES,
+        moved=6 * half * rim * LANES,
         in_specs=[IN_HBM] * (1 + len(fields)),
         out_specs=[IN_VMEM] * len(out_shape),
         out_shape=out_shape,
-        scratch_shapes=[pltpu.VMEM((1, rim * LANES), BF16)] * slabs
-        + [pltpu.SemaphoreType.DMA((3 * slabs + len(fields),))],
+        scratch_shapes=[pltpu.VMEM((1, rim * LANES), BF16)] * half
+        + [pltpu.SemaphoreType.DMA((3 * half + len(fields),))],
     )(row, *fields)
 
 
@@ -446,13 +452,13 @@
         copy.wait()
 
 
-def join_pieces(row, slabs, arrays, pieces):
+def join_pieces(row, slabs, arrays, pieces, late=0):
     sizes = [arrays[piece[0]].shape[-2] * LANES for piece in pieces]
     begun = [] if row is None else [row]
     return call(
         functools.partial(join_pieces_body, pieces, slabs // 2, NCELL // slabs // LANES, len(begun), len(arrays)),
         "join_pieces",
-        moved=6 * sum(sizes),
+        moved=6 * sum(sizes) + late,
         in_specs=[IN_HBM] * len(begun) + [IN_VMEM] * len(arrays),
         out_specs=IN_HBM,
         out_shape=jax.ShapeDtypeStruct((1, NCELL), BF16),
@@ -565,7 +571,7 @@
     lax.fori_loop(0, steps, finish, 0)
 
 
-def gradient_pieces(arrays, views, observed, precision, numbers):
+def gradient_pieces(arrays, views, observed, precision, numbers, gates, late=0):
     count = observed.shape[0]
     out = pltpu.HBM((len(views), count, LANES), BF16)
     size = len(views) * count * LANES
@@ -573,13 +579,14 @@
         functools.partial(gradient_pieces_body, views, len(arrays), len(numbers)),
         "gradient_pieces",
         flops=30 * size,
-        moved=8 * size,
+        moved=8 * size + late,
         in_specs=[IN_VMEM] * (len(arrays) + 2)
-        + [pl.BlockSpec(memory_space=pltpu.SMEM)] * len(numbers),
+        + [pl.BlockSpec(memory_space=pltpu.SMEM)] * len(numbers)
+        + [IN_VMEM] * len(gates),
         out_specs=[IN_HBM, IN_VMEM],
         out_shape=[out, jax.ShapeDtypeStruct((8, LANES), F32)],
         scratch_shapes=[pltpu.VMEM(out.shape, BF16), pltpu.SemaphoreType.DMA((count // BLOCK,))],
-    )(*arrays, observed, precision, *numbers)
+    )(*arrays, observed, precision, *numbers, *gates)
 
 
 def mix(mixer, own, numbers_ref, total, states, slopes):
@@ -672,7 +679,7 @@
     return lax.all_to_all(pieces, "slab", 0, 0, axis_index_groups=groups, tiled=True)
 
 
-GRADIENTS = ((8, 9, 10, 11), (12, 13, 14, 15), (0, 1, 2, 3, 4, 5, 6, 7))
+GRADIENTS = ((8,), (9, 10, 11), (0, 1, 2, 3, 4, 5, 6, 7), (12, 13, 14, 15))
 
 
 def by_halves(particles, observed, precision, spread, anneal, step_size):
@@ -681,29 +688,31 @@
     lines = NCELL // slabs // LANES
     row = in_hbm(particles)
     fields = [in_hbm(field.reshape(-1, LANES)) for field in (observed, precision)]
-    near, *far = split_pieces(row, slabs, fields)
-    far, (obs, prec) = far[:half], far[half:]
-    near = swap_near(near, slabs)
+    *far, obs, prec = split_pieces(row, slabs, False, fields)
     far = [exchange(piece, half + x, slabs) for x, piece in enumerate(far)]
+    near = swap_near(split_pieces(row, slabs, True, [])[0], slabs)
     grads = []
     numbers = [spread, anneal, step_size]
-    for group in GRADIENTS:
+    for n, group in enumerate(GRADIENTS):
         if group[0] < half:
             arrays, views = [near], [(0, k, 0) for k in group]
         else:
             arrays, views = [far[k - half] for k in group], [(j, None, 0) for j in range(len(group))]
-        slopes, rows = gradient_pieces(arrays, tuple(views), obs, prec, [] if grads else numbers)
+        gates = [numbers] if n else []
+        given = [] if n else numbers
+        slopes, rows = gradient_pieces(arrays, tuple(views), obs, prec, given, gates, 0 if n else LATE)
         grads.append(in_hbm(slopes))
-        numbers = numbers if len(grads) > 1 else rows
-    grams = swap(gram_pieces(near, far, lines, grads[:1]))
+        numbers = numbers if n else rows
+    grams = swap(gram_pieces(near, far, lines, grads[:2]))
     new_near, *new_far = update_pieces(numbers, grams, near, far, grads, GRADIENTS, lines)
     new_near = swap_near(new_near, slabs)
     new_far = [exchange(piece, half + x, slabs) for x, piece in enumerate(new_far)]
-    row = join_pieces(None, slabs, [new_near], [(0, k, k) for k in range(half)])
-    for group in ((0, 1, 2, 3), (4, 5)):
+    row = join_pieces(None, slabs, new_far[:1], [(0, None, half)], LATE)
+    row = join_pieces(row, slabs, [new_near], [(0, k, k) for k in range(half)])
+    for group in ((1, 2, 3), (4, 5), (6, 7)):
         pieces = [(n, None, half + x) for n, x in enumerate(group)]
         row = join_pieces(row, slabs, [new_far[x] for x in group], pieces)
-    return join_pieces(row, slabs, new_far[6:], [(n, None, half + 6 + n) for n in range(half - 6)])
+    return row
 
 
 def on_device(particles, observed, precision, spread, anneal, step_size):

time: 133 us -> 134 us (level)
  Pallas kernels: 25.1 us -> 28.5 us
  waiting for transfers between devices: 70.3 us -> 68 us
    ppermute x16, waiting for transfers between devices: 70 us -> 67.6 us  [exchange(): return lax.ppermute(piece, 'slab', [(i, i ^ k) for i in range(slabs)])]
    pallas_call x3 -> x4, Pallas kernels: 7.33 us -> 9.18 us  [gradient_pieces(): call(functools.partial(gradient_pieces_body, views, len(arrays), len(numb...]
    pallas_call x1 -> x2, Pallas kernels: 3.83 us -> 4.77 us  [split_pieces(): call(functools.partial(split_pieces_body, positions, half, lines, len(fie...]
    pallas_call x4 -> x5, Pallas kernels: 5.16 us -> 5.81 us  [join_pieces(): call(functools.partial(join_pieces_body, pieces, slabs // 2, NCELL // sla...]
  transfers between devices with their start and end apart: 19 -> 19, of which waited for: 16 -> 15; matrix products, arithmetic and copies ran while one was open for 0% -> 0% of each run, Pallas kernels for 9% -> 12%
where the time goes in v12:
time: 134 us
  waiting for transfers between devices  68 us (51%)
  starting transfers between devices  35.3 us (26%)
  Pallas kernels  28.5 us (21%)
  between operations  2.08 us (2%)
    ppermute x16, waiting for transfers between devices, exchange(): return lax.ppermute(piece, 'slab', [(i, i ^ k) for i in range(slabs)])  67.6 us
    ppermute x16, starting transfers between devices, exchange(): return lax.ppermute(piece, 'slab', [(i, i ^ k) for i in range(slabs)])  20.2 us
    all_to_all x2, starting transfers between devices, swap_near(): lax.all_to_all(pieces, 'slab', 0, 0, axis_index_groups=groups, tiled=True)  10.2 us
    pallas_call x4, Pallas kernels, gradient_pieces(): call(functools.partial(gradient_pieces_body, views, len(arrays), len(numb...  9.18 us
    pallas_call x5, Pallas kernels, join_pieces(): call(functools.partial(join_pieces_body, pieces, slabs // 2, NCELL // sla...  5.81 us
    pallas_call x1, Pallas kernels, update_pieces(): call(functools.partial(update_pieces_body, half, lines, groups), 'update_...  5.34 us
    all_to_all x1, starting transfers between devices, swap(): lax.all_to_all(slabs, 'slab', split_axis=0, concat_axis=0, tiled=True)  4.84 us
    pallas_call x2, Pallas kernels, split_pieces(): call(functools.partial(split_pieces_body, positions, half, lines, len(fie...  4.77 us
  transfers between devices with their start and end apart: 19, of which 15 were waited for; matrix products, arithmetic and copies ran while one was open for 0% of the time, Pallas kernels for 12%

profile of v12, /device:TPU:9, one launch (start us, length us, event | category | flops | bytes accessed | tf_op | source)
XLA Modules:
  0.0 133.9 jit_solution(3266767540747670845)
XLA Ops:
  0.0 2.8 %split_pieces.2 = bf16[8,528,128]{2,1,0:T(8,128)(2,1)} custom-call(bf16[1,1048576]{1,0:T(2,128)(2,1)} %row_ref.3), custom_call_target="tpu_custom_call" | custom-call | bytes 3244032 | tf_op jit(solution)/shard_map/split_pieces/pallas_call | solution.py:428
  2.8 4.6 %all-to-all-start = ((bf16[8,528,128]{2,1,0:T(8,128)(2,1)}), bf16[8,528,128]{2,1,0:T(8,128)(2,1)S(1)}, u32[]{:S(2)}, u32[]{:S(2)}) async-start(bf16[8,528,128]{2,1,0:T(8,128)(2,1)} %split_pieces.2), calls=%async_computation | async-start | bytes 2162688 | tf_op jit(solution)/shard_map/all_to_all | solution.py:679
  7.4 1.9 %split_pieces.3 = (bf16[528,128]{1,0:T(8,128)(2,1)S(1)}, bf16[528,128]{1,0:T(8,128)(2,1)S(1)}, bf16[528,128]{1,0:T(8,128)(2,1)S(1)}, bf16[528,128]{1,0:T(8,128)(...) custom-call(bf16[1,1048576]{1,0:T(2,128)(2,1)} %row_ref.3, ...), custom_call_target="tpu_custom_call" | custom-call | bytes 3244032 | tf_op jit(solution)/shard_map/split_pieces/pallas_call | solution.py:428
  9.4 2.4 %collective-permute-start = (bf16[528,128]{1,0:T(8,128)(2,1)S(1)}, bf16[528,128]{1,0:T(8,128)(2,1)S(1)}, u32[]{:S(2)}, u32[]{:S(2)}) collective-permute-start(bf16[528,128]{1,0:T(8,128)(2,1)S(1)} %get-tuple-element.29), channel_id=1, source_target_pairs={{0,8},{1,9},{2,10},{3,11},{4,12},{5,13},{6,14},{7,15},{8,0},{9,1},... | collective-permute-start | bytes 405512 | tf_op jit(solution)/shard_map/ppermute | solution.py:674
  11.7 0.6 collective-permute-start.1
  12.3 3.2 %collective-permute-start.2 = (bf16[528,128]{1,0:T(8,128)(2,1)S(1)}, bf16[528,128]{1,0:T(8,128)(2,1)S(1)}, u32[]{:S(2)}, u32[]{:S(2)}) collective-permute-start(bf16[528,128]{1,0:T(8,128)(2,1)S(1)} %get-tuple-element.31), channel_id=1, source_target_pairs={{0,10},{1,11},{2,8},{3,9},{4,14},{5,15},{6,12},{7,13},{8,2},{9,3},... | collective-permute-start | bytes 405512 | tf_op jit(solution)/shard_map/ppermute | solution.py:674
  15.5 0.3 collective-permute-start.3
  15.8 1.0 collective-permute-start.4
  16.8 8.4 %collective-permute-done.refs_0_ = bf16[528,128]{1,0:T(8,128)(2,1)S(1)} collective-permute-done((bf16[528,128]{1,0:T(8,128)(2,1)S(1)}, bf16[528,128]{1,0:T(8,128)(2,1)S(1)}, u32[]{:S(2)}, u32[]{:S(2)}) %collective-permute-start) | collective-permute-done | bytes 135200 | tf_op jit(solution)/shard_map/ppermute | solution.py:674
  25.2 0.0 collective-permute-start.5
  25.2 3.6 %collective-permute-done.1.refs_0_.refs_1_ = bf16[528,128]{1,0:T(8,128)(2,1)S(1)} collective-permute-done((bf16[528,128]{1,0:T(8,128)(2,1)S(1)}, bf16[528,128]{1,0:T(8,128)(2,1)S(1)}, u32[]{:S(2)}, u32[]{:S(2)}) %collective-permute-start.1) | collective-permute-done | bytes 135200 | tf_op jit(solution)/shard_map/ppermute | solution.py:674
  28.8 0.3 collective-permute-start.6
  29.1 11.2 %collective-permute-done.2.refs_1_.refs_2_ = bf16[528,128]{1,0:T(8,128)(2,1)S(1)} collective-permute-done((bf16[528,128]{1,0:T(8,128)(2,1)S(1)}, bf16[528,128]{1,0:T(8,128)(2,1)S(1)}, u32[]{:S(2)}, u32[]{:S(2)}) %collective-permute-start.2) | collective-permute-done | bytes 135200 | tf_op jit(solution)/shard_map/ppermute | solution.py:674
  42.3 1.4 %gradient_pieces.4 = (bf16[1,512,128]{2,1,0:T(8,128)(2,1)}, f32[8,128]{1,0:T(8,128)S(1)}) custom-call(bf16[528,128]{1,0:T(8,128)(2,1)S(1)} %collective-permute-done.refs_0_, bf16[512,128]{1,0:T(8,128)(2,1)S(1)} %get-tuple-element.37.refs_1_.refs_3_.refs_4_, bf16[512,128]{1,0:T(8,128)(2,1)S(1)} %get-tuple-element.38.refs_2_.refs_4_.refs_5_, ...), custom_call_target="tpu_custom_call" | custom-call | flops 1966080 | bytes 400524288 | tf_op jit(solution)/shard_map/gradient_pieces/pallas_call | solution.py:578
  43.7 2.3 %gradient_pieces.5 = (bf16[3,512,128]{2,1,0:T(8,128)(2,1)}, f32[8,128]{1,0:T(8,128)}) custom-call(bf16[528,128]{1,0:T(8,128)(2,1)S(1)} %collective-permute-done.1.refs_0_.refs_1_, bf16[528,128]{1,0:T(8,128)(2,1)S(1)} %collective-permute-done.2.refs_1_.refs_2_, bf16[528,128]{1,0:T(8,128)(2,1)S(1)} %collective-permute-done.3.refs_2_.refs_3_, ...), custom_call_target="tpu_custom_call" | custom-call | flops 5898240 | bytes 1572864 | tf_op jit(solution)/shard_map/gradient_pieces/pallas_call | solution.py:578
  46.0 1.8 %collective-permute-done.4.refs_4_.refs_0_ = bf16[528,128]{1,0:T(8,128)(2,1)S(1)} collective-permute-done((bf16[528,128]{1,0:T(8,128)(2,1)S(1)}, bf16[528,128]{1,0:T(8,128)(2,1)S(1)}, u32[]{:S(2)}, u32[]{:S(2)}) %collective-permute-start.4) | collective-permute-done | bytes 135200 | tf_op jit(solution)/shard_map/ppermute | solution.py:674
  47.8 4.8 %collective-permute-done.5.refs_5_.refs_1_ = bf16[528,128]{1,0:T(8,128)(2,1)S(1)} collective-permute-done((bf16[528,128]{1,0:T(8,128)(2,1)S(1)}, bf16[528,128]{1,0:T(8,128)(2,1)S(1)}, u32[]{:S(2)}, u32[]{:S(2)}) %collective-permute-start.5) | collective-permute-done | bytes 135200 | tf_op jit(solution)/shard_map/ppermute | solution.py:674
  52.6 3.9 %collective-permute-done.6.refs_6_.refs_2_ = bf16[528,128]{1,0:T(8,128)(2,1)S(1)} collective-permute-done((bf16[528,128]{1,0:T(8,128)(2,1)S(1)}, bf16[528,128]{1,0:T(8,128)(2,1)S(1)}, u32[]{:S(2)}, u32[]{:S(2)}) %collective-permute-start.6) | collective-permute-done | bytes 135200 | tf_op jit(solution)/shard_map/ppermute | solution.py:674
  56.5 2.9 %collective-permute-done.7.refs_7_.refs_3_ = bf16[528,128]{1,0:T(8,128)(2,1)S(1)} collective-permute-done((bf16[528,128]{1,0:T(8,128)(2,1)S(1)}, bf16[528,128]{1,0:T(8,128)(2,1)S(1)}, u32[]{:S(2)}, u32[]{:S(2)}) %collective-permute-start.7) | collective-permute-done | bytes 135200 | tf_op jit(solution)/shard_map/ppermute | solution.py:674
  59.4 0.0 all-to-all-done.near_ref.refs_0_
  59.4 3.4 %gram_pieces.1 = f32[16,16,128]{2,1,0:T(8,128)} custom-call(bf16[8,528,128]{2,1,0:T(8,128)(2,1)S(1)} %all-to-all-done.near_ref.refs_0_, bf16[528,128]{1,0:T(8,128)(2,1)S(1)} %collective-permute-done.refs_0_, bf16[528,128]{1,0:T(8,128)(2,1)S(1)} %collective-permute-done.1.refs_0_.refs_1_, bf16[528,128]{1,0:T(8,128)(2,1)S(1)} %collective-permute-done.2.refs_1_.refs_2_, ...), custom_call_target="tpu_custom_call" | custom-call | flops 536870912 | bytes 2097152 | tf_op jit(solution)/shard_map/gram_pieces/pallas_call | solution.py:507
  62.8 4.8 %all-to-all-start.1 = ((f32[16,16,128]{2,1,0:T(8,128)}), f32[16,16,128]{2,1,0:T(8,128)S(1)}, u32[]{:S(2)}, u32[]{:S(2)}) async-start(f32[16,16,128]{2,1,0:T(8,128)} %gram_pieces.1), calls=%async_computation.1 | async-start | bytes 262144 | tf_op jit(solution)/shard_map/all_to_all | solution.py:368
  67.7 2.4 %gradient_pieces.7 = (bf16[4,512,128]{2,1,0:T(8,128)(2,1)}, f32[8,128]{1,0:T(8,128)}) custom-call(bf16[528,128]{1,0:T(8,128)(2,1)S(1)} %collective-permute-done.4.refs_4_.refs_0_, bf16[528,128]{1,0:T(8,128)(2,1)S(1)} %collective-permute-done.5.refs_5_.refs_1_, bf16[528,128]{1,0:T(8,128)(2,1)S(1)} %collective-permute-done.6.refs_6_.refs_2_, ...), custom_call_target="tpu_custom_call" | custom-call | flops 7864320 | bytes 2097152 | tf_op jit(solution)/shard_map/gradient_pieces/pallas_call | solution.py:578
  70.1 3.1 %gradient_pieces.6 = (bf16[8,512,128]{2,1,0:T(8,128)(2,1)}, f32[8,128]{1,0:T(8,128)}) custom-call(bf16[8,528,128]{2,1,0:T(8,128)(2,1)S(1)} %all-to-all-done.near_ref.refs_0_, bf16[512,128]{1,0:T(8,128)(2,1)S(1)} %get-tuple-element.37.refs_1_.refs_3_.refs_4_, bf16[512,128]{1,0:T(8,128)(2,1)S(1)} %get-tuple-element.38.refs_2_.refs_4_.refs_5_, ...), custom_call_target="tpu_custom_call" | custom-call | flops 15728640 | bytes 4194304 | tf_op jit(solution)/shard_map/gradient_pieces/pallas_call | solution.py:578
  73.2 0.4 all-to-all-done.1.refs_9_
  73.6 5.3 %update_pieces.1 = (bf16[8,512,128]{2,1,0:T(8,128)(2,1)}, bf16[512,128]{1,0:T(8,128)(2,1)}, bf16[512,128]{1,0:T(8,128)(2,1)S(1)}, bf16[512,128]{1,0:T(8,128)(2,1...) custom-call(bf16[8,528,128]{2,1,0:T(8,128)(2,1)S(1)} %all-to-all-don, ...), custom_call_target="tpu_custom_call" | custom-call | flops 1073741824 | bytes 6291456 | tf_op jit(solution)/shard_map/update_pieces/pallas_call | solution.py:656
  78.9 5.6 %all-to-all-start.2 = ((bf16[8,512,128]{2,1,0:T(8,128)(2,1)}), bf16[8,512,128]{2,1,0:T(8,128)(2,1)S(1)}, u32[]{:S(2)}, u32[]{:S(2)}) async-start(bf16[8,512,128]{2,1,0:T(8,128)(2,1)} %get-tuple-element.45), calls=%async_computation.2 | async-start | bytes 2097152 | tf_op jit(solution)/shard_map/all_to_all | solution.py:679
  84.5 0.3 collective-permute-start.8
  84.9 2.6 %collective-permute-start.9 = (bf16[512,128]{1,0:T(8,128)(2,1)S(1)}, bf16[512,128]{1,0:T(8,128)(2,1)S(1)}, u32[]{:S(2)}, u32[]{:S(2)}) collective-permute-start(bf16[512,128]{1,0:T(8,128)(2,1)S(1)} %get-tuple-element.46), channel_id=1, source_target_pairs={{0,9},{1,8},{2,11},{3,10},{4,13},{5,12},{6,15},{7,14},{8,1},{9,0},... | collective-permute-start | bytes 393224 | tf_op jit(solution)/shard_map/ppermute | solution.py:674
  87.4 1.2 collective-permute-start.10
  88.7 2.1 %collective-permute-start.11 = (bf16[512,128]{1,0:T(8,128)(2,1)S(1)}, bf16[512,128]{1,0:T(8,128)(2,1)S(1)}, u32[]{:S(2)}, u32[]{:S(2)}) collective-permute-start(bf16[512,128]{1,0:T(8,128)(2,1)S(1)} %get-tuple-element.48), channel_id=1, source_target_pairs={{0,11},{1,10},{2,9},{3,8},{4,15},{5,14},{6,13},{7,12},{8,3},{9,2},... | collective-permute-start | bytes 393224 | tf_op jit(solution)/shard_map/ppermute | solution.py:674
  90.8 0.0 collective-permute-start.12
  90.8 9.2 %collective-permute-done.8.refs_0_ = bf16[512,128]{1,0:T(8,128)(2,1)S(1)} collective-permute-done((bf16[512,128]{1,0:T(8,128)(2,1)}, bf16[512,128]{1,0:T(8,128)(2,1)S(1)}, u32[]{:S(2)}, u32[]{:S(2)}) %collective-permute-start.8) | collective-permute-done | bytes 131104 | tf_op jit(solution)/shard_map/ppermute | solution.py:674
  99.9 2.0 %collective-permute-start.13 = (bf16[512,128]{1,0:T(8,128)(2,1)S(1)}, bf16[512,128]{1,0:T(8,128)(2,1)S(1)}, u32[]{:S(2)}, u32[]{:S(2)}) collective-permute-start(bf16[512,128]{1,0:T(8,128)(2,1)S(1)} %get-tuple-element.50), channel_id=1, source_target_pairs={{0,13},{1,12},{2,15},{3,14},{4,9},{5,8},{6,11},{7,10},{8,5},{9,4},... | collective-permute-start | bytes 393224 | tf_op jit(solution)/shard_map/ppermute | solution.py:674
  101.9 1.5 %collective-permute-done.9.refs_1_ = bf16[512,128]{1,0:T(8,128)(2,1)S(1)} collective-permute-done((bf16[512,128]{1,0:T(8,128)(2,1)S(1)}, bf16[512,128]{1,0:T(8,128)(2,1)S(1)}, u32[]{:S(2)}, u32[]{:S(2)}) %collective-permute-start.9) | collective-permute-done | bytes 131104 | tf_op jit(solution)/shard_map/ppermute | solution.py:674
  103.5 2.3 %collective-permute-start.14 = (bf16[512,128]{1,0:T(8,128)(2,1)S(1)}, bf16[512,128]{1,0:T(8,128)(2,1)S(1)}, u32[]{:S(2)}, u32[]{:S(2)}) collective-permute-start(bf16[512,128]{1,0:T(8,128)(2,1)S(1)} %get-tuple-element.51), channel_id=1, source_target_pairs={{0,14},{1,15},{2,12},{3,13},{4,10},{5,11},{6,8},{7,9},{8,6},{9,7},... | collective-permute-start | bytes 393224 | tf_op jit(solution)/shard_map/ppermute | solution.py:674
  105.7 0.7 collective-permute-done.10.refs_2_
  106.5 2.0 %collective-permute-start.15 = (bf16[512,128]{1,0:T(8,128)(2,1)S(1)}, bf16[512,128]{1,0:T(8,128)(2,1)S(1)}, u32[]{:S(2)}, u32[]{:S(2)}) collective-permute-start(bf16[512,128]{1,0:T(8,128)(2,1)S(1)} %get-tuple-element.52), channel_id=1, source_target_pairs={{0,15},{1,14},{2,13},{3,12},{4,11},{5,10},{6,9},{7,8},{8,7},{9,6},... | collective-permute-start | bytes 393224 | tf_op jit(solution)/shard_map/ppermute | solution.py:674
  108.5 0.7 join_pieces.5.refs_0_
  109.2 2.5 %join_pieces.6.refs_0_ = bf16[1,1048576]{1,0:T(2,128)(2,1)} custom-call(bf16[1,1048576]{1,0:T(2,128)(2,1)} %join_pieces.5.refs_0_, bf16[8,512,128]{2,1,0:T(8,128)(2,1)S(1)} %all-to-all-done.2.refs_1_), custom_call_target="tpu_custom_call", output_to_operand_aliasing={{}: (0, {})} | custom-call | bytes 3145728 | tf_op jit(solution)/shard_map/join_pieces/pallas_call | solution.py:458
  111.7 0.0 collective-permute-done.11.refs_3_
  111.7 0.9 join_pieces.7.refs_0_
  112.6 10.6 %collective-permute-done.12.refs_1_ = bf16[512,128]{1,0:T(8,128)(2,1)S(1)} collective-permute-done((bf16[512,128]{1,0:T(8,128)(2,1)S(1)}, bf16[512,128]{1,0:T(8,128)(2,1)S(1)}, u32[]{:S(2)}, u32[]{:S(2)}) %collective-permute-start.12) | collective-permute-done | bytes 131104 | tf_op jit(solution)/shard_map/ppermute | solution.py:674
  123.2 3.7 %collective-permute-done.13.refs_2_ = bf16[512,128]{1,0:T(8,128)(2,1)S(1)} collective-permute-done((bf16[512,128]{1,0:T(8,128)(2,1)S(1)}, bf16[512,128]{1,0:T(8,128)(2,1)S(1)}, u32[]{:S(2)}, u32[]{:S(2)}) %collective-permute-start.13) | collective-permute-done | bytes 131104 | tf_op jit(solution)/shard_map/ppermute | solution.py:674
  126.9 0.8 join_pieces.8.refs_0_
  127.7 2.0 %collective-permute-done.14.refs_1_ = bf16[512,128]{1,0:T(8,128)(2,1)S(1)} collective-permute-done((bf16[512,128]{1,0:T(8,128)(2,1)S(1)}, bf16[512,128]{1,0:T(8,128)(2,1)S(1)}, u32[]{:S(2)}, u32[]{:S(2)}) %collective-permute-start.14) | collective-permute-done | bytes 131104 | tf_op jit(solution)/shard_map/ppermute | solution.py:674
  129.7 3.3 %collective-permute-done.15.refs_2_ = bf16[512,128]{1,0:T(8,128)(2,1)S(1)} collective-permute-done((bf16[512,128]{1,0:T(8,128)(2,1)S(1)}, bf16[512,128]{1,0:T(8,128)(2,1)S(1)}, u32[]{:S(2)}, u32[]{:S(2)}) %collective-permute-start.15) | collective-permute-done | bytes 131104 | tf_op jit(solution)/shard_map/ppermute | solution.py:674
  133.0 0.8 join_pieces.9
  (3 shorter events, 0.0 us)
Async XLA Ops:
  2.8 56.5 %all-to-all-start = ((bf16[8,528,128]{2,1,0:T(8,128)(2,1)}), bf16[8,528,128]{2,1,0:T(8,128)(2,1)S(1)}, u32[]{:S(2)}, u32[]{:S(2)}) async-start(bf16[8,528,128]{2,1,0:T(8,128)(2,1)} %split_pieces.2), calls=%async_computation | async-start | bytes 2162688 | tf_op jit(solution)/shard_map/all_to_all | solution.py:679
  9.4 15.9 %collective-permute-start = (bf16[528,128]{1,0:T(8,128)(2,1)S(1)}, bf16[528,128]{1,0:T(8,128)(2,1)S(1)}, u32[]{:S(2)}, u32[]{:S(2)}) collective-permute-start(bf16[528,128]{1,0:T(8,128)(2,1)S(1)} %get-tuple-element.29), channel_id=1, source_target_pairs={{0,8},{1,9},{2,10},{3,11},{4,12},{5,13},{6,14},{7,15},{8,0},{9,1},... | collective-permute-start | bytes 405512 | tf_op jit(solution)/shard_map/ppermute | solution.py:674
  11.7 17.1 %collective-permute-start.1 = (bf16[528,128]{1,0:T(8,128)(2,1)S(1)}, bf16[528,128]{1,0:T(8,128)(2,1)S(1)}, u32[]{:S(2)}, u32[]{:S(2)}) collective-permute-start(bf16[528,128]{1,0:T(8,128)(2,1)S(1)} %get-tuple-element.30), channel_id=1, source_target_pairs={{0,9},{1,8},{2,11},{3,10},{4,13},{5,12},{6,15},{7,14},{8,1},{9,0},... | collective-permute-start | bytes 405512 | tf_op jit(solution)/shard_map/ppermute | solution.py:674
  12.3 28.0 %collective-permute-start.2 = (bf16[528,128]{1,0:T(8,128)(2,1)S(1)}, bf16[528,128]{1,0:T(8,128)(2,1)S(1)}, u32[]{:S(2)}, u32[]{:S(2)}) collective-permute-start(bf16[528,128]{1,0:T(8,128)(2,1)S(1)} %get-tuple-element.31), channel_id=1, source_target_pairs={{0,10},{1,11},{2,8},{3,9},{4,14},{5,15},{6,12},{7,13},{8,2},{9,3},... | collective-permute-start | bytes 405512 | tf_op jit(solution)/shard_map/ppermute | solution.py:674
  15.5 28.1 %collective-permute-start.3 = (bf16[528,128]{1,0:T(8,128)(2,1)S(1)}, bf16[528,128]{1,0:T(8,128)(2,1)S(1)}, u32[]{:S(2)}, u32[]{:S(2)}) collective-permute-start(bf16[528,128]{1,0:T(8,128)(2,1)S(1)} %get-tuple-element.32), channel_id=1, source_target_pairs={{0,11},{1,10},{2,9},{3,8},{4,15},{5,14},{6,13},{7,12},{8,3},{9,2},... | collective-permute-start | bytes 405512 | tf_op jit(solution)/shard_map/ppermute | solution.py:674
  15.8 32.0 %collective-permute-start.4 = (bf16[528,128]{1,0:T(8,128)(2,1)S(1)}, bf16[528,128]{1,0:T(8,128)(2,1)S(1)}, u32[]{:S(2)}, u32[]{:S(2)}) collective-permute-start(bf16[528,128]{1,0:T(8,128)(2,1)S(1)} %get-tuple-element.33), channel_id=1, source_target_pairs={{0,12},{1,13},{2,14},{3,15},{4,8},{5,9},{6,10},{7,11},{8,4},{9,5},... | collective-permute-start | bytes 405512 | tf_op jit(solution)/shard_map/ppermute | solution.py:674
  25.2 27.4 %collective-permute-start.5 = (bf16[528,128]{1,0:T(8,128)(2,1)S(1)}, bf16[528,128]{1,0:T(8,128)(2,1)S(1)}, u32[]{:S(2)}, u32[]{:S(2)}) collective-permute-start(bf16[528,128]{1,0:T(8,128)(2,1)S(1)} %get-tuple-element.34), channel_id=1, source_target_pairs={{0,13},{1,12},{2,15},{3,14},{4,9},{5,8},{6,11},{7,10},{8,5},{9,4},... | collective-permute-start | bytes 405512 | tf_op jit(solution)/shard_map/ppermute | solution.py:674
  28.8 27.6 %collective-permute-start.6 = (bf16[528,128]{1,0:T(8,128)(2,1)S(1)}, bf16[528,128]{1,0:T(8,128)(2,1)S(1)}, u32[]{:S(2)}, u32[]{:S(2)}) collective-permute-start(bf16[528,128]{1,0:T(8,128)(2,1)S(1)} %get-tuple-element.35), channel_id=1, source_target_pairs={{0,14},{1,15},{2,12},{3,13},{4,10},{5,11},{6,8},{7,9},{8,6},{9,7},... | collective-permute-start | bytes 405512 | tf_op jit(solution)/shard_map/ppermute | solution.py:674
  40.3 19.1 %collective-permute-start.7 = (bf16[528,128]{1,0:T(8,128)(2,1)S(1)}, bf16[528,128]{1,0:T(8,128)(2,1)S(1)}, u32[]{:S(2)}, u32[]{:S(2)}) collective-permute-start(bf16[528,128]{1,0:T(8,128)(2,1)S(1)} %get-tuple-element.36), channel_id=1, source_target_pairs={{0,15},{1,14},{2,13},{3,12},{4,11},{5,10},{6,9},{7,8},{8,7},{9,6},... | collective-permute-start | bytes 405512 | tf_op jit(solution)/shard_map/ppermute | solution.py:674
  62.8 10.7 %all-to-all-start.1 = ((f32[16,16,128]{2,1,0:T(8,128)}), f32[16,16,128]{2,1,0:T(8,128)S(1)}, u32[]{:S(2)}, u32[]{:S(2)}) async-start(f32[16,16,128]{2,1,0:T(8,128)} %gram_pieces.1), calls=%async_computation.1 | async-start | bytes 262144 | tf_op jit(solution)/shard_map/all_to_all | solution.py:368
  78.9 30.3 %all-to-all-start.2 = ((bf16[8,512,128]{2,1,0:T(8,128)(2,1)}), bf16[8,512,128]{2,1,0:T(8,128)(2,1)S(1)}, u32[]{:S(2)}, u32[]{:S(2)}) async-start(bf16[8,512,128]{2,1,0:T(8,128)(2,1)} %get-tuple-element.45), calls=%async_computation.2 | async-start | bytes 2097152 | tf_op jit(solution)/shard_map/all_to_all | solution.py:679
  84.5 15.4 %collective-permute-start.8 = (bf16[512,128]{1,0:T(8,128)(2,1)}, bf16[512,128]{1,0:T(8,128)(2,1)S(1)}, u32[]{:S(2)}, u32[]{:S(2)}) collective-permute-start(bf16[512,128]{1,0:T(8,128)(2,1)} %get-tuple-element.44), channel_id=1, source_target_pairs={{0,8},{1,9},{2,10},{3,11},{4,12},{5,13},{6,14},{7,15},{8,0},{9,1},... | collective-permute-start | bytes 393224 | tf_op jit(solution)/shard_map/ppermute | solution.py:674
  84.9 18.6 %collective-permute-start.9 = (bf16[512,128]{1,0:T(8,128)(2,1)S(1)}, bf16[512,128]{1,0:T(8,128)(2,1)S(1)}, u32[]{:S(2)}, u32[]{:S(2)}) collective-permute-start(bf16[512,128]{1,0:T(8,128)(2,1)S(1)} %get-tuple-element.46), channel_id=1, source_target_pairs={{0,9},{1,8},{2,11},{3,10},{4,13},{5,12},{6,15},{7,14},{8,1},{9,0},... | collective-permute-start | bytes 393224 | tf_op jit(solution)/shard_map/ppermute | solution.py:674
  87.4 19.0 %collective-permute-start.10 = (bf16[512,128]{1,0:T(8,128)(2,1)S(1)}, bf16[512,128]{1,0:T(8,128)(2,1)S(1)}, u32[]{:S(2)}, u32[]{:S(2)}) collective-permute-start(bf16[512,128]{1,0:T(8,128)(2,1)S(1)} %get-tuple-element.47), channel_id=1, source_target_pairs={{0,10},{1,11},{2,8},{3,9},{4,14},{5,15},{6,12},{7,13},{8,2},{9,3},... | collective-permute-start | bytes 393224 | tf_op jit(solution)/shard_map/ppermute | solution.py:674
  88.7 23.0 %collective-permute-start.11 = (bf16[512,128]{1,0:T(8,128)(2,1)S(1)}, bf16[512,128]{1,0:T(8,128)(2,1)S(1)}, u32[]{:S(2)}, u32[]{:S(2)}) collective-permute-start(bf16[512,128]{1,0:T(8,128)(2,1)S(1)} %get-tuple-element.48), channel_id=1, source_target_pairs={{0,11},{1,10},{2,9},{3,8},{4,15},{5,14},{6,13},{7,12},{8,3},{9,2},... | collective-permute-start | bytes 393224 | tf_op jit(solution)/shard_map/ppermute | solution.py:674
  90.8 32.5 %collective-permute-start.12 = (bf16[512,128]{1,0:T(8,128)(2,1)S(1)}, bf16[512,128]{1,0:T(8,128)(2,1)S(1)}, u32[]{:S(2)}, u32[]{:S(2)}) collective-permute-start(bf16[512,128]{1,0:T(8,128)(2,1)S(1)} %get-tuple-element.49), channel_id=1, source_target_pairs={{0,12},{1,13},{2,14},{3,15},{4,8},{5,9},{6,10},{7,11},{8,4},{9,5},... | collective-permute-start | bytes 393224 | tf_op jit(solution)/shard_map/ppermute | solution.py:674
  99.9 26.9 %collective-permute-start.13 = (bf16[512,128]{1,0:T(8,128)(2,1)S(1)}, bf16[512,128]{1,0:T(8,128)(2,1)S(1)}, u32[]{:S(2)}, u32[]{:S(2)}) collective-permute-start(bf16[512,128]{1,0:T(8,128)(2,1)S(1)} %get-tuple-element.50), channel_id=1, source_target_pairs={{0,13},{1,12},{2,15},{3,14},{4,9},{5,8},{6,11},{7,10},{8,5},{9,4},... | collective-permute-start | bytes 393224 | tf_op jit(solution)/shard_map/ppermute | solution.py:674
  103.5 26.3 %collective-permute-start.14 = (bf16[512,128]{1,0:T(8,128)(2,1)S(1)}, bf16[512,128]{1,0:T(8,128)(2,1)S(1)}, u32[]{:S(2)}, u32[]{:S(2)}) collective-permute-start(bf16[512,128]{1,0:T(8,128)(2,1)S(1)} %get-tuple-element.51), channel_id=1, source_target_pairs={{0,14},{1,15},{2,12},{3,13},{4,10},{5,11},{6,8},{7,9},{8,6},{9,7},... | collective-permute-start | bytes 393224 | tf_op jit(solution)/shard_map/ppermute | solution.py:674
  106.5 26.6 %collective-permute-start.15 = (bf16[512,128]{1,0:T(8,128)(2,1)S(1)}, bf16[512,128]{1,0:T(8,128)(2,1)S(1)}, u32[]{:S(2)}, u32[]{:S(2)}) collective-permute-start(bf16[512,128]{1,0:T(8,128)(2,1)S(1)} %get-tuple-element.52), channel_id=1, source_target_pairs={{0,15},{1,14},{2,13},{3,12},{4,11},{5,10},{6,9},{7,8},{8,7},{9,6},... | collective-permute-start | bytes 393224 | tf_op jit(solution)/shard_map/ppermute | solution.py:674

commit v13 on v9

--- a/solution.py
+++ b/solution.py
@@ -374,90 +374,124 @@
     return pl.ds(pl.multiple_of(start, TILE), count)
 
 
-def split_pieces_body(slabs, lines, fields, row_ref, *refs):
+def split_pieces_body(slabs, raw, lines, fields, row_ref, *refs):
     half = slabs // 2
     field_refs, near_out, far_outs = refs[:fields], refs[fields], refs[fields + 1 : fields + 1 + half]
     slab_refs, helds, sems = refs[fields + 1 + half : -slabs - 1], refs[-slabs - 1 : -1], refs[-1]
     cells = lines * LANES
     end = row_ref.shape[1]
+    started = []
+
+    def fetch(source, target):
+        started.append(pltpu.make_async_copy(source, target, sems.at[len(started)]))
+        started[-1].start()
+        return started[-1]
+
     copies = []
     for at, held in enumerate(helds):
         slab = device_at(at, half)
-        parts = (
-            (slab * cells, cells, 0),
-            (jnp.minimum((slab + 1) * cells, end - GRID_Y), GRID_Y, cells),
-            (jnp.maximum(slab * cells - GRID_Y, 0), GRID_Y, cells + GRID_Y),
-        )
-        for n, (start, size, to) in enumerate(parts):
+        parts = [
+            (slab * cells, cells),
+            (jnp.minimum((slab + 1) * cells, end - GRID_Y), GRID_Y),
+            (jnp.maximum(slab * cells - GRID_Y, 0), GRID_Y),
+        ]
+        if at < half:
+            other = slab ^ half
+            parts += [(other * cells, raw * LANES + GRID_Y), (jnp.maximum(other * cells - GRID_Y, 0), GRID_Y)]
+        mine, to = [], 0
+        for start, size in parts:
             source = row_ref.at[:, pl.ds(pl.multiple_of(start, GRID_Y), size)]
-            copies.append(pltpu.make_async_copy(source, held.at[:, pl.ds(to, size)], sems.at[3 * at + n]))
-            copies[-1].start()
-    start = lax.axis_index("slab").astype(jnp.int32) * lines
-    for n, (field_ref, slab_ref) in enumerate(zip(field_refs, slab_refs)):
-        copies.append(pltpu.make_async_copy(field_ref.at[lines_of(start, lines), :], slab_ref, sems.at[3 * slabs + n]))
-        copies[-1].start()
+            mine.append(fetch(source, held.at[:, pl.ds(to, size)]))
+            to += size
+        copies.append(mine)
+    me = lax.axis_index("slab").astype(jnp.int32)
+    fetches = []
+    for n, target in enumerate(slab_refs):
+        start = (me if n < fields else me ^ half) * lines
+        fetches.append(fetch(field_refs[n % fields].at[lines_of(start, target.shape[0]), :], target))
+
+    def grid_row(held, at):
+        return held[:, pl.ds(at, GRID_Y)].astype(F32).reshape(LINE, LANES)
 
     for at, held in enumerate(helds):
         out_ref = near_out.at[at] if at < half else far_outs[at - half]
-        for copy in copies[3 * at : 3 * at + 3]:
+        for copy in copies[at]:
             copy.wait()
         slab = device_at(at, half)
         out_ref[:lines, :] = held[:, :cells].reshape(lines, LANES)
-        below = held[:, cells : cells + GRID_Y].astype(F32).reshape(LINE, LANES)
-        above = held[:, cells + GRID_Y :].astype(F32).reshape(LINE, LANES)
-        below = jnp.where(slab == slabs - 1, 0.0, below)
-        above = jnp.where(slab == 0, 0.0, above)
-        out_ref[lines:, :] = jnp.concatenate([below, above], axis=0).astype(BF16)
-    for copy in copies[3 * slabs :]:
+        below = jnp.where(slab == slabs - 1, 0.0, grid_row(held, cells))
+        above = jnp.where(slab == 0, 0.0, grid_row(held, cells + GRID_Y))
+        out_ref[lines : lines + TILE, :] = jnp.concatenate([below, above], axis=0).astype(BF16)
+        if at < half:
+            start = cells + 2 * GRID_Y
+            to = lines + TILE
+            out_ref[to : to + raw, :] = held[:, start : start + raw * LANES].reshape(raw, LANES)
+            below = grid_row(held, start + raw * LANES)
+            above = jnp.where(slab ^ half == 0, 0.0, grid_row(held, start + raw * LANES + GRID_Y))
+            out_ref[to + raw :, :] = jnp.concatenate([below, above], axis=0).astype(BF16)
+    for copy in fetches:
         copy.wait()
 
 
-def split_pieces(row, slabs, fields):
+def split_pieces(row, slabs, raw, fields):
     lines = row.shape[1] // slabs // LANES
     half = slabs // 2
     rim = lines + TILE
-    out_shape = [jax.ShapeDtypeStruct((half, rim, LANES), BF16)]
+    size = rim + raw + TILE
+    out_shape = [jax.ShapeDtypeStruct((half, size, LANES), BF16)]
     out_shape += [jax.ShapeDtypeStruct((rim, LANES), BF16)] * half
     out_shape += [jax.ShapeDtypeStruct((lines, LANES), BF16)] * len(fields)
-    return call(
-        functools.partial(split_pieces_body, slabs, lines, len(fields)),
+    out_shape += [jax.ShapeDtypeStruct((raw, LANES), BF16)] * len(fields)
+    return call(
+        functools.partial(split_pieces_body, slabs, raw, lines, len(fields)),
         "split_pieces",
-        moved=6 * slabs * rim * LANES,
+        moved=6 * half * (rim + size) * LANES,
         in_specs=[IN_HBM] * (1 + len(fields)),
         out_specs=[IN_VMEM] * len(out_shape),
         out_shape=out_shape,
-        scratch_shapes=[pltpu.VMEM((1, rim * LANES), BF16)] * slabs
-        + [pltpu.SemaphoreType.DMA((3 * slabs + len(fields),))],
+        scratch_shapes=[pltpu.VMEM((1, size * LANES), BF16)] * half
+        + [pltpu.VMEM((1, rim * LANES), BF16)] * half
+        + [pltpu.SemaphoreType.DMA((8 * slabs + 2 * len(fields),))],
     )(row, *fields)
 
 
-def join_pieces_body(pieces, half, lines, begun, arrays, *refs):
+def join_pieces_body(pieces, half, raw, lines, begun, arrays, *refs):
     row_ref, helds, sems = refs[begun + arrays], refs[begun + arrays + 1 : -1], refs[-1]
+    cells = lines * LANES
+    skip = raw * LANES
     copies = []
     for (array, lead, at), held in zip(pieces, helds):
         ref = refs[begun + array]
         piece = ref[...] if lead is None else ref[lead]
         held[...] = piece.reshape(held.shape)
-        start = device_at(at, half) * lines * LANES
-        target = row_ref.at[:, pl.ds(pl.multiple_of(start, GRID_Y), held.shape[1])]
-        copies.append(pltpu.make_async_copy(held, target, sems.at[len(copies)]))
-        copies[-1].start()
+        slab = device_at(at, half)
+        if at < half:
+            parts = [(0, cells, slab * cells), (cells, skip, (slab ^ half) * cells)]
+        else:
+            parts = [(0, cells - skip, slab * cells + skip)]
+        for begin, size, start in parts:
+            target = row_ref.at[:, pl.ds(pl.multiple_of(start, GRID_Y), size)]
+            copies.append(pltpu.make_async_copy(held.at[:, pl.ds(begin, size)], target, sems.at[len(copies)]))
+            copies[-1].start()
     for copy in copies:
         copy.wait()
 
 
-def join_pieces(row, slabs, arrays, pieces):
+def join_pieces(row, slabs, raw, arrays, pieces):
     sizes = [arrays[piece[0]].shape[-2] * LANES for piece in pieces]
     begun = [] if row is None else [row]
     return call(
-        functools.partial(join_pieces_body, pieces, slabs // 2, NCELL // slabs // LANES, len(begun), len(arrays)),
+        functools.partial(
+            join_pieces_body, pieces, slabs // 2, raw, NCELL // slabs // LANES, len(begun), len(arrays)
+        ),
         "join_pieces",
         moved=6 * sum(sizes),
         in_specs=[IN_HBM] * len(begun) + [IN_VMEM] * len(arrays),
         out_specs=IN_HBM,
         out_shape=jax.ShapeDtypeStruct((1, NCELL), BF16),
         input_output_aliases={0: 0} if begun else {},
-        scratch_shapes=[pltpu.VMEM((1, size), BF16) for size in sizes] + [pltpu.SemaphoreType.DMA((len(sizes),))],
+        scratch_shapes=[pltpu.VMEM((1, size), BF16) for size in sizes]
+        + [pltpu.SemaphoreType.DMA((2 * len(sizes),))],
     )(*begun, *arrays)
 
 
@@ -495,7 +529,7 @@
     out_ref[...] = jnp.broadcast_to(gram[None], out_ref.shape)
 
 
-def gram_pieces(near, far, lines, gates):
+def gram_pieces(near, far, lines, gates, early):
     total = 2 * len(far)
     wide = total * TILE
     return call(
@@ -503,11 +537,37 @@
         "gram_pieces",
         flops=2 * wide * wide * LANES * (lines // TILE),
         moved=2 * total * lines * LANES,
-        in_specs=[IN_VMEM] * (1 + len(far)) + [IN_HBM] * len(gates),
+        in_specs=[IN_VMEM] * (1 + len(far)) + [IN_HBM] * len(gates) + [IN_VMEM] * len(early),
         out_specs=IN_VMEM,
         out_shape=jax.ShapeDtypeStruct((total, total, LANES), F32),
         scratch_shapes=[pltpu.VMEM((wide, wide), F32)],
-    )(near, *far, *gates)
+    )(near, *far, *gates, *early)
+
+
+def block_gradient(load, i, count, observed, precision):
+    start = i * BLOCK
+    at = lines_of(start, BLOCK)
+    shape = (BLOCK // LINE, LINE, LANES)
+    lane = lax.broadcasted_iota(jnp.int32, (1, LINE, LANES), 2)
+    line = lax.broadcasted_iota(jnp.int32, (1, LINE, LANES), 1)
+    obs = observed[at, :].astype(F32).reshape(shape)
+    prec = precision[at, :].astype(F32).reshape(shape)
+    here = load(start, BLOCK).astype(F32)
+    before = load(jnp.where(i == 0, count, start - TILE), TILE).astype(F32)
+    after = load(start + BLOCK, TILE).astype(F32)
+    above = jnp.concatenate([before[LINE:], here[:-LINE]], axis=0).reshape(shape)
+    below = jnp.concatenate([here[LINE:], after[:LINE]], axis=0).reshape(shape)
+    field = here.reshape(shape)
+    turned = pltpu.roll(field, 1, 2)
+    carried = jnp.where(line == 0, 0.0, pltpu.roll(turned, 1, 1))
+    left = jnp.where(lane == 0, carried, turned)
+    turned = pltpu.roll(field, LANES - 1, 2)
+    carried = jnp.where(line == LINE - 1, 0.0, pltpu.roll(turned, LINE - 1, 1))
+    right = jnp.where(lane == LANES - 1, carried, turned)
+    laplace = (4.0 + mass_term) * field - (below + above + right + left)
+    squash = jnp.tanh(field)
+    result = prec * (obs - squash) * (1.0 - squash * squash) - prior_scale * laplace
+    return result.reshape(BLOCK, LANES).astype(BF16)
 
 
 def gradient_pieces_body(views, arrays, numbers, *refs):
@@ -516,10 +576,6 @@
     for n, number_ref in enumerate(number_refs):
         rows_ref[n : n + 1, :] = jnp.full((1, LANES), number_ref[0], F32)
     count = observed.shape[0]
-    rows = BLOCK // LINE
-    shape = (rows, LINE, LANES)
-    lane = lax.broadcasted_iota(jnp.int32, (1, LINE, LANES), 2)
-    line = lax.broadcasted_iota(jnp.int32, (1, LINE, LANES), 1)
     steps = count // BLOCK
 
     def store(i):
@@ -527,33 +583,13 @@
         return pltpu.make_async_copy(grads.at[:, at, :], out_ref.at[:, at, :], sems.at[i])
 
     def step(i, carry):
-        start = i * BLOCK
-        at = lines_of(start, BLOCK)
-        obs = observed[at, :].astype(F32).reshape(shape)
-        prec = precision[at, :].astype(F32).reshape(shape)
-        for p, (array, lead, base) in enumerate(views):
-
-            def load(begin, size):
-                part = lines_of(base + begin, size)
-                value = refs[array][part, :] if lead is None else refs[array][lead, part, :]
-                return value.astype(F32)
-
-            here = load(start, BLOCK)
-            before = load(jnp.where(i == 0, count, start - TILE), TILE)
-            after = load(start + BLOCK, TILE)
-            above = jnp.concatenate([before[LINE:], here[:-LINE]], axis=0).reshape(shape)
-            below = jnp.concatenate([here[LINE:], after[:LINE]], axis=0).reshape(shape)
-            field = here.reshape(shape)
-            turned = pltpu.roll(field, 1, 2)
-            carried = jnp.where(line == 0, 0.0, pltpu.roll(turned, 1, 1))
-            left = jnp.where(lane == 0, carried, turned)
-            turned = pltpu.roll(field, LANES - 1, 2)
-            carried = jnp.where(line == LINE - 1, 0.0, pltpu.roll(turned, LINE - 1, 1))
-            right = jnp.where(lane == LANES - 1, carried, turned)
-            laplace = (4.0 + mass_term) * field - (below + above + right + left)
-            squash = jnp.tanh(field)
-            result = prec * (obs - squash) * (1.0 - squash * squash) - prior_scale * laplace
-            grads[p, at, :] = result.reshape(BLOCK, LANES).astype(BF16)
+        for p, (array, lead) in enumerate(views):
+
+            def load(start, size):
+                part = lines_of(start, size)
+                return refs[array][part, :] if lead is None else refs[array][lead, part, :]
+
+            grads[p, lines_of(i * BLOCK, BLOCK), :] = block_gradient(load, i, count, observed, precision)
         store(i).start()
         return carry
 
@@ -582,6 +618,27 @@
     )(*arrays, observed, precision, *numbers)
 
 
+def raw_body(raw, lines, near_ref, *refs):
+    out_ref = refs[-1]
+    for k in range(near_ref.shape[0]):
+        out_ref[k, :raw, :] = near_ref[k, :raw, :]
+        below = near_ref[k, raw : raw + TILE, :].astype(F32)[:LINE]
+        above = near_ref[k, lines : lines + TILE, :].astype(F32)[LINE:]
+        out_ref[k, raw:, :] = jnp.concatenate([below, above], axis=0).astype(BF16)
+
+
+def raw_states(near, raw, lines, gates):
+    out = jax.ShapeDtypeStruct((near.shape[0], raw + TILE, LANES), BF16)
+    return call(
+        functools.partial(raw_body, raw, lines),
+        "raw_states",
+        moved=4 * out.size,
+        in_specs=[IN_VMEM] * (1 + len(gates)),
+        out_specs=IN_VMEM,
+        out_shape=out,
+    )(near, *gates)
+
+
 def mix(mixer, own, numbers_ref, total, states, slopes):
     high = mixer.shape[0]
     rate = numbers_ref[2:3, :1] / total
@@ -592,11 +649,12 @@
     return (states[:high].astype(F32) * own[...] + rate * (drive - coeff * pulled)).astype(BF16)
 
 
-def update_pieces_body(half, lines, groups, near_ref, *refs):
+def update_pieces_body(half, raw, lines, groups, near_ref, *refs):
     total = 2 * half
-    far_refs, numbers_ref, grams_ref, refs = refs[:half], refs[half], refs[half + 1], refs[half + 2 :]
-    group_refs, near_out, far_outs = refs[: len(groups)], refs[-5 - half], refs[-4 - half : -4]
-    mixer, own, grads, sems = refs[-4:]
+    far_refs, refs = refs[:half], refs[half:]
+    across_ref, raw_observed, raw_precision, numbers_ref, grams_ref, *refs = refs
+    group_refs, near_out, far_outs = refs[: len(groups)], refs[len(groups)], refs[len(groups) + 1 : -5]
+    mixer, own, grads, raw_grads, sems = refs[-5:]
     wide = total * TILE
     high = half * TILE
     fetches = []
@@ -605,6 +663,20 @@
             fetches.append(pltpu.make_async_copy(group_ref.at[j], grads.at[at], sems.at[len(fetches)]))
     for fetch in fetches:
         fetch.start()
+
+    def raw_gradient(i, carry):
+        for k in range(total):
+
+            def load(start, size):
+                if k < half:
+                    return near_ref[k, lines_of(lines + TILE + start, size), :]
+                return across_ref[k - half, lines_of(start, size), :]
+
+            part = lines_of(i * BLOCK, BLOCK)
+            raw_grads[k, part, :] = block_gradient(load, i, raw, raw_observed, raw_precision)
+        return carry
+
+    lax.fori_loop(0, raw // BLOCK, raw_gradient, 0)
     gram = jnp.sum(grams_ref[...], axis=0)[:, :total]
     spread, anneal, step_size = (numbers_ref[k : k + 1, :1] for k in range(3))
     rate = step_size / total
@@ -625,42 +697,64 @@
     for fetch in fetches:
         fetch.wait()
 
-    def step(i, carry):
+    def slab_step(with_far, i, carry):
+        rows = wide if with_far else high
         for t in range(BLOCK // TILE):
             at = i * BLOCK + t * TILE
             part = lines_of(at, TILE)
             states = [near_ref[:, part, :].reshape(high, LANES)] + [ref[part, :] for ref in far_refs]
             slopes = grads[:, part, :].reshape(wide, LANES)
-            new = mix(mixer, own, numbers_ref, total, jnp.concatenate(states, axis=0), slopes)
+            states = jnp.concatenate(states, axis=0)
+            new = mix(mixer.at[:rows, :], own.at[:rows, :], numbers_ref, total, states, slopes)
             near_out[:, part, :] = new[:high].reshape(half, TILE, LANES)
-            for x, far_out in enumerate(far_outs):
-                far_out[part, :] = new[high + x * TILE : high + (x + 1) * TILE]
+            if with_far:
+                for x, far_out in enumerate(far_outs):
+                    far_out[lines_of(at - raw, TILE), :] = new[high + x * TILE : high + (x + 1) * TILE]
         return carry
 
-    lax.fori_loop(0, lines // BLOCK, step, 0)
-
-
-def update_pieces(numbers, grams, near, far, grads, groups, lines):
+    here = lax.axis_index("slab").astype(jnp.int32) % half
+
+    def raw_step(i, carry):
+        for t in range(BLOCK // TILE):
+            at = i * BLOCK + t * TILE
+            part = lines_of(at, TILE)
+            states = [near_ref[:, lines_of(lines + TILE + at, TILE), :].reshape(high, LANES)]
+            slopes = [raw_grads[:half, part, :].reshape(high, LANES)]
+            for x in range(half):
+                states += [across_ref[here ^ x, part, :]]
+                slopes += [raw_grads[half + (here ^ x), part, :]]
+            states, slopes = jnp.concatenate(states, axis=0), jnp.concatenate(slopes, axis=0)
+            new = mix(mixer.at[:high, :], own.at[:high, :], numbers_ref, total, states, slopes)
+            near_out[:, lines_of(lines + at, TILE), :] = new.reshape(half, TILE, LANES)
+        return carry
+
+    lax.fori_loop(0, raw // BLOCK, raw_step, 0)
+    lax.fori_loop(0, raw // BLOCK, functools.partial(slab_step, False), 0)
+    lax.fori_loop(raw // BLOCK, lines // BLOCK, functools.partial(slab_step, True), 0)
+
+
+def update_pieces(numbers, grams, near, far, across, raw_fields, grads, groups, raw, lines):
     half = len(far)
     total = 2 * half
     wide = total * TILE
-    out_shape = [jax.ShapeDtypeStruct((half, lines, LANES), BF16)]
-    out_shape += [jax.ShapeDtypeStruct((lines, LANES), BF16)] * half
-    return call(
-        functools.partial(update_pieces_body, half, lines, groups),
+    out_shape = [jax.ShapeDtypeStruct((half, lines + raw, LANES), BF16)]
+    out_shape += [jax.ShapeDtypeStruct((lines - raw, LANES), BF16)] * half
+    return call(
+        functools.partial(update_pieces_body, half, raw, lines, groups),
         "update_pieces",
         flops=4 * wide * wide * LANES * (lines // TILE),
         moved=6 * total * lines * LANES,
-        in_specs=[IN_VMEM] * (half + 3) + [IN_HBM] * len(groups),
+        in_specs=[IN_VMEM] * (half + 6) + [IN_HBM] * len(groups),
         out_specs=[IN_VMEM] * len(out_shape),
         out_shape=out_shape,
         scratch_shapes=[
             pltpu.VMEM((wide, wide), BF16),
             pltpu.VMEM((wide, LANES), F32),
             pltpu.VMEM((total, lines, LANES), BF16),
+            pltpu.VMEM((total, raw, LANES), BF16),
             pltpu.SemaphoreType.DMA((total,)),
         ],
-    )(near, *far, numbers, grams, *grads)
+    )(near, *far, across, *raw_fields, numbers, grams, *grads)
 
 
 def exchange(piece, k, slabs):
@@ -672,6 +766,7 @@
     return lax.all_to_all(pieces, "slab", 0, 0, axis_index_groups=groups, tiled=True)
 
 
+RAW = 128
 GRADIENTS = ((8, 9, 10, 11), (12, 13, 14, 15), (0, 1, 2, 3, 4, 5, 6, 7))
 
 
@@ -681,29 +776,33 @@
     lines = NCELL // slabs // LANES
     row = in_hbm(particles)
     fields = [in_hbm(field.reshape(-1, LANES)) for field in (observed, precision)]
-    near, *far = split_pieces(row, slabs, fields)
-    far, (obs, prec) = far[:half], far[half:]
+    near, *far = split_pieces(row, slabs, RAW, fields)
+    far, (obs, prec, *raw_fields) = far[:half], far[half:]
     near = swap_near(near, slabs)
     far = [exchange(piece, half + x, slabs) for x, piece in enumerate(far)]
+    raw_near = raw_states(near, RAW, lines, far)
+    across = exchange(raw_near, half, slabs)
     grads = []
     numbers = [spread, anneal, step_size]
     for group in GRADIENTS:
         if group[0] < half:
-            arrays, views = [near], [(0, k, 0) for k in group]
+            arrays, views = [near], [(0, k) for k in group]
         else:
-            arrays, views = [far[k - half] for k in group], [(j, None, 0) for j in range(len(group))]
+            arrays, views = [far[k - half] for k in group], [(j, None) for j in range(len(group))]
         slopes, rows = gradient_pieces(arrays, tuple(views), obs, prec, [] if grads else numbers)
         grads.append(in_hbm(slopes))
         numbers = numbers if len(grads) > 1 else rows
-    grams = swap(gram_pieces(near, far, lines, grads[:1]))
-    new_near, *new_far = update_pieces(numbers, grams, near, far, grads, GRADIENTS, lines)
+    grams = swap(gram_pieces(near, far, lines, grads[:1], [raw_near]))
+    new_near, *new_far = update_pieces(
+        numbers, grams, near, far, across, raw_fields, grads, GRADIENTS, RAW, lines
+    )
     new_near = swap_near(new_near, slabs)
     new_far = [exchange(piece, half + x, slabs) for x, piece in enumerate(new_far)]
-    row = join_pieces(None, slabs, [new_near], [(0, k, k) for k in range(half)])
+    row = join_pieces(None, slabs, RAW, [new_near], [(0, k, k) for k in range(half)])
     for group in ((0, 1, 2, 3), (4, 5)):
         pieces = [(n, None, half + x) for n, x in enumerate(group)]
-        row = join_pieces(row, slabs, [new_far[x] for x in group], pieces)
-    return join_pieces(row, slabs, new_far[6:], [(n, None, half + 6 + n) for n in range(half - 6)])
+        row = join_pieces(row, slabs, RAW, [new_far[x] for x in group], pieces)
+    return join_pieces(row, slabs, RAW, new_far[6:], [(n, None, half + 6 + n) for n in range(half - 6)])
 
 
 def on_device(particles, observed, precision, spread, anneal, step_size):

time: 133 us -> 132 us (level)
  local copies, waits for them, and re-layouts: 0 us -> 2.97 us
  starting transfers between devices: 35.2 us -> 32.9 us
  waiting for transfers between devices: 70.3 us -> 68.2 us
    ppermute x16 -> x17, waiting for transfers between devices: 70 us -> 65.6 us  [exchange(): return lax.ppermute(piece, 'slab', [(i, i ^ k) for i in range(slabs)])]
    unnamed x0 -> x14, local copies, waits for them, and re-layouts: none -> 2.97 us
    ppermute x16 -> x17, starting transfers between devices: 20.1 us -> 17.8 us  [exchange(): return lax.ppermute(piece, 'slab', [(i, i ^ k) for i in range(slabs)])]
    all_to_all x1, waiting for transfers between devices: 0.35 us -> 2.58 us  [swap(): lax.all_to_all(slabs, 'slab', split_axis=0, concat_axis=0, tiled=True)]
    pallas_call x6 -> x7, Pallas kernels: 14.3 us -> 15.1 us  [the longest x4 5.54 us: join_pieces(): call(functools.partial(join_pieces_body, pieces, slabs // 2, raw, NCELL /...]
  transfers between devices with their start and end apart: 19 -> 20, of which waited for: 16 -> 15; matrix products, arithmetic and copies ran while one was open for 0% -> 0% of each run, Pallas kernels for 9% -> 12%
where the time goes in v13:
time: 132 us
  waiting for transfers between devices  68.2 us (52%)
  starting transfers between devices  32.9 us (25%)
  Pallas kernels  25.9 us (20%)
  local copies, waits for them, and re-layouts  2.97 us (2%)
  between operations  2.07 us (2%)
    ppermute x17, waiting for transfers between devices, exchange(): return lax.ppermute(piece, 'slab', [(i, i ^ k) for i in range(slabs)])  65.6 us
    ppermute x17, starting transfers between devices, exchange(): return lax.ppermute(piece, 'slab', [(i, i ^ k) for i in range(slabs)])  17.8 us
    all_to_all x2, starting transfers between devices, swap_near(): lax.all_to_all(pieces, 'slab', 0, 0, axis_index_groups=groups, tiled=True)  9.34 us
    pallas_call x3, Pallas kernels, gradient_pieces(): call(functools.partial(gradient_pieces_body, views, len(arrays), len(numb...  7.34 us
    all_to_all x1, starting transfers between devices, swap(): lax.all_to_all(slabs, 'slab', split_axis=0, concat_axis=0, tiled=True)  5.75 us
    pallas_call x4, Pallas kernels, join_pieces(): call(functools.partial(join_pieces_body, pieces, slabs // 2, raw, NCELL /...  5.54 us
    pallas_call x1, Pallas kernels, split_pieces(): call(functools.partial(split_pieces_body, slabs, raw, lines, len(fields))...  4.88 us
    pallas_call x1, Pallas kernels, update_pieces(): call(functools.partial(update_pieces_body, half, raw, lines, groups), 'up...  4.67 us
  transfers between devices with their start and end apart: 20, of which 15 were waited for; matrix products, arithmetic and copies ran while one was open for 0% of the time, Pallas kernels for 12%

profile of v13, /device:TPU:9, one launch (start us, length us, event | category | flops | bytes accessed | tf_op | source)
XLA Modules:
  0.0 132.0 jit_solution(13203129773890690020)
XLA Ops:
  0.0 4.9 %split_pieces.1 = (bf16[8,672,128]{2,1,0:T(8,128)(2,1)}, bf16[528,128]{1,0:T(8,128)(2,1)S(1)}, bf16[528,128]{1,0:T(8,128)(2,1)S(1)}, bf16[528,128]{1,0:T(8,128)(...) custom-call(bf16[1,1048576]{1,0:T(2,128)(2,1)} %row_ref.1, ...), custom_call_target="tpu_custom_call" | custom-call | bytes 7372800 | tf_op jit(solution)/shard_map/split_pieces/pallas_call | solution.py:445
  4.9 4.6 %all-to-all-start = ((bf16[8,672,128]{2,1,0:T(8,128)(2,1)}), bf16[8,672,128]{2,1,0:T(8,128)(2,1)S(1)}, u32[]{:S(2)}, u32[]{:S(2)}) async-start(bf16[8,672,128]{2,1,0:T(8,128)(2,1)} %get-tuple-element.31), calls=%async_computation | async-start | bytes 2752512 | tf_op jit(solution)/shard_map/all_to_all | solution.py:766
  9.5 2.3 %collective-permute-start = (bf16[528,128]{1,0:T(8,128)(2,1)S(1)}, bf16[528,128]{1,0:T(8,128)(2,1)S(1)}, u32[]{:S(2)}, u32[]{:S(2)}) collective-permute-start(bf16[528,128]{1,0:T(8,128)(2,1)S(1)} %get-tuple-element.32), channel_id=1, source_target_pairs={{0,8},{1,9},{2,10},{3,11},{4,12},{5,13},{6,14},{7,15},{8,0},{9,1},... | collective-permute-start | bytes 405512 | tf_op jit(solution)/shard_map/ppermute | solution.py:761
  11.8 0.6 collective-permute-start.1
  12.4 3.2 %collective-permute-start.2 = (bf16[528,128]{1,0:T(8,128)(2,1)S(1)}, bf16[528,128]{1,0:T(8,128)(2,1)S(1)}, u32[]{:S(2)}, u32[]{:S(2)}) collective-permute-start(bf16[528,128]{1,0:T(8,128)(2,1)S(1)} %get-tuple-element.34), channel_id=1, source_target_pairs={{0,10},{1,11},{2,8},{3,9},{4,14},{5,15},{6,12},{7,13},{8,2},{9,3},... | collective-permute-start | bytes 405512 | tf_op jit(solution)/shard_map/ppermute | solution.py:761
  15.6 0.3 collective-permute-start.3
  15.9 1.0 collective-permute-start.4
  16.9 13.5 %collective-permute-done.refs_0_ = bf16[528,128]{1,0:T(8,128)(2,1)S(1)} collective-permute-done((bf16[528,128]{1,0:T(8,128)(2,1)S(1)}, bf16[528,128]{1,0:T(8,128)(2,1)S(1)}, u32[]{:S(2)}, u32[]{:S(2)}) %collective-permute-start) | collective-permute-done | bytes 135200 | tf_op jit(solution)/shard_map/ppermute | solution.py:761
  30.4 0.0 collective-permute-start.5
  30.4 3.6 %collective-permute-done.1.refs_1_ = bf16[528,128]{1,0:T(8,128)(2,1)S(1)} collective-permute-done((bf16[528,128]{1,0:T(8,128)(2,1)S(1)}, bf16[528,128]{1,0:T(8,128)(2,1)S(1)}, u32[]{:S(2)}, u32[]{:S(2)}) %collective-permute-start.1) | collective-permute-done | bytes 135200 | tf_op jit(solution)/shard_map/ppermute | solution.py:761
  34.0 0.3 collective-permute-start.6
  34.3 2.8 %collective-permute-done.2.refs_2_ = bf16[528,128]{1,0:T(8,128)(2,1)S(1)} collective-permute-done((bf16[528,128]{1,0:T(8,128)(2,1)S(1)}, bf16[528,128]{1,0:T(8,128)(2,1)S(1)}, u32[]{:S(2)}, u32[]{:S(2)}) %collective-permute-start.2) | collective-permute-done | bytes 135200 | tf_op jit(solution)/shard_map/ppermute | solution.py:761
  39.1 1.7 %collective-permute-done.3.refs_3_ = bf16[528,128]{1,0:T(8,128)(2,1)S(1)} collective-permute-done((bf16[528,128]{1,0:T(8,128)(2,1)S(1)}, bf16[528,128]{1,0:T(8,128)(2,1)S(1)}, u32[]{:S(2)}, u32[]{:S(2)}) %collective-permute-start.3) | collective-permute-done | bytes 135200 | tf_op jit(solution)/shard_map/ppermute | solution.py:761
  40.7 1.8 %gradient_pieces.3 = (bf16[4,512,128]{2,1,0:T(8,128)(2,1)}, f32[8,128]{1,0:T(8,128)S(1)}) custom-call(bf16[528,128]{1,0:T(8,128)(2,1)S(1)} %collective-permute-done.refs_0_, bf16[528,128]{1,0:T(8,128)(2,1)S(1)} %collective-permute-done.1.refs_1_, bf16[528,128]{1,0:T(8,128)(2,1)S(1)} %collective-permute-done.2.refs_2_, ...), custom_call_target="tpu_custom_call" | custom-call | flops 7864320 | bytes 2097152 | tf_op jit(solution)/shard_map/gradient_pieces/pallas_call | solution.py:608
  42.5 6.7 %collective-permute-done.4.refs_4_.refs_0_ = bf16[528,128]{1,0:T(8,128)(2,1)S(1)} collective-permute-done((bf16[528,128]{1,0:T(8,128)(2,1)S(1)}, bf16[528,128]{1,0:T(8,128)(2,1)S(1)}, u32[]{:S(2)}, u32[]{:S(2)}) %collective-permute-start.4) | collective-permute-done | bytes 135200 | tf_op jit(solution)/shard_map/ppermute | solution.py:761
  49.2 4.7 %collective-permute-done.5.refs_5_.refs_1_ = bf16[528,128]{1,0:T(8,128)(2,1)S(1)} collective-permute-done((bf16[528,128]{1,0:T(8,128)(2,1)S(1)}, bf16[528,128]{1,0:T(8,128)(2,1)S(1)}, u32[]{:S(2)}, u32[]{:S(2)}) %collective-permute-start.5) | collective-permute-done | bytes 135200 | tf_op jit(solution)/shard_map/ppermute | solution.py:761
  54.0 3.8 %collective-permute-done.6.refs_6_.refs_2_ = bf16[528,128]{1,0:T(8,128)(2,1)S(1)} collective-permute-done((bf16[528,128]{1,0:T(8,128)(2,1)S(1)}, bf16[528,128]{1,0:T(8,128)(2,1)S(1)}, u32[]{:S(2)}, u32[]{:S(2)}) %collective-permute-start.6) | collective-permute-done | bytes 135200 | tf_op jit(solution)/shard_map/ppermute | solution.py:761
  57.8 2.9 %collective-permute-done.7.refs_7_.refs_3_ = bf16[528,128]{1,0:T(8,128)(2,1)S(1)} collective-permute-done((bf16[528,128]{1,0:T(8,128)(2,1)S(1)}, bf16[528,128]{1,0:T(8,128)(2,1)S(1)}, u32[]{:S(2)}, u32[]{:S(2)}) %collective-permute-start.7) | collective-permute-done | bytes 135200 | tf_op jit(solution)/shard_map/ppermute | solution.py:761
  60.7 0.1 collective-permute-start.8
  60.8 3.4 %gram_pieces.1 = f32[16,16,128]{2,1,0:T(8,128)} custom-call(bf16[8,672,128]{2,1,0:T(8,128)(2,1)S(1)} %all-to-all-done.near_ref.refs_0_, bf16[528,128]{1,0:T(8,128)(2,1)S(1)} %collective-permute-done.refs_0_, bf16[528,128]{1,0:T(8,128)(2,1)S(1)} %collective-permute-done.1.refs_1_, bf16[528,128]{1,0:T(8,128)(2,1)S(1)} %collective-permute-done.2.refs_2_, ...), custom_call_target="tpu_custom_call" | custom-call | flops 536870912 | bytes 2097152 | tf_op jit(solution)/shard_map/gram_pieces/pallas_call | solution.py:535
  64.2 5.8 %all-to-all-start.1 = ((f32[16,16,128]{2,1,0:T(8,128)}), f32[16,16,128]{2,1,0:T(8,128)S(1)}, u32[]{:S(2)}, u32[]{:S(2)}) async-start(f32[16,16,128]{2,1,0:T(8,128)} %gram_pieces.1), calls=%async_computation.1 | async-start | bytes 262144 | tf_op jit(solution)/shard_map/all_to_all | solution.py:365
  70.0 2.4 %gradient_pieces.4 = (bf16[4,512,128]{2,1,0:T(8,128)(2,1)}, f32[8,128]{1,0:T(8,128)}) custom-call(bf16[528,128]{1,0:T(8,128)(2,1)S(1)} %collective-permute-done.4.refs_4_.refs_0_, bf16[528,128]{1,0:T(8,128)(2,1)S(1)} %collective-permute-done.5.refs_5_.refs_1_, bf16[528,128]{1,0:T(8,128)(2,1)S(1)} %collective-permute-done.6.refs_6_.refs_2_, ...), custom_call_target="tpu_custom_call" | custom-call | flops 7864320 | bytes 2097152 | tf_op jit(solution)/shard_map/gradient_pieces/pallas_call | solution.py:608
  72.4 3.1 %gradient_pieces.5 = (bf16[8,512,128]{2,1,0:T(8,128)(2,1)}, f32[8,128]{1,0:T(8,128)}) custom-call(bf16[8,672,128]{2,1,0:T(8,128)(2,1)S(1)} %all-to-all-done.near_ref.refs_0_, bf16[512,128]{1,0:T(8,128)(2,1)S(1)} %get-tuple-element.42.refs_4_.refs_1_, bf16[512,128]{1,0:T(8,128)(2,1)S(1)} %get-tuple-element.43.refs_5_.refs_2_), custom_call_target="tpu_custom_call" | custom-call | flops 15728640 | bytes 4194304 | tf_op jit(solution)/shard_map/gradient_pieces/pallas_call | solution.py:608
  75.5 2.6 %all-to-all-done.1.refs_12_ = f32[16,16,128]{2,1,0:T(8,128)S(1)} async-done(((f32[16,16,128]{2,1,0:T(8,128)}), f32[16,16,128]{2,1,0:T(8,128)S(1)}, u32[]{:S(2)}, u32[]{:S(2)}) %all-to-all-start.1) | async-done | bytes 131104 | tf_op jit(solution)/shard_map/all_to_all | solution.py:365
  78.1 4.7 %update_pieces.1 = (bf16[8,640,128]{2,1,0:T(8,128)(2,1)S(1)}, bf16[384,128]{1,0:T(8,128)(2,1)S(1)}, bf16[384,128]{1,0:T(8,128)(2,1)S(1)}, bf16[384,128]{1,0:T(8,...) custom-call(bf16[8,672,128]{2,1,0:T(8,128)(2,1)S(1)} %all-to-all-don, ...), custom_call_target="tpu_custom_call" | custom-call | flops 1073741824 | bytes 6291456 | tf_op jit(solution)/shard_map/update_pieces/pallas_call | solution.py:742
  82.8 1.0 copy-done
  83.9 0.6 copy-done.1
  84.5 0.6 copy-done.3
  85.1 0.6 copy-done.5
  85.8 4.8 %all-to-all-start.2 = ((bf16[8,640,128]{2,1,0:T(8,128)(2,1)}), bf16[8,640,128]{2,1,0:T(8,128)(2,1)S(1)}, u32[]{:S(2)}, u32[]{:S(2)}) async-start(bf16[8,640,128]{2,1,0:T(8,128)(2,1)} %copy-done), calls=%async_computation.2 | async-start | bytes 2621440 | tf_op jit(solution)/shard_map/all_to_all | solution.py:766
  90.5 1.2 collective-permute-start.9
  91.7 1.7 %collective-permute-start.10 = (bf16[384,128]{1,0:T(8,128)(2,1)S(1)}, bf16[384,128]{1,0:T(8,128)(2,1)S(1)}, u32[]{:S(2)}, u32[]{:S(2)}) collective-permute-start(bf16[384,128]{1,0:T(8,128)(2,1)S(1)} %copy-done.4), channel_id=1, source_target_pairs={{0,9},{1,8},{2,11},{3,10},{4,13},{5,12},{6,15},{7,14},{8,1},{9,0},... | collective-permute-start | bytes 294920 | tf_op jit(solution)/shard_map/ppermute | solution.py:761
  93.4 2.1 %collective-permute-start.11 = (bf16[384,128]{1,0:T(8,128)(2,1)S(1)}, bf16[384,128]{1,0:T(8,128)(2,1)S(1)}, u32[]{:S(2)}, u32[]{:S(2)}) collective-permute-start(bf16[384,128]{1,0:T(8,128)(2,1)S(1)} %copy-done.2), channel_id=1, source_target_pairs={{0,10},{1,11},{2,8},{3,9},{4,14},{5,15},{6,12},{7,13},{8,2},{9,3},... | collective-permute-start | bytes 294920 | tf_op jit(solution)/shard_map/ppermute | solution.py:761
  95.5 1.2 collective-permute-start.12
  96.7 0.0 collective-permute-start.13
  96.8 12.0 %collective-permute-done.9.refs_1_ = bf16[384,128]{1,0:T(8,128)(2,1)S(1)} collective-permute-done((bf16[384,128]{1,0:T(8,128)(2,1)S(1)}, bf16[384,128]{1,0:T(8,128)(2,1)S(1)}, u32[]{:S(2)}, u32[]{:S(2)}) %collective-permute-start.9) | collective-permute-done | bytes 98336 | tf_op jit(solution)/shard_map/ppermute | solution.py:761
  108.8 1.1 collective-permute-start.14
  109.9 1.7 %collective-permute-done.10.refs_2_ = bf16[384,128]{1,0:T(8,128)(2,1)S(1)} collective-permute-done((bf16[384,128]{1,0:T(8,128)(2,1)S(1)}, bf16[384,128]{1,0:T(8,128)(2,1)S(1)}, u32[]{:S(2)}, u32[]{:S(2)}) %collective-permute-start.10) | collective-permute-done | bytes 98336 | tf_op jit(solution)/shard_map/ppermute | solution.py:761
  111.6 1.5 %collective-permute-start.15 = (bf16[384,128]{1,0:T(8,128)(2,1)S(1)}, bf16[384,128]{1,0:T(8,128)(2,1)S(1)}, u32[]{:S(2)}, u32[]{:S(2)}) collective-permute-start(bf16[384,128]{1,0:T(8,128)(2,1)S(1)} %get-tuple-element.55), channel_id=1, source_target_pairs={{0,14},{1,15},{2,12},{3,13},{4,10},{5,11},{6,8},{7,9},{8,6},{9,7},... | collective-permute-start | bytes 294920 | tf_op jit(solution)/shard_map/ppermute | solution.py:761
  113.1 0.9 collective-permute-done.11.refs_3_
  114.0 1.2 collective-permute-start.16
  115.1 3.0 %join_pieces.4.refs_0_ = bf16[1,1048576]{1,0:T(2,128)(2,1)} custom-call(bf16[8,640,128]{2,1,0:T(8,128)(2,1)S(1)} %all-to-all-done.2.refs_0_), custom_call_target="tpu_custom_call" | custom-call | bytes 3932160 | tf_op jit(solution)/shard_map/join_pieces/pallas_call | solution.py:483
  118.1 1.0 join_pieces.5.refs_0_
  119.1 7.0 %collective-permute-done.14.refs_2_ = bf16[384,128]{1,0:T(8,128)(2,1)S(1)} collective-permute-done((bf16[384,128]{1,0:T(8,128)(2,1)S(1)}, bf16[384,128]{1,0:T(8,128)(2,1)S(1)}, u32[]{:S(2)}, u32[]{:S(2)}) %collective-permute-start.14) | collective-permute-done | bytes 98336 | tf_op jit(solution)/shard_map/ppermute | solution.py:761
  126.1 0.8 join_pieces.6.refs_0_
  126.9 2.2 %collective-permute-done.15.refs_1_ = bf16[384,128]{1,0:T(8,128)(2,1)S(1)} collective-permute-done((bf16[384,128]{1,0:T(8,128)(2,1)S(1)}, bf16[384,128]{1,0:T(8,128)(2,1)S(1)}, u32[]{:S(2)}, u32[]{:S(2)}) %collective-permute-start.15) | collective-permute-done | bytes 98336 | tf_op jit(solution)/shard_map/ppermute | solution.py:761
  129.1 2.1 %collective-permute-done.16.refs_2_ = bf16[384,128]{1,0:T(8,128)(2,1)S(1)} collective-permute-done((bf16[384,128]{1,0:T(8,128)(2,1)S(1)}, bf16[384,128]{1,0:T(8,128)(2,1)S(1)}, u32[]{:S(2)}, u32[]{:S(2)}) %collective-permute-start.16) | collective-permute-done | bytes 98336 | tf_op jit(solution)/shard_map/ppermute | solution.py:761
  131.2 0.8 join_pieces.7
  (17 shorter events, 0.1 us)
Async XLA Ops:
  4.9 55.8 %all-to-all-start = ((bf16[8,672,128]{2,1,0:T(8,128)(2,1)}), bf16[8,672,128]{2,1,0:T(8,128)(2,1)S(1)}, u32[]{:S(2)}, u32[]{:S(2)}) async-start(bf16[8,672,128]{2,1,0:T(8,128)(2,1)} %get-tuple-element.31), calls=%async_computation | async-start | bytes 2752512 | tf_op jit(solution)/shard_map/all_to_all | solution.py:766
  9.5 20.9 %collective-permute-start = (bf16[528,128]{1,0:T(8,128)(2,1)S(1)}, bf16[528,128]{1,0:T(8,128)(2,1)S(1)}, u32[]{:S(2)}, u32[]{:S(2)}) collective-permute-start(bf16[528,128]{1,0:T(8,128)(2,1)S(1)} %get-tuple-element.32), channel_id=1, source_target_pairs={{0,8},{1,9},{2,10},{3,11},{4,12},{5,13},{6,14},{7,15},{8,0},{9,1},... | collective-permute-start | bytes 405512 | tf_op jit(solution)/shard_map/ppermute | solution.py:761
  11.8 22.2 %collective-permute-start.1 = (bf16[528,128]{1,0:T(8,128)(2,1)S(1)}, bf16[528,128]{1,0:T(8,128)(2,1)S(1)}, u32[]{:S(2)}, u32[]{:S(2)}) collective-permute-start(bf16[528,128]{1,0:T(8,128)(2,1)S(1)} %get-tuple-element.33), channel_id=1, source_target_pairs={{0,9},{1,8},{2,11},{3,10},{4,13},{5,12},{6,15},{7,14},{8,1},{9,0},... | collective-permute-start | bytes 405512 | tf_op jit(solution)/shard_map/ppermute | solution.py:761
  12.4 24.8 %collective-permute-start.2 = (bf16[528,128]{1,0:T(8,128)(2,1)S(1)}, bf16[528,128]{1,0:T(8,128)(2,1)S(1)}, u32[]{:S(2)}, u32[]{:S(2)}) collective-permute-start(bf16[528,128]{1,0:T(8,128)(2,1)S(1)} %get-tuple-element.34), channel_id=1, source_target_pairs={{0,10},{1,11},{2,8},{3,9},{4,14},{5,15},{6,12},{7,13},{8,2},{9,3},... | collective-permute-start | bytes 405512 | tf_op jit(solution)/shard_map/ppermute | solution.py:761
  15.6 25.2 %collective-permute-start.3 = (bf16[528,128]{1,0:T(8,128)(2,1)S(1)}, bf16[528,128]{1,0:T(8,128)(2,1)S(1)}, u32[]{:S(2)}, u32[]{:S(2)}) collective-permute-start(bf16[528,128]{1,0:T(8,128)(2,1)S(1)} %get-tuple-element.35), channel_id=1, source_target_pairs={{0,11},{1,10},{2,9},{3,8},{4,15},{5,14},{6,13},{7,12},{8,3},{9,2},... | collective-permute-start | bytes 405512 | tf_op jit(solution)/shard_map/ppermute | solution.py:761
  15.9 33.4 %collective-permute-start.4 = (bf16[528,128]{1,0:T(8,128)(2,1)S(1)}, bf16[528,128]{1,0:T(8,128)(2,1)S(1)}, u32[]{:S(2)}, u32[]{:S(2)}) collective-permute-start(bf16[528,128]{1,0:T(8,128)(2,1)S(1)} %get-tuple-element.36), channel_id=1, source_target_pairs={{0,12},{1,13},{2,14},{3,15},{4,8},{5,9},{6,10},{7,11},{8,4},{9,5},... | collective-permute-start | bytes 405512 | tf_op jit(solution)/shard_map/ppermute | solution.py:761
  30.4 23.6 %collective-permute-start.5 = (bf16[528,128]{1,0:T(8,128)(2,1)S(1)}, bf16[528,128]{1,0:T(8,128)(2,1)S(1)}, u32[]{:S(2)}, u32[]{:S(2)}) collective-permute-start(bf16[528,128]{1,0:T(8,128)(2,1)S(1)} %get-tuple-element.37), channel_id=1, source_target_pairs={{0,13},{1,12},{2,15},{3,14},{4,9},{5,8},{6,11},{7,10},{8,5},{9,4},... | collective-permute-start | bytes 405512 | tf_op jit(solution)/shard_map/ppermute | solution.py:761
  34.0 23.8 %collective-permute-start.6 = (bf16[528,128]{1,0:T(8,128)(2,1)S(1)}, bf16[528,128]{1,0:T(8,128)(2,1)S(1)}, u32[]{:S(2)}, u32[]{:S(2)}) collective-permute-start(bf16[528,128]{1,0:T(8,128)(2,1)S(1)} %get-tuple-element.38), channel_id=1, source_target_pairs={{0,14},{1,15},{2,12},{3,13},{4,10},{5,11},{6,8},{7,9},{8,6},{9,7},... | collective-permute-start | bytes 405512 | tf_op jit(solution)/shard_map/ppermute | solution.py:761
  37.1 23.5 %collective-permute-start.7 = (bf16[528,128]{1,0:T(8,128)(2,1)S(1)}, bf16[528,128]{1,0:T(8,128)(2,1)S(1)}, u32[]{:S(2)}, u32[]{:S(2)}) collective-permute-start(bf16[528,128]{1,0:T(8,128)(2,1)S(1)} %get-tuple-element.39), channel_id=1, source_target_pairs={{0,15},{1,14},{2,13},{3,12},{4,11},{5,10},{6,9},{7,8},{8,7},{9,6},... | collective-permute-start | bytes 405512 | tf_op jit(solution)/shard_map/ppermute | solution.py:761
  60.7 17.4 %collective-permute-start.8 = (bf16[8,144,128]{2,1,0:T(8,128)(2,1)S(1)}, bf16[8,144,128]{2,1,0:T(8,128)(2,1)S(1)}, u32[]{:S(2)}, u32[]{:S(2)}) collective-permute-start(bf16[8,144,128]{2,1,0:T(8,128)(2,1)S(1)} %raw_states.1.refs_9_), channel_id=1, source_target_pairs={{0,8},{1,9},{2,10},{3,11},{4,12},{5,13},{6,14},{7,15},{8,0},{9,1},... | collective-permute-start | bytes 884744 | tf_op jit(solution)/shard_map/ppermute | solution.py:761
  64.2 13.9 %all-to-all-start.1 = ((f32[16,16,128]{2,1,0:T(8,128)}), f32[16,16,128]{2,1,0:T(8,128)S(1)}, u32[]{:S(2)}, u32[]{:S(2)}) async-start(f32[16,16,128]{2,1,0:T(8,128)} %gram_pieces.1), calls=%async_computation.1 | async-start | bytes 262144 | tf_op jit(solution)/shard_map/all_to_all | solution.py:365
  82.8 1.1 copy-start
  83.9 0.6 copy-start.1
  84.5 0.6 copy-start.3
  85.1 0.6 copy-start.5
  85.8 4.8 %copy-start.6 = (bf16[384,128]{1,0:T(8,128)(2,1)S(1)}, bf16[384,128]{1,0:T(8,128)(2,1)}, u32[]{:S(2)}) copy-start(bf16[384,128]{1,0:T(8,128)(2,1)} %copy-done.5) | copy-start | bytes 294916
  85.8 5.9 %copy-start.4 = (bf16[384,128]{1,0:T(8,128)(2,1)S(1)}, bf16[384,128]{1,0:T(8,128)(2,1)}, u32[]{:S(2)}) copy-start(bf16[384,128]{1,0:T(8,128)(2,1)} %copy-done.3) | copy-start | bytes 294916
  85.8 7.7 %copy-start.2 = (bf16[384,128]{1,0:T(8,128)(2,1)S(1)}, bf16[384,128]{1,0:T(8,128)(2,1)}, u32[]{:S(2)}) copy-start(bf16[384,128]{1,0:T(8,128)(2,1)} %copy-done.1) | copy-start | bytes 294916
  85.8 29.4 %all-to-all-start.2 = ((bf16[8,640,128]{2,1,0:T(8,128)(2,1)}), bf16[8,640,128]{2,1,0:T(8,128)(2,1)S(1)}, u32[]{:S(2)}, u32[]{:S(2)}) async-start(bf16[8,640,128]{2,1,0:T(8,128)(2,1)} %copy-done), calls=%async_computation.2 | async-start | bytes 2621440 | tf_op jit(solution)/shard_map/all_to_all | solution.py:766
  90.5 18.3 %collective-permute-start.9 = (bf16[384,128]{1,0:T(8,128)(2,1)S(1)}, bf16[384,128]{1,0:T(8,128)(2,1)S(1)}, u32[]{:S(2)}, u32[]{:S(2)}) collective-permute-start(bf16[384,128]{1,0:T(8,128)(2,1)S(1)} %copy-done.6), channel_id=1, source_target_pairs={{0,8},{1,9},{2,10},{3,11},{4,12},{5,13},{6,14},{7,15},{8,0},{9,1},... | collective-permute-start | bytes 294920 | tf_op jit(solution)/shard_map/ppermute | solution.py:761
  91.7 19.9 %collective-permute-start.10 = (bf16[384,128]{1,0:T(8,128)(2,1)S(1)}, bf16[384,128]{1,0:T(8,128)(2,1)S(1)}, u32[]{:S(2)}, u32[]{:S(2)}) collective-permute-start(bf16[384,128]{1,0:T(8,128)(2,1)S(1)} %copy-done.4), channel_id=1, source_target_pairs={{0,9},{1,8},{2,11},{3,10},{4,13},{5,12},{6,15},{7,14},{8,1},{9,0},... | collective-permute-start | bytes 294920 | tf_op jit(solution)/shard_map/ppermute | solution.py:761
  93.4 20.5 %collective-permute-start.11 = (bf16[384,128]{1,0:T(8,128)(2,1)S(1)}, bf16[384,128]{1,0:T(8,128)(2,1)S(1)}, u32[]{:S(2)}, u32[]{:S(2)}) collective-permute-start(bf16[384,128]{1,0:T(8,128)(2,1)S(1)} %copy-done.2), channel_id=1, source_target_pairs={{0,10},{1,11},{2,8},{3,9},{4,14},{5,15},{6,12},{7,13},{8,2},{9,3},... | collective-permute-start | bytes 294920 | tf_op jit(solution)/shard_map/ppermute | solution.py:761
  95.5 22.6 %collective-permute-start.12 = (bf16[384,128]{1,0:T(8,128)(2,1)S(1)}, bf16[384,128]{1,0:T(8,128)(2,1)S(1)}, u32[]{:S(2)}, u32[]{:S(2)}) collective-permute-start(bf16[384,128]{1,0:T(8,128)(2,1)S(1)} %get-tuple-element.52), channel_id=1, source_target_pairs={{0,11},{1,10},{2,9},{3,8},{4,15},{5,14},{6,13},{7,12},{8,3},{9,2},... | collective-permute-start | bytes 294920 | tf_op jit(solution)/shard_map/ppermute | solution.py:761
  96.7 22.4 %collective-permute-start.13 = (bf16[384,128]{1,0:T(8,128)(2,1)S(1)}, bf16[384,128]{1,0:T(8,128)(2,1)S(1)}, u32[]{:S(2)}, u32[]{:S(2)}) collective-permute-start(bf16[384,128]{1,0:T(8,128)(2,1)S(1)} %get-tuple-element.53), channel_id=1, source_target_pairs={{0,12},{1,13},{2,14},{3,15},{4,8},{5,9},{6,10},{7,11},{8,4},{9,5},... | collective-permute-start | bytes 294920 | tf_op jit(solution)/shard_map/ppermute | solution.py:761
  108.8 17.3 %collective-permute-start.14 = (bf16[384,128]{1,0:T(8,128)(2,1)S(1)}, bf16[384,128]{1,0:T(8,128)(2,1)S(1)}, u32[]{:S(2)}, u32[]{:S(2)}) collective-permute-start(bf16[384,128]{1,0:T(8,128)(2,1)S(1)} %get-tuple-element.54), channel_id=1, source_target_pairs={{0,13},{1,12},{2,15},{3,14},{4,9},{5,8},{6,11},{7,10},{8,5},{9,4},... | collective-permute-start | bytes 294920 | tf_op jit(solution)/shard_map/ppermute | solution.py:761
  111.6 17.5 %collective-permute-start.15 = (bf16[384,128]{1,0:T(8,128)(2,1)S(1)}, bf16[384,128]{1,0:T(8,128)(2,1)S(1)}, u32[]{:S(2)}, u32[]{:S(2)}) collective-permute-start(bf16[384,128]{1,0:T(8,128)(2,1)S(1)} %get-tuple-element.55), channel_id=1, source_target_pairs={{0,14},{1,15},{2,12},{3,13},{4,10},{5,11},{6,8},{7,9},{8,6},{9,7},... | collective-permute-start | bytes 294920 | tf_op jit(solution)/shard_map/ppermute | solution.py:761
  114.0 17.3 %collective-permute-start.16 = (bf16[384,128]{1,0:T(8,128)(2,1)S(1)}, bf16[384,128]{1,0:T(8,128)(2,1)S(1)}, u32[]{:S(2)}, u32[]{:S(2)}) collective-permute-start(bf16[384,128]{1,0:T(8,128)(2,1)S(1)} %get-tuple-element.56), channel_id=1, source_target_pairs={{0,15},{1,14},{2,13},{3,12},{4,11},{5,10},{6,9},{7,8},{8,7},{9,6},... | collective-permute-start | bytes 294920 | tf_op jit(solution)/shard_map/ppermute | solution.py:761

commit v14 on v13

--- a/solution.py
+++ b/solution.py
@@ -522,9 +522,11 @@
     lax.fori_loop(0, lines // TILE // tiles, step, 0)
     equal = jnp.where(same_line(total), pairs[...], 0.0)
     exact = {"precision": lax.Precision.HIGHEST, "preferred_element_type": F32}
-    owner = owners(total, F32)
-    half_way = jnp.dot(equal, owner, **exact)
-    gram = lax.dot_general(owner, half_way, (((0,), (0,)), ((), ())), **exact)
+    rows = jnp.sum(equal.reshape(total, TILE, wide), axis=1)
+    gram = jnp.dot(rows, owners(total, F32), **exact)
+    row = lax.broadcasted_iota(jnp.int32, (total, total), 0)
+    col = lax.broadcasted_iota(jnp.int32, (total, total), 1)
+    gram = jnp.dot((row == device_at(col, half)).astype(F32), gram, **exact)
     gram = jnp.concatenate([gram, jnp.zeros((total, LANES - total), F32)], axis=1)
     out_ref[...] = jnp.broadcast_to(gram[None], out_ref.shape)
 
@@ -653,8 +655,8 @@
     total = 2 * half
     far_refs, refs = refs[:half], refs[half:]
     across_ref, raw_observed, raw_precision, numbers_ref, grams_ref, *refs = refs
-    group_refs, near_out, far_outs = refs[: len(groups)], refs[len(groups)], refs[len(groups) + 1 : -5]
-    mixer, own, grads, raw_grads, sems = refs[-5:]
+    group_refs, near_to, far_tos = refs[: len(groups)], refs[len(groups)], refs[len(groups) + 1 : -8]
+    near_out, far_out, mixer, own, grads, raw_grads, sems, out_sems = refs[-8:]
     wide = total * TILE
     high = half * TILE
     fetches = []
@@ -697,6 +699,14 @@
     for fetch in fetches:
         fetch.wait()
 
+    def near_store(i):
+        part = lines_of(i * BLOCK, BLOCK)
+        return pltpu.make_async_copy(near_out.at[:, part, :], near_to.at[:, part, :], out_sems.at[i, 0])
+
+    def far_store(x, i):
+        part = lines_of(i * BLOCK - raw, BLOCK)
+        return pltpu.make_async_copy(far_out.at[x, part, :], far_tos[x].at[part, :], out_sems.at[i, 1 + x])
+
     def slab_step(with_far, i, carry):
         rows = wide if with_far else high
         for t in range(BLOCK // TILE):
@@ -708,8 +718,11 @@
             new = mix(mixer.at[:rows, :], own.at[:rows, :], numbers_ref, total, states, slopes)
             near_out[:, part, :] = new[:high].reshape(half, TILE, LANES)
             if with_far:
-                for x, far_out in enumerate(far_outs):
-                    far_out[lines_of(at - raw, TILE), :] = new[high + x * TILE : high + (x + 1) * TILE]
+                far_out[:, lines_of(at - raw, TILE), :] = new[high:].reshape(half, TILE, LANES)
+        near_store(i).start()
+        if with_far:
+            for x in range(half):
+                far_store(x, i).start()
         return carry
 
     here = lax.axis_index("slab").astype(jnp.int32) % half
@@ -726,33 +739,48 @@
             states, slopes = jnp.concatenate(states, axis=0), jnp.concatenate(slopes, axis=0)
             new = mix(mixer.at[:high, :], own.at[:high, :], numbers_ref, total, states, slopes)
             near_out[:, lines_of(lines + at, TILE), :] = new.reshape(half, TILE, LANES)
+        near_store(lines // BLOCK + i).start()
+        return carry
+
+    def finish(i, carry):
+        near_store(i).wait()
+        return carry
+
+    def finish_far(i, carry):
+        for x in range(half):
+            far_store(x, i).wait()
         return carry
 
     lax.fori_loop(0, raw // BLOCK, raw_step, 0)
     lax.fori_loop(0, raw // BLOCK, functools.partial(slab_step, False), 0)
     lax.fori_loop(raw // BLOCK, lines // BLOCK, functools.partial(slab_step, True), 0)
+    lax.fori_loop(0, (lines + raw) // BLOCK, finish, 0)
+    lax.fori_loop(raw // BLOCK, lines // BLOCK, finish_far, 0)
 
 
 def update_pieces(numbers, grams, near, far, across, raw_fields, grads, groups, raw, lines):
     half = len(far)
     total = 2 * half
     wide = total * TILE
-    out_shape = [jax.ShapeDtypeStruct((half, lines + raw, LANES), BF16)]
-    out_shape += [jax.ShapeDtypeStruct((lines - raw, LANES), BF16)] * half
+    out_shape = [pltpu.HBM((half, lines + raw, LANES), BF16)]
+    out_shape += [pltpu.HBM((lines - raw, LANES), BF16)] * half
     return call(
         functools.partial(update_pieces_body, half, raw, lines, groups),
         "update_pieces",
         flops=4 * wide * wide * LANES * (lines // TILE),
         moved=6 * total * lines * LANES,
         in_specs=[IN_VMEM] * (half + 6) + [IN_HBM] * len(groups),
-        out_specs=[IN_VMEM] * len(out_shape),
+        out_specs=[IN_HBM] * len(out_shape),
         out_shape=out_shape,
         scratch_shapes=[
+            pltpu.VMEM((half, lines + raw, LANES), BF16),
+            pltpu.VMEM((half, lines - raw, LANES), BF16),
             pltpu.VMEM((wide, wide), BF16),
             pltpu.VMEM((wide, LANES), F32),
             pltpu.VMEM((total, lines, LANES), BF16),
             pltpu.VMEM((total, raw, LANES), BF16),
             pltpu.SemaphoreType.DMA((total,)),
+            pltpu.SemaphoreType.DMA(((lines + raw) // BLOCK, 1 + half)),
         ],
     )(near, *far, across, *raw_fields, numbers, grams, *grads)
 

time: 132 us -> 131 us (level)
  local copies, waits for them, and re-layouts: 2.97 us -> 0.03 us
  Pallas kernels: 25.9 us -> 27.3 us
    unnamed x14 -> x16, local copies, waits for them, and re-layouts: 2.97 us -> 0.03 us
    pallas_call x1, Pallas kernels: 4.67 us -> 6.27 us  [update_pieces(): call(functools.partial(update_pieces_body, half, raw, lines, groups), 'up...]
where the time goes in v14:
time: 131 us
  waiting for transfers between devices  68.4 us (52%)
  starting transfers between devices  33 us (25%)
  Pallas kernels  27.3 us (21%)
  between operations  2.13 us (2%)
    ppermute x17, waiting for transfers between devices, exchange(): return lax.ppermute(piece, 'slab', [(i, i ^ k) for i in range(slabs)])  65.5 us
    ppermute x17, starting transfers between devices, exchange(): return lax.ppermute(piece, 'slab', [(i, i ^ k) for i in range(slabs)])  17.9 us
    all_to_all x2, starting transfers between devices, swap_near(): lax.all_to_all(pieces, 'slab', 0, 0, axis_index_groups=groups, tiled=True)  9.37 us
    pallas_call x3, Pallas kernels, gradient_pieces(): call(functools.partial(gradient_pieces_body, views, len(arrays), len(numb...  7.36 us
    pallas_call x1, Pallas kernels, update_pieces(): call(functools.partial(update_pieces_body, half, raw, lines, groups), 'up...  6.27 us
    all_to_all x1, starting transfers between devices, swap(): lax.all_to_all(slabs, 'slab', split_axis=0, concat_axis=0, tiled=True)  5.75 us
    pallas_call x4, Pallas kernels, join_pieces(): call(functools.partial(join_pieces_body, pieces, slabs // 2, raw, NCELL /...  5.54 us
    pallas_call x1, Pallas kernels, split_pieces(): call(functools.partial(split_pieces_body, slabs, raw, lines, len(fields))...  4.88 us
  transfers between devices with their start and end apart: 20, of which 15 were waited for; matrix products, arithmetic and copies ran while one was open for 0% of the time, Pallas kernels for 12%

profile of v14, /device:TPU:9, one launch (start us, length us, event | category | flops | bytes accessed | tf_op | source)
XLA Modules:
  0.0 130.8 jit_solution(3678011143714583160)
XLA Ops:
  0.0 4.9 %split_pieces.1 = (bf16[8,672,128]{2,1,0:T(8,128)(2,1)}, bf16[528,128]{1,0:T(8,128)(2,1)S(1)}, bf16[528,128]{1,0:T(8,128)(2,1)S(1)}, bf16[528,128]{1,0:T(8,128)(...) custom-call(bf16[1,1048576]{1,0:T(2,128)(2,1)} %row_ref.1, ...), custom_call_target="tpu_custom_call" | custom-call | bytes 7372800 | tf_op jit(solution)/shard_map/split_pieces/pallas_call | solution.py:445
  4.9 4.6 %all-to-all-start = ((bf16[8,672,128]{2,1,0:T(8,128)(2,1)}), bf16[8,672,128]{2,1,0:T(8,128)(2,1)S(1)}, u32[]{:S(2)}, u32[]{:S(2)}) async-start(bf16[8,672,128]{2,1,0:T(8,128)(2,1)} %get-tuple-element.31), calls=%async_computation | async-start | bytes 2752512 | tf_op jit(solution)/shard_map/all_to_all | solution.py:794
  9.5 2.3 %collective-permute-start = (bf16[528,128]{1,0:T(8,128)(2,1)S(1)}, bf16[528,128]{1,0:T(8,128)(2,1)S(1)}, u32[]{:S(2)}, u32[]{:S(2)}) collective-permute-start(bf16[528,128]{1,0:T(8,128)(2,1)S(1)} %get-tuple-element.32), channel_id=1, source_target_pairs={{0,8},{1,9},{2,10},{3,11},{4,12},{5,13},{6,14},{7,15},{8,0},{9,1},... | collective-permute-start | bytes 405512 | tf_op jit(solution)/shard_map/ppermute | solution.py:789
  11.8 0.6 collective-permute-start.1
  12.4 3.2 %collective-permute-start.2 = (bf16[528,128]{1,0:T(8,128)(2,1)S(1)}, bf16[528,128]{1,0:T(8,128)(2,1)S(1)}, u32[]{:S(2)}, u32[]{:S(2)}) collective-permute-start(bf16[528,128]{1,0:T(8,128)(2,1)S(1)} %get-tuple-element.34), channel_id=1, source_target_pairs={{0,10},{1,11},{2,8},{3,9},{4,14},{5,15},{6,12},{7,13},{8,2},{9,3},... | collective-permute-start | bytes 405512 | tf_op jit(solution)/shard_map/ppermute | solution.py:789
  15.6 0.3 collective-permute-start.3
  15.9 1.0 collective-permute-start.4
  16.9 13.5 %collective-permute-done.refs_0_ = bf16[528,128]{1,0:T(8,128)(2,1)S(1)} collective-permute-done((bf16[528,128]{1,0:T(8,128)(2,1)S(1)}, bf16[528,128]{1,0:T(8,128)(2,1)S(1)}, u32[]{:S(2)}, u32[]{:S(2)}) %collective-permute-start) | collective-permute-done | bytes 135200 | tf_op jit(solution)/shard_map/ppermute | solution.py:789
  30.4 0.0 collective-permute-start.5
  30.4 3.6 %collective-permute-done.1.refs_1_ = bf16[528,128]{1,0:T(8,128)(2,1)S(1)} collective-permute-done((bf16[528,128]{1,0:T(8,128)(2,1)S(1)}, bf16[528,128]{1,0:T(8,128)(2,1)S(1)}, u32[]{:S(2)}, u32[]{:S(2)}) %collective-permute-start.1) | collective-permute-done | bytes 135200 | tf_op jit(solution)/shard_map/ppermute | solution.py:789
  34.0 0.3 collective-permute-start.6
  34.3 2.8 %collective-permute-done.2.refs_2_ = bf16[528,128]{1,0:T(8,128)(2,1)S(1)} collective-permute-done((bf16[528,128]{1,0:T(8,128)(2,1)S(1)}, bf16[528,128]{1,0:T(8,128)(2,1)S(1)}, u32[]{:S(2)}, u32[]{:S(2)}) %collective-permute-start.2) | collective-permute-done | bytes 135200 | tf_op jit(solution)/shard_map/ppermute | solution.py:789
  37.1 0.0 collective-permute-start.7
  39.1 1.7 %collective-permute-done.3.refs_3_ = bf16[528,128]{1,0:T(8,128)(2,1)S(1)} collective-permute-done((bf16[528,128]{1,0:T(8,128)(2,1)S(1)}, bf16[528,128]{1,0:T(8,128)(2,1)S(1)}, u32[]{:S(2)}, u32[]{:S(2)}) %collective-permute-start.3) | collective-permute-done | bytes 135200 | tf_op jit(solution)/shard_map/ppermute | solution.py:789
  40.7 1.8 %gradient_pieces.3 = (bf16[4,512,128]{2,1,0:T(8,128)(2,1)}, f32[8,128]{1,0:T(8,128)S(1)}) custom-call(bf16[528,128]{1,0:T(8,128)(2,1)S(1)} %collective-permute-done.refs_0_, bf16[528,128]{1,0:T(8,128)(2,1)S(1)} %collective-permute-done.1.refs_1_, bf16[528,128]{1,0:T(8,128)(2,1)S(1)} %collective-permute-done.2.refs_2_, ...), custom_call_target="tpu_custom_call" | custom-call | flops 7864320 | bytes 2097152 | tf_op jit(solution)/shard_map/gradient_pieces/pallas_call | solution.py:610
  42.5 6.7 %collective-permute-done.4.refs_4_.refs_0_ = bf16[528,128]{1,0:T(8,128)(2,1)S(1)} collective-permute-done((bf16[528,128]{1,0:T(8,128)(2,1)S(1)}, bf16[528,128]{1,0:T(8,128)(2,1)S(1)}, u32[]{:S(2)}, u32[]{:S(2)}) %collective-permute-start.4) | collective-permute-done | bytes 135200 | tf_op jit(solution)/shard_map/ppermute | solution.py:789
  49.2 4.7 %collective-permute-done.5.refs_5_.refs_1_ = bf16[528,128]{1,0:T(8,128)(2,1)S(1)} collective-permute-done((bf16[528,128]{1,0:T(8,128)(2,1)S(1)}, bf16[528,128]{1,0:T(8,128)(2,1)S(1)}, u32[]{:S(2)}, u32[]{:S(2)}) %collective-permute-start.5) | collective-permute-done | bytes 135200 | tf_op jit(solution)/shard_map/ppermute | solution.py:789
  54.0 3.8 %collective-permute-done.6.refs_6_.refs_2_ = bf16[528,128]{1,0:T(8,128)(2,1)S(1)} collective-permute-done((bf16[528,128]{1,0:T(8,128)(2,1)S(1)}, bf16[528,128]{1,0:T(8,128)(2,1)S(1)}, u32[]{:S(2)}, u32[]{:S(2)}) %collective-permute-start.6) | collective-permute-done | bytes 135200 | tf_op jit(solution)/shard_map/ppermute | solution.py:789
  57.8 2.9 %collective-permute-done.7.refs_7_.refs_3_ = bf16[528,128]{1,0:T(8,128)(2,1)S(1)} collective-permute-done((bf16[528,128]{1,0:T(8,128)(2,1)S(1)}, bf16[528,128]{1,0:T(8,128)(2,1)S(1)}, u32[]{:S(2)}, u32[]{:S(2)}) %collective-permute-start.7) | collective-permute-done | bytes 135200 | tf_op jit(solution)/shard_map/ppermute | solution.py:789
  60.7 0.0 all-to-all-done.near_ref.refs_0_
  60.7 0.1 collective-permute-start.8
  60.8 3.2 %gram_pieces.1 = f32[16,16,128]{2,1,0:T(8,128)} custom-call(bf16[8,672,128]{2,1,0:T(8,128)(2,1)S(1)} %all-to-all-done.near_ref.refs_0_, bf16[528,128]{1,0:T(8,128)(2,1)S(1)} %collective-permute-done.refs_0_, bf16[528,128]{1,0:T(8,128)(2,1)S(1)} %collective-permute-done.1.refs_1_, bf16[528,128]{1,0:T(8,128)(2,1)S(1)} %collective-permute-done.2.refs_2_, ...), custom_call_target="tpu_custom_call" | custom-call | flops 536870912 | bytes 2097152 | tf_op jit(solution)/shard_map/gram_pieces/pallas_call | solution.py:537
  64.0 5.8 %all-to-all-start.1 = ((f32[16,16,128]{2,1,0:T(8,128)}), f32[16,16,128]{2,1,0:T(8,128)S(1)}, u32[]{:S(2)}, u32[]{:S(2)}) async-start(f32[16,16,128]{2,1,0:T(8,128)} %gram_pieces.1), calls=%async_computation.1 | async-start | bytes 262144 | tf_op jit(solution)/shard_map/all_to_all | solution.py:365
  69.7 2.4 %gradient_pieces.4 = (bf16[4,512,128]{2,1,0:T(8,128)(2,1)}, f32[8,128]{1,0:T(8,128)}) custom-call(bf16[528,128]{1,0:T(8,128)(2,1)S(1)} %collective-permute-done.4.refs_4_.refs_0_, bf16[528,128]{1,0:T(8,128)(2,1)S(1)} %collective-permute-done.5.refs_5_.refs_1_, bf16[528,128]{1,0:T(8,128)(2,1)S(1)} %collective-permute-done.6.refs_6_.refs_2_, ...), custom_call_target="tpu_custom_call" | custom-call | flops 7864320 | bytes 2097152 | tf_op jit(solution)/shard_map/gradient_pieces/pallas_call | solution.py:610
  72.1 3.2 %gradient_pieces.5 = (bf16[8,512,128]{2,1,0:T(8,128)(2,1)}, f32[8,128]{1,0:T(8,128)}) custom-call(bf16[8,672,128]{2,1,0:T(8,128)(2,1)S(1)} %all-to-all-done.near_ref.refs_0_, bf16[512,128]{1,0:T(8,128)(2,1)S(1)} %get-tuple-element.42.refs_4_.refs_1_, bf16[512,128]{1,0:T(8,128)(2,1)S(1)} %get-tuple-element.43.refs_5_.refs_2_), custom_call_target="tpu_custom_call" | custom-call | flops 15728640 | bytes 4194304 | tf_op jit(solution)/shard_map/gradient_pieces/pallas_call | solution.py:610
  75.3 2.8 %all-to-all-done.1.refs_12_ = f32[16,16,128]{2,1,0:T(8,128)S(1)} async-done(((f32[16,16,128]{2,1,0:T(8,128)}), f32[16,16,128]{2,1,0:T(8,128)S(1)}, u32[]{:S(2)}, u32[]{:S(2)}) %all-to-all-start.1) | async-done | bytes 131104 | tf_op jit(solution)/shard_map/all_to_all | solution.py:365
  78.1 0.0 collective-permute-done.8.refs_8_
  78.1 6.3 %update_pieces.1 = (bf16[8,640,128]{2,1,0:T(8,128)(2,1)}, bf16[384,128]{1,0:T(8,128)(2,1)}, bf16[384,128]{1,0:T(8,128)(2,1)}, bf16[384,128]{1,0:T(8,128)(2,1)}, ...) custom-call(bf16[8,672,128]{2,1,0:T(8,128)(2,1)S(1)} %all-to-all-don, ...), custom_call_target="tpu_custom_call" | custom-call | flops 1073741824 | bytes 6291456 | tf_op jit(solution)/shard_map/update_pieces/pallas_call | solution.py:767
  84.5 4.8 %all-to-all-start.2 = ((bf16[8,640,128]{2,1,0:T(8,128)(2,1)}), bf16[8,640,128]{2,1,0:T(8,128)(2,1)S(1)}, u32[]{:S(2)}, u32[]{:S(2)}) async-start(bf16[8,640,128]{2,1,0:T(8,128)(2,1)} %get-tuple-element.48), calls=%async_computation.2 | async-start | bytes 2621440 | tf_op jit(solution)/shard_map/all_to_all | solution.py:794
  89.3 1.2 collective-permute-start.9
  90.4 1.7 %collective-permute-start.10 = (bf16[384,128]{1,0:T(8,128)(2,1)S(1)}, bf16[384,128]{1,0:T(8,128)(2,1)S(1)}, u32[]{:S(2)}, u32[]{:S(2)}) collective-permute-start(bf16[384,128]{1,0:T(8,128)(2,1)S(1)} %copy-done.6), channel_id=1, source_target_pairs={{0,9},{1,8},{2,11},{3,10},{4,13},{5,12},{6,15},{7,14},{8,1},{9,0},... | collective-permute-start | bytes 294920 | tf_op jit(solution)/shard_map/ppermute | solution.py:789
  92.2 2.1 %collective-permute-start.11 = (bf16[384,128]{1,0:T(8,128)(2,1)S(1)}, bf16[384,128]{1,0:T(8,128)(2,1)S(1)}, u32[]{:S(2)}, u32[]{:S(2)}) collective-permute-start(bf16[384,128]{1,0:T(8,128)(2,1)S(1)} %copy-done.5), channel_id=1, source_target_pairs={{0,10},{1,11},{2,8},{3,9},{4,14},{5,15},{6,12},{7,13},{8,2},{9,3},... | collective-permute-start | bytes 294920 | tf_op jit(solution)/shard_map/ppermute | solution.py:789
  94.2 1.2 collective-permute-start.12
  95.5 0.0 collective-permute-start.13
  95.5 12.0 %collective-permute-done.9.refs_1_ = bf16[384,128]{1,0:T(8,128)(2,1)S(1)} collective-permute-done((bf16[384,128]{1,0:T(8,128)(2,1)S(1)}, bf16[384,128]{1,0:T(8,128)(2,1)S(1)}, u32[]{:S(2)}, u32[]{:S(2)}) %collective-permute-start.9) | collective-permute-done | bytes 98336 | tf_op jit(solution)/shard_map/ppermute | solution.py:789
  107.6 1.1 collective-permute-start.14
  108.7 1.6 %collective-permute-done.10.refs_2_ = bf16[384,128]{1,0:T(8,128)(2,1)S(1)} collective-permute-done((bf16[384,128]{1,0:T(8,128)(2,1)S(1)}, bf16[384,128]{1,0:T(8,128)(2,1)S(1)}, u32[]{:S(2)}, u32[]{:S(2)}) %collective-permute-start.10) | collective-permute-done | bytes 98336 | tf_op jit(solution)/shard_map/ppermute | solution.py:789
  110.3 1.5 %collective-permute-start.15 = (bf16[384,128]{1,0:T(8,128)(2,1)S(1)}, bf16[384,128]{1,0:T(8,128)(2,1)S(1)}, u32[]{:S(2)}, u32[]{:S(2)}) collective-permute-start(bf16[384,128]{1,0:T(8,128)(2,1)S(1)} %copy-done.1), channel_id=1, source_target_pairs={{0,14},{1,15},{2,12},{3,13},{4,10},{5,11},{6,8},{7,9},{8,6},{9,7},... | collective-permute-start | bytes 294920 | tf_op jit(solution)/shard_map/ppermute | solution.py:789
  111.8 0.9 collective-permute-done.11.refs_3_
  112.7 1.2 collective-permute-start.16
  113.9 0.0 all-to-all-done.2.refs_0_
  113.9 3.0 %join_pieces.4.refs_0_ = bf16[1,1048576]{1,0:T(2,128)(2,1)} custom-call(bf16[8,640,128]{2,1,0:T(8,128)(2,1)S(1)} %all-to-all-done.2.refs_0_), custom_call_target="tpu_custom_call" | custom-call | bytes 3932160 | tf_op jit(solution)/shard_map/join_pieces/pallas_call | solution.py:483
  116.9 1.0 join_pieces.5.refs_0_
  117.9 7.0 %collective-permute-done.14.refs_2_ = bf16[384,128]{1,0:T(8,128)(2,1)S(1)} collective-permute-done((bf16[384,128]{1,0:T(8,128)(2,1)S(1)}, bf16[384,128]{1,0:T(8,128)(2,1)S(1)}, u32[]{:S(2)}, u32[]{:S(2)}) %collective-permute-start.14) | collective-permute-done | bytes 98336 | tf_op jit(solution)/shard_map/ppermute | solution.py:789
  124.8 0.8 join_pieces.6.refs_0_
  125.6 2.2 %collective-permute-done.15.refs_1_ = bf16[384,128]{1,0:T(8,128)(2,1)S(1)} collective-permute-done((bf16[384,128]{1,0:T(8,128)(2,1)S(1)}, bf16[384,128]{1,0:T(8,128)(2,1)S(1)}, u32[]{:S(2)}, u32[]{:S(2)}) %collective-permute-start.15) | collective-permute-done | bytes 98336 | tf_op jit(solution)/shard_map/ppermute | solution.py:789
  127.8 2.1 %collective-permute-done.16.refs_2_ = bf16[384,128]{1,0:T(8,128)(2,1)S(1)} collective-permute-done((bf16[384,128]{1,0:T(8,128)(2,1)S(1)}, bf16[384,128]{1,0:T(8,128)(2,1)S(1)}, u32[]{:S(2)}, u32[]{:S(2)}) %collective-permute-start.16) | collective-permute-done | bytes 98336 | tf_op jit(solution)/shard_map/ppermute | solution.py:789
  130.0 0.8 join_pieces.7
  (19 shorter events, 0.1 us)
Async XLA Ops:
  4.9 55.8 %all-to-all-start = ((bf16[8,672,128]{2,1,0:T(8,128)(2,1)}), bf16[8,672,128]{2,1,0:T(8,128)(2,1)S(1)}, u32[]{:S(2)}, u32[]{:S(2)}) async-start(bf16[8,672,128]{2,1,0:T(8,128)(2,1)} %get-tuple-element.31), calls=%async_computation | async-start | bytes 2752512 | tf_op jit(solution)/shard_map/all_to_all | solution.py:794
  9.5 20.9 %collective-permute-start = (bf16[528,128]{1,0:T(8,128)(2,1)S(1)}, bf16[528,128]{1,0:T(8,128)(2,1)S(1)}, u32[]{:S(2)}, u32[]{:S(2)}) collective-permute-start(bf16[528,128]{1,0:T(8,128)(2,1)S(1)} %get-tuple-element.32), channel_id=1, source_target_pairs={{0,8},{1,9},{2,10},{3,11},{4,12},{5,13},{6,14},{7,15},{8,0},{9,1},... | collective-permute-start | bytes 405512 | tf_op jit(solution)/shard_map/ppermute | solution.py:789
  11.8 22.2 %collective-permute-start.1 = (bf16[528,128]{1,0:T(8,128)(2,1)S(1)}, bf16[528,128]{1,0:T(8,128)(2,1)S(1)}, u32[]{:S(2)}, u32[]{:S(2)}) collective-permute-start(bf16[528,128]{1,0:T(8,128)(2,1)S(1)} %get-tuple-element.33), channel_id=1, source_target_pairs={{0,9},{1,8},{2,11},{3,10},{4,13},{5,12},{6,15},{7,14},{8,1},{9,0},... | collective-permute-start | bytes 405512 | tf_op jit(solution)/shard_map/ppermute | solution.py:789
  12.4 24.8 %collective-permute-start.2 = (bf16[528,128]{1,0:T(8,128)(2,1)S(1)}, bf16[528,128]{1,0:T(8,128)(2,1)S(1)}, u32[]{:S(2)}, u32[]{:S(2)}) collective-permute-start(bf16[528,128]{1,0:T(8,128)(2,1)S(1)} %get-tuple-element.34), channel_id=1, source_target_pairs={{0,10},{1,11},{2,8},{3,9},{4,14},{5,15},{6,12},{7,13},{8,2},{9,3},... | collective-permute-start | bytes 405512 | tf_op jit(solution)/shard_map/ppermute | solution.py:789
  15.6 25.2 %collective-permute-start.3 = (bf16[528,128]{1,0:T(8,128)(2,1)S(1)}, bf16[528,128]{1,0:T(8,128)(2,1)S(1)}, u32[]{:S(2)}, u32[]{:S(2)}) collective-permute-start(bf16[528,128]{1,0:T(8,128)(2,1)S(1)} %get-tuple-element.35), channel_id=1, source_target_pairs={{0,11},{1,10},{2,9},{3,8},{4,15},{5,14},{6,13},{7,12},{8,3},{9,2},... | collective-permute-start | bytes 405512 | tf_op jit(solution)/shard_map/ppermute | solution.py:789
  15.9 33.4 %collective-permute-start.4 = (bf16[528,128]{1,0:T(8,128)(2,1)S(1)}, bf16[528,128]{1,0:T(8,128)(2,1)S(1)}, u32[]{:S(2)}, u32[]{:S(2)}) collective-permute-start(bf16[528,128]{1,0:T(8,128)(2,1)S(1)} %get-tuple-element.36), channel_id=1, source_target_pairs={{0,12},{1,13},{2,14},{3,15},{4,8},{5,9},{6,10},{7,11},{8,4},{9,5},... | collective-permute-start | bytes 405512 | tf_op jit(solution)/shard_map/ppermute | solution.py:789
  30.4 23.6 %collective-permute-start.5 = (bf16[528,128]{1,0:T(8,128)(2,1)S(1)}, bf16[528,128]{1,0:T(8,128)(2,1)S(1)}, u32[]{:S(2)}, u32[]{:S(2)}) collective-permute-start(bf16[528,128]{1,0:T(8,128)(2,1)S(1)} %get-tuple-element.37), channel_id=1, source_target_pairs={{0,13},{1,12},{2,15},{3,14},{4,9},{5,8},{6,11},{7,10},{8,5},{9,4},... | collective-permute-start | bytes 405512 | tf_op jit(solution)/shard_map/ppermute | solution.py:789
  34.0 23.8 %collective-permute-start.6 = (bf16[528,128]{1,0:T(8,128)(2,1)S(1)}, bf16[528,128]{1,0:T(8,128)(2,1)S(1)}, u32[]{:S(2)}, u32[]{:S(2)}) collective-permute-start(bf16[528,128]{1,0:T(8,128)(2,1)S(1)} %get-tuple-element.38), channel_id=1, source_target_pairs={{0,14},{1,15},{2,12},{3,13},{4,10},{5,11},{6,8},{7,9},{8,6},{9,7},... | collective-permute-start | bytes 405512 | tf_op jit(solution)/shard_map/ppermute | solution.py:789
  37.1 23.5 %collective-permute-start.7 = (bf16[528,128]{1,0:T(8,128)(2,1)S(1)}, bf16[528,128]{1,0:T(8,128)(2,1)S(1)}, u32[]{:S(2)}, u32[]{:S(2)}) collective-permute-start(bf16[528,128]{1,0:T(8,128)(2,1)S(1)} %get-tuple-element.39), channel_id=1, source_target_pairs={{0,15},{1,14},{2,13},{3,12},{4,11},{5,10},{6,9},{7,8},{8,7},{9,6},... | collective-permute-start | bytes 405512 | tf_op jit(solution)/shard_map/ppermute | solution.py:789
  60.7 17.4 %collective-permute-start.8 = (bf16[8,144,128]{2,1,0:T(8,128)(2,1)S(1)}, bf16[8,144,128]{2,1,0:T(8,128)(2,1)S(1)}, u32[]{:S(2)}, u32[]{:S(2)}) collective-permute-start(bf16[8,144,128]{2,1,0:T(8,128)(2,1)S(1)} %raw_states.1.refs_9_), channel_id=1, source_target_pairs={{0,8},{1,9},{2,10},{3,11},{4,12},{5,13},{6,14},{7,15},{8,0},{9,1},... | collective-permute-start | bytes 884744 | tf_op jit(solution)/shard_map/ppermute | solution.py:789
  64.0 14.1 %all-to-all-start.1 = ((f32[16,16,128]{2,1,0:T(8,128)}), f32[16,16,128]{2,1,0:T(8,128)S(1)}, u32[]{:S(2)}, u32[]{:S(2)}) async-start(f32[16,16,128]{2,1,0:T(8,128)} %gram_pieces.1), calls=%async_computation.1 | async-start | bytes 262144 | tf_op jit(solution)/shard_map/all_to_all | solution.py:365
  84.4 4.9 %copy-start.7 = (bf16[384,128]{1,0:T(8,128)(2,1)S(1)}, bf16[384,128]{1,0:T(8,128)(2,1)}, u32[]{:S(2)}) copy-start(bf16[384,128]{1,0:T(8,128)(2,1)} %get-tuple-element.49) | copy-start | bytes 294916
  84.4 6.0 %copy-start.6 = (bf16[384,128]{1,0:T(8,128)(2,1)S(1)}, bf16[384,128]{1,0:T(8,128)(2,1)}, u32[]{:S(2)}) copy-start(bf16[384,128]{1,0:T(8,128)(2,1)} %get-tuple-element.50) | copy-start | bytes 294916
  84.4 7.7 %copy-start.5 = (bf16[384,128]{1,0:T(8,128)(2,1)S(1)}, bf16[384,128]{1,0:T(8,128)(2,1)}, u32[]{:S(2)}) copy-start(bf16[384,128]{1,0:T(8,128)(2,1)} %get-tuple-element.51) | copy-start | bytes 294916
  84.4 9.8 %copy-start.4 = (bf16[384,128]{1,0:T(8,128)(2,1)S(1)}, bf16[384,128]{1,0:T(8,128)(2,1)}, u32[]{:S(2)}) copy-start(bf16[384,128]{1,0:T(8,128)(2,1)} %get-tuple-element.52) | copy-start | bytes 294916
  84.4 11.0 %copy-start.3 = (bf16[384,128]{1,0:T(8,128)(2,1)S(1)}, bf16[384,128]{1,0:T(8,128)(2,1)}, u32[]{:S(2)}) copy-start(bf16[384,128]{1,0:T(8,128)(2,1)} %get-tuple-element.53) | copy-start | bytes 294916
  84.5 23.1 %copy-start.2 = (bf16[384,128]{1,0:T(8,128)(2,1)S(1)}, bf16[384,128]{1,0:T(8,128)(2,1)}, u32[]{:S(2)}) copy-start(bf16[384,128]{1,0:T(8,128)(2,1)} %get-tuple-element.54) | copy-start | bytes 294916
  84.5 25.9 %copy-start.1 = (bf16[384,128]{1,0:T(8,128)(2,1)S(1)}, bf16[384,128]{1,0:T(8,128)(2,1)}, u32[]{:S(2)}) copy-start(bf16[384,128]{1,0:T(8,128)(2,1)} %get-tuple-element.55) | copy-start | bytes 294916
  84.5 28.2 %copy-start = (bf16[384,128]{1,0:T(8,128)(2,1)S(1)}, bf16[384,128]{1,0:T(8,128)(2,1)}, u32[]{:S(2)}) copy-start(bf16[384,128]{1,0:T(8,128)(2,1)} %get-tuple-element.56) | copy-start | bytes 294916
  84.5 29.4 %all-to-all-start.2 = ((bf16[8,640,128]{2,1,0:T(8,128)(2,1)}), bf16[8,640,128]{2,1,0:T(8,128)(2,1)S(1)}, u32[]{:S(2)}, u32[]{:S(2)}) async-start(bf16[8,640,128]{2,1,0:T(8,128)(2,1)} %get-tuple-element.48), calls=%async_computation.2 | async-start | bytes 2621440 | tf_op jit(solution)/shard_map/all_to_all | solution.py:794
  89.3 18.3 %collective-permute-start.9 = (bf16[384,128]{1,0:T(8,128)(2,1)S(1)}, bf16[384,128]{1,0:T(8,128)(2,1)S(1)}, u32[]{:S(2)}, u32[]{:S(2)}) collective-permute-start(bf16[384,128]{1,0:T(8,128)(2,1)S(1)} %copy-done.7), channel_id=1, source_target_pairs={{0,8},{1,9},{2,10},{3,11},{4,12},{5,13},{6,14},{7,15},{8,0},{9,1},... | collective-permute-start | bytes 294920 | tf_op jit(solution)/shard_map/ppermute | solution.py:789
  90.4 19.9 %collective-permute-start.10 = (bf16[384,128]{1,0:T(8,128)(2,1)S(1)}, bf16[384,128]{1,0:T(8,128)(2,1)S(1)}, u32[]{:S(2)}, u32[]{:S(2)}) collective-permute-start(bf16[384,128]{1,0:T(8,128)(2,1)S(1)} %copy-done.6), channel_id=1, source_target_pairs={{0,9},{1,8},{2,11},{3,10},{4,13},{5,12},{6,15},{7,14},{8,1},{9,0},... | collective-permute-start | bytes 294920 | tf_op jit(solution)/shard_map/ppermute | solution.py:789
  92.2 20.5 %collective-permute-start.11 = (bf16[384,128]{1,0:T(8,128)(2,1)S(1)}, bf16[384,128]{1,0:T(8,128)(2,1)S(1)}, u32[]{:S(2)}, u32[]{:S(2)}) collective-permute-start(bf16[384,128]{1,0:T(8,128)(2,1)S(1)} %copy-done.5), channel_id=1, source_target_pairs={{0,10},{1,11},{2,8},{3,9},{4,14},{5,15},{6,12},{7,13},{8,2},{9,3},... | collective-permute-start | bytes 294920 | tf_op jit(solution)/shard_map/ppermute | solution.py:789
  94.2 22.6 %collective-permute-start.12 = (bf16[384,128]{1,0:T(8,128)(2,1)S(1)}, bf16[384,128]{1,0:T(8,128)(2,1)S(1)}, u32[]{:S(2)}, u32[]{:S(2)}) collective-permute-start(bf16[384,128]{1,0:T(8,128)(2,1)S(1)} %copy-done.4), channel_id=1, source_target_pairs={{0,11},{1,10},{2,9},{3,8},{4,15},{5,14},{6,13},{7,12},{8,3},{9,2},... | collective-permute-start | bytes 294920 | tf_op jit(solution)/shard_map/ppermute | solution.py:789
  95.5 22.4 %collective-permute-start.13 = (bf16[384,128]{1,0:T(8,128)(2,1)S(1)}, bf16[384,128]{1,0:T(8,128)(2,1)S(1)}, u32[]{:S(2)}, u32[]{:S(2)}) collective-permute-start(bf16[384,128]{1,0:T(8,128)(2,1)S(1)} %copy-done.3), channel_id=1, source_target_pairs={{0,12},{1,13},{2,14},{3,15},{4,8},{5,9},{6,10},{7,11},{8,4},{9,5},... | collective-permute-start | bytes 294920 | tf_op jit(solution)/shard_map/ppermute | solution.py:789
  107.6 17.3 %collective-permute-start.14 = (bf16[384,128]{1,0:T(8,128)(2,1)S(1)}, bf16[384,128]{1,0:T(8,128)(2,1)S(1)}, u32[]{:S(2)}, u32[]{:S(2)}) collective-permute-start(bf16[384,128]{1,0:T(8,128)(2,1)S(1)} %copy-done.2), channel_id=1, source_target_pairs={{0,13},{1,12},{2,15},{3,14},{4,9},{5,8},{6,11},{7,10},{8,5},{9,4},... | collective-permute-start | bytes 294920 | tf_op jit(solution)/shard_map/ppermute | solution.py:789
  110.3 17.5 %collective-permute-start.15 = (bf16[384,128]{1,0:T(8,128)(2,1)S(1)}, bf16[384,128]{1,0:T(8,128)(2,1)S(1)}, u32[]{:S(2)}, u32[]{:S(2)}) collective-permute-start(bf16[384,128]{1,0:T(8,128)(2,1)S(1)} %copy-done.1), channel_id=1, source_target_pairs={{0,14},{1,15},{2,12},{3,13},{4,10},{5,11},{6,8},{7,9},{8,6},{9,7},... | collective-permute-start | bytes 294920 | tf_op jit(solution)/shard_map/ppermute | solution.py:789
  112.7 17.3 %collective-permute-start.16 = (bf16[384,128]{1,0:T(8,128)(2,1)S(1)}, bf16[384,128]{1,0:T(8,128)(2,1)S(1)}, u32[]{:S(2)}, u32[]{:S(2)}) collective-permute-start(bf16[384,128]{1,0:T(8,128)(2,1)S(1)} %copy-done), channel_id=1, source_target_pairs={{0,15},{1,14},{2,13},{3,12},{4,11},{5,10},{6,9},{7,8},{8,7},{9,6},... | collective-permute-start | bytes 294920 | tf_op jit(solution)/shard_map/ppermute | solution.py:789

commit v15 on v14

--- a/solution.py
+++ b/solution.py
@@ -655,8 +655,8 @@
     total = 2 * half
     far_refs, refs = refs[:half], refs[half:]
     across_ref, raw_observed, raw_precision, numbers_ref, grams_ref, *refs = refs
-    group_refs, near_to, far_tos = refs[: len(groups)], refs[len(groups)], refs[len(groups) + 1 : -8]
-    near_out, far_out, mixer, own, grads, raw_grads, sems, out_sems = refs[-8:]
+    group_refs, near_to, far_outs = refs[: len(groups)], refs[len(groups)], refs[len(groups) + 1 : -7]
+    near_out, mixer, own, grads, raw_grads, sems, out_sems = refs[-7:]
     wide = total * TILE
     high = half * TILE
     fetches = []
@@ -701,11 +701,7 @@
 
     def near_store(i):
         part = lines_of(i * BLOCK, BLOCK)
-        return pltpu.make_async_copy(near_out.at[:, part, :], near_to.at[:, part, :], out_sems.at[i, 0])
-
-    def far_store(x, i):
-        part = lines_of(i * BLOCK - raw, BLOCK)
-        return pltpu.make_async_copy(far_out.at[x, part, :], far_tos[x].at[part, :], out_sems.at[i, 1 + x])
+        return pltpu.make_async_copy(near_out.at[:, part, :], near_to.at[:, part, :], out_sems.at[i])
 
     def slab_step(with_far, i, carry):
         rows = wide if with_far else high
@@ -718,11 +714,9 @@
             new = mix(mixer.at[:rows, :], own.at[:rows, :], numbers_ref, total, states, slopes)
             near_out[:, part, :] = new[:high].reshape(half, TILE, LANES)
             if with_far:
-                far_out[:, lines_of(at - raw, TILE), :] = new[high:].reshape(half, TILE, LANES)
+                for x, far_out in enumerate(far_outs):
+                    far_out[lines_of(at - raw, TILE), :] = new[high + x * TILE : high + (x + 1) * TILE]
         near_store(i).start()
-        if with_far:
-            for x in range(half):
-                far_store(x, i).start()
         return carry
 
     here = lax.axis_index("slab").astype(jnp.int32) % half
@@ -746,16 +740,10 @@
         near_store(i).wait()
         return carry
 
-    def finish_far(i, carry):
-        for x in range(half):
-            far_store(x, i).wait()
-        return carry
-
     lax.fori_loop(0, raw // BLOCK, raw_step, 0)
     lax.fori_loop(0, raw // BLOCK, functools.partial(slab_step, False), 0)
     lax.fori_loop(raw // BLOCK, lines // BLOCK, functools.partial(slab_step, True), 0)
     lax.fori_loop(0, (lines + raw) // BLOCK, finish, 0)
-    lax.fori_loop(raw // BLOCK, lines // BLOCK, finish_far, 0)
 
 
 def update_pieces(numbers, grams, near, far, across, raw_fields, grads, groups, raw, lines):
@@ -763,24 +751,23 @@
     total = 2 * half
     wide = total * TILE
     out_shape = [pltpu.HBM((half, lines + raw, LANES), BF16)]
-    out_shape += [pltpu.HBM((lines - raw, LANES), BF16)] * half
+    out_shape += [jax.ShapeDtypeStruct((lines - raw, LANES), BF16)] * half
     return call(
         functools.partial(update_pieces_body, half, raw, lines, groups),
         "update_pieces",
         flops=4 * wide * wide * LANES * (lines // TILE),
         moved=6 * total * lines * LANES,
         in_specs=[IN_VMEM] * (half + 6) + [IN_HBM] * len(groups),
-        out_specs=[IN_HBM] * len(out_shape),
+        out_specs=[IN_HBM] + [IN_VMEM] * half,
         out_shape=out_shape,
         scratch_shapes=[
             pltpu.VMEM((half, lines + raw, LANES), BF16),
-            pltpu.VMEM((half, lines - raw, LANES), BF16),
             pltpu.VMEM((wide, wide), BF16),
             pltpu.VMEM((wide, LANES), F32),
             pltpu.VMEM((total, lines, LANES), BF16),
             pltpu.VMEM((total, raw, LANES), BF16),
             pltpu.SemaphoreType.DMA((total,)),
-            pltpu.SemaphoreType.DMA(((lines + raw) // BLOCK, 1 + half)),
+            pltpu.SemaphoreType.DMA(((lines + raw) // BLOCK,)),
         ],
     )(near, *far, across, *raw_fields, numbers, grams, *grads)
 

time: 131 us -> 132 us (level)
  local copies, waits for them, and re-layouts: 0.03 us -> 1.9 us
    unnamed x16 -> x12, local copies, waits for them, and re-layouts: 0.03 us -> 1.9 us
where the time goes in v15:
time: 132 us
  waiting for transfers between devices  68.4 us (52%)
  starting transfers between devices  33 us (25%)
  Pallas kernels  26.3 us (20%)
  between operations  2.07 us (2%)
  local copies, waits for them, and re-layouts  1.9 us (1%)
    ppermute x17, waiting for transfers between devices, exchange(): return lax.ppermute(piece, 'slab', [(i, i ^ k) for i in range(slabs)])  65.6 us
    ppermute x17, starting transfers between devices, exchange(): return lax.ppermute(piece, 'slab', [(i, i ^ k) for i in range(slabs)])  17.9 us
    all_to_all x2, starting transfers between devices, swap_near(): lax.all_to_all(pieces, 'slab', 0, 0, axis_index_groups=groups, tiled=True)  9.35 us
    pallas_call x3, Pallas kernels, gradient_pieces(): call(functools.partial(gradient_pieces_body, views, len(arrays), len(numb...  7.33 us
    all_to_all x1, starting transfers between devices, swap(): lax.all_to_all(slabs, 'slab', split_axis=0, concat_axis=0, tiled=True)  5.75 us
    pallas_call x4, Pallas kernels, join_pieces(): call(functools.partial(join_pieces_body, pieces, slabs // 2, raw, NCELL /...  5.54 us
    pallas_call x1, Pallas kernels, update_pieces(): call(functools.partial(update_pieces_body, half, raw, lines, groups), 'up...  5.38 us
    pallas_call x1, Pallas kernels, split_pieces(): call(functools.partial(split_pieces_body, slabs, raw, lines, len(fields))...  4.88 us
  transfers between devices with their start and end apart: 20, of which 15 were waited for; matrix products, arithmetic and copies ran while one was open for 0% of the time, Pallas kernels for 12%

profile of v15, /device:TPU:9, one launch (start us, length us, event | category | flops | bytes accessed | tf_op | source)
XLA Modules:
  0.0 131.7 jit_solution(12421097935918480081)
XLA Ops:
  0.0 4.9 %split_pieces.1 = (bf16[8,672,128]{2,1,0:T(8,128)(2,1)}, bf16[528,128]{1,0:T(8,128)(2,1)S(1)}, bf16[528,128]{1,0:T(8,128)(2,1)S(1)}, bf16[528,128]{1,0:T(8,128)(...) custom-call(bf16[1,1048576]{1,0:T(2,128)(2,1)} %row_ref.1, ...), custom_call_target="tpu_custom_call" | custom-call | bytes 7372800 | tf_op jit(solution)/shard_map/split_pieces/pallas_call | solution.py:445
  4.9 4.6 %all-to-all-start = ((bf16[8,672,128]{2,1,0:T(8,128)(2,1)}), bf16[8,672,128]{2,1,0:T(8,128)(2,1)S(1)}, u32[]{:S(2)}, u32[]{:S(2)}) async-start(bf16[8,672,128]{2,1,0:T(8,128)(2,1)} %get-tuple-element.31), calls=%async_computation | async-start | bytes 2752512 | tf_op jit(solution)/shard_map/all_to_all | solution.py:781
  9.5 2.3 %collective-permute-start = (bf16[528,128]{1,0:T(8,128)(2,1)S(1)}, bf16[528,128]{1,0:T(8,128)(2,1)S(1)}, u32[]{:S(2)}, u32[]{:S(2)}) collective-permute-start(bf16[528,128]{1,0:T(8,128)(2,1)S(1)} %get-tuple-element.32), channel_id=1, source_target_pairs={{0,8},{1,9},{2,10},{3,11},{4,12},{5,13},{6,14},{7,15},{8,0},{9,1},... | collective-permute-start | bytes 405512 | tf_op jit(solution)/shard_map/ppermute | solution.py:776
  11.8 0.6 collective-permute-start.1
  12.4 3.2 %collective-permute-start.2 = (bf16[528,128]{1,0:T(8,128)(2,1)S(1)}, bf16[528,128]{1,0:T(8,128)(2,1)S(1)}, u32[]{:S(2)}, u32[]{:S(2)}) collective-permute-start(bf16[528,128]{1,0:T(8,128)(2,1)S(1)} %get-tuple-element.34), channel_id=1, source_target_pairs={{0,10},{1,11},{2,8},{3,9},{4,14},{5,15},{6,12},{7,13},{8,2},{9,3},... | collective-permute-start | bytes 405512 | tf_op jit(solution)/shard_map/ppermute | solution.py:776
  15.6 0.3 collective-permute-start.3
  15.9 1.0 collective-permute-start.4
  16.9 13.5 %collective-permute-done.refs_0_ = bf16[528,128]{1,0:T(8,128)(2,1)S(1)} collective-permute-done((bf16[528,128]{1,0:T(8,128)(2,1)S(1)}, bf16[528,128]{1,0:T(8,128)(2,1)S(1)}, u32[]{:S(2)}, u32[]{:S(2)}) %collective-permute-start) | collective-permute-done | bytes 135200 | tf_op jit(solution)/shard_map/ppermute | solution.py:776
  30.4 0.0 collective-permute-start.5
  30.4 3.6 %collective-permute-done.1.refs_1_ = bf16[528,128]{1,0:T(8,128)(2,1)S(1)} collective-permute-done((bf16[528,128]{1,0:T(8,128)(2,1)S(1)}, bf16[528,128]{1,0:T(8,128)(2,1)S(1)}, u32[]{:S(2)}, u32[]{:S(2)}) %collective-permute-start.1) | collective-permute-done | bytes 135200 | tf_op jit(solution)/shard_map/ppermute | solution.py:776
  34.0 0.3 collective-permute-start.6
  34.3 2.8 %collective-permute-done.2.refs_2_ = bf16[528,128]{1,0:T(8,128)(2,1)S(1)} collective-permute-done((bf16[528,128]{1,0:T(8,128)(2,1)S(1)}, bf16[528,128]{1,0:T(8,128)(2,1)S(1)}, u32[]{:S(2)}, u32[]{:S(2)}) %collective-permute-start.2) | collective-permute-done | bytes 135200 | tf_op jit(solution)/shard_map/ppermute | solution.py:776
  37.1 0.0 collective-permute-start.7
  39.1 1.7 %collective-permute-done.3.refs_3_ = bf16[528,128]{1,0:T(8,128)(2,1)S(1)} collective-permute-done((bf16[528,128]{1,0:T(8,128)(2,1)S(1)}, bf16[528,128]{1,0:T(8,128)(2,1)S(1)}, u32[]{:S(2)}, u32[]{:S(2)}) %collective-permute-start.3) | collective-permute-done | bytes 135200 | tf_op jit(solution)/shard_map/ppermute | solution.py:776
  40.7 1.8 %gradient_pieces.3 = (bf16[4,512,128]{2,1,0:T(8,128)(2,1)}, f32[8,128]{1,0:T(8,128)S(1)}) custom-call(bf16[528,128]{1,0:T(8,128)(2,1)S(1)} %collective-permute-done.refs_0_, bf16[528,128]{1,0:T(8,128)(2,1)S(1)} %collective-permute-done.1.refs_1_, bf16[528,128]{1,0:T(8,128)(2,1)S(1)} %collective-permute-done.2.refs_2_, ...), custom_call_target="tpu_custom_call" | custom-call | flops 7864320 | bytes 2097152 | tf_op jit(solution)/shard_map/gradient_pieces/pallas_call | solution.py:610
  42.6 6.7 %collective-permute-done.4.refs_4_.refs_0_ = bf16[528,128]{1,0:T(8,128)(2,1)S(1)} collective-permute-done((bf16[528,128]{1,0:T(8,128)(2,1)S(1)}, bf16[528,128]{1,0:T(8,128)(2,1)S(1)}, u32[]{:S(2)}, u32[]{:S(2)}) %collective-permute-start.4) | collective-permute-done | bytes 135200 | tf_op jit(solution)/shard_map/ppermute | solution.py:776
  49.2 4.7 %collective-permute-done.5.refs_5_.refs_1_ = bf16[528,128]{1,0:T(8,128)(2,1)S(1)} collective-permute-done((bf16[528,128]{1,0:T(8,128)(2,1)S(1)}, bf16[528,128]{1,0:T(8,128)(2,1)S(1)}, u32[]{:S(2)}, u32[]{:S(2)}) %collective-permute-start.5) | collective-permute-done | bytes 135200 | tf_op jit(solution)/shard_map/ppermute | solution.py:776
  54.0 3.8 %collective-permute-done.6.refs_6_.refs_2_ = bf16[528,128]{1,0:T(8,128)(2,1)S(1)} collective-permute-done((bf16[528,128]{1,0:T(8,128)(2,1)S(1)}, bf16[528,128]{1,0:T(8,128)(2,1)S(1)}, u32[]{:S(2)}, u32[]{:S(2)}) %collective-permute-start.6) | collective-permute-done | bytes 135200 | tf_op jit(solution)/shard_map/ppermute | solution.py:776
  57.8 2.9 %collective-permute-done.7.refs_7_.refs_3_ = bf16[528,128]{1,0:T(8,128)(2,1)S(1)} collective-permute-done((bf16[528,128]{1,0:T(8,128)(2,1)S(1)}, bf16[528,128]{1,0:T(8,128)(2,1)S(1)}, u32[]{:S(2)}, u32[]{:S(2)}) %collective-permute-start.7) | collective-permute-done | bytes 135200 | tf_op jit(solution)/shard_map/ppermute | solution.py:776
  60.7 0.1 collective-permute-start.8
  60.8 3.2 %gram_pieces.1 = f32[16,16,128]{2,1,0:T(8,128)} custom-call(bf16[8,672,128]{2,1,0:T(8,128)(2,1)S(1)} %all-to-all-done.near_ref.refs_0_, bf16[528,128]{1,0:T(8,128)(2,1)S(1)} %collective-permute-done.refs_0_, bf16[528,128]{1,0:T(8,128)(2,1)S(1)} %collective-permute-done.1.refs_1_, bf16[528,128]{1,0:T(8,128)(2,1)S(1)} %collective-permute-done.2.refs_2_, ...), custom_call_target="tpu_custom_call" | custom-call | flops 536870912 | bytes 2097152 | tf_op jit(solution)/shard_map/gram_pieces/pallas_call | solution.py:537
  64.0 5.8 %all-to-all-start.1 = ((f32[16,16,128]{2,1,0:T(8,128)}), f32[16,16,128]{2,1,0:T(8,128)S(1)}, u32[]{:S(2)}, u32[]{:S(2)}) async-start(f32[16,16,128]{2,1,0:T(8,128)} %gram_pieces.1), calls=%async_computation.1 | async-start | bytes 262144 | tf_op jit(solution)/shard_map/all_to_all | solution.py:365
  69.7 2.4 %gradient_pieces.4 = (bf16[4,512,128]{2,1,0:T(8,128)(2,1)}, f32[8,128]{1,0:T(8,128)}) custom-call(bf16[528,128]{1,0:T(8,128)(2,1)S(1)} %collective-permute-done.4.refs_4_.refs_0_, bf16[528,128]{1,0:T(8,128)(2,1)S(1)} %collective-permute-done.5.refs_5_.refs_1_, bf16[528,128]{1,0:T(8,128)(2,1)S(1)} %collective-permute-done.6.refs_6_.refs_2_, ...), custom_call_target="tpu_custom_call" | custom-call | flops 7864320 | bytes 2097152 | tf_op jit(solution)/shard_map/gradient_pieces/pallas_call | solution.py:610
  72.1 3.1 %gradient_pieces.5 = (bf16[8,512,128]{2,1,0:T(8,128)(2,1)}, f32[8,128]{1,0:T(8,128)}) custom-call(bf16[8,672,128]{2,1,0:T(8,128)(2,1)S(1)} %all-to-all-done.near_ref.refs_0_, bf16[512,128]{1,0:T(8,128)(2,1)S(1)} %get-tuple-element.42.refs_4_.refs_1_, bf16[512,128]{1,0:T(8,128)(2,1)S(1)} %get-tuple-element.43.refs_5_.refs_2_), custom_call_target="tpu_custom_call" | custom-call | flops 15728640 | bytes 4194304 | tf_op jit(solution)/shard_map/gradient_pieces/pallas_call | solution.py:610
  75.3 2.9 %all-to-all-done.1.refs_12_ = f32[16,16,128]{2,1,0:T(8,128)S(1)} async-done(((f32[16,16,128]{2,1,0:T(8,128)}), f32[16,16,128]{2,1,0:T(8,128)S(1)}, u32[]{:S(2)}, u32[]{:S(2)}) %all-to-all-start.1) | async-done | bytes 131104 | tf_op jit(solution)/shard_map/all_to_all | solution.py:365
  78.1 5.4 %update_pieces.1 = (bf16[8,640,128]{2,1,0:T(8,128)(2,1)}, bf16[384,128]{1,0:T(8,128)(2,1)S(1)}, bf16[384,128]{1,0:T(8,128)(2,1)S(1)}, bf16[384,128]{1,0:T(8,128)...) custom-call(bf16[8,672,128]{2,1,0:T(8,128)(2,1)S(1)} %all-to-all-don, ...), custom_call_target="tpu_custom_call" | custom-call | flops 1073741824 | bytes 6291456 | tf_op jit(solution)/shard_map/update_pieces/pallas_call | solution.py:755
  83.5 0.6 copy-done
  84.1 0.6 copy-done.2
  84.8 0.6 copy-done.4
  85.4 4.8 %all-to-all-start.2 = ((bf16[8,640,128]{2,1,0:T(8,128)(2,1)}), bf16[8,640,128]{2,1,0:T(8,128)(2,1)S(1)}, u32[]{:S(2)}, u32[]{:S(2)}) async-start(bf16[8,640,128]{2,1,0:T(8,128)(2,1)} %get-tuple-element.48), calls=%async_computation.2 | async-start | bytes 2621440 | tf_op jit(solution)/shard_map/all_to_all | solution.py:781
  90.2 1.2 collective-permute-start.9
  91.4 1.7 %collective-permute-start.10 = (bf16[384,128]{1,0:T(8,128)(2,1)S(1)}, bf16[384,128]{1,0:T(8,128)(2,1)S(1)}, u32[]{:S(2)}, u32[]{:S(2)}) collective-permute-start(bf16[384,128]{1,0:T(8,128)(2,1)S(1)} %copy-done.3), channel_id=1, source_target_pairs={{0,9},{1,8},{2,11},{3,10},{4,13},{5,12},{6,15},{7,14},{8,1},{9,0},... | collective-permute-start | bytes 294920 | tf_op jit(solution)/shard_map/ppermute | solution.py:776
  93.1 2.1 %collective-permute-start.11 = (bf16[384,128]{1,0:T(8,128)(2,1)S(1)}, bf16[384,128]{1,0:T(8,128)(2,1)S(1)}, u32[]{:S(2)}, u32[]{:S(2)}) collective-permute-start(bf16[384,128]{1,0:T(8,128)(2,1)S(1)} %copy-done.1), channel_id=1, source_target_pairs={{0,10},{1,11},{2,8},{3,9},{4,14},{5,15},{6,12},{7,13},{8,2},{9,3},... | collective-permute-start | bytes 294920 | tf_op jit(solution)/shard_map/ppermute | solution.py:776
  95.2 1.2 collective-permute-start.12
  96.4 0.0 collective-permute-start.13
  96.4 12.0 %collective-permute-done.9.refs_1_ = bf16[384,128]{1,0:T(8,128)(2,1)S(1)} collective-permute-done((bf16[384,128]{1,0:T(8,128)(2,1)S(1)}, bf16[384,128]{1,0:T(8,128)(2,1)S(1)}, u32[]{:S(2)}, u32[]{:S(2)}) %collective-permute-start.9) | collective-permute-done | bytes 98336 | tf_op jit(solution)/shard_map/ppermute | solution.py:776
  108.5 1.1 collective-permute-start.14
  109.6 1.7 %collective-permute-done.10.refs_2_ = bf16[384,128]{1,0:T(8,128)(2,1)S(1)} collective-permute-done((bf16[384,128]{1,0:T(8,128)(2,1)S(1)}, bf16[384,128]{1,0:T(8,128)(2,1)S(1)}, u32[]{:S(2)}, u32[]{:S(2)}) %collective-permute-start.10) | collective-permute-done | bytes 98336 | tf_op jit(solution)/shard_map/ppermute | solution.py:776
  111.2 1.5 %collective-permute-start.15 = (bf16[384,128]{1,0:T(8,128)(2,1)S(1)}, bf16[384,128]{1,0:T(8,128)(2,1)S(1)}, u32[]{:S(2)}, u32[]{:S(2)}) collective-permute-start(bf16[384,128]{1,0:T(8,128)(2,1)S(1)} %get-tuple-element.55), channel_id=1, source_target_pairs={{0,14},{1,15},{2,12},{3,13},{4,10},{5,11},{6,8},{7,9},{8,6},{9,7},... | collective-permute-start | bytes 294920 | tf_op jit(solution)/shard_map/ppermute | solution.py:776
  112.7 0.9 collective-permute-done.11.refs_3_
  113.6 1.2 collective-permute-start.16
  114.8 3.0 %join_pieces.4.refs_0_ = bf16[1,1048576]{1,0:T(2,128)(2,1)} custom-call(bf16[8,640,128]{2,1,0:T(8,128)(2,1)S(1)} %all-to-all-done.2.refs_0_), custom_call_target="tpu_custom_call" | custom-call | bytes 3932160 | tf_op jit(solution)/shard_map/join_pieces/pallas_call | solution.py:483
  117.8 1.0 join_pieces.5.refs_0_
  118.8 7.0 %collective-permute-done.14.refs_2_ = bf16[384,128]{1,0:T(8,128)(2,1)S(1)} collective-permute-done((bf16[384,128]{1,0:T(8,128)(2,1)S(1)}, bf16[384,128]{1,0:T(8,128)(2,1)S(1)}, u32[]{:S(2)}, u32[]{:S(2)}) %collective-permute-start.14) | collective-permute-done | bytes 98336 | tf_op jit(solution)/shard_map/ppermute | solution.py:776
  125.7 0.8 join_pieces.6.refs_0_
  126.6 2.2 %collective-permute-done.15.refs_1_ = bf16[384,128]{1,0:T(8,128)(2,1)S(1)} collective-permute-done((bf16[384,128]{1,0:T(8,128)(2,1)S(1)}, bf16[384,128]{1,0:T(8,128)(2,1)S(1)}, u32[]{:S(2)}, u32[]{:S(2)}) %collective-permute-start.15) | collective-permute-done | bytes 98336 | tf_op jit(solution)/shard_map/ppermute | solution.py:776
  128.8 2.1 %collective-permute-done.16.refs_2_ = bf16[384,128]{1,0:T(8,128)(2,1)S(1)} collective-permute-done((bf16[384,128]{1,0:T(8,128)(2,1)S(1)}, bf16[384,128]{1,0:T(8,128)(2,1)S(1)}, u32[]{:S(2)}, u32[]{:S(2)}) %collective-permute-start.16) | collective-permute-done | bytes 98336 | tf_op jit(solution)/shard_map/ppermute | solution.py:776
  130.9 0.8 join_pieces.7
  (15 shorter events, 0.1 us)
Async XLA Ops:
  4.9 55.8 %all-to-all-start = ((bf16[8,672,128]{2,1,0:T(8,128)(2,1)}), bf16[8,672,128]{2,1,0:T(8,128)(2,1)S(1)}, u32[]{:S(2)}, u32[]{:S(2)}) async-start(bf16[8,672,128]{2,1,0:T(8,128)(2,1)} %get-tuple-element.31), calls=%async_computation | async-start | bytes 2752512 | tf_op jit(solution)/shard_map/all_to_all | solution.py:781
  9.5 20.9 %collective-permute-start = (bf16[528,128]{1,0:T(8,128)(2,1)S(1)}, bf16[528,128]{1,0:T(8,128)(2,1)S(1)}, u32[]{:S(2)}, u32[]{:S(2)}) collective-permute-start(bf16[528,128]{1,0:T(8,128)(2,1)S(1)} %get-tuple-element.32), channel_id=1, source_target_pairs={{0,8},{1,9},{2,10},{3,11},{4,12},{5,13},{6,14},{7,15},{8,0},{9,1},... | collective-permute-start | bytes 405512 | tf_op jit(solution)/shard_map/ppermute | solution.py:776
  11.8 22.2 %collective-permute-start.1 = (bf16[528,128]{1,0:T(8,128)(2,1)S(1)}, bf16[528,128]{1,0:T(8,128)(2,1)S(1)}, u32[]{:S(2)}, u32[]{:S(2)}) collective-permute-start(bf16[528,128]{1,0:T(8,128)(2,1)S(1)} %get-tuple-element.33), channel_id=1, source_target_pairs={{0,9},{1,8},{2,11},{3,10},{4,13},{5,12},{6,15},{7,14},{8,1},{9,0},... | collective-permute-start | bytes 405512 | tf_op jit(solution)/shard_map/ppermute | solution.py:776
  12.4 24.8 %collective-permute-start.2 = (bf16[528,128]{1,0:T(8,128)(2,1)S(1)}, bf16[528,128]{1,0:T(8,128)(2,1)S(1)}, u32[]{:S(2)}, u32[]{:S(2)}) collective-permute-start(bf16[528,128]{1,0:T(8,128)(2,1)S(1)} %get-tuple-element.34), channel_id=1, source_target_pairs={{0,10},{1,11},{2,8},{3,9},{4,14},{5,15},{6,12},{7,13},{8,2},{9,3},... | collective-permute-start | bytes 405512 | tf_op jit(solution)/shard_map/ppermute | solution.py:776
  15.6 25.2 %collective-permute-start.3 = (bf16[528,128]{1,0:T(8,128)(2,1)S(1)}, bf16[528,128]{1,0:T(8,128)(2,1)S(1)}, u32[]{:S(2)}, u32[]{:S(2)}) collective-permute-start(bf16[528,128]{1,0:T(8,128)(2,1)S(1)} %get-tuple-element.35), channel_id=1, source_target_pairs={{0,11},{1,10},{2,9},{3,8},{4,15},{5,14},{6,13},{7,12},{8,3},{9,2},... | collective-permute-start | bytes 405512 | tf_op jit(solution)/shard_map/ppermute | solution.py:776
  15.9 33.4 %collective-permute-start.4 = (bf16[528,128]{1,0:T(8,128)(2,1)S(1)}, bf16[528,128]{1,0:T(8,128)(2,1)S(1)}, u32[]{:S(2)}, u32[]{:S(2)}) collective-permute-start(bf16[528,128]{1,0:T(8,128)(2,1)S(1)} %get-tuple-element.36), channel_id=1, source_target_pairs={{0,12},{1,13},{2,14},{3,15},{4,8},{5,9},{6,10},{7,11},{8,4},{9,5},... | collective-permute-start | bytes 405512 | tf_op jit(solution)/shard_map/ppermute | solution.py:776
  30.4 23.6 %collective-permute-start.5 = (bf16[528,128]{1,0:T(8,128)(2,1)S(1)}, bf16[528,128]{1,0:T(8,128)(2,1)S(1)}, u32[]{:S(2)}, u32[]{:S(2)}) collective-permute-start(bf16[528,128]{1,0:T(8,128)(2,1)S(1)} %get-tuple-element.37), channel_id=1, source_target_pairs={{0,13},{1,12},{2,15},{3,14},{4,9},{5,8},{6,11},{7,10},{8,5},{9,4},... | collective-permute-start | bytes 405512 | tf_op jit(solution)/shard_map/ppermute | solution.py:776
  34.0 23.8 %collective-permute-start.6 = (bf16[528,128]{1,0:T(8,128)(2,1)S(1)}, bf16[528,128]{1,0:T(8,128)(2,1)S(1)}, u32[]{:S(2)}, u32[]{:S(2)}) collective-permute-start(bf16[528,128]{1,0:T(8,128)(2,1)S(1)} %get-tuple-element.38), channel_id=1, source_target_pairs={{0,14},{1,15},{2,12},{3,13},{4,10},{5,11},{6,8},{7,9},{8,6},{9,7},... | collective-permute-start | bytes 405512 | tf_op jit(solution)/shard_map/ppermute | solution.py:776
  37.1 23.5 %collective-permute-start.7 = (bf16[528,128]{1,0:T(8,128)(2,1)S(1)}, bf16[528,128]{1,0:T(8,128)(2,1)S(1)}, u32[]{:S(2)}, u32[]{:S(2)}) collective-permute-start(bf16[528,128]{1,0:T(8,128)(2,1)S(1)} %get-tuple-element.39), channel_id=1, source_target_pairs={{0,15},{1,14},{2,13},{3,12},{4,11},{5,10},{6,9},{7,8},{8,7},{9,6},... | collective-permute-start | bytes 405512 | tf_op jit(solution)/shard_map/ppermute | solution.py:776
  60.7 17.4 %collective-permute-start.8 = (bf16[8,144,128]{2,1,0:T(8,128)(2,1)S(1)}, bf16[8,144,128]{2,1,0:T(8,128)(2,1)S(1)}, u32[]{:S(2)}, u32[]{:S(2)}) collective-permute-start(bf16[8,144,128]{2,1,0:T(8,128)(2,1)S(1)} %raw_states.1.refs_9_), channel_id=1, source_target_pairs={{0,8},{1,9},{2,10},{3,11},{4,12},{5,13},{6,14},{7,15},{8,0},{9,1},... | collective-permute-start | bytes 884744 | tf_op jit(solution)/shard_map/ppermute | solution.py:776
  64.0 14.1 %all-to-all-start.1 = ((f32[16,16,128]{2,1,0:T(8,128)}), f32[16,16,128]{2,1,0:T(8,128)S(1)}, u32[]{:S(2)}, u32[]{:S(2)}) async-start(f32[16,16,128]{2,1,0:T(8,128)} %gram_pieces.1), calls=%async_computation.1 | async-start | bytes 262144 | tf_op jit(solution)/shard_map/all_to_all | solution.py:365
  83.5 0.6 copy-start
  84.1 0.6 copy-start.2
  84.8 0.6 copy-start.4
  85.4 4.8 %copy-start.5 = (bf16[384,128]{1,0:T(8,128)(2,1)S(1)}, bf16[384,128]{1,0:T(8,128)(2,1)}, u32[]{:S(2)}) copy-start(bf16[384,128]{1,0:T(8,128)(2,1)} %copy-done.4) | copy-start | bytes 294916
  85.4 5.9 %copy-start.3 = (bf16[384,128]{1,0:T(8,128)(2,1)S(1)}, bf16[384,128]{1,0:T(8,128)(2,1)}, u32[]{:S(2)}) copy-start(bf16[384,128]{1,0:T(8,128)(2,1)} %copy-done.2) | copy-start | bytes 294916
  85.4 7.7 %copy-start.1 = (bf16[384,128]{1,0:T(8,128)(2,1)S(1)}, bf16[384,128]{1,0:T(8,128)(2,1)}, u32[]{:S(2)}) copy-start(bf16[384,128]{1,0:T(8,128)(2,1)} %copy-done) | copy-start | bytes 294916
  85.4 29.4 %all-to-all-start.2 = ((bf16[8,640,128]{2,1,0:T(8,128)(2,1)}), bf16[8,640,128]{2,1,0:T(8,128)(2,1)S(1)}, u32[]{:S(2)}, u32[]{:S(2)}) async-start(bf16[8,640,128]{2,1,0:T(8,128)(2,1)} %get-tuple-element.48), calls=%async_computation.2 | async-start | bytes 2621440 | tf_op jit(solution)/shard_map/all_to_all | solution.py:781
  90.2 18.3 %collective-permute-start.9 = (bf16[384,128]{1,0:T(8,128)(2,1)S(1)}, bf16[384,128]{1,0:T(8,128)(2,1)S(1)}, u32[]{:S(2)}, u32[]{:S(2)}) collective-permute-start(bf16[384,128]{1,0:T(8,128)(2,1)S(1)} %copy-done.5), channel_id=1, source_target_pairs={{0,8},{1,9},{2,10},{3,11},{4,12},{5,13},{6,14},{7,15},{8,0},{9,1},... | collective-permute-start | bytes 294920 | tf_op jit(solution)/shard_map/ppermute | solution.py:776
  91.4 19.9 %collective-permute-start.10 = (bf16[384,128]{1,0:T(8,128)(2,1)S(1)}, bf16[384,128]{1,0:T(8,128)(2,1)S(1)}, u32[]{:S(2)}, u32[]{:S(2)}) collective-permute-start(bf16[384,128]{1,0:T(8,128)(2,1)S(1)} %copy-done.3), channel_id=1, source_target_pairs={{0,9},{1,8},{2,11},{3,10},{4,13},{5,12},{6,15},{7,14},{8,1},{9,0},... | collective-permute-start | bytes 294920 | tf_op jit(solution)/shard_map/ppermute | solution.py:776
  93.1 20.5 %collective-permute-start.11 = (bf16[384,128]{1,0:T(8,128)(2,1)S(1)}, bf16[384,128]{1,0:T(8,128)(2,1)S(1)}, u32[]{:S(2)}, u32[]{:S(2)}) collective-permute-start(bf16[384,128]{1,0:T(8,128)(2,1)S(1)} %copy-done.1), channel_id=1, source_target_pairs={{0,10},{1,11},{2,8},{3,9},{4,14},{5,15},{6,12},{7,13},{8,2},{9,3},... | collective-permute-start | bytes 294920 | tf_op jit(solution)/shard_map/ppermute | solution.py:776
  95.2 22.6 %collective-permute-start.12 = (bf16[384,128]{1,0:T(8,128)(2,1)S(1)}, bf16[384,128]{1,0:T(8,128)(2,1)S(1)}, u32[]{:S(2)}, u32[]{:S(2)}) collective-permute-start(bf16[384,128]{1,0:T(8,128)(2,1)S(1)} %get-tuple-element.52), channel_id=1, source_target_pairs={{0,11},{1,10},{2,9},{3,8},{4,15},{5,14},{6,13},{7,12},{8,3},{9,2},... | collective-permute-start | bytes 294920 | tf_op jit(solution)/shard_map/ppermute | solution.py:776
  96.4 22.4 %collective-permute-start.13 = (bf16[384,128]{1,0:T(8,128)(2,1)S(1)}, bf16[384,128]{1,0:T(8,128)(2,1)S(1)}, u32[]{:S(2)}, u32[]{:S(2)}) collective-permute-start(bf16[384,128]{1,0:T(8,128)(2,1)S(1)} %get-tuple-element.53), channel_id=1, source_target_pairs={{0,12},{1,13},{2,14},{3,15},{4,8},{5,9},{6,10},{7,11},{8,4},{9,5},... | collective-permute-start | bytes 294920 | tf_op jit(solution)/shard_map/ppermute | solution.py:776
  108.5 17.3 %collective-permute-start.14 = (bf16[384,128]{1,0:T(8,128)(2,1)S(1)}, bf16[384,128]{1,0:T(8,128)(2,1)S(1)}, u32[]{:S(2)}, u32[]{:S(2)}) collective-permute-start(bf16[384,128]{1,0:T(8,128)(2,1)S(1)} %get-tuple-element.54), channel_id=1, source_target_pairs={{0,13},{1,12},{2,15},{3,14},{4,9},{5,8},{6,11},{7,10},{8,5},{9,4},... | collective-permute-start | bytes 294920 | tf_op jit(solution)/shard_map/ppermute | solution.py:776
  111.2 17.5 %collective-permute-start.15 = (bf16[384,128]{1,0:T(8,128)(2,1)S(1)}, bf16[384,128]{1,0:T(8,128)(2,1)S(1)}, u32[]{:S(2)}, u32[]{:S(2)}) collective-permute-start(bf16[384,128]{1,0:T(8,128)(2,1)S(1)} %get-tuple-element.55), channel_id=1, source_target_pairs={{0,14},{1,15},{2,12},{3,13},{4,10},{5,11},{6,8},{7,9},{8,6},{9,7},... | collective-permute-start | bytes 294920 | tf_op jit(solution)/shard_map/ppermute | solution.py:776
  113.6 17.3 %collective-permute-start.16 = (bf16[384,128]{1,0:T(8,128)(2,1)S(1)}, bf16[384,128]{1,0:T(8,128)(2,1)S(1)}, u32[]{:S(2)}, u32[]{:S(2)}) collective-permute-start(bf16[384,128]{1,0:T(8,128)(2,1)S(1)} %get-tuple-element.56), channel_id=1, source_target_pairs={{0,15},{1,14},{2,13},{3,12},{4,11},{5,10},{6,9},{7,8},{8,7},{9,6},... | collective-permute-start | bytes 294920 | tf_op jit(solution)/shard_map/ppermute | solution.py:776

commit v16 on v13

--- a/solution.py
+++ b/solution.py
@@ -455,44 +455,59 @@
     )(row, *fields)
 
 
-def join_pieces_body(pieces, half, raw, lines, begun, arrays, *refs):
-    row_ref, helds, sems = refs[begun + arrays], refs[begun + arrays + 1 : -1], refs[-1]
+def join_pieces_body(positions, half, raw, lines, begun, arrays, *refs):
+    pieces, row_ref, held, sems = refs[begun : begun + arrays], refs[begun + arrays], refs[begun + arrays + 1], refs[-1]
+    near = positions[0] < half
+    size = held.shape[1] // len(positions)
     cells = lines * LANES
     skip = raw * LANES
+    fetches = []
+    if near:
+        here = refs[-2]
+        for n in range(len(positions)):
+            fetches.append(pltpu.make_async_copy(pieces[0].at[n], here.at[n], sems.at[2 * len(positions) + n]))
+            fetches[-1].start()
     copies = []
-    for (array, lead, at), held in zip(pieces, helds):
-        ref = refs[begun + array]
-        piece = ref[...] if lead is None else ref[lead]
-        held[...] = piece.reshape(held.shape)
+    for n, at in enumerate(positions):
         slab = device_at(at, half)
-        if at < half:
+        if near:
+            fetches[n].wait()
+            piece = here[n]
             parts = [(0, cells, slab * cells), (cells, skip, (slab ^ half) * cells)]
         else:
+            piece = pieces[n][...]
             parts = [(0, cells - skip, slab * cells + skip)]
-        for begin, size, start in parts:
-            target = row_ref.at[:, pl.ds(pl.multiple_of(start, GRID_Y), size)]
-            copies.append(pltpu.make_async_copy(held.at[:, pl.ds(begin, size)], target, sems.at[len(copies)]))
+        held[:, pl.ds(n * size, size)] = piece.reshape(1, size)
+        for begin, count, start in parts:
+            target = row_ref.at[:, pl.ds(pl.multiple_of(start, GRID_Y), count)]
+            source = held.at[:, pl.ds(n * size + begin, count)]
+            copies.append(pltpu.make_async_copy(source, target, sems.at[len(copies)]))
             copies[-1].start()
     for copy in copies:
         copy.wait()
 
 
-def join_pieces(row, slabs, raw, arrays, pieces):
-    sizes = [arrays[piece[0]].shape[-2] * LANES for piece in pieces]
+def join_pieces(row, slabs, raw, pieces, positions):
+    half = slabs // 2
+    near = positions[0] < half
+    shape = pieces[0].shape
+    size = shape[-2] * LANES
+    count = len(positions)
     begun = [] if row is None else [row]
     return call(
         functools.partial(
-            join_pieces_body, pieces, slabs // 2, raw, NCELL // slabs // LANES, len(begun), len(arrays)
+            join_pieces_body, positions, half, raw, NCELL // slabs // LANES, len(begun), len(pieces)
         ),
         "join_pieces",
-        moved=6 * sum(sizes),
-        in_specs=[IN_HBM] * len(begun) + [IN_VMEM] * len(arrays),
+        moved=6 * size * count,
+        in_specs=[IN_HBM] * len(begun) + [IN_HBM if near else IN_VMEM] * len(pieces),
         out_specs=IN_HBM,
         out_shape=jax.ShapeDtypeStruct((1, NCELL), BF16),
         input_output_aliases={0: 0} if begun else {},
-        scratch_shapes=[pltpu.VMEM((1, size), BF16) for size in sizes]
-        + [pltpu.SemaphoreType.DMA((2 * len(sizes),))],
-    )(*begun, *arrays)
+        scratch_shapes=[pltpu.VMEM((1, size * count), BF16)]
+        + [pltpu.VMEM(shape, BF16)] * near
+        + [pltpu.SemaphoreType.DMA((3 * count,))],
+    )(*begun, *pieces)
 
 
 def owners(total, dtype):
@@ -522,9 +537,11 @@
     lax.fori_loop(0, lines // TILE // tiles, step, 0)
     equal = jnp.where(same_line(total), pairs[...], 0.0)
     exact = {"precision": lax.Precision.HIGHEST, "preferred_element_type": F32}
-    owner = owners(total, F32)
-    half_way = jnp.dot(equal, owner, **exact)
-    gram = lax.dot_general(owner, half_way, (((0,), (0,)), ((), ())), **exact)
+    rows = jnp.sum(equal.reshape(total, TILE, wide), axis=1)
+    gram = jnp.dot(rows, owners(total, F32), **exact)
+    row = lax.broadcasted_iota(jnp.int32, (total, total), 0)
+    col = lax.broadcasted_iota(jnp.int32, (total, total), 1)
+    gram = jnp.dot((row == device_at(col, half)).astype(F32), gram, **exact)
     gram = jnp.concatenate([gram, jnp.zeros((total, LANES - total), F32)], axis=1)
     out_ref[...] = jnp.broadcast_to(gram[None], out_ref.shape)
 
@@ -798,11 +815,10 @@
     )
     new_near = swap_near(new_near, slabs)
     new_far = [exchange(piece, half + x, slabs) for x, piece in enumerate(new_far)]
-    row = join_pieces(None, slabs, RAW, [new_near], [(0, k, k) for k in range(half)])
-    for group in ((0, 1, 2, 3), (4, 5)):
-        pieces = [(n, None, half + x) for n, x in enumerate(group)]
-        row = join_pieces(row, slabs, RAW, [new_far[x] for x in group], pieces)
-    return join_pieces(row, slabs, RAW, new_far[6:], [(n, None, half + 6 + n) for n in range(half - 6)])
+    row = join_pieces(None, slabs, RAW, [in_hbm(new_near)], tuple(range(half)))
+    for group in ((0, 1, 2, 3), (4, 5), (6, 7)):
+        row = join_pieces(row, slabs, RAW, [new_far[x] for x in group], tuple(half + x for x in group))
+    return row
 
 
 def on_device(particles, observed, precision, spread, anneal, step_size):

time: 132 us -> 133 us (level)
  no operation moved by 1% of the time
where the time goes in v16:
time: 133 us
  waiting for transfers between devices  67.3 us (51%)
  starting transfers between devices  33.6 us (25%)
  Pallas kernels  26.7 us (20%)
  local copies, waits for them, and re-layouts  3 us (2%)
  between operations  2.07 us (2%)
    ppermute x17, waiting for transfers between devices, exchange(): return lax.ppermute(piece, 'slab', [(i, i ^ k) for i in range(slabs)])  64.5 us
    ppermute x17, starting transfers between devices, exchange(): return lax.ppermute(piece, 'slab', [(i, i ^ k) for i in range(slabs)])  17.9 us
    all_to_all x2, starting transfers between devices, swap_near(): lax.all_to_all(pieces, 'slab', 0, 0, axis_index_groups=groups, tiled=True)  10 us
    pallas_call x3, Pallas kernels, gradient_pieces(): call(functools.partial(gradient_pieces_body, views, len(arrays), len(numb...  7.34 us
    pallas_call x4, Pallas kernels, join_pieces(): call(functools.partial(join_pieces_body, positions, half, raw, NCELL // s...  6.65 us
    all_to_all x1, starting transfers between devices, swap(): lax.all_to_all(slabs, 'slab', split_axis=0, concat_axis=0, tiled=True)  5.75 us
    pallas_call x1, Pallas kernels, split_pieces(): call(functools.partial(split_pieces_body, slabs, raw, lines, len(fields))...  4.88 us
    pallas_call x1, Pallas kernels, update_pieces(): call(functools.partial(update_pieces_body, half, raw, lines, groups), 'up...  4.67 us
  transfers between devices with their start and end apart: 20, of which 15 were waited for; matrix products, arithmetic and copies ran while one was open for 0% of the time, Pallas kernels for 12%

profile of v16, /device:TPU:9, one launch (start us, length us, event | category | flops | bytes accessed | tf_op | source)
XLA Modules:
  0.0 132.7 jit_solution(11451084820839979578)
XLA Ops:
  0.0 4.9 %split_pieces.1 = (bf16[8,672,128]{2,1,0:T(8,128)(2,1)}, bf16[528,128]{1,0:T(8,128)(2,1)S(1)}, bf16[528,128]{1,0:T(8,128)(2,1)S(1)}, bf16[528,128]{1,0:T(8,128)(...) custom-call(bf16[1,1048576]{1,0:T(2,128)(2,1)} %row_ref.1, ...), custom_call_target="tpu_custom_call" | custom-call | bytes 7372800 | tf_op jit(solution)/shard_map/split_pieces/pallas_call | solution.py:445
  4.9 4.6 %all-to-all-start = ((bf16[8,672,128]{2,1,0:T(8,128)(2,1)}), bf16[8,672,128]{2,1,0:T(8,128)(2,1)S(1)}, u32[]{:S(2)}, u32[]{:S(2)}) async-start(bf16[8,672,128]{2,1,0:T(8,128)(2,1)} %get-tuple-element.31), calls=%async_computation | async-start | bytes 2752512 | tf_op jit(solution)/shard_map/all_to_all | solution.py:783
  9.5 2.3 %collective-permute-start = (bf16[528,128]{1,0:T(8,128)(2,1)S(1)}, bf16[528,128]{1,0:T(8,128)(2,1)S(1)}, u32[]{:S(2)}, u32[]{:S(2)}) collective-permute-start(bf16[528,128]{1,0:T(8,128)(2,1)S(1)} %get-tuple-element.32), channel_id=1, source_target_pairs={{0,8},{1,9},{2,10},{3,11},{4,12},{5,13},{6,14},{7,15},{8,0},{9,1},... | collective-permute-start | bytes 405512 | tf_op jit(solution)/shard_map/ppermute | solution.py:778
  11.8 0.6 collective-permute-start.1
  12.4 3.2 %collective-permute-start.2 = (bf16[528,128]{1,0:T(8,128)(2,1)S(1)}, bf16[528,128]{1,0:T(8,128)(2,1)S(1)}, u32[]{:S(2)}, u32[]{:S(2)}) collective-permute-start(bf16[528,128]{1,0:T(8,128)(2,1)S(1)} %get-tuple-element.34), channel_id=1, source_target_pairs={{0,10},{1,11},{2,8},{3,9},{4,14},{5,15},{6,12},{7,13},{8,2},{9,3},... | collective-permute-start | bytes 405512 | tf_op jit(solution)/shard_map/ppermute | solution.py:778
  15.6 0.3 collective-permute-start.3
  15.9 1.0 collective-permute-start.4
  16.9 13.5 %collective-permute-done.refs_0_ = bf16[528,128]{1,0:T(8,128)(2,1)S(1)} collective-permute-done((bf16[528,128]{1,0:T(8,128)(2,1)S(1)}, bf16[528,128]{1,0:T(8,128)(2,1)S(1)}, u32[]{:S(2)}, u32[]{:S(2)}) %collective-permute-start) | collective-permute-done | bytes 135200 | tf_op jit(solution)/shard_map/ppermute | solution.py:778
  30.4 0.0 collective-permute-start.5
  30.4 3.6 %collective-permute-done.1.refs_1_ = bf16[528,128]{1,0:T(8,128)(2,1)S(1)} collective-permute-done((bf16[528,128]{1,0:T(8,128)(2,1)S(1)}, bf16[528,128]{1,0:T(8,128)(2,1)S(1)}, u32[]{:S(2)}, u32[]{:S(2)}) %collective-permute-start.1) | collective-permute-done | bytes 135200 | tf_op jit(solution)/shard_map/ppermute | solution.py:778
  34.0 0.3 collective-permute-start.6
  34.3 2.8 %collective-permute-done.2.refs_2_ = bf16[528,128]{1,0:T(8,128)(2,1)S(1)} collective-permute-done((bf16[528,128]{1,0:T(8,128)(2,1)S(1)}, bf16[528,128]{1,0:T(8,128)(2,1)S(1)}, u32[]{:S(2)}, u32[]{:S(2)}) %collective-permute-start.2) | collective-permute-done | bytes 135200 | tf_op jit(solution)/shard_map/ppermute | solution.py:778
  39.1 1.7 %collective-permute-done.3.refs_3_ = bf16[528,128]{1,0:T(8,128)(2,1)S(1)} collective-permute-done((bf16[528,128]{1,0:T(8,128)(2,1)S(1)}, bf16[528,128]{1,0:T(8,128)(2,1)S(1)}, u32[]{:S(2)}, u32[]{:S(2)}) %collective-permute-start.3) | collective-permute-done | bytes 135200 | tf_op jit(solution)/shard_map/ppermute | solution.py:778
  40.7 1.8 %gradient_pieces.3 = (bf16[4,512,128]{2,1,0:T(8,128)(2,1)}, f32[8,128]{1,0:T(8,128)S(1)}) custom-call(bf16[528,128]{1,0:T(8,128)(2,1)S(1)} %collective-permute-done.refs_0_, bf16[528,128]{1,0:T(8,128)(2,1)S(1)} %collective-permute-done.1.refs_1_, bf16[528,128]{1,0:T(8,128)(2,1)S(1)} %collective-permute-done.2.refs_2_, ...), custom_call_target="tpu_custom_call" | custom-call | flops 7864320 | bytes 2097152 | tf_op jit(solution)/shard_map/gradient_pieces/pallas_call | solution.py:625
  42.5 6.7 %collective-permute-done.4.refs_4_.refs_0_ = bf16[528,128]{1,0:T(8,128)(2,1)S(1)} collective-permute-done((bf16[528,128]{1,0:T(8,128)(2,1)S(1)}, bf16[528,128]{1,0:T(8,128)(2,1)S(1)}, u32[]{:S(2)}, u32[]{:S(2)}) %collective-permute-start.4) | collective-permute-done | bytes 135200 | tf_op jit(solution)/shard_map/ppermute | solution.py:778
  49.2 4.7 %collective-permute-done.5.refs_5_.refs_1_ = bf16[528,128]{1,0:T(8,128)(2,1)S(1)} collective-permute-done((bf16[528,128]{1,0:T(8,128)(2,1)S(1)}, bf16[528,128]{1,0:T(8,128)(2,1)S(1)}, u32[]{:S(2)}, u32[]{:S(2)}) %collective-permute-start.5) | collective-permute-done | bytes 135200 | tf_op jit(solution)/shard_map/ppermute | solution.py:778
  54.0 3.8 %collective-permute-done.6.refs_6_.refs_2_ = bf16[528,128]{1,0:T(8,128)(2,1)S(1)} collective-permute-done((bf16[528,128]{1,0:T(8,128)(2,1)S(1)}, bf16[528,128]{1,0:T(8,128)(2,1)S(1)}, u32[]{:S(2)}, u32[]{:S(2)}) %collective-permute-start.6) | collective-permute-done | bytes 135200 | tf_op jit(solution)/shard_map/ppermute | solution.py:778
  57.8 2.9 %collective-permute-done.7.refs_7_.refs_3_ = bf16[528,128]{1,0:T(8,128)(2,1)S(1)} collective-permute-done((bf16[528,128]{1,0:T(8,128)(2,1)S(1)}, bf16[528,128]{1,0:T(8,128)(2,1)S(1)}, u32[]{:S(2)}, u32[]{:S(2)}) %collective-permute-start.7) | collective-permute-done | bytes 135200 | tf_op jit(solution)/shard_map/ppermute | solution.py:778
  60.7 0.1 collective-permute-start.8
  60.8 3.2 %gram_pieces.1 = f32[16,16,128]{2,1,0:T(8,128)} custom-call(bf16[8,672,128]{2,1,0:T(8,128)(2,1)S(1)} %all-to-all-done.near_ref.refs_0_, bf16[528,128]{1,0:T(8,128)(2,1)S(1)} %collective-permute-done.refs_0_, bf16[528,128]{1,0:T(8,128)(2,1)S(1)} %collective-permute-done.1.refs_1_, bf16[528,128]{1,0:T(8,128)(2,1)S(1)} %collective-permute-done.2.refs_2_, ...), custom_call_target="tpu_custom_call" | custom-call | flops 536870912 | bytes 2097152 | tf_op jit(solution)/shard_map/gram_pieces/pallas_call | solution.py:552
  64.0 5.8 %all-to-all-start.1 = ((f32[16,16,128]{2,1,0:T(8,128)}), f32[16,16,128]{2,1,0:T(8,128)S(1)}, u32[]{:S(2)}, u32[]{:S(2)}) async-start(f32[16,16,128]{2,1,0:T(8,128)} %gram_pieces.1), calls=%async_computation.1 | async-start | bytes 262144 | tf_op jit(solution)/shard_map/all_to_all | solution.py:365
  69.7 2.4 %gradient_pieces.4 = (bf16[4,512,128]{2,1,0:T(8,128)(2,1)}, f32[8,128]{1,0:T(8,128)}) custom-call(bf16[528,128]{1,0:T(8,128)(2,1)S(1)} %collective-permute-done.4.refs_4_.refs_0_, bf16[528,128]{1,0:T(8,128)(2,1)S(1)} %collective-permute-done.5.refs_5_.refs_1_, bf16[528,128]{1,0:T(8,128)(2,1)S(1)} %collective-permute-done.6.refs_6_.refs_2_, ...), custom_call_target="tpu_custom_call" | custom-call | flops 7864320 | bytes 2097152 | tf_op jit(solution)/shard_map/gradient_pieces/pallas_call | solution.py:625
  72.1 3.1 %gradient_pieces.5 = (bf16[8,512,128]{2,1,0:T(8,128)(2,1)}, f32[8,128]{1,0:T(8,128)}) custom-call(bf16[8,672,128]{2,1,0:T(8,128)(2,1)S(1)} %all-to-all-done.near_ref.refs_0_, bf16[512,128]{1,0:T(8,128)(2,1)S(1)} %get-tuple-element.42.refs_4_.refs_1_, bf16[512,128]{1,0:T(8,128)(2,1)S(1)} %get-tuple-element.43.refs_5_.refs_2_), custom_call_target="tpu_custom_call" | custom-call | flops 15728640 | bytes 4194304 | tf_op jit(solution)/shard_map/gradient_pieces/pallas_call | solution.py:625
  75.3 2.8 %all-to-all-done.1.refs_12_ = f32[16,16,128]{2,1,0:T(8,128)S(1)} async-done(((f32[16,16,128]{2,1,0:T(8,128)}), f32[16,16,128]{2,1,0:T(8,128)S(1)}, u32[]{:S(2)}, u32[]{:S(2)}) %all-to-all-start.1) | async-done | bytes 131104 | tf_op jit(solution)/shard_map/all_to_all | solution.py:365
  78.1 4.7 %update_pieces.1 = (bf16[8,640,128]{2,1,0:T(8,128)(2,1)S(1)}, bf16[384,128]{1,0:T(8,128)(2,1)S(1)}, bf16[384,128]{1,0:T(8,128)(2,1)S(1)}, bf16[384,128]{1,0:T(8,...) custom-call(bf16[8,672,128]{2,1,0:T(8,128)(2,1)S(1)} %all-to-all-don, ...), custom_call_target="tpu_custom_call" | custom-call | flops 1073741824 | bytes 6291456 | tf_op jit(solution)/shard_map/update_pieces/pallas_call | solution.py:759
  82.8 1.0 copy-done
  83.9 0.6 copy-done.1
  84.5 0.7 copy-done.3
  85.1 0.6 copy-done.5
  85.8 5.4 %all-to-all-start.2 = ((bf16[8,640,128]{2,1,0:T(8,128)(2,1)}), bf16[8,640,128]{2,1,0:T(8,128)(2,1)}, u32[]{:S(2)}, u32[]{:S(2)}) async-start(bf16[8,640,128]{2,1,0:T(8,128)(2,1)} %copy-done), calls=%async_computation.2 | async-start | bytes 2621440 | tf_op jit(solution)/shard_map/all_to_all | solution.py:783
  91.2 1.2 collective-permute-start.9
  92.4 1.7 %collective-permute-start.10 = (bf16[384,128]{1,0:T(8,128)(2,1)S(1)}, bf16[384,128]{1,0:T(8,128)(2,1)S(1)}, u32[]{:S(2)}, u32[]{:S(2)}) collective-permute-start(bf16[384,128]{1,0:T(8,128)(2,1)S(1)} %copy-done.4), channel_id=1, source_target_pairs={{0,9},{1,8},{2,11},{3,10},{4,13},{5,12},{6,15},{7,14},{8,1},{9,0},... | collective-permute-start | bytes 294920 | tf_op jit(solution)/shard_map/ppermute | solution.py:778
  94.1 2.1 %collective-permute-start.11 = (bf16[384,128]{1,0:T(8,128)(2,1)S(1)}, bf16[384,128]{1,0:T(8,128)(2,1)S(1)}, u32[]{:S(2)}, u32[]{:S(2)}) collective-permute-start(bf16[384,128]{1,0:T(8,128)(2,1)S(1)} %copy-done.2), channel_id=1, source_target_pairs={{0,10},{1,11},{2,8},{3,9},{4,14},{5,15},{6,12},{7,13},{8,2},{9,3},... | collective-permute-start | bytes 294920 | tf_op jit(solution)/shard_map/ppermute | solution.py:778
  96.2 1.2 collective-permute-start.12
  97.4 0.0 collective-permute-start.13
  97.5 12.0 %collective-permute-done.9.refs_1_ = bf16[384,128]{1,0:T(8,128)(2,1)S(1)} collective-permute-done((bf16[384,128]{1,0:T(8,128)(2,1)S(1)}, bf16[384,128]{1,0:T(8,128)(2,1)S(1)}, u32[]{:S(2)}, u32[]{:S(2)}) %collective-permute-start.9) | collective-permute-done | bytes 98336 | tf_op jit(solution)/shard_map/ppermute | solution.py:778
  109.5 1.1 collective-permute-start.14
  110.6 1.7 %collective-permute-done.10.refs_2_ = bf16[384,128]{1,0:T(8,128)(2,1)S(1)} collective-permute-done((bf16[384,128]{1,0:T(8,128)(2,1)S(1)}, bf16[384,128]{1,0:T(8,128)(2,1)S(1)}, u32[]{:S(2)}, u32[]{:S(2)}) %collective-permute-start.10) | collective-permute-done | bytes 98336 | tf_op jit(solution)/shard_map/ppermute | solution.py:778
  112.3 1.5 %collective-permute-start.15 = (bf16[384,128]{1,0:T(8,128)(2,1)S(1)}, bf16[384,128]{1,0:T(8,128)(2,1)S(1)}, u32[]{:S(2)}, u32[]{:S(2)}) collective-permute-start(bf16[384,128]{1,0:T(8,128)(2,1)S(1)} %get-tuple-element.55), channel_id=1, source_target_pairs={{0,14},{1,15},{2,12},{3,13},{4,10},{5,11},{6,8},{7,9},{8,6},{9,7},... | collective-permute-start | bytes 294920 | tf_op jit(solution)/shard_map/ppermute | solution.py:778
  113.8 0.9 collective-permute-done.11.refs_3_
  114.7 1.2 collective-permute-start.16
  115.9 4.0 %join_pieces.4.refs_0_ = bf16[1,1048576]{1,0:T(2,128)(2,1)} custom-call(bf16[8,640,128]{2,1,0:T(8,128)(2,1)} %all-to-all-done.2.refs_0_), custom_call_target="tpu_custom_call" | custom-call | bytes 3932160 | tf_op jit(solution)/shard_map/join_pieces/pallas_call | solution.py:497
  119.9 1.0 join_pieces.5.refs_0_
  120.9 5.9 %collective-permute-done.14.refs_2_ = bf16[384,128]{1,0:T(8,128)(2,1)S(1)} collective-permute-done((bf16[384,128]{1,0:T(8,128)(2,1)S(1)}, bf16[384,128]{1,0:T(8,128)(2,1)S(1)}, u32[]{:S(2)}, u32[]{:S(2)}) %collective-permute-start.14) | collective-permute-done | bytes 98336 | tf_op jit(solution)/shard_map/ppermute | solution.py:778
  126.8 0.8 join_pieces.6.refs_0_
  127.6 2.2 %collective-permute-done.15.refs_1_ = bf16[384,128]{1,0:T(8,128)(2,1)S(1)} collective-permute-done((bf16[384,128]{1,0:T(8,128)(2,1)S(1)}, bf16[384,128]{1,0:T(8,128)(2,1)S(1)}, u32[]{:S(2)}, u32[]{:S(2)}) %collective-permute-start.15) | collective-permute-done | bytes 98336 | tf_op jit(solution)/shard_map/ppermute | solution.py:778
  129.8 2.1 %collective-permute-done.16.refs_2_ = bf16[384,128]{1,0:T(8,128)(2,1)S(1)} collective-permute-done((bf16[384,128]{1,0:T(8,128)(2,1)S(1)}, bf16[384,128]{1,0:T(8,128)(2,1)S(1)}, u32[]{:S(2)}, u32[]{:S(2)}) %collective-permute-start.16) | collective-permute-done | bytes 98336 | tf_op jit(solution)/shard_map/ppermute | solution.py:778
  131.9 0.8 join_pieces.7
  (17 shorter events, 0.1 us)
Async XLA Ops:
  4.9 55.8 %all-to-all-start = ((bf16[8,672,128]{2,1,0:T(8,128)(2,1)}), bf16[8,672,128]{2,1,0:T(8,128)(2,1)S(1)}, u32[]{:S(2)}, u32[]{:S(2)}) async-start(bf16[8,672,128]{2,1,0:T(8,128)(2,1)} %get-tuple-element.31), calls=%async_computation | async-start | bytes 2752512 | tf_op jit(solution)/shard_map/all_to_all | solution.py:783
  9.5 20.9 %collective-permute-start = (bf16[528,128]{1,0:T(8,128)(2,1)S(1)}, bf16[528,128]{1,0:T(8,128)(2,1)S(1)}, u32[]{:S(2)}, u32[]{:S(2)}) collective-permute-start(bf16[528,128]{1,0:T(8,128)(2,1)S(1)} %get-tuple-element.32), channel_id=1, source_target_pairs={{0,8},{1,9},{2,10},{3,11},{4,12},{5,13},{6,14},{7,15},{8,0},{9,1},... | collective-permute-start | bytes 405512 | tf_op jit(solution)/shard_map/ppermute | solution.py:778
  11.8 22.2 %collective-permute-start.1 = (bf16[528,128]{1,0:T(8,128)(2,1)S(1)}, bf16[528,128]{1,0:T(8,128)(2,1)S(1)}, u32[]{:S(2)}, u32[]{:S(2)}) collective-permute-start(bf16[528,128]{1,0:T(8,128)(2,1)S(1)} %get-tuple-element.33), channel_id=1, source_target_pairs={{0,9},{1,8},{2,11},{3,10},{4,13},{5,12},{6,15},{7,14},{8,1},{9,0},... | collective-permute-start | bytes 405512 | tf_op jit(solution)/shard_map/ppermute | solution.py:778
  12.4 24.8 %collective-permute-start.2 = (bf16[528,128]{1,0:T(8,128)(2,1)S(1)}, bf16[528,128]{1,0:T(8,128)(2,1)S(1)}, u32[]{:S(2)}, u32[]{:S(2)}) collective-permute-start(bf16[528,128]{1,0:T(8,128)(2,1)S(1)} %get-tuple-element.34), channel_id=1, source_target_pairs={{0,10},{1,11},{2,8},{3,9},{4,14},{5,15},{6,12},{7,13},{8,2},{9,3},... | collective-permute-start | bytes 405512 | tf_op jit(solution)/shard_map/ppermute | solution.py:778
  15.6 25.2 %collective-permute-start.3 = (bf16[528,128]{1,0:T(8,128)(2,1)S(1)}, bf16[528,128]{1,0:T(8,128)(2,1)S(1)}, u32[]{:S(2)}, u32[]{:S(2)}) collective-permute-start(bf16[528,128]{1,0:T(8,128)(2,1)S(1)} %get-tuple-element.35), channel_id=1, source_target_pairs={{0,11},{1,10},{2,9},{3,8},{4,15},{5,14},{6,13},{7,12},{8,3},{9,2},... | collective-permute-start | bytes 405512 | tf_op jit(solution)/shard_map/ppermute | solution.py:778
  15.9 33.4 %collective-permute-start.4 = (bf16[528,128]{1,0:T(8,128)(2,1)S(1)}, bf16[528,128]{1,0:T(8,128)(2,1)S(1)}, u32[]{:S(2)}, u32[]{:S(2)}) collective-permute-start(bf16[528,128]{1,0:T(8,128)(2,1)S(1)} %get-tuple-element.36), channel_id=1, source_target_pairs={{0,12},{1,13},{2,14},{3,15},{4,8},{5,9},{6,10},{7,11},{8,4},{9,5},... | collective-permute-start | bytes 405512 | tf_op jit(solution)/shard_map/ppermute | solution.py:778
  30.4 23.6 %collective-permute-start.5 = (bf16[528,128]{1,0:T(8,128)(2,1)S(1)}, bf16[528,128]{1,0:T(8,128)(2,1)S(1)}, u32[]{:S(2)}, u32[]{:S(2)}) collective-permute-start(bf16[528,128]{1,0:T(8,128)(2,1)S(1)} %get-tuple-element.37), channel_id=1, source_target_pairs={{0,13},{1,12},{2,15},{3,14},{4,9},{5,8},{6,11},{7,10},{8,5},{9,4},... | collective-permute-start | bytes 405512 | tf_op jit(solution)/shard_map/ppermute | solution.py:778
  34.0 23.8 %collective-permute-start.6 = (bf16[528,128]{1,0:T(8,128)(2,1)S(1)}, bf16[528,128]{1,0:T(8,128)(2,1)S(1)}, u32[]{:S(2)}, u32[]{:S(2)}) collective-permute-start(bf16[528,128]{1,0:T(8,128)(2,1)S(1)} %get-tuple-element.38), channel_id=1, source_target_pairs={{0,14},{1,15},{2,12},{3,13},{4,10},{5,11},{6,8},{7,9},{8,6},{9,7},... | collective-permute-start | bytes 405512 | tf_op jit(solution)/shard_map/ppermute | solution.py:778
  37.1 23.5 %collective-permute-start.7 = (bf16[528,128]{1,0:T(8,128)(2,1)S(1)}, bf16[528,128]{1,0:T(8,128)(2,1)S(1)}, u32[]{:S(2)}, u32[]{:S(2)}) collective-permute-start(bf16[528,128]{1,0:T(8,128)(2,1)S(1)} %get-tuple-element.39), channel_id=1, source_target_pairs={{0,15},{1,14},{2,13},{3,12},{4,11},{5,10},{6,9},{7,8},{8,7},{9,6},... | collective-permute-start | bytes 405512 | tf_op jit(solution)/shard_map/ppermute | solution.py:778
  60.7 17.4 %collective-permute-start.8 = (bf16[8,144,128]{2,1,0:T(8,128)(2,1)S(1)}, bf16[8,144,128]{2,1,0:T(8,128)(2,1)S(1)}, u32[]{:S(2)}, u32[]{:S(2)}) collective-permute-start(bf16[8,144,128]{2,1,0:T(8,128)(2,1)S(1)} %raw_states.1.refs_9_), channel_id=1, source_target_pairs={{0,8},{1,9},{2,10},{3,11},{4,12},{5,13},{6,14},{7,15},{8,0},{9,1},... | collective-permute-start | bytes 884744 | tf_op jit(solution)/shard_map/ppermute | solution.py:778
  64.0 14.2 %all-to-all-start.1 = ((f32[16,16,128]{2,1,0:T(8,128)}), f32[16,16,128]{2,1,0:T(8,128)S(1)}, u32[]{:S(2)}, u32[]{:S(2)}) async-start(f32[16,16,128]{2,1,0:T(8,128)} %gram_pieces.1), calls=%async_computation.1 | async-start | bytes 262144 | tf_op jit(solution)/shard_map/all_to_all | solution.py:365
  82.8 1.1 copy-start
  83.9 0.6 copy-start.1
  84.5 0.7 copy-start.3
  85.1 0.7 copy-start.5
  85.8 5.4 %copy-start.6 = (bf16[384,128]{1,0:T(8,128)(2,1)S(1)}, bf16[384,128]{1,0:T(8,128)(2,1)}, u32[]{:S(2)}) copy-start(bf16[384,128]{1,0:T(8,128)(2,1)} %copy-done.5) | copy-start | bytes 294916
  85.8 6.6 %copy-start.4 = (bf16[384,128]{1,0:T(8,128)(2,1)S(1)}, bf16[384,128]{1,0:T(8,128)(2,1)}, u32[]{:S(2)}) copy-start(bf16[384,128]{1,0:T(8,128)(2,1)} %copy-done.3) | copy-start | bytes 294916
  85.8 8.3 %copy-start.2 = (bf16[384,128]{1,0:T(8,128)(2,1)S(1)}, bf16[384,128]{1,0:T(8,128)(2,1)}, u32[]{:S(2)}) copy-start(bf16[384,128]{1,0:T(8,128)(2,1)} %copy-done.1) | copy-start | bytes 294916
  85.8 30.0 %all-to-all-start.2 = ((bf16[8,640,128]{2,1,0:T(8,128)(2,1)}), bf16[8,640,128]{2,1,0:T(8,128)(2,1)}, u32[]{:S(2)}, u32[]{:S(2)}) async-start(bf16[8,640,128]{2,1,0:T(8,128)(2,1)} %copy-done), calls=%async_computation.2 | async-start | bytes 2621440 | tf_op jit(solution)/shard_map/all_to_all | solution.py:783
  91.2 18.3 %collective-permute-start.9 = (bf16[384,128]{1,0:T(8,128)(2,1)S(1)}, bf16[384,128]{1,0:T(8,128)(2,1)S(1)}, u32[]{:S(2)}, u32[]{:S(2)}) collective-permute-start(bf16[384,128]{1,0:T(8,128)(2,1)S(1)} %copy-done.6), channel_id=1, source_target_pairs={{0,8},{1,9},{2,10},{3,11},{4,12},{5,13},{6,14},{7,15},{8,0},{9,1},... | collective-permute-start | bytes 294920 | tf_op jit(solution)/shard_map/ppermute | solution.py:778
  92.4 19.9 %collective-permute-start.10 = (bf16[384,128]{1,0:T(8,128)(2,1)S(1)}, bf16[384,128]{1,0:T(8,128)(2,1)S(1)}, u32[]{:S(2)}, u32[]{:S(2)}) collective-permute-start(bf16[384,128]{1,0:T(8,128)(2,1)S(1)} %copy-done.4), channel_id=1, source_target_pairs={{0,9},{1,8},{2,11},{3,10},{4,13},{5,12},{6,15},{7,14},{8,1},{9,0},... | collective-permute-start | bytes 294920 | tf_op jit(solution)/shard_map/ppermute | solution.py:778
  94.1 20.5 %collective-permute-start.11 = (bf16[384,128]{1,0:T(8,128)(2,1)S(1)}, bf16[384,128]{1,0:T(8,128)(2,1)S(1)}, u32[]{:S(2)}, u32[]{:S(2)}) collective-permute-start(bf16[384,128]{1,0:T(8,128)(2,1)S(1)} %copy-done.2), channel_id=1, source_target_pairs={{0,10},{1,11},{2,8},{3,9},{4,14},{5,15},{6,12},{7,13},{8,2},{9,3},... | collective-permute-start | bytes 294920 | tf_op jit(solution)/shard_map/ppermute | solution.py:778
  96.2 23.7 %collective-permute-start.12 = (bf16[384,128]{1,0:T(8,128)(2,1)S(1)}, bf16[384,128]{1,0:T(8,128)(2,1)S(1)}, u32[]{:S(2)}, u32[]{:S(2)}) collective-permute-start(bf16[384,128]{1,0:T(8,128)(2,1)S(1)} %get-tuple-element.52), channel_id=1, source_target_pairs={{0,11},{1,10},{2,9},{3,8},{4,15},{5,14},{6,13},{7,12},{8,3},{9,2},... | collective-permute-start | bytes 294920 | tf_op jit(solution)/shard_map/ppermute | solution.py:778
  97.4 23.5 %collective-permute-start.13 = (bf16[384,128]{1,0:T(8,128)(2,1)S(1)}, bf16[384,128]{1,0:T(8,128)(2,1)S(1)}, u32[]{:S(2)}, u32[]{:S(2)}) collective-permute-start(bf16[384,128]{1,0:T(8,128)(2,1)S(1)} %get-tuple-element.53), channel_id=1, source_target_pairs={{0,12},{1,13},{2,14},{3,15},{4,8},{5,9},{6,10},{7,11},{8,4},{9,5},... | collective-permute-start | bytes 294920 | tf_op jit(solution)/shard_map/ppermute | solution.py:778
  109.5 17.3 %collective-permute-start.14 = (bf16[384,128]{1,0:T(8,128)(2,1)S(1)}, bf16[384,128]{1,0:T(8,128)(2,1)S(1)}, u32[]{:S(2)}, u32[]{:S(2)}) collective-permute-start(bf16[384,128]{1,0:T(8,128)(2,1)S(1)} %get-tuple-element.54), channel_id=1, source_target_pairs={{0,13},{1,12},{2,15},{3,14},{4,9},{5,8},{6,11},{7,10},{8,5},{9,4},... | collective-permute-start | bytes 294920 | tf_op jit(solution)/shard_map/ppermute | solution.py:778
  112.3 17.5 %collective-permute-start.15 = (bf16[384,128]{1,0:T(8,128)(2,1)S(1)}, bf16[384,128]{1,0:T(8,128)(2,1)S(1)}, u32[]{:S(2)}, u32[]{:S(2)}) collective-permute-start(bf16[384,128]{1,0:T(8,128)(2,1)S(1)} %get-tuple-element.55), channel_id=1, source_target_pairs={{0,14},{1,15},{2,12},{3,13},{4,10},{5,11},{6,8},{7,9},{8,6},{9,7},... | collective-permute-start | bytes 294920 | tf_op jit(solution)/shard_map/ppermute | solution.py:778
  114.7 17.3 %collective-permute-start.16 = (bf16[384,128]{1,0:T(8,128)(2,1)S(1)}, bf16[384,128]{1,0:T(8,128)(2,1)S(1)}, u32[]{:S(2)}, u32[]{:S(2)}) collective-permute-start(bf16[384,128]{1,0:T(8,128)(2,1)S(1)} %get-tuple-element.56), channel_id=1, source_target_pairs={{0,15},{1,14},{2,13},{3,12},{4,11},{5,10},{6,9},{7,8},{8,7},{9,6},... | collective-permute-start | bytes 294920 | tf_op jit(solution)/shard_map/ppermute | solution.py:778

commit v17 on v14

--- a/solution.py
+++ b/solution.py
@@ -506,7 +506,7 @@
     half = total // 2
     pieces, out_ref, pairs = refs[:half], refs[-2], refs[-1]
     wide = total * TILE
-    tiles = 4
+    tiles = 8
     pairs[...] = jnp.zeros_like(pairs)
 
     def step(i, carry):
@@ -699,13 +699,20 @@
     for fetch in fetches:
         fetch.wait()
 
-    def near_store(i):
-        part = lines_of(i * BLOCK, BLOCK)
-        return pltpu.make_async_copy(near_out.at[:, part, :], near_to.at[:, part, :], out_sems.at[i, 0])
-
-    def far_store(x, i):
-        part = lines_of(i * BLOCK - raw, BLOCK)
-        return pltpu.make_async_copy(far_out.at[x, part, :], far_tos[x].at[part, :], out_sems.at[i, 1 + x])
+    stores = []
+
+    def store(source, target, at):
+        stores.append(pltpu.make_async_copy(source, target, out_sems.at[at]))
+        stores[-1].start()
+
+    def store_near(first, last, at):
+        part = pl.ds(first, last - first)
+        store(near_out.at[:, part, :], near_to.at[:, part, :], (half, at))
+
+    def store_far(first, last, at):
+        part = pl.ds(first - raw, last - first)
+        for x, far_to in enumerate(far_tos):
+            store(far_out.at[x, part, :], far_to.at[part, :], (x, at))
 
     def slab_step(with_far, i, carry):
         rows = wide if with_far else high
@@ -719,10 +726,6 @@
             near_out[:, part, :] = new[:high].reshape(half, TILE, LANES)
             if with_far:
                 far_out[:, lines_of(at - raw, TILE), :] = new[high:].reshape(half, TILE, LANES)
-        near_store(i).start()
-        if with_far:
-            for x in range(half):
-                far_store(x, i).start()
         return carry
 
     here = lax.axis_index("slab").astype(jnp.int32) % half
@@ -739,23 +742,20 @@
             states, slopes = jnp.concatenate(states, axis=0), jnp.concatenate(slopes, axis=0)
             new = mix(mixer.at[:high, :], own.at[:high, :], numbers_ref, total, states, slopes)
             near_out[:, lines_of(lines + at, TILE), :] = new.reshape(half, TILE, LANES)
-        near_store(lines // BLOCK + i).start()
         return carry
 
-    def finish(i, carry):
-        near_store(i).wait()
-        return carry
-
-    def finish_far(i, carry):
-        for x in range(half):
-            far_store(x, i).wait()
-        return carry
-
     lax.fori_loop(0, raw // BLOCK, raw_step, 0)
+    store_near(lines, lines + raw, 0)
     lax.fori_loop(0, raw // BLOCK, functools.partial(slab_step, False), 0)
-    lax.fori_loop(raw // BLOCK, lines // BLOCK, functools.partial(slab_step, True), 0)
-    lax.fori_loop(0, (lines + raw) // BLOCK, finish, 0)
-    lax.fori_loop(raw // BLOCK, lines // BLOCK, finish_far, 0)
+    middle = (raw + 2 * lines) // 3 // BLOCK * BLOCK
+    lax.fori_loop(raw // BLOCK, middle // BLOCK, functools.partial(slab_step, True), 0)
+    store_near(0, middle, 1)
+    store_far(raw, middle, 0)
+    lax.fori_loop(middle // BLOCK, lines // BLOCK, functools.partial(slab_step, True), 0)
+    store_near(middle, lines, 2)
+    store_far(middle, lines, 1)
+    for copy in stores:
+        copy.wait()
 
 
 def update_pieces(numbers, grams, near, far, across, raw_fields, grads, groups, raw, lines):
@@ -780,7 +780,7 @@
             pltpu.VMEM((total, lines, LANES), BF16),
             pltpu.VMEM((total, raw, LANES), BF16),
             pltpu.SemaphoreType.DMA((total,)),
-            pltpu.SemaphoreType.DMA(((lines + raw) // BLOCK, 1 + half)),
+            pltpu.SemaphoreType.DMA((half + 1, 3)),
         ],
     )(near, *far, across, *raw_fields, numbers, grams, *grads)
 

time: 131 us -> 131 us (level)
  Pallas kernels: 27.3 us -> 25.9 us
  transfers between devices with their start and end apart: 20 -> 20, of which waited for: 15 -> 15; matrix products, arithmetic and copies ran while one was open for 0% -> 0% of each run, Pallas kernels for 12% -> 11%
where the time goes in v17:
time: 131 us; the launch traced here: 130 us
  waiting for transfers between devices  69.1 us (53%)
  starting transfers between devices  33 us (25%)
  Pallas kernels  25.9 us (20%)
  between operations  2.13 us (2%)
    ppermute x17, waiting for transfers between devices, exchange(): return lax.ppermute(piece, 'slab', [(i, i ^ k) for i in range(slabs)])  65.5 us
    ppermute x17, starting transfers between devices, exchange(): return lax.ppermute(piece, 'slab', [(i, i ^ k) for i in range(slabs)])  17.9 us
    all_to_all x2, starting transfers between devices, swap_near(): lax.all_to_all(pieces, 'slab', 0, 0, axis_index_groups=groups, tiled=True)  9.37 us
    pallas_call x3, Pallas kernels, gradient_pieces(): call(functools.partial(gradient_pieces_body, views, len(arrays), len(numb...  7.36 us
    all_to_all x1, starting transfers between devices, swap(): lax.all_to_all(slabs, 'slab', split_axis=0, concat_axis=0, tiled=True)  5.74 us
    pallas_call x1, Pallas kernels, update_pieces(): call(functools.partial(update_pieces_body, half, raw, lines, groups), 'up...  5.67 us
    pallas_call x4, Pallas kernels, join_pieces(): call(functools.partial(join_pieces_body, pieces, slabs // 2, raw, NCELL /...  5.54 us
    pallas_call x1, Pallas kernels, split_pieces(): call(functools.partial(split_pieces_body, slabs, raw, lines, len(fields))...  4.88 us
  transfers between devices with their start and end apart: 20, of which 15 were waited for; matrix products, arithmetic and copies ran while one was open for 0% of the time, Pallas kernels for 11%

profile of v17, /device:TPU:9, one launch (start us, length us, event | category | flops | bytes accessed | tf_op | source)
XLA Modules:
  0.0 130.2 jit_solution(731184630307715599)
XLA Ops:
  0.0 4.9 %split_pieces.1 = (bf16[8,672,128]{2,1,0:T(8,128)(2,1)}, bf16[528,128]{1,0:T(8,128)(2,1)S(1)}, bf16[528,128]{1,0:T(8,128)(2,1)S(1)}, bf16[528,128]{1,0:T(8,128)(...) custom-call(bf16[1,1048576]{1,0:T(2,128)(2,1)} %row_ref.1, ...), custom_call_target="tpu_custom_call" | custom-call | bytes 7372800 | tf_op jit(solution)/shard_map/split_pieces/pallas_call | solution.py:445
  4.9 4.6 %all-to-all-start = ((bf16[8,672,128]{2,1,0:T(8,128)(2,1)}), bf16[8,672,128]{2,1,0:T(8,128)(2,1)S(1)}, u32[]{:S(2)}, u32[]{:S(2)}) async-start(bf16[8,672,128]{2,1,0:T(8,128)(2,1)} %get-tuple-element.31), calls=%async_computation | async-start | bytes 2752512 | tf_op jit(solution)/shard_map/all_to_all | solution.py:794
  9.5 2.3 %collective-permute-start = (bf16[528,128]{1,0:T(8,128)(2,1)S(1)}, bf16[528,128]{1,0:T(8,128)(2,1)S(1)}, u32[]{:S(2)}, u32[]{:S(2)}) collective-permute-start(bf16[528,128]{1,0:T(8,128)(2,1)S(1)} %get-tuple-element.32), channel_id=1, source_target_pairs={{0,8},{1,9},{2,10},{3,11},{4,12},{5,13},{6,14},{7,15},{8,0},{9,1},... | collective-permute-start | bytes 405512 | tf_op jit(solution)/shard_map/ppermute | solution.py:789
  11.8 0.6 collective-permute-start.1
  12.4 3.2 %collective-permute-start.2 = (bf16[528,128]{1,0:T(8,128)(2,1)S(1)}, bf16[528,128]{1,0:T(8,128)(2,1)S(1)}, u32[]{:S(2)}, u32[]{:S(2)}) collective-permute-start(bf16[528,128]{1,0:T(8,128)(2,1)S(1)} %get-tuple-element.34), channel_id=1, source_target_pairs={{0,10},{1,11},{2,8},{3,9},{4,14},{5,15},{6,12},{7,13},{8,2},{9,3},... | collective-permute-start | bytes 405512 | tf_op jit(solution)/shard_map/ppermute | solution.py:789
  15.6 0.3 collective-permute-start.3
  15.9 1.0 collective-permute-start.4
  16.9 13.5 %collective-permute-done.refs_0_ = bf16[528,128]{1,0:T(8,128)(2,1)S(1)} collective-permute-done((bf16[528,128]{1,0:T(8,128)(2,1)S(1)}, bf16[528,128]{1,0:T(8,128)(2,1)S(1)}, u32[]{:S(2)}, u32[]{:S(2)}) %collective-permute-start) | collective-permute-done | bytes 135200 | tf_op jit(solution)/shard_map/ppermute | solution.py:789
  30.4 0.0 collective-permute-start.5
  30.4 3.6 %collective-permute-done.1.refs_1_ = bf16[528,128]{1,0:T(8,128)(2,1)S(1)} collective-permute-done((bf16[528,128]{1,0:T(8,128)(2,1)S(1)}, bf16[528,128]{1,0:T(8,128)(2,1)S(1)}, u32[]{:S(2)}, u32[]{:S(2)}) %collective-permute-start.1) | collective-permute-done | bytes 135200 | tf_op jit(solution)/shard_map/ppermute | solution.py:789
  34.0 0.3 collective-permute-start.6
  34.3 2.8 %collective-permute-done.2.refs_2_ = bf16[528,128]{1,0:T(8,128)(2,1)S(1)} collective-permute-done((bf16[528,128]{1,0:T(8,128)(2,1)S(1)}, bf16[528,128]{1,0:T(8,128)(2,1)S(1)}, u32[]{:S(2)}, u32[]{:S(2)}) %collective-permute-start.2) | collective-permute-done | bytes 135200 | tf_op jit(solution)/shard_map/ppermute | solution.py:789
  39.1 1.7 %collective-permute-done.3.refs_3_ = bf16[528,128]{1,0:T(8,128)(2,1)S(1)} collective-permute-done((bf16[528,128]{1,0:T(8,128)(2,1)S(1)}, bf16[528,128]{1,0:T(8,128)(2,1)S(1)}, u32[]{:S(2)}, u32[]{:S(2)}) %collective-permute-start.3) | collective-permute-done | bytes 135200 | tf_op jit(solution)/shard_map/ppermute | solution.py:789
  40.7 1.8 %gradient_pieces.3 = (bf16[4,512,128]{2,1,0:T(8,128)(2,1)}, f32[8,128]{1,0:T(8,128)S(1)}) custom-call(bf16[528,128]{1,0:T(8,128)(2,1)S(1)} %collective-permute-done.refs_0_, bf16[528,128]{1,0:T(8,128)(2,1)S(1)} %collective-permute-done.1.refs_1_, bf16[528,128]{1,0:T(8,128)(2,1)S(1)} %collective-permute-done.2.refs_2_, ...), custom_call_target="tpu_custom_call" | custom-call | flops 7864320 | bytes 2097152 | tf_op jit(solution)/shard_map/gradient_pieces/pallas_call | solution.py:610
  42.5 6.7 %collective-permute-done.4.refs_4_.refs_0_ = bf16[528,128]{1,0:T(8,128)(2,1)S(1)} collective-permute-done((bf16[528,128]{1,0:T(8,128)(2,1)S(1)}, bf16[528,128]{1,0:T(8,128)(2,1)S(1)}, u32[]{:S(2)}, u32[]{:S(2)}) %collective-permute-start.4) | collective-permute-done | bytes 135200 | tf_op jit(solution)/shard_map/ppermute | solution.py:789
  49.2 4.7 %collective-permute-done.5.refs_5_.refs_1_ = bf16[528,128]{1,0:T(8,128)(2,1)S(1)} collective-permute-done((bf16[528,128]{1,0:T(8,128)(2,1)S(1)}, bf16[528,128]{1,0:T(8,128)(2,1)S(1)}, u32[]{:S(2)}, u32[]{:S(2)}) %collective-permute-start.5) | collective-permute-done | bytes 135200 | tf_op jit(solution)/shard_map/ppermute | solution.py:789
  54.0 3.8 %collective-permute-done.6.refs_6_.refs_2_ = bf16[528,128]{1,0:T(8,128)(2,1)S(1)} collective-permute-done((bf16[528,128]{1,0:T(8,128)(2,1)S(1)}, bf16[528,128]{1,0:T(8,128)(2,1)S(1)}, u32[]{:S(2)}, u32[]{:S(2)}) %collective-permute-start.6) | collective-permute-done | bytes 135200 | tf_op jit(solution)/shard_map/ppermute | solution.py:789
  57.8 2.9 %collective-permute-done.7.refs_7_.refs_3_ = bf16[528,128]{1,0:T(8,128)(2,1)S(1)} collective-permute-done((bf16[528,128]{1,0:T(8,128)(2,1)S(1)}, bf16[528,128]{1,0:T(8,128)(2,1)S(1)}, u32[]{:S(2)}, u32[]{:S(2)}) %collective-permute-start.7) | collective-permute-done | bytes 135200 | tf_op jit(solution)/shard_map/ppermute | solution.py:789
  60.7 0.0 all-to-all-done.near_ref.refs_0_
  60.7 0.1 collective-permute-start.8
  60.8 2.4 %gram_pieces.1 = f32[16,16,128]{2,1,0:T(8,128)} custom-call(bf16[8,672,128]{2,1,0:T(8,128)(2,1)S(1)} %all-to-all-done.near_ref.refs_0_, bf16[528,128]{1,0:T(8,128)(2,1)S(1)} %collective-permute-done.refs_0_, bf16[528,128]{1,0:T(8,128)(2,1)S(1)} %collective-permute-done.1.refs_1_, bf16[528,128]{1,0:T(8,128)(2,1)S(1)} %collective-permute-done.2.refs_2_, ...), custom_call_target="tpu_custom_call" | custom-call | flops 536870912 | bytes 2097152 | tf_op jit(solution)/shard_map/gram_pieces/pallas_call | solution.py:537
  63.2 5.7 %all-to-all-start.1 = ((f32[16,16,128]{2,1,0:T(8,128)}), f32[16,16,128]{2,1,0:T(8,128)S(1)}, u32[]{:S(2)}, u32[]{:S(2)}) async-start(f32[16,16,128]{2,1,0:T(8,128)} %gram_pieces.1), calls=%async_computation.1 | async-start | bytes 262144 | tf_op jit(solution)/shard_map/all_to_all | solution.py:365
  68.9 2.4 %gradient_pieces.4 = (bf16[4,512,128]{2,1,0:T(8,128)(2,1)}, f32[8,128]{1,0:T(8,128)}) custom-call(bf16[528,128]{1,0:T(8,128)(2,1)S(1)} %collective-permute-done.4.refs_4_.refs_0_, bf16[528,128]{1,0:T(8,128)(2,1)S(1)} %collective-permute-done.5.refs_5_.refs_1_, bf16[528,128]{1,0:T(8,128)(2,1)S(1)} %collective-permute-done.6.refs_6_.refs_2_, ...), custom_call_target="tpu_custom_call" | custom-call | flops 7864320 | bytes 2097152 | tf_op jit(solution)/shard_map/gradient_pieces/pallas_call | solution.py:610
  71.3 3.2 %gradient_pieces.5 = (bf16[8,512,128]{2,1,0:T(8,128)(2,1)}, f32[8,128]{1,0:T(8,128)}) custom-call(bf16[8,672,128]{2,1,0:T(8,128)(2,1)S(1)} %all-to-all-done.near_ref.refs_0_, bf16[512,128]{1,0:T(8,128)(2,1)S(1)} %get-tuple-element.42.refs_4_.refs_1_, bf16[512,128]{1,0:T(8,128)(2,1)S(1)} %get-tuple-element.43.refs_5_.refs_2_), custom_call_target="tpu_custom_call" | custom-call | flops 15728640 | bytes 4194304 | tf_op jit(solution)/shard_map/gradient_pieces/pallas_call | solution.py:610
  74.5 3.6 %all-to-all-done.1.refs_12_ = f32[16,16,128]{2,1,0:T(8,128)S(1)} async-done(((f32[16,16,128]{2,1,0:T(8,128)}), f32[16,16,128]{2,1,0:T(8,128)S(1)}, u32[]{:S(2)}, u32[]{:S(2)}) %all-to-all-start.1) | async-done | bytes 131104 | tf_op jit(solution)/shard_map/all_to_all | solution.py:365
  78.1 0.0 collective-permute-done.8.refs_8_
  78.1 5.7 %update_pieces.1 = (bf16[8,640,128]{2,1,0:T(8,128)(2,1)}, bf16[384,128]{1,0:T(8,128)(2,1)}, bf16[384,128]{1,0:T(8,128)(2,1)}, bf16[384,128]{1,0:T(8,128)(2,1)}, ...) custom-call(bf16[8,672,128]{2,1,0:T(8,128)(2,1)S(1)} %all-to-all-don, ...), custom_call_target="tpu_custom_call" | custom-call | flops 1073741824 | bytes 6291456 | tf_op jit(solution)/shard_map/update_pieces/pallas_call | solution.py:767
  83.9 4.8 %all-to-all-start.2 = ((bf16[8,640,128]{2,1,0:T(8,128)(2,1)}), bf16[8,640,128]{2,1,0:T(8,128)(2,1)S(1)}, u32[]{:S(2)}, u32[]{:S(2)}) async-start(bf16[8,640,128]{2,1,0:T(8,128)(2,1)} %get-tuple-element.48), calls=%async_computation.2 | async-start | bytes 2621440 | tf_op jit(solution)/shard_map/all_to_all | solution.py:794
  88.7 1.2 collective-permute-start.9
  89.8 1.7 %collective-permute-start.10 = (bf16[384,128]{1,0:T(8,128)(2,1)S(1)}, bf16[384,128]{1,0:T(8,128)(2,1)S(1)}, u32[]{:S(2)}, u32[]{:S(2)}) collective-permute-start(bf16[384,128]{1,0:T(8,128)(2,1)S(1)} %copy-done.6), channel_id=1, source_target_pairs={{0,9},{1,8},{2,11},{3,10},{4,13},{5,12},{6,15},{7,14},{8,1},{9,0},... | collective-permute-start | bytes 294920 | tf_op jit(solution)/shard_map/ppermute | solution.py:789
  91.6 2.1 %collective-permute-start.11 = (bf16[384,128]{1,0:T(8,128)(2,1)S(1)}, bf16[384,128]{1,0:T(8,128)(2,1)S(1)}, u32[]{:S(2)}, u32[]{:S(2)}) collective-permute-start(bf16[384,128]{1,0:T(8,128)(2,1)S(1)} %copy-done.5), channel_id=1, source_target_pairs={{0,10},{1,11},{2,8},{3,9},{4,14},{5,15},{6,12},{7,13},{8,2},{9,3},... | collective-permute-start | bytes 294920 | tf_op jit(solution)/shard_map/ppermute | solution.py:789
  93.7 1.2 collective-permute-start.12
  94.9 0.0 collective-permute-start.13
  94.9 12.0 %collective-permute-done.9.refs_1_ = bf16[384,128]{1,0:T(8,128)(2,1)S(1)} collective-permute-done((bf16[384,128]{1,0:T(8,128)(2,1)S(1)}, bf16[384,128]{1,0:T(8,128)(2,1)S(1)}, u32[]{:S(2)}, u32[]{:S(2)}) %collective-permute-start.9) | collective-permute-done | bytes 98336 | tf_op jit(solution)/shard_map/ppermute | solution.py:789
  107.0 1.1 collective-permute-start.14
  108.1 1.6 %collective-permute-done.10.refs_2_ = bf16[384,128]{1,0:T(8,128)(2,1)S(1)} collective-permute-done((bf16[384,128]{1,0:T(8,128)(2,1)S(1)}, bf16[384,128]{1,0:T(8,128)(2,1)S(1)}, u32[]{:S(2)}, u32[]{:S(2)}) %collective-permute-start.10) | collective-permute-done | bytes 98336 | tf_op jit(solution)/shard_map/ppermute | solution.py:789
  109.7 1.5 %collective-permute-start.15 = (bf16[384,128]{1,0:T(8,128)(2,1)S(1)}, bf16[384,128]{1,0:T(8,128)(2,1)S(1)}, u32[]{:S(2)}, u32[]{:S(2)}) collective-permute-start(bf16[384,128]{1,0:T(8,128)(2,1)S(1)} %copy-done.1), channel_id=1, source_target_pairs={{0,14},{1,15},{2,12},{3,13},{4,10},{5,11},{6,8},{7,9},{8,6},{9,7},... | collective-permute-start | bytes 294920 | tf_op jit(solution)/shard_map/ppermute | solution.py:789
  111.2 0.9 collective-permute-done.11.refs_3_
  112.1 1.2 collective-permute-start.16
  113.3 3.0 %join_pieces.4.refs_0_ = bf16[1,1048576]{1,0:T(2,128)(2,1)} custom-call(bf16[8,640,128]{2,1,0:T(8,128)(2,1)S(1)} %all-to-all-done.2.refs_0_), custom_call_target="tpu_custom_call" | custom-call | bytes 3932160 | tf_op jit(solution)/shard_map/join_pieces/pallas_call | solution.py:483
  116.3 0.0 collective-permute-done.12.refs_4_
  116.3 1.0 join_pieces.5.refs_0_
  117.3 0.0 collective-permute-done.13.refs_1_
  117.3 7.0 %collective-permute-done.14.refs_2_ = bf16[384,128]{1,0:T(8,128)(2,1)S(1)} collective-permute-done((bf16[384,128]{1,0:T(8,128)(2,1)S(1)}, bf16[384,128]{1,0:T(8,128)(2,1)S(1)}, u32[]{:S(2)}, u32[]{:S(2)}) %collective-permute-start.14) | collective-permute-done | bytes 98336 | tf_op jit(solution)/shard_map/ppermute | solution.py:789
  124.2 0.8 join_pieces.6.refs_0_
  125.0 2.2 %collective-permute-done.15.refs_1_ = bf16[384,128]{1,0:T(8,128)(2,1)S(1)} collective-permute-done((bf16[384,128]{1,0:T(8,128)(2,1)S(1)}, bf16[384,128]{1,0:T(8,128)(2,1)S(1)}, u32[]{:S(2)}, u32[]{:S(2)}) %collective-permute-start.15) | collective-permute-done | bytes 98336 | tf_op jit(solution)/shard_map/ppermute | solution.py:789
  127.2 2.1 %collective-permute-done.16.refs_2_ = bf16[384,128]{1,0:T(8,128)(2,1)S(1)} collective-permute-done((bf16[384,128]{1,0:T(8,128)(2,1)S(1)}, bf16[384,128]{1,0:T(8,128)(2,1)S(1)}, u32[]{:S(2)}, u32[]{:S(2)}) %collective-permute-start.16) | collective-permute-done | bytes 98336 | tf_op jit(solution)/shard_map/ppermute | solution.py:789
  129.4 0.8 join_pieces.7
  (19 shorter events, 0.1 us)
Async XLA Ops:
  4.9 55.8 %all-to-all-start = ((bf16[8,672,128]{2,1,0:T(8,128)(2,1)}), bf16[8,672,128]{2,1,0:T(8,128)(2,1)S(1)}, u32[]{:S(2)}, u32[]{:S(2)}) async-start(bf16[8,672,128]{2,1,0:T(8,128)(2,1)} %get-tuple-element.31), calls=%async_computation | async-start | bytes 2752512 | tf_op jit(solution)/shard_map/all_to_all | solution.py:794
  9.5 20.9 %collective-permute-start = (bf16[528,128]{1,0:T(8,128)(2,1)S(1)}, bf16[528,128]{1,0:T(8,128)(2,1)S(1)}, u32[]{:S(2)}, u32[]{:S(2)}) collective-permute-start(bf16[528,128]{1,0:T(8,128)(2,1)S(1)} %get-tuple-element.32), channel_id=1, source_target_pairs={{0,8},{1,9},{2,10},{3,11},{4,12},{5,13},{6,14},{7,15},{8,0},{9,1},... | collective-permute-start | bytes 405512 | tf_op jit(solution)/shard_map/ppermute | solution.py:789
  11.8 22.2 %collective-permute-start.1 = (bf16[528,128]{1,0:T(8,128)(2,1)S(1)}, bf16[528,128]{1,0:T(8,128)(2,1)S(1)}, u32[]{:S(2)}, u32[]{:S(2)}) collective-permute-start(bf16[528,128]{1,0:T(8,128)(2,1)S(1)} %get-tuple-element.33), channel_id=1, source_target_pairs={{0,9},{1,8},{2,11},{3,10},{4,13},{5,12},{6,15},{7,14},{8,1},{9,0},... | collective-permute-start | bytes 405512 | tf_op jit(solution)/shard_map/ppermute | solution.py:789
  12.4 24.8 %collective-permute-start.2 = (bf16[528,128]{1,0:T(8,128)(2,1)S(1)}, bf16[528,128]{1,0:T(8,128)(2,1)S(1)}, u32[]{:S(2)}, u32[]{:S(2)}) collective-permute-start(bf16[528,128]{1,0:T(8,128)(2,1)S(1)} %get-tuple-element.34), channel_id=1, source_target_pairs={{0,10},{1,11},{2,8},{3,9},{4,14},{5,15},{6,12},{7,13},{8,2},{9,3},... | collective-permute-start | bytes 405512 | tf_op jit(solution)/shard_map/ppermute | solution.py:789
  15.6 25.2 %collective-permute-start.3 = (bf16[528,128]{1,0:T(8,128)(2,1)S(1)}, bf16[528,128]{1,0:T(8,128)(2,1)S(1)}, u32[]{:S(2)}, u32[]{:S(2)}) collective-permute-start(bf16[528,128]{1,0:T(8,128)(2,1)S(1)} %get-tuple-element.35), channel_id=1, source_target_pairs={{0,11},{1,10},{2,9},{3,8},{4,15},{5,14},{6,13},{7,12},{8,3},{9,2},... | collective-permute-start | bytes 405512 | tf_op jit(solution)/shard_map/ppermute | solution.py:789
  15.9 33.4 %collective-permute-start.4 = (bf16[528,128]{1,0:T(8,128)(2,1)S(1)}, bf16[528,128]{1,0:T(8,128)(2,1)S(1)}, u32[]{:S(2)}, u32[]{:S(2)}) collective-permute-start(bf16[528,128]{1,0:T(8,128)(2,1)S(1)} %get-tuple-element.36), channel_id=1, source_target_pairs={{0,12},{1,13},{2,14},{3,15},{4,8},{5,9},{6,10},{7,11},{8,4},{9,5},... | collective-permute-start | bytes 405512 | tf_op jit(solution)/shard_map/ppermute | solution.py:789
  30.4 23.6 %collective-permute-start.5 = (bf16[528,128]{1,0:T(8,128)(2,1)S(1)}, bf16[528,128]{1,0:T(8,128)(2,1)S(1)}, u32[]{:S(2)}, u32[]{:S(2)}) collective-permute-start(bf16[528,128]{1,0:T(8,128)(2,1)S(1)} %get-tuple-element.37), channel_id=1, source_target_pairs={{0,13},{1,12},{2,15},{3,14},{4,9},{5,8},{6,11},{7,10},{8,5},{9,4},... | collective-permute-start | bytes 405512 | tf_op jit(solution)/shard_map/ppermute | solution.py:789
  34.0 23.8 %collective-permute-start.6 = (bf16[528,128]{1,0:T(8,128)(2,1)S(1)}, bf16[528,128]{1,0:T(8,128)(2,1)S(1)}, u32[]{:S(2)}, u32[]{:S(2)}) collective-permute-start(bf16[528,128]{1,0:T(8,128)(2,1)S(1)} %get-tuple-element.38), channel_id=1, source_target_pairs={{0,14},{1,15},{2,12},{3,13},{4,10},{5,11},{6,8},{7,9},{8,6},{9,7},... | collective-permute-start | bytes 405512 | tf_op jit(solution)/shard_map/ppermute | solution.py:789
  37.1 23.5 %collective-permute-start.7 = (bf16[528,128]{1,0:T(8,128)(2,1)S(1)}, bf16[528,128]{1,0:T(8,128)(2,1)S(1)}, u32[]{:S(2)}, u32[]{:S(2)}) collective-permute-start(bf16[528,128]{1,0:T(8,128)(2,1)S(1)} %get-tuple-element.39), channel_id=1, source_target_pairs={{0,15},{1,14},{2,13},{3,12},{4,11},{5,10},{6,9},{7,8},{8,7},{9,6},... | collective-permute-start | bytes 405512 | tf_op jit(solution)/shard_map/ppermute | solution.py:789
  60.7 17.4 %collective-permute-start.8 = (bf16[8,144,128]{2,1,0:T(8,128)(2,1)S(1)}, bf16[8,144,128]{2,1,0:T(8,128)(2,1)S(1)}, u32[]{:S(2)}, u32[]{:S(2)}) collective-permute-start(bf16[8,144,128]{2,1,0:T(8,128)(2,1)S(1)} %raw_states.1.refs_9_), channel_id=1, source_target_pairs={{0,8},{1,9},{2,10},{3,11},{4,12},{5,13},{6,14},{7,15},{8,0},{9,1},... | collective-permute-start | bytes 884744 | tf_op jit(solution)/shard_map/ppermute | solution.py:789
  63.2 14.9 %all-to-all-start.1 = ((f32[16,16,128]{2,1,0:T(8,128)}), f32[16,16,128]{2,1,0:T(8,128)S(1)}, u32[]{:S(2)}, u32[]{:S(2)}) async-start(f32[16,16,128]{2,1,0:T(8,128)} %gram_pieces.1), calls=%async_computation.1 | async-start | bytes 262144 | tf_op jit(solution)/shard_map/all_to_all | solution.py:365
  83.8 4.9 %copy-start.7 = (bf16[384,128]{1,0:T(8,128)(2,1)S(1)}, bf16[384,128]{1,0:T(8,128)(2,1)}, u32[]{:S(2)}) copy-start(bf16[384,128]{1,0:T(8,128)(2,1)} %get-tuple-element.49) | copy-start | bytes 294916
  83.8 6.0 %copy-start.6 = (bf16[384,128]{1,0:T(8,128)(2,1)S(1)}, bf16[384,128]{1,0:T(8,128)(2,1)}, u32[]{:S(2)}) copy-start(bf16[384,128]{1,0:T(8,128)(2,1)} %get-tuple-element.50) | copy-start | bytes 294916
  83.8 7.7 %copy-start.5 = (bf16[384,128]{1,0:T(8,128)(2,1)S(1)}, bf16[384,128]{1,0:T(8,128)(2,1)}, u32[]{:S(2)}) copy-start(bf16[384,128]{1,0:T(8,128)(2,1)} %get-tuple-element.51) | copy-start | bytes 294916
  83.8 9.8 %copy-start.4 = (bf16[384,128]{1,0:T(8,128)(2,1)S(1)}, bf16[384,128]{1,0:T(8,128)(2,1)}, u32[]{:S(2)}) copy-start(bf16[384,128]{1,0:T(8,128)(2,1)} %get-tuple-element.52) | copy-start | bytes 294916
  83.8 11.0 %copy-start.3 = (bf16[384,128]{1,0:T(8,128)(2,1)S(1)}, bf16[384,128]{1,0:T(8,128)(2,1)}, u32[]{:S(2)}) copy-start(bf16[384,128]{1,0:T(8,128)(2,1)} %get-tuple-element.53) | copy-start | bytes 294916
  83.9 23.1 %copy-start.2 = (bf16[384,128]{1,0:T(8,128)(2,1)S(1)}, bf16[384,128]{1,0:T(8,128)(2,1)}, u32[]{:S(2)}) copy-start(bf16[384,128]{1,0:T(8,128)(2,1)} %get-tuple-element.54) | copy-start | bytes 294916
  83.9 25.9 %copy-start.1 = (bf16[384,128]{1,0:T(8,128)(2,1)S(1)}, bf16[384,128]{1,0:T(8,128)(2,1)}, u32[]{:S(2)}) copy-start(bf16[384,128]{1,0:T(8,128)(2,1)} %get-tuple-element.55) | copy-start | bytes 294916
  83.9 28.2 %copy-start = (bf16[384,128]{1,0:T(8,128)(2,1)S(1)}, bf16[384,128]{1,0:T(8,128)(2,1)}, u32[]{:S(2)}) copy-start(bf16[384,128]{1,0:T(8,128)(2,1)} %get-tuple-element.56) | copy-start | bytes 294916
  83.9 29.4 %all-to-all-start.2 = ((bf16[8,640,128]{2,1,0:T(8,128)(2,1)}), bf16[8,640,128]{2,1,0:T(8,128)(2,1)S(1)}, u32[]{:S(2)}, u32[]{:S(2)}) async-start(bf16[8,640,128]{2,1,0:T(8,128)(2,1)} %get-tuple-element.48), calls=%async_computation.2 | async-start | bytes 2621440 | tf_op jit(solution)/shard_map/all_to_all | solution.py:794
  88.7 18.3 %collective-permute-start.9 = (bf16[384,128]{1,0:T(8,128)(2,1)S(1)}, bf16[384,128]{1,0:T(8,128)(2,1)S(1)}, u32[]{:S(2)}, u32[]{:S(2)}) collective-permute-start(bf16[384,128]{1,0:T(8,128)(2,1)S(1)} %copy-done.7), channel_id=1, source_target_pairs={{0,8},{1,9},{2,10},{3,11},{4,12},{5,13},{6,14},{7,15},{8,0},{9,1},... | collective-permute-start | bytes 294920 | tf_op jit(solution)/shard_map/ppermute | solution.py:789
  89.8 19.9 %collective-permute-start.10 = (bf16[384,128]{1,0:T(8,128)(2,1)S(1)}, bf16[384,128]{1,0:T(8,128)(2,1)S(1)}, u32[]{:S(2)}, u32[]{:S(2)}) collective-permute-start(bf16[384,128]{1,0:T(8,128)(2,1)S(1)} %copy-done.6), channel_id=1, source_target_pairs={{0,9},{1,8},{2,11},{3,10},{4,13},{5,12},{6,15},{7,14},{8,1},{9,0},... | collective-permute-start | bytes 294920 | tf_op jit(solution)/shard_map/ppermute | solution.py:789
  91.6 20.5 %collective-permute-start.11 = (bf16[384,128]{1,0:T(8,128)(2,1)S(1)}, bf16[384,128]{1,0:T(8,128)(2,1)S(1)}, u32[]{:S(2)}, u32[]{:S(2)}) collective-permute-start(bf16[384,128]{1,0:T(8,128)(2,1)S(1)} %copy-done.5), channel_id=1, source_target_pairs={{0,10},{1,11},{2,8},{3,9},{4,14},{5,15},{6,12},{7,13},{8,2},{9,3},... | collective-permute-start | bytes 294920 | tf_op jit(solution)/shard_map/ppermute | solution.py:789
  93.7 22.6 %collective-permute-start.12 = (bf16[384,128]{1,0:T(8,128)(2,1)S(1)}, bf16[384,128]{1,0:T(8,128)(2,1)S(1)}, u32[]{:S(2)}, u32[]{:S(2)}) collective-permute-start(bf16[384,128]{1,0:T(8,128)(2,1)S(1)} %copy-done.4), channel_id=1, source_target_pairs={{0,11},{1,10},{2,9},{3,8},{4,15},{5,14},{6,13},{7,12},{8,3},{9,2},... | collective-permute-start | bytes 294920 | tf_op jit(solution)/shard_map/ppermute | solution.py:789
  94.9 22.4 %collective-permute-start.13 = (bf16[384,128]{1,0:T(8,128)(2,1)S(1)}, bf16[384,128]{1,0:T(8,128)(2,1)S(1)}, u32[]{:S(2)}, u32[]{:S(2)}) collective-permute-start(bf16[384,128]{1,0:T(8,128)(2,1)S(1)} %copy-done.3), channel_id=1, source_target_pairs={{0,12},{1,13},{2,14},{3,15},{4,8},{5,9},{6,10},{7,11},{8,4},{9,5},... | collective-permute-start | bytes 294920 | tf_op jit(solution)/shard_map/ppermute | solution.py:789
  107.0 17.3 %collective-permute-start.14 = (bf16[384,128]{1,0:T(8,128)(2,1)S(1)}, bf16[384,128]{1,0:T(8,128)(2,1)S(1)}, u32[]{:S(2)}, u32[]{:S(2)}) collective-permute-start(bf16[384,128]{1,0:T(8,128)(2,1)S(1)} %copy-done.2), channel_id=1, source_target_pairs={{0,13},{1,12},{2,15},{3,14},{4,9},{5,8},{6,11},{7,10},{8,5},{9,4},... | collective-permute-start | bytes 294920 | tf_op jit(solution)/shard_map/ppermute | solution.py:789
  109.7 17.5 %collective-permute-start.15 = (bf16[384,128]{1,0:T(8,128)(2,1)S(1)}, bf16[384,128]{1,0:T(8,128)(2,1)S(1)}, u32[]{:S(2)}, u32[]{:S(2)}) collective-permute-start(bf16[384,128]{1,0:T(8,128)(2,1)S(1)} %copy-done.1), channel_id=1, source_target_pairs={{0,14},{1,15},{2,12},{3,13},{4,10},{5,11},{6,8},{7,9},{8,6},{9,7},... | collective-permute-start | bytes 294920 | tf_op jit(solution)/shard_map/ppermute | solution.py:789
  112.1 17.3 %collective-permute-start.16 = (bf16[384,128]{1,0:T(8,128)(2,1)S(1)}, bf16[384,128]{1,0:T(8,128)(2,1)S(1)}, u32[]{:S(2)}, u32[]{:S(2)}) collective-permute-start(bf16[384,128]{1,0:T(8,128)(2,1)S(1)} %copy-done), channel_id=1, source_target_pairs={{0,15},{1,14},{2,13},{3,12},{4,11},{5,10},{6,9},{7,8},{8,7},{9,6},... | collective-permute-start | bytes 294920 | tf_op jit(solution)/shard_map/ppermute | solution.py:789

commit v18 on v17

--- a/solution.py
+++ b/solution.py
@@ -794,7 +794,7 @@
     return lax.all_to_all(pieces, "slab", 0, 0, axis_index_groups=groups, tiled=True)
 
 
-RAW = 128
+RAW = 64
 GRADIENTS = ((8, 9, 10, 11), (12, 13, 14, 15), (0, 1, 2, 3, 4, 5, 6, 7))
 
 

time: 131 us -> 134 us (1.023)
  starting transfers between devices: 33 us -> 38.7 us
  waiting for transfers between devices: 69.1 us -> 66.9 us
    ppermute x17, starting transfers between devices: 17.9 us -> 22 us  [exchange(): return lax.ppermute(piece, 'slab', [(i, i ^ k) for i in range(slabs)])]
    all_to_all x1, waiting for transfers between devices: 3.59 us -> 0.01 us  [swap(): lax.all_to_all(slabs, 'slab', split_axis=0, concat_axis=0, tiled=True)]
    all_to_all x2, starting transfers between devices: 9.37 us -> 11.9 us  [swap_near(): lax.all_to_all(pieces, 'slab', 0, 0, axis_index_groups=groups, tiled=True)]
    ppermute x17, waiting for transfers between devices: 65.5 us -> 66.9 us  [exchange(): return lax.ppermute(piece, 'slab', [(i, i ^ k) for i in range(slabs)])]
  transfers between devices with their start and end apart: 20 -> 20, of which waited for: 15 -> 15; matrix products, arithmetic and copies ran while one was open for 0% -> 0% of each run, Pallas kernels for 11% -> 9%
where the time goes in v18:
time: 134 us
  waiting for transfers between devices  66.9 us (50%)
  starting transfers between devices  38.7 us (29%)
  Pallas kernels  26 us (19%)
  between operations  2.12 us (2%)
    ppermute x17, waiting for transfers between devices, exchange(): return lax.ppermute(piece, 'slab', [(i, i ^ k) for i in range(slabs)])  66.9 us
    ppermute x17, starting transfers between devices, exchange(): return lax.ppermute(piece, 'slab', [(i, i ^ k) for i in range(slabs)])  22 us
    all_to_all x2, starting transfers between devices, swap_near(): lax.all_to_all(pieces, 'slab', 0, 0, axis_index_groups=groups, tiled=True)  11.9 us
    pallas_call x3, Pallas kernels, gradient_pieces(): call(functools.partial(gradient_pieces_body, views, len(arrays), len(numb...  7.36 us
    pallas_call x1, Pallas kernels, update_pieces(): call(functools.partial(update_pieces_body, half, raw, lines, groups), 'up...  6.02 us
    pallas_call x4, Pallas kernels, join_pieces(): call(functools.partial(join_pieces_body, pieces, slabs // 2, raw, NCELL /...  5.41 us
    all_to_all x1, starting transfers between devices, swap(): lax.all_to_all(slabs, 'slab', split_axis=0, concat_axis=0, tiled=True)  4.84 us
    pallas_call x1, Pallas kernels, split_pieces(): call(functools.partial(split_pieces_body, slabs, raw, lines, len(fields))...  4.75 us
  transfers between devices with their start and end apart: 20, of which 15 were waited for; matrix products, arithmetic and copies ran while one was open for 0% of the time, Pallas kernels for 9%

profile of v18, /device:TPU:9, one launch (start us, length us, event | category | flops | bytes accessed | tf_op | source)
XLA Modules:
  0.0 133.8 jit_solution(4719934257030446543)
XLA Ops:
  0.0 4.8 %split_pieces.1 = (bf16[8,608,128]{2,1,0:T(8,128)(2,1)}, bf16[528,128]{1,0:T(8,128)(2,1)S(1)}, bf16[528,128]{1,0:T(8,128)(2,1)S(1)}, bf16[528,128]{1,0:T(8,128)(...) custom-call(bf16[1,1048576]{1,0:T(2,128)(2,1)} %row_ref.1, ...), custom_call_target="tpu_custom_call" | custom-call | bytes 6979584 | tf_op jit(solution)/shard_map/split_pieces/pallas_call | solution.py:445
  4.8 4.6 %all-to-all-start = ((bf16[8,608,128]{2,1,0:T(8,128)(2,1)}), bf16[8,608,128]{2,1,0:T(8,128)(2,1)S(1)}, u32[]{:S(2)}, u32[]{:S(2)}) async-start(bf16[8,608,128]{2,1,0:T(8,128)(2,1)} %get-tuple-element.31), calls=%async_computation | async-start | bytes 2490368 | tf_op jit(solution)/shard_map/all_to_all | solution.py:794
  9.3 2.3 %collective-permute-start = (bf16[528,128]{1,0:T(8,128)(2,1)S(1)}, bf16[528,128]{1,0:T(8,128)(2,1)S(1)}, u32[]{:S(2)}, u32[]{:S(2)}) collective-permute-start(bf16[528,128]{1,0:T(8,128)(2,1)S(1)} %get-tuple-element.32), channel_id=1, source_target_pairs={{0,8},{1,9},{2,10},{3,11},{4,12},{5,13},{6,14},{7,15},{8,0},{9,1},... | collective-permute-start | bytes 405512 | tf_op jit(solution)/shard_map/ppermute | solution.py:789
  11.7 0.6 collective-permute-start.1
  12.2 3.2 %collective-permute-start.2 = (bf16[528,128]{1,0:T(8,128)(2,1)S(1)}, bf16[528,128]{1,0:T(8,128)(2,1)S(1)}, u32[]{:S(2)}, u32[]{:S(2)}) collective-permute-start(bf16[528,128]{1,0:T(8,128)(2,1)S(1)} %get-tuple-element.34), channel_id=1, source_target_pairs={{0,10},{1,11},{2,8},{3,9},{4,14},{5,15},{6,12},{7,13},{8,2},{9,3},... | collective-permute-start | bytes 405512 | tf_op jit(solution)/shard_map/ppermute | solution.py:789
  15.4 0.3 collective-permute-start.3
  15.7 1.0 collective-permute-start.4
  16.7 12.1 %collective-permute-done.refs_0_ = bf16[528,128]{1,0:T(8,128)(2,1)S(1)} collective-permute-done((bf16[528,128]{1,0:T(8,128)(2,1)S(1)}, bf16[528,128]{1,0:T(8,128)(2,1)S(1)}, u32[]{:S(2)}, u32[]{:S(2)}) %collective-permute-start) | collective-permute-done | bytes 135200 | tf_op jit(solution)/shard_map/ppermute | solution.py:789
  28.9 0.0 collective-permute-start.5
  28.9 3.6 %collective-permute-done.1.refs_1_ = bf16[528,128]{1,0:T(8,128)(2,1)S(1)} collective-permute-done((bf16[528,128]{1,0:T(8,128)(2,1)S(1)}, bf16[528,128]{1,0:T(8,128)(2,1)S(1)}, u32[]{:S(2)}, u32[]{:S(2)}) %collective-permute-start.1) | collective-permute-done | bytes 135200 | tf_op jit(solution)/shard_map/ppermute | solution.py:789
  32.5 0.3 collective-permute-start.6
  32.8 2.8 %collective-permute-done.2.refs_2_ = bf16[528,128]{1,0:T(8,128)(2,1)S(1)} collective-permute-done((bf16[528,128]{1,0:T(8,128)(2,1)S(1)}, bf16[528,128]{1,0:T(8,128)(2,1)S(1)}, u32[]{:S(2)}, u32[]{:S(2)}) %collective-permute-start.2) | collective-permute-done | bytes 135200 | tf_op jit(solution)/shard_map/ppermute | solution.py:789
  35.6 0.0 collective-permute-start.7
  37.6 1.7 %collective-permute-done.3.refs_3_ = bf16[528,128]{1,0:T(8,128)(2,1)S(1)} collective-permute-done((bf16[528,128]{1,0:T(8,128)(2,1)S(1)}, bf16[528,128]{1,0:T(8,128)(2,1)S(1)}, u32[]{:S(2)}, u32[]{:S(2)}) %collective-permute-start.3) | collective-permute-done | bytes 135200 | tf_op jit(solution)/shard_map/ppermute | solution.py:789
  39.2 1.8 %gradient_pieces.3 = (bf16[4,512,128]{2,1,0:T(8,128)(2,1)}, f32[8,128]{1,0:T(8,128)S(1)}) custom-call(bf16[528,128]{1,0:T(8,128)(2,1)S(1)} %collective-permute-done.refs_0_, bf16[528,128]{1,0:T(8,128)(2,1)S(1)} %collective-permute-done.1.refs_1_, bf16[528,128]{1,0:T(8,128)(2,1)S(1)} %collective-permute-done.2.refs_2_, ...), custom_call_target="tpu_custom_call" | custom-call | flops 7864320 | bytes 2097152 | tf_op jit(solution)/shard_map/gradient_pieces/pallas_call | solution.py:610
  41.0 8.1 %collective-permute-done.4.refs_4_.refs_0_ = bf16[528,128]{1,0:T(8,128)(2,1)S(1)} collective-permute-done((bf16[528,128]{1,0:T(8,128)(2,1)S(1)}, bf16[528,128]{1,0:T(8,128)(2,1)S(1)}, u32[]{:S(2)}, u32[]{:S(2)}) %collective-permute-start.4) | collective-permute-done | bytes 135200 | tf_op jit(solution)/shard_map/ppermute | solution.py:789
  49.1 3.4 %collective-permute-done.5.refs_5_.refs_1_ = bf16[528,128]{1,0:T(8,128)(2,1)S(1)} collective-permute-done((bf16[528,128]{1,0:T(8,128)(2,1)S(1)}, bf16[528,128]{1,0:T(8,128)(2,1)S(1)}, u32[]{:S(2)}, u32[]{:S(2)}) %collective-permute-start.5) | collective-permute-done | bytes 135200 | tf_op jit(solution)/shard_map/ppermute | solution.py:789
  52.5 4.0 %collective-permute-done.6.refs_6_.refs_2_ = bf16[528,128]{1,0:T(8,128)(2,1)S(1)} collective-permute-done((bf16[528,128]{1,0:T(8,128)(2,1)S(1)}, bf16[528,128]{1,0:T(8,128)(2,1)S(1)}, u32[]{:S(2)}, u32[]{:S(2)}) %collective-permute-start.6) | collective-permute-done | bytes 135200 | tf_op jit(solution)/shard_map/ppermute | solution.py:789
  56.4 2.9 %collective-permute-done.7.refs_7_.refs_3_ = bf16[528,128]{1,0:T(8,128)(2,1)S(1)} collective-permute-done((bf16[528,128]{1,0:T(8,128)(2,1)S(1)}, bf16[528,128]{1,0:T(8,128)(2,1)S(1)}, u32[]{:S(2)}, u32[]{:S(2)}) %collective-permute-start.7) | collective-permute-done | bytes 135200 | tf_op jit(solution)/shard_map/ppermute | solution.py:789
  59.3 0.0 all-to-all-done.near_ref.refs_0_
  59.3 2.4 %gram_pieces.1 = f32[16,16,128]{2,1,0:T(8,128)} custom-call(bf16[8,608,128]{2,1,0:T(8,128)(2,1)S(1)} %all-to-all-done.near_ref.refs_0_, bf16[528,128]{1,0:T(8,128)(2,1)S(1)} %collective-permute-done.refs_0_, bf16[528,128]{1,0:T(8,128)(2,1)S(1)} %collective-permute-done.1.refs_1_, bf16[528,128]{1,0:T(8,128)(2,1)S(1)} %collective-permute-done.2.refs_2_, ...), custom_call_target="tpu_custom_call" | custom-call | flops 536870912 | bytes 2097152 | tf_op jit(solution)/shard_map/gram_pieces/pallas_call | solution.py:537
  61.7 4.8 %all-to-all-start.1 = ((f32[16,16,128]{2,1,0:T(8,128)}), f32[16,16,128]{2,1,0:T(8,128)S(1)}, u32[]{:S(2)}, u32[]{:S(2)}) async-start(f32[16,16,128]{2,1,0:T(8,128)} %gram_pieces.1), calls=%async_computation.1 | async-start | bytes 262144 | tf_op jit(solution)/shard_map/all_to_all | solution.py:365
  66.6 2.1 %collective-permute-start.8 = (bf16[8,80,128]{2,1,0:T(8,128)(2,1)S(1)}, bf16[8,80,128]{2,1,0:T(8,128)(2,1)S(1)}, u32[]{:S(2)}, u32[]{:S(2)}) collective-permute-start(bf16[8,80,128]{2,1,0:T(8,128)(2,1)S(1)} %raw_states.1.refs_9_), channel_id=1, source_target_pairs={{0,8},{1,9},{2,10},{3,11},{4,12},{5,13},{6,14},{7,15},{8,0},{9,1},... | collective-permute-start | bytes 491528 | tf_op jit(solution)/shard_map/ppermute | solution.py:789
  68.7 2.4 %gradient_pieces.4 = (bf16[4,512,128]{2,1,0:T(8,128)(2,1)}, f32[8,128]{1,0:T(8,128)}) custom-call(bf16[528,128]{1,0:T(8,128)(2,1)S(1)} %collective-permute-done.4.refs_4_.refs_0_, bf16[528,128]{1,0:T(8,128)(2,1)S(1)} %collective-permute-done.5.refs_5_.refs_1_, bf16[528,128]{1,0:T(8,128)(2,1)S(1)} %collective-permute-done.6.refs_6_.refs_2_, ...), custom_call_target="tpu_custom_call" | custom-call | flops 7864320 | bytes 2097152 | tf_op jit(solution)/shard_map/gradient_pieces/pallas_call | solution.py:610
  71.0 3.2 %gradient_pieces.5 = (bf16[8,512,128]{2,1,0:T(8,128)(2,1)}, f32[8,128]{1,0:T(8,128)}) custom-call(bf16[8,608,128]{2,1,0:T(8,128)(2,1)S(1)} %all-to-all-done.near_ref.refs_0_, bf16[512,128]{1,0:T(8,128)(2,1)S(1)} %get-tuple-element.42.refs_4_.refs_1_, bf16[512,128]{1,0:T(8,128)(2,1)S(1)} %get-tuple-element.43.refs_5_.refs_2_), custom_call_target="tpu_custom_call" | custom-call | flops 15728640 | bytes 4194304 | tf_op jit(solution)/shard_map/gradient_pieces/pallas_call | solution.py:610
  74.2 2.6 %collective-permute-done.8.refs_8_ = bf16[8,80,128]{2,1,0:T(8,128)(2,1)S(1)} collective-permute-done((bf16[8,80,128]{2,1,0:T(8,128)(2,1)S(1)}, bf16[8,80,128]{2,1,0:T(8,128)(2,1)S(1)}, u32[]{:S(2)}, u32[]{:S(2)}) %collective-permute-start.8) | collective-permute-done | bytes 163872 | tf_op jit(solution)/shard_map/ppermute | solution.py:789
  76.8 6.0 %update_pieces.1 = (bf16[8,576,128]{2,1,0:T(8,128)(2,1)}, bf16[448,128]{1,0:T(8,128)(2,1)}, bf16[448,128]{1,0:T(8,128)(2,1)}, bf16[448,128]{1,0:T(8,128)(2,1)}, ...) custom-call(bf16[8,608,128]{2,1,0:T(8,128)(2,1)S(1)} %all-to-all-don, ...), custom_call_target="tpu_custom_call" | custom-call | flops 1073741824 | bytes 6291456 | tf_op jit(solution)/shard_map/update_pieces/pallas_call | solution.py:767
  82.9 7.3 %all-to-all-start.2 = ((bf16[8,576,128]{2,1,0:T(8,128)(2,1)}), bf16[8,576,128]{2,1,0:T(8,128)(2,1)S(1)}, u32[]{:S(2)}, u32[]{:S(2)}) async-start(bf16[8,576,128]{2,1,0:T(8,128)(2,1)} %get-tuple-element.48), calls=%async_computation.2 | async-start | bytes 2359296 | tf_op jit(solution)/shard_map/all_to_all | solution.py:794
  90.3 0.4 collective-permute-start.9
  90.7 2.5 %collective-permute-start.10 = (bf16[448,128]{1,0:T(8,128)(2,1)S(1)}, bf16[448,128]{1,0:T(8,128)(2,1)S(1)}, u32[]{:S(2)}, u32[]{:S(2)}) collective-permute-start(bf16[448,128]{1,0:T(8,128)(2,1)S(1)} %copy-done.6), channel_id=1, source_target_pairs={{0,9},{1,8},{2,11},{3,10},{4,13},{5,12},{6,15},{7,14},{8,1},{9,0},... | collective-permute-start | bytes 344072 | tf_op jit(solution)/shard_map/ppermute | solution.py:789
  93.2 1.3 collective-permute-start.11
  94.5 2.0 %collective-permute-start.12 = (bf16[448,128]{1,0:T(8,128)(2,1)S(1)}, bf16[448,128]{1,0:T(8,128)(2,1)S(1)}, u32[]{:S(2)}, u32[]{:S(2)}) collective-permute-start(bf16[448,128]{1,0:T(8,128)(2,1)S(1)} %copy-done.4), channel_id=1, source_target_pairs={{0,11},{1,10},{2,9},{3,8},{4,15},{5,14},{6,13},{7,12},{8,3},{9,2},... | collective-permute-start | bytes 344072 | tf_op jit(solution)/shard_map/ppermute | solution.py:789
  96.5 0.0 collective-permute-start.13
  96.5 10.3 %collective-permute-done.9.refs_1_ = bf16[448,128]{1,0:T(8,128)(2,1)S(1)} collective-permute-done((bf16[448,128]{1,0:T(8,128)(2,1)S(1)}, bf16[448,128]{1,0:T(8,128)(2,1)S(1)}, u32[]{:S(2)}, u32[]{:S(2)}) %collective-permute-start.9) | collective-permute-done | bytes 114720 | tf_op jit(solution)/shard_map/ppermute | solution.py:789
  106.8 1.9 %collective-permute-start.14 = (bf16[448,128]{1,0:T(8,128)(2,1)S(1)}, bf16[448,128]{1,0:T(8,128)(2,1)S(1)}, u32[]{:S(2)}, u32[]{:S(2)}) collective-permute-start(bf16[448,128]{1,0:T(8,128)(2,1)S(1)} %copy-done.2), channel_id=1, source_target_pairs={{0,13},{1,12},{2,15},{3,14},{4,9},{5,8},{6,11},{7,10},{8,5},{9,4},... | collective-permute-start | bytes 344072 | tf_op jit(solution)/shard_map/ppermute | solution.py:789
  108.7 1.3 collective-permute-done.10.refs_2_
  110.0 2.1 %collective-permute-start.15 = (bf16[448,128]{1,0:T(8,128)(2,1)S(1)}, bf16[448,128]{1,0:T(8,128)(2,1)S(1)}, u32[]{:S(2)}, u32[]{:S(2)}) collective-permute-start(bf16[448,128]{1,0:T(8,128)(2,1)S(1)} %copy-done.1), channel_id=1, source_target_pairs={{0,14},{1,15},{2,12},{3,13},{4,10},{5,11},{6,8},{7,9},{8,6},{9,7},... | collective-permute-start | bytes 344072 | tf_op jit(solution)/shard_map/ppermute | solution.py:789
  112.1 0.5 collective-permute-done.11.refs_3_
  112.6 1.9 %collective-permute-start.16 = (bf16[448,128]{1,0:T(8,128)(2,1)S(1)}, bf16[448,128]{1,0:T(8,128)(2,1)S(1)}, u32[]{:S(2)}, u32[]{:S(2)}) collective-permute-start(bf16[448,128]{1,0:T(8,128)(2,1)S(1)} %copy-done), channel_id=1, source_target_pairs={{0,15},{1,14},{2,13},{3,12},{4,11},{5,10},{6,9},{7,8},{8,7},{9,6},... | collective-permute-start | bytes 344072 | tf_op jit(solution)/shard_map/ppermute | solution.py:789
  114.5 0.0 all-to-all-done.2.refs_0_
  114.5 2.7 %join_pieces.4.refs_0_ = bf16[1,1048576]{1,0:T(2,128)(2,1)} custom-call(bf16[8,576,128]{2,1,0:T(8,128)(2,1)S(1)} %all-to-all-done.2.refs_0_), custom_call_target="tpu_custom_call" | custom-call | bytes 3538944 | tf_op jit(solution)/shard_map/join_pieces/pallas_call | solution.py:483
  117.3 0.0 collective-permute-done.12.refs_4_
  117.3 1.0 join_pieces.5.refs_0_
  118.4 8.7 %collective-permute-done.14.refs_2_ = bf16[448,128]{1,0:T(8,128)(2,1)S(1)} collective-permute-done((bf16[448,128]{1,0:T(8,128)(2,1)S(1)}, bf16[448,128]{1,0:T(8,128)(2,1)S(1)}, u32[]{:S(2)}, u32[]{:S(2)}) %collective-permute-start.14) | collective-permute-done | bytes 114720 | tf_op jit(solution)/shard_map/ppermute | solution.py:789
  127.1 0.8 join_pieces.6.refs_0_
  127.9 2.5 %collective-permute-done.15.refs_1_ = bf16[448,128]{1,0:T(8,128)(2,1)S(1)} collective-permute-done((bf16[448,128]{1,0:T(8,128)(2,1)S(1)}, bf16[448,128]{1,0:T(8,128)(2,1)S(1)}, u32[]{:S(2)}, u32[]{:S(2)}) %collective-permute-start.15) | collective-permute-done | bytes 114720 | tf_op jit(solution)/shard_map/ppermute | solution.py:789
  130.4 2.5 %collective-permute-done.16.refs_2_ = bf16[448,128]{1,0:T(8,128)(2,1)S(1)} collective-permute-done((bf16[448,128]{1,0:T(8,128)(2,1)S(1)}, bf16[448,128]{1,0:T(8,128)(2,1)S(1)}, u32[]{:S(2)}, u32[]{:S(2)}) %collective-permute-start.16) | collective-permute-done | bytes 114720 | tf_op jit(solution)/shard_map/ppermute | solution.py:789
  132.9 0.8 join_pieces.7
  (19 shorter events, 0.1 us)
Async XLA Ops:
  4.8 54.6 %all-to-all-start = ((bf16[8,608,128]{2,1,0:T(8,128)(2,1)}), bf16[8,608,128]{2,1,0:T(8,128)(2,1)S(1)}, u32[]{:S(2)}, u32[]{:S(2)}) async-start(bf16[8,608,128]{2,1,0:T(8,128)(2,1)} %get-tuple-element.31), calls=%async_computation | async-start | bytes 2490368 | tf_op jit(solution)/shard_map/all_to_all | solution.py:794
  9.3 19.5 %collective-permute-start = (bf16[528,128]{1,0:T(8,128)(2,1)S(1)}, bf16[528,128]{1,0:T(8,128)(2,1)S(1)}, u32[]{:S(2)}, u32[]{:S(2)}) collective-permute-start(bf16[528,128]{1,0:T(8,128)(2,1)S(1)} %get-tuple-element.32), channel_id=1, source_target_pairs={{0,8},{1,9},{2,10},{3,11},{4,12},{5,13},{6,14},{7,15},{8,0},{9,1},... | collective-permute-start | bytes 405512 | tf_op jit(solution)/shard_map/ppermute | solution.py:789
  11.7 20.8 %collective-permute-start.1 = (bf16[528,128]{1,0:T(8,128)(2,1)S(1)}, bf16[528,128]{1,0:T(8,128)(2,1)S(1)}, u32[]{:S(2)}, u32[]{:S(2)}) collective-permute-start(bf16[528,128]{1,0:T(8,128)(2,1)S(1)} %get-tuple-element.33), channel_id=1, source_target_pairs={{0,9},{1,8},{2,11},{3,10},{4,13},{5,12},{6,15},{7,14},{8,1},{9,0},... | collective-permute-start | bytes 405512 | tf_op jit(solution)/shard_map/ppermute | solution.py:789
  12.2 23.4 %collective-permute-start.2 = (bf16[528,128]{1,0:T(8,128)(2,1)S(1)}, bf16[528,128]{1,0:T(8,128)(2,1)S(1)}, u32[]{:S(2)}, u32[]{:S(2)}) collective-permute-start(bf16[528,128]{1,0:T(8,128)(2,1)S(1)} %get-tuple-element.34), channel_id=1, source_target_pairs={{0,10},{1,11},{2,8},{3,9},{4,14},{5,15},{6,12},{7,13},{8,2},{9,3},... | collective-permute-start | bytes 405512 | tf_op jit(solution)/shard_map/ppermute | solution.py:789
  15.4 23.8 %collective-permute-start.3 = (bf16[528,128]{1,0:T(8,128)(2,1)S(1)}, bf16[528,128]{1,0:T(8,128)(2,1)S(1)}, u32[]{:S(2)}, u32[]{:S(2)}) collective-permute-start(bf16[528,128]{1,0:T(8,128)(2,1)S(1)} %get-tuple-element.35), channel_id=1, source_target_pairs={{0,11},{1,10},{2,9},{3,8},{4,15},{5,14},{6,13},{7,12},{8,3},{9,2},... | collective-permute-start | bytes 405512 | tf_op jit(solution)/shard_map/ppermute | solution.py:789
  15.7 33.3 %collective-permute-start.4 = (bf16[528,128]{1,0:T(8,128)(2,1)S(1)}, bf16[528,128]{1,0:T(8,128)(2,1)S(1)}, u32[]{:S(2)}, u32[]{:S(2)}) collective-permute-start(bf16[528,128]{1,0:T(8,128)(2,1)S(1)} %get-tuple-element.36), channel_id=1, source_target_pairs={{0,12},{1,13},{2,14},{3,15},{4,8},{5,9},{6,10},{7,11},{8,4},{9,5},... | collective-permute-start | bytes 405512 | tf_op jit(solution)/shard_map/ppermute | solution.py:789
  28.9 23.6 %collective-permute-start.5 = (bf16[528,128]{1,0:T(8,128)(2,1)S(1)}, bf16[528,128]{1,0:T(8,128)(2,1)S(1)}, u32[]{:S(2)}, u32[]{:S(2)}) collective-permute-start(bf16[528,128]{1,0:T(8,128)(2,1)S(1)} %get-tuple-element.37), channel_id=1, source_target_pairs={{0,13},{1,12},{2,15},{3,14},{4,9},{5,8},{6,11},{7,10},{8,5},{9,4},... | collective-permute-start | bytes 405512 | tf_op jit(solution)/shard_map/ppermute | solution.py:789
  32.5 23.9 %collective-permute-start.6 = (bf16[528,128]{1,0:T(8,128)(2,1)S(1)}, bf16[528,128]{1,0:T(8,128)(2,1)S(1)}, u32[]{:S(2)}, u32[]{:S(2)}) collective-permute-start(bf16[528,128]{1,0:T(8,128)(2,1)S(1)} %get-tuple-element.38), channel_id=1, source_target_pairs={{0,14},{1,15},{2,12},{3,13},{4,10},{5,11},{6,8},{7,9},{8,6},{9,7},... | collective-permute-start | bytes 405512 | tf_op jit(solution)/shard_map/ppermute | solution.py:789
  35.6 23.7 %collective-permute-start.7 = (bf16[528,128]{1,0:T(8,128)(2,1)S(1)}, bf16[528,128]{1,0:T(8,128)(2,1)S(1)}, u32[]{:S(2)}, u32[]{:S(2)}) collective-permute-start(bf16[528,128]{1,0:T(8,128)(2,1)S(1)} %get-tuple-element.39), channel_id=1, source_target_pairs={{0,15},{1,14},{2,13},{3,12},{4,11},{5,10},{6,9},{7,8},{8,7},{9,6},... | collective-permute-start | bytes 405512 | tf_op jit(solution)/shard_map/ppermute | solution.py:789
  61.7 15.1 %all-to-all-start.1 = ((f32[16,16,128]{2,1,0:T(8,128)}), f32[16,16,128]{2,1,0:T(8,128)S(1)}, u32[]{:S(2)}, u32[]{:S(2)}) async-start(f32[16,16,128]{2,1,0:T(8,128)} %gram_pieces.1), calls=%async_computation.1 | async-start | bytes 262144 | tf_op jit(solution)/shard_map/all_to_all | solution.py:365
  66.6 10.3 %collective-permute-start.8 = (bf16[8,80,128]{2,1,0:T(8,128)(2,1)S(1)}, bf16[8,80,128]{2,1,0:T(8,128)(2,1)S(1)}, u32[]{:S(2)}, u32[]{:S(2)}) collective-permute-start(bf16[8,80,128]{2,1,0:T(8,128)(2,1)S(1)} %raw_states.1.refs_9_), channel_id=1, source_target_pairs={{0,8},{1,9},{2,10},{3,11},{4,12},{5,13},{6,14},{7,15},{8,0},{9,1},... | collective-permute-start | bytes 491528 | tf_op jit(solution)/shard_map/ppermute | solution.py:789
  82.9 7.4 %copy-start.7 = (bf16[448,128]{1,0:T(8,128)(2,1)S(1)}, bf16[448,128]{1,0:T(8,128)(2,1)}, u32[]{:S(2)}) copy-start(bf16[448,128]{1,0:T(8,128)(2,1)} %get-tuple-element.49) | copy-start | bytes 344068
  82.9 7.8 %copy-start.6 = (bf16[448,128]{1,0:T(8,128)(2,1)S(1)}, bf16[448,128]{1,0:T(8,128)(2,1)}, u32[]{:S(2)}) copy-start(bf16[448,128]{1,0:T(8,128)(2,1)} %get-tuple-element.50) | copy-start | bytes 344068
  82.9 10.3 %copy-start.5 = (bf16[448,128]{1,0:T(8,128)(2,1)S(1)}, bf16[448,128]{1,0:T(8,128)(2,1)}, u32[]{:S(2)}) copy-start(bf16[448,128]{1,0:T(8,128)(2,1)} %get-tuple-element.51) | copy-start | bytes 344068
  82.9 11.6 %copy-start.4 = (bf16[448,128]{1,0:T(8,128)(2,1)S(1)}, bf16[448,128]{1,0:T(8,128)(2,1)}, u32[]{:S(2)}) copy-start(bf16[448,128]{1,0:T(8,128)(2,1)} %get-tuple-element.52) | copy-start | bytes 344068
  82.9 13.6 %copy-start.3 = (bf16[448,128]{1,0:T(8,128)(2,1)S(1)}, bf16[448,128]{1,0:T(8,128)(2,1)}, u32[]{:S(2)}) copy-start(bf16[448,128]{1,0:T(8,128)(2,1)} %get-tuple-element.53) | copy-start | bytes 344068
  82.9 23.9 %copy-start.2 = (bf16[448,128]{1,0:T(8,128)(2,1)S(1)}, bf16[448,128]{1,0:T(8,128)(2,1)}, u32[]{:S(2)}) copy-start(bf16[448,128]{1,0:T(8,128)(2,1)} %get-tuple-element.54) | copy-start | bytes 344068
  82.9 27.1 %copy-start.1 = (bf16[448,128]{1,0:T(8,128)(2,1)S(1)}, bf16[448,128]{1,0:T(8,128)(2,1)}, u32[]{:S(2)}) copy-start(bf16[448,128]{1,0:T(8,128)(2,1)} %get-tuple-element.55) | copy-start | bytes 344068
  82.9 29.7 %copy-start = (bf16[448,128]{1,0:T(8,128)(2,1)S(1)}, bf16[448,128]{1,0:T(8,128)(2,1)}, u32[]{:S(2)}) copy-start(bf16[448,128]{1,0:T(8,128)(2,1)} %get-tuple-element.56) | copy-start | bytes 344068
  82.9 31.6 %all-to-all-start.2 = ((bf16[8,576,128]{2,1,0:T(8,128)(2,1)}), bf16[8,576,128]{2,1,0:T(8,128)(2,1)S(1)}, u32[]{:S(2)}, u32[]{:S(2)}) async-start(bf16[8,576,128]{2,1,0:T(8,128)(2,1)} %get-tuple-element.48), calls=%async_computation.2 | async-start | bytes 2359296 | tf_op jit(solution)/shard_map/all_to_all | solution.py:794
  90.3 16.5 %collective-permute-start.9 = (bf16[448,128]{1,0:T(8,128)(2,1)S(1)}, bf16[448,128]{1,0:T(8,128)(2,1)S(1)}, u32[]{:S(2)}, u32[]{:S(2)}) collective-permute-start(bf16[448,128]{1,0:T(8,128)(2,1)S(1)} %copy-done.7), channel_id=1, source_target_pairs={{0,8},{1,9},{2,10},{3,11},{4,12},{5,13},{6,14},{7,15},{8,0},{9,1},... | collective-permute-start | bytes 344072 | tf_op jit(solution)/shard_map/ppermute | solution.py:789
  90.7 19.3 %collective-permute-start.10 = (bf16[448,128]{1,0:T(8,128)(2,1)S(1)}, bf16[448,128]{1,0:T(8,128)(2,1)S(1)}, u32[]{:S(2)}, u32[]{:S(2)}) collective-permute-start(bf16[448,128]{1,0:T(8,128)(2,1)S(1)} %copy-done.6), channel_id=1, source_target_pairs={{0,9},{1,8},{2,11},{3,10},{4,13},{5,12},{6,15},{7,14},{8,1},{9,0},... | collective-permute-start | bytes 344072 | tf_op jit(solution)/shard_map/ppermute | solution.py:789
  93.2 19.5 %collective-permute-start.11 = (bf16[448,128]{1,0:T(8,128)(2,1)S(1)}, bf16[448,128]{1,0:T(8,128)(2,1)S(1)}, u32[]{:S(2)}, u32[]{:S(2)}) collective-permute-start(bf16[448,128]{1,0:T(8,128)(2,1)S(1)} %copy-done.5), channel_id=1, source_target_pairs={{0,10},{1,11},{2,8},{3,9},{4,14},{5,15},{6,12},{7,13},{8,2},{9,3},... | collective-permute-start | bytes 344072 | tf_op jit(solution)/shard_map/ppermute | solution.py:789
  94.5 22.8 %collective-permute-start.12 = (bf16[448,128]{1,0:T(8,128)(2,1)S(1)}, bf16[448,128]{1,0:T(8,128)(2,1)S(1)}, u32[]{:S(2)}, u32[]{:S(2)}) collective-permute-start(bf16[448,128]{1,0:T(8,128)(2,1)S(1)} %copy-done.4), channel_id=1, source_target_pairs={{0,11},{1,10},{2,9},{3,8},{4,15},{5,14},{6,13},{7,12},{8,3},{9,2},... | collective-permute-start | bytes 344072 | tf_op jit(solution)/shard_map/ppermute | solution.py:789
  96.5 21.9 %collective-permute-start.13 = (bf16[448,128]{1,0:T(8,128)(2,1)S(1)}, bf16[448,128]{1,0:T(8,128)(2,1)S(1)}, u32[]{:S(2)}, u32[]{:S(2)}) collective-permute-start(bf16[448,128]{1,0:T(8,128)(2,1)S(1)} %copy-done.3), channel_id=1, source_target_pairs={{0,12},{1,13},{2,14},{3,15},{4,8},{5,9},{6,10},{7,11},{8,4},{9,5},... | collective-permute-start | bytes 344072 | tf_op jit(solution)/shard_map/ppermute | solution.py:789
  106.8 20.3 %collective-permute-start.14 = (bf16[448,128]{1,0:T(8,128)(2,1)S(1)}, bf16[448,128]{1,0:T(8,128)(2,1)S(1)}, u32[]{:S(2)}, u32[]{:S(2)}) collective-permute-start(bf16[448,128]{1,0:T(8,128)(2,1)S(1)} %copy-done.2), channel_id=1, source_target_pairs={{0,13},{1,12},{2,15},{3,14},{4,9},{5,8},{6,11},{7,10},{8,5},{9,4},... | collective-permute-start | bytes 344072 | tf_op jit(solution)/shard_map/ppermute | solution.py:789
  110.0 20.4 %collective-permute-start.15 = (bf16[448,128]{1,0:T(8,128)(2,1)S(1)}, bf16[448,128]{1,0:T(8,128)(2,1)S(1)}, u32[]{:S(2)}, u32[]{:S(2)}) collective-permute-start(bf16[448,128]{1,0:T(8,128)(2,1)S(1)} %copy-done.1), channel_id=1, source_target_pairs={{0,14},{1,15},{2,12},{3,13},{4,10},{5,11},{6,8},{7,9},{8,6},{9,7},... | collective-permute-start | bytes 344072 | tf_op jit(solution)/shard_map/ppermute | solution.py:789
  112.6 20.3 %collective-permute-start.16 = (bf16[448,128]{1,0:T(8,128)(2,1)S(1)}, bf16[448,128]{1,0:T(8,128)(2,1)S(1)}, u32[]{:S(2)}, u32[]{:S(2)}) collective-permute-start(bf16[448,128]{1,0:T(8,128)(2,1)S(1)} %copy-done), channel_id=1, source_target_pairs={{0,15},{1,14},{2,13},{3,12},{4,11},{5,10},{6,9},{7,8},{8,7},{9,6},... | collective-permute-start | bytes 344072 | tf_op jit(solution)/shard_map/ppermute | solution.py:789

commit v19 on v17

--- a/solution.py
+++ b/solution.py
@@ -377,59 +377,45 @@
 def split_pieces_body(slabs, raw, lines, fields, row_ref, *refs):
     half = slabs // 2
     field_refs, near_out, far_outs = refs[:fields], refs[fields], refs[fields + 1 : fields + 1 + half]
-    slab_refs, helds, sems = refs[fields + 1 + half : -slabs - 1], refs[-slabs - 1 : -1], refs[-1]
+    slab_refs, held, sems = refs[fields + 1 + half : -2], refs[-2], refs[-1]
     cells = lines * LANES
     end = row_ref.shape[1]
-    started = []
-
-    def fetch(source, target):
-        started.append(pltpu.make_async_copy(source, target, sems.at[len(started)]))
-        started[-1].start()
-        return started[-1]
-
+    me = lax.axis_index("slab").astype(jnp.int32)
     copies = []
-    for at, held in enumerate(helds):
-        slab = device_at(at, half)
-        parts = [
-            (slab * cells, cells),
-            (jnp.minimum((slab + 1) * cells, end - GRID_Y), GRID_Y),
-            (jnp.maximum(slab * cells - GRID_Y, 0), GRID_Y),
-        ]
-        if at < half:
-            other = slab ^ half
-            parts += [(other * cells, raw * LANES + GRID_Y), (jnp.maximum(other * cells - GRID_Y, 0), GRID_Y)]
-        mine, to = [], 0
-        for start, size in parts:
-            source = row_ref.at[:, pl.ds(pl.multiple_of(start, GRID_Y), size)]
-            mine.append(fetch(source, held.at[:, pl.ds(to, size)]))
-            to += size
-        copies.append(mine)
-    me = lax.axis_index("slab").astype(jnp.int32)
-    fetches = []
+    for slab in range(slabs):
+        part = pl.ds(slab * cells, cells)
+        copies.append(pltpu.make_async_copy(row_ref.at[:, part], held.at[:, part], sems.at[slab]))
     for n, target in enumerate(slab_refs):
         start = (me if n < fields else me ^ half) * lines
-        fetches.append(fetch(field_refs[n % fields].at[lines_of(start, target.shape[0]), :], target))
-
-    def grid_row(held, at):
-        return held[:, pl.ds(at, GRID_Y)].astype(F32).reshape(LINE, LANES)
-
-    for at, held in enumerate(helds):
+        source = field_refs[n % fields].at[lines_of(start, target.shape[0]), :]
+        copies.append(pltpu.make_async_copy(source, target, sems.at[slabs + n]))
+    for copy in copies:
+        copy.start()
+    for copy in copies[:slabs]:
+        copy.wait()
+
+    def part(start, size):
+        return held[:, pl.ds(pl.multiple_of(start, GRID_Y), size)]
+
+    def grid_row(start):
+        return part(start, GRID_Y).astype(F32).reshape(LINE, LANES)
+
+    for at in range(slabs):
         out_ref = near_out.at[at] if at < half else far_outs[at - half]
-        for copy in copies[at]:
-            copy.wait()
         slab = device_at(at, half)
-        out_ref[:lines, :] = held[:, :cells].reshape(lines, LANES)
-        below = jnp.where(slab == slabs - 1, 0.0, grid_row(held, cells))
-        above = jnp.where(slab == 0, 0.0, grid_row(held, cells + GRID_Y))
+        start = slab * cells
+        out_ref[:lines, :] = part(start, cells).reshape(lines, LANES)
+        below = jnp.where(slab == slabs - 1, 0.0, grid_row(jnp.minimum(start + cells, end - GRID_Y)))
+        above = jnp.where(slab == 0, 0.0, grid_row(jnp.maximum(start - GRID_Y, 0)))
         out_ref[lines : lines + TILE, :] = jnp.concatenate([below, above], axis=0).astype(BF16)
         if at < half:
-            start = cells + 2 * GRID_Y
+            start = (slab ^ half) * cells
             to = lines + TILE
-            out_ref[to : to + raw, :] = held[:, start : start + raw * LANES].reshape(raw, LANES)
-            below = grid_row(held, start + raw * LANES)
-            above = jnp.where(slab ^ half == 0, 0.0, grid_row(held, start + raw * LANES + GRID_Y))
+            out_ref[to : to + raw, :] = part(start, raw * LANES).reshape(raw, LANES)
+            below = grid_row(start + raw * LANES)
+            above = jnp.where(slab ^ half == 0, 0.0, grid_row(jnp.maximum(start - GRID_Y, 0)))
             out_ref[to + raw :, :] = jnp.concatenate([below, above], axis=0).astype(BF16)
-    for copy in fetches:
+    for copy in copies[slabs:]:
         copy.wait()
 
 
@@ -449,9 +435,7 @@
         in_specs=[IN_HBM] * (1 + len(fields)),
         out_specs=[IN_VMEM] * len(out_shape),
         out_shape=out_shape,
-        scratch_shapes=[pltpu.VMEM((1, size * LANES), BF16)] * half
-        + [pltpu.VMEM((1, rim * LANES), BF16)] * half
-        + [pltpu.SemaphoreType.DMA((8 * slabs + 2 * len(fields),))],
+        scratch_shapes=[pltpu.VMEM(row.shape, BF16), pltpu.SemaphoreType.DMA((slabs + 2 * len(fields),))],
     )(row, *fields)
 
 
@@ -585,10 +569,10 @@
         return pltpu.make_async_copy(grads.at[:, at, :], out_ref.at[:, at, :], sems.at[i])
 
     def step(i, carry):
-        for p, (array, lead) in enumerate(views):
+        for p, (array, lead, base) in enumerate(views):
 
             def load(start, size):
-                part = lines_of(start, size)
+                part = lines_of(base + start, size)
                 return refs[array][part, :] if lead is None else refs[array][lead, part, :]
 
             grads[p, lines_of(i * BLOCK, BLOCK), :] = block_gradient(load, i, count, observed, precision)
@@ -654,7 +638,7 @@
 def update_pieces_body(half, raw, lines, groups, near_ref, *refs):
     total = 2 * half
     far_refs, refs = refs[:half], refs[half:]
-    across_ref, raw_observed, raw_precision, numbers_ref, grams_ref, *refs = refs
+    across_ref, numbers_ref, grams_ref, raw_grads_ref, *refs = refs
     group_refs, near_to, far_tos = refs[: len(groups)], refs[len(groups)], refs[len(groups) + 1 : -8]
     near_out, far_out, mixer, own, grads, raw_grads, sems, out_sems = refs[-8:]
     wide = total * TILE
@@ -663,22 +647,9 @@
     for group, group_ref in zip(groups, group_refs):
         for j, at in enumerate(group):
             fetches.append(pltpu.make_async_copy(group_ref.at[j], grads.at[at], sems.at[len(fetches)]))
+    fetches.append(pltpu.make_async_copy(raw_grads_ref, raw_grads, sems.at[total]))
     for fetch in fetches:
         fetch.start()
-
-    def raw_gradient(i, carry):
-        for k in range(total):
-
-            def load(start, size):
-                if k < half:
-                    return near_ref[k, lines_of(lines + TILE + start, size), :]
-                return across_ref[k - half, lines_of(start, size), :]
-
-            part = lines_of(i * BLOCK, BLOCK)
-            raw_grads[k, part, :] = block_gradient(load, i, raw, raw_observed, raw_precision)
-        return carry
-
-    lax.fori_loop(0, raw // BLOCK, raw_gradient, 0)
     gram = jnp.sum(grams_ref[...], axis=0)[:, :total]
     spread, anneal, step_size = (numbers_ref[k : k + 1, :1] for k in range(3))
     rate = step_size / total
@@ -758,7 +729,7 @@
         copy.wait()
 
 
-def update_pieces(numbers, grams, near, far, across, raw_fields, grads, groups, raw, lines):
+def update_pieces(numbers, grams, near, far, across, raw_grads, grads, groups, raw, lines):
     half = len(far)
     total = 2 * half
     wide = total * TILE
@@ -769,7 +740,7 @@
         "update_pieces",
         flops=4 * wide * wide * LANES * (lines // TILE),
         moved=6 * total * lines * LANES,
-        in_specs=[IN_VMEM] * (half + 6) + [IN_HBM] * len(groups),
+        in_specs=[IN_VMEM] * (half + 4) + [IN_HBM] * (1 + len(groups)),
         out_specs=[IN_HBM] * len(out_shape),
         out_shape=out_shape,
         scratch_shapes=[
@@ -779,10 +750,10 @@
             pltpu.VMEM((wide, LANES), F32),
             pltpu.VMEM((total, lines, LANES), BF16),
             pltpu.VMEM((total, raw, LANES), BF16),
-            pltpu.SemaphoreType.DMA((total,)),
+            pltpu.SemaphoreType.DMA((total + 1,)),
             pltpu.SemaphoreType.DMA((half + 1, 3)),
         ],
-    )(near, *far, across, *raw_fields, numbers, grams, *grads)
+    )(near, *far, across, numbers, grams, raw_grads, *grads)
 
 
 def exchange(piece, k, slabs):
@@ -814,15 +785,17 @@
     numbers = [spread, anneal, step_size]
     for group in GRADIENTS:
         if group[0] < half:
-            arrays, views = [near], [(0, k) for k in group]
+            arrays, views = [near], [(0, k, 0) for k in group]
         else:
-            arrays, views = [far[k - half] for k in group], [(j, None) for j in range(len(group))]
+            arrays, views = [far[k - half] for k in group], [(j, None, 0) for j in range(len(group))]
         slopes, rows = gradient_pieces(arrays, tuple(views), obs, prec, [] if grads else numbers)
         grads.append(in_hbm(slopes))
         numbers = numbers if len(grads) > 1 else rows
     grams = swap(gram_pieces(near, far, lines, grads[:1], [raw_near]))
+    views = [(0, k, lines + TILE) for k in range(half)] + [(1, k, 0) for k in range(half)]
+    raw_grads, _ = gradient_pieces([near, across], tuple(views), *raw_fields, [])
     new_near, *new_far = update_pieces(
-        numbers, grams, near, far, across, raw_fields, grads, GRADIENTS, RAW, lines
+        numbers, grams, near, far, across, in_hbm(raw_grads), grads, GRADIENTS, RAW, lines
     )
     new_near = swap_near(new_near, slabs)
     new_far = [exchange(piece, half + x, slabs) for x, piece in enumerate(new_far)]

time: 131 us -> 130 us (level)
  waiting for transfers between devices: 69.1 us -> 63.6 us
  starting transfers between devices: 33 us -> 37 us
    ppermute x17, waiting for transfers between devices: 65.5 us -> 62.4 us  [exchange(): return lax.ppermute(piece, 'slab', [(i, i ^ k) for i in range(slabs)])]
    ppermute x17, starting transfers between devices: 17.9 us -> 20.4 us  [exchange(): return lax.ppermute(piece, 'slab', [(i, i ^ k) for i in range(slabs)])]
    all_to_all x1, waiting for transfers between devices: 3.59 us -> 1.16 us  [swap(): lax.all_to_all(slabs, 'slab', split_axis=0, concat_axis=0, tiled=True)]
    pallas_call x3 -> x4, Pallas kernels: 7.36 us -> 9.57 us  [gradient_pieces(): call(functools.partial(gradient_pieces_body, views, len(arrays), len(numb...]
    all_to_all x2, starting transfers between devices: 9.37 us -> 10.9 us  [swap_near(): lax.all_to_all(pieces, 'slab', 0, 0, axis_index_groups=groups, tiled=True)]
  transfers between devices with their start and end apart: 20 -> 20, of which waited for: 15 -> 15; matrix products, arithmetic and copies ran while one was open for 0% -> 0% of each run, Pallas kernels for 11% -> 12%
where the time goes in v19:
time: 130 us
  waiting for transfers between devices  63.6 us (49%)
  starting transfers between devices  37 us (28%)
  Pallas kernels  26.5 us (20%)
  between operations  2.15 us (2%)
    ppermute x17, waiting for transfers between devices, exchange(): return lax.ppermute(piece, 'slab', [(i, i ^ k) for i in range(slabs)])  62.4 us
    ppermute x17, starting transfers between devices, exchange(): return lax.ppermute(piece, 'slab', [(i, i ^ k) for i in range(slabs)])  20.4 us
    all_to_all x2, starting transfers between devices, swap_near(): lax.all_to_all(pieces, 'slab', 0, 0, axis_index_groups=groups, tiled=True)  10.9 us
    pallas_call x4, Pallas kernels, gradient_pieces(): call(functools.partial(gradient_pieces_body, views, len(arrays), len(numb...  9.57 us
    pallas_call x1, Pallas kernels, update_pieces(): call(functools.partial(update_pieces_body, half, raw, lines, groups), 'up...  5.88 us
    all_to_all x1, starting transfers between devices, swap(): lax.all_to_all(slabs, 'slab', split_axis=0, concat_axis=0, tiled=True)  5.75 us
    pallas_call x4, Pallas kernels, join_pieces(): call(functools.partial(join_pieces_body, pieces, slabs // 2, raw, NCELL /...  5.55 us
    pallas_call x1, Pallas kernels, split_pieces(): call(functools.partial(split_pieces_body, slabs, raw, lines, len(fields))...  3.75 us
  transfers between devices with their start and end apart: 20, of which 15 were waited for; matrix products, arithmetic and copies ran while one was open for 0% of the time, Pallas kernels for 12%

profile of v19, /device:TPU:9, one launch (start us, length us, event | category | flops | bytes accessed | tf_op | source)
XLA Modules:
  0.0 129.9 jit_solution(2201859919008493745)
XLA Ops:
  0.0 3.7 %split_pieces.1 = (bf16[8,672,128]{2,1,0:T(8,128)(2,1)}, bf16[528,128]{1,0:T(8,128)(2,1)S(1)}, bf16[528,128]{1,0:T(8,128)(2,1)S(1)}, bf16[528,128]{1,0:T(8,128)(...) custom-call(bf16[1,1048576]{1,0:T(2,128)(2,1)} %row_ref.1, ...), custom_call_target="tpu_custom_call" | custom-call | bytes 7372800 | tf_op jit(solution)/shard_map/split_pieces/pallas_call | solution.py:431
  3.8 4.6 %all-to-all-start = ((bf16[8,672,128]{2,1,0:T(8,128)(2,1)}), bf16[8,672,128]{2,1,0:T(8,128)(2,1)S(1)}, u32[]{:S(2)}, u32[]{:S(2)}) async-start(bf16[8,672,128]{2,1,0:T(8,128)(2,1)} %get-tuple-element.32), calls=%async_computation | async-start | bytes 2752512 | tf_op jit(solution)/shard_map/all_to_all | solution.py:765
  8.3 2.3 %collective-permute-start = (bf16[528,128]{1,0:T(8,128)(2,1)S(1)}, bf16[528,128]{1,0:T(8,128)(2,1)S(1)}, u32[]{:S(2)}, u32[]{:S(2)}) collective-permute-start(bf16[528,128]{1,0:T(8,128)(2,1)S(1)} %get-tuple-element.33), channel_id=1, source_target_pairs={{0,8},{1,9},{2,10},{3,11},{4,12},{5,13},{6,14},{7,15},{8,0},{9,1},... | collective-permute-start | bytes 405512 | tf_op jit(solution)/shard_map/ppermute | solution.py:760
  10.6 0.6 collective-permute-start.1
  11.2 3.2 %collective-permute-start.2 = (bf16[528,128]{1,0:T(8,128)(2,1)S(1)}, bf16[528,128]{1,0:T(8,128)(2,1)S(1)}, u32[]{:S(2)}, u32[]{:S(2)}) collective-permute-start(bf16[528,128]{1,0:T(8,128)(2,1)S(1)} %get-tuple-element.35), channel_id=1, source_target_pairs={{0,10},{1,11},{2,8},{3,9},{4,14},{5,15},{6,12},{7,13},{8,2},{9,3},... | collective-permute-start | bytes 405512 | tf_op jit(solution)/shard_map/ppermute | solution.py:760
  14.4 0.3 collective-permute-start.3
  14.7 1.0 collective-permute-start.4
  15.7 13.5 %collective-permute-done.refs_0_ = bf16[528,128]{1,0:T(8,128)(2,1)S(1)} collective-permute-done((bf16[528,128]{1,0:T(8,128)(2,1)S(1)}, bf16[528,128]{1,0:T(8,128)(2,1)S(1)}, u32[]{:S(2)}, u32[]{:S(2)}) %collective-permute-start) | collective-permute-done | bytes 135200 | tf_op jit(solution)/shard_map/ppermute | solution.py:760
  29.3 0.0 collective-permute-start.5
  29.3 3.6 %collective-permute-done.1.refs_1_ = bf16[528,128]{1,0:T(8,128)(2,1)S(1)} collective-permute-done((bf16[528,128]{1,0:T(8,128)(2,1)S(1)}, bf16[528,128]{1,0:T(8,128)(2,1)S(1)}, u32[]{:S(2)}, u32[]{:S(2)}) %collective-permute-start.1) | collective-permute-done | bytes 135200 | tf_op jit(solution)/shard_map/ppermute | solution.py:760
  32.9 0.3 collective-permute-start.6
  33.2 2.8 %collective-permute-done.2.refs_2_ = bf16[528,128]{1,0:T(8,128)(2,1)S(1)} collective-permute-done((bf16[528,128]{1,0:T(8,128)(2,1)S(1)}, bf16[528,128]{1,0:T(8,128)(2,1)S(1)}, u32[]{:S(2)}, u32[]{:S(2)}) %collective-permute-start.2) | collective-permute-done | bytes 135200 | tf_op jit(solution)/shard_map/ppermute | solution.py:760
  37.9 1.7 %collective-permute-done.3.refs_3_ = bf16[528,128]{1,0:T(8,128)(2,1)S(1)} collective-permute-done((bf16[528,128]{1,0:T(8,128)(2,1)S(1)}, bf16[528,128]{1,0:T(8,128)(2,1)S(1)}, u32[]{:S(2)}, u32[]{:S(2)}) %collective-permute-start.3) | collective-permute-done | bytes 135200 | tf_op jit(solution)/shard_map/ppermute | solution.py:760
  39.6 1.8 %gradient_pieces.4 = (bf16[4,512,128]{2,1,0:T(8,128)(2,1)}, f32[8,128]{1,0:T(8,128)S(1)}) custom-call(bf16[528,128]{1,0:T(8,128)(2,1)S(1)} %collective-permute-done.refs_0_, bf16[528,128]{1,0:T(8,128)(2,1)S(1)} %collective-permute-done.1.refs_1_, bf16[528,128]{1,0:T(8,128)(2,1)S(1)} %collective-permute-done.2.refs_2_, ...), custom_call_target="tpu_custom_call" | custom-call | flops 7864320 | bytes 2097152 | tf_op jit(solution)/shard_map/gradient_pieces/pallas_call | solution.py:594
  41.4 6.7 %collective-permute-done.4.refs_4_.refs_0_ = bf16[528,128]{1,0:T(8,128)(2,1)S(1)} collective-permute-done((bf16[528,128]{1,0:T(8,128)(2,1)S(1)}, bf16[528,128]{1,0:T(8,128)(2,1)S(1)}, u32[]{:S(2)}, u32[]{:S(2)}) %collective-permute-start.4) | collective-permute-done | bytes 135200 | tf_op jit(solution)/shard_map/ppermute | solution.py:760
  48.1 4.7 %collective-permute-done.5.refs_5_.refs_1_ = bf16[528,128]{1,0:T(8,128)(2,1)S(1)} collective-permute-done((bf16[528,128]{1,0:T(8,128)(2,1)S(1)}, bf16[528,128]{1,0:T(8,128)(2,1)S(1)}, u32[]{:S(2)}, u32[]{:S(2)}) %collective-permute-start.5) | collective-permute-done | bytes 135200 | tf_op jit(solution)/shard_map/ppermute | solution.py:760
  52.9 3.8 %collective-permute-done.6.refs_6_.refs_2_ = bf16[528,128]{1,0:T(8,128)(2,1)S(1)} collective-permute-done((bf16[528,128]{1,0:T(8,128)(2,1)S(1)}, bf16[528,128]{1,0:T(8,128)(2,1)S(1)}, u32[]{:S(2)}, u32[]{:S(2)}) %collective-permute-start.6) | collective-permute-done | bytes 135200 | tf_op jit(solution)/shard_map/ppermute | solution.py:760
  56.7 2.9 %collective-permute-done.7.refs_7_.refs_3_ = bf16[528,128]{1,0:T(8,128)(2,1)S(1)} collective-permute-done((bf16[528,128]{1,0:T(8,128)(2,1)S(1)}, bf16[528,128]{1,0:T(8,128)(2,1)S(1)}, u32[]{:S(2)}, u32[]{:S(2)}) %collective-permute-start.7) | collective-permute-done | bytes 135200 | tf_op jit(solution)/shard_map/ppermute | solution.py:760
  59.6 0.1 collective-permute-start.8
  59.7 1.7 %gram_pieces.1 = f32[16,16,128]{2,1,0:T(8,128)S(1)} custom-call(bf16[8,672,128]{2,1,0:T(8,128)(2,1)S(1)} %all-to-all-done.near_ref.refs_0_, bf16[528,128]{1,0:T(8,128)(2,1)S(1)} %collective-permute-done.refs_0_, bf16[528,128]{1,0:T(8,128)(2,1)S(1)} %collective-permute-done.1.refs_1_, bf16[528,128]{1,0:T(8,128)(2,1)S(1)} %collective-permute-done.2.refs_2_, ...), custom_call_target="tpu_custom_call" | custom-call | flops 536870912 | bytes 2097152 | tf_op jit(solution)/shard_map/gram_pieces/pallas_call | solution.py:521
  61.4 0.0 copy-start
  61.4 0.6 copy-done
  62.1 5.7 %all-to-all-start.1 = ((f32[16,16,128]{2,1,0:T(8,128)}), f32[16,16,128]{2,1,0:T(8,128)S(1)}, u32[]{:S(2)}, u32[]{:S(2)}) async-start(f32[16,16,128]{2,1,0:T(8,128)} %copy-done), calls=%async_computation.1 | async-start | bytes 262144 | tf_op jit(solution)/shard_map/all_to_all | solution.py:365
  67.8 2.4 %gradient_pieces.6 = (bf16[4,512,128]{2,1,0:T(8,128)(2,1)}, f32[8,128]{1,0:T(8,128)}) custom-call(bf16[528,128]{1,0:T(8,128)(2,1)S(1)} %collective-permute-done.4.refs_4_.refs_0_, bf16[528,128]{1,0:T(8,128)(2,1)S(1)} %collective-permute-done.5.refs_5_.refs_1_, bf16[528,128]{1,0:T(8,128)(2,1)S(1)} %collective-permute-done.6.refs_6_.refs_2_, ...), custom_call_target="tpu_custom_call" | custom-call | flops 7864320 | bytes 2097152 | tf_op jit(solution)/shard_map/gradient_pieces/pallas_call | solution.py:594
  70.2 3.2 %gradient_pieces.7 = (bf16[8,512,128]{2,1,0:T(8,128)(2,1)}, f32[8,128]{1,0:T(8,128)}) custom-call(bf16[8,672,128]{2,1,0:T(8,128)(2,1)S(1)} %all-to-all-done.near_ref.refs_0_, bf16[512,128]{1,0:T(8,128)(2,1)S(1)} %get-tuple-element.41.refs_4_.refs_1_, bf16[512,128]{1,0:T(8,128)(2,1)S(1)} %get-tuple-element.42.refs_5_.refs_2_), custom_call_target="tpu_custom_call" | custom-call | flops 15728640 | bytes 4194304 | tf_op jit(solution)/shard_map/gradient_pieces/pallas_call | solution.py:594
  73.4 0.2 collective-permute-done.8.refs_1_.refs_8_
  73.6 2.2 %gradient_pieces.5 = (bf16[16,128,128]{2,1,0:T(8,128)(2,1)}, f32[8,128]{1,0:T(8,128)}) custom-call(bf16[8,672,128]{2,1,0:T(8,128)(2,1)S(1)} %all-to-all-done.near_ref.refs_0_, bf16[8,144,128]{2,1,0:T(8,128)(2,1)S(1)} %collective-permute-done.8.refs_1_.refs_8_, bf16[128,128]{1,0:T(8,128)(2,1)S(1)} %get-tuple-element.45.refs_2_, ...), custom_call_target="tpu_custom_call" | custom-call | flops 7864320 | bytes 2097152 | tf_op jit(solution)/shard_map/gradient_pieces/pallas_call | solution.py:594
  75.8 1.2 all-to-all-done.1.refs_10_
  77.0 5.9 %update_pieces.1 = (bf16[8,640,128]{2,1,0:T(8,128)(2,1)}, bf16[384,128]{1,0:T(8,128)(2,1)}, bf16[384,128]{1,0:T(8,128)(2,1)}, bf16[384,128]{1,0:T(8,128)(2,1)}, ...) custom-call(bf16[8,672,128]{2,1,0:T(8,128)(2,1)S(1)} %all-to-all-don, ...), custom_call_target="tpu_custom_call" | custom-call | flops 1073741824 | bytes 6291456 | tf_op jit(solution)/shard_map/update_pieces/pallas_call | solution.py:738
  83.0 6.3 %all-to-all-start.2 = ((bf16[8,640,128]{2,1,0:T(8,128)(2,1)}), bf16[8,640,128]{2,1,0:T(8,128)(2,1)S(1)}, u32[]{:S(2)}, u32[]{:S(2)}) async-start(bf16[8,640,128]{2,1,0:T(8,128)(2,1)} %get-tuple-element.50), calls=%async_computation.2 | async-start | bytes 2621440 | tf_op jit(solution)/shard_map/all_to_all | solution.py:765
  89.2 0.3 collective-permute-start.9
  89.6 2.6 %collective-permute-start.10 = (bf16[384,128]{1,0:T(8,128)(2,1)S(1)}, bf16[384,128]{1,0:T(8,128)(2,1)S(1)}, u32[]{:S(2)}, u32[]{:S(2)}) collective-permute-start(bf16[384,128]{1,0:T(8,128)(2,1)S(1)} %copy-done.7), channel_id=1, source_target_pairs={{0,9},{1,8},{2,11},{3,10},{4,13},{5,12},{6,15},{7,14},{8,1},{9,0},... | collective-permute-start | bytes 294920 | tf_op jit(solution)/shard_map/ppermute | solution.py:760
  92.1 1.2 collective-permute-start.11
  93.4 2.1 %collective-permute-start.12 = (bf16[384,128]{1,0:T(8,128)(2,1)S(1)}, bf16[384,128]{1,0:T(8,128)(2,1)S(1)}, u32[]{:S(2)}, u32[]{:S(2)}) collective-permute-start(bf16[384,128]{1,0:T(8,128)(2,1)S(1)} %copy-done.5), channel_id=1, source_target_pairs={{0,11},{1,10},{2,9},{3,8},{4,15},{5,14},{6,13},{7,12},{8,3},{9,2},... | collective-permute-start | bytes 294920 | tf_op jit(solution)/shard_map/ppermute | solution.py:760
  95.5 0.0 collective-permute-start.13
  95.5 11.0 %collective-permute-done.9.refs_1_ = bf16[384,128]{1,0:T(8,128)(2,1)S(1)} collective-permute-done((bf16[384,128]{1,0:T(8,128)(2,1)S(1)}, bf16[384,128]{1,0:T(8,128)(2,1)S(1)}, u32[]{:S(2)}, u32[]{:S(2)}) %collective-permute-start.9) | collective-permute-done | bytes 98336 | tf_op jit(solution)/shard_map/ppermute | solution.py:760
  106.5 2.2 %collective-permute-start.14 = (bf16[384,128]{1,0:T(8,128)(2,1)S(1)}, bf16[384,128]{1,0:T(8,128)(2,1)S(1)}, u32[]{:S(2)}, u32[]{:S(2)}) collective-permute-start(bf16[384,128]{1,0:T(8,128)(2,1)S(1)} %copy-done.3), channel_id=1, source_target_pairs={{0,13},{1,12},{2,15},{3,14},{4,9},{5,8},{6,11},{7,10},{8,5},{9,4},... | collective-permute-start | bytes 294920 | tf_op jit(solution)/shard_map/ppermute | solution.py:760
  108.6 1.0 collective-permute-done.10.refs_2_
  109.6 2.1 %collective-permute-start.15 = (bf16[384,128]{1,0:T(8,128)(2,1)S(1)}, bf16[384,128]{1,0:T(8,128)(2,1)S(1)}, u32[]{:S(2)}, u32[]{:S(2)}) collective-permute-start(bf16[384,128]{1,0:T(8,128)(2,1)S(1)} %copy-done.2), channel_id=1, source_target_pairs={{0,14},{1,15},{2,12},{3,13},{4,10},{5,11},{6,8},{7,9},{8,6},{9,7},... | collective-permute-start | bytes 294920 | tf_op jit(solution)/shard_map/ppermute | solution.py:760
  111.8 0.0 collective-permute-done.11.refs_3_
  111.8 2.1 %collective-permute-start.16 = (bf16[384,128]{1,0:T(8,128)(2,1)S(1)}, bf16[384,128]{1,0:T(8,128)(2,1)S(1)}, u32[]{:S(2)}, u32[]{:S(2)}) collective-permute-start(bf16[384,128]{1,0:T(8,128)(2,1)S(1)} %copy-done.1), channel_id=1, source_target_pairs={{0,15},{1,14},{2,13},{3,12},{4,11},{5,10},{6,9},{7,8},{8,7},{9,6},... | collective-permute-start | bytes 294920 | tf_op jit(solution)/shard_map/ppermute | solution.py:760
  113.9 3.0 %join_pieces.4.refs_0_ = bf16[1,1048576]{1,0:T(2,128)(2,1)} custom-call(bf16[8,640,128]{2,1,0:T(8,128)(2,1)S(1)} %all-to-all-done.2.refs_0_), custom_call_target="tpu_custom_call" | custom-call | bytes 3932160 | tf_op jit(solution)/shard_map/join_pieces/pallas_call | solution.py:467
  116.8 1.0 join_pieces.5.refs_0_
  117.8 6.1 %collective-permute-done.14.refs_2_ = bf16[384,128]{1,0:T(8,128)(2,1)S(1)} collective-permute-done((bf16[384,128]{1,0:T(8,128)(2,1)S(1)}, bf16[384,128]{1,0:T(8,128)(2,1)S(1)}, u32[]{:S(2)}, u32[]{:S(2)}) %collective-permute-start.14) | collective-permute-done | bytes 98336 | tf_op jit(solution)/shard_map/ppermute | solution.py:760
  123.9 0.8 join_pieces.6.refs_0_
  124.8 2.3 %collective-permute-done.15.refs_1_ = bf16[384,128]{1,0:T(8,128)(2,1)S(1)} collective-permute-done((bf16[384,128]{1,0:T(8,128)(2,1)S(1)}, bf16[384,128]{1,0:T(8,128)(2,1)S(1)}, u32[]{:S(2)}, u32[]{:S(2)}) %collective-permute-start.15) | collective-permute-done | bytes 98336 | tf_op jit(solution)/shard_map/ppermute | solution.py:760
  127.0 2.1 %collective-permute-done.16.refs_2_ = bf16[384,128]{1,0:T(8,128)(2,1)S(1)} collective-permute-done((bf16[384,128]{1,0:T(8,128)(2,1)S(1)}, bf16[384,128]{1,0:T(8,128)(2,1)S(1)}, u32[]{:S(2)}, u32[]{:S(2)}) %collective-permute-start.16) | collective-permute-done | bytes 98336 | tf_op jit(solution)/shard_map/ppermute | solution.py:760
  129.1 0.8 join_pieces.7
  (22 shorter events, 0.1 us)
Async XLA Ops:
  3.8 55.8 %all-to-all-start = ((bf16[8,672,128]{2,1,0:T(8,128)(2,1)}), bf16[8,672,128]{2,1,0:T(8,128)(2,1)S(1)}, u32[]{:S(2)}, u32[]{:S(2)}) async-start(bf16[8,672,128]{2,1,0:T(8,128)(2,1)} %get-tuple-element.32), calls=%async_computation | async-start | bytes 2752512 | tf_op jit(solution)/shard_map/all_to_all | solution.py:765
  8.3 20.9 %collective-permute-start = (bf16[528,128]{1,0:T(8,128)(2,1)S(1)}, bf16[528,128]{1,0:T(8,128)(2,1)S(1)}, u32[]{:S(2)}, u32[]{:S(2)}) collective-permute-start(bf16[528,128]{1,0:T(8,128)(2,1)S(1)} %get-tuple-element.33), channel_id=1, source_target_pairs={{0,8},{1,9},{2,10},{3,11},{4,12},{5,13},{6,14},{7,15},{8,0},{9,1},... | collective-permute-start | bytes 405512 | tf_op jit(solution)/shard_map/ppermute | solution.py:760
  10.6 22.2 %collective-permute-start.1 = (bf16[528,128]{1,0:T(8,128)(2,1)S(1)}, bf16[528,128]{1,0:T(8,128)(2,1)S(1)}, u32[]{:S(2)}, u32[]{:S(2)}) collective-permute-start(bf16[528,128]{1,0:T(8,128)(2,1)S(1)} %get-tuple-element.34), channel_id=1, source_target_pairs={{0,9},{1,8},{2,11},{3,10},{4,13},{5,12},{6,15},{7,14},{8,1},{9,0},... | collective-permute-start | bytes 405512 | tf_op jit(solution)/shard_map/ppermute | solution.py:760
  11.2 24.8 %collective-permute-start.2 = (bf16[528,128]{1,0:T(8,128)(2,1)S(1)}, bf16[528,128]{1,0:T(8,128)(2,1)S(1)}, u32[]{:S(2)}, u32[]{:S(2)}) collective-permute-start(bf16[528,128]{1,0:T(8,128)(2,1)S(1)} %get-tuple-element.35), channel_id=1, source_target_pairs={{0,10},{1,11},{2,8},{3,9},{4,14},{5,15},{6,12},{7,13},{8,2},{9,3},... | collective-permute-start | bytes 405512 | tf_op jit(solution)/shard_map/ppermute | solution.py:760
  14.4 25.2 %collective-permute-start.3 = (bf16[528,128]{1,0:T(8,128)(2,1)S(1)}, bf16[528,128]{1,0:T(8,128)(2,1)S(1)}, u32[]{:S(2)}, u32[]{:S(2)}) collective-permute-start(bf16[528,128]{1,0:T(8,128)(2,1)S(1)} %get-tuple-element.36), channel_id=1, source_target_pairs={{0,11},{1,10},{2,9},{3,8},{4,15},{5,14},{6,13},{7,12},{8,3},{9,2},... | collective-permute-start | bytes 405512 | tf_op jit(solution)/shard_map/ppermute | solution.py:760
  14.7 33.4 %collective-permute-start.4 = (bf16[528,128]{1,0:T(8,128)(2,1)S(1)}, bf16[528,128]{1,0:T(8,128)(2,1)S(1)}, u32[]{:S(2)}, u32[]{:S(2)}) collective-permute-start(bf16[528,128]{1,0:T(8,128)(2,1)S(1)} %get-tuple-element.37), channel_id=1, source_target_pairs={{0,12},{1,13},{2,14},{3,15},{4,8},{5,9},{6,10},{7,11},{8,4},{9,5},... | collective-permute-start | bytes 405512 | tf_op jit(solution)/shard_map/ppermute | solution.py:760
  29.3 23.6 %collective-permute-start.5 = (bf16[528,128]{1,0:T(8,128)(2,1)S(1)}, bf16[528,128]{1,0:T(8,128)(2,1)S(1)}, u32[]{:S(2)}, u32[]{:S(2)}) collective-permute-start(bf16[528,128]{1,0:T(8,128)(2,1)S(1)} %get-tuple-element.38), channel_id=1, source_target_pairs={{0,13},{1,12},{2,15},{3,14},{4,9},{5,8},{6,11},{7,10},{8,5},{9,4},... | collective-permute-start | bytes 405512 | tf_op jit(solution)/shard_map/ppermute | solution.py:760
  32.9 23.8 %collective-permute-start.6 = (bf16[528,128]{1,0:T(8,128)(2,1)S(1)}, bf16[528,128]{1,0:T(8,128)(2,1)S(1)}, u32[]{:S(2)}, u32[]{:S(2)}) collective-permute-start(bf16[528,128]{1,0:T(8,128)(2,1)S(1)} %get-tuple-element.39), channel_id=1, source_target_pairs={{0,14},{1,15},{2,12},{3,13},{4,10},{5,11},{6,8},{7,9},{8,6},{9,7},... | collective-permute-start | bytes 405512 | tf_op jit(solution)/shard_map/ppermute | solution.py:760
  36.0 23.5 %collective-permute-start.7 = (bf16[528,128]{1,0:T(8,128)(2,1)S(1)}, bf16[528,128]{1,0:T(8,128)(2,1)S(1)}, u32[]{:S(2)}, u32[]{:S(2)}) collective-permute-start(bf16[528,128]{1,0:T(8,128)(2,1)S(1)} %get-tuple-element.40), channel_id=1, source_target_pairs={{0,15},{1,14},{2,13},{3,12},{4,11},{5,10},{6,9},{7,8},{8,7},{9,6},... | collective-permute-start | bytes 405512 | tf_op jit(solution)/shard_map/ppermute | solution.py:760
  59.6 14.0 %collective-permute-start.8 = (bf16[8,144,128]{2,1,0:T(8,128)(2,1)S(1)}, bf16[8,144,128]{2,1,0:T(8,128)(2,1)S(1)}, u32[]{:S(2)}, u32[]{:S(2)}) collective-permute-start(bf16[8,144,128]{2,1,0:T(8,128)(2,1)S(1)} %raw_states.1.refs_9_), channel_id=1, source_target_pairs={{0,8},{1,9},{2,10},{3,11},{4,12},{5,13},{6,14},{7,15},{8,0},{9,1},... | collective-permute-start | bytes 884744 | tf_op jit(solution)/shard_map/ppermute | solution.py:760
  61.4 0.7 copy-start
  62.1 14.9 %all-to-all-start.1 = ((f32[16,16,128]{2,1,0:T(8,128)}), f32[16,16,128]{2,1,0:T(8,128)S(1)}, u32[]{:S(2)}, u32[]{:S(2)}) async-start(f32[16,16,128]{2,1,0:T(8,128)} %copy-done), calls=%async_computation.1 | async-start | bytes 262144 | tf_op jit(solution)/shard_map/all_to_all | solution.py:365
  82.9 6.4 %copy-start.8 = (bf16[384,128]{1,0:T(8,128)(2,1)S(1)}, bf16[384,128]{1,0:T(8,128)(2,1)}, u32[]{:S(2)}) copy-start(bf16[384,128]{1,0:T(8,128)(2,1)} %get-tuple-element.51) | copy-start | bytes 294916
  82.9 6.7 %copy-start.7 = (bf16[384,128]{1,0:T(8,128)(2,1)S(1)}, bf16[384,128]{1,0:T(8,128)(2,1)}, u32[]{:S(2)}) copy-start(bf16[384,128]{1,0:T(8,128)(2,1)} %get-tuple-element.52) | copy-start | bytes 294916
  82.9 9.2 %copy-start.6 = (bf16[384,128]{1,0:T(8,128)(2,1)S(1)}, bf16[384,128]{1,0:T(8,128)(2,1)}, u32[]{:S(2)}) copy-start(bf16[384,128]{1,0:T(8,128)(2,1)} %get-tuple-element.53) | copy-start | bytes 294916
  82.9 10.4 %copy-start.5 = (bf16[384,128]{1,0:T(8,128)(2,1)S(1)}, bf16[384,128]{1,0:T(8,128)(2,1)}, u32[]{:S(2)}) copy-start(bf16[384,128]{1,0:T(8,128)(2,1)} %get-tuple-element.54) | copy-start | bytes 294916
  82.9 12.5 %copy-start.4 = (bf16[384,128]{1,0:T(8,128)(2,1)S(1)}, bf16[384,128]{1,0:T(8,128)(2,1)}, u32[]{:S(2)}) copy-start(bf16[384,128]{1,0:T(8,128)(2,1)} %get-tuple-element.55) | copy-start | bytes 294916
  82.9 23.6 %copy-start.3 = (bf16[384,128]{1,0:T(8,128)(2,1)S(1)}, bf16[384,128]{1,0:T(8,128)(2,1)}, u32[]{:S(2)}) copy-start(bf16[384,128]{1,0:T(8,128)(2,1)} %get-tuple-element.56) | copy-start | bytes 294916
  82.9 26.7 %copy-start.2 = (bf16[384,128]{1,0:T(8,128)(2,1)S(1)}, bf16[384,128]{1,0:T(8,128)(2,1)}, u32[]{:S(2)}) copy-start(bf16[384,128]{1,0:T(8,128)(2,1)} %get-tuple-element.57) | copy-start | bytes 294916
  82.9 28.8 %copy-start.1 = (bf16[384,128]{1,0:T(8,128)(2,1)S(1)}, bf16[384,128]{1,0:T(8,128)(2,1)}, u32[]{:S(2)}) copy-start(bf16[384,128]{1,0:T(8,128)(2,1)} %get-tuple-element.58) | copy-start | bytes 294916
  83.0 30.9 %all-to-all-start.2 = ((bf16[8,640,128]{2,1,0:T(8,128)(2,1)}), bf16[8,640,128]{2,1,0:T(8,128)(2,1)S(1)}, u32[]{:S(2)}, u32[]{:S(2)}) async-start(bf16[8,640,128]{2,1,0:T(8,128)(2,1)} %get-tuple-element.50), calls=%async_computation.2 | async-start | bytes 2621440 | tf_op jit(solution)/shard_map/all_to_all | solution.py:765
  89.2 17.2 %collective-permute-start.9 = (bf16[384,128]{1,0:T(8,128)(2,1)S(1)}, bf16[384,128]{1,0:T(8,128)(2,1)S(1)}, u32[]{:S(2)}, u32[]{:S(2)}) collective-permute-start(bf16[384,128]{1,0:T(8,128)(2,1)S(1)} %copy-done.8), channel_id=1, source_target_pairs={{0,8},{1,9},{2,10},{3,11},{4,12},{5,13},{6,14},{7,15},{8,0},{9,1},... | collective-permute-start | bytes 294920 | tf_op jit(solution)/shard_map/ppermute | solution.py:760
  89.6 20.1 %collective-permute-start.10 = (bf16[384,128]{1,0:T(8,128)(2,1)S(1)}, bf16[384,128]{1,0:T(8,128)(2,1)S(1)}, u32[]{:S(2)}, u32[]{:S(2)}) collective-permute-start(bf16[384,128]{1,0:T(8,128)(2,1)S(1)} %copy-done.7), channel_id=1, source_target_pairs={{0,9},{1,8},{2,11},{3,10},{4,13},{5,12},{6,15},{7,14},{8,1},{9,0},... | collective-permute-start | bytes 294920 | tf_op jit(solution)/shard_map/ppermute | solution.py:760
  92.1 19.7 %collective-permute-start.11 = (bf16[384,128]{1,0:T(8,128)(2,1)S(1)}, bf16[384,128]{1,0:T(8,128)(2,1)S(1)}, u32[]{:S(2)}, u32[]{:S(2)}) collective-permute-start(bf16[384,128]{1,0:T(8,128)(2,1)S(1)} %copy-done.6), channel_id=1, source_target_pairs={{0,10},{1,11},{2,8},{3,9},{4,14},{5,15},{6,12},{7,13},{8,2},{9,3},... | collective-permute-start | bytes 294920 | tf_op jit(solution)/shard_map/ppermute | solution.py:760
  93.4 23.5 %collective-permute-start.12 = (bf16[384,128]{1,0:T(8,128)(2,1)S(1)}, bf16[384,128]{1,0:T(8,128)(2,1)S(1)}, u32[]{:S(2)}, u32[]{:S(2)}) collective-permute-start(bf16[384,128]{1,0:T(8,128)(2,1)S(1)} %copy-done.5), channel_id=1, source_target_pairs={{0,11},{1,10},{2,9},{3,8},{4,15},{5,14},{6,13},{7,12},{8,3},{9,2},... | collective-permute-start | bytes 294920 | tf_op jit(solution)/shard_map/ppermute | solution.py:760
  95.5 22.4 %collective-permute-start.13 = (bf16[384,128]{1,0:T(8,128)(2,1)S(1)}, bf16[384,128]{1,0:T(8,128)(2,1)S(1)}, u32[]{:S(2)}, u32[]{:S(2)}) collective-permute-start(bf16[384,128]{1,0:T(8,128)(2,1)S(1)} %copy-done.4), channel_id=1, source_target_pairs={{0,12},{1,13},{2,14},{3,15},{4,8},{5,9},{6,10},{7,11},{8,4},{9,5},... | collective-permute-start | bytes 294920 | tf_op jit(solution)/shard_map/ppermute | solution.py:760
  106.5 17.5 %collective-permute-start.14 = (bf16[384,128]{1,0:T(8,128)(2,1)S(1)}, bf16[384,128]{1,0:T(8,128)(2,1)S(1)}, u32[]{:S(2)}, u32[]{:S(2)}) collective-permute-start(bf16[384,128]{1,0:T(8,128)(2,1)S(1)} %copy-done.3), channel_id=1, source_target_pairs={{0,13},{1,12},{2,15},{3,14},{4,9},{5,8},{6,11},{7,10},{8,5},{9,4},... | collective-permute-start | bytes 294920 | tf_op jit(solution)/shard_map/ppermute | solution.py:760
  109.6 17.4 %collective-permute-start.15 = (bf16[384,128]{1,0:T(8,128)(2,1)S(1)}, bf16[384,128]{1,0:T(8,128)(2,1)S(1)}, u32[]{:S(2)}, u32[]{:S(2)}) collective-permute-start(bf16[384,128]{1,0:T(8,128)(2,1)S(1)} %copy-done.2), channel_id=1, source_target_pairs={{0,14},{1,15},{2,12},{3,13},{4,10},{5,11},{6,8},{7,9},{8,6},{9,7},... | collective-permute-start | bytes 294920 | tf_op jit(solution)/shard_map/ppermute | solution.py:760
  111.8 17.3 %collective-permute-start.16 = (bf16[384,128]{1,0:T(8,128)(2,1)S(1)}, bf16[384,128]{1,0:T(8,128)(2,1)S(1)}, u32[]{:S(2)}, u32[]{:S(2)}) collective-permute-start(bf16[384,128]{1,0:T(8,128)(2,1)S(1)} %copy-done.1), channel_id=1, source_target_pairs={{0,15},{1,14},{2,13},{3,12},{4,11},{5,10},{6,9},{7,8},{8,7},{9,6},... | collective-permute-start | bytes 294920 | tf_op jit(solution)/shard_map/ppermute | solution.py:760

commit v20 on v19

--- a/solution.py
+++ b/solution.py
@@ -643,13 +643,18 @@
     near_out, far_out, mixer, own, grads, raw_grads, sems, out_sems = refs[-8:]
     wide = total * TILE
     high = half * TILE
+    raw_fetch = pltpu.make_async_copy(raw_grads_ref, raw_grads, sems.at[len(groups), 0])
+    raw_fetch.start()
+    middle = (raw + 2 * lines) // 3 // BLOCK * BLOCK
+    parts = ((0, raw), (raw, middle), (middle, lines))
     fetches = []
-    for group, group_ref in zip(groups, group_refs):
-        for j, at in enumerate(group):
-            fetches.append(pltpu.make_async_copy(group_ref.at[j], grads.at[at], sems.at[len(fetches)]))
-    fetches.append(pltpu.make_async_copy(raw_grads_ref, raw_grads, sems.at[total]))
-    for fetch in fetches:
-        fetch.start()
+    for n, (first, last) in enumerate(parts):
+        part = pl.ds(first, last - first)
+        fetches.append([])
+        for g, (group, group_ref) in enumerate(zip(groups, group_refs)):
+            target = grads.at[pl.ds(group[0], len(group)), part, :]
+            fetches[n].append(pltpu.make_async_copy(group_ref.at[:, part, :], target, sems.at[g, n]))
+            fetches[n][-1].start()
     gram = jnp.sum(grams_ref[...], axis=0)[:, :total]
     spread, anneal, step_size = (numbers_ref[k : k + 1, :1] for k in range(3))
     rate = step_size / total
@@ -667,8 +672,6 @@
     mixer[...] = full.astype(BF16)
     ksum = jnp.sum(full, axis=1, keepdims=True)
     own[...] = jnp.broadcast_to(1.0 + rate * coeff * ksum, (wide, LANES))
-    for fetch in fetches:
-        fetch.wait()
 
     stores = []
 
@@ -715,16 +718,16 @@
             near_out[:, lines_of(lines + at, TILE), :] = new.reshape(half, TILE, LANES)
         return carry
 
+    raw_fetch.wait()
     lax.fori_loop(0, raw // BLOCK, raw_step, 0)
     store_near(lines, lines + raw, 0)
-    lax.fori_loop(0, raw // BLOCK, functools.partial(slab_step, False), 0)
-    middle = (raw + 2 * lines) // 3 // BLOCK * BLOCK
-    lax.fori_loop(raw // BLOCK, middle // BLOCK, functools.partial(slab_step, True), 0)
-    store_near(0, middle, 1)
-    store_far(raw, middle, 0)
-    lax.fori_loop(middle // BLOCK, lines // BLOCK, functools.partial(slab_step, True), 0)
-    store_near(middle, lines, 2)
-    store_far(middle, lines, 1)
+    for n, (first, last) in enumerate(parts):
+        for fetch in fetches[n]:
+            fetch.wait()
+        lax.fori_loop(first // BLOCK, last // BLOCK, functools.partial(slab_step, n > 0), 0)
+        store_near(first, last, 1 + n)
+        if n:
+            store_far(first, last, n - 1)
     for copy in stores:
         copy.wait()
 
@@ -750,8 +753,8 @@
             pltpu.VMEM((wide, LANES), F32),
             pltpu.VMEM((total, lines, LANES), BF16),
             pltpu.VMEM((total, raw, LANES), BF16),
-            pltpu.SemaphoreType.DMA((total + 1,)),
-            pltpu.SemaphoreType.DMA((half + 1, 3)),
+            pltpu.SemaphoreType.DMA((len(groups) + 1, 3)),
+            pltpu.SemaphoreType.DMA((half + 1, 4)),
         ],
     )(near, *far, across, numbers, grams, raw_grads, *grads)
 

time: 130 us -> 130 us (level)
  no operation moved by 1% of the time
where the time goes in v20:
time: 130 us; the launch traced here: 129 us
  waiting for transfers between devices  63.6 us (49%)
  starting transfers between devices  37 us (28%)
  Pallas kernels  25.8 us (20%)
  between operations  2.15 us (2%)
    ppermute x17, waiting for transfers between devices, exchange(): return lax.ppermute(piece, 'slab', [(i, i ^ k) for i in range(slabs)])  62.4 us
    ppermute x17, starting transfers between devices, exchange(): return lax.ppermute(piece, 'slab', [(i, i ^ k) for i in range(slabs)])  20.4 us
    all_to_all x2, starting transfers between devices, swap_near(): lax.all_to_all(pieces, 'slab', 0, 0, axis_index_groups=groups, tiled=True)  10.9 us
    pallas_call x4, Pallas kernels, gradient_pieces(): call(functools.partial(gradient_pieces_body, views, len(arrays), len(numb...  9.57 us
    all_to_all x1, starting transfers between devices, swap(): lax.all_to_all(slabs, 'slab', split_axis=0, concat_axis=0, tiled=True)  5.75 us
    pallas_call x4, Pallas kernels, join_pieces(): call(functools.partial(join_pieces_body, pieces, slabs // 2, raw, NCELL /...  5.55 us
    pallas_call x1, Pallas kernels, update_pieces(): call(functools.partial(update_pieces_body, half, raw, lines, groups), 'up...  5.19 us
    pallas_call x1, Pallas kernels, split_pieces(): call(functools.partial(split_pieces_body, slabs, raw, lines, len(fields))...  3.75 us
  transfers between devices with their start and end apart: 20, of which 15 were waited for; matrix products, arithmetic and copies ran while one was open for 0% of the time, Pallas kernels for 12%

profile of v20, /device:TPU:9, one launch (start us, length us, event | category | flops | bytes accessed | tf_op | source)
XLA Modules:
  0.0 129.2 jit_solution(4297180645759515837)
XLA Ops:
  0.0 3.7 %split_pieces.1 = (bf16[8,672,128]{2,1,0:T(8,128)(2,1)}, bf16[528,128]{1,0:T(8,128)(2,1)S(1)}, bf16[528,128]{1,0:T(8,128)(2,1)S(1)}, bf16[528,128]{1,0:T(8,128)(...) custom-call(bf16[1,1048576]{1,0:T(2,128)(2,1)} %row_ref.1, ...), custom_call_target="tpu_custom_call" | custom-call | bytes 7372800 | tf_op jit(solution)/shard_map/split_pieces/pallas_call | solution.py:431
  3.8 4.6 %all-to-all-start = ((bf16[8,672,128]{2,1,0:T(8,128)(2,1)}), bf16[8,672,128]{2,1,0:T(8,128)(2,1)S(1)}, u32[]{:S(2)}, u32[]{:S(2)}) async-start(bf16[8,672,128]{2,1,0:T(8,128)(2,1)} %get-tuple-element.32), calls=%async_computation | async-start | bytes 2752512 | tf_op jit(solution)/shard_map/all_to_all | solution.py:768
  8.3 2.3 %collective-permute-start = (bf16[528,128]{1,0:T(8,128)(2,1)S(1)}, bf16[528,128]{1,0:T(8,128)(2,1)S(1)}, u32[]{:S(2)}, u32[]{:S(2)}) collective-permute-start(bf16[528,128]{1,0:T(8,128)(2,1)S(1)} %get-tuple-element.33), channel_id=1, source_target_pairs={{0,8},{1,9},{2,10},{3,11},{4,12},{5,13},{6,14},{7,15},{8,0},{9,1},... | collective-permute-start | bytes 405512 | tf_op jit(solution)/shard_map/ppermute | solution.py:763
  10.6 0.6 collective-permute-start.1
  11.2 3.2 %collective-permute-start.2 = (bf16[528,128]{1,0:T(8,128)(2,1)S(1)}, bf16[528,128]{1,0:T(8,128)(2,1)S(1)}, u32[]{:S(2)}, u32[]{:S(2)}) collective-permute-start(bf16[528,128]{1,0:T(8,128)(2,1)S(1)} %get-tuple-element.35), channel_id=1, source_target_pairs={{0,10},{1,11},{2,8},{3,9},{4,14},{5,15},{6,12},{7,13},{8,2},{9,3},... | collective-permute-start | bytes 405512 | tf_op jit(solution)/shard_map/ppermute | solution.py:763
  14.4 0.3 collective-permute-start.3
  14.7 1.0 collective-permute-start.4
  15.7 13.5 %collective-permute-done.refs_0_ = bf16[528,128]{1,0:T(8,128)(2,1)S(1)} collective-permute-done((bf16[528,128]{1,0:T(8,128)(2,1)S(1)}, bf16[528,128]{1,0:T(8,128)(2,1)S(1)}, u32[]{:S(2)}, u32[]{:S(2)}) %collective-permute-start) | collective-permute-done | bytes 135200 | tf_op jit(solution)/shard_map/ppermute | solution.py:763
  29.3 0.0 collective-permute-start.5
  29.3 3.6 %collective-permute-done.1.refs_1_ = bf16[528,128]{1,0:T(8,128)(2,1)S(1)} collective-permute-done((bf16[528,128]{1,0:T(8,128)(2,1)S(1)}, bf16[528,128]{1,0:T(8,128)(2,1)S(1)}, u32[]{:S(2)}, u32[]{:S(2)}) %collective-permute-start.1) | collective-permute-done | bytes 135200 | tf_op jit(solution)/shard_map/ppermute | solution.py:763
  32.9 0.3 collective-permute-start.6
  33.2 2.8 %collective-permute-done.2.refs_2_ = bf16[528,128]{1,0:T(8,128)(2,1)S(1)} collective-permute-done((bf16[528,128]{1,0:T(8,128)(2,1)S(1)}, bf16[528,128]{1,0:T(8,128)(2,1)S(1)}, u32[]{:S(2)}, u32[]{:S(2)}) %collective-permute-start.2) | collective-permute-done | bytes 135200 | tf_op jit(solution)/shard_map/ppermute | solution.py:763
  36.0 0.0 collective-permute-start.7
  37.9 1.7 %collective-permute-done.3.refs_3_ = bf16[528,128]{1,0:T(8,128)(2,1)S(1)} collective-permute-done((bf16[528,128]{1,0:T(8,128)(2,1)S(1)}, bf16[528,128]{1,0:T(8,128)(2,1)S(1)}, u32[]{:S(2)}, u32[]{:S(2)}) %collective-permute-start.3) | collective-permute-done | bytes 135200 | tf_op jit(solution)/shard_map/ppermute | solution.py:763
  39.6 1.8 %gradient_pieces.4 = (bf16[4,512,128]{2,1,0:T(8,128)(2,1)}, f32[8,128]{1,0:T(8,128)S(1)}) custom-call(bf16[528,128]{1,0:T(8,128)(2,1)S(1)} %collective-permute-done.refs_0_, bf16[528,128]{1,0:T(8,128)(2,1)S(1)} %collective-permute-done.1.refs_1_, bf16[528,128]{1,0:T(8,128)(2,1)S(1)} %collective-permute-done.2.refs_2_, ...), custom_call_target="tpu_custom_call" | custom-call | flops 7864320 | bytes 2097152 | tf_op jit(solution)/shard_map/gradient_pieces/pallas_call | solution.py:594
  41.4 6.7 %collective-permute-done.4.refs_4_.refs_0_ = bf16[528,128]{1,0:T(8,128)(2,1)S(1)} collective-permute-done((bf16[528,128]{1,0:T(8,128)(2,1)S(1)}, bf16[528,128]{1,0:T(8,128)(2,1)S(1)}, u32[]{:S(2)}, u32[]{:S(2)}) %collective-permute-start.4) | collective-permute-done | bytes 135200 | tf_op jit(solution)/shard_map/ppermute | solution.py:763
  48.1 4.7 %collective-permute-done.5.refs_5_.refs_1_ = bf16[528,128]{1,0:T(8,128)(2,1)S(1)} collective-permute-done((bf16[528,128]{1,0:T(8,128)(2,1)S(1)}, bf16[528,128]{1,0:T(8,128)(2,1)S(1)}, u32[]{:S(2)}, u32[]{:S(2)}) %collective-permute-start.5) | collective-permute-done | bytes 135200 | tf_op jit(solution)/shard_map/ppermute | solution.py:763
  52.9 3.8 %collective-permute-done.6.refs_6_.refs_2_ = bf16[528,128]{1,0:T(8,128)(2,1)S(1)} collective-permute-done((bf16[528,128]{1,0:T(8,128)(2,1)S(1)}, bf16[528,128]{1,0:T(8,128)(2,1)S(1)}, u32[]{:S(2)}, u32[]{:S(2)}) %collective-permute-start.6) | collective-permute-done | bytes 135200 | tf_op jit(solution)/shard_map/ppermute | solution.py:763
  56.7 2.9 %collective-permute-done.7.refs_7_.refs_3_ = bf16[528,128]{1,0:T(8,128)(2,1)S(1)} collective-permute-done((bf16[528,128]{1,0:T(8,128)(2,1)S(1)}, bf16[528,128]{1,0:T(8,128)(2,1)S(1)}, u32[]{:S(2)}, u32[]{:S(2)}) %collective-permute-start.7) | collective-permute-done | bytes 135200 | tf_op jit(solution)/shard_map/ppermute | solution.py:763
  59.6 0.1 collective-permute-start.8
  59.7 1.7 %gram_pieces.1 = f32[16,16,128]{2,1,0:T(8,128)S(1)} custom-call(bf16[8,672,128]{2,1,0:T(8,128)(2,1)S(1)} %all-to-all-done.near_ref.refs_0_, bf16[528,128]{1,0:T(8,128)(2,1)S(1)} %collective-permute-done.refs_0_, bf16[528,128]{1,0:T(8,128)(2,1)S(1)} %collective-permute-done.1.refs_1_, bf16[528,128]{1,0:T(8,128)(2,1)S(1)} %collective-permute-done.2.refs_2_, ...), custom_call_target="tpu_custom_call" | custom-call | flops 536870912 | bytes 2097152 | tf_op jit(solution)/shard_map/gram_pieces/pallas_call | solution.py:521
  61.4 0.0 copy-start
  61.4 0.6 copy-done
  62.1 5.7 %all-to-all-start.1 = ((f32[16,16,128]{2,1,0:T(8,128)}), f32[16,16,128]{2,1,0:T(8,128)S(1)}, u32[]{:S(2)}, u32[]{:S(2)}) async-start(f32[16,16,128]{2,1,0:T(8,128)} %copy-done), calls=%async_computation.1 | async-start | bytes 262144 | tf_op jit(solution)/shard_map/all_to_all | solution.py:365
  67.8 2.4 %gradient_pieces.6 = (bf16[4,512,128]{2,1,0:T(8,128)(2,1)}, f32[8,128]{1,0:T(8,128)}) custom-call(bf16[528,128]{1,0:T(8,128)(2,1)S(1)} %collective-permute-done.4.refs_4_.refs_0_, bf16[528,128]{1,0:T(8,128)(2,1)S(1)} %collective-permute-done.5.refs_5_.refs_1_, bf16[528,128]{1,0:T(8,128)(2,1)S(1)} %collective-permute-done.6.refs_6_.refs_2_, ...), custom_call_target="tpu_custom_call" | custom-call | flops 7864320 | bytes 2097152 | tf_op jit(solution)/shard_map/gradient_pieces/pallas_call | solution.py:594
  70.2 3.2 %gradient_pieces.7 = (bf16[8,512,128]{2,1,0:T(8,128)(2,1)}, f32[8,128]{1,0:T(8,128)}) custom-call(bf16[8,672,128]{2,1,0:T(8,128)(2,1)S(1)} %all-to-all-done.near_ref.refs_0_, bf16[512,128]{1,0:T(8,128)(2,1)S(1)} %get-tuple-element.41.refs_4_.refs_1_, bf16[512,128]{1,0:T(8,128)(2,1)S(1)} %get-tuple-element.42.refs_5_.refs_2_), custom_call_target="tpu_custom_call" | custom-call | flops 15728640 | bytes 4194304 | tf_op jit(solution)/shard_map/gradient_pieces/pallas_call | solution.py:594
  73.4 0.2 collective-permute-done.8.refs_1_.refs_8_
  73.6 2.2 %gradient_pieces.5 = (bf16[16,128,128]{2,1,0:T(8,128)(2,1)}, f32[8,128]{1,0:T(8,128)}) custom-call(bf16[8,672,128]{2,1,0:T(8,128)(2,1)S(1)} %all-to-all-done.near_ref.refs_0_, bf16[8,144,128]{2,1,0:T(8,128)(2,1)S(1)} %collective-permute-done.8.refs_1_.refs_8_, bf16[128,128]{1,0:T(8,128)(2,1)S(1)} %get-tuple-element.45.refs_2_, ...), custom_call_target="tpu_custom_call" | custom-call | flops 7864320 | bytes 2097152 | tf_op jit(solution)/shard_map/gradient_pieces/pallas_call | solution.py:594
  75.8 1.2 all-to-all-done.1.refs_10_
  77.0 5.2 %update_pieces.1 = (bf16[8,640,128]{2,1,0:T(8,128)(2,1)}, bf16[384,128]{1,0:T(8,128)(2,1)}, bf16[384,128]{1,0:T(8,128)(2,1)}, bf16[384,128]{1,0:T(8,128)(2,1)}, ...) custom-call(bf16[8,672,128]{2,1,0:T(8,128)(2,1)S(1)} %all-to-all-don, ...), custom_call_target="tpu_custom_call" | custom-call | flops 1073741824 | bytes 6291456 | tf_op jit(solution)/shard_map/update_pieces/pallas_call | solution.py:741
  82.3 6.3 %all-to-all-start.2 = ((bf16[8,640,128]{2,1,0:T(8,128)(2,1)}), bf16[8,640,128]{2,1,0:T(8,128)(2,1)S(1)}, u32[]{:S(2)}, u32[]{:S(2)}) async-start(bf16[8,640,128]{2,1,0:T(8,128)(2,1)} %get-tuple-element.50), calls=%async_computation.2 | async-start | bytes 2621440 | tf_op jit(solution)/shard_map/all_to_all | solution.py:768
  88.6 0.3 collective-permute-start.9
  88.9 2.6 %collective-permute-start.10 = (bf16[384,128]{1,0:T(8,128)(2,1)S(1)}, bf16[384,128]{1,0:T(8,128)(2,1)S(1)}, u32[]{:S(2)}, u32[]{:S(2)}) collective-permute-start(bf16[384,128]{1,0:T(8,128)(2,1)S(1)} %copy-done.7), channel_id=1, source_target_pairs={{0,9},{1,8},{2,11},{3,10},{4,13},{5,12},{6,15},{7,14},{8,1},{9,0},... | collective-permute-start | bytes 294920 | tf_op jit(solution)/shard_map/ppermute | solution.py:763
  91.5 1.2 collective-permute-start.11
  92.7 2.1 %collective-permute-start.12 = (bf16[384,128]{1,0:T(8,128)(2,1)S(1)}, bf16[384,128]{1,0:T(8,128)(2,1)S(1)}, u32[]{:S(2)}, u32[]{:S(2)}) collective-permute-start(bf16[384,128]{1,0:T(8,128)(2,1)S(1)} %copy-done.5), channel_id=1, source_target_pairs={{0,11},{1,10},{2,9},{3,8},{4,15},{5,14},{6,13},{7,12},{8,3},{9,2},... | collective-permute-start | bytes 294920 | tf_op jit(solution)/shard_map/ppermute | solution.py:763
  94.8 11.0 %collective-permute-done.9.refs_1_ = bf16[384,128]{1,0:T(8,128)(2,1)S(1)} collective-permute-done((bf16[384,128]{1,0:T(8,128)(2,1)S(1)}, bf16[384,128]{1,0:T(8,128)(2,1)S(1)}, u32[]{:S(2)}, u32[]{:S(2)}) %collective-permute-start.9) | collective-permute-done | bytes 98336 | tf_op jit(solution)/shard_map/ppermute | solution.py:763
  105.8 2.2 %collective-permute-start.14 = (bf16[384,128]{1,0:T(8,128)(2,1)S(1)}, bf16[384,128]{1,0:T(8,128)(2,1)S(1)}, u32[]{:S(2)}, u32[]{:S(2)}) collective-permute-start(bf16[384,128]{1,0:T(8,128)(2,1)S(1)} %copy-done.3), channel_id=1, source_target_pairs={{0,13},{1,12},{2,15},{3,14},{4,9},{5,8},{6,11},{7,10},{8,5},{9,4},... | collective-permute-start | bytes 294920 | tf_op jit(solution)/shard_map/ppermute | solution.py:763
  108.0 1.0 collective-permute-done.10.refs_2_
  109.0 2.1 %collective-permute-start.15 = (bf16[384,128]{1,0:T(8,128)(2,1)S(1)}, bf16[384,128]{1,0:T(8,128)(2,1)S(1)}, u32[]{:S(2)}, u32[]{:S(2)}) collective-permute-start(bf16[384,128]{1,0:T(8,128)(2,1)S(1)} %copy-done.2), channel_id=1, source_target_pairs={{0,14},{1,15},{2,12},{3,13},{4,10},{5,11},{6,8},{7,9},{8,6},{9,7},... | collective-permute-start | bytes 294920 | tf_op jit(solution)/shard_map/ppermute | solution.py:763
  111.1 0.0 collective-permute-done.11.refs_3_
  111.1 2.1 %collective-permute-start.16 = (bf16[384,128]{1,0:T(8,128)(2,1)S(1)}, bf16[384,128]{1,0:T(8,128)(2,1)S(1)}, u32[]{:S(2)}, u32[]{:S(2)}) collective-permute-start(bf16[384,128]{1,0:T(8,128)(2,1)S(1)} %copy-done.1), channel_id=1, source_target_pairs={{0,15},{1,14},{2,13},{3,12},{4,11},{5,10},{6,9},{7,8},{8,7},{9,6},... | collective-permute-start | bytes 294920 | tf_op jit(solution)/shard_map/ppermute | solution.py:763
  113.2 3.0 %join_pieces.4.refs_0_ = bf16[1,1048576]{1,0:T(2,128)(2,1)} custom-call(bf16[8,640,128]{2,1,0:T(8,128)(2,1)S(1)} %all-to-all-done.2.refs_0_), custom_call_target="tpu_custom_call" | custom-call | bytes 3932160 | tf_op jit(solution)/shard_map/join_pieces/pallas_call | solution.py:467
  116.2 1.0 join_pieces.5.refs_0_
  117.2 6.1 %collective-permute-done.14.refs_2_ = bf16[384,128]{1,0:T(8,128)(2,1)S(1)} collective-permute-done((bf16[384,128]{1,0:T(8,128)(2,1)S(1)}, bf16[384,128]{1,0:T(8,128)(2,1)S(1)}, u32[]{:S(2)}, u32[]{:S(2)}) %collective-permute-start.14) | collective-permute-done | bytes 98336 | tf_op jit(solution)/shard_map/ppermute | solution.py:763
  123.3 0.8 join_pieces.6.refs_0_
  124.1 2.3 %collective-permute-done.15.refs_1_ = bf16[384,128]{1,0:T(8,128)(2,1)S(1)} collective-permute-done((bf16[384,128]{1,0:T(8,128)(2,1)S(1)}, bf16[384,128]{1,0:T(8,128)(2,1)S(1)}, u32[]{:S(2)}, u32[]{:S(2)}) %collective-permute-start.15) | collective-permute-done | bytes 98336 | tf_op jit(solution)/shard_map/ppermute | solution.py:763
  126.3 2.1 %collective-permute-done.16.refs_2_ = bf16[384,128]{1,0:T(8,128)(2,1)S(1)} collective-permute-done((bf16[384,128]{1,0:T(8,128)(2,1)S(1)}, bf16[384,128]{1,0:T(8,128)(2,1)S(1)}, u32[]{:S(2)}, u32[]{:S(2)}) %collective-permute-start.16) | collective-permute-done | bytes 98336 | tf_op jit(solution)/shard_map/ppermute | solution.py:763
  128.4 0.8 join_pieces.7
  (22 shorter events, 0.1 us)
Async XLA Ops:
  3.8 55.8 %all-to-all-start = ((bf16[8,672,128]{2,1,0:T(8,128)(2,1)}), bf16[8,672,128]{2,1,0:T(8,128)(2,1)S(1)}, u32[]{:S(2)}, u32[]{:S(2)}) async-start(bf16[8,672,128]{2,1,0:T(8,128)(2,1)} %get-tuple-element.32), calls=%async_computation | async-start | bytes 2752512 | tf_op jit(solution)/shard_map/all_to_all | solution.py:768
  8.3 20.9 %collective-permute-start = (bf16[528,128]{1,0:T(8,128)(2,1)S(1)}, bf16[528,128]{1,0:T(8,128)(2,1)S(1)}, u32[]{:S(2)}, u32[]{:S(2)}) collective-permute-start(bf16[528,128]{1,0:T(8,128)(2,1)S(1)} %get-tuple-element.33), channel_id=1, source_target_pairs={{0,8},{1,9},{2,10},{3,11},{4,12},{5,13},{6,14},{7,15},{8,0},{9,1},... | collective-permute-start | bytes 405512 | tf_op jit(solution)/shard_map/ppermute | solution.py:763
  10.6 22.2 %collective-permute-start.1 = (bf16[528,128]{1,0:T(8,128)(2,1)S(1)}, bf16[528,128]{1,0:T(8,128)(2,1)S(1)}, u32[]{:S(2)}, u32[]{:S(2)}) collective-permute-start(bf16[528,128]{1,0:T(8,128)(2,1)S(1)} %get-tuple-element.34), channel_id=1, source_target_pairs={{0,9},{1,8},{2,11},{3,10},{4,13},{5,12},{6,15},{7,14},{8,1},{9,0},... | collective-permute-start | bytes 405512 | tf_op jit(solution)/shard_map/ppermute | solution.py:763
  11.2 24.8 %collective-permute-start.2 = (bf16[528,128]{1,0:T(8,128)(2,1)S(1)}, bf16[528,128]{1,0:T(8,128)(2,1)S(1)}, u32[]{:S(2)}, u32[]{:S(2)}) collective-permute-start(bf16[528,128]{1,0:T(8,128)(2,1)S(1)} %get-tuple-element.35), channel_id=1, source_target_pairs={{0,10},{1,11},{2,8},{3,9},{4,14},{5,15},{6,12},{7,13},{8,2},{9,3},... | collective-permute-start | bytes 405512 | tf_op jit(solution)/shard_map/ppermute | solution.py:763
  14.4 25.2 %collective-permute-start.3 = (bf16[528,128]{1,0:T(8,128)(2,1)S(1)}, bf16[528,128]{1,0:T(8,128)(2,1)S(1)}, u32[]{:S(2)}, u32[]{:S(2)}) collective-permute-start(bf16[528,128]{1,0:T(8,128)(2,1)S(1)} %get-tuple-element.36), channel_id=1, source_target_pairs={{0,11},{1,10},{2,9},{3,8},{4,15},{5,14},{6,13},{7,12},{8,3},{9,2},... | collective-permute-start | bytes 405512 | tf_op jit(solution)/shard_map/ppermute | solution.py:763
  14.7 33.4 %collective-permute-start.4 = (bf16[528,128]{1,0:T(8,128)(2,1)S(1)}, bf16[528,128]{1,0:T(8,128)(2,1)S(1)}, u32[]{:S(2)}, u32[]{:S(2)}) collective-permute-start(bf16[528,128]{1,0:T(8,128)(2,1)S(1)} %get-tuple-element.37), channel_id=1, source_target_pairs={{0,12},{1,13},{2,14},{3,15},{4,8},{5,9},{6,10},{7,11},{8,4},{9,5},... | collective-permute-start | bytes 405512 | tf_op jit(solution)/shard_map/ppermute | solution.py:763
  29.3 23.6 %collective-permute-start.5 = (bf16[528,128]{1,0:T(8,128)(2,1)S(1)}, bf16[528,128]{1,0:T(8,128)(2,1)S(1)}, u32[]{:S(2)}, u32[]{:S(2)}) collective-permute-start(bf16[528,128]{1,0:T(8,128)(2,1)S(1)} %get-tuple-element.38), channel_id=1, source_target_pairs={{0,13},{1,12},{2,15},{3,14},{4,9},{5,8},{6,11},{7,10},{8,5},{9,4},... | collective-permute-start | bytes 405512 | tf_op jit(solution)/shard_map/ppermute | solution.py:763
  32.9 23.8 %collective-permute-start.6 = (bf16[528,128]{1,0:T(8,128)(2,1)S(1)}, bf16[528,128]{1,0:T(8,128)(2,1)S(1)}, u32[]{:S(2)}, u32[]{:S(2)}) collective-permute-start(bf16[528,128]{1,0:T(8,128)(2,1)S(1)} %get-tuple-element.39), channel_id=1, source_target_pairs={{0,14},{1,15},{2,12},{3,13},{4,10},{5,11},{6,8},{7,9},{8,6},{9,7},... | collective-permute-start | bytes 405512 | tf_op jit(solution)/shard_map/ppermute | solution.py:763
  36.0 23.5 %collective-permute-start.7 = (bf16[528,128]{1,0:T(8,128)(2,1)S(1)}, bf16[528,128]{1,0:T(8,128)(2,1)S(1)}, u32[]{:S(2)}, u32[]{:S(2)}) collective-permute-start(bf16[528,128]{1,0:T(8,128)(2,1)S(1)} %get-tuple-element.40), channel_id=1, source_target_pairs={{0,15},{1,14},{2,13},{3,12},{4,11},{5,10},{6,9},{7,8},{8,7},{9,6},... | collective-permute-start | bytes 405512 | tf_op jit(solution)/shard_map/ppermute | solution.py:763
  59.6 14.0 %collective-permute-start.8 = (bf16[8,144,128]{2,1,0:T(8,128)(2,1)S(1)}, bf16[8,144,128]{2,1,0:T(8,128)(2,1)S(1)}, u32[]{:S(2)}, u32[]{:S(2)}) collective-permute-start(bf16[8,144,128]{2,1,0:T(8,128)(2,1)S(1)} %raw_states.1.refs_9_), channel_id=1, source_target_pairs={{0,8},{1,9},{2,10},{3,11},{4,12},{5,13},{6,14},{7,15},{8,0},{9,1},... | collective-permute-start | bytes 884744 | tf_op jit(solution)/shard_map/ppermute | solution.py:763
  61.4 0.7 copy-start
  62.1 14.9 %all-to-all-start.1 = ((f32[16,16,128]{2,1,0:T(8,128)}), f32[16,16,128]{2,1,0:T(8,128)S(1)}, u32[]{:S(2)}, u32[]{:S(2)}) async-start(f32[16,16,128]{2,1,0:T(8,128)} %copy-done), calls=%async_computation.1 | async-start | bytes 262144 | tf_op jit(solution)/shard_map/all_to_all | solution.py:365
  82.2 6.4 %copy-start.8 = (bf16[384,128]{1,0:T(8,128)(2,1)S(1)}, bf16[384,128]{1,0:T(8,128)(2,1)}, u32[]{:S(2)}) copy-start(bf16[384,128]{1,0:T(8,128)(2,1)} %get-tuple-element.51) | copy-start | bytes 294916
  82.2 6.7 %copy-start.7 = (bf16[384,128]{1,0:T(8,128)(2,1)S(1)}, bf16[384,128]{1,0:T(8,128)(2,1)}, u32[]{:S(2)}) copy-start(bf16[384,128]{1,0:T(8,128)(2,1)} %get-tuple-element.52) | copy-start | bytes 294916
  82.2 9.2 %copy-start.6 = (bf16[384,128]{1,0:T(8,128)(2,1)S(1)}, bf16[384,128]{1,0:T(8,128)(2,1)}, u32[]{:S(2)}) copy-start(bf16[384,128]{1,0:T(8,128)(2,1)} %get-tuple-element.53) | copy-start | bytes 294916
  82.2 10.4 %copy-start.5 = (bf16[384,128]{1,0:T(8,128)(2,1)S(1)}, bf16[384,128]{1,0:T(8,128)(2,1)}, u32[]{:S(2)}) copy-start(bf16[384,128]{1,0:T(8,128)(2,1)} %get-tuple-element.54) | copy-start | bytes 294916
  82.2 12.5 %copy-start.4 = (bf16[384,128]{1,0:T(8,128)(2,1)S(1)}, bf16[384,128]{1,0:T(8,128)(2,1)}, u32[]{:S(2)}) copy-start(bf16[384,128]{1,0:T(8,128)(2,1)} %get-tuple-element.55) | copy-start | bytes 294916
  82.2 23.6 %copy-start.3 = (bf16[384,128]{1,0:T(8,128)(2,1)S(1)}, bf16[384,128]{1,0:T(8,128)(2,1)}, u32[]{:S(2)}) copy-start(bf16[384,128]{1,0:T(8,128)(2,1)} %get-tuple-element.56) | copy-start | bytes 294916
  82.3 26.7 %copy-start.2 = (bf16[384,128]{1,0:T(8,128)(2,1)S(1)}, bf16[384,128]{1,0:T(8,128)(2,1)}, u32[]{:S(2)}) copy-start(bf16[384,128]{1,0:T(8,128)(2,1)} %get-tuple-element.57) | copy-start | bytes 294916
  82.3 28.8 %copy-start.1 = (bf16[384,128]{1,0:T(8,128)(2,1)S(1)}, bf16[384,128]{1,0:T(8,128)(2,1)}, u32[]{:S(2)}) copy-start(bf16[384,128]{1,0:T(8,128)(2,1)} %get-tuple-element.58) | copy-start | bytes 294916
  82.3 30.9 %all-to-all-start.2 = ((bf16[8,640,128]{2,1,0:T(8,128)(2,1)}), bf16[8,640,128]{2,1,0:T(8,128)(2,1)S(1)}, u32[]{:S(2)}, u32[]{:S(2)}) async-start(bf16[8,640,128]{2,1,0:T(8,128)(2,1)} %get-tuple-element.50), calls=%async_computation.2 | async-start | bytes 2621440 | tf_op jit(solution)/shard_map/all_to_all | solution.py:768
  88.6 17.2 %collective-permute-start.9 = (bf16[384,128]{1,0:T(8,128)(2,1)S(1)}, bf16[384,128]{1,0:T(8,128)(2,1)S(1)}, u32[]{:S(2)}, u32[]{:S(2)}) collective-permute-start(bf16[384,128]{1,0:T(8,128)(2,1)S(1)} %copy-done.8), channel_id=1, source_target_pairs={{0,8},{1,9},{2,10},{3,11},{4,12},{5,13},{6,14},{7,15},{8,0},{9,1},... | collective-permute-start | bytes 294920 | tf_op jit(solution)/shard_map/ppermute | solution.py:763
  88.9 20.1 %collective-permute-start.10 = (bf16[384,128]{1,0:T(8,128)(2,1)S(1)}, bf16[384,128]{1,0:T(8,128)(2,1)S(1)}, u32[]{:S(2)}, u32[]{:S(2)}) collective-permute-start(bf16[384,128]{1,0:T(8,128)(2,1)S(1)} %copy-done.7), channel_id=1, source_target_pairs={{0,9},{1,8},{2,11},{3,10},{4,13},{5,12},{6,15},{7,14},{8,1},{9,0},... | collective-permute-start | bytes 294920 | tf_op jit(solution)/shard_map/ppermute | solution.py:763
  91.5 19.7 %collective-permute-start.11 = (bf16[384,128]{1,0:T(8,128)(2,1)S(1)}, bf16[384,128]{1,0:T(8,128)(2,1)S(1)}, u32[]{:S(2)}, u32[]{:S(2)}) collective-permute-start(bf16[384,128]{1,0:T(8,128)(2,1)S(1)} %copy-done.6), channel_id=1, source_target_pairs={{0,10},{1,11},{2,8},{3,9},{4,14},{5,15},{6,12},{7,13},{8,2},{9,3},... | collective-permute-start | bytes 294920 | tf_op jit(solution)/shard_map/ppermute | solution.py:763
  92.7 23.5 %collective-permute-start.12 = (bf16[384,128]{1,0:T(8,128)(2,1)S(1)}, bf16[384,128]{1,0:T(8,128)(2,1)S(1)}, u32[]{:S(2)}, u32[]{:S(2)}) collective-permute-start(bf16[384,128]{1,0:T(8,128)(2,1)S(1)} %copy-done.5), channel_id=1, source_target_pairs={{0,11},{1,10},{2,9},{3,8},{4,15},{5,14},{6,13},{7,12},{8,3},{9,2},... | collective-permute-start | bytes 294920 | tf_op jit(solution)/shard_map/ppermute | solution.py:763
  94.8 22.4 %collective-permute-start.13 = (bf16[384,128]{1,0:T(8,128)(2,1)S(1)}, bf16[384,128]{1,0:T(8,128)(2,1)S(1)}, u32[]{:S(2)}, u32[]{:S(2)}) collective-permute-start(bf16[384,128]{1,0:T(8,128)(2,1)S(1)} %copy-done.4), channel_id=1, source_target_pairs={{0,12},{1,13},{2,14},{3,15},{4,8},{5,9},{6,10},{7,11},{8,4},{9,5},... | collective-permute-start | bytes 294920 | tf_op jit(solution)/shard_map/ppermute | solution.py:763
  105.8 17.5 %collective-permute-start.14 = (bf16[384,128]{1,0:T(8,128)(2,1)S(1)}, bf16[384,128]{1,0:T(8,128)(2,1)S(1)}, u32[]{:S(2)}, u32[]{:S(2)}) collective-permute-start(bf16[384,128]{1,0:T(8,128)(2,1)S(1)} %copy-done.3), channel_id=1, source_target_pairs={{0,13},{1,12},{2,15},{3,14},{4,9},{5,8},{6,11},{7,10},{8,5},{9,4},... | collective-permute-start | bytes 294920 | tf_op jit(solution)/shard_map/ppermute | solution.py:763
  109.0 17.4 %collective-permute-start.15 = (bf16[384,128]{1,0:T(8,128)(2,1)S(1)}, bf16[384,128]{1,0:T(8,128)(2,1)S(1)}, u32[]{:S(2)}, u32[]{:S(2)}) collective-permute-start(bf16[384,128]{1,0:T(8,128)(2,1)S(1)} %copy-done.2), channel_id=1, source_target_pairs={{0,14},{1,15},{2,12},{3,13},{4,10},{5,11},{6,8},{7,9},{8,6},{9,7},... | collective-permute-start | bytes 294920 | tf_op jit(solution)/shard_map/ppermute | solution.py:763
  111.1 17.3 %collective-permute-start.16 = (bf16[384,128]{1,0:T(8,128)(2,1)S(1)}, bf16[384,128]{1,0:T(8,128)(2,1)S(1)}, u32[]{:S(2)}, u32[]{:S(2)}) collective-permute-start(bf16[384,128]{1,0:T(8,128)(2,1)S(1)} %copy-done.1), channel_id=1, source_target_pairs={{0,15},{1,14},{2,13},{3,12},{4,11},{5,10},{6,9},{7,8},{8,7},{9,6},... | collective-permute-start | bytes 294920 | tf_op jit(solution)/shard_map/ppermute | solution.py:763

commit v21 on v20

--- a/solution.py
+++ b/solution.py
@@ -437,6 +437,21 @@
         out_shape=out_shape,
         scratch_shapes=[pltpu.VMEM(row.shape, BF16), pltpu.SemaphoreType.DMA((slabs + 2 * len(fields),))],
     )(row, *fields)
+
+
+def copy_body(piece_ref, *refs):
+    refs[-1][...] = piece_ref[...]
+
+
+def copy_after(piece, gates):
+    return call(
+        copy_body,
+        "copy_after",
+        moved=4 * piece.size,
+        in_specs=[IN_VMEM] * (1 + len(gates)),
+        out_specs=IN_VMEM,
+        out_shape=jax.ShapeDtypeStruct(piece.shape, piece.dtype),
+    )(piece, *gates)
 
 
 def join_pieces_body(pieces, half, raw, lines, begun, arrays, *refs):
@@ -781,19 +796,20 @@
     near, *far = split_pieces(row, slabs, RAW, fields)
     far, (obs, prec, *raw_fields) = far[:half], far[half:]
     near = swap_near(near, slabs)
+    views = tuple((0, k, 0) for k in range(half))
+    near_grads, rows = gradient_pieces([near], views, obs, prec, [])
+    far[-1] = copy_after(far[-1], [rows])
     far = [exchange(piece, half + x, slabs) for x, piece in enumerate(far)]
     raw_near = raw_states(near, RAW, lines, far)
     across = exchange(raw_near, half, slabs)
     grads = []
     numbers = [spread, anneal, step_size]
-    for group in GRADIENTS:
-        if group[0] < half:
-            arrays, views = [near], [(0, k, 0) for k in group]
-        else:
-            arrays, views = [far[k - half] for k in group], [(j, None, 0) for j in range(len(group))]
+    for group in GRADIENTS[:-1]:
+        arrays, views = [far[k - half] for k in group], [(j, None, 0) for j in range(len(group))]
         slopes, rows = gradient_pieces(arrays, tuple(views), obs, prec, [] if grads else numbers)
         grads.append(in_hbm(slopes))
         numbers = numbers if len(grads) > 1 else rows
+    grads.append(in_hbm(near_grads))
     grams = swap(gram_pieces(near, far, lines, grads[:1], [raw_near]))
     views = [(0, k, lines + TILE) for k in range(half)] + [(1, k, 0) for k in range(half)]
     raw_grads, _ = gradient_pieces([near, across], tuple(views), *raw_fields, [])

time: 130 us -> 130 us (level)
  starting transfers between devices: 37 us -> 43.2 us
  waiting for transfers between devices: 63.6 us -> 57.7 us
    ppermute x17, waiting for transfers between devices: 62.4 us -> 37.1 us  [exchange(): return lax.ppermute(piece, 'slab', [(i, i ^ k) for i in range(slabs)])]
    all_to_all x2, waiting for transfers between devices: 0.01 us -> 19.3 us  [swap_near(): lax.all_to_all(pieces, 'slab', 0, 0, axis_index_groups=groups, tiled=True)]
    ppermute x17, starting transfers between devices: 20.4 us -> 25.7 us  [exchange(): return lax.ppermute(piece, 'slab', [(i, i ^ k) for i in range(slabs)])]
  transfers between devices with their start and end apart: 20 -> 20, of which waited for: 15 -> 10; matrix products, arithmetic and copies ran while one was open for 0% -> 0% of each run, Pallas kernels for 12% -> 12%
where the time goes in v21:
time: 130 us; the launch traced here: 129 us
  waiting for transfers between devices  57.7 us (44%)
  starting transfers between devices  43.2 us (33%)
  Pallas kernels  25.3 us (19%)
  between operations  2.19 us (2%)
    ppermute x17, waiting for transfers between devices, exchange(): return lax.ppermute(piece, 'slab', [(i, i ^ k) for i in range(slabs)])  37.1 us
    ppermute x17, starting transfers between devices, exchange(): return lax.ppermute(piece, 'slab', [(i, i ^ k) for i in range(slabs)])  25.7 us
    all_to_all x2, waiting for transfers between devices, swap_near(): lax.all_to_all(pieces, 'slab', 0, 0, axis_index_groups=groups, tiled=True)  19.3 us
    all_to_all x2, starting transfers between devices, swap_near(): lax.all_to_all(pieces, 'slab', 0, 0, axis_index_groups=groups, tiled=True)  11 us
    pallas_call x4, Pallas kernels, gradient_pieces(): call(functools.partial(gradient_pieces_body, views, len(arrays), len(numb...  9 us
    all_to_all x1, starting transfers between devices, swap(): lax.all_to_all(slabs, 'slab', split_axis=0, concat_axis=0, tiled=True)  6.53 us
    pallas_call x4, Pallas kernels, join_pieces(): call(functools.partial(join_pieces_body, pieces, slabs // 2, raw, NCELL /...  5.54 us
    pallas_call x1, Pallas kernels, update_pieces(): call(functools.partial(update_pieces_body, half, raw, lines, groups), 'up...  5.19 us
  transfers between devices with their start and end apart: 20, of which 10 were waited for; matrix products, arithmetic and copies ran while one was open for 0% of the time, Pallas kernels for 12%

profile of v21, /device:TPU:9, one launch (start us, length us, event | category | flops | bytes accessed | tf_op | source)
XLA Modules:
  0.0 129.1 jit_solution(2469115408828887726)
XLA Ops:
  0.0 3.7 %split_pieces.1 = (bf16[8,672,128]{2,1,0:T(8,128)(2,1)}, bf16[528,128]{1,0:T(8,128)(2,1)S(1)}, bf16[528,128]{1,0:T(8,128)(2,1)S(1)}, bf16[528,128]{1,0:T(8,128)(...) custom-call(bf16[1,1048576]{1,0:T(2,128)(2,1)} %row_ref.1, ...), custom_call_target="tpu_custom_call" | custom-call | bytes 7372800 | tf_op jit(solution)/shard_map/split_pieces/pallas_call | solution.py:431
  3.8 4.6 %all-to-all-start = ((bf16[8,672,128]{2,1,0:T(8,128)(2,1)}), bf16[8,672,128]{2,1,0:T(8,128)(2,1)S(1)}, u32[]{:S(2)}, u32[]{:S(2)}) async-start(bf16[8,672,128]{2,1,0:T(8,128)(2,1)} %get-tuple-element.33), calls=%async_computation | async-start | bytes 2752512 | tf_op jit(solution)/shard_map/all_to_all | solution.py:783
  8.3 2.3 %collective-permute-start = (bf16[528,128]{1,0:T(8,128)(2,1)S(1)}, bf16[528,128]{1,0:T(8,128)(2,1)S(1)}, u32[]{:S(2)}, u32[]{:S(2)}) collective-permute-start(bf16[528,128]{1,0:T(8,128)(2,1)S(1)} %get-tuple-element.34), channel_id=1, source_target_pairs={{0,8},{1,9},{2,10},{3,11},{4,12},{5,13},{6,14},{7,15},{8,0},{9,1},... | collective-permute-start | bytes 405512 | tf_op jit(solution)/shard_map/ppermute | solution.py:778
  10.6 0.6 collective-permute-start.1
  11.2 3.2 %collective-permute-start.2 = (bf16[528,128]{1,0:T(8,128)(2,1)S(1)}, bf16[528,128]{1,0:T(8,128)(2,1)S(1)}, u32[]{:S(2)}, u32[]{:S(2)}) collective-permute-start(bf16[528,128]{1,0:T(8,128)(2,1)S(1)} %get-tuple-element.36), channel_id=1, source_target_pairs={{0,10},{1,11},{2,8},{3,9},{4,14},{5,15},{6,12},{7,13},{8,2},{9,3},... | collective-permute-start | bytes 405512 | tf_op jit(solution)/shard_map/ppermute | solution.py:778
  14.4 0.3 collective-permute-start.3
  14.7 1.0 collective-permute-start.4
  15.7 19.3 %all-to-all-done.refs_0_.near_ref = bf16[8,672,128]{2,1,0:T(8,128)(2,1)S(1)} async-done(((bf16[8,672,128]{2,1,0:T(8,128)(2,1)}), bf16[8,672,128]{2,1,0:T(8,128)(2,1)S(1)}, u32[]{:S(2)}, u32[]{:S(2)}) %all-to-all-start) | async-done | bytes 1376288 | tf_op jit(solution)/shard_map/all_to_all | solution.py:783
  35.0 2.6 %gradient_pieces.4 = (bf16[8,512,128]{2,1,0:T(8,128)(2,1)}, f32[8,128]{1,0:T(8,128)S(1)}) custom-call(bf16[8,672,128]{2,1,0:T(8,128)(2,1)S(1)} %all-to-all-done.refs_0_.near_ref, bf16[512,128]{1,0:T(8,128)(2,1)S(1)} %get-tuple-element.42.refs_1_.refs_4_, bf16[512,128]{1,0:T(8,128)(2,1)S(1)} %get-tuple-element.43.refs_2_.refs_5_), custom_call_target="tpu_custom_call" | custom-call | flops 15728640 | bytes 4194304 | tf_op jit(solution)/shard_map/gradient_pieces/pallas_call | solution.py:609
  37.6 2.2 %collective-permute-start.5 = (bf16[528,128]{1,0:T(8,128)(2,1)S(1)}, bf16[528,128]{1,0:T(8,128)(2,1)S(1)}, u32[]{:S(2)}, u32[]{:S(2)}) collective-permute-start(bf16[528,128]{1,0:T(8,128)(2,1)S(1)} %get-tuple-element.39), channel_id=1, source_target_pairs={{0,13},{1,12},{2,15},{3,14},{4,9},{5,8},{6,11},{7,10},{8,5},{9,4},... | collective-permute-start | bytes 405512 | tf_op jit(solution)/shard_map/ppermute | solution.py:778
  39.9 0.0 collective-permute-done.1.refs_1_
  39.9 1.0 collective-permute-start.6
  40.8 0.0 collective-permute-done.2.refs_2_
  40.8 1.4 %collective-permute-start.7 = (bf16[528,128]{1,0:T(8,128)(2,1)S(1)}, bf16[528,128]{1,0:T(8,128)(2,1)S(1)}, u32[]{:S(2)}, u32[]{:S(2)}) collective-permute-start(bf16[528,128]{1,0:T(8,128)(2,1)S(1)} %copy_after.1), channel_id=1, source_target_pairs={{0,15},{1,14},{2,13},{3,12},{4,11},{5,10},{6,9},{7,8},{8,7},{9,6},... | collective-permute-start | bytes 405512 | tf_op jit(solution)/shard_map/ppermute | solution.py:778
  44.2 1.8 %gradient_pieces.5 = (bf16[4,512,128]{2,1,0:T(8,128)(2,1)}, f32[8,128]{1,0:T(8,128)S(1)}) custom-call(bf16[528,128]{1,0:T(8,128)(2,1)S(1)} %collective-permute-done.refs_0_, bf16[528,128]{1,0:T(8,128)(2,1)S(1)} %collective-permute-done.1.refs_1_, bf16[528,128]{1,0:T(8,128)(2,1)S(1)} %collective-permute-done.2.refs_2_, ...), custom_call_target="tpu_custom_call" | custom-call | flops 7864320 | bytes 2097152 | tf_op jit(solution)/shard_map/gradient_pieces/pallas_call | solution.py:609
  46.1 0.0 collective-permute-done.5.refs_5_.refs_1_
  46.1 10.0 %collective-permute-done.6.refs_6_.refs_2_ = bf16[528,128]{1,0:T(8,128)(2,1)S(1)} collective-permute-done((bf16[528,128]{1,0:T(8,128)(2,1)S(1)}, bf16[528,128]{1,0:T(8,128)(2,1)S(1)}, u32[]{:S(2)}, u32[]{:S(2)}) %collective-permute-start.6) | collective-permute-done | bytes 135200 | tf_op jit(solution)/shard_map/ppermute | solution.py:778
  56.1 3.2 %collective-permute-done.7.refs_7_.refs_3_ = bf16[528,128]{1,0:T(8,128)(2,1)S(1)} collective-permute-done((bf16[528,128]{1,0:T(8,128)(2,1)S(1)}, bf16[528,128]{1,0:T(8,128)(2,1)S(1)}, u32[]{:S(2)}, u32[]{:S(2)}) %collective-permute-start.7) | collective-permute-done | bytes 135200 | tf_op jit(solution)/shard_map/ppermute | solution.py:778
  59.3 0.1 collective-permute-start.8
  59.4 1.7 %gram_pieces.1 = f32[16,16,128]{2,1,0:T(8,128)S(1)} custom-call(bf16[8,672,128]{2,1,0:T(8,128)(2,1)S(1)} %all-to-all-done.refs_0_.near_ref, bf16[528,128]{1,0:T(8,128)(2,1)S(1)} %collective-permute-done.refs_0_, bf16[528,128]{1,0:T(8,128)(2,1)S(1)} %collective-permute-done.1.refs_1_, bf16[528,128]{1,0:T(8,128)(2,1)S(1)} %collective-permute-done.2.refs_2_, ...), custom_call_target="tpu_custom_call" | custom-call | flops 536870912 | bytes 2097152 | tf_op jit(solution)/shard_map/gram_pieces/pallas_call | solution.py:536
  61.2 0.0 copy-start
  61.2 0.6 copy-done
  61.8 6.5 %all-to-all-start.1 = ((f32[16,16,128]{2,1,0:T(8,128)}), f32[16,16,128]{2,1,0:T(8,128)S(1)}, u32[]{:S(2)}, u32[]{:S(2)}) async-start(f32[16,16,128]{2,1,0:T(8,128)} %copy-done), calls=%async_computation.1 | async-start | bytes 262144 | tf_op jit(solution)/shard_map/all_to_all | solution.py:365
  68.4 2.4 %gradient_pieces.7 = (bf16[4,512,128]{2,1,0:T(8,128)(2,1)}, f32[8,128]{1,0:T(8,128)}) custom-call(bf16[528,128]{1,0:T(8,128)(2,1)S(1)} %collective-permute-done.4.refs_4_.refs_0_, bf16[528,128]{1,0:T(8,128)(2,1)S(1)} %collective-permute-done.5.refs_5_.refs_1_, bf16[528,128]{1,0:T(8,128)(2,1)S(1)} %collective-permute-done.6.refs_6_.refs_2_, ...), custom_call_target="tpu_custom_call" | custom-call | flops 7864320 | bytes 2097152 | tf_op jit(solution)/shard_map/gradient_pieces/pallas_call | solution.py:609
  70.8 2.9 %collective-permute-done.8.refs_1_.refs_8_ = bf16[8,144,128]{2,1,0:T(8,128)(2,1)S(1)} collective-permute-done((bf16[8,144,128]{2,1,0:T(8,128)(2,1)S(1)}, bf16[8,144,128]{2,1,0:T(8,128)(2,1)S(1)}, u32[]{:S(2)}, u32[]{:S(2)}) %collective-permute-start.8) | collective-permute-done | bytes 294944 | tf_op jit(solution)/shard_map/ppermute | solution.py:778
  73.7 2.2 %gradient_pieces.6 = (bf16[16,128,128]{2,1,0:T(8,128)(2,1)}, f32[8,128]{1,0:T(8,128)}) custom-call(bf16[8,672,128]{2,1,0:T(8,128)(2,1)S(1)} %all-to-all-done.refs_0_.near_ref, bf16[8,144,128]{2,1,0:T(8,128)(2,1)S(1)} %collective-permute-done.8.refs_1_.refs_8_, bf16[128,128]{1,0:T(8,128)(2,1)S(1)} %get-tuple-element.47.refs_2_, ...), custom_call_target="tpu_custom_call" | custom-call | flops 7864320 | bytes 2097152 | tf_op jit(solution)/shard_map/gradient_pieces/pallas_call | solution.py:609
  75.9 1.4 %all-to-all-done.1.refs_10_ = f32[16,16,128]{2,1,0:T(8,128)S(1)} async-done(((f32[16,16,128]{2,1,0:T(8,128)}), f32[16,16,128]{2,1,0:T(8,128)S(1)}, u32[]{:S(2)}, u32[]{:S(2)}) %all-to-all-start.1) | async-done | bytes 131104 | tf_op jit(solution)/shard_map/all_to_all | solution.py:365
  77.3 5.2 %update_pieces.1 = (bf16[8,640,128]{2,1,0:T(8,128)(2,1)}, bf16[384,128]{1,0:T(8,128)(2,1)}, bf16[384,128]{1,0:T(8,128)(2,1)}, bf16[384,128]{1,0:T(8,128)(2,1)}, ...) custom-call(bf16[8,672,128]{2,1,0:T(8,128)(2,1)S(1)} %all-to-all-don, ...), custom_call_target="tpu_custom_call" | custom-call | flops 1073741824 | bytes 6291456 | tf_op jit(solution)/shard_map/update_pieces/pallas_call | solution.py:756
  82.5 6.4 %all-to-all-start.2 = ((bf16[8,640,128]{2,1,0:T(8,128)(2,1)}), bf16[8,640,128]{2,1,0:T(8,128)(2,1)S(1)}, u32[]{:S(2)}, u32[]{:S(2)}) async-start(bf16[8,640,128]{2,1,0:T(8,128)(2,1)} %get-tuple-element.52), calls=%async_computation.2 | async-start | bytes 2621440 | tf_op jit(solution)/shard_map/all_to_all | solution.py:783
  89.0 0.0 collective-permute-start.9
  89.0 2.9 %collective-permute-start.10 = (bf16[384,128]{1,0:T(8,128)(2,1)S(1)}, bf16[384,128]{1,0:T(8,128)(2,1)S(1)}, u32[]{:S(2)}, u32[]{:S(2)}) collective-permute-start(bf16[384,128]{1,0:T(8,128)(2,1)S(1)} %copy-done.7), channel_id=1, source_target_pairs={{0,9},{1,8},{2,11},{3,10},{4,13},{5,12},{6,15},{7,14},{8,1},{9,0},... | collective-permute-start | bytes 294920 | tf_op jit(solution)/shard_map/ppermute | solution.py:778
  91.8 0.7 collective-permute-start.11
  92.6 2.6 %collective-permute-start.12 = (bf16[384,128]{1,0:T(8,128)(2,1)S(1)}, bf16[384,128]{1,0:T(8,128)(2,1)S(1)}, u32[]{:S(2)}, u32[]{:S(2)}) collective-permute-start(bf16[384,128]{1,0:T(8,128)(2,1)S(1)} %copy-done.5), channel_id=1, source_target_pairs={{0,11},{1,10},{2,9},{3,8},{4,15},{5,14},{6,13},{7,12},{8,3},{9,2},... | collective-permute-start | bytes 294920 | tf_op jit(solution)/shard_map/ppermute | solution.py:778
  95.2 0.0 collective-permute-start.13
  95.2 10.7 %collective-permute-done.9.refs_1_ = bf16[384,128]{1,0:T(8,128)(2,1)S(1)} collective-permute-done((bf16[384,128]{1,0:T(8,128)(2,1)S(1)}, bf16[384,128]{1,0:T(8,128)(2,1)S(1)}, u32[]{:S(2)}, u32[]{:S(2)}) %collective-permute-start.9) | collective-permute-done | bytes 98336 | tf_op jit(solution)/shard_map/ppermute | solution.py:778
  105.9 2.5 %collective-permute-start.14 = (bf16[384,128]{1,0:T(8,128)(2,1)S(1)}, bf16[384,128]{1,0:T(8,128)(2,1)S(1)}, u32[]{:S(2)}, u32[]{:S(2)}) collective-permute-start(bf16[384,128]{1,0:T(8,128)(2,1)S(1)} %copy-done.3), channel_id=1, source_target_pairs={{0,13},{1,12},{2,15},{3,14},{4,9},{5,8},{6,11},{7,10},{8,5},{9,4},... | collective-permute-start | bytes 294920 | tf_op jit(solution)/shard_map/ppermute | solution.py:778
  108.4 0.3 collective-permute-done.10.refs_2_
  108.6 2.8 %collective-permute-start.15 = (bf16[384,128]{1,0:T(8,128)(2,1)S(1)}, bf16[384,128]{1,0:T(8,128)(2,1)S(1)}, u32[]{:S(2)}, u32[]{:S(2)}) collective-permute-start(bf16[384,128]{1,0:T(8,128)(2,1)S(1)} %copy-done.2), channel_id=1, source_target_pairs={{0,14},{1,15},{2,12},{3,13},{4,10},{5,11},{6,8},{7,9},{8,6},{9,7},... | collective-permute-start | bytes 294920 | tf_op jit(solution)/shard_map/ppermute | solution.py:778
  111.5 0.0 collective-permute-done.11.refs_3_
  111.5 2.1 %collective-permute-start.16 = (bf16[384,128]{1,0:T(8,128)(2,1)S(1)}, bf16[384,128]{1,0:T(8,128)(2,1)S(1)}, u32[]{:S(2)}, u32[]{:S(2)}) collective-permute-start(bf16[384,128]{1,0:T(8,128)(2,1)S(1)} %copy-done.1), channel_id=1, source_target_pairs={{0,15},{1,14},{2,13},{3,12},{4,11},{5,10},{6,9},{7,8},{8,7},{9,6},... | collective-permute-start | bytes 294920 | tf_op jit(solution)/shard_map/ppermute | solution.py:778
  113.6 0.0 all-to-all-done.2.refs_0_
  113.6 3.0 %join_pieces.4.refs_0_ = bf16[1,1048576]{1,0:T(2,128)(2,1)} custom-call(bf16[8,640,128]{2,1,0:T(8,128)(2,1)S(1)} %all-to-all-done.2.refs_0_), custom_call_target="tpu_custom_call" | custom-call | bytes 3932160 | tf_op jit(solution)/shard_map/join_pieces/pallas_call | solution.py:482
  116.6 1.0 join_pieces.5.refs_0_
  117.5 5.7 %collective-permute-done.14.refs_2_ = bf16[384,128]{1,0:T(8,128)(2,1)S(1)} collective-permute-done((bf16[384,128]{1,0:T(8,128)(2,1)S(1)}, bf16[384,128]{1,0:T(8,128)(2,1)S(1)}, u32[]{:S(2)}, u32[]{:S(2)}) %collective-permute-start.14) | collective-permute-done | bytes 98336 | tf_op jit(solution)/shard_map/ppermute | solution.py:778
  123.2 0.8 join_pieces.6.refs_0_
  124.0 2.2 %collective-permute-done.15.refs_1_ = bf16[384,128]{1,0:T(8,128)(2,1)S(1)} collective-permute-done((bf16[384,128]{1,0:T(8,128)(2,1)S(1)}, bf16[384,128]{1,0:T(8,128)(2,1)S(1)}, u32[]{:S(2)}, u32[]{:S(2)}) %collective-permute-start.15) | collective-permute-done | bytes 98336 | tf_op jit(solution)/shard_map/ppermute | solution.py:778
  126.2 2.1 %collective-permute-done.16.refs_2_ = bf16[384,128]{1,0:T(8,128)(2,1)S(1)} collective-permute-done((bf16[384,128]{1,0:T(8,128)(2,1)S(1)}, bf16[384,128]{1,0:T(8,128)(2,1)S(1)}, u32[]{:S(2)}, u32[]{:S(2)}) %collective-permute-start.16) | collective-permute-done | bytes 98336 | tf_op jit(solution)/shard_map/ppermute | solution.py:778
  128.3 0.8 join_pieces.7
  (23 shorter events, 0.1 us)
Async XLA Ops:
  3.8 31.3 %all-to-all-start = ((bf16[8,672,128]{2,1,0:T(8,128)(2,1)}), bf16[8,672,128]{2,1,0:T(8,128)(2,1)S(1)}, u32[]{:S(2)}, u32[]{:S(2)}) async-start(bf16[8,672,128]{2,1,0:T(8,128)(2,1)} %get-tuple-element.33), calls=%async_computation | async-start | bytes 2752512 | tf_op jit(solution)/shard_map/all_to_all | solution.py:783
  8.3 29.3 %collective-permute-start = (bf16[528,128]{1,0:T(8,128)(2,1)S(1)}, bf16[528,128]{1,0:T(8,128)(2,1)S(1)}, u32[]{:S(2)}, u32[]{:S(2)}) collective-permute-start(bf16[528,128]{1,0:T(8,128)(2,1)S(1)} %get-tuple-element.34), channel_id=1, source_target_pairs={{0,8},{1,9},{2,10},{3,11},{4,12},{5,13},{6,14},{7,15},{8,0},{9,1},... | collective-permute-start | bytes 405512 | tf_op jit(solution)/shard_map/ppermute | solution.py:778
  10.6 29.2 %collective-permute-start.1 = (bf16[528,128]{1,0:T(8,128)(2,1)S(1)}, bf16[528,128]{1,0:T(8,128)(2,1)S(1)}, u32[]{:S(2)}, u32[]{:S(2)}) collective-permute-start(bf16[528,128]{1,0:T(8,128)(2,1)S(1)} %get-tuple-element.35), channel_id=1, source_target_pairs={{0,9},{1,8},{2,11},{3,10},{4,13},{5,12},{6,15},{7,14},{8,1},{9,0},... | collective-permute-start | bytes 405512 | tf_op jit(solution)/shard_map/ppermute | solution.py:778
  11.2 29.6 %collective-permute-start.2 = (bf16[528,128]{1,0:T(8,128)(2,1)S(1)}, bf16[528,128]{1,0:T(8,128)(2,1)S(1)}, u32[]{:S(2)}, u32[]{:S(2)}) collective-permute-start(bf16[528,128]{1,0:T(8,128)(2,1)S(1)} %get-tuple-element.36), channel_id=1, source_target_pairs={{0,10},{1,11},{2,8},{3,9},{4,14},{5,15},{6,12},{7,13},{8,2},{9,3},... | collective-permute-start | bytes 405512 | tf_op jit(solution)/shard_map/ppermute | solution.py:778
  14.4 29.8 %collective-permute-start.3 = (bf16[528,128]{1,0:T(8,128)(2,1)S(1)}, bf16[528,128]{1,0:T(8,128)(2,1)S(1)}, u32[]{:S(2)}, u32[]{:S(2)}) collective-permute-start(bf16[528,128]{1,0:T(8,128)(2,1)S(1)} %get-tuple-element.37), channel_id=1, source_target_pairs={{0,11},{1,10},{2,9},{3,8},{4,15},{5,14},{6,13},{7,12},{8,3},{9,2},... | collective-permute-start | bytes 405512 | tf_op jit(solution)/shard_map/ppermute | solution.py:778
  14.7 31.3 %collective-permute-start.4 = (bf16[528,128]{1,0:T(8,128)(2,1)S(1)}, bf16[528,128]{1,0:T(8,128)(2,1)S(1)}, u32[]{:S(2)}, u32[]{:S(2)}) collective-permute-start(bf16[528,128]{1,0:T(8,128)(2,1)S(1)} %get-tuple-element.38), channel_id=1, source_target_pairs={{0,12},{1,13},{2,14},{3,15},{4,8},{5,9},{6,10},{7,11},{8,4},{9,5},... | collective-permute-start | bytes 405512 | tf_op jit(solution)/shard_map/ppermute | solution.py:778
  37.6 8.4 %collective-permute-start.5 = (bf16[528,128]{1,0:T(8,128)(2,1)S(1)}, bf16[528,128]{1,0:T(8,128)(2,1)S(1)}, u32[]{:S(2)}, u32[]{:S(2)}) collective-permute-start(bf16[528,128]{1,0:T(8,128)(2,1)S(1)} %get-tuple-element.39), channel_id=1, source_target_pairs={{0,13},{1,12},{2,15},{3,14},{4,9},{5,8},{6,11},{7,10},{8,5},{9,4},... | collective-permute-start | bytes 405512 | tf_op jit(solution)/shard_map/ppermute | solution.py:778
  39.9 16.2 %collective-permute-start.6 = (bf16[528,128]{1,0:T(8,128)(2,1)S(1)}, bf16[528,128]{1,0:T(8,128)(2,1)S(1)}, u32[]{:S(2)}, u32[]{:S(2)}) collective-permute-start(bf16[528,128]{1,0:T(8,128)(2,1)S(1)} %get-tuple-element.40), channel_id=1, source_target_pairs={{0,14},{1,15},{2,12},{3,13},{4,10},{5,11},{6,8},{7,9},{8,6},{9,7},... | collective-permute-start | bytes 405512 | tf_op jit(solution)/shard_map/ppermute | solution.py:778
  40.8 18.5 %collective-permute-start.7 = (bf16[528,128]{1,0:T(8,128)(2,1)S(1)}, bf16[528,128]{1,0:T(8,128)(2,1)S(1)}, u32[]{:S(2)}, u32[]{:S(2)}) collective-permute-start(bf16[528,128]{1,0:T(8,128)(2,1)S(1)} %copy_after.1), channel_id=1, source_target_pairs={{0,15},{1,14},{2,13},{3,12},{4,11},{5,10},{6,9},{7,8},{8,7},{9,6},... | collective-permute-start | bytes 405512 | tf_op jit(solution)/shard_map/ppermute | solution.py:778
  59.3 14.3 %collective-permute-start.8 = (bf16[8,144,128]{2,1,0:T(8,128)(2,1)S(1)}, bf16[8,144,128]{2,1,0:T(8,128)(2,1)S(1)}, u32[]{:S(2)}, u32[]{:S(2)}) collective-permute-start(bf16[8,144,128]{2,1,0:T(8,128)(2,1)S(1)} %raw_states.1.refs_9_), channel_id=1, source_target_pairs={{0,8},{1,9},{2,10},{3,11},{4,12},{5,13},{6,14},{7,15},{8,0},{9,1},... | collective-permute-start | bytes 884744 | tf_op jit(solution)/shard_map/ppermute | solution.py:778
  61.2 0.7 copy-start
  61.8 15.4 %all-to-all-start.1 = ((f32[16,16,128]{2,1,0:T(8,128)}), f32[16,16,128]{2,1,0:T(8,128)S(1)}, u32[]{:S(2)}, u32[]{:S(2)}) async-start(f32[16,16,128]{2,1,0:T(8,128)} %copy-done), calls=%async_computation.1 | async-start | bytes 262144 | tf_op jit(solution)/shard_map/all_to_all | solution.py:365
  82.5 6.5 %copy-start.8 = (bf16[384,128]{1,0:T(8,128)(2,1)S(1)}, bf16[384,128]{1,0:T(8,128)(2,1)}, u32[]{:S(2)}) copy-start(bf16[384,128]{1,0:T(8,128)(2,1)} %get-tuple-element.53) | copy-start | bytes 294916
  82.5 6.5 %copy-start.7 = (bf16[384,128]{1,0:T(8,128)(2,1)S(1)}, bf16[384,128]{1,0:T(8,128)(2,1)}, u32[]{:S(2)}) copy-start(bf16[384,128]{1,0:T(8,128)(2,1)} %get-tuple-element.54) | copy-start | bytes 294916
  82.5 9.4 %copy-start.6 = (bf16[384,128]{1,0:T(8,128)(2,1)S(1)}, bf16[384,128]{1,0:T(8,128)(2,1)}, u32[]{:S(2)}) copy-start(bf16[384,128]{1,0:T(8,128)(2,1)} %get-tuple-element.55) | copy-start | bytes 294916
  82.5 10.1 %copy-start.5 = (bf16[384,128]{1,0:T(8,128)(2,1)S(1)}, bf16[384,128]{1,0:T(8,128)(2,1)}, u32[]{:S(2)}) copy-start(bf16[384,128]{1,0:T(8,128)(2,1)} %get-tuple-element.56) | copy-start | bytes 294916
  82.5 12.7 %copy-start.4 = (bf16[384,128]{1,0:T(8,128)(2,1)S(1)}, bf16[384,128]{1,0:T(8,128)(2,1)}, u32[]{:S(2)}) copy-start(bf16[384,128]{1,0:T(8,128)(2,1)} %get-tuple-element.57) | copy-start | bytes 294916
  82.5 23.4 %copy-start.3 = (bf16[384,128]{1,0:T(8,128)(2,1)S(1)}, bf16[384,128]{1,0:T(8,128)(2,1)}, u32[]{:S(2)}) copy-start(bf16[384,128]{1,0:T(8,128)(2,1)} %get-tuple-element.58) | copy-start | bytes 294916
  82.5 26.1 %copy-start.2 = (bf16[384,128]{1,0:T(8,128)(2,1)S(1)}, bf16[384,128]{1,0:T(8,128)(2,1)}, u32[]{:S(2)}) copy-start(bf16[384,128]{1,0:T(8,128)(2,1)} %get-tuple-element.59) | copy-start | bytes 294916
  82.5 29.0 %copy-start.1 = (bf16[384,128]{1,0:T(8,128)(2,1)S(1)}, bf16[384,128]{1,0:T(8,128)(2,1)}, u32[]{:S(2)}) copy-start(bf16[384,128]{1,0:T(8,128)(2,1)} %get-tuple-element.60) | copy-start | bytes 294916
  82.5 31.0 %all-to-all-start.2 = ((bf16[8,640,128]{2,1,0:T(8,128)(2,1)}), bf16[8,640,128]{2,1,0:T(8,128)(2,1)S(1)}, u32[]{:S(2)}, u32[]{:S(2)}) async-start(bf16[8,640,128]{2,1,0:T(8,128)(2,1)} %get-tuple-element.52), calls=%async_computation.2 | async-start | bytes 2621440 | tf_op jit(solution)/shard_map/all_to_all | solution.py:783
  89.0 16.9 %collective-permute-start.9 = (bf16[384,128]{1,0:T(8,128)(2,1)S(1)}, bf16[384,128]{1,0:T(8,128)(2,1)S(1)}, u32[]{:S(2)}, u32[]{:S(2)}) collective-permute-start(bf16[384,128]{1,0:T(8,128)(2,1)S(1)} %copy-done.8), channel_id=1, source_target_pairs={{0,8},{1,9},{2,10},{3,11},{4,12},{5,13},{6,14},{7,15},{8,0},{9,1},... | collective-permute-start | bytes 294920 | tf_op jit(solution)/shard_map/ppermute | solution.py:778
  89.0 19.7 %collective-permute-start.10 = (bf16[384,128]{1,0:T(8,128)(2,1)S(1)}, bf16[384,128]{1,0:T(8,128)(2,1)S(1)}, u32[]{:S(2)}, u32[]{:S(2)}) collective-permute-start(bf16[384,128]{1,0:T(8,128)(2,1)S(1)} %copy-done.7), channel_id=1, source_target_pairs={{0,9},{1,8},{2,11},{3,10},{4,13},{5,12},{6,15},{7,14},{8,1},{9,0},... | collective-permute-start | bytes 294920 | tf_op jit(solution)/shard_map/ppermute | solution.py:778
  91.8 19.6 %collective-permute-start.11 = (bf16[384,128]{1,0:T(8,128)(2,1)S(1)}, bf16[384,128]{1,0:T(8,128)(2,1)S(1)}, u32[]{:S(2)}, u32[]{:S(2)}) collective-permute-start(bf16[384,128]{1,0:T(8,128)(2,1)S(1)} %copy-done.6), channel_id=1, source_target_pairs={{0,10},{1,11},{2,8},{3,9},{4,14},{5,15},{6,12},{7,13},{8,2},{9,3},... | collective-permute-start | bytes 294920 | tf_op jit(solution)/shard_map/ppermute | solution.py:778
  92.6 24.0 %collective-permute-start.12 = (bf16[384,128]{1,0:T(8,128)(2,1)S(1)}, bf16[384,128]{1,0:T(8,128)(2,1)S(1)}, u32[]{:S(2)}, u32[]{:S(2)}) collective-permute-start(bf16[384,128]{1,0:T(8,128)(2,1)S(1)} %copy-done.5), channel_id=1, source_target_pairs={{0,11},{1,10},{2,9},{3,8},{4,15},{5,14},{6,13},{7,12},{8,3},{9,2},... | collective-permute-start | bytes 294920 | tf_op jit(solution)/shard_map/ppermute | solution.py:778
  95.2 22.4 %collective-permute-start.13 = (bf16[384,128]{1,0:T(8,128)(2,1)S(1)}, bf16[384,128]{1,0:T(8,128)(2,1)S(1)}, u32[]{:S(2)}, u32[]{:S(2)}) collective-permute-start(bf16[384,128]{1,0:T(8,128)(2,1)S(1)} %copy-done.4), channel_id=1, source_target_pairs={{0,12},{1,13},{2,14},{3,15},{4,8},{5,9},{6,10},{7,11},{8,4},{9,5},... | collective-permute-start | bytes 294920 | tf_op jit(solution)/shard_map/ppermute | solution.py:778
  105.9 17.3 %collective-permute-start.14 = (bf16[384,128]{1,0:T(8,128)(2,1)S(1)}, bf16[384,128]{1,0:T(8,128)(2,1)S(1)}, u32[]{:S(2)}, u32[]{:S(2)}) collective-permute-start(bf16[384,128]{1,0:T(8,128)(2,1)S(1)} %copy-done.3), channel_id=1, source_target_pairs={{0,13},{1,12},{2,15},{3,14},{4,9},{5,8},{6,11},{7,10},{8,5},{9,4},... | collective-permute-start | bytes 294920 | tf_op jit(solution)/shard_map/ppermute | solution.py:778
  108.6 17.5 %collective-permute-start.15 = (bf16[384,128]{1,0:T(8,128)(2,1)S(1)}, bf16[384,128]{1,0:T(8,128)(2,1)S(1)}, u32[]{:S(2)}, u32[]{:S(2)}) collective-permute-start(bf16[384,128]{1,0:T(8,128)(2,1)S(1)} %copy-done.2), channel_id=1, source_target_pairs={{0,14},{1,15},{2,12},{3,13},{4,10},{5,11},{6,8},{7,9},{8,6},{9,7},... | collective-permute-start | bytes 294920 | tf_op jit(solution)/shard_map/ppermute | solution.py:778
  111.5 16.8 %collective-permute-start.16 = (bf16[384,128]{1,0:T(8,128)(2,1)S(1)}, bf16[384,128]{1,0:T(8,128)(2,1)S(1)}, u32[]{:S(2)}, u32[]{:S(2)}) collective-permute-start(bf16[384,128]{1,0:T(8,128)(2,1)S(1)} %copy-done.1), channel_id=1, source_target_pairs={{0,15},{1,14},{2,13},{3,12},{4,11},{5,10},{6,9},{7,8},{8,7},{9,6},... | collective-permute-start | bytes 294920 | tf_op jit(solution)/shard_map/ppermute | solution.py:778

commit v22 on v20

--- a/solution.py
+++ b/solution.py
@@ -638,13 +638,11 @@
 def update_pieces_body(half, raw, lines, groups, near_ref, *refs):
     total = 2 * half
     far_refs, refs = refs[:half], refs[half:]
-    across_ref, numbers_ref, grams_ref, raw_grads_ref, *refs = refs
+    across_ref, raw_observed, raw_precision, numbers_ref, grams_ref, *refs = refs
     group_refs, near_to, far_tos = refs[: len(groups)], refs[len(groups)], refs[len(groups) + 1 : -8]
     near_out, far_out, mixer, own, grads, raw_grads, sems, out_sems = refs[-8:]
     wide = total * TILE
     high = half * TILE
-    raw_fetch = pltpu.make_async_copy(raw_grads_ref, raw_grads, sems.at[len(groups), 0])
-    raw_fetch.start()
     middle = (raw + 2 * lines) // 3 // BLOCK * BLOCK
     parts = ((0, raw), (raw, middle), (middle, lines))
     fetches = []
@@ -655,6 +653,20 @@
             target = grads.at[pl.ds(group[0], len(group)), part, :]
             fetches[n].append(pltpu.make_async_copy(group_ref.at[:, part, :], target, sems.at[g, n]))
             fetches[n][-1].start()
+
+    def raw_gradient(i, carry):
+        for k in range(total):
+
+            def load(start, size):
+                if k < half:
+                    return near_ref[k, lines_of(lines + TILE + start, size), :]
+                return across_ref[k - half, lines_of(start, size), :]
+
+            part = lines_of(i * BLOCK, BLOCK)
+            raw_grads[k, part, :] = block_gradient(load, i, raw, raw_observed, raw_precision)
+        return carry
+
+    lax.fori_loop(0, raw // BLOCK, raw_gradient, 0)
     gram = jnp.sum(grams_ref[...], axis=0)[:, :total]
     spread, anneal, step_size = (numbers_ref[k : k + 1, :1] for k in range(3))
     rate = step_size / total
@@ -718,7 +730,6 @@
             near_out[:, lines_of(lines + at, TILE), :] = new.reshape(half, TILE, LANES)
         return carry
 
-    raw_fetch.wait()
     lax.fori_loop(0, raw // BLOCK, raw_step, 0)
     store_near(lines, lines + raw, 0)
     for n, (first, last) in enumerate(parts):
@@ -732,7 +743,7 @@
         copy.wait()
 
 
-def update_pieces(numbers, grams, near, far, across, raw_grads, grads, groups, raw, lines):
+def update_pieces(numbers, grams, near, far, across, raw_fields, grads, groups, raw, lines):
     half = len(far)
     total = 2 * half
     wide = total * TILE
@@ -743,7 +754,7 @@
         "update_pieces",
         flops=4 * wide * wide * LANES * (lines // TILE),
         moved=6 * total * lines * LANES,
-        in_specs=[IN_VMEM] * (half + 4) + [IN_HBM] * (1 + len(groups)),
+        in_specs=[IN_VMEM] * (half + 6) + [IN_HBM] * len(groups),
         out_specs=[IN_HBM] * len(out_shape),
         out_shape=out_shape,
         scratch_shapes=[
@@ -753,10 +764,10 @@
             pltpu.VMEM((wide, LANES), F32),
             pltpu.VMEM((total, lines, LANES), BF16),
             pltpu.VMEM((total, raw, LANES), BF16),
-            pltpu.SemaphoreType.DMA((len(groups) + 1, 3)),
+            pltpu.SemaphoreType.DMA((len(groups), 3)),
             pltpu.SemaphoreType.DMA((half + 1, 4)),
         ],
-    )(near, *far, across, numbers, grams, raw_grads, *grads)
+    )(near, *far, across, *raw_fields, numbers, grams, *grads)
 
 
 def exchange(piece, k, slabs):
@@ -795,10 +806,8 @@
         grads.append(in_hbm(slopes))
         numbers = numbers if len(grads) > 1 else rows
     grams = swap(gram_pieces(near, far, lines, grads[:1], [raw_near]))
-    views = [(0, k, lines + TILE) for k in range(half)] + [(1, k, 0) for k in range(half)]
-    raw_grads, _ = gradient_pieces([near, across], tuple(views), *raw_fields, [])
     new_near, *new_far = update_pieces(
-        numbers, grams, near, far, across, in_hbm(raw_grads), grads, GRADIENTS, RAW, lines
+        numbers, grams, near, far, across, raw_fields, grads, GRADIENTS, RAW, lines
     )
     new_near = swap_near(new_near, slabs)
     new_far = [exchange(piece, half + x, slabs) for x, piece in enumerate(new_far)]

time: 130 us -> 129 us (level)
  waiting for transfers between devices: 63.6 us -> 69.1 us
  starting transfers between devices: 37 us -> 33 us
    ppermute x17, waiting for transfers between devices: 62.4 us -> 65.6 us  [exchange(): return lax.ppermute(piece, 'slab', [(i, i ^ k) for i in range(slabs)])]
    ppermute x17, starting transfers between devices: 20.4 us -> 17.9 us  [exchange(): return lax.ppermute(piece, 'slab', [(i, i ^ k) for i in range(slabs)])]
    all_to_all x1, waiting for transfers between devices: 1.16 us -> 3.59 us  [swap(): lax.all_to_all(slabs, 'slab', split_axis=0, concat_axis=0, tiled=True)]
    pallas_call x4 -> x3, Pallas kernels: 9.57 us -> 7.36 us  [gradient_pieces(): call(functools.partial(gradient_pieces_body, views, len(arrays), len(numb...]
    all_to_all x2, starting transfers between devices: 10.9 us -> 9.36 us  [swap_near(): lax.all_to_all(pieces, 'slab', 0, 0, axis_index_groups=groups, tiled=True)]
  transfers between devices with their start and end apart: 20 -> 20, of which waited for: 15 -> 15; matrix products, arithmetic and copies ran while one was open for 0% -> 0% of each run, Pallas kernels for 12% -> 11%
where the time goes in v22:
time: 129 us
  waiting for transfers between devices  69.1 us (54%)
  starting transfers between devices  33 us (26%)
  Pallas kernels  24.6 us (19%)
  between operations  2.13 us (2%)
    ppermute x17, waiting for transfers between devices, exchange(): return lax.ppermute(piece, 'slab', [(i, i ^ k) for i in range(slabs)])  65.6 us
    ppermute x17, starting transfers between devices, exchange(): return lax.ppermute(piece, 'slab', [(i, i ^ k) for i in range(slabs)])  17.9 us
    all_to_all x2, starting transfers between devices, swap_near(): lax.all_to_all(pieces, 'slab', 0, 0, axis_index_groups=groups, tiled=True)  9.36 us
    pallas_call x3, Pallas kernels, gradient_pieces(): call(functools.partial(gradient_pieces_body, views, len(arrays), len(numb...  7.36 us
    all_to_all x1, starting transfers between devices, swap(): lax.all_to_all(slabs, 'slab', split_axis=0, concat_axis=0, tiled=True)  5.75 us
    pallas_call x4, Pallas kernels, join_pieces(): call(functools.partial(join_pieces_body, pieces, slabs // 2, raw, NCELL /...  5.54 us
    pallas_call x1, Pallas kernels, update_pieces(): call(functools.partial(update_pieces_body, half, raw, lines, groups), 'up...  5.51 us
    pallas_call x1, Pallas kernels, split_pieces(): call(functools.partial(split_pieces_body, slabs, raw, lines, len(fields))...  3.75 us
  transfers between devices with their start and end apart: 20, of which 15 were waited for; matrix products, arithmetic and copies ran while one was open for 0% of the time, Pallas kernels for 11%

profile of v22, /device:TPU:9, one launch (start us, length us, event | category | flops | bytes accessed | tf_op | source)
XLA Modules:
  0.0 128.9 jit_solution(14277389378235380528)
XLA Ops:
  0.0 3.7 %split_pieces.1 = (bf16[8,672,128]{2,1,0:T(8,128)(2,1)}, bf16[528,128]{1,0:T(8,128)(2,1)S(1)}, bf16[528,128]{1,0:T(8,128)(2,1)S(1)}, bf16[528,128]{1,0:T(8,128)(...) custom-call(bf16[1,1048576]{1,0:T(2,128)(2,1)} %row_ref.1, ...), custom_call_target="tpu_custom_call" | custom-call | bytes 7372800 | tf_op jit(solution)/shard_map/split_pieces/pallas_call | solution.py:431
  3.8 4.6 %all-to-all-start = ((bf16[8,672,128]{2,1,0:T(8,128)(2,1)}), bf16[8,672,128]{2,1,0:T(8,128)(2,1)S(1)}, u32[]{:S(2)}, u32[]{:S(2)}) async-start(bf16[8,672,128]{2,1,0:T(8,128)(2,1)} %get-tuple-element.31), calls=%async_computation | async-start | bytes 2752512 | tf_op jit(solution)/shard_map/all_to_all | solution.py:779
  8.3 2.3 %collective-permute-start = (bf16[528,128]{1,0:T(8,128)(2,1)S(1)}, bf16[528,128]{1,0:T(8,128)(2,1)S(1)}, u32[]{:S(2)}, u32[]{:S(2)}) collective-permute-start(bf16[528,128]{1,0:T(8,128)(2,1)S(1)} %get-tuple-element.32), channel_id=1, source_target_pairs={{0,8},{1,9},{2,10},{3,11},{4,12},{5,13},{6,14},{7,15},{8,0},{9,1},... | collective-permute-start | bytes 405512 | tf_op jit(solution)/shard_map/ppermute | solution.py:774
  10.6 0.6 collective-permute-start.1
  11.2 3.2 %collective-permute-start.2 = (bf16[528,128]{1,0:T(8,128)(2,1)S(1)}, bf16[528,128]{1,0:T(8,128)(2,1)S(1)}, u32[]{:S(2)}, u32[]{:S(2)}) collective-permute-start(bf16[528,128]{1,0:T(8,128)(2,1)S(1)} %get-tuple-element.34), channel_id=1, source_target_pairs={{0,10},{1,11},{2,8},{3,9},{4,14},{5,15},{6,12},{7,13},{8,2},{9,3},... | collective-permute-start | bytes 405512 | tf_op jit(solution)/shard_map/ppermute | solution.py:774
  14.4 0.3 collective-permute-start.3
  14.7 1.0 collective-permute-start.4
  15.7 13.5 %collective-permute-done.refs_0_ = bf16[528,128]{1,0:T(8,128)(2,1)S(1)} collective-permute-done((bf16[528,128]{1,0:T(8,128)(2,1)S(1)}, bf16[528,128]{1,0:T(8,128)(2,1)S(1)}, u32[]{:S(2)}, u32[]{:S(2)}) %collective-permute-start) | collective-permute-done | bytes 135200 | tf_op jit(solution)/shard_map/ppermute | solution.py:774
  29.3 0.0 collective-permute-start.5
  29.3 3.6 %collective-permute-done.1.refs_1_ = bf16[528,128]{1,0:T(8,128)(2,1)S(1)} collective-permute-done((bf16[528,128]{1,0:T(8,128)(2,1)S(1)}, bf16[528,128]{1,0:T(8,128)(2,1)S(1)}, u32[]{:S(2)}, u32[]{:S(2)}) %collective-permute-start.1) | collective-permute-done | bytes 135200 | tf_op jit(solution)/shard_map/ppermute | solution.py:774
  32.9 0.3 collective-permute-start.6
  33.2 2.8 %collective-permute-done.2.refs_2_ = bf16[528,128]{1,0:T(8,128)(2,1)S(1)} collective-permute-done((bf16[528,128]{1,0:T(8,128)(2,1)S(1)}, bf16[528,128]{1,0:T(8,128)(2,1)S(1)}, u32[]{:S(2)}, u32[]{:S(2)}) %collective-permute-start.2) | collective-permute-done | bytes 135200 | tf_op jit(solution)/shard_map/ppermute | solution.py:774
  36.0 0.0 collective-permute-start.7
  37.9 1.7 %collective-permute-done.3.refs_3_ = bf16[528,128]{1,0:T(8,128)(2,1)S(1)} collective-permute-done((bf16[528,128]{1,0:T(8,128)(2,1)S(1)}, bf16[528,128]{1,0:T(8,128)(2,1)S(1)}, u32[]{:S(2)}, u32[]{:S(2)}) %collective-permute-start.3) | collective-permute-done | bytes 135200 | tf_op jit(solution)/shard_map/ppermute | solution.py:774
  39.6 1.8 %gradient_pieces.3 = (bf16[4,512,128]{2,1,0:T(8,128)(2,1)}, f32[8,128]{1,0:T(8,128)S(1)}) custom-call(bf16[528,128]{1,0:T(8,128)(2,1)S(1)} %collective-permute-done.refs_0_, bf16[528,128]{1,0:T(8,128)(2,1)S(1)} %collective-permute-done.1.refs_1_, bf16[528,128]{1,0:T(8,128)(2,1)S(1)} %collective-permute-done.2.refs_2_, ...), custom_call_target="tpu_custom_call" | custom-call | flops 7864320 | bytes 2097152 | tf_op jit(solution)/shard_map/gradient_pieces/pallas_call | solution.py:594
  41.4 6.7 %collective-permute-done.4.refs_4_.refs_0_ = bf16[528,128]{1,0:T(8,128)(2,1)S(1)} collective-permute-done((bf16[528,128]{1,0:T(8,128)(2,1)S(1)}, bf16[528,128]{1,0:T(8,128)(2,1)S(1)}, u32[]{:S(2)}, u32[]{:S(2)}) %collective-permute-start.4) | collective-permute-done | bytes 135200 | tf_op jit(solution)/shard_map/ppermute | solution.py:774
  48.1 4.7 %collective-permute-done.5.refs_5_.refs_1_ = bf16[528,128]{1,0:T(8,128)(2,1)S(1)} collective-permute-done((bf16[528,128]{1,0:T(8,128)(2,1)S(1)}, bf16[528,128]{1,0:T(8,128)(2,1)S(1)}, u32[]{:S(2)}, u32[]{:S(2)}) %collective-permute-start.5) | collective-permute-done | bytes 135200 | tf_op jit(solution)/shard_map/ppermute | solution.py:774
  52.9 3.8 %collective-permute-done.6.refs_6_.refs_2_ = bf16[528,128]{1,0:T(8,128)(2,1)S(1)} collective-permute-done((bf16[528,128]{1,0:T(8,128)(2,1)S(1)}, bf16[528,128]{1,0:T(8,128)(2,1)S(1)}, u32[]{:S(2)}, u32[]{:S(2)}) %collective-permute-start.6) | collective-permute-done | bytes 135200 | tf_op jit(solution)/shard_map/ppermute | solution.py:774
  56.7 2.9 %collective-permute-done.7.refs_7_.refs_3_ = bf16[528,128]{1,0:T(8,128)(2,1)S(1)} collective-permute-done((bf16[528,128]{1,0:T(8,128)(2,1)S(1)}, bf16[528,128]{1,0:T(8,128)(2,1)S(1)}, u32[]{:S(2)}, u32[]{:S(2)}) %collective-permute-start.7) | collective-permute-done | bytes 135200 | tf_op jit(solution)/shard_map/ppermute | solution.py:774
  59.5 0.0 all-to-all-done.near_ref.refs_0_
  59.6 0.1 collective-permute-start.8
  59.7 2.4 %gram_pieces.1 = f32[16,16,128]{2,1,0:T(8,128)} custom-call(bf16[8,672,128]{2,1,0:T(8,128)(2,1)S(1)} %all-to-all-done.near_ref.refs_0_, bf16[528,128]{1,0:T(8,128)(2,1)S(1)} %collective-permute-done.refs_0_, bf16[528,128]{1,0:T(8,128)(2,1)S(1)} %collective-permute-done.1.refs_1_, bf16[528,128]{1,0:T(8,128)(2,1)S(1)} %collective-permute-done.2.refs_2_, ...), custom_call_target="tpu_custom_call" | custom-call | flops 536870912 | bytes 2097152 | tf_op jit(solution)/shard_map/gram_pieces/pallas_call | solution.py:521
  62.1 5.7 %all-to-all-start.1 = ((f32[16,16,128]{2,1,0:T(8,128)}), f32[16,16,128]{2,1,0:T(8,128)S(1)}, u32[]{:S(2)}, u32[]{:S(2)}) async-start(f32[16,16,128]{2,1,0:T(8,128)} %gram_pieces.1), calls=%async_computation.1 | async-start | bytes 262144 | tf_op jit(solution)/shard_map/all_to_all | solution.py:365
  67.8 2.4 %gradient_pieces.4 = (bf16[4,512,128]{2,1,0:T(8,128)(2,1)}, f32[8,128]{1,0:T(8,128)}) custom-call(bf16[528,128]{1,0:T(8,128)(2,1)S(1)} %collective-permute-done.4.refs_4_.refs_0_, bf16[528,128]{1,0:T(8,128)(2,1)S(1)} %collective-permute-done.5.refs_5_.refs_1_, bf16[528,128]{1,0:T(8,128)(2,1)S(1)} %collective-permute-done.6.refs_6_.refs_2_, ...), custom_call_target="tpu_custom_call" | custom-call | flops 7864320 | bytes 2097152 | tf_op jit(solution)/shard_map/gradient_pieces/pallas_call | solution.py:594
  70.2 3.2 %gradient_pieces.5 = (bf16[8,512,128]{2,1,0:T(8,128)(2,1)}, f32[8,128]{1,0:T(8,128)}) custom-call(bf16[8,672,128]{2,1,0:T(8,128)(2,1)S(1)} %all-to-all-done.near_ref.refs_0_, bf16[512,128]{1,0:T(8,128)(2,1)S(1)} %get-tuple-element.42.refs_4_.refs_1_, bf16[512,128]{1,0:T(8,128)(2,1)S(1)} %get-tuple-element.43.refs_5_.refs_2_), custom_call_target="tpu_custom_call" | custom-call | flops 15728640 | bytes 4194304 | tf_op jit(solution)/shard_map/gradient_pieces/pallas_call | solution.py:594
  73.4 3.6 %all-to-all-done.1.refs_12_ = f32[16,16,128]{2,1,0:T(8,128)S(1)} async-done(((f32[16,16,128]{2,1,0:T(8,128)}), f32[16,16,128]{2,1,0:T(8,128)S(1)}, u32[]{:S(2)}, u32[]{:S(2)}) %all-to-all-start.1) | async-done | bytes 131104 | tf_op jit(solution)/shard_map/all_to_all | solution.py:365
  77.0 0.0 collective-permute-done.8.refs_8_
  77.0 5.5 %update_pieces.1 = (bf16[8,640,128]{2,1,0:T(8,128)(2,1)}, bf16[384,128]{1,0:T(8,128)(2,1)}, bf16[384,128]{1,0:T(8,128)(2,1)}, bf16[384,128]{1,0:T(8,128)(2,1)}, ...) custom-call(bf16[8,672,128]{2,1,0:T(8,128)(2,1)S(1)} %all-to-all-don, ...), custom_call_target="tpu_custom_call" | custom-call | flops 1073741824 | bytes 6291456 | tf_op jit(solution)/shard_map/update_pieces/pallas_call | solution.py:752
  82.6 4.8 %all-to-all-start.2 = ((bf16[8,640,128]{2,1,0:T(8,128)(2,1)}), bf16[8,640,128]{2,1,0:T(8,128)(2,1)S(1)}, u32[]{:S(2)}, u32[]{:S(2)}) async-start(bf16[8,640,128]{2,1,0:T(8,128)(2,1)} %get-tuple-element.48), calls=%async_computation.2 | async-start | bytes 2621440 | tf_op jit(solution)/shard_map/all_to_all | solution.py:779
  87.4 1.2 collective-permute-start.9
  88.5 1.7 %collective-permute-start.10 = (bf16[384,128]{1,0:T(8,128)(2,1)S(1)}, bf16[384,128]{1,0:T(8,128)(2,1)S(1)}, u32[]{:S(2)}, u32[]{:S(2)}) collective-permute-start(bf16[384,128]{1,0:T(8,128)(2,1)S(1)} %copy-done.6), channel_id=1, source_target_pairs={{0,9},{1,8},{2,11},{3,10},{4,13},{5,12},{6,15},{7,14},{8,1},{9,0},... | collective-permute-start | bytes 294920 | tf_op jit(solution)/shard_map/ppermute | solution.py:774
  90.3 2.1 %collective-permute-start.11 = (bf16[384,128]{1,0:T(8,128)(2,1)S(1)}, bf16[384,128]{1,0:T(8,128)(2,1)S(1)}, u32[]{:S(2)}, u32[]{:S(2)}) collective-permute-start(bf16[384,128]{1,0:T(8,128)(2,1)S(1)} %copy-done.5), channel_id=1, source_target_pairs={{0,10},{1,11},{2,8},{3,9},{4,14},{5,15},{6,12},{7,13},{8,2},{9,3},... | collective-permute-start | bytes 294920 | tf_op jit(solution)/shard_map/ppermute | solution.py:774
  92.4 1.2 collective-permute-start.12
  93.6 0.0 collective-permute-start.13
  93.6 12.0 %collective-permute-done.9.refs_1_ = bf16[384,128]{1,0:T(8,128)(2,1)S(1)} collective-permute-done((bf16[384,128]{1,0:T(8,128)(2,1)S(1)}, bf16[384,128]{1,0:T(8,128)(2,1)S(1)}, u32[]{:S(2)}, u32[]{:S(2)}) %collective-permute-start.9) | collective-permute-done | bytes 98336 | tf_op jit(solution)/shard_map/ppermute | solution.py:774
  105.7 1.1 collective-permute-start.14
  106.8 1.6 %collective-permute-done.10.refs_2_ = bf16[384,128]{1,0:T(8,128)(2,1)S(1)} collective-permute-done((bf16[384,128]{1,0:T(8,128)(2,1)S(1)}, bf16[384,128]{1,0:T(8,128)(2,1)S(1)}, u32[]{:S(2)}, u32[]{:S(2)}) %collective-permute-start.10) | collective-permute-done | bytes 98336 | tf_op jit(solution)/shard_map/ppermute | solution.py:774
  108.4 1.5 %collective-permute-start.15 = (bf16[384,128]{1,0:T(8,128)(2,1)S(1)}, bf16[384,128]{1,0:T(8,128)(2,1)S(1)}, u32[]{:S(2)}, u32[]{:S(2)}) collective-permute-start(bf16[384,128]{1,0:T(8,128)(2,1)S(1)} %copy-done.1), channel_id=1, source_target_pairs={{0,14},{1,15},{2,12},{3,13},{4,10},{5,11},{6,8},{7,9},{8,6},{9,7},... | collective-permute-start | bytes 294920 | tf_op jit(solution)/shard_map/ppermute | solution.py:774
  109.9 0.9 collective-permute-done.11.refs_3_
  110.8 1.2 collective-permute-start.16
  112.0 0.0 all-to-all-done.2.refs_0_
  112.0 3.0 %join_pieces.4.refs_0_ = bf16[1,1048576]{1,0:T(2,128)(2,1)} custom-call(bf16[8,640,128]{2,1,0:T(8,128)(2,1)S(1)} %all-to-all-done.2.refs_0_), custom_call_target="tpu_custom_call" | custom-call | bytes 3932160 | tf_op jit(solution)/shard_map/join_pieces/pallas_call | solution.py:467
  115.0 1.0 join_pieces.5.refs_0_
  116.0 7.0 %collective-permute-done.14.refs_2_ = bf16[384,128]{1,0:T(8,128)(2,1)S(1)} collective-permute-done((bf16[384,128]{1,0:T(8,128)(2,1)S(1)}, bf16[384,128]{1,0:T(8,128)(2,1)S(1)}, u32[]{:S(2)}, u32[]{:S(2)}) %collective-permute-start.14) | collective-permute-done | bytes 98336 | tf_op jit(solution)/shard_map/ppermute | solution.py:774
  122.9 0.8 join_pieces.6.refs_0_
  123.7 2.2 %collective-permute-done.15.refs_1_ = bf16[384,128]{1,0:T(8,128)(2,1)S(1)} collective-permute-done((bf16[384,128]{1,0:T(8,128)(2,1)S(1)}, bf16[384,128]{1,0:T(8,128)(2,1)S(1)}, u32[]{:S(2)}, u32[]{:S(2)}) %collective-permute-start.15) | collective-permute-done | bytes 98336 | tf_op jit(solution)/shard_map/ppermute | solution.py:774
  126.0 2.1 %collective-permute-done.16.refs_2_ = bf16[384,128]{1,0:T(8,128)(2,1)S(1)} collective-permute-done((bf16[384,128]{1,0:T(8,128)(2,1)S(1)}, bf16[384,128]{1,0:T(8,128)(2,1)S(1)}, u32[]{:S(2)}, u32[]{:S(2)}) %collective-permute-start.16) | collective-permute-done | bytes 98336 | tf_op jit(solution)/shard_map/ppermute | solution.py:774
  128.1 0.8 join_pieces.7
  (19 shorter events, 0.1 us)
Async XLA Ops:
  3.8 55.8 %all-to-all-start = ((bf16[8,672,128]{2,1,0:T(8,128)(2,1)}), bf16[8,672,128]{2,1,0:T(8,128)(2,1)S(1)}, u32[]{:S(2)}, u32[]{:S(2)}) async-start(bf16[8,672,128]{2,1,0:T(8,128)(2,1)} %get-tuple-element.31), calls=%async_computation | async-start | bytes 2752512 | tf_op jit(solution)/shard_map/all_to_all | solution.py:779
  8.3 20.9 %collective-permute-start = (bf16[528,128]{1,0:T(8,128)(2,1)S(1)}, bf16[528,128]{1,0:T(8,128)(2,1)S(1)}, u32[]{:S(2)}, u32[]{:S(2)}) collective-permute-start(bf16[528,128]{1,0:T(8,128)(2,1)S(1)} %get-tuple-element.32), channel_id=1, source_target_pairs={{0,8},{1,9},{2,10},{3,11},{4,12},{5,13},{6,14},{7,15},{8,0},{9,1},... | collective-permute-start | bytes 405512 | tf_op jit(solution)/shard_map/ppermute | solution.py:774
  10.6 22.2 %collective-permute-start.1 = (bf16[528,128]{1,0:T(8,128)(2,1)S(1)}, bf16[528,128]{1,0:T(8,128)(2,1)S(1)}, u32[]{:S(2)}, u32[]{:S(2)}) collective-permute-start(bf16[528,128]{1,0:T(8,128)(2,1)S(1)} %get-tuple-element.33), channel_id=1, source_target_pairs={{0,9},{1,8},{2,11},{3,10},{4,13},{5,12},{6,15},{7,14},{8,1},{9,0},... | collective-permute-start | bytes 405512 | tf_op jit(solution)/shard_map/ppermute | solution.py:774
  11.2 24.8 %collective-permute-start.2 = (bf16[528,128]{1,0:T(8,128)(2,1)S(1)}, bf16[528,128]{1,0:T(8,128)(2,1)S(1)}, u32[]{:S(2)}, u32[]{:S(2)}) collective-permute-start(bf16[528,128]{1,0:T(8,128)(2,1)S(1)} %get-tuple-element.34), channel_id=1, source_target_pairs={{0,10},{1,11},{2,8},{3,9},{4,14},{5,15},{6,12},{7,13},{8,2},{9,3},... | collective-permute-start | bytes 405512 | tf_op jit(solution)/shard_map/ppermute | solution.py:774
  14.4 25.2 %collective-permute-start.3 = (bf16[528,128]{1,0:T(8,128)(2,1)S(1)}, bf16[528,128]{1,0:T(8,128)(2,1)S(1)}, u32[]{:S(2)}, u32[]{:S(2)}) collective-permute-start(bf16[528,128]{1,0:T(8,128)(2,1)S(1)} %get-tuple-element.35), channel_id=1, source_target_pairs={{0,11},{1,10},{2,9},{3,8},{4,15},{5,14},{6,13},{7,12},{8,3},{9,2},... | collective-permute-start | bytes 405512 | tf_op jit(solution)/shard_map/ppermute | solution.py:774
  14.7 33.4 %collective-permute-start.4 = (bf16[528,128]{1,0:T(8,128)(2,1)S(1)}, bf16[528,128]{1,0:T(8,128)(2,1)S(1)}, u32[]{:S(2)}, u32[]{:S(2)}) collective-permute-start(bf16[528,128]{1,0:T(8,128)(2,1)S(1)} %get-tuple-element.36), channel_id=1, source_target_pairs={{0,12},{1,13},{2,14},{3,15},{4,8},{5,9},{6,10},{7,11},{8,4},{9,5},... | collective-permute-start | bytes 405512 | tf_op jit(solution)/shard_map/ppermute | solution.py:774
  29.3 23.6 %collective-permute-start.5 = (bf16[528,128]{1,0:T(8,128)(2,1)S(1)}, bf16[528,128]{1,0:T(8,128)(2,1)S(1)}, u32[]{:S(2)}, u32[]{:S(2)}) collective-permute-start(bf16[528,128]{1,0:T(8,128)(2,1)S(1)} %get-tuple-element.37), channel_id=1, source_target_pairs={{0,13},{1,12},{2,15},{3,14},{4,9},{5,8},{6,11},{7,10},{8,5},{9,4},... | collective-permute-start | bytes 405512 | tf_op jit(solution)/shard_map/ppermute | solution.py:774
  32.9 23.8 %collective-permute-start.6 = (bf16[528,128]{1,0:T(8,128)(2,1)S(1)}, bf16[528,128]{1,0:T(8,128)(2,1)S(1)}, u32[]{:S(2)}, u32[]{:S(2)}) collective-permute-start(bf16[528,128]{1,0:T(8,128)(2,1)S(1)} %get-tuple-element.38), channel_id=1, source_target_pairs={{0,14},{1,15},{2,12},{3,13},{4,10},{5,11},{6,8},{7,9},{8,6},{9,7},... | collective-permute-start | bytes 405512 | tf_op jit(solution)/shard_map/ppermute | solution.py:774
  36.0 23.5 %collective-permute-start.7 = (bf16[528,128]{1,0:T(8,128)(2,1)S(1)}, bf16[528,128]{1,0:T(8,128)(2,1)S(1)}, u32[]{:S(2)}, u32[]{:S(2)}) collective-permute-start(bf16[528,128]{1,0:T(8,128)(2,1)S(1)} %get-tuple-element.39), channel_id=1, source_target_pairs={{0,15},{1,14},{2,13},{3,12},{4,11},{5,10},{6,9},{7,8},{8,7},{9,6},... | collective-permute-start | bytes 405512 | tf_op jit(solution)/shard_map/ppermute | solution.py:774
  59.6 17.4 %collective-permute-start.8 = (bf16[8,144,128]{2,1,0:T(8,128)(2,1)S(1)}, bf16[8,144,128]{2,1,0:T(8,128)(2,1)S(1)}, u32[]{:S(2)}, u32[]{:S(2)}) collective-permute-start(bf16[8,144,128]{2,1,0:T(8,128)(2,1)S(1)} %raw_states.1.refs_9_), channel_id=1, source_target_pairs={{0,8},{1,9},{2,10},{3,11},{4,12},{5,13},{6,14},{7,15},{8,0},{9,1},... | collective-permute-start | bytes 884744 | tf_op jit(solution)/shard_map/ppermute | solution.py:774
  62.1 14.9 %all-to-all-start.1 = ((f32[16,16,128]{2,1,0:T(8,128)}), f32[16,16,128]{2,1,0:T(8,128)S(1)}, u32[]{:S(2)}, u32[]{:S(2)}) async-start(f32[16,16,128]{2,1,0:T(8,128)} %gram_pieces.1), calls=%async_computation.1 | async-start | bytes 262144 | tf_op jit(solution)/shard_map/all_to_all | solution.py:365
  82.5 4.9 %copy-start.7 = (bf16[384,128]{1,0:T(8,128)(2,1)S(1)}, bf16[384,128]{1,0:T(8,128)(2,1)}, u32[]{:S(2)}) copy-start(bf16[384,128]{1,0:T(8,128)(2,1)} %get-tuple-element.49) | copy-start | bytes 294916
  82.5 6.0 %copy-start.6 = (bf16[384,128]{1,0:T(8,128)(2,1)S(1)}, bf16[384,128]{1,0:T(8,128)(2,1)}, u32[]{:S(2)}) copy-start(bf16[384,128]{1,0:T(8,128)(2,1)} %get-tuple-element.50) | copy-start | bytes 294916
  82.5 7.7 %copy-start.5 = (bf16[384,128]{1,0:T(8,128)(2,1)S(1)}, bf16[384,128]{1,0:T(8,128)(2,1)}, u32[]{:S(2)}) copy-start(bf16[384,128]{1,0:T(8,128)(2,1)} %get-tuple-element.51) | copy-start | bytes 294916
  82.5 9.8 %copy-start.4 = (bf16[384,128]{1,0:T(8,128)(2,1)S(1)}, bf16[384,128]{1,0:T(8,128)(2,1)}, u32[]{:S(2)}) copy-start(bf16[384,128]{1,0:T(8,128)(2,1)} %get-tuple-element.52) | copy-start | bytes 294916
  82.5 11.0 %copy-start.3 = (bf16[384,128]{1,0:T(8,128)(2,1)S(1)}, bf16[384,128]{1,0:T(8,128)(2,1)}, u32[]{:S(2)}) copy-start(bf16[384,128]{1,0:T(8,128)(2,1)} %get-tuple-element.53) | copy-start | bytes 294916
  82.6 23.1 %copy-start.2 = (bf16[384,128]{1,0:T(8,128)(2,1)S(1)}, bf16[384,128]{1,0:T(8,128)(2,1)}, u32[]{:S(2)}) copy-start(bf16[384,128]{1,0:T(8,128)(2,1)} %get-tuple-element.54) | copy-start | bytes 294916
  82.6 25.9 %copy-start.1 = (bf16[384,128]{1,0:T(8,128)(2,1)S(1)}, bf16[384,128]{1,0:T(8,128)(2,1)}, u32[]{:S(2)}) copy-start(bf16[384,128]{1,0:T(8,128)(2,1)} %get-tuple-element.55) | copy-start | bytes 294916
  82.6 28.2 %copy-start = (bf16[384,128]{1,0:T(8,128)(2,1)S(1)}, bf16[384,128]{1,0:T(8,128)(2,1)}, u32[]{:S(2)}) copy-start(bf16[384,128]{1,0:T(8,128)(2,1)} %get-tuple-element.56) | copy-start | bytes 294916
  82.6 29.4 %all-to-all-start.2 = ((bf16[8,640,128]{2,1,0:T(8,128)(2,1)}), bf16[8,640,128]{2,1,0:T(8,128)(2,1)S(1)}, u32[]{:S(2)}, u32[]{:S(2)}) async-start(bf16[8,640,128]{2,1,0:T(8,128)(2,1)} %get-tuple-element.48), calls=%async_computation.2 | async-start | bytes 2621440 | tf_op jit(solution)/shard_map/all_to_all | solution.py:779
  87.4 18.3 %collective-permute-start.9 = (bf16[384,128]{1,0:T(8,128)(2,1)S(1)}, bf16[384,128]{1,0:T(8,128)(2,1)S(1)}, u32[]{:S(2)}, u32[]{:S(2)}) collective-permute-start(bf16[384,128]{1,0:T(8,128)(2,1)S(1)} %copy-done.7), channel_id=1, source_target_pairs={{0,8},{1,9},{2,10},{3,11},{4,12},{5,13},{6,14},{7,15},{8,0},{9,1},... | collective-permute-start | bytes 294920 | tf_op jit(solution)/shard_map/ppermute | solution.py:774
  88.5 19.9 %collective-permute-start.10 = (bf16[384,128]{1,0:T(8,128)(2,1)S(1)}, bf16[384,128]{1,0:T(8,128)(2,1)S(1)}, u32[]{:S(2)}, u32[]{:S(2)}) collective-permute-start(bf16[384,128]{1,0:T(8,128)(2,1)S(1)} %copy-done.6), channel_id=1, source_target_pairs={{0,9},{1,8},{2,11},{3,10},{4,13},{5,12},{6,15},{7,14},{8,1},{9,0},... | collective-permute-start | bytes 294920 | tf_op jit(solution)/shard_map/ppermute | solution.py:774
  90.3 20.5 %collective-permute-start.11 = (bf16[384,128]{1,0:T(8,128)(2,1)S(1)}, bf16[384,128]{1,0:T(8,128)(2,1)S(1)}, u32[]{:S(2)}, u32[]{:S(2)}) collective-permute-start(bf16[384,128]{1,0:T(8,128)(2,1)S(1)} %copy-done.5), channel_id=1, source_target_pairs={{0,10},{1,11},{2,8},{3,9},{4,14},{5,15},{6,12},{7,13},{8,2},{9,3},... | collective-permute-start | bytes 294920 | tf_op jit(solution)/shard_map/ppermute | solution.py:774
  92.4 22.6 %collective-permute-start.12 = (bf16[384,128]{1,0:T(8,128)(2,1)S(1)}, bf16[384,128]{1,0:T(8,128)(2,1)S(1)}, u32[]{:S(2)}, u32[]{:S(2)}) collective-permute-start(bf16[384,128]{1,0:T(8,128)(2,1)S(1)} %copy-done.4), channel_id=1, source_target_pairs={{0,11},{1,10},{2,9},{3,8},{4,15},{5,14},{6,13},{7,12},{8,3},{9,2},... | collective-permute-start | bytes 294920 | tf_op jit(solution)/shard_map/ppermute | solution.py:774
  93.6 22.4 %collective-permute-start.13 = (bf16[384,128]{1,0:T(8,128)(2,1)S(1)}, bf16[384,128]{1,0:T(8,128)(2,1)S(1)}, u32[]{:S(2)}, u32[]{:S(2)}) collective-permute-start(bf16[384,128]{1,0:T(8,128)(2,1)S(1)} %copy-done.3), channel_id=1, source_target_pairs={{0,12},{1,13},{2,14},{3,15},{4,8},{5,9},{6,10},{7,11},{8,4},{9,5},... | collective-permute-start | bytes 294920 | tf_op jit(solution)/shard_map/ppermute | solution.py:774
  105.7 17.3 %collective-permute-start.14 = (bf16[384,128]{1,0:T(8,128)(2,1)S(1)}, bf16[384,128]{1,0:T(8,128)(2,1)S(1)}, u32[]{:S(2)}, u32[]{:S(2)}) collective-permute-start(bf16[384,128]{1,0:T(8,128)(2,1)S(1)} %copy-done.2), channel_id=1, source_target_pairs={{0,13},{1,12},{2,15},{3,14},{4,9},{5,8},{6,11},{7,10},{8,5},{9,4},... | collective-permute-start | bytes 294920 | tf_op jit(solution)/shard_map/ppermute | solution.py:774
  108.4 17.5 %collective-permute-start.15 = (bf16[384,128]{1,0:T(8,128)(2,1)S(1)}, bf16[384,128]{1,0:T(8,128)(2,1)S(1)}, u32[]{:S(2)}, u32[]{:S(2)}) collective-permute-start(bf16[384,128]{1,0:T(8,128)(2,1)S(1)} %copy-done.1), channel_id=1, source_target_pairs={{0,14},{1,15},{2,12},{3,13},{4,10},{5,11},{6,8},{7,9},{8,6},{9,7},... | collective-permute-start | bytes 294920 | tf_op jit(solution)/shard_map/ppermute | solution.py:774
  110.8 17.3 %collective-permute-start.16 = (bf16[384,128]{1,0:T(8,128)(2,1)S(1)}, bf16[384,128]{1,0:T(8,128)(2,1)S(1)}, u32[]{:S(2)}, u32[]{:S(2)}) collective-permute-start(bf16[384,128]{1,0:T(8,128)(2,1)S(1)} %copy-done), channel_id=1, source_target_pairs={{0,15},{1,14},{2,13},{3,12},{4,11},{5,10},{6,9},{7,8},{8,7},{9,6},... | collective-permute-start | bytes 294920 | tf_op jit(solution)/shard_map/ppermute | solution.py:774

commit v23 on v22

--- a/solution.py
+++ b/solution.py
@@ -793,7 +793,7 @@
     far, (obs, prec, *raw_fields) = far[:half], far[half:]
     near = swap_near(near, slabs)
     far = [exchange(piece, half + x, slabs) for x, piece in enumerate(far)]
-    raw_near = raw_states(near, RAW, lines, far)
+    raw_near = raw_states(near, RAW, lines, far[:-1])
     across = exchange(raw_near, half, slabs)
     grads = []
     numbers = [spread, anneal, step_size]

time: 129 us -> 131 us (1.016)
  starting transfers between devices: 33 us -> 41.3 us
  waiting for transfers between devices: 69.1 us -> 62.7 us
    all_to_all x1, starting transfers between devices: 5.75 us -> 10.8 us  [swap(): lax.all_to_all(slabs, 'slab', split_axis=0, concat_axis=0, tiled=True)]
    all_to_all x1, waiting for transfers between devices: 3.59 us -> 0.3 us  [swap(): lax.all_to_all(slabs, 'slab', split_axis=0, concat_axis=0, tiled=True)]
    ppermute x17, waiting for transfers between devices: 65.6 us -> 62.4 us  [exchange(): return lax.ppermute(piece, 'slab', [(i, i ^ k) for i in range(slabs)])]
    ppermute x17, starting transfers between devices: 17.9 us -> 20.2 us  [exchange(): return lax.ppermute(piece, 'slab', [(i, i ^ k) for i in range(slabs)])]
where the time goes in v23:
time: 131 us
  waiting for transfers between devices  62.7 us (48%)
  starting transfers between devices  41.3 us (32%)
  Pallas kernels  24.6 us (19%)
  between operations  2.13 us (2%)
    ppermute x17, waiting for transfers between devices, exchange(): return lax.ppermute(piece, 'slab', [(i, i ^ k) for i in range(slabs)])  62.4 us
    ppermute x17, starting transfers between devices, exchange(): return lax.ppermute(piece, 'slab', [(i, i ^ k) for i in range(slabs)])  20.2 us
    all_to_all x1, starting transfers between devices, swap(): lax.all_to_all(slabs, 'slab', split_axis=0, concat_axis=0, tiled=True)  10.8 us
    all_to_all x2, starting transfers between devices, swap_near(): lax.all_to_all(pieces, 'slab', 0, 0, axis_index_groups=groups, tiled=True)  10.4 us
    pallas_call x3, Pallas kernels, gradient_pieces(): call(functools.partial(gradient_pieces_body, views, len(arrays), len(numb...  7.36 us
    pallas_call x4, Pallas kernels, join_pieces(): call(functools.partial(join_pieces_body, pieces, slabs // 2, raw, NCELL /...  5.54 us
    pallas_call x1, Pallas kernels, update_pieces(): call(functools.partial(update_pieces_body, half, raw, lines, groups), 'up...  5.51 us
    pallas_call x1, Pallas kernels, split_pieces(): call(functools.partial(split_pieces_body, slabs, raw, lines, len(fields))...  3.76 us
  transfers between devices with their start and end apart: 20, of which 15 were waited for; matrix products, arithmetic and copies ran while one was open for 0% of the time, Pallas kernels for 11%

profile of v23, /device:TPU:9, one launch (start us, length us, event | category | flops | bytes accessed | tf_op | source)
XLA Modules:
  0.0 130.7 jit_solution(12371960060375903999)
XLA Ops:
  0.0 3.8 %split_pieces.1 = (bf16[8,672,128]{2,1,0:T(8,128)(2,1)}, bf16[528,128]{1,0:T(8,128)(2,1)S(1)}, bf16[528,128]{1,0:T(8,128)(2,1)S(1)}, bf16[528,128]{1,0:T(8,128)(...) custom-call(bf16[1,1048576]{1,0:T(2,128)(2,1)} %row_ref.1, ...), custom_call_target="tpu_custom_call" | custom-call | bytes 7372800 | tf_op jit(solution)/shard_map/split_pieces/pallas_call | solution.py:431
  3.8 4.6 %all-to-all-start = ((bf16[8,672,128]{2,1,0:T(8,128)(2,1)}), bf16[8,672,128]{2,1,0:T(8,128)(2,1)S(1)}, u32[]{:S(2)}, u32[]{:S(2)}) async-start(bf16[8,672,128]{2,1,0:T(8,128)(2,1)} %get-tuple-element.31), calls=%async_computation | async-start | bytes 2752512 | tf_op jit(solution)/shard_map/all_to_all | solution.py:779
  8.4 2.3 %collective-permute-start = (bf16[528,128]{1,0:T(8,128)(2,1)S(1)}, bf16[528,128]{1,0:T(8,128)(2,1)S(1)}, u32[]{:S(2)}, u32[]{:S(2)}) collective-permute-start(bf16[528,128]{1,0:T(8,128)(2,1)S(1)} %get-tuple-element.32), channel_id=1, source_target_pairs={{0,8},{1,9},{2,10},{3,11},{4,12},{5,13},{6,14},{7,15},{8,0},{9,1},... | collective-permute-start | bytes 405512 | tf_op jit(solution)/shard_map/ppermute | solution.py:774
  10.7 0.6 collective-permute-start.1
  11.2 3.2 %collective-permute-start.2 = (bf16[528,128]{1,0:T(8,128)(2,1)S(1)}, bf16[528,128]{1,0:T(8,128)(2,1)S(1)}, u32[]{:S(2)}, u32[]{:S(2)}) collective-permute-start(bf16[528,128]{1,0:T(8,128)(2,1)S(1)} %get-tuple-element.34), channel_id=1, source_target_pairs={{0,10},{1,11},{2,8},{3,9},{4,14},{5,15},{6,12},{7,13},{8,2},{9,3},... | collective-permute-start | bytes 405512 | tf_op jit(solution)/shard_map/ppermute | solution.py:774
  14.5 0.3 collective-permute-start.3
  14.7 1.0 collective-permute-start.4
  15.8 13.5 %collective-permute-done.refs_0_ = bf16[528,128]{1,0:T(8,128)(2,1)S(1)} collective-permute-done((bf16[528,128]{1,0:T(8,128)(2,1)S(1)}, bf16[528,128]{1,0:T(8,128)(2,1)S(1)}, u32[]{:S(2)}, u32[]{:S(2)}) %collective-permute-start) | collective-permute-done | bytes 135200 | tf_op jit(solution)/shard_map/ppermute | solution.py:774
  29.3 0.0 collective-permute-start.5
  29.3 3.6 %collective-permute-done.1.refs_1_ = bf16[528,128]{1,0:T(8,128)(2,1)S(1)} collective-permute-done((bf16[528,128]{1,0:T(8,128)(2,1)S(1)}, bf16[528,128]{1,0:T(8,128)(2,1)S(1)}, u32[]{:S(2)}, u32[]{:S(2)}) %collective-permute-start.1) | collective-permute-done | bytes 135200 | tf_op jit(solution)/shard_map/ppermute | solution.py:774
  32.9 0.3 collective-permute-start.6
  33.2 2.8 %collective-permute-done.2.refs_2_ = bf16[528,128]{1,0:T(8,128)(2,1)S(1)} collective-permute-done((bf16[528,128]{1,0:T(8,128)(2,1)S(1)}, bf16[528,128]{1,0:T(8,128)(2,1)S(1)}, u32[]{:S(2)}, u32[]{:S(2)}) %collective-permute-start.2) | collective-permute-done | bytes 135200 | tf_op jit(solution)/shard_map/ppermute | solution.py:774
  36.0 0.0 collective-permute-start.7
  38.0 1.7 %collective-permute-done.3.refs_3_ = bf16[528,128]{1,0:T(8,128)(2,1)S(1)} collective-permute-done((bf16[528,128]{1,0:T(8,128)(2,1)S(1)}, bf16[528,128]{1,0:T(8,128)(2,1)S(1)}, u32[]{:S(2)}, u32[]{:S(2)}) %collective-permute-start.3) | collective-permute-done | bytes 135200 | tf_op jit(solution)/shard_map/ppermute | solution.py:774
  39.6 1.8 %gradient_pieces.3 = (bf16[4,512,128]{2,1,0:T(8,128)(2,1)}, f32[8,128]{1,0:T(8,128)S(1)}) custom-call(bf16[528,128]{1,0:T(8,128)(2,1)S(1)} %collective-permute-done.refs_0_, bf16[528,128]{1,0:T(8,128)(2,1)S(1)} %collective-permute-done.1.refs_1_, bf16[528,128]{1,0:T(8,128)(2,1)S(1)} %collective-permute-done.2.refs_2_, ...), custom_call_target="tpu_custom_call" | custom-call | flops 7864320 | bytes 2097152 | tf_op jit(solution)/shard_map/gradient_pieces/pallas_call | solution.py:594
  41.4 6.7 %collective-permute-done.4.refs_4_.refs_0_ = bf16[528,128]{1,0:T(8,128)(2,1)S(1)} collective-permute-done((bf16[528,128]{1,0:T(8,128)(2,1)S(1)}, bf16[528,128]{1,0:T(8,128)(2,1)S(1)}, u32[]{:S(2)}, u32[]{:S(2)}) %collective-permute-start.4) | collective-permute-done | bytes 135200 | tf_op jit(solution)/shard_map/ppermute | solution.py:774
  48.1 4.7 %collective-permute-done.5.refs_5_.refs_1_ = bf16[528,128]{1,0:T(8,128)(2,1)S(1)} collective-permute-done((bf16[528,128]{1,0:T(8,128)(2,1)S(1)}, bf16[528,128]{1,0:T(8,128)(2,1)S(1)}, u32[]{:S(2)}, u32[]{:S(2)}) %collective-permute-start.5) | collective-permute-done | bytes 135200 | tf_op jit(solution)/shard_map/ppermute | solution.py:774
  52.9 3.8 %collective-permute-done.6.refs_6_.refs_2_ = bf16[528,128]{1,0:T(8,128)(2,1)S(1)} collective-permute-done((bf16[528,128]{1,0:T(8,128)(2,1)S(1)}, bf16[528,128]{1,0:T(8,128)(2,1)S(1)}, u32[]{:S(2)}, u32[]{:S(2)}) %collective-permute-start.6) | collective-permute-done | bytes 135200 | tf_op jit(solution)/shard_map/ppermute | solution.py:774
  56.7 0.0 all-to-all-done.near_ref.refs_0_
  56.7 0.1 collective-permute-start.8
  56.8 2.8 %collective-permute-done.7.refs_7_.refs_3_ = bf16[528,128]{1,0:T(8,128)(2,1)S(1)} collective-permute-done((bf16[528,128]{1,0:T(8,128)(2,1)}, bf16[528,128]{1,0:T(8,128)(2,1)S(1)}, u32[]{:S(2)}, u32[]{:S(2)}) %collective-permute-start.7) | collective-permute-done | bytes 135200 | tf_op jit(solution)/shard_map/ppermute | solution.py:774
  59.6 2.4 %gram_pieces.1 = f32[16,16,128]{2,1,0:T(8,128)} custom-call(bf16[8,672,128]{2,1,0:T(8,128)(2,1)S(1)} %all-to-all-done.near_ref.refs_0_, bf16[528,128]{1,0:T(8,128)(2,1)S(1)} %collective-permute-done.refs_0_, bf16[528,128]{1,0:T(8,128)(2,1)S(1)} %collective-permute-done.1.refs_1_, bf16[528,128]{1,0:T(8,128)(2,1)S(1)} %collective-permute-done.2.refs_2_, ...), custom_call_target="tpu_custom_call" | custom-call | flops 536870912 | bytes 2097152 | tf_op jit(solution)/shard_map/gram_pieces/pallas_call | solution.py:521
  62.0 10.8 %all-to-all-start.1 = ((f32[16,16,128]{2,1,0:T(8,128)}), f32[16,16,128]{2,1,0:T(8,128)S(1)}, u32[]{:S(2)}, u32[]{:S(2)}) async-start(f32[16,16,128]{2,1,0:T(8,128)} %gram_pieces.1), calls=%async_computation.1 | async-start | bytes 262144 | tf_op jit(solution)/shard_map/all_to_all | solution.py:365
  72.7 2.4 %gradient_pieces.4 = (bf16[4,512,128]{2,1,0:T(8,128)(2,1)}, f32[8,128]{1,0:T(8,128)}) custom-call(bf16[528,128]{1,0:T(8,128)(2,1)S(1)} %collective-permute-done.4.refs_4_.refs_0_, bf16[528,128]{1,0:T(8,128)(2,1)S(1)} %collective-permute-done.5.refs_5_.refs_1_, bf16[528,128]{1,0:T(8,128)(2,1)S(1)} %collective-permute-done.6.refs_6_.refs_2_, ...), custom_call_target="tpu_custom_call" | custom-call | flops 7864320 | bytes 2097152 | tf_op jit(solution)/shard_map/gradient_pieces/pallas_call | solution.py:594
  75.1 3.2 %gradient_pieces.5 = (bf16[8,512,128]{2,1,0:T(8,128)(2,1)}, f32[8,128]{1,0:T(8,128)}) custom-call(bf16[8,672,128]{2,1,0:T(8,128)(2,1)S(1)} %all-to-all-done.near_ref.refs_0_, bf16[512,128]{1,0:T(8,128)(2,1)S(1)} %get-tuple-element.42.refs_4_.refs_1_, bf16[512,128]{1,0:T(8,128)(2,1)S(1)} %get-tuple-element.43.refs_5_.refs_2_), custom_call_target="tpu_custom_call" | custom-call | flops 15728640 | bytes 4194304 | tf_op jit(solution)/shard_map/gradient_pieces/pallas_call | solution.py:594
  78.3 0.3 all-to-all-done.1.refs_12_
  78.6 0.0 collective-permute-done.8.refs_8_
  78.6 5.5 %update_pieces.1 = (bf16[8,640,128]{2,1,0:T(8,128)(2,1)}, bf16[384,128]{1,0:T(8,128)(2,1)}, bf16[384,128]{1,0:T(8,128)(2,1)}, bf16[384,128]{1,0:T(8,128)(2,1)}, ...) custom-call(bf16[8,672,128]{2,1,0:T(8,128)(2,1)S(1)} %all-to-all-don, ...), custom_call_target="tpu_custom_call" | custom-call | flops 1073741824 | bytes 6291456 | tf_op jit(solution)/shard_map/update_pieces/pallas_call | solution.py:752
  84.2 5.8 %all-to-all-start.2 = ((bf16[8,640,128]{2,1,0:T(8,128)(2,1)}), bf16[8,640,128]{2,1,0:T(8,128)(2,1)S(1)}, u32[]{:S(2)}, u32[]{:S(2)}) async-start(bf16[8,640,128]{2,1,0:T(8,128)(2,1)} %get-tuple-element.48), calls=%async_computation.2 | async-start | bytes 2621440 | tf_op jit(solution)/shard_map/all_to_all | solution.py:779
  90.0 0.4 collective-permute-start.9
  90.4 2.5 %collective-permute-start.10 = (bf16[384,128]{1,0:T(8,128)(2,1)S(1)}, bf16[384,128]{1,0:T(8,128)(2,1)S(1)}, u32[]{:S(2)}, u32[]{:S(2)}) collective-permute-start(bf16[384,128]{1,0:T(8,128)(2,1)S(1)} %copy-done.6), channel_id=1, source_target_pairs={{0,9},{1,8},{2,11},{3,10},{4,13},{5,12},{6,15},{7,14},{8,1},{9,0},... | collective-permute-start | bytes 294920 | tf_op jit(solution)/shard_map/ppermute | solution.py:774
  92.9 1.3 collective-permute-start.11
  94.2 2.0 %collective-permute-start.12 = (bf16[384,128]{1,0:T(8,128)(2,1)S(1)}, bf16[384,128]{1,0:T(8,128)(2,1)S(1)}, u32[]{:S(2)}, u32[]{:S(2)}) collective-permute-start(bf16[384,128]{1,0:T(8,128)(2,1)S(1)} %copy-done.4), channel_id=1, source_target_pairs={{0,11},{1,10},{2,9},{3,8},{4,15},{5,14},{6,13},{7,12},{8,3},{9,2},... | collective-permute-start | bytes 294920 | tf_op jit(solution)/shard_map/ppermute | solution.py:774
  96.2 11.3 %collective-permute-done.9.refs_1_ = bf16[384,128]{1,0:T(8,128)(2,1)S(1)} collective-permute-done((bf16[384,128]{1,0:T(8,128)(2,1)S(1)}, bf16[384,128]{1,0:T(8,128)(2,1)S(1)}, u32[]{:S(2)}, u32[]{:S(2)}) %collective-permute-start.9) | collective-permute-done | bytes 98336 | tf_op jit(solution)/shard_map/ppermute | solution.py:774
  107.5 1.9 %collective-permute-start.14 = (bf16[384,128]{1,0:T(8,128)(2,1)S(1)}, bf16[384,128]{1,0:T(8,128)(2,1)S(1)}, u32[]{:S(2)}, u32[]{:S(2)}) collective-permute-start(bf16[384,128]{1,0:T(8,128)(2,1)S(1)} %copy-done.2), channel_id=1, source_target_pairs={{0,13},{1,12},{2,15},{3,14},{4,9},{5,8},{6,11},{7,10},{8,5},{9,4},... | collective-permute-start | bytes 294920 | tf_op jit(solution)/shard_map/ppermute | solution.py:774
  109.4 0.9 collective-permute-done.10.refs_2_
  110.3 2.3 %collective-permute-start.15 = (bf16[384,128]{1,0:T(8,128)(2,1)S(1)}, bf16[384,128]{1,0:T(8,128)(2,1)S(1)}, u32[]{:S(2)}, u32[]{:S(2)}) collective-permute-start(bf16[384,128]{1,0:T(8,128)(2,1)S(1)} %copy-done.1), channel_id=1, source_target_pairs={{0,14},{1,15},{2,12},{3,13},{4,10},{5,11},{6,8},{7,9},{8,6},{9,7},... | collective-permute-start | bytes 294920 | tf_op jit(solution)/shard_map/ppermute | solution.py:774
  112.5 0.1 collective-permute-done.11.refs_3_
  112.6 2.0 %collective-permute-start.16 = (bf16[384,128]{1,0:T(8,128)(2,1)S(1)}, bf16[384,128]{1,0:T(8,128)(2,1)S(1)}, u32[]{:S(2)}, u32[]{:S(2)}) collective-permute-start(bf16[384,128]{1,0:T(8,128)(2,1)S(1)} %copy-done), channel_id=1, source_target_pairs={{0,15},{1,14},{2,13},{3,12},{4,11},{5,10},{6,9},{7,8},{8,7},{9,6},... | collective-permute-start | bytes 294920 | tf_op jit(solution)/shard_map/ppermute | solution.py:774
  114.6 0.0 all-to-all-done.2.refs_0_
  114.6 3.0 %join_pieces.4.refs_0_ = bf16[1,1048576]{1,0:T(2,128)(2,1)} custom-call(bf16[8,640,128]{2,1,0:T(8,128)(2,1)S(1)} %all-to-all-done.2.refs_0_), custom_call_target="tpu_custom_call" | custom-call | bytes 3932160 | tf_op jit(solution)/shard_map/join_pieces/pallas_call | solution.py:467
  117.6 0.0 collective-permute-done.12.refs_4_
  117.6 1.0 join_pieces.5.refs_0_
  118.6 6.2 %collective-permute-done.14.refs_2_ = bf16[384,128]{1,0:T(8,128)(2,1)S(1)} collective-permute-done((bf16[384,128]{1,0:T(8,128)(2,1)S(1)}, bf16[384,128]{1,0:T(8,128)(2,1)S(1)}, u32[]{:S(2)}, u32[]{:S(2)}) %collective-permute-start.14) | collective-permute-done | bytes 98336 | tf_op jit(solution)/shard_map/ppermute | solution.py:774
  124.8 0.8 join_pieces.6.refs_0_
  125.6 2.2 %collective-permute-done.15.refs_1_ = bf16[384,128]{1,0:T(8,128)(2,1)S(1)} collective-permute-done((bf16[384,128]{1,0:T(8,128)(2,1)S(1)}, bf16[384,128]{1,0:T(8,128)(2,1)S(1)}, u32[]{:S(2)}, u32[]{:S(2)}) %collective-permute-start.15) | collective-permute-done | bytes 98336 | tf_op jit(solution)/shard_map/ppermute | solution.py:774
  127.8 2.1 %collective-permute-done.16.refs_2_ = bf16[384,128]{1,0:T(8,128)(2,1)S(1)} collective-permute-done((bf16[384,128]{1,0:T(8,128)(2,1)S(1)}, bf16[384,128]{1,0:T(8,128)(2,1)S(1)}, u32[]{:S(2)}, u32[]{:S(2)}) %collective-permute-start.16) | collective-permute-done | bytes 98336 | tf_op jit(solution)/shard_map/ppermute | solution.py:774
  129.9 0.8 join_pieces.7
  (19 shorter events, 0.1 us)
Async XLA Ops:
  3.8 52.9 %all-to-all-start = ((bf16[8,672,128]{2,1,0:T(8,128)(2,1)}), bf16[8,672,128]{2,1,0:T(8,128)(2,1)S(1)}, u32[]{:S(2)}, u32[]{:S(2)}) async-start(bf16[8,672,128]{2,1,0:T(8,128)(2,1)} %get-tuple-element.31), calls=%async_computation | async-start | bytes 2752512 | tf_op jit(solution)/shard_map/all_to_all | solution.py:779
  8.4 20.9 %collective-permute-start = (bf16[528,128]{1,0:T(8,128)(2,1)S(1)}, bf16[528,128]{1,0:T(8,128)(2,1)S(1)}, u32[]{:S(2)}, u32[]{:S(2)}) collective-permute-start(bf16[528,128]{1,0:T(8,128)(2,1)S(1)} %get-tuple-element.32), channel_id=1, source_target_pairs={{0,8},{1,9},{2,10},{3,11},{4,12},{5,13},{6,14},{7,15},{8,0},{9,1},... | collective-permute-start | bytes 405512 | tf_op jit(solution)/shard_map/ppermute | solution.py:774
  10.7 22.2 %collective-permute-start.1 = (bf16[528,128]{1,0:T(8,128)(2,1)S(1)}, bf16[528,128]{1,0:T(8,128)(2,1)S(1)}, u32[]{:S(2)}, u32[]{:S(2)}) collective-permute-start(bf16[528,128]{1,0:T(8,128)(2,1)S(1)} %get-tuple-element.33), channel_id=1, source_target_pairs={{0,9},{1,8},{2,11},{3,10},{4,13},{5,12},{6,15},{7,14},{8,1},{9,0},... | collective-permute-start | bytes 405512 | tf_op jit(solution)/shard_map/ppermute | solution.py:774
  11.2 24.8 %collective-permute-start.2 = (bf16[528,128]{1,0:T(8,128)(2,1)S(1)}, bf16[528,128]{1,0:T(8,128)(2,1)S(1)}, u32[]{:S(2)}, u32[]{:S(2)}) collective-permute-start(bf16[528,128]{1,0:T(8,128)(2,1)S(1)} %get-tuple-element.34), channel_id=1, source_target_pairs={{0,10},{1,11},{2,8},{3,9},{4,14},{5,15},{6,12},{7,13},{8,2},{9,3},... | collective-permute-start | bytes 405512 | tf_op jit(solution)/shard_map/ppermute | solution.py:774
  14.5 25.2 %collective-permute-start.3 = (bf16[528,128]{1,0:T(8,128)(2,1)S(1)}, bf16[528,128]{1,0:T(8,128)(2,1)S(1)}, u32[]{:S(2)}, u32[]{:S(2)}) collective-permute-start(bf16[528,128]{1,0:T(8,128)(2,1)S(1)} %get-tuple-element.35), channel_id=1, source_target_pairs={{0,11},{1,10},{2,9},{3,8},{4,15},{5,14},{6,13},{7,12},{8,3},{9,2},... | collective-permute-start | bytes 405512 | tf_op jit(solution)/shard_map/ppermute | solution.py:774
  14.7 33.4 %collective-permute-start.4 = (bf16[528,128]{1,0:T(8,128)(2,1)S(1)}, bf16[528,128]{1,0:T(8,128)(2,1)S(1)}, u32[]{:S(2)}, u32[]{:S(2)}) collective-permute-start(bf16[528,128]{1,0:T(8,128)(2,1)S(1)} %get-tuple-element.36), channel_id=1, source_target_pairs={{0,12},{1,13},{2,14},{3,15},{4,8},{5,9},{6,10},{7,11},{8,4},{9,5},... | collective-permute-start | bytes 405512 | tf_op jit(solution)/shard_map/ppermute | solution.py:774
  29.3 23.6 %collective-permute-start.5 = (bf16[528,128]{1,0:T(8,128)(2,1)S(1)}, bf16[528,128]{1,0:T(8,128)(2,1)S(1)}, u32[]{:S(2)}, u32[]{:S(2)}) collective-permute-start(bf16[528,128]{1,0:T(8,128)(2,1)S(1)} %get-tuple-element.37), channel_id=1, source_target_pairs={{0,13},{1,12},{2,15},{3,14},{4,9},{5,8},{6,11},{7,10},{8,5},{9,4},... | collective-permute-start | bytes 405512 | tf_op jit(solution)/shard_map/ppermute | solution.py:774
  32.9 23.8 %collective-permute-start.6 = (bf16[528,128]{1,0:T(8,128)(2,1)S(1)}, bf16[528,128]{1,0:T(8,128)(2,1)S(1)}, u32[]{:S(2)}, u32[]{:S(2)}) collective-permute-start(bf16[528,128]{1,0:T(8,128)(2,1)S(1)} %get-tuple-element.38), channel_id=1, source_target_pairs={{0,14},{1,15},{2,12},{3,13},{4,10},{5,11},{6,8},{7,9},{8,6},{9,7},... | collective-permute-start | bytes 405512 | tf_op jit(solution)/shard_map/ppermute | solution.py:774
  36.0 23.5 %collective-permute-start.7 = (bf16[528,128]{1,0:T(8,128)(2,1)}, bf16[528,128]{1,0:T(8,128)(2,1)S(1)}, u32[]{:S(2)}, u32[]{:S(2)}) collective-permute-start(bf16[528,128]{1,0:T(8,128)(2,1)} %get-tuple-element.39), channel_id=1, source_target_pairs={{0,15},{1,14},{2,13},{3,12},{4,11},{5,10},{6,9},{7,8},{8,7},{9,6},... | collective-permute-start | bytes 405512 | tf_op jit(solution)/shard_map/ppermute | solution.py:774
  56.7 21.9 %collective-permute-start.8 = (bf16[8,144,128]{2,1,0:T(8,128)(2,1)S(1)}, bf16[8,144,128]{2,1,0:T(8,128)(2,1)S(1)}, u32[]{:S(2)}, u32[]{:S(2)}) collective-permute-start(bf16[8,144,128]{2,1,0:T(8,128)(2,1)S(1)} %raw_states.1.refs_9_), channel_id=1, source_target_pairs={{0,8},{1,9},{2,10},{3,11},{4,12},{5,13},{6,14},{7,15},{8,0},{9,1},... | collective-permute-start | bytes 884744 | tf_op jit(solution)/shard_map/ppermute | solution.py:774
  62.0 16.6 %all-to-all-start.1 = ((f32[16,16,128]{2,1,0:T(8,128)}), f32[16,16,128]{2,1,0:T(8,128)S(1)}, u32[]{:S(2)}, u32[]{:S(2)}) async-start(f32[16,16,128]{2,1,0:T(8,128)} %gram_pieces.1), calls=%async_computation.1 | async-start | bytes 262144 | tf_op jit(solution)/shard_map/all_to_all | solution.py:365
  84.1 5.9 %copy-start.7 = (bf16[384,128]{1,0:T(8,128)(2,1)S(1)}, bf16[384,128]{1,0:T(8,128)(2,1)}, u32[]{:S(2)}) copy-start(bf16[384,128]{1,0:T(8,128)(2,1)} %get-tuple-element.49) | copy-start | bytes 294916
  84.1 6.2 %copy-start.6 = (bf16[384,128]{1,0:T(8,128)(2,1)S(1)}, bf16[384,128]{1,0:T(8,128)(2,1)}, u32[]{:S(2)}) copy-start(bf16[384,128]{1,0:T(8,128)(2,1)} %get-tuple-element.50) | copy-start | bytes 294916
  84.1 8.7 %copy-start.5 = (bf16[384,128]{1,0:T(8,128)(2,1)S(1)}, bf16[384,128]{1,0:T(8,128)(2,1)}, u32[]{:S(2)}) copy-start(bf16[384,128]{1,0:T(8,128)(2,1)} %get-tuple-element.51) | copy-start | bytes 294916
  84.2 10.0 %copy-start.4 = (bf16[384,128]{1,0:T(8,128)(2,1)S(1)}, bf16[384,128]{1,0:T(8,128)(2,1)}, u32[]{:S(2)}) copy-start(bf16[384,128]{1,0:T(8,128)(2,1)} %get-tuple-element.52) | copy-start | bytes 294916
  84.2 12.0 %copy-start.3 = (bf16[384,128]{1,0:T(8,128)(2,1)S(1)}, bf16[384,128]{1,0:T(8,128)(2,1)}, u32[]{:S(2)}) copy-start(bf16[384,128]{1,0:T(8,128)(2,1)} %get-tuple-element.53) | copy-start | bytes 294916
  84.2 23.3 %copy-start.2 = (bf16[384,128]{1,0:T(8,128)(2,1)S(1)}, bf16[384,128]{1,0:T(8,128)(2,1)}, u32[]{:S(2)}) copy-start(bf16[384,128]{1,0:T(8,128)(2,1)} %get-tuple-element.54) | copy-start | bytes 294916
  84.2 26.1 %copy-start.1 = (bf16[384,128]{1,0:T(8,128)(2,1)S(1)}, bf16[384,128]{1,0:T(8,128)(2,1)}, u32[]{:S(2)}) copy-start(bf16[384,128]{1,0:T(8,128)(2,1)} %get-tuple-element.55) | copy-start | bytes 294916
  84.2 28.4 %copy-start = (bf16[384,128]{1,0:T(8,128)(2,1)S(1)}, bf16[384,128]{1,0:T(8,128)(2,1)}, u32[]{:S(2)}) copy-start(bf16[384,128]{1,0:T(8,128)(2,1)} %get-tuple-element.56) | copy-start | bytes 294916
  84.2 30.4 %all-to-all-start.2 = ((bf16[8,640,128]{2,1,0:T(8,128)(2,1)}), bf16[8,640,128]{2,1,0:T(8,128)(2,1)S(1)}, u32[]{:S(2)}, u32[]{:S(2)}) async-start(bf16[8,640,128]{2,1,0:T(8,128)(2,1)} %get-tuple-element.48), calls=%async_computation.2 | async-start | bytes 2621440 | tf_op jit(solution)/shard_map/all_to_all | solution.py:779
  90.0 17.5 %collective-permute-start.9 = (bf16[384,128]{1,0:T(8,128)(2,1)S(1)}, bf16[384,128]{1,0:T(8,128)(2,1)S(1)}, u32[]{:S(2)}, u32[]{:S(2)}) collective-permute-start(bf16[384,128]{1,0:T(8,128)(2,1)S(1)} %copy-done.7), channel_id=1, source_target_pairs={{0,8},{1,9},{2,10},{3,11},{4,12},{5,13},{6,14},{7,15},{8,0},{9,1},... | collective-permute-start | bytes 294920 | tf_op jit(solution)/shard_map/ppermute | solution.py:774
  90.4 19.9 %collective-permute-start.10 = (bf16[384,128]{1,0:T(8,128)(2,1)S(1)}, bf16[384,128]{1,0:T(8,128)(2,1)S(1)}, u32[]{:S(2)}, u32[]{:S(2)}) collective-permute-start(bf16[384,128]{1,0:T(8,128)(2,1)S(1)} %copy-done.6), channel_id=1, source_target_pairs={{0,9},{1,8},{2,11},{3,10},{4,13},{5,12},{6,15},{7,14},{8,1},{9,0},... | collective-permute-start | bytes 294920 | tf_op jit(solution)/shard_map/ppermute | solution.py:774
  92.9 19.7 %collective-permute-start.11 = (bf16[384,128]{1,0:T(8,128)(2,1)S(1)}, bf16[384,128]{1,0:T(8,128)(2,1)S(1)}, u32[]{:S(2)}, u32[]{:S(2)}) collective-permute-start(bf16[384,128]{1,0:T(8,128)(2,1)S(1)} %copy-done.5), channel_id=1, source_target_pairs={{0,10},{1,11},{2,8},{3,9},{4,14},{5,15},{6,12},{7,13},{8,2},{9,3},... | collective-permute-start | bytes 294920 | tf_op jit(solution)/shard_map/ppermute | solution.py:774
  94.2 23.4 %collective-permute-start.12 = (bf16[384,128]{1,0:T(8,128)(2,1)S(1)}, bf16[384,128]{1,0:T(8,128)(2,1)S(1)}, u32[]{:S(2)}, u32[]{:S(2)}) collective-permute-start(bf16[384,128]{1,0:T(8,128)(2,1)S(1)} %copy-done.4), channel_id=1, source_target_pairs={{0,11},{1,10},{2,9},{3,8},{4,15},{5,14},{6,13},{7,12},{8,3},{9,2},... | collective-permute-start | bytes 294920 | tf_op jit(solution)/shard_map/ppermute | solution.py:774
  96.2 22.4 %collective-permute-start.13 = (bf16[384,128]{1,0:T(8,128)(2,1)S(1)}, bf16[384,128]{1,0:T(8,128)(2,1)S(1)}, u32[]{:S(2)}, u32[]{:S(2)}) collective-permute-start(bf16[384,128]{1,0:T(8,128)(2,1)S(1)} %copy-done.3), channel_id=1, source_target_pairs={{0,12},{1,13},{2,14},{3,15},{4,8},{5,9},{6,10},{7,11},{8,4},{9,5},... | collective-permute-start | bytes 294920 | tf_op jit(solution)/shard_map/ppermute | solution.py:774
  107.5 17.3 %collective-permute-start.14 = (bf16[384,128]{1,0:T(8,128)(2,1)S(1)}, bf16[384,128]{1,0:T(8,128)(2,1)S(1)}, u32[]{:S(2)}, u32[]{:S(2)}) collective-permute-start(bf16[384,128]{1,0:T(8,128)(2,1)S(1)} %copy-done.2), channel_id=1, source_target_pairs={{0,13},{1,12},{2,15},{3,14},{4,9},{5,8},{6,11},{7,10},{8,5},{9,4},... | collective-permute-start | bytes 294920 | tf_op jit(solution)/shard_map/ppermute | solution.py:774
  110.3 17.6 %collective-permute-start.15 = (bf16[384,128]{1,0:T(8,128)(2,1)S(1)}, bf16[384,128]{1,0:T(8,128)(2,1)S(1)}, u32[]{:S(2)}, u32[]{:S(2)}) collective-permute-start(bf16[384,128]{1,0:T(8,128)(2,1)S(1)} %copy-done.1), channel_id=1, source_target_pairs={{0,14},{1,15},{2,12},{3,13},{4,10},{5,11},{6,8},{7,9},{8,6},{9,7},... | collective-permute-start | bytes 294920 | tf_op jit(solution)/shard_map/ppermute | solution.py:774
  112.6 17.3 %collective-permute-start.16 = (bf16[384,128]{1,0:T(8,128)(2,1)S(1)}, bf16[384,128]{1,0:T(8,128)(2,1)S(1)}, u32[]{:S(2)}, u32[]{:S(2)}) collective-permute-start(bf16[384,128]{1,0:T(8,128)(2,1)S(1)} %copy-done), channel_id=1, source_target_pairs={{0,15},{1,14},{2,13},{3,12},{4,11},{5,10},{6,9},{7,8},{8,7},{9,6},... | collective-permute-start | bytes 294920 | tf_op jit(solution)/shard_map/ppermute | solution.py:774

commit v24 on v22

--- a/solution.py
+++ b/solution.py
@@ -154,7 +154,7 @@
     wide = total * TILE
     row = lax.broadcasted_iota(jnp.int32, (wide, wide), 0)
     col = lax.broadcasted_iota(jnp.int32, (wide, wide), 1)
-    return row % TILE == col % TILE
+    return (row ^ col) & (TILE - 1) == 0
 
 
 def members(total, dtype):
@@ -638,13 +638,15 @@
 def update_pieces_body(half, raw, lines, groups, near_ref, *refs):
     total = 2 * half
     far_refs, refs = refs[:half], refs[half:]
-    across_ref, raw_observed, raw_precision, numbers_ref, grams_ref, *refs = refs
+    across_ref, raw_observed, raw_precision, numbers_ref, grams_ref, raw_grads_ref, *refs = refs
     group_refs, near_to, far_tos = refs[: len(groups)], refs[len(groups)], refs[len(groups) + 1 : -8]
     near_out, far_out, mixer, own, grads, raw_grads, sems, out_sems = refs[-8:]
     wide = total * TILE
     high = half * TILE
+    raw_fetch = pltpu.make_async_copy(raw_grads_ref, raw_grads.at[pl.ds(0, half), :, :], sems.at[len(groups), 0])
+    raw_fetch.start()
     middle = (raw + 2 * lines) // 3 // BLOCK * BLOCK
-    parts = ((0, raw), (raw, middle), (middle, lines))
+    parts = ((0, raw), (raw, middle), (middle, lines - BLOCK), (lines - BLOCK, lines))
     fetches = []
     for n, (first, last) in enumerate(parts):
         part = pl.ds(first, last - first)
@@ -655,15 +657,13 @@
             fetches[n][-1].start()
 
     def raw_gradient(i, carry):
-        for k in range(total):
+        for k in range(half):
 
             def load(start, size):
-                if k < half:
-                    return near_ref[k, lines_of(lines + TILE + start, size), :]
-                return across_ref[k - half, lines_of(start, size), :]
+                return across_ref[k, lines_of(start, size), :]
 
             part = lines_of(i * BLOCK, BLOCK)
-            raw_grads[k, part, :] = block_gradient(load, i, raw, raw_observed, raw_precision)
+            raw_grads[half + k, part, :] = block_gradient(load, i, raw, raw_observed, raw_precision)
         return carry
 
     lax.fori_loop(0, raw // BLOCK, raw_gradient, 0)
@@ -730,6 +730,7 @@
             near_out[:, lines_of(lines + at, TILE), :] = new.reshape(half, TILE, LANES)
         return carry
 
+    raw_fetch.wait()
     lax.fori_loop(0, raw // BLOCK, raw_step, 0)
     store_near(lines, lines + raw, 0)
     for n, (first, last) in enumerate(parts):
@@ -743,7 +744,7 @@
         copy.wait()
 
 
-def update_pieces(numbers, grams, near, far, across, raw_fields, grads, groups, raw, lines):
+def update_pieces(numbers, grams, near, far, across, raw_fields, raw_grads, grads, groups, raw, lines):
     half = len(far)
     total = 2 * half
     wide = total * TILE
@@ -754,7 +755,7 @@
         "update_pieces",
         flops=4 * wide * wide * LANES * (lines // TILE),
         moved=6 * total * lines * LANES,
-        in_specs=[IN_VMEM] * (half + 6) + [IN_HBM] * len(groups),
+        in_specs=[IN_VMEM] * (half + 6) + [IN_HBM] * (1 + len(groups)),
         out_specs=[IN_HBM] * len(out_shape),
         out_shape=out_shape,
         scratch_shapes=[
@@ -764,10 +765,10 @@
             pltpu.VMEM((wide, LANES), F32),
             pltpu.VMEM((total, lines, LANES), BF16),
             pltpu.VMEM((total, raw, LANES), BF16),
-            pltpu.SemaphoreType.DMA((len(groups), 3)),
-            pltpu.SemaphoreType.DMA((half + 1, 4)),
+            pltpu.SemaphoreType.DMA((len(groups) + 1, 4)),
+            pltpu.SemaphoreType.DMA((half + 1, 5)),
         ],
-    )(near, *far, across, *raw_fields, numbers, grams, *grads)
+    )(near, *far, across, *raw_fields, numbers, grams, raw_grads, *grads)
 
 
 def exchange(piece, k, slabs):
@@ -806,8 +807,10 @@
         grads.append(in_hbm(slopes))
         numbers = numbers if len(grads) > 1 else rows
     grams = swap(gram_pieces(near, far, lines, grads[:1], [raw_near]))
+    views = tuple((0, k, lines + TILE) for k in range(half))
+    raw_grads = in_hbm(gradient_pieces([near], views, *raw_fields, [])[0])
     new_near, *new_far = update_pieces(
-        numbers, grams, near, far, across, raw_fields, grads, GRADIENTS, RAW, lines
+        numbers, grams, near, far, across, raw_fields, raw_grads, grads, GRADIENTS, RAW, lines
     )
     new_near = swap_near(new_near, slabs)
     new_far = [exchange(piece, half + x, slabs) for x, piece in enumerate(new_far)]

time: 129 us -> 129 us (level)
  waiting for transfers between devices: 69.1 us -> 67.4 us
  Pallas kernels: 24.6 us -> 26 us
    all_to_all x1, waiting for transfers between devices: 3.59 us -> 1.87 us  [swap(): lax.all_to_all(slabs, 'slab', split_axis=0, concat_axis=0, tiled=True)]
    pallas_call x3 -> x4, Pallas kernels: 7.36 us -> 9.06 us  [gradient_pieces(): call(functools.partial(gradient_pieces_body, views, len(arrays), len(numb...]
  transfers between devices with their start and end apart: 20 -> 20, of which waited for: 15 -> 15; matrix products, arithmetic and copies ran while one was open for 0% -> 0% of each run, Pallas kernels for 11% -> 13%
where the time goes in v24:
time: 129 us
  waiting for transfers between devices  67.4 us (52%)
  starting transfers between devices  33 us (26%)
  Pallas kernels  26 us (20%)
  between operations  2.13 us (2%)
    ppermute x17, waiting for transfers between devices, exchange(): return lax.ppermute(piece, 'slab', [(i, i ^ k) for i in range(slabs)])  65.6 us
    ppermute x17, starting transfers between devices, exchange(): return lax.ppermute(piece, 'slab', [(i, i ^ k) for i in range(slabs)])  17.9 us
    all_to_all x2, starting transfers between devices, swap_near(): lax.all_to_all(pieces, 'slab', 0, 0, axis_index_groups=groups, tiled=True)  9.36 us
    pallas_call x4, Pallas kernels, gradient_pieces(): call(functools.partial(gradient_pieces_body, views, len(arrays), len(numb...  9.06 us
    all_to_all x1, starting transfers between devices, swap(): lax.all_to_all(slabs, 'slab', split_axis=0, concat_axis=0, tiled=True)  5.75 us
    pallas_call x4, Pallas kernels, join_pieces(): call(functools.partial(join_pieces_body, pieces, slabs // 2, raw, NCELL /...  5.54 us
    pallas_call x1, Pallas kernels, update_pieces(): call(functools.partial(update_pieces_body, half, raw, lines, groups), 'up...  5.19 us
    pallas_call x1, Pallas kernels, split_pieces(): call(functools.partial(split_pieces_body, slabs, raw, lines, len(fields))...  3.75 us
  transfers between devices with their start and end apart: 20, of which 15 were waited for; matrix products, arithmetic and copies ran while one was open for 0% of the time, Pallas kernels for 13%

profile of v24, /device:TPU:9, one launch (start us, length us, event | category | flops | bytes accessed | tf_op | source)
XLA Modules:
  0.0 128.5 jit_solution(3377019794812399853)
XLA Ops:
  0.0 3.7 %split_pieces.1 = (bf16[8,672,128]{2,1,0:T(8,128)(2,1)}, bf16[528,128]{1,0:T(8,128)(2,1)S(1)}, bf16[528,128]{1,0:T(8,128)(2,1)S(1)}, bf16[528,128]{1,0:T(8,128)(...) custom-call(bf16[1,1048576]{1,0:T(2,128)(2,1)} %row_ref.1, ...), custom_call_target="tpu_custom_call" | custom-call | bytes 7372800 | tf_op jit(solution)/shard_map/split_pieces/pallas_call | solution.py:431
  3.8 4.6 %all-to-all-start = ((bf16[8,672,128]{2,1,0:T(8,128)(2,1)}), bf16[8,672,128]{2,1,0:T(8,128)(2,1)S(1)}, u32[]{:S(2)}, u32[]{:S(2)}) async-start(bf16[8,672,128]{2,1,0:T(8,128)(2,1)} %get-tuple-element.32), calls=%async_computation | async-start | bytes 2752512 | tf_op jit(solution)/shard_map/all_to_all | solution.py:780
  8.3 2.3 %collective-permute-start = (bf16[528,128]{1,0:T(8,128)(2,1)S(1)}, bf16[528,128]{1,0:T(8,128)(2,1)S(1)}, u32[]{:S(2)}, u32[]{:S(2)}) collective-permute-start(bf16[528,128]{1,0:T(8,128)(2,1)S(1)} %get-tuple-element.33), channel_id=1, source_target_pairs={{0,8},{1,9},{2,10},{3,11},{4,12},{5,13},{6,14},{7,15},{8,0},{9,1},... | collective-permute-start | bytes 405512 | tf_op jit(solution)/shard_map/ppermute | solution.py:775
  10.6 0.6 collective-permute-start.1
  11.2 3.2 %collective-permute-start.2 = (bf16[528,128]{1,0:T(8,128)(2,1)S(1)}, bf16[528,128]{1,0:T(8,128)(2,1)S(1)}, u32[]{:S(2)}, u32[]{:S(2)}) collective-permute-start(bf16[528,128]{1,0:T(8,128)(2,1)S(1)} %get-tuple-element.35), channel_id=1, source_target_pairs={{0,10},{1,11},{2,8},{3,9},{4,14},{5,15},{6,12},{7,13},{8,2},{9,3},... | collective-permute-start | bytes 405512 | tf_op jit(solution)/shard_map/ppermute | solution.py:775
  14.4 0.3 collective-permute-start.3
  14.7 1.0 collective-permute-start.4
  15.7 13.5 %collective-permute-done.refs_0_ = bf16[528,128]{1,0:T(8,128)(2,1)S(1)} collective-permute-done((bf16[528,128]{1,0:T(8,128)(2,1)S(1)}, bf16[528,128]{1,0:T(8,128)(2,1)S(1)}, u32[]{:S(2)}, u32[]{:S(2)}) %collective-permute-start) | collective-permute-done | bytes 135200 | tf_op jit(solution)/shard_map/ppermute | solution.py:775
  29.3 0.0 collective-permute-start.5
  29.3 3.6 %collective-permute-done.1.refs_1_ = bf16[528,128]{1,0:T(8,128)(2,1)S(1)} collective-permute-done((bf16[528,128]{1,0:T(8,128)(2,1)S(1)}, bf16[528,128]{1,0:T(8,128)(2,1)S(1)}, u32[]{:S(2)}, u32[]{:S(2)}) %collective-permute-start.1) | collective-permute-done | bytes 135200 | tf_op jit(solution)/shard_map/ppermute | solution.py:775
  32.9 0.3 collective-permute-start.6
  33.2 2.8 %collective-permute-done.2.refs_2_ = bf16[528,128]{1,0:T(8,128)(2,1)S(1)} collective-permute-done((bf16[528,128]{1,0:T(8,128)(2,1)S(1)}, bf16[528,128]{1,0:T(8,128)(2,1)S(1)}, u32[]{:S(2)}, u32[]{:S(2)}) %collective-permute-start.2) | collective-permute-done | bytes 135200 | tf_op jit(solution)/shard_map/ppermute | solution.py:775
  37.9 1.7 %collective-permute-done.3.refs_3_ = bf16[528,128]{1,0:T(8,128)(2,1)S(1)} collective-permute-done((bf16[528,128]{1,0:T(8,128)(2,1)S(1)}, bf16[528,128]{1,0:T(8,128)(2,1)S(1)}, u32[]{:S(2)}, u32[]{:S(2)}) %collective-permute-start.3) | collective-permute-done | bytes 135200 | tf_op jit(solution)/shard_map/ppermute | solution.py:775
  39.6 1.8 %gradient_pieces.4 = (bf16[4,512,128]{2,1,0:T(8,128)(2,1)}, f32[8,128]{1,0:T(8,128)S(1)}) custom-call(bf16[528,128]{1,0:T(8,128)(2,1)S(1)} %collective-permute-done.refs_0_, bf16[528,128]{1,0:T(8,128)(2,1)S(1)} %collective-permute-done.1.refs_1_, bf16[528,128]{1,0:T(8,128)(2,1)S(1)} %collective-permute-done.2.refs_2_, ...), custom_call_target="tpu_custom_call" | custom-call | flops 7864320 | bytes 2097152 | tf_op jit(solution)/shard_map/gradient_pieces/pallas_call | solution.py:594
  41.4 6.7 %collective-permute-done.4.refs_4_.refs_0_ = bf16[528,128]{1,0:T(8,128)(2,1)S(1)} collective-permute-done((bf16[528,128]{1,0:T(8,128)(2,1)S(1)}, bf16[528,128]{1,0:T(8,128)(2,1)S(1)}, u32[]{:S(2)}, u32[]{:S(2)}) %collective-permute-start.4) | collective-permute-done | bytes 135200 | tf_op jit(solution)/shard_map/ppermute | solution.py:775
  48.1 4.7 %collective-permute-done.5.refs_5_.refs_1_ = bf16[528,128]{1,0:T(8,128)(2,1)S(1)} collective-permute-done((bf16[528,128]{1,0:T(8,128)(2,1)S(1)}, bf16[528,128]{1,0:T(8,128)(2,1)S(1)}, u32[]{:S(2)}, u32[]{:S(2)}) %collective-permute-start.5) | collective-permute-done | bytes 135200 | tf_op jit(solution)/shard_map/ppermute | solution.py:775
  52.9 3.8 %collective-permute-done.6.refs_6_.refs_2_ = bf16[528,128]{1,0:T(8,128)(2,1)S(1)} collective-permute-done((bf16[528,128]{1,0:T(8,128)(2,1)S(1)}, bf16[528,128]{1,0:T(8,128)(2,1)S(1)}, u32[]{:S(2)}, u32[]{:S(2)}) %collective-permute-start.6) | collective-permute-done | bytes 135200 | tf_op jit(solution)/shard_map/ppermute | solution.py:775
  56.7 2.9 %collective-permute-done.7.refs_7_.refs_3_ = bf16[528,128]{1,0:T(8,128)(2,1)S(1)} collective-permute-done((bf16[528,128]{1,0:T(8,128)(2,1)S(1)}, bf16[528,128]{1,0:T(8,128)(2,1)S(1)}, u32[]{:S(2)}, u32[]{:S(2)}) %collective-permute-start.7) | collective-permute-done | bytes 135200 | tf_op jit(solution)/shard_map/ppermute | solution.py:775
  59.6 0.1 collective-permute-start.8
  59.7 2.4 %gram_pieces.1 = f32[16,16,128]{2,1,0:T(8,128)} custom-call(bf16[8,672,128]{2,1,0:T(8,128)(2,1)S(1)} %all-to-all-done.near_ref.refs_0_, bf16[528,128]{1,0:T(8,128)(2,1)S(1)} %collective-permute-done.refs_0_, bf16[528,128]{1,0:T(8,128)(2,1)S(1)} %collective-permute-done.1.refs_1_, bf16[528,128]{1,0:T(8,128)(2,1)S(1)} %collective-permute-done.2.refs_2_, ...), custom_call_target="tpu_custom_call" | custom-call | flops 536870912 | bytes 2097152 | tf_op jit(solution)/shard_map/gram_pieces/pallas_call | solution.py:521
  62.1 5.7 %all-to-all-start.1 = ((f32[16,16,128]{2,1,0:T(8,128)}), f32[16,16,128]{2,1,0:T(8,128)S(1)}, u32[]{:S(2)}, u32[]{:S(2)}) async-start(f32[16,16,128]{2,1,0:T(8,128)} %gram_pieces.1), calls=%async_computation.1 | async-start | bytes 262144 | tf_op jit(solution)/shard_map/all_to_all | solution.py:365
  67.8 2.4 %gradient_pieces.6 = (bf16[4,512,128]{2,1,0:T(8,128)(2,1)}, f32[8,128]{1,0:T(8,128)}) custom-call(bf16[528,128]{1,0:T(8,128)(2,1)S(1)} %collective-permute-done.4.refs_4_.refs_0_, bf16[528,128]{1,0:T(8,128)(2,1)S(1)} %collective-permute-done.5.refs_5_.refs_1_, bf16[528,128]{1,0:T(8,128)(2,1)S(1)} %collective-permute-done.6.refs_6_.refs_2_, ...), custom_call_target="tpu_custom_call" | custom-call | flops 7864320 | bytes 2097152 | tf_op jit(solution)/shard_map/gradient_pieces/pallas_call | solution.py:594
  70.2 1.7 %gradient_pieces.5 = (bf16[8,128,128]{2,1,0:T(8,128)(2,1)}, f32[8,128]{1,0:T(8,128)}) custom-call(bf16[8,672,128]{2,1,0:T(8,128)(2,1)S(1)} %all-to-all-done.near_ref.refs_0_, bf16[128,128]{1,0:T(8,128)(2,1)S(1)} %get-tuple-element.41.refs_1_.refs_9_, bf16[128,128]{1,0:T(8,128)(2,1)S(1)} %get-tuple-element.42.refs_2_.refs_10_), custom_call_target="tpu_custom_call" | custom-call | flops 3932160 | bytes 1048576 | tf_op jit(solution)/shard_map/gradient_pieces/pallas_call | solution.py:594
  72.0 3.2 %gradient_pieces.7 = (bf16[8,512,128]{2,1,0:T(8,128)(2,1)}, f32[8,128]{1,0:T(8,128)}) custom-call(bf16[8,672,128]{2,1,0:T(8,128)(2,1)S(1)} %all-to-all-done.near_ref.refs_0_, bf16[512,128]{1,0:T(8,128)(2,1)S(1)} %get-tuple-element.43.refs_4_.refs_1_, bf16[512,128]{1,0:T(8,128)(2,1)S(1)} %get-tuple-element.44.refs_5_.refs_2_), custom_call_target="tpu_custom_call" | custom-call | flops 15728640 | bytes 4194304 | tf_op jit(solution)/shard_map/gradient_pieces/pallas_call | solution.py:594
  75.1 1.9 %all-to-all-done.1.refs_12_ = f32[16,16,128]{2,1,0:T(8,128)S(1)} async-done(((f32[16,16,128]{2,1,0:T(8,128)}), f32[16,16,128]{2,1,0:T(8,128)S(1)}, u32[]{:S(2)}, u32[]{:S(2)}) %all-to-all-start.1) | async-done | bytes 131104 | tf_op jit(solution)/shard_map/all_to_all | solution.py:365
  77.0 0.0 collective-permute-done.8.refs_8_
  77.0 5.2 %update_pieces.1 = (bf16[8,640,128]{2,1,0:T(8,128)(2,1)}, bf16[384,128]{1,0:T(8,128)(2,1)}, bf16[384,128]{1,0:T(8,128)(2,1)}, bf16[384,128]{1,0:T(8,128)(2,1)}, ...) custom-call(bf16[8,672,128]{2,1,0:T(8,128)(2,1)S(1)} %all-to-all-don, ...), custom_call_target="tpu_custom_call" | custom-call | flops 1073741824 | bytes 6291456 | tf_op jit(solution)/shard_map/update_pieces/pallas_call | solution.py:753
  82.3 4.8 %all-to-all-start.2 = ((bf16[8,640,128]{2,1,0:T(8,128)(2,1)}), bf16[8,640,128]{2,1,0:T(8,128)(2,1)S(1)}, u32[]{:S(2)}, u32[]{:S(2)}) async-start(bf16[8,640,128]{2,1,0:T(8,128)(2,1)} %get-tuple-element.50), calls=%async_computation.2 | async-start | bytes 2621440 | tf_op jit(solution)/shard_map/all_to_all | solution.py:780
  87.1 1.2 collective-permute-start.9
  88.2 1.7 %collective-permute-start.10 = (bf16[384,128]{1,0:T(8,128)(2,1)S(1)}, bf16[384,128]{1,0:T(8,128)(2,1)S(1)}, u32[]{:S(2)}, u32[]{:S(2)}) collective-permute-start(bf16[384,128]{1,0:T(8,128)(2,1)S(1)} %copy-done.6), channel_id=1, source_target_pairs={{0,9},{1,8},{2,11},{3,10},{4,13},{5,12},{6,15},{7,14},{8,1},{9,0},... | collective-permute-start | bytes 294920 | tf_op jit(solution)/shard_map/ppermute | solution.py:775
  89.9 2.1 %collective-permute-start.11 = (bf16[384,128]{1,0:T(8,128)(2,1)S(1)}, bf16[384,128]{1,0:T(8,128)(2,1)S(1)}, u32[]{:S(2)}, u32[]{:S(2)}) collective-permute-start(bf16[384,128]{1,0:T(8,128)(2,1)S(1)} %copy-done.5), channel_id=1, source_target_pairs={{0,10},{1,11},{2,8},{3,9},{4,14},{5,15},{6,12},{7,13},{8,2},{9,3},... | collective-permute-start | bytes 294920 | tf_op jit(solution)/shard_map/ppermute | solution.py:775
  92.0 1.2 collective-permute-start.12
  93.3 0.0 collective-permute-start.13
  93.3 12.0 %collective-permute-done.9.refs_1_ = bf16[384,128]{1,0:T(8,128)(2,1)S(1)} collective-permute-done((bf16[384,128]{1,0:T(8,128)(2,1)S(1)}, bf16[384,128]{1,0:T(8,128)(2,1)S(1)}, u32[]{:S(2)}, u32[]{:S(2)}) %collective-permute-start.9) | collective-permute-done | bytes 98336 | tf_op jit(solution)/shard_map/ppermute | solution.py:775
  105.3 1.1 collective-permute-start.14
  106.5 1.6 %collective-permute-done.10.refs_2_ = bf16[384,128]{1,0:T(8,128)(2,1)S(1)} collective-permute-done((bf16[384,128]{1,0:T(8,128)(2,1)S(1)}, bf16[384,128]{1,0:T(8,128)(2,1)S(1)}, u32[]{:S(2)}, u32[]{:S(2)}) %collective-permute-start.10) | collective-permute-done | bytes 98336 | tf_op jit(solution)/shard_map/ppermute | solution.py:775
  108.1 1.5 %collective-permute-start.15 = (bf16[384,128]{1,0:T(8,128)(2,1)S(1)}, bf16[384,128]{1,0:T(8,128)(2,1)S(1)}, u32[]{:S(2)}, u32[]{:S(2)}) collective-permute-start(bf16[384,128]{1,0:T(8,128)(2,1)S(1)} %copy-done.1), channel_id=1, source_target_pairs={{0,14},{1,15},{2,12},{3,13},{4,10},{5,11},{6,8},{7,9},{8,6},{9,7},... | collective-permute-start | bytes 294920 | tf_op jit(solution)/shard_map/ppermute | solution.py:775
  109.6 0.9 collective-permute-done.11.refs_3_
  110.5 1.2 collective-permute-start.16
  111.7 3.0 %join_pieces.4.refs_0_ = bf16[1,1048576]{1,0:T(2,128)(2,1)} custom-call(bf16[8,640,128]{2,1,0:T(8,128)(2,1)S(1)} %all-to-all-done.2.refs_0_), custom_call_target="tpu_custom_call" | custom-call | bytes 3932160 | tf_op jit(solution)/shard_map/join_pieces/pallas_call | solution.py:467
  114.6 0.0 collective-permute-done.12.refs_4_
  114.7 1.0 join_pieces.5.refs_0_
  115.6 0.0 collective-permute-done.13.refs_1_
  115.6 7.0 %collective-permute-done.14.refs_2_ = bf16[384,128]{1,0:T(8,128)(2,1)S(1)} collective-permute-done((bf16[384,128]{1,0:T(8,128)(2,1)S(1)}, bf16[384,128]{1,0:T(8,128)(2,1)S(1)}, u32[]{:S(2)}, u32[]{:S(2)}) %collective-permute-start.14) | collective-permute-done | bytes 98336 | tf_op jit(solution)/shard_map/ppermute | solution.py:775
  122.6 0.8 join_pieces.6.refs_0_
  123.4 2.2 %collective-permute-done.15.refs_1_ = bf16[384,128]{1,0:T(8,128)(2,1)S(1)} collective-permute-done((bf16[384,128]{1,0:T(8,128)(2,1)S(1)}, bf16[384,128]{1,0:T(8,128)(2,1)S(1)}, u32[]{:S(2)}, u32[]{:S(2)}) %collective-permute-start.15) | collective-permute-done | bytes 98336 | tf_op jit(solution)/shard_map/ppermute | solution.py:775
  125.6 2.1 %collective-permute-done.16.refs_2_ = bf16[384,128]{1,0:T(8,128)(2,1)S(1)} collective-permute-done((bf16[384,128]{1,0:T(8,128)(2,1)S(1)}, bf16[384,128]{1,0:T(8,128)(2,1)S(1)}, u32[]{:S(2)}, u32[]{:S(2)}) %collective-permute-start.16) | collective-permute-done | bytes 98336 | tf_op jit(solution)/shard_map/ppermute | solution.py:775
  127.7 0.8 join_pieces.7
  (20 shorter events, 0.1 us)
Async XLA Ops:
  3.8 55.8 %all-to-all-start = ((bf16[8,672,128]{2,1,0:T(8,128)(2,1)}), bf16[8,672,128]{2,1,0:T(8,128)(2,1)S(1)}, u32[]{:S(2)}, u32[]{:S(2)}) async-start(bf16[8,672,128]{2,1,0:T(8,128)(2,1)} %get-tuple-element.32), calls=%async_computation | async-start | bytes 2752512 | tf_op jit(solution)/shard_map/all_to_all | solution.py:780
  8.3 20.9 %collective-permute-start = (bf16[528,128]{1,0:T(8,128)(2,1)S(1)}, bf16[528,128]{1,0:T(8,128)(2,1)S(1)}, u32[]{:S(2)}, u32[]{:S(2)}) collective-permute-start(bf16[528,128]{1,0:T(8,128)(2,1)S(1)} %get-tuple-element.33), channel_id=1, source_target_pairs={{0,8},{1,9},{2,10},{3,11},{4,12},{5,13},{6,14},{7,15},{8,0},{9,1},... | collective-permute-start | bytes 405512 | tf_op jit(solution)/shard_map/ppermute | solution.py:775
  10.6 22.2 %collective-permute-start.1 = (bf16[528,128]{1,0:T(8,128)(2,1)S(1)}, bf16[528,128]{1,0:T(8,128)(2,1)S(1)}, u32[]{:S(2)}, u32[]{:S(2)}) collective-permute-start(bf16[528,128]{1,0:T(8,128)(2,1)S(1)} %get-tuple-element.34), channel_id=1, source_target_pairs={{0,9},{1,8},{2,11},{3,10},{4,13},{5,12},{6,15},{7,14},{8,1},{9,0},... | collective-permute-start | bytes 405512 | tf_op jit(solution)/shard_map/ppermute | solution.py:775
  11.2 24.8 %collective-permute-start.2 = (bf16[528,128]{1,0:T(8,128)(2,1)S(1)}, bf16[528,128]{1,0:T(8,128)(2,1)S(1)}, u32[]{:S(2)}, u32[]{:S(2)}) collective-permute-start(bf16[528,128]{1,0:T(8,128)(2,1)S(1)} %get-tuple-element.35), channel_id=1, source_target_pairs={{0,10},{1,11},{2,8},{3,9},{4,14},{5,15},{6,12},{7,13},{8,2},{9,3},... | collective-permute-start | bytes 405512 | tf_op jit(solution)/shard_map/ppermute | solution.py:775
  14.4 25.2 %collective-permute-start.3 = (bf16[528,128]{1,0:T(8,128)(2,1)S(1)}, bf16[528,128]{1,0:T(8,128)(2,1)S(1)}, u32[]{:S(2)}, u32[]{:S(2)}) collective-permute-start(bf16[528,128]{1,0:T(8,128)(2,1)S(1)} %get-tuple-element.36), channel_id=1, source_target_pairs={{0,11},{1,10},{2,9},{3,8},{4,15},{5,14},{6,13},{7,12},{8,3},{9,2},... | collective-permute-start | bytes 405512 | tf_op jit(solution)/shard_map/ppermute | solution.py:775
  14.7 33.4 %collective-permute-start.4 = (bf16[528,128]{1,0:T(8,128)(2,1)S(1)}, bf16[528,128]{1,0:T(8,128)(2,1)S(1)}, u32[]{:S(2)}, u32[]{:S(2)}) collective-permute-start(bf16[528,128]{1,0:T(8,128)(2,1)S(1)} %get-tuple-element.37), channel_id=1, source_target_pairs={{0,12},{1,13},{2,14},{3,15},{4,8},{5,9},{6,10},{7,11},{8,4},{9,5},... | collective-permute-start | bytes 405512 | tf_op jit(solution)/shard_map/ppermute | solution.py:775
  29.3 23.6 %collective-permute-start.5 = (bf16[528,128]{1,0:T(8,128)(2,1)S(1)}, bf16[528,128]{1,0:T(8,128)(2,1)S(1)}, u32[]{:S(2)}, u32[]{:S(2)}) collective-permute-start(bf16[528,128]{1,0:T(8,128)(2,1)S(1)} %get-tuple-element.38), channel_id=1, source_target_pairs={{0,13},{1,12},{2,15},{3,14},{4,9},{5,8},{6,11},{7,10},{8,5},{9,4},... | collective-permute-start | bytes 405512 | tf_op jit(solution)/shard_map/ppermute | solution.py:775
  32.9 23.8 %collective-permute-start.6 = (bf16[528,128]{1,0:T(8,128)(2,1)S(1)}, bf16[528,128]{1,0:T(8,128)(2,1)S(1)}, u32[]{:S(2)}, u32[]{:S(2)}) collective-permute-start(bf16[528,128]{1,0:T(8,128)(2,1)S(1)} %get-tuple-element.39), channel_id=1, source_target_pairs={{0,14},{1,15},{2,12},{3,13},{4,10},{5,11},{6,8},{7,9},{8,6},{9,7},... | collective-permute-start | bytes 405512 | tf_op jit(solution)/shard_map/ppermute | solution.py:775
  36.0 23.5 %collective-permute-start.7 = (bf16[528,128]{1,0:T(8,128)(2,1)S(1)}, bf16[528,128]{1,0:T(8,128)(2,1)S(1)}, u32[]{:S(2)}, u32[]{:S(2)}) collective-permute-start(bf16[528,128]{1,0:T(8,128)(2,1)S(1)} %get-tuple-element.40), channel_id=1, source_target_pairs={{0,15},{1,14},{2,13},{3,12},{4,11},{5,10},{6,9},{7,8},{8,7},{9,6},... | collective-permute-start | bytes 405512 | tf_op jit(solution)/shard_map/ppermute | solution.py:775
  59.6 17.4 %collective-permute-start.8 = (bf16[8,144,128]{2,1,0:T(8,128)(2,1)S(1)}, bf16[8,144,128]{2,1,0:T(8,128)(2,1)S(1)}, u32[]{:S(2)}, u32[]{:S(2)}) collective-permute-start(bf16[8,144,128]{2,1,0:T(8,128)(2,1)S(1)} %raw_states.1.refs_9_), channel_id=1, source_target_pairs={{0,8},{1,9},{2,10},{3,11},{4,12},{5,13},{6,14},{7,15},{8,0},{9,1},... | collective-permute-start | bytes 884744 | tf_op jit(solution)/shard_map/ppermute | solution.py:775
  62.1 14.9 %all-to-all-start.1 = ((f32[16,16,128]{2,1,0:T(8,128)}), f32[16,16,128]{2,1,0:T(8,128)S(1)}, u32[]{:S(2)}, u32[]{:S(2)}) async-start(f32[16,16,128]{2,1,0:T(8,128)} %gram_pieces.1), calls=%async_computation.1 | async-start | bytes 262144 | tf_op jit(solution)/shard_map/all_to_all | solution.py:365
  82.2 4.9 %copy-start.7 = (bf16[384,128]{1,0:T(8,128)(2,1)S(1)}, bf16[384,128]{1,0:T(8,128)(2,1)}, u32[]{:S(2)}) copy-start(bf16[384,128]{1,0:T(8,128)(2,1)} %get-tuple-element.51) | copy-start | bytes 294916
  82.2 6.0 %copy-start.6 = (bf16[384,128]{1,0:T(8,128)(2,1)S(1)}, bf16[384,128]{1,0:T(8,128)(2,1)}, u32[]{:S(2)}) copy-start(bf16[384,128]{1,0:T(8,128)(2,1)} %get-tuple-element.52) | copy-start | bytes 294916
  82.2 7.7 %copy-start.5 = (bf16[384,128]{1,0:T(8,128)(2,1)S(1)}, bf16[384,128]{1,0:T(8,128)(2,1)}, u32[]{:S(2)}) copy-start(bf16[384,128]{1,0:T(8,128)(2,1)} %get-tuple-element.53) | copy-start | bytes 294916
  82.2 9.8 %copy-start.4 = (bf16[384,128]{1,0:T(8,128)(2,1)S(1)}, bf16[384,128]{1,0:T(8,128)(2,1)}, u32[]{:S(2)}) copy-start(bf16[384,128]{1,0:T(8,128)(2,1)} %get-tuple-element.54) | copy-start | bytes 294916
  82.2 11.0 %copy-start.3 = (bf16[384,128]{1,0:T(8,128)(2,1)S(1)}, bf16[384,128]{1,0:T(8,128)(2,1)}, u32[]{:S(2)}) copy-start(bf16[384,128]{1,0:T(8,128)(2,1)} %get-tuple-element.55) | copy-start | bytes 294916
  82.2 23.1 %copy-start.2 = (bf16[384,128]{1,0:T(8,128)(2,1)S(1)}, bf16[384,128]{1,0:T(8,128)(2,1)}, u32[]{:S(2)}) copy-start(bf16[384,128]{1,0:T(8,128)(2,1)} %get-tuple-element.56) | copy-start | bytes 294916
  82.2 25.9 %copy-start.1 = (bf16[384,128]{1,0:T(8,128)(2,1)S(1)}, bf16[384,128]{1,0:T(8,128)(2,1)}, u32[]{:S(2)}) copy-start(bf16[384,128]{1,0:T(8,128)(2,1)} %get-tuple-element.57) | copy-start | bytes 294916
  82.3 28.2 %copy-start = (bf16[384,128]{1,0:T(8,128)(2,1)S(1)}, bf16[384,128]{1,0:T(8,128)(2,1)}, u32[]{:S(2)}) copy-start(bf16[384,128]{1,0:T(8,128)(2,1)} %get-tuple-element.58) | copy-start | bytes 294916
  82.3 29.4 %all-to-all-start.2 = ((bf16[8,640,128]{2,1,0:T(8,128)(2,1)}), bf16[8,640,128]{2,1,0:T(8,128)(2,1)S(1)}, u32[]{:S(2)}, u32[]{:S(2)}) async-start(bf16[8,640,128]{2,1,0:T(8,128)(2,1)} %get-tuple-element.50), calls=%async_computation.2 | async-start | bytes 2621440 | tf_op jit(solution)/shard_map/all_to_all | solution.py:780
  87.1 18.3 %collective-permute-start.9 = (bf16[384,128]{1,0:T(8,128)(2,1)S(1)}, bf16[384,128]{1,0:T(8,128)(2,1)S(1)}, u32[]{:S(2)}, u32[]{:S(2)}) collective-permute-start(bf16[384,128]{1,0:T(8,128)(2,1)S(1)} %copy-done.7), channel_id=1, source_target_pairs={{0,8},{1,9},{2,10},{3,11},{4,12},{5,13},{6,14},{7,15},{8,0},{9,1},... | collective-permute-start | bytes 294920 | tf_op jit(solution)/shard_map/ppermute | solution.py:775
  88.2 19.9 %collective-permute-start.10 = (bf16[384,128]{1,0:T(8,128)(2,1)S(1)}, bf16[384,128]{1,0:T(8,128)(2,1)S(1)}, u32[]{:S(2)}, u32[]{:S(2)}) collective-permute-start(bf16[384,128]{1,0:T(8,128)(2,1)S(1)} %copy-done.6), channel_id=1, source_target_pairs={{0,9},{1,8},{2,11},{3,10},{4,13},{5,12},{6,15},{7,14},{8,1},{9,0},... | collective-permute-start | bytes 294920 | tf_op jit(solution)/shard_map/ppermute | solution.py:775
  89.9 20.5 %collective-permute-start.11 = (bf16[384,128]{1,0:T(8,128)(2,1)S(1)}, bf16[384,128]{1,0:T(8,128)(2,1)S(1)}, u32[]{:S(2)}, u32[]{:S(2)}) collective-permute-start(bf16[384,128]{1,0:T(8,128)(2,1)S(1)} %copy-done.5), channel_id=1, source_target_pairs={{0,10},{1,11},{2,8},{3,9},{4,14},{5,15},{6,12},{7,13},{8,2},{9,3},... | collective-permute-start | bytes 294920 | tf_op jit(solution)/shard_map/ppermute | solution.py:775
  92.0 22.6 %collective-permute-start.12 = (bf16[384,128]{1,0:T(8,128)(2,1)S(1)}, bf16[384,128]{1,0:T(8,128)(2,1)S(1)}, u32[]{:S(2)}, u32[]{:S(2)}) collective-permute-start(bf16[384,128]{1,0:T(8,128)(2,1)S(1)} %copy-done.4), channel_id=1, source_target_pairs={{0,11},{1,10},{2,9},{3,8},{4,15},{5,14},{6,13},{7,12},{8,3},{9,2},... | collective-permute-start | bytes 294920 | tf_op jit(solution)/shard_map/ppermute | solution.py:775
  93.3 22.4 %collective-permute-start.13 = (bf16[384,128]{1,0:T(8,128)(2,1)S(1)}, bf16[384,128]{1,0:T(8,128)(2,1)S(1)}, u32[]{:S(2)}, u32[]{:S(2)}) collective-permute-start(bf16[384,128]{1,0:T(8,128)(2,1)S(1)} %copy-done.3), channel_id=1, source_target_pairs={{0,12},{1,13},{2,14},{3,15},{4,8},{5,9},{6,10},{7,11},{8,4},{9,5},... | collective-permute-start | bytes 294920 | tf_op jit(solution)/shard_map/ppermute | solution.py:775
  105.3 17.3 %collective-permute-start.14 = (bf16[384,128]{1,0:T(8,128)(2,1)S(1)}, bf16[384,128]{1,0:T(8,128)(2,1)S(1)}, u32[]{:S(2)}, u32[]{:S(2)}) collective-permute-start(bf16[384,128]{1,0:T(8,128)(2,1)S(1)} %copy-done.2), channel_id=1, source_target_pairs={{0,13},{1,12},{2,15},{3,14},{4,9},{5,8},{6,11},{7,10},{8,5},{9,4},... | collective-permute-start | bytes 294920 | tf_op jit(solution)/shard_map/ppermute | solution.py:775
  108.1 17.5 %collective-permute-start.15 = (bf16[384,128]{1,0:T(8,128)(2,1)S(1)}, bf16[384,128]{1,0:T(8,128)(2,1)S(1)}, u32[]{:S(2)}, u32[]{:S(2)}) collective-permute-start(bf16[384,128]{1,0:T(8,128)(2,1)S(1)} %copy-done.1), channel_id=1, source_target_pairs={{0,14},{1,15},{2,12},{3,13},{4,10},{5,11},{6,8},{7,9},{8,6},{9,7},... | collective-permute-start | bytes 294920 | tf_op jit(solution)/shard_map/ppermute | solution.py:775
  110.5 17.3 %collective-permute-start.16 = (bf16[384,128]{1,0:T(8,128)(2,1)S(1)}, bf16[384,128]{1,0:T(8,128)(2,1)S(1)}, u32[]{:S(2)}, u32[]{:S(2)}) collective-permute-start(bf16[384,128]{1,0:T(8,128)(2,1)S(1)} %copy-done), channel_id=1, source_target_pairs={{0,15},{1,14},{2,13},{3,12},{4,11},{5,10},{6,9},{7,8},{8,7},{9,6},... | collective-permute-start | bytes 294920 | tf_op jit(solution)/shard_map/ppermute | solution.py:775

commit v25 on v24

--- a/solution.py
+++ b/solution.py
@@ -381,37 +381,37 @@
     cells = lines * LANES
     end = row_ref.shape[1]
     me = lax.axis_index("slab").astype(jnp.int32)
+
+    def part(start, size):
+        return pl.ds(pl.multiple_of(start, GRID_Y), size)
+
+    def grid_row(start):
+        return held[:, part(start, GRID_Y)].astype(F32).reshape(LINE, LANES)
+
     copies = []
-    for slab in range(slabs):
-        part = pl.ds(slab * cells, cells)
-        copies.append(pltpu.make_async_copy(row_ref.at[:, part], held.at[:, part], sems.at[slab]))
+    for at in range(slabs):
+        cut = part(device_at(at, half) * cells, cells)
+        copies.append(pltpu.make_async_copy(row_ref.at[:, cut], held.at[:, cut], sems.at[at]))
     for n, target in enumerate(slab_refs):
         start = (me if n < fields else me ^ half) * lines
         source = field_refs[n % fields].at[lines_of(start, target.shape[0]), :]
         copies.append(pltpu.make_async_copy(source, target, sems.at[slabs + n]))
     for copy in copies:
         copy.start()
-    for copy in copies[:slabs]:
-        copy.wait()
-
-    def part(start, size):
-        return held[:, pl.ds(pl.multiple_of(start, GRID_Y), size)]
-
-    def grid_row(start):
-        return part(start, GRID_Y).astype(F32).reshape(LINE, LANES)
-
-    for at in range(slabs):
-        out_ref = near_out.at[at] if at < half else far_outs[at - half]
+    outs = [near_out.at[at] for at in range(half)] + list(far_outs)
+    for at, out_ref in enumerate(outs):
+        copies[at].wait()
+        out_ref[:lines, :] = held[:, part(device_at(at, half) * cells, cells)].reshape(lines, LANES)
+    for at, out_ref in enumerate(outs):
         slab = device_at(at, half)
         start = slab * cells
-        out_ref[:lines, :] = part(start, cells).reshape(lines, LANES)
         below = jnp.where(slab == slabs - 1, 0.0, grid_row(jnp.minimum(start + cells, end - GRID_Y)))
         above = jnp.where(slab == 0, 0.0, grid_row(jnp.maximum(start - GRID_Y, 0)))
         out_ref[lines : lines + TILE, :] = jnp.concatenate([below, above], axis=0).astype(BF16)
         if at < half:
             start = (slab ^ half) * cells
             to = lines + TILE
-            out_ref[to : to + raw, :] = part(start, raw * LANES).reshape(raw, LANES)
+            out_ref[to : to + raw, :] = held[:, part(start, raw * LANES)].reshape(raw, LANES)
             below = grid_row(start + raw * LANES)
             above = jnp.where(slab ^ half == 0, 0.0, grid_row(jnp.maximum(start - GRID_Y, 0)))
             out_ref[to + raw :, :] = jnp.concatenate([below, above], axis=0).astype(BF16)

time: 129 us -> 129 us (level)
  no operation moved by 1% of the time
where the time goes in v25:
time: 129 us; the launch traced here: 128 us
  waiting for transfers between devices  67.4 us (52%)
  starting transfers between devices  33 us (26%)
  Pallas kernels  25.8 us (20%)
  between operations  2.13 us (2%)
    ppermute x17, waiting for transfers between devices, exchange(): return lax.ppermute(piece, 'slab', [(i, i ^ k) for i in range(slabs)])  65.6 us
    ppermute x17, starting transfers between devices, exchange(): return lax.ppermute(piece, 'slab', [(i, i ^ k) for i in range(slabs)])  17.9 us
    all_to_all x2, starting transfers between devices, swap_near(): lax.all_to_all(pieces, 'slab', 0, 0, axis_index_groups=groups, tiled=True)  9.36 us
    pallas_call x4, Pallas kernels, gradient_pieces(): call(functools.partial(gradient_pieces_body, views, len(arrays), len(numb...  9.06 us
    all_to_all x1, starting transfers between devices, swap(): lax.all_to_all(slabs, 'slab', split_axis=0, concat_axis=0, tiled=True)  5.75 us
    pallas_call x4, Pallas kernels, join_pieces(): call(functools.partial(join_pieces_body, pieces, slabs // 2, raw, NCELL /...  5.54 us
    pallas_call x1, Pallas kernels, update_pieces(): call(functools.partial(update_pieces_body, half, raw, lines, groups), 'up...  5.19 us
    pallas_call x1, Pallas kernels, split_pieces(): call(functools.partial(split_pieces_body, slabs, raw, lines, len(fields))...  3.53 us
  transfers between devices with their start and end apart: 20, of which 15 were waited for; matrix products, arithmetic and copies ran while one was open for 0% of the time, Pallas kernels for 13%

profile of v25, /device:TPU:9, one launch (start us, length us, event | category | flops | bytes accessed | tf_op | source)
XLA Modules:
  0.0 128.3 jit_solution(8263227103400380605)
XLA Ops:
  0.0 3.5 %split_pieces.1 = (bf16[8,672,128]{2,1,0:T(8,128)(2,1)}, bf16[528,128]{1,0:T(8,128)(2,1)S(1)}, bf16[528,128]{1,0:T(8,128)(2,1)S(1)}, bf16[528,128]{1,0:T(8,128)(...) custom-call(bf16[1,1048576]{1,0:T(2,128)(2,1)} %row_ref.1, ...), custom_call_target="tpu_custom_call" | custom-call | bytes 7372800 | tf_op jit(solution)/shard_map/split_pieces/pallas_call | solution.py:431
  3.5 4.6 %all-to-all-start = ((bf16[8,672,128]{2,1,0:T(8,128)(2,1)}), bf16[8,672,128]{2,1,0:T(8,128)(2,1)S(1)}, u32[]{:S(2)}, u32[]{:S(2)}) async-start(bf16[8,672,128]{2,1,0:T(8,128)(2,1)} %get-tuple-element.32), calls=%async_computation | async-start | bytes 2752512 | tf_op jit(solution)/shard_map/all_to_all | solution.py:780
  8.1 2.3 %collective-permute-start = (bf16[528,128]{1,0:T(8,128)(2,1)S(1)}, bf16[528,128]{1,0:T(8,128)(2,1)S(1)}, u32[]{:S(2)}, u32[]{:S(2)}) collective-permute-start(bf16[528,128]{1,0:T(8,128)(2,1)S(1)} %get-tuple-element.33), channel_id=1, source_target_pairs={{0,8},{1,9},{2,10},{3,11},{4,12},{5,13},{6,14},{7,15},{8,0},{9,1},... | collective-permute-start | bytes 405512 | tf_op jit(solution)/shard_map/ppermute | solution.py:775
  10.4 0.6 collective-permute-start.1
  11.0 3.2 %collective-permute-start.2 = (bf16[528,128]{1,0:T(8,128)(2,1)S(1)}, bf16[528,128]{1,0:T(8,128)(2,1)S(1)}, u32[]{:S(2)}, u32[]{:S(2)}) collective-permute-start(bf16[528,128]{1,0:T(8,128)(2,1)S(1)} %get-tuple-element.35), channel_id=1, source_target_pairs={{0,10},{1,11},{2,8},{3,9},{4,14},{5,15},{6,12},{7,13},{8,2},{9,3},... | collective-permute-start | bytes 405512 | tf_op jit(solution)/shard_map/ppermute | solution.py:775
  14.2 0.3 collective-permute-start.3
  14.5 1.0 collective-permute-start.4
  15.5 13.5 %collective-permute-done.refs_0_ = bf16[528,128]{1,0:T(8,128)(2,1)S(1)} collective-permute-done((bf16[528,128]{1,0:T(8,128)(2,1)S(1)}, bf16[528,128]{1,0:T(8,128)(2,1)S(1)}, u32[]{:S(2)}, u32[]{:S(2)}) %collective-permute-start) | collective-permute-done | bytes 135200 | tf_op jit(solution)/shard_map/ppermute | solution.py:775
  29.0 0.0 collective-permute-start.5
  29.1 3.6 %collective-permute-done.1.refs_1_ = bf16[528,128]{1,0:T(8,128)(2,1)S(1)} collective-permute-done((bf16[528,128]{1,0:T(8,128)(2,1)S(1)}, bf16[528,128]{1,0:T(8,128)(2,1)S(1)}, u32[]{:S(2)}, u32[]{:S(2)}) %collective-permute-start.1) | collective-permute-done | bytes 135200 | tf_op jit(solution)/shard_map/ppermute | solution.py:775
  32.7 0.3 collective-permute-start.6
  33.0 2.8 %collective-permute-done.2.refs_2_ = bf16[528,128]{1,0:T(8,128)(2,1)S(1)} collective-permute-done((bf16[528,128]{1,0:T(8,128)(2,1)S(1)}, bf16[528,128]{1,0:T(8,128)(2,1)S(1)}, u32[]{:S(2)}, u32[]{:S(2)}) %collective-permute-start.2) | collective-permute-done | bytes 135200 | tf_op jit(solution)/shard_map/ppermute | solution.py:775
  35.8 0.0 collective-permute-start.7
  37.7 1.7 %collective-permute-done.3.refs_3_ = bf16[528,128]{1,0:T(8,128)(2,1)S(1)} collective-permute-done((bf16[528,128]{1,0:T(8,128)(2,1)S(1)}, bf16[528,128]{1,0:T(8,128)(2,1)S(1)}, u32[]{:S(2)}, u32[]{:S(2)}) %collective-permute-start.3) | collective-permute-done | bytes 135200 | tf_op jit(solution)/shard_map/ppermute | solution.py:775
  39.4 1.8 %gradient_pieces.4 = (bf16[4,512,128]{2,1,0:T(8,128)(2,1)}, f32[8,128]{1,0:T(8,128)S(1)}) custom-call(bf16[528,128]{1,0:T(8,128)(2,1)S(1)} %collective-permute-done.refs_0_, bf16[528,128]{1,0:T(8,128)(2,1)S(1)} %collective-permute-done.1.refs_1_, bf16[528,128]{1,0:T(8,128)(2,1)S(1)} %collective-permute-done.2.refs_2_, ...), custom_call_target="tpu_custom_call" | custom-call | flops 7864320 | bytes 2097152 | tf_op jit(solution)/shard_map/gradient_pieces/pallas_call | solution.py:594
  41.2 6.7 %collective-permute-done.4.refs_4_.refs_0_ = bf16[528,128]{1,0:T(8,128)(2,1)S(1)} collective-permute-done((bf16[528,128]{1,0:T(8,128)(2,1)S(1)}, bf16[528,128]{1,0:T(8,128)(2,1)S(1)}, u32[]{:S(2)}, u32[]{:S(2)}) %collective-permute-start.4) | collective-permute-done | bytes 135200 | tf_op jit(solution)/shard_map/ppermute | solution.py:775
  47.9 4.7 %collective-permute-done.5.refs_5_.refs_1_ = bf16[528,128]{1,0:T(8,128)(2,1)S(1)} collective-permute-done((bf16[528,128]{1,0:T(8,128)(2,1)S(1)}, bf16[528,128]{1,0:T(8,128)(2,1)S(1)}, u32[]{:S(2)}, u32[]{:S(2)}) %collective-permute-start.5) | collective-permute-done | bytes 135200 | tf_op jit(solution)/shard_map/ppermute | solution.py:775
  52.6 3.8 %collective-permute-done.6.refs_6_.refs_2_ = bf16[528,128]{1,0:T(8,128)(2,1)S(1)} collective-permute-done((bf16[528,128]{1,0:T(8,128)(2,1)S(1)}, bf16[528,128]{1,0:T(8,128)(2,1)S(1)}, u32[]{:S(2)}, u32[]{:S(2)}) %collective-permute-start.6) | collective-permute-done | bytes 135200 | tf_op jit(solution)/shard_map/ppermute | solution.py:775
  56.4 2.9 %collective-permute-done.7.refs_7_.refs_3_ = bf16[528,128]{1,0:T(8,128)(2,1)S(1)} collective-permute-done((bf16[528,128]{1,0:T(8,128)(2,1)S(1)}, bf16[528,128]{1,0:T(8,128)(2,1)S(1)}, u32[]{:S(2)}, u32[]{:S(2)}) %collective-permute-start.7) | collective-permute-done | bytes 135200 | tf_op jit(solution)/shard_map/ppermute | solution.py:775
  59.3 0.0 all-to-all-done.near_ref.refs_0_
  59.4 0.1 collective-permute-start.8
  59.4 2.4 %gram_pieces.1 = f32[16,16,128]{2,1,0:T(8,128)} custom-call(bf16[8,672,128]{2,1,0:T(8,128)(2,1)S(1)} %all-to-all-done.near_ref.refs_0_, bf16[528,128]{1,0:T(8,128)(2,1)S(1)} %collective-permute-done.refs_0_, bf16[528,128]{1,0:T(8,128)(2,1)S(1)} %collective-permute-done.1.refs_1_, bf16[528,128]{1,0:T(8,128)(2,1)S(1)} %collective-permute-done.2.refs_2_, ...), custom_call_target="tpu_custom_call" | custom-call | flops 536870912 | bytes 2097152 | tf_op jit(solution)/shard_map/gram_pieces/pallas_call | solution.py:521
  61.9 5.7 %all-to-all-start.1 = ((f32[16,16,128]{2,1,0:T(8,128)}), f32[16,16,128]{2,1,0:T(8,128)S(1)}, u32[]{:S(2)}, u32[]{:S(2)}) async-start(f32[16,16,128]{2,1,0:T(8,128)} %gram_pieces.1), calls=%async_computation.1 | async-start | bytes 262144 | tf_op jit(solution)/shard_map/all_to_all | solution.py:365
  67.6 2.4 %gradient_pieces.6 = (bf16[4,512,128]{2,1,0:T(8,128)(2,1)}, f32[8,128]{1,0:T(8,128)}) custom-call(bf16[528,128]{1,0:T(8,128)(2,1)S(1)} %collective-permute-done.4.refs_4_.refs_0_, bf16[528,128]{1,0:T(8,128)(2,1)S(1)} %collective-permute-done.5.refs_5_.refs_1_, bf16[528,128]{1,0:T(8,128)(2,1)S(1)} %collective-permute-done.6.refs_6_.refs_2_, ...), custom_call_target="tpu_custom_call" | custom-call | flops 7864320 | bytes 2097152 | tf_op jit(solution)/shard_map/gradient_pieces/pallas_call | solution.py:594
  70.0 1.7 %gradient_pieces.5 = (bf16[8,128,128]{2,1,0:T(8,128)(2,1)}, f32[8,128]{1,0:T(8,128)}) custom-call(bf16[8,672,128]{2,1,0:T(8,128)(2,1)S(1)} %all-to-all-done.near_ref.refs_0_, bf16[128,128]{1,0:T(8,128)(2,1)S(1)} %get-tuple-element.41.refs_1_.refs_9_, bf16[128,128]{1,0:T(8,128)(2,1)S(1)} %get-tuple-element.42.refs_2_.refs_10_), custom_call_target="tpu_custom_call" | custom-call | flops 3932160 | bytes 1048576 | tf_op jit(solution)/shard_map/gradient_pieces/pallas_call | solution.py:594
  71.7 3.2 %gradient_pieces.7 = (bf16[8,512,128]{2,1,0:T(8,128)(2,1)}, f32[8,128]{1,0:T(8,128)}) custom-call(bf16[8,672,128]{2,1,0:T(8,128)(2,1)S(1)} %all-to-all-done.near_ref.refs_0_, bf16[512,128]{1,0:T(8,128)(2,1)S(1)} %get-tuple-element.43.refs_4_.refs_1_, bf16[512,128]{1,0:T(8,128)(2,1)S(1)} %get-tuple-element.44.refs_5_.refs_2_), custom_call_target="tpu_custom_call" | custom-call | flops 15728640 | bytes 4194304 | tf_op jit(solution)/shard_map/gradient_pieces/pallas_call | solution.py:594
  74.9 1.9 %all-to-all-done.1.refs_12_ = f32[16,16,128]{2,1,0:T(8,128)S(1)} async-done(((f32[16,16,128]{2,1,0:T(8,128)}), f32[16,16,128]{2,1,0:T(8,128)S(1)}, u32[]{:S(2)}, u32[]{:S(2)}) %all-to-all-start.1) | async-done | bytes 131104 | tf_op jit(solution)/shard_map/all_to_all | solution.py:365
  76.8 5.2 %update_pieces.1 = (bf16[8,640,128]{2,1,0:T(8,128)(2,1)}, bf16[384,128]{1,0:T(8,128)(2,1)}, bf16[384,128]{1,0:T(8,128)(2,1)}, bf16[384,128]{1,0:T(8,128)(2,1)}, ...) custom-call(bf16[8,672,128]{2,1,0:T(8,128)(2,1)S(1)} %all-to-all-don, ...), custom_call_target="tpu_custom_call" | custom-call | flops 1073741824 | bytes 6291456 | tf_op jit(solution)/shard_map/update_pieces/pallas_call | solution.py:753
  82.0 4.8 %all-to-all-start.2 = ((bf16[8,640,128]{2,1,0:T(8,128)(2,1)}), bf16[8,640,128]{2,1,0:T(8,128)(2,1)S(1)}, u32[]{:S(2)}, u32[]{:S(2)}) async-start(bf16[8,640,128]{2,1,0:T(8,128)(2,1)} %get-tuple-element.50), calls=%async_computation.2 | async-start | bytes 2621440 | tf_op jit(solution)/shard_map/all_to_all | solution.py:780
  86.8 1.2 collective-permute-start.9
  88.0 1.7 %collective-permute-start.10 = (bf16[384,128]{1,0:T(8,128)(2,1)S(1)}, bf16[384,128]{1,0:T(8,128)(2,1)S(1)}, u32[]{:S(2)}, u32[]{:S(2)}) collective-permute-start(bf16[384,128]{1,0:T(8,128)(2,1)S(1)} %copy-done.6), channel_id=1, source_target_pairs={{0,9},{1,8},{2,11},{3,10},{4,13},{5,12},{6,15},{7,14},{8,1},{9,0},... | collective-permute-start | bytes 294920 | tf_op jit(solution)/shard_map/ppermute | solution.py:775
  89.7 2.1 %collective-permute-start.11 = (bf16[384,128]{1,0:T(8,128)(2,1)S(1)}, bf16[384,128]{1,0:T(8,128)(2,1)S(1)}, u32[]{:S(2)}, u32[]{:S(2)}) collective-permute-start(bf16[384,128]{1,0:T(8,128)(2,1)S(1)} %copy-done.5), channel_id=1, source_target_pairs={{0,10},{1,11},{2,8},{3,9},{4,14},{5,15},{6,12},{7,13},{8,2},{9,3},... | collective-permute-start | bytes 294920 | tf_op jit(solution)/shard_map/ppermute | solution.py:775
  91.8 1.2 collective-permute-start.12
  93.0 0.0 collective-permute-start.13
  93.1 12.0 %collective-permute-done.9.refs_1_ = bf16[384,128]{1,0:T(8,128)(2,1)S(1)} collective-permute-done((bf16[384,128]{1,0:T(8,128)(2,1)S(1)}, bf16[384,128]{1,0:T(8,128)(2,1)S(1)}, u32[]{:S(2)}, u32[]{:S(2)}) %collective-permute-start.9) | collective-permute-done | bytes 98336 | tf_op jit(solution)/shard_map/ppermute | solution.py:775
  105.1 1.1 collective-permute-start.14
  106.2 1.6 %collective-permute-done.10.refs_2_ = bf16[384,128]{1,0:T(8,128)(2,1)S(1)} collective-permute-done((bf16[384,128]{1,0:T(8,128)(2,1)S(1)}, bf16[384,128]{1,0:T(8,128)(2,1)S(1)}, u32[]{:S(2)}, u32[]{:S(2)}) %collective-permute-start.10) | collective-permute-done | bytes 98336 | tf_op jit(solution)/shard_map/ppermute | solution.py:775
  107.9 1.5 %collective-permute-start.15 = (bf16[384,128]{1,0:T(8,128)(2,1)S(1)}, bf16[384,128]{1,0:T(8,128)(2,1)S(1)}, u32[]{:S(2)}, u32[]{:S(2)}) collective-permute-start(bf16[384,128]{1,0:T(8,128)(2,1)S(1)} %copy-done.1), channel_id=1, source_target_pairs={{0,14},{1,15},{2,12},{3,13},{4,10},{5,11},{6,8},{7,9},{8,6},{9,7},... | collective-permute-start | bytes 294920 | tf_op jit(solution)/shard_map/ppermute | solution.py:775
  109.4 0.9 collective-permute-done.11.refs_3_
  110.2 1.2 collective-permute-start.16
  111.4 0.0 all-to-all-done.2.refs_0_
  111.4 3.0 %join_pieces.4.refs_0_ = bf16[1,1048576]{1,0:T(2,128)(2,1)} custom-call(bf16[8,640,128]{2,1,0:T(8,128)(2,1)S(1)} %all-to-all-done.2.refs_0_), custom_call_target="tpu_custom_call" | custom-call | bytes 3932160 | tf_op jit(solution)/shard_map/join_pieces/pallas_call | solution.py:467
  114.4 1.0 join_pieces.5.refs_0_
  115.4 7.0 %collective-permute-done.14.refs_2_ = bf16[384,128]{1,0:T(8,128)(2,1)S(1)} collective-permute-done((bf16[384,128]{1,0:T(8,128)(2,1)S(1)}, bf16[384,128]{1,0:T(8,128)(2,1)S(1)}, u32[]{:S(2)}, u32[]{:S(2)}) %collective-permute-start.14) | collective-permute-done | bytes 98336 | tf_op jit(solution)/shard_map/ppermute | solution.py:775
  122.4 0.8 join_pieces.6.refs_0_
  123.2 2.2 %collective-permute-done.15.refs_1_ = bf16[384,128]{1,0:T(8,128)(2,1)S(1)} collective-permute-done((bf16[384,128]{1,0:T(8,128)(2,1)S(1)}, bf16[384,128]{1,0:T(8,128)(2,1)S(1)}, u32[]{:S(2)}, u32[]{:S(2)}) %collective-permute-start.15) | collective-permute-done | bytes 98336 | tf_op jit(solution)/shard_map/ppermute | solution.py:775
  125.4 2.1 %collective-permute-done.16.refs_2_ = bf16[384,128]{1,0:T(8,128)(2,1)S(1)} collective-permute-done((bf16[384,128]{1,0:T(8,128)(2,1)S(1)}, bf16[384,128]{1,0:T(8,128)(2,1)S(1)}, u32[]{:S(2)}, u32[]{:S(2)}) %collective-permute-start.16) | collective-permute-done | bytes 98336 | tf_op jit(solution)/shard_map/ppermute | solution.py:775
  127.5 0.8 join_pieces.7
  (20 shorter events, 0.1 us)
Async XLA Ops:
  3.5 55.8 %all-to-all-start = ((bf16[8,672,128]{2,1,0:T(8,128)(2,1)}), bf16[8,672,128]{2,1,0:T(8,128)(2,1)S(1)}, u32[]{:S(2)}, u32[]{:S(2)}) async-start(bf16[8,672,128]{2,1,0:T(8,128)(2,1)} %get-tuple-element.32), calls=%async_computation | async-start | bytes 2752512 | tf_op jit(solution)/shard_map/all_to_all | solution.py:780
  8.1 20.9 %collective-permute-start = (bf16[528,128]{1,0:T(8,128)(2,1)S(1)}, bf16[528,128]{1,0:T(8,128)(2,1)S(1)}, u32[]{:S(2)}, u32[]{:S(2)}) collective-permute-start(bf16[528,128]{1,0:T(8,128)(2,1)S(1)} %get-tuple-element.33), channel_id=1, source_target_pairs={{0,8},{1,9},{2,10},{3,11},{4,12},{5,13},{6,14},{7,15},{8,0},{9,1},... | collective-permute-start | bytes 405512 | tf_op jit(solution)/shard_map/ppermute | solution.py:775
  10.4 22.2 %collective-permute-start.1 = (bf16[528,128]{1,0:T(8,128)(2,1)S(1)}, bf16[528,128]{1,0:T(8,128)(2,1)S(1)}, u32[]{:S(2)}, u32[]{:S(2)}) collective-permute-start(bf16[528,128]{1,0:T(8,128)(2,1)S(1)} %get-tuple-element.34), channel_id=1, source_target_pairs={{0,9},{1,8},{2,11},{3,10},{4,13},{5,12},{6,15},{7,14},{8,1},{9,0},... | collective-permute-start | bytes 405512 | tf_op jit(solution)/shard_map/ppermute | solution.py:775
  11.0 24.8 %collective-permute-start.2 = (bf16[528,128]{1,0:T(8,128)(2,1)S(1)}, bf16[528,128]{1,0:T(8,128)(2,1)S(1)}, u32[]{:S(2)}, u32[]{:S(2)}) collective-permute-start(bf16[528,128]{1,0:T(8,128)(2,1)S(1)} %get-tuple-element.35), channel_id=1, source_target_pairs={{0,10},{1,11},{2,8},{3,9},{4,14},{5,15},{6,12},{7,13},{8,2},{9,3},... | collective-permute-start | bytes 405512 | tf_op jit(solution)/shard_map/ppermute | solution.py:775
  14.2 25.2 %collective-permute-start.3 = (bf16[528,128]{1,0:T(8,128)(2,1)S(1)}, bf16[528,128]{1,0:T(8,128)(2,1)S(1)}, u32[]{:S(2)}, u32[]{:S(2)}) collective-permute-start(bf16[528,128]{1,0:T(8,128)(2,1)S(1)} %get-tuple-element.36), channel_id=1, source_target_pairs={{0,11},{1,10},{2,9},{3,8},{4,15},{5,14},{6,13},{7,12},{8,3},{9,2},... | collective-permute-start | bytes 405512 | tf_op jit(solution)/shard_map/ppermute | solution.py:775
  14.5 33.4 %collective-permute-start.4 = (bf16[528,128]{1,0:T(8,128)(2,1)S(1)}, bf16[528,128]{1,0:T(8,128)(2,1)S(1)}, u32[]{:S(2)}, u32[]{:S(2)}) collective-permute-start(bf16[528,128]{1,0:T(8,128)(2,1)S(1)} %get-tuple-element.37), channel_id=1, source_target_pairs={{0,12},{1,13},{2,14},{3,15},{4,8},{5,9},{6,10},{7,11},{8,4},{9,5},... | collective-permute-start | bytes 405512 | tf_op jit(solution)/shard_map/ppermute | solution.py:775
  29.0 23.6 %collective-permute-start.5 = (bf16[528,128]{1,0:T(8,128)(2,1)S(1)}, bf16[528,128]{1,0:T(8,128)(2,1)S(1)}, u32[]{:S(2)}, u32[]{:S(2)}) collective-permute-start(bf16[528,128]{1,0:T(8,128)(2,1)S(1)} %get-tuple-element.38), channel_id=1, source_target_pairs={{0,13},{1,12},{2,15},{3,14},{4,9},{5,8},{6,11},{7,10},{8,5},{9,4},... | collective-permute-start | bytes 405512 | tf_op jit(solution)/shard_map/ppermute | solution.py:775
  32.7 23.8 %collective-permute-start.6 = (bf16[528,128]{1,0:T(8,128)(2,1)S(1)}, bf16[528,128]{1,0:T(8,128)(2,1)S(1)}, u32[]{:S(2)}, u32[]{:S(2)}) collective-permute-start(bf16[528,128]{1,0:T(8,128)(2,1)S(1)} %get-tuple-element.39), channel_id=1, source_target_pairs={{0,14},{1,15},{2,12},{3,13},{4,10},{5,11},{6,8},{7,9},{8,6},{9,7},... | collective-permute-start | bytes 405512 | tf_op jit(solution)/shard_map/ppermute | solution.py:775
  35.8 23.5 %collective-permute-start.7 = (bf16[528,128]{1,0:T(8,128)(2,1)S(1)}, bf16[528,128]{1,0:T(8,128)(2,1)S(1)}, u32[]{:S(2)}, u32[]{:S(2)}) collective-permute-start(bf16[528,128]{1,0:T(8,128)(2,1)S(1)} %get-tuple-element.40), channel_id=1, source_target_pairs={{0,15},{1,14},{2,13},{3,12},{4,11},{5,10},{6,9},{7,8},{8,7},{9,6},... | collective-permute-start | bytes 405512 | tf_op jit(solution)/shard_map/ppermute | solution.py:775
  59.4 17.4 %collective-permute-start.8 = (bf16[8,144,128]{2,1,0:T(8,128)(2,1)S(1)}, bf16[8,144,128]{2,1,0:T(8,128)(2,1)S(1)}, u32[]{:S(2)}, u32[]{:S(2)}) collective-permute-start(bf16[8,144,128]{2,1,0:T(8,128)(2,1)S(1)} %raw_states.1.refs_9_), channel_id=1, source_target_pairs={{0,8},{1,9},{2,10},{3,11},{4,12},{5,13},{6,14},{7,15},{8,0},{9,1},... | collective-permute-start | bytes 884744 | tf_op jit(solution)/shard_map/ppermute | solution.py:775
  61.9 14.9 %all-to-all-start.1 = ((f32[16,16,128]{2,1,0:T(8,128)}), f32[16,16,128]{2,1,0:T(8,128)S(1)}, u32[]{:S(2)}, u32[]{:S(2)}) async-start(f32[16,16,128]{2,1,0:T(8,128)} %gram_pieces.1), calls=%async_computation.1 | async-start | bytes 262144 | tf_op jit(solution)/shard_map/all_to_all | solution.py:365
  82.0 4.9 %copy-start.7 = (bf16[384,128]{1,0:T(8,128)(2,1)S(1)}, bf16[384,128]{1,0:T(8,128)(2,1)}, u32[]{:S(2)}) copy-start(bf16[384,128]{1,0:T(8,128)(2,1)} %get-tuple-element.51) | copy-start | bytes 294916
  82.0 6.0 %copy-start.6 = (bf16[384,128]{1,0:T(8,128)(2,1)S(1)}, bf16[384,128]{1,0:T(8,128)(2,1)}, u32[]{:S(2)}) copy-start(bf16[384,128]{1,0:T(8,128)(2,1)} %get-tuple-element.52) | copy-start | bytes 294916
  82.0 7.7 %copy-start.5 = (bf16[384,128]{1,0:T(8,128)(2,1)S(1)}, bf16[384,128]{1,0:T(8,128)(2,1)}, u32[]{:S(2)}) copy-start(bf16[384,128]{1,0:T(8,128)(2,1)} %get-tuple-element.53) | copy-start | bytes 294916
  82.0 9.8 %copy-start.4 = (bf16[384,128]{1,0:T(8,128)(2,1)S(1)}, bf16[384,128]{1,0:T(8,128)(2,1)}, u32[]{:S(2)}) copy-start(bf16[384,128]{1,0:T(8,128)(2,1)} %get-tuple-element.54) | copy-start | bytes 294916
  82.0 11.0 %copy-start.3 = (bf16[384,128]{1,0:T(8,128)(2,1)S(1)}, bf16[384,128]{1,0:T(8,128)(2,1)}, u32[]{:S(2)}) copy-start(bf16[384,128]{1,0:T(8,128)(2,1)} %get-tuple-element.55) | copy-start | bytes 294916
  82.0 23.1 %copy-start.2 = (bf16[384,128]{1,0:T(8,128)(2,1)S(1)}, bf16[384,128]{1,0:T(8,128)(2,1)}, u32[]{:S(2)}) copy-start(bf16[384,128]{1,0:T(8,128)(2,1)} %get-tuple-element.56) | copy-start | bytes 294916
  82.0 25.9 %copy-start.1 = (bf16[384,128]{1,0:T(8,128)(2,1)S(1)}, bf16[384,128]{1,0:T(8,128)(2,1)}, u32[]{:S(2)}) copy-start(bf16[384,128]{1,0:T(8,128)(2,1)} %get-tuple-element.57) | copy-start | bytes 294916
  82.0 28.2 %copy-start = (bf16[384,128]{1,0:T(8,128)(2,1)S(1)}, bf16[384,128]{1,0:T(8,128)(2,1)}, u32[]{:S(2)}) copy-start(bf16[384,128]{1,0:T(8,128)(2,1)} %get-tuple-element.58) | copy-start | bytes 294916
  82.0 29.4 %all-to-all-start.2 = ((bf16[8,640,128]{2,1,0:T(8,128)(2,1)}), bf16[8,640,128]{2,1,0:T(8,128)(2,1)S(1)}, u32[]{:S(2)}, u32[]{:S(2)}) async-start(bf16[8,640,128]{2,1,0:T(8,128)(2,1)} %get-tuple-element.50), calls=%async_computation.2 | async-start | bytes 2621440 | tf_op jit(solution)/shard_map/all_to_all | solution.py:780
  86.8 18.3 %collective-permute-start.9 = (bf16[384,128]{1,0:T(8,128)(2,1)S(1)}, bf16[384,128]{1,0:T(8,128)(2,1)S(1)}, u32[]{:S(2)}, u32[]{:S(2)}) collective-permute-start(bf16[384,128]{1,0:T(8,128)(2,1)S(1)} %copy-done.7), channel_id=1, source_target_pairs={{0,8},{1,9},{2,10},{3,11},{4,12},{5,13},{6,14},{7,15},{8,0},{9,1},... | collective-permute-start | bytes 294920 | tf_op jit(solution)/shard_map/ppermute | solution.py:775
  88.0 19.9 %collective-permute-start.10 = (bf16[384,128]{1,0:T(8,128)(2,1)S(1)}, bf16[384,128]{1,0:T(8,128)(2,1)S(1)}, u32[]{:S(2)}, u32[]{:S(2)}) collective-permute-start(bf16[384,128]{1,0:T(8,128)(2,1)S(1)} %copy-done.6), channel_id=1, source_target_pairs={{0,9},{1,8},{2,11},{3,10},{4,13},{5,12},{6,15},{7,14},{8,1},{9,0},... | collective-permute-start | bytes 294920 | tf_op jit(solution)/shard_map/ppermute | solution.py:775
  89.7 20.5 %collective-permute-start.11 = (bf16[384,128]{1,0:T(8,128)(2,1)S(1)}, bf16[384,128]{1,0:T(8,128)(2,1)S(1)}, u32[]{:S(2)}, u32[]{:S(2)}) collective-permute-start(bf16[384,128]{1,0:T(8,128)(2,1)S(1)} %copy-done.5), channel_id=1, source_target_pairs={{0,10},{1,11},{2,8},{3,9},{4,14},{5,15},{6,12},{7,13},{8,2},{9,3},... | collective-permute-start | bytes 294920 | tf_op jit(solution)/shard_map/ppermute | solution.py:775
  91.8 22.6 %collective-permute-start.12 = (bf16[384,128]{1,0:T(8,128)(2,1)S(1)}, bf16[384,128]{1,0:T(8,128)(2,1)S(1)}, u32[]{:S(2)}, u32[]{:S(2)}) collective-permute-start(bf16[384,128]{1,0:T(8,128)(2,1)S(1)} %copy-done.4), channel_id=1, source_target_pairs={{0,11},{1,10},{2,9},{3,8},{4,15},{5,14},{6,13},{7,12},{8,3},{9,2},... | collective-permute-start | bytes 294920 | tf_op jit(solution)/shard_map/ppermute | solution.py:775
  93.0 22.4 %collective-permute-start.13 = (bf16[384,128]{1,0:T(8,128)(2,1)S(1)}, bf16[384,128]{1,0:T(8,128)(2,1)S(1)}, u32[]{:S(2)}, u32[]{:S(2)}) collective-permute-start(bf16[384,128]{1,0:T(8,128)(2,1)S(1)} %copy-done.3), channel_id=1, source_target_pairs={{0,12},{1,13},{2,14},{3,15},{4,8},{5,9},{6,10},{7,11},{8,4},{9,5},... | collective-permute-start | bytes 294920 | tf_op jit(solution)/shard_map/ppermute | solution.py:775
  105.1 17.3 %collective-permute-start.14 = (bf16[384,128]{1,0:T(8,128)(2,1)S(1)}, bf16[384,128]{1,0:T(8,128)(2,1)S(1)}, u32[]{:S(2)}, u32[]{:S(2)}) collective-permute-start(bf16[384,128]{1,0:T(8,128)(2,1)S(1)} %copy-done.2), channel_id=1, source_target_pairs={{0,13},{1,12},{2,15},{3,14},{4,9},{5,8},{6,11},{7,10},{8,5},{9,4},... | collective-permute-start | bytes 294920 | tf_op jit(solution)/shard_map/ppermute | solution.py:775
  107.9 17.5 %collective-permute-start.15 = (bf16[384,128]{1,0:T(8,128)(2,1)S(1)}, bf16[384,128]{1,0:T(8,128)(2,1)S(1)}, u32[]{:S(2)}, u32[]{:S(2)}) collective-permute-start(bf16[384,128]{1,0:T(8,128)(2,1)S(1)} %copy-done.1), channel_id=1, source_target_pairs={{0,14},{1,15},{2,12},{3,13},{4,10},{5,11},{6,8},{7,9},{8,6},{9,7},... | collective-permute-start | bytes 294920 | tf_op jit(solution)/shard_map/ppermute | solution.py:775
  110.2 17.3 %collective-permute-start.16 = (bf16[384,128]{1,0:T(8,128)(2,1)S(1)}, bf16[384,128]{1,0:T(8,128)(2,1)S(1)}, u32[]{:S(2)}, u32[]{:S(2)}) collective-permute-start(bf16[384,128]{1,0:T(8,128)(2,1)S(1)} %copy-done), channel_id=1, source_target_pairs={{0,15},{1,14},{2,13},{3,12},{4,11},{5,10},{6,9},{7,8},{8,7},{9,6},... | collective-permute-start | bytes 294920 | tf_op jit(solution)/shard_map/ppermute | solution.py:775

commit v26 on v25

--- a/solution.py
+++ b/solution.py
@@ -780,7 +780,7 @@
     return lax.all_to_all(pieces, "slab", 0, 0, axis_index_groups=groups, tiled=True)
 
 
-RAW = 128
+RAW = 192
 GRADIENTS = ((8, 9, 10, 11), (12, 13, 14, 15), (0, 1, 2, 3, 4, 5, 6, 7))
 
 

time: 129 us -> 135 us (1.047)
  waiting for transfers between devices: 67.4 us -> 72.3 us
  Pallas kernels: 25.8 us -> 27.7 us
    ppermute x17, waiting for transfers between devices: 65.6 us -> 70.4 us  [exchange(): return lax.ppermute(piece, 'slab', [(i, i ^ k) for i in range(slabs)])]
    pallas_call x1, Pallas kernels: 5.19 us -> 6.6 us  [update_pieces(): call(functools.partial(update_pieces_body, half, raw, lines, groups), 'up...]
  transfers between devices with their start and end apart: 20 -> 20, of which waited for: 15 -> 14; matrix products, arithmetic and copies ran while one was open for 0% -> 0% of each run, Pallas kernels for 13% -> 12%
where the time goes in v26:
time: 135 us; the launch traced here: 134 us
  waiting for transfers between devices  72.3 us (54%)
  starting transfers between devices  32.2 us (24%)
  Pallas kernels  27.7 us (21%)
  between operations  2.13 us (2%)
    ppermute x17, waiting for transfers between devices, exchange(): return lax.ppermute(piece, 'slab', [(i, i ^ k) for i in range(slabs)])  70.4 us
    ppermute x17, starting transfers between devices, exchange(): return lax.ppermute(piece, 'slab', [(i, i ^ k) for i in range(slabs)])  17.2 us
    pallas_call x4, Pallas kernels, gradient_pieces(): call(functools.partial(gradient_pieces_body, views, len(arrays), len(numb...  9.34 us
    all_to_all x2, starting transfers between devices, swap_near(): lax.all_to_all(pieces, 'slab', 0, 0, axis_index_groups=groups, tiled=True)  9.31 us
    pallas_call x1, Pallas kernels, update_pieces(): call(functools.partial(update_pieces_body, half, raw, lines, groups), 'up...  6.6 us
    all_to_all x1, starting transfers between devices, swap(): lax.all_to_all(slabs, 'slab', split_axis=0, concat_axis=0, tiled=True)  5.76 us
    pallas_call x4, Pallas kernels, join_pieces(): call(functools.partial(join_pieces_body, pieces, slabs // 2, raw, NCELL /...  5.67 us
    pallas_call x1, Pallas kernels, split_pieces(): call(functools.partial(split_pieces_body, slabs, raw, lines, len(fields))...  3.66 us
  transfers between devices with their start and end apart: 20, of which 14 were waited for; matrix products, arithmetic and copies ran while one was open for 0% of the time, Pallas kernels for 12%

profile of v26, /device:TPU:9, one launch (start us, length us, event | category | flops | bytes accessed | tf_op | source)
XLA Modules:
  0.0 134.4 jit_solution(17937342956064309044)
XLA Ops:
  0.0 3.7 %split_pieces.1 = (bf16[8,736,128]{2,1,0:T(8,128)(2,1)}, bf16[528,128]{1,0:T(8,128)(2,1)S(1)}, bf16[528,128]{1,0:T(8,128)(2,1)S(1)}, bf16[528,128]{1,0:T(8,128)(...) custom-call(bf16[1,1048576]{1,0:T(2,128)(2,1)} %row_ref.1, ...), custom_call_target="tpu_custom_call" | custom-call | bytes 7766016 | tf_op jit(solution)/shard_map/split_pieces/pallas_call | solution.py:431
  3.7 4.6 %all-to-all-start = ((bf16[8,736,128]{2,1,0:T(8,128)(2,1)}), bf16[8,736,128]{2,1,0:T(8,128)(2,1)S(1)}, u32[]{:S(2)}, u32[]{:S(2)}) async-start(bf16[8,736,128]{2,1,0:T(8,128)(2,1)} %get-tuple-element.32), calls=%async_computation | async-start | bytes 3014656 | tf_op jit(solution)/shard_map/all_to_all | solution.py:780
  8.2 2.3 %collective-permute-start = (bf16[528,128]{1,0:T(8,128)(2,1)S(1)}, bf16[528,128]{1,0:T(8,128)(2,1)S(1)}, u32[]{:S(2)}, u32[]{:S(2)}) collective-permute-start(bf16[528,128]{1,0:T(8,128)(2,1)S(1)} %get-tuple-element.33), channel_id=1, source_target_pairs={{0,8},{1,9},{2,10},{3,11},{4,12},{5,13},{6,14},{7,15},{8,0},{9,1},... | collective-permute-start | bytes 405512 | tf_op jit(solution)/shard_map/ppermute | solution.py:775
  10.6 0.6 collective-permute-start.1
  11.1 3.2 %collective-permute-start.2 = (bf16[528,128]{1,0:T(8,128)(2,1)S(1)}, bf16[528,128]{1,0:T(8,128)(2,1)S(1)}, u32[]{:S(2)}, u32[]{:S(2)}) collective-permute-start(bf16[528,128]{1,0:T(8,128)(2,1)S(1)} %get-tuple-element.35), channel_id=1, source_target_pairs={{0,10},{1,11},{2,8},{3,9},{4,14},{5,15},{6,12},{7,13},{8,2},{9,3},... | collective-permute-start | bytes 405512 | tf_op jit(solution)/shard_map/ppermute | solution.py:775
  14.3 0.3 collective-permute-start.3
  14.6 1.0 collective-permute-start.4
  15.6 14.9 %collective-permute-done.refs_0_ = bf16[528,128]{1,0:T(8,128)(2,1)S(1)} collective-permute-done((bf16[528,128]{1,0:T(8,128)(2,1)S(1)}, bf16[528,128]{1,0:T(8,128)(2,1)S(1)}, u32[]{:S(2)}, u32[]{:S(2)}) %collective-permute-start) | collective-permute-done | bytes 135200 | tf_op jit(solution)/shard_map/ppermute | solution.py:775
  30.6 0.0 collective-permute-start.5
  30.6 3.6 %collective-permute-done.1.refs_1_ = bf16[528,128]{1,0:T(8,128)(2,1)S(1)} collective-permute-done((bf16[528,128]{1,0:T(8,128)(2,1)S(1)}, bf16[528,128]{1,0:T(8,128)(2,1)S(1)}, u32[]{:S(2)}, u32[]{:S(2)}) %collective-permute-start.1) | collective-permute-done | bytes 135200 | tf_op jit(solution)/shard_map/ppermute | solution.py:775
  34.2 0.3 collective-permute-start.6
  34.5 2.8 %collective-permute-done.2.refs_2_ = bf16[528,128]{1,0:T(8,128)(2,1)S(1)} collective-permute-done((bf16[528,128]{1,0:T(8,128)(2,1)S(1)}, bf16[528,128]{1,0:T(8,128)(2,1)S(1)}, u32[]{:S(2)}, u32[]{:S(2)}) %collective-permute-start.2) | collective-permute-done | bytes 135200 | tf_op jit(solution)/shard_map/ppermute | solution.py:775
  37.3 0.0 collective-permute-start.7
  37.3 3.6 %collective-permute-done.3.refs_3_ = bf16[528,128]{1,0:T(8,128)(2,1)S(1)} collective-permute-done((bf16[528,128]{1,0:T(8,128)(2,1)}, bf16[528,128]{1,0:T(8,128)(2,1)S(1)}, u32[]{:S(2)}, u32[]{:S(2)}) %collective-permute-start.3) | collective-permute-done | bytes 135200 | tf_op jit(solution)/shard_map/ppermute | solution.py:775
  40.9 0.0 collective-permute-done.4.refs_4_.refs_0_
  40.9 13.2 %collective-permute-done.5.refs_5_.refs_1_ = bf16[528,128]{1,0:T(8,128)(2,1)S(1)} collective-permute-done((bf16[528,128]{1,0:T(8,128)(2,1)S(1)}, bf16[528,128]{1,0:T(8,128)(2,1)S(1)}, u32[]{:S(2)}, u32[]{:S(2)}) %collective-permute-start.5) | collective-permute-done | bytes 135200 | tf_op jit(solution)/shard_map/ppermute | solution.py:775
  54.2 3.8 %collective-permute-done.6.refs_6_.refs_2_ = bf16[528,128]{1,0:T(8,128)(2,1)S(1)} collective-permute-done((bf16[528,128]{1,0:T(8,128)(2,1)S(1)}, bf16[528,128]{1,0:T(8,128)(2,1)S(1)}, u32[]{:S(2)}, u32[]{:S(2)}) %collective-permute-start.6) | collective-permute-done | bytes 135200 | tf_op jit(solution)/shard_map/ppermute | solution.py:775
  58.0 2.9 %collective-permute-done.7.refs_7_.refs_3_ = bf16[528,128]{1,0:T(8,128)(2,1)S(1)} collective-permute-done((bf16[528,128]{1,0:T(8,128)(2,1)S(1)}, bf16[528,128]{1,0:T(8,128)(2,1)S(1)}, u32[]{:S(2)}, u32[]{:S(2)}) %collective-permute-start.7) | collective-permute-done | bytes 135200 | tf_op jit(solution)/shard_map/ppermute | solution.py:775
  60.9 0.0 all-to-all-done.near_ref.refs_0_
  60.9 0.1 collective-permute-start.8
  62.9 1.8 %gradient_pieces.4 = (bf16[4,512,128]{2,1,0:T(8,128)(2,1)}, f32[8,128]{1,0:T(8,128)S(1)}) custom-call(bf16[528,128]{1,0:T(8,128)(2,1)S(1)} %collective-permute-done.refs_0_, bf16[528,128]{1,0:T(8,128)(2,1)S(1)} %collective-permute-done.1.refs_1_, bf16[528,128]{1,0:T(8,128)(2,1)S(1)} %collective-permute-done.2.refs_2_, ...), custom_call_target="tpu_custom_call" | custom-call | flops 7864320 | bytes 2097152 | tf_op jit(solution)/shard_map/gradient_pieces/pallas_call | solution.py:594
  64.7 2.4 %gram_pieces.1 = f32[16,16,128]{2,1,0:T(8,128)} custom-call(bf16[8,736,128]{2,1,0:T(8,128)(2,1)S(1)} %all-to-all-done.near_ref.refs_0_, bf16[528,128]{1,0:T(8,128)(2,1)S(1)} %collective-permute-done.refs_0_, bf16[528,128]{1,0:T(8,128)(2,1)S(1)} %collective-permute-done.1.refs_1_, bf16[528,128]{1,0:T(8,128)(2,1)S(1)} %collective-permute-done.2.refs_2_, ...), custom_call_target="tpu_custom_call" | custom-call | flops 536870912 | bytes 2097152 | tf_op jit(solution)/shard_map/gram_pieces/pallas_call | solution.py:521
  67.1 5.8 %all-to-all-start.1 = ((f32[16,16,128]{2,1,0:T(8,128)}), f32[16,16,128]{2,1,0:T(8,128)S(1)}, u32[]{:S(2)}, u32[]{:S(2)}) async-start(f32[16,16,128]{2,1,0:T(8,128)} %gram_pieces.1), calls=%async_computation.1 | async-start | bytes 262144 | tf_op jit(solution)/shard_map/all_to_all | solution.py:365
  72.9 2.4 %gradient_pieces.6 = (bf16[4,512,128]{2,1,0:T(8,128)(2,1)}, f32[8,128]{1,0:T(8,128)}) custom-call(bf16[528,128]{1,0:T(8,128)(2,1)S(1)} %collective-permute-done.4.refs_4_.refs_0_, bf16[528,128]{1,0:T(8,128)(2,1)S(1)} %collective-permute-done.5.refs_5_.refs_1_, bf16[528,128]{1,0:T(8,128)(2,1)S(1)} %collective-permute-done.6.refs_6_.refs_2_, ...), custom_call_target="tpu_custom_call" | custom-call | flops 7864320 | bytes 2097152 | tf_op jit(solution)/shard_map/gradient_pieces/pallas_call | solution.py:594
  75.3 2.0 %gradient_pieces.5 = (bf16[8,192,128]{2,1,0:T(8,128)(2,1)}, f32[8,128]{1,0:T(8,128)}) custom-call(bf16[8,736,128]{2,1,0:T(8,128)(2,1)S(1)} %all-to-all-done.near_ref.refs_0_, bf16[192,128]{1,0:T(8,128)(2,1)S(1)} %get-tuple-element.41.refs_1_.refs_9_, bf16[192,128]{1,0:T(8,128)(2,1)S(1)} %get-tuple-element.42.refs_2_.refs_10_), custom_call_target="tpu_custom_call" | custom-call | flops 5898240 | bytes 1572864 | tf_op jit(solution)/shard_map/gradient_pieces/pallas_call | solution.py:594
  77.3 3.2 %gradient_pieces.7 = (bf16[8,512,128]{2,1,0:T(8,128)(2,1)}, f32[8,128]{1,0:T(8,128)}) custom-call(bf16[8,736,128]{2,1,0:T(8,128)(2,1)S(1)} %all-to-all-done.near_ref.refs_0_, bf16[512,128]{1,0:T(8,128)(2,1)S(1)} %get-tuple-element.43.refs_4_.refs_1_, bf16[512,128]{1,0:T(8,128)(2,1)S(1)} %get-tuple-element.44.refs_5_.refs_2_), custom_call_target="tpu_custom_call" | custom-call | flops 15728640 | bytes 4194304 | tf_op jit(solution)/shard_map/gradient_pieces/pallas_call | solution.py:594
  80.5 1.9 %all-to-all-done.1.refs_12_ = f32[16,16,128]{2,1,0:T(8,128)S(1)} async-done(((f32[16,16,128]{2,1,0:T(8,128)}), f32[16,16,128]{2,1,0:T(8,128)S(1)}, u32[]{:S(2)}, u32[]{:S(2)}) %all-to-all-start.1) | async-done | bytes 131104 | tf_op jit(solution)/shard_map/all_to_all | solution.py:365
  82.4 0.0 collective-permute-done.8.refs_8_
  82.4 6.6 %update_pieces.1 = (bf16[8,704,128]{2,1,0:T(8,128)(2,1)}, bf16[320,128]{1,0:T(8,128)(2,1)}, bf16[320,128]{1,0:T(8,128)(2,1)}, bf16[320,128]{1,0:T(8,128)(2,1)}, ...) custom-call(bf16[8,736,128]{2,1,0:T(8,128)(2,1)S(1)} %all-to-all-don, ...), custom_call_target="tpu_custom_call" | custom-call | flops 1073741824 | bytes 6291456 | tf_op jit(solution)/shard_map/update_pieces/pallas_call | solution.py:753
  89.1 4.7 %all-to-all-start.2 = ((bf16[8,704,128]{2,1,0:T(8,128)(2,1)}), bf16[8,704,128]{2,1,0:T(8,128)(2,1)S(1)}, u32[]{:S(2)}, u32[]{:S(2)}) async-start(bf16[8,704,128]{2,1,0:T(8,128)(2,1)} %get-tuple-element.50), calls=%async_computation.2 | async-start | bytes 2883584 | tf_op jit(solution)/shard_map/all_to_all | solution.py:780
  93.8 2.8 %collective-permute-start.9 = (bf16[320,128]{1,0:T(8,128)(2,1)S(1)}, bf16[320,128]{1,0:T(8,128)(2,1)S(1)}, u32[]{:S(2)}, u32[]{:S(2)}) collective-permute-start(bf16[320,128]{1,0:T(8,128)(2,1)S(1)} %copy-done.7), channel_id=1, source_target_pairs={{0,8},{1,9},{2,10},{3,11},{4,12},{5,13},{6,14},{7,15},{8,0},{9,1},... | collective-permute-start | bytes 245768 | tf_op jit(solution)/shard_map/ppermute | solution.py:775
  96.6 0.3 collective-permute-start.10
  96.9 3.5 %collective-permute-start.11 = (bf16[320,128]{1,0:T(8,128)(2,1)S(1)}, bf16[320,128]{1,0:T(8,128)(2,1)S(1)}, u32[]{:S(2)}, u32[]{:S(2)}) collective-permute-start(bf16[320,128]{1,0:T(8,128)(2,1)S(1)} %copy-done.5), channel_id=1, source_target_pairs={{0,10},{1,11},{2,8},{3,9},{4,14},{5,15},{6,12},{7,13},{8,2},{9,3},... | collective-permute-start | bytes 245768 | tf_op jit(solution)/shard_map/ppermute | solution.py:775
  100.4 0.3 collective-permute-start.12
  100.7 0.9 collective-permute-start.13
  101.7 13.1 %collective-permute-done.9.refs_1_ = bf16[320,128]{1,0:T(8,128)(2,1)S(1)} collective-permute-done((bf16[320,128]{1,0:T(8,128)(2,1)S(1)}, bf16[320,128]{1,0:T(8,128)(2,1)S(1)}, u32[]{:S(2)}, u32[]{:S(2)}) %collective-permute-start.9) | collective-permute-done | bytes 81952 | tf_op jit(solution)/shard_map/ppermute | solution.py:775
  114.8 0.0 collective-permute-start.14
  114.8 2.4 %collective-permute-done.10.refs_2_ = bf16[320,128]{1,0:T(8,128)(2,1)S(1)} collective-permute-done((bf16[320,128]{1,0:T(8,128)(2,1)S(1)}, bf16[320,128]{1,0:T(8,128)(2,1)S(1)}, u32[]{:S(2)}, u32[]{:S(2)}) %collective-permute-start.10) | collective-permute-done | bytes 81952 | tf_op jit(solution)/shard_map/ppermute | solution.py:775
  117.2 1.2 collective-permute-start.15
  118.4 0.8 collective-permute-done.11.refs_3_
  119.2 0.3 collective-permute-start.16
  119.5 3.2 %join_pieces.4.refs_0_ = bf16[1,1048576]{1,0:T(2,128)(2,1)} custom-call(bf16[8,704,128]{2,1,0:T(8,128)(2,1)S(1)} %all-to-all-done.2.refs_0_), custom_call_target="tpu_custom_call" | custom-call | bytes 4325376 | tf_op jit(solution)/shard_map/join_pieces/pallas_call | solution.py:467
  122.7 0.9 join_pieces.5.refs_0_
  123.6 5.6 %collective-permute-done.14.refs_2_ = bf16[320,128]{1,0:T(8,128)(2,1)S(1)} collective-permute-done((bf16[320,128]{1,0:T(8,128)(2,1)S(1)}, bf16[320,128]{1,0:T(8,128)(2,1)S(1)}, u32[]{:S(2)}, u32[]{:S(2)}) %collective-permute-start.14) | collective-permute-done | bytes 81952 | tf_op jit(solution)/shard_map/ppermute | solution.py:775
  129.2 0.8 join_pieces.6.refs_0_
  130.0 1.9 %collective-permute-done.15.refs_1_ = bf16[320,128]{1,0:T(8,128)(2,1)S(1)} collective-permute-done((bf16[320,128]{1,0:T(8,128)(2,1)S(1)}, bf16[320,128]{1,0:T(8,128)(2,1)S(1)}, u32[]{:S(2)}, u32[]{:S(2)}) %collective-permute-start.15) | collective-permute-done | bytes 81952 | tf_op jit(solution)/shard_map/ppermute | solution.py:775
  131.9 1.8 %collective-permute-done.16.refs_2_ = bf16[320,128]{1,0:T(8,128)(2,1)S(1)} collective-permute-done((bf16[320,128]{1,0:T(8,128)(2,1)S(1)}, bf16[320,128]{1,0:T(8,128)(2,1)S(1)}, u32[]{:S(2)}, u32[]{:S(2)}) %collective-permute-start.16) | collective-permute-done | bytes 81952 | tf_op jit(solution)/shard_map/ppermute | solution.py:775
  133.6 0.8 join_pieces.7
  (20 shorter events, 0.1 us)
Async XLA Ops:
  3.7 57.2 %all-to-all-start = ((bf16[8,736,128]{2,1,0:T(8,128)(2,1)}), bf16[8,736,128]{2,1,0:T(8,128)(2,1)S(1)}, u32[]{:S(2)}, u32[]{:S(2)}) async-start(bf16[8,736,128]{2,1,0:T(8,128)(2,1)} %get-tuple-element.32), calls=%async_computation | async-start | bytes 3014656 | tf_op jit(solution)/shard_map/all_to_all | solution.py:780
  8.2 22.3 %collective-permute-start = (bf16[528,128]{1,0:T(8,128)(2,1)S(1)}, bf16[528,128]{1,0:T(8,128)(2,1)S(1)}, u32[]{:S(2)}, u32[]{:S(2)}) collective-permute-start(bf16[528,128]{1,0:T(8,128)(2,1)S(1)} %get-tuple-element.33), channel_id=1, source_target_pairs={{0,8},{1,9},{2,10},{3,11},{4,12},{5,13},{6,14},{7,15},{8,0},{9,1},... | collective-permute-start | bytes 405512 | tf_op jit(solution)/shard_map/ppermute | solution.py:775
  10.6 23.6 %collective-permute-start.1 = (bf16[528,128]{1,0:T(8,128)(2,1)S(1)}, bf16[528,128]{1,0:T(8,128)(2,1)S(1)}, u32[]{:S(2)}, u32[]{:S(2)}) collective-permute-start(bf16[528,128]{1,0:T(8,128)(2,1)S(1)} %get-tuple-element.34), channel_id=1, source_target_pairs={{0,9},{1,8},{2,11},{3,10},{4,13},{5,12},{6,15},{7,14},{8,1},{9,0},... | collective-permute-start | bytes 405512 | tf_op jit(solution)/shard_map/ppermute | solution.py:775
  11.1 26.2 %collective-permute-start.2 = (bf16[528,128]{1,0:T(8,128)(2,1)S(1)}, bf16[528,128]{1,0:T(8,128)(2,1)S(1)}, u32[]{:S(2)}, u32[]{:S(2)}) collective-permute-start(bf16[528,128]{1,0:T(8,128)(2,1)S(1)} %get-tuple-element.35), channel_id=1, source_target_pairs={{0,10},{1,11},{2,8},{3,9},{4,14},{5,15},{6,12},{7,13},{8,2},{9,3},... | collective-permute-start | bytes 405512 | tf_op jit(solution)/shard_map/ppermute | solution.py:775
  14.3 26.6 %collective-permute-start.3 = (bf16[528,128]{1,0:T(8,128)(2,1)}, bf16[528,128]{1,0:T(8,128)(2,1)S(1)}, u32[]{:S(2)}, u32[]{:S(2)}) collective-permute-start(bf16[528,128]{1,0:T(8,128)(2,1)} %get-tuple-element.36), channel_id=1, source_target_pairs={{0,11},{1,10},{2,9},{3,8},{4,15},{5,14},{6,13},{7,12},{8,3},{9,2},... | collective-permute-start | bytes 405512 | tf_op jit(solution)/shard_map/ppermute | solution.py:775
  14.6 26.3 %collective-permute-start.4 = (bf16[528,128]{1,0:T(8,128)(2,1)}, bf16[528,128]{1,0:T(8,128)(2,1)S(1)}, u32[]{:S(2)}, u32[]{:S(2)}) collective-permute-start(bf16[528,128]{1,0:T(8,128)(2,1)} %get-tuple-element.37), channel_id=1, source_target_pairs={{0,12},{1,13},{2,14},{3,15},{4,8},{5,9},{6,10},{7,11},{8,4},{9,5},... | collective-permute-start | bytes 405512 | tf_op jit(solution)/shard_map/ppermute | solution.py:775
  30.6 23.6 %collective-permute-start.5 = (bf16[528,128]{1,0:T(8,128)(2,1)S(1)}, bf16[528,128]{1,0:T(8,128)(2,1)S(1)}, u32[]{:S(2)}, u32[]{:S(2)}) collective-permute-start(bf16[528,128]{1,0:T(8,128)(2,1)S(1)} %get-tuple-element.38), channel_id=1, source_target_pairs={{0,13},{1,12},{2,15},{3,14},{4,9},{5,8},{6,11},{7,10},{8,5},{9,4},... | collective-permute-start | bytes 405512 | tf_op jit(solution)/shard_map/ppermute | solution.py:775
  34.2 23.8 %collective-permute-start.6 = (bf16[528,128]{1,0:T(8,128)(2,1)S(1)}, bf16[528,128]{1,0:T(8,128)(2,1)S(1)}, u32[]{:S(2)}, u32[]{:S(2)}) collective-permute-start(bf16[528,128]{1,0:T(8,128)(2,1)S(1)} %get-tuple-element.39), channel_id=1, source_target_pairs={{0,14},{1,15},{2,12},{3,13},{4,10},{5,11},{6,8},{7,9},{8,6},{9,7},... | collective-permute-start | bytes 405512 | tf_op jit(solution)/shard_map/ppermute | solution.py:775
  37.3 23.5 %collective-permute-start.7 = (bf16[528,128]{1,0:T(8,128)(2,1)S(1)}, bf16[528,128]{1,0:T(8,128)(2,1)S(1)}, u32[]{:S(2)}, u32[]{:S(2)}) collective-permute-start(bf16[528,128]{1,0:T(8,128)(2,1)S(1)} %get-tuple-element.40), channel_id=1, source_target_pairs={{0,15},{1,14},{2,13},{3,12},{4,11},{5,10},{6,9},{7,8},{8,7},{9,6},... | collective-permute-start | bytes 405512 | tf_op jit(solution)/shard_map/ppermute | solution.py:775
  60.9 21.5 %collective-permute-start.8 = (bf16[8,208,128]{2,1,0:T(8,128)(2,1)S(1)}, bf16[8,208,128]{2,1,0:T(8,128)(2,1)}, u32[]{:S(2)}, u32[]{:S(2)}) collective-permute-start(bf16[8,208,128]{2,1,0:T(8,128)(2,1)S(1)} %raw_states.1.refs_9_), channel_id=1, source_target_pairs={{0,8},{1,9},{2,10},{3,11},{4,12},{5,13},{6,14},{7,15},{8,0},{9,1},... | collective-permute-start | bytes 1277960 | tf_op jit(solution)/shard_map/ppermute | solution.py:775
  67.1 15.3 %all-to-all-start.1 = ((f32[16,16,128]{2,1,0:T(8,128)}), f32[16,16,128]{2,1,0:T(8,128)S(1)}, u32[]{:S(2)}, u32[]{:S(2)}) async-start(f32[16,16,128]{2,1,0:T(8,128)} %gram_pieces.1), calls=%async_computation.1 | async-start | bytes 262144 | tf_op jit(solution)/shard_map/all_to_all | solution.py:365
  89.0 4.8 %copy-start.7 = (bf16[320,128]{1,0:T(8,128)(2,1)S(1)}, bf16[320,128]{1,0:T(8,128)(2,1)}, u32[]{:S(2)}) copy-start(bf16[320,128]{1,0:T(8,128)(2,1)} %get-tuple-element.51) | copy-start | bytes 245764
  89.0 7.6 %copy-start.6 = (bf16[320,128]{1,0:T(8,128)(2,1)S(1)}, bf16[320,128]{1,0:T(8,128)(2,1)}, u32[]{:S(2)}) copy-start(bf16[320,128]{1,0:T(8,128)(2,1)} %get-tuple-element.52) | copy-start | bytes 245764
  89.0 7.9 %copy-start.5 = (bf16[320,128]{1,0:T(8,128)(2,1)S(1)}, bf16[320,128]{1,0:T(8,128)(2,1)}, u32[]{:S(2)}) copy-start(bf16[320,128]{1,0:T(8,128)(2,1)} %get-tuple-element.53) | copy-start | bytes 245764
  89.0 11.4 %copy-start.4 = (bf16[320,128]{1,0:T(8,128)(2,1)S(1)}, bf16[320,128]{1,0:T(8,128)(2,1)}, u32[]{:S(2)}) copy-start(bf16[320,128]{1,0:T(8,128)(2,1)} %get-tuple-element.54) | copy-start | bytes 245764
  89.0 11.7 %copy-start.3 = (bf16[320,128]{1,0:T(8,128)(2,1)S(1)}, bf16[320,128]{1,0:T(8,128)(2,1)}, u32[]{:S(2)}) copy-start(bf16[320,128]{1,0:T(8,128)(2,1)} %get-tuple-element.55) | copy-start | bytes 245764
  89.0 25.7 %copy-start.2 = (bf16[320,128]{1,0:T(8,128)(2,1)S(1)}, bf16[320,128]{1,0:T(8,128)(2,1)}, u32[]{:S(2)}) copy-start(bf16[320,128]{1,0:T(8,128)(2,1)} %get-tuple-element.56) | copy-start | bytes 245764
  89.1 28.1 %copy-start.1 = (bf16[320,128]{1,0:T(8,128)(2,1)S(1)}, bf16[320,128]{1,0:T(8,128)(2,1)}, u32[]{:S(2)}) copy-start(bf16[320,128]{1,0:T(8,128)(2,1)} %get-tuple-element.57) | copy-start | bytes 245764
  89.1 30.1 %copy-start = (bf16[320,128]{1,0:T(8,128)(2,1)S(1)}, bf16[320,128]{1,0:T(8,128)(2,1)}, u32[]{:S(2)}) copy-start(bf16[320,128]{1,0:T(8,128)(2,1)} %get-tuple-element.58) | copy-start | bytes 245764
  89.1 30.4 %all-to-all-start.2 = ((bf16[8,704,128]{2,1,0:T(8,128)(2,1)}), bf16[8,704,128]{2,1,0:T(8,128)(2,1)S(1)}, u32[]{:S(2)}, u32[]{:S(2)}) async-start(bf16[8,704,128]{2,1,0:T(8,128)(2,1)} %get-tuple-element.50), calls=%async_computation.2 | async-start | bytes 2883584 | tf_op jit(solution)/shard_map/all_to_all | solution.py:780
  93.8 20.9 %collective-permute-start.9 = (bf16[320,128]{1,0:T(8,128)(2,1)S(1)}, bf16[320,128]{1,0:T(8,128)(2,1)S(1)}, u32[]{:S(2)}, u32[]{:S(2)}) collective-permute-start(bf16[320,128]{1,0:T(8,128)(2,1)S(1)} %copy-done.7), channel_id=1, source_target_pairs={{0,8},{1,9},{2,10},{3,11},{4,12},{5,13},{6,14},{7,15},{8,0},{9,1},... | collective-permute-start | bytes 245768 | tf_op jit(solution)/shard_map/ppermute | solution.py:775
  96.6 20.6 %collective-permute-start.10 = (bf16[320,128]{1,0:T(8,128)(2,1)S(1)}, bf16[320,128]{1,0:T(8,128)(2,1)S(1)}, u32[]{:S(2)}, u32[]{:S(2)}) collective-permute-start(bf16[320,128]{1,0:T(8,128)(2,1)S(1)} %copy-done.6), channel_id=1, source_target_pairs={{0,9},{1,8},{2,11},{3,10},{4,13},{5,12},{6,15},{7,14},{8,1},{9,0},... | collective-permute-start | bytes 245768 | tf_op jit(solution)/shard_map/ppermute | solution.py:775
  96.9 22.3 %collective-permute-start.11 = (bf16[320,128]{1,0:T(8,128)(2,1)S(1)}, bf16[320,128]{1,0:T(8,128)(2,1)S(1)}, u32[]{:S(2)}, u32[]{:S(2)}) collective-permute-start(bf16[320,128]{1,0:T(8,128)(2,1)S(1)} %copy-done.5), channel_id=1, source_target_pairs={{0,10},{1,11},{2,8},{3,9},{4,14},{5,15},{6,12},{7,13},{8,2},{9,3},... | collective-permute-start | bytes 245768 | tf_op jit(solution)/shard_map/ppermute | solution.py:775
  100.4 22.3 %collective-permute-start.12 = (bf16[320,128]{1,0:T(8,128)(2,1)S(1)}, bf16[320,128]{1,0:T(8,128)(2,1)S(1)}, u32[]{:S(2)}, u32[]{:S(2)}) collective-permute-start(bf16[320,128]{1,0:T(8,128)(2,1)S(1)} %copy-done.4), channel_id=1, source_target_pairs={{0,11},{1,10},{2,9},{3,8},{4,15},{5,14},{6,13},{7,12},{8,3},{9,2},... | collective-permute-start | bytes 245768 | tf_op jit(solution)/shard_map/ppermute | solution.py:775
  100.7 22.9 %collective-permute-start.13 = (bf16[320,128]{1,0:T(8,128)(2,1)S(1)}, bf16[320,128]{1,0:T(8,128)(2,1)S(1)}, u32[]{:S(2)}, u32[]{:S(2)}) collective-permute-start(bf16[320,128]{1,0:T(8,128)(2,1)S(1)} %copy-done.3), channel_id=1, source_target_pairs={{0,12},{1,13},{2,14},{3,15},{4,8},{5,9},{6,10},{7,11},{8,4},{9,5},... | collective-permute-start | bytes 245768 | tf_op jit(solution)/shard_map/ppermute | solution.py:775
  114.8 14.5 %collective-permute-start.14 = (bf16[320,128]{1,0:T(8,128)(2,1)S(1)}, bf16[320,128]{1,0:T(8,128)(2,1)S(1)}, u32[]{:S(2)}, u32[]{:S(2)}) collective-permute-start(bf16[320,128]{1,0:T(8,128)(2,1)S(1)} %copy-done.2), channel_id=1, source_target_pairs={{0,13},{1,12},{2,15},{3,14},{4,9},{5,8},{6,11},{7,10},{8,5},{9,4},... | collective-permute-start | bytes 245768 | tf_op jit(solution)/shard_map/ppermute | solution.py:775
  117.2 14.7 %collective-permute-start.15 = (bf16[320,128]{1,0:T(8,128)(2,1)S(1)}, bf16[320,128]{1,0:T(8,128)(2,1)S(1)}, u32[]{:S(2)}, u32[]{:S(2)}) collective-permute-start(bf16[320,128]{1,0:T(8,128)(2,1)S(1)} %copy-done.1), channel_id=1, source_target_pairs={{0,14},{1,15},{2,12},{3,13},{4,10},{5,11},{6,8},{7,9},{8,6},{9,7},... | collective-permute-start | bytes 245768 | tf_op jit(solution)/shard_map/ppermute | solution.py:775
  119.2 14.5 %collective-permute-start.16 = (bf16[320,128]{1,0:T(8,128)(2,1)S(1)}, bf16[320,128]{1,0:T(8,128)(2,1)S(1)}, u32[]{:S(2)}, u32[]{:S(2)}) collective-permute-start(bf16[320,128]{1,0:T(8,128)(2,1)S(1)} %copy-done), channel_id=1, source_target_pairs={{0,15},{1,14},{2,13},{3,12},{4,11},{5,10},{6,9},{7,8},{8,7},{9,6},... | collective-permute-start | bytes 245768 | tf_op jit(solution)/shard_map/ppermute | solution.py:775

commit v27 on v25

--- a/solution.py
+++ b/solution.py
@@ -511,7 +511,8 @@
     row = lax.broadcasted_iota(jnp.int32, (total, total), 0)
     col = lax.broadcasted_iota(jnp.int32, (total, total), 1)
     gram = jnp.dot((row == device_at(col, half)).astype(F32), gram, **exact)
-    gram = jnp.concatenate([gram, jnp.zeros((total, LANES - total), F32)], axis=1)
+    filler = jnp.zeros((half, LANES - 2 * total), F32)
+    gram = jnp.concatenate([gram[:half], gram[half:], filler], axis=1)
     out_ref[...] = jnp.broadcast_to(gram[None], out_ref.shape)
 
 
@@ -525,7 +526,7 @@
         moved=2 * total * lines * LANES,
         in_specs=[IN_VMEM] * (1 + len(far)) + [IN_HBM] * len(gates) + [IN_VMEM] * len(early),
         out_specs=IN_VMEM,
-        out_shape=jax.ShapeDtypeStruct((total, total, LANES), F32),
+        out_shape=jax.ShapeDtypeStruct((total, total // 2, LANES), F32),
         scratch_shapes=[pltpu.VMEM((wide, wide), F32)],
     )(near, *far, *gates, *early)
 
@@ -667,7 +668,8 @@
         return carry
 
     lax.fori_loop(0, raw // BLOCK, raw_gradient, 0)
-    gram = jnp.sum(grams_ref[...], axis=0)[:, :total]
+    gram = jnp.sum(grams_ref[...], axis=0)
+    gram = jnp.concatenate([gram[:, :total], gram[:, total : 2 * total]], axis=0)
     spread, anneal, step_size = (numbers_ref[k : k + 1, :1] for k in range(3))
     rate = step_size / total
     coeff = 2.0 * anneal / spread

time: 129 us -> 131 us (1.016)
  waiting for transfers between devices: 67.4 us -> 71.8 us
  starting transfers between devices: 33 us -> 31 us
    ppermute x17, waiting for transfers between devices: 65.6 us -> 71.8 us  [exchange(): return lax.ppermute(piece, 'slab', [(i, i ^ k) for i in range(slabs)])]
    all_to_all x1, waiting for transfers between devices: 1.86 us -> 0.01 us  [swap(): lax.all_to_all(slabs, 'slab', split_axis=0, concat_axis=0, tiled=True)]
    ppermute x17, starting transfers between devices: 17.9 us -> 16.3 us  [exchange(): return lax.ppermute(piece, 'slab', [(i, i ^ k) for i in range(slabs)])]
  transfers between devices with their start and end apart: 20 -> 20, of which waited for: 15 -> 14; matrix products, arithmetic and copies ran while one was open for 0% -> 0% of each run, Pallas kernels for 13% -> 12%
where the time goes in v27:
time: 131 us
  waiting for transfers between devices  71.8 us (55%)
  starting transfers between devices  31 us (24%)
  Pallas kernels  25.9 us (20%)
  between operations  2.14 us (2%)
    ppermute x17, waiting for transfers between devices, exchange(): return lax.ppermute(piece, 'slab', [(i, i ^ k) for i in range(slabs)])  71.8 us
    ppermute x17, starting transfers between devices, exchange(): return lax.ppermute(piece, 'slab', [(i, i ^ k) for i in range(slabs)])  16.3 us
    pallas_call x4, Pallas kernels, gradient_pieces(): call(functools.partial(gradient_pieces_body, views, len(arrays), len(numb...  9.08 us
    all_to_all x2, starting transfers between devices, swap_near(): lax.all_to_all(pieces, 'slab', 0, 0, axis_index_groups=groups, tiled=True)  8.93 us
    all_to_all x1, starting transfers between devices, swap(): lax.all_to_all(slabs, 'slab', split_axis=0, concat_axis=0, tiled=True)  5.76 us
    pallas_call x4, Pallas kernels, join_pieces(): call(functools.partial(join_pieces_body, pieces, slabs // 2, raw, NCELL /...  5.55 us
    pallas_call x1, Pallas kernels, update_pieces(): call(functools.partial(update_pieces_body, half, raw, lines, groups), 'up...  5.28 us
    pallas_call x1, Pallas kernels, split_pieces(): call(functools.partial(split_pieces_body, slabs, raw, lines, len(fields))...  3.55 us
  transfers between devices with their start and end apart: 20, of which 14 were waited for; matrix products, arithmetic and copies ran while one was open for 0% of the time, Pallas kernels for 12%

profile of v27, /device:TPU:9, one launch (start us, length us, event | category | flops | bytes accessed | tf_op | source)
XLA Modules:
  0.0 130.9 jit_solution(9780587304992922200)
XLA Ops:
  0.0 3.6 %split_pieces.1 = (bf16[8,672,128]{2,1,0:T(8,128)(2,1)}, bf16[528,128]{1,0:T(8,128)(2,1)S(1)}, bf16[528,128]{1,0:T(8,128)(2,1)S(1)}, bf16[528,128]{1,0:T(8,128)(...) custom-call(bf16[1,1048576]{1,0:T(2,128)(2,1)} %row_ref.1, ...), custom_call_target="tpu_custom_call" | custom-call | bytes 7372800 | tf_op jit(solution)/shard_map/split_pieces/pallas_call | solution.py:431
  3.6 4.6 %all-to-all-start = ((bf16[8,672,128]{2,1,0:T(8,128)(2,1)}), bf16[8,672,128]{2,1,0:T(8,128)(2,1)S(1)}, u32[]{:S(2)}, u32[]{:S(2)}) async-start(bf16[8,672,128]{2,1,0:T(8,128)(2,1)} %get-tuple-element.32), calls=%async_computation | async-start | bytes 2752512 | tf_op jit(solution)/shard_map/all_to_all | solution.py:782
  8.1 2.3 %collective-permute-start = (bf16[528,128]{1,0:T(8,128)(2,1)S(1)}, bf16[528,128]{1,0:T(8,128)(2,1)S(1)}, u32[]{:S(2)}, u32[]{:S(2)}) collective-permute-start(bf16[528,128]{1,0:T(8,128)(2,1)S(1)} %get-tuple-element.33), channel_id=1, source_target_pairs={{0,8},{1,9},{2,10},{3,11},{4,12},{5,13},{6,14},{7,15},{8,0},{9,1},... | collective-permute-start | bytes 405512 | tf_op jit(solution)/shard_map/ppermute | solution.py:777
  10.5 0.6 collective-permute-start.1
  11.0 3.2 %collective-permute-start.2 = (bf16[528,128]{1,0:T(8,128)(2,1)S(1)}, bf16[528,128]{1,0:T(8,128)(2,1)S(1)}, u32[]{:S(2)}, u32[]{:S(2)}) collective-permute-start(bf16[528,128]{1,0:T(8,128)(2,1)S(1)} %get-tuple-element.35), channel_id=1, source_target_pairs={{0,10},{1,11},{2,8},{3,9},{4,14},{5,15},{6,12},{7,13},{8,2},{9,3},... | collective-permute-start | bytes 405512 | tf_op jit(solution)/shard_map/ppermute | solution.py:777
  14.2 0.3 collective-permute-start.3
  14.5 1.0 collective-permute-start.4
  15.5 13.5 %collective-permute-done.refs_0_ = bf16[528,128]{1,0:T(8,128)(2,1)S(1)} collective-permute-done((bf16[528,128]{1,0:T(8,128)(2,1)S(1)}, bf16[528,128]{1,0:T(8,128)(2,1)S(1)}, u32[]{:S(2)}, u32[]{:S(2)}) %collective-permute-start) | collective-permute-done | bytes 135200 | tf_op jit(solution)/shard_map/ppermute | solution.py:777
  29.1 0.0 collective-permute-start.5
  29.1 3.6 %collective-permute-done.1.refs_1_ = bf16[528,128]{1,0:T(8,128)(2,1)S(1)} collective-permute-done((bf16[528,128]{1,0:T(8,128)(2,1)S(1)}, bf16[528,128]{1,0:T(8,128)(2,1)S(1)}, u32[]{:S(2)}, u32[]{:S(2)}) %collective-permute-start.1) | collective-permute-done | bytes 135200 | tf_op jit(solution)/shard_map/ppermute | solution.py:777
  32.7 0.3 collective-permute-start.6
  33.0 2.8 %collective-permute-done.2.refs_2_ = bf16[528,128]{1,0:T(8,128)(2,1)S(1)} collective-permute-done((bf16[528,128]{1,0:T(8,128)(2,1)S(1)}, bf16[528,128]{1,0:T(8,128)(2,1)S(1)}, u32[]{:S(2)}, u32[]{:S(2)}) %collective-permute-start.2) | collective-permute-done | bytes 135200 | tf_op jit(solution)/shard_map/ppermute | solution.py:777
  35.8 0.0 collective-permute-start.7
  35.8 3.6 %collective-permute-done.3.refs_3_ = bf16[528,128]{1,0:T(8,128)(2,1)S(1)} collective-permute-done((bf16[528,128]{1,0:T(8,128)(2,1)}, bf16[528,128]{1,0:T(8,128)(2,1)S(1)}, u32[]{:S(2)}, u32[]{:S(2)}) %collective-permute-start.3) | collective-permute-done | bytes 135200 | tf_op jit(solution)/shard_map/ppermute | solution.py:777
  39.4 8.5 %collective-permute-done.4.refs_4_.refs_0_ = bf16[528,128]{1,0:T(8,128)(2,1)S(1)} collective-permute-done((bf16[528,128]{1,0:T(8,128)(2,1)S(1)}, bf16[528,128]{1,0:T(8,128)(2,1)S(1)}, u32[]{:S(2)}, u32[]{:S(2)}) %collective-permute-start.4) | collective-permute-done | bytes 135200 | tf_op jit(solution)/shard_map/ppermute | solution.py:777
  47.9 4.7 %collective-permute-done.5.refs_5_.refs_1_ = bf16[528,128]{1,0:T(8,128)(2,1)S(1)} collective-permute-done((bf16[528,128]{1,0:T(8,128)(2,1)S(1)}, bf16[528,128]{1,0:T(8,128)(2,1)S(1)}, u32[]{:S(2)}, u32[]{:S(2)}) %collective-permute-start.5) | collective-permute-done | bytes 135200 | tf_op jit(solution)/shard_map/ppermute | solution.py:777
  52.7 3.8 %collective-permute-done.6.refs_6_.refs_2_ = bf16[528,128]{1,0:T(8,128)(2,1)S(1)} collective-permute-done((bf16[528,128]{1,0:T(8,128)(2,1)S(1)}, bf16[528,128]{1,0:T(8,128)(2,1)S(1)}, u32[]{:S(2)}, u32[]{:S(2)}) %collective-permute-start.6) | collective-permute-done | bytes 135200 | tf_op jit(solution)/shard_map/ppermute | solution.py:777
  56.5 2.9 %collective-permute-done.7.refs_7_.refs_3_ = bf16[528,128]{1,0:T(8,128)(2,1)S(1)} collective-permute-done((bf16[528,128]{1,0:T(8,128)(2,1)S(1)}, bf16[528,128]{1,0:T(8,128)(2,1)S(1)}, u32[]{:S(2)}, u32[]{:S(2)}) %collective-permute-start.7) | collective-permute-done | bytes 135200 | tf_op jit(solution)/shard_map/ppermute | solution.py:777
  59.4 0.0 all-to-all-done.near_ref.refs_0_
  59.4 0.1 collective-permute-start.8
  61.4 1.8 %gradient_pieces.4 = (bf16[4,512,128]{2,1,0:T(8,128)(2,1)}, f32[8,128]{1,0:T(8,128)S(1)}) custom-call(bf16[528,128]{1,0:T(8,128)(2,1)S(1)} %collective-permute-done.refs_0_, bf16[528,128]{1,0:T(8,128)(2,1)S(1)} %collective-permute-done.1.refs_1_, bf16[528,128]{1,0:T(8,128)(2,1)S(1)} %collective-permute-done.2.refs_2_, ...), custom_call_target="tpu_custom_call" | custom-call | flops 7864320 | bytes 2097152 | tf_op jit(solution)/shard_map/gradient_pieces/pallas_call | solution.py:595
  63.2 2.5 %gram_pieces.1 = f32[16,8,128]{2,1,0:T(8,128)} custom-call(bf16[8,672,128]{2,1,0:T(8,128)(2,1)S(1)} %all-to-all-done.near_ref.refs_0_, bf16[528,128]{1,0:T(8,128)(2,1)S(1)} %collective-permute-done.refs_0_, bf16[528,128]{1,0:T(8,128)(2,1)S(1)} %collective-permute-done.1.refs_1_, bf16[528,128]{1,0:T(8,128)(2,1)S(1)} %collective-permute-done.2.refs_2_, ...), custom_call_target="tpu_custom_call" | custom-call | flops 536870912 | bytes 2097152 | tf_op jit(solution)/shard_map/gram_pieces/pallas_call | solution.py:522
  65.7 5.8 %all-to-all-start.1 = ((f32[16,8,128]{2,1,0:T(8,128)}), f32[16,8,128]{2,1,0:T(8,128)S(1)}, u32[]{:S(2)}, u32[]{:S(2)}) async-start(f32[16,8,128]{2,1,0:T(8,128)} %gram_pieces.1), calls=%async_computation.1 | async-start | bytes 131072 | tf_op jit(solution)/shard_map/all_to_all | solution.py:365
  71.4 2.4 %gradient_pieces.6 = (bf16[4,512,128]{2,1,0:T(8,128)(2,1)}, f32[8,128]{1,0:T(8,128)}) custom-call(bf16[528,128]{1,0:T(8,128)(2,1)S(1)} %collective-permute-done.4.refs_4_.refs_0_, bf16[528,128]{1,0:T(8,128)(2,1)S(1)} %collective-permute-done.5.refs_5_.refs_1_, bf16[528,128]{1,0:T(8,128)(2,1)S(1)} %collective-permute-done.6.refs_6_.refs_2_, ...), custom_call_target="tpu_custom_call" | custom-call | flops 7864320 | bytes 2097152 | tf_op jit(solution)/shard_map/gradient_pieces/pallas_call | solution.py:595
  73.8 1.7 %gradient_pieces.5 = (bf16[8,128,128]{2,1,0:T(8,128)(2,1)}, f32[8,128]{1,0:T(8,128)}) custom-call(bf16[8,672,128]{2,1,0:T(8,128)(2,1)S(1)} %all-to-all-done.near_ref.refs_0_, bf16[128,128]{1,0:T(8,128)(2,1)S(1)} %get-tuple-element.41.refs_1_.refs_9_, bf16[128,128]{1,0:T(8,128)(2,1)S(1)} %get-tuple-element.42.refs_2_.refs_10_), custom_call_target="tpu_custom_call" | custom-call | flops 3932160 | bytes 1048576 | tf_op jit(solution)/shard_map/gradient_pieces/pallas_call | solution.py:595
  75.6 3.2 %gradient_pieces.7 = (bf16[8,512,128]{2,1,0:T(8,128)(2,1)}, f32[8,128]{1,0:T(8,128)}) custom-call(bf16[8,672,128]{2,1,0:T(8,128)(2,1)S(1)} %all-to-all-done.near_ref.refs_0_, bf16[512,128]{1,0:T(8,128)(2,1)S(1)} %get-tuple-element.43.refs_4_.refs_1_, bf16[512,128]{1,0:T(8,128)(2,1)S(1)} %get-tuple-element.44.refs_5_.refs_2_), custom_call_target="tpu_custom_call" | custom-call | flops 15728640 | bytes 4194304 | tf_op jit(solution)/shard_map/gradient_pieces/pallas_call | solution.py:595
  78.7 0.0 all-to-all-done.1.refs_12_
  78.8 5.3 %update_pieces.1 = (bf16[8,640,128]{2,1,0:T(8,128)(2,1)}, bf16[384,128]{1,0:T(8,128)(2,1)}, bf16[384,128]{1,0:T(8,128)(2,1)}, bf16[384,128]{1,0:T(8,128)(2,1)}, ...) custom-call(bf16[8,672,128]{2,1,0:T(8,128)(2,1)S(1)} %all-to-all-don, ...), custom_call_target="tpu_custom_call" | custom-call | flops 1073741824 | bytes 6291456 | tf_op jit(solution)/shard_map/update_pieces/pallas_call | solution.py:755
  84.1 4.3 %all-to-all-start.2 = ((bf16[8,640,128]{2,1,0:T(8,128)(2,1)}), bf16[8,640,128]{2,1,0:T(8,128)(2,1)S(1)}, u32[]{:S(2)}, u32[]{:S(2)}) async-start(bf16[8,640,128]{2,1,0:T(8,128)(2,1)} %get-tuple-element.50), calls=%async_computation.2 | async-start | bytes 2621440 | tf_op jit(solution)/shard_map/all_to_all | solution.py:782
  88.5 2.1 %collective-permute-start.9 = (bf16[384,128]{1,0:T(8,128)(2,1)S(1)}, bf16[384,128]{1,0:T(8,128)(2,1)S(1)}, u32[]{:S(2)}, u32[]{:S(2)}) collective-permute-start(bf16[384,128]{1,0:T(8,128)(2,1)S(1)} %copy-done.7), channel_id=1, source_target_pairs={{0,8},{1,9},{2,10},{3,11},{4,12},{5,13},{6,14},{7,15},{8,0},{9,1},... | collective-permute-start | bytes 294920 | tf_op jit(solution)/shard_map/ppermute | solution.py:777
  90.6 0.8 collective-permute-start.10
  91.4 3.0 %collective-permute-start.11 = (bf16[384,128]{1,0:T(8,128)(2,1)S(1)}, bf16[384,128]{1,0:T(8,128)(2,1)S(1)}, u32[]{:S(2)}, u32[]{:S(2)}) collective-permute-start(bf16[384,128]{1,0:T(8,128)(2,1)S(1)} %copy-done.5), channel_id=1, source_target_pairs={{0,10},{1,11},{2,8},{3,9},{4,14},{5,15},{6,12},{7,13},{8,2},{9,3},... | collective-permute-start | bytes 294920 | tf_op jit(solution)/shard_map/ppermute | solution.py:777
  94.4 0.3 collective-permute-start.12
  94.7 0.9 collective-permute-start.13
  95.7 12.0 %collective-permute-done.9.refs_1_ = bf16[384,128]{1,0:T(8,128)(2,1)S(1)} collective-permute-done((bf16[384,128]{1,0:T(8,128)(2,1)S(1)}, bf16[384,128]{1,0:T(8,128)(2,1)S(1)}, u32[]{:S(2)}, u32[]{:S(2)}) %collective-permute-start.9) | collective-permute-done | bytes 98336 | tf_op jit(solution)/shard_map/ppermute | solution.py:777
  107.7 0.2 collective-permute-start.14
  107.8 2.6 %collective-permute-done.10.refs_2_ = bf16[384,128]{1,0:T(8,128)(2,1)S(1)} collective-permute-done((bf16[384,128]{1,0:T(8,128)(2,1)S(1)}, bf16[384,128]{1,0:T(8,128)(2,1)S(1)}, u32[]{:S(2)}, u32[]{:S(2)}) %collective-permute-start.10) | collective-permute-done | bytes 98336 | tf_op jit(solution)/shard_map/ppermute | solution.py:777
  110.4 0.8 collective-permute-start.15
  111.3 1.5 %collective-permute-done.11.refs_3_ = bf16[384,128]{1,0:T(8,128)(2,1)S(1)} collective-permute-done((bf16[384,128]{1,0:T(8,128)(2,1)S(1)}, bf16[384,128]{1,0:T(8,128)(2,1)S(1)}, u32[]{:S(2)}, u32[]{:S(2)}) %collective-permute-start.11) | collective-permute-done | bytes 98336 | tf_op jit(solution)/shard_map/ppermute | solution.py:777
  112.8 0.3 collective-permute-start.16
  113.1 3.0 %join_pieces.4.refs_0_ = bf16[1,1048576]{1,0:T(2,128)(2,1)} custom-call(bf16[8,640,128]{2,1,0:T(8,128)(2,1)S(1)} %all-to-all-done.2.refs_0_), custom_call_target="tpu_custom_call" | custom-call | bytes 3932160 | tf_op jit(solution)/shard_map/join_pieces/pallas_call | solution.py:467
  116.0 0.0 collective-permute-done.12.refs_4_
  116.0 1.0 join_pieces.5.refs_0_
  117.0 7.9 %collective-permute-done.14.refs_2_ = bf16[384,128]{1,0:T(8,128)(2,1)S(1)} collective-permute-done((bf16[384,128]{1,0:T(8,128)(2,1)S(1)}, bf16[384,128]{1,0:T(8,128)(2,1)S(1)}, u32[]{:S(2)}, u32[]{:S(2)}) %collective-permute-start.14) | collective-permute-done | bytes 98336 | tf_op jit(solution)/shard_map/ppermute | solution.py:777
  124.9 0.8 join_pieces.6.refs_0_
  125.8 2.2 %collective-permute-done.15.refs_1_ = bf16[384,128]{1,0:T(8,128)(2,1)S(1)} collective-permute-done((bf16[384,128]{1,0:T(8,128)(2,1)S(1)}, bf16[384,128]{1,0:T(8,128)(2,1)S(1)}, u32[]{:S(2)}, u32[]{:S(2)}) %collective-permute-start.15) | collective-permute-done | bytes 98336 | tf_op jit(solution)/shard_map/ppermute | solution.py:777
  128.0 2.1 %collective-permute-done.16.refs_2_ = bf16[384,128]{1,0:T(8,128)(2,1)S(1)} collective-permute-done((bf16[384,128]{1,0:T(8,128)(2,1)S(1)}, bf16[384,128]{1,0:T(8,128)(2,1)S(1)}, u32[]{:S(2)}, u32[]{:S(2)}) %collective-permute-start.16) | collective-permute-done | bytes 98336 | tf_op jit(solution)/shard_map/ppermute | solution.py:777
  130.1 0.8 join_pieces.7
  (20 shorter events, 0.1 us)
Async XLA Ops:
  3.6 55.8 %all-to-all-start = ((bf16[8,672,128]{2,1,0:T(8,128)(2,1)}), bf16[8,672,128]{2,1,0:T(8,128)(2,1)S(1)}, u32[]{:S(2)}, u32[]{:S(2)}) async-start(bf16[8,672,128]{2,1,0:T(8,128)(2,1)} %get-tuple-element.32), calls=%async_computation | async-start | bytes 2752512 | tf_op jit(solution)/shard_map/all_to_all | solution.py:782
  8.1 20.9 %collective-permute-start = (bf16[528,128]{1,0:T(8,128)(2,1)S(1)}, bf16[528,128]{1,0:T(8,128)(2,1)S(1)}, u32[]{:S(2)}, u32[]{:S(2)}) collective-permute-start(bf16[528,128]{1,0:T(8,128)(2,1)S(1)} %get-tuple-element.33), channel_id=1, source_target_pairs={{0,8},{1,9},{2,10},{3,11},{4,12},{5,13},{6,14},{7,15},{8,0},{9,1},... | collective-permute-start | bytes 405512 | tf_op jit(solution)/shard_map/ppermute | solution.py:777
  10.5 22.2 %collective-permute-start.1 = (bf16[528,128]{1,0:T(8,128)(2,1)S(1)}, bf16[528,128]{1,0:T(8,128)(2,1)S(1)}, u32[]{:S(2)}, u32[]{:S(2)}) collective-permute-start(bf16[528,128]{1,0:T(8,128)(2,1)S(1)} %get-tuple-element.34), channel_id=1, source_target_pairs={{0,9},{1,8},{2,11},{3,10},{4,13},{5,12},{6,15},{7,14},{8,1},{9,0},... | collective-permute-start | bytes 405512 | tf_op jit(solution)/shard_map/ppermute | solution.py:777
  11.0 24.8 %collective-permute-start.2 = (bf16[528,128]{1,0:T(8,128)(2,1)S(1)}, bf16[528,128]{1,0:T(8,128)(2,1)S(1)}, u32[]{:S(2)}, u32[]{:S(2)}) collective-permute-start(bf16[528,128]{1,0:T(8,128)(2,1)S(1)} %get-tuple-element.35), channel_id=1, source_target_pairs={{0,10},{1,11},{2,8},{3,9},{4,14},{5,15},{6,12},{7,13},{8,2},{9,3},... | collective-permute-start | bytes 405512 | tf_op jit(solution)/shard_map/ppermute | solution.py:777
  14.2 25.2 %collective-permute-start.3 = (bf16[528,128]{1,0:T(8,128)(2,1)}, bf16[528,128]{1,0:T(8,128)(2,1)S(1)}, u32[]{:S(2)}, u32[]{:S(2)}) collective-permute-start(bf16[528,128]{1,0:T(8,128)(2,1)} %get-tuple-element.36), channel_id=1, source_target_pairs={{0,11},{1,10},{2,9},{3,8},{4,15},{5,14},{6,13},{7,12},{8,3},{9,2},... | collective-permute-start | bytes 405512 | tf_op jit(solution)/shard_map/ppermute | solution.py:777
  14.5 33.4 %collective-permute-start.4 = (bf16[528,128]{1,0:T(8,128)(2,1)S(1)}, bf16[528,128]{1,0:T(8,128)(2,1)S(1)}, u32[]{:S(2)}, u32[]{:S(2)}) collective-permute-start(bf16[528,128]{1,0:T(8,128)(2,1)S(1)} %get-tuple-element.37), channel_id=1, source_target_pairs={{0,12},{1,13},{2,14},{3,15},{4,8},{5,9},{6,10},{7,11},{8,4},{9,5},... | collective-permute-start | bytes 405512 | tf_op jit(solution)/shard_map/ppermute | solution.py:777
  29.1 23.6 %collective-permute-start.5 = (bf16[528,128]{1,0:T(8,128)(2,1)S(1)}, bf16[528,128]{1,0:T(8,128)(2,1)S(1)}, u32[]{:S(2)}, u32[]{:S(2)}) collective-permute-start(bf16[528,128]{1,0:T(8,128)(2,1)S(1)} %get-tuple-element.38), channel_id=1, source_target_pairs={{0,13},{1,12},{2,15},{3,14},{4,9},{5,8},{6,11},{7,10},{8,5},{9,4},... | collective-permute-start | bytes 405512 | tf_op jit(solution)/shard_map/ppermute | solution.py:777
  32.7 23.8 %collective-permute-start.6 = (bf16[528,128]{1,0:T(8,128)(2,1)S(1)}, bf16[528,128]{1,0:T(8,128)(2,1)S(1)}, u32[]{:S(2)}, u32[]{:S(2)}) collective-permute-start(bf16[528,128]{1,0:T(8,128)(2,1)S(1)} %get-tuple-element.39), channel_id=1, source_target_pairs={{0,14},{1,15},{2,12},{3,13},{4,10},{5,11},{6,8},{7,9},{8,6},{9,7},... | collective-permute-start | bytes 405512 | tf_op jit(solution)/shard_map/ppermute | solution.py:777
  35.8 23.5 %collective-permute-start.7 = (bf16[528,128]{1,0:T(8,128)(2,1)S(1)}, bf16[528,128]{1,0:T(8,128)(2,1)S(1)}, u32[]{:S(2)}, u32[]{:S(2)}) collective-permute-start(bf16[528,128]{1,0:T(8,128)(2,1)S(1)} %get-tuple-element.40), channel_id=1, source_target_pairs={{0,15},{1,14},{2,13},{3,12},{4,11},{5,10},{6,9},{7,8},{8,7},{9,6},... | collective-permute-start | bytes 405512 | tf_op jit(solution)/shard_map/ppermute | solution.py:777
  59.4 19.4 %collective-permute-start.8 = (bf16[8,144,128]{2,1,0:T(8,128)(2,1)S(1)}, bf16[8,144,128]{2,1,0:T(8,128)(2,1)S(1)}, u32[]{:S(2)}, u32[]{:S(2)}) collective-permute-start(bf16[8,144,128]{2,1,0:T(8,128)(2,1)S(1)} %raw_states.1.refs_9_), channel_id=1, source_target_pairs={{0,8},{1,9},{2,10},{3,11},{4,12},{5,13},{6,14},{7,15},{8,0},{9,1},... | collective-permute-start | bytes 884744 | tf_op jit(solution)/shard_map/ppermute | solution.py:777
  65.7 13.1 %all-to-all-start.1 = ((f32[16,8,128]{2,1,0:T(8,128)}), f32[16,8,128]{2,1,0:T(8,128)S(1)}, u32[]{:S(2)}, u32[]{:S(2)}) async-start(f32[16,8,128]{2,1,0:T(8,128)} %gram_pieces.1), calls=%async_computation.1 | async-start | bytes 131072 | tf_op jit(solution)/shard_map/all_to_all | solution.py:365
  84.0 4.4 %copy-start.7 = (bf16[384,128]{1,0:T(8,128)(2,1)S(1)}, bf16[384,128]{1,0:T(8,128)(2,1)}, u32[]{:S(2)}) copy-start(bf16[384,128]{1,0:T(8,128)(2,1)} %get-tuple-element.51) | copy-start | bytes 294916
  84.1 6.5 %copy-start.6 = (bf16[384,128]{1,0:T(8,128)(2,1)S(1)}, bf16[384,128]{1,0:T(8,128)(2,1)}, u32[]{:S(2)}) copy-start(bf16[384,128]{1,0:T(8,128)(2,1)} %get-tuple-element.52) | copy-start | bytes 294916
  84.1 7.3 %copy-start.5 = (bf16[384,128]{1,0:T(8,128)(2,1)S(1)}, bf16[384,128]{1,0:T(8,128)(2,1)}, u32[]{:S(2)}) copy-start(bf16[384,128]{1,0:T(8,128)(2,1)} %get-tuple-element.53) | copy-start | bytes 294916
  84.1 10.3 %copy-start.4 = (bf16[384,128]{1,0:T(8,128)(2,1)S(1)}, bf16[384,128]{1,0:T(8,128)(2,1)}, u32[]{:S(2)}) copy-start(bf16[384,128]{1,0:T(8,128)(2,1)} %get-tuple-element.54) | copy-start | bytes 294916
  84.1 10.6 %copy-start.3 = (bf16[384,128]{1,0:T(8,128)(2,1)S(1)}, bf16[384,128]{1,0:T(8,128)(2,1)}, u32[]{:S(2)}) copy-start(bf16[384,128]{1,0:T(8,128)(2,1)} %get-tuple-element.55) | copy-start | bytes 294916
  84.1 23.6 %copy-start.2 = (bf16[384,128]{1,0:T(8,128)(2,1)S(1)}, bf16[384,128]{1,0:T(8,128)(2,1)}, u32[]{:S(2)}) copy-start(bf16[384,128]{1,0:T(8,128)(2,1)} %get-tuple-element.56) | copy-start | bytes 294916
  84.1 26.3 %copy-start.1 = (bf16[384,128]{1,0:T(8,128)(2,1)S(1)}, bf16[384,128]{1,0:T(8,128)(2,1)}, u32[]{:S(2)}) copy-start(bf16[384,128]{1,0:T(8,128)(2,1)} %get-tuple-element.57) | copy-start | bytes 294916
  84.1 28.7 %copy-start = (bf16[384,128]{1,0:T(8,128)(2,1)S(1)}, bf16[384,128]{1,0:T(8,128)(2,1)}, u32[]{:S(2)}) copy-start(bf16[384,128]{1,0:T(8,128)(2,1)} %get-tuple-element.58) | copy-start | bytes 294916
  84.1 28.9 %all-to-all-start.2 = ((bf16[8,640,128]{2,1,0:T(8,128)(2,1)}), bf16[8,640,128]{2,1,0:T(8,128)(2,1)S(1)}, u32[]{:S(2)}, u32[]{:S(2)}) async-start(bf16[8,640,128]{2,1,0:T(8,128)(2,1)} %get-tuple-element.50), calls=%async_computation.2 | async-start | bytes 2621440 | tf_op jit(solution)/shard_map/all_to_all | solution.py:782
  88.5 19.2 %collective-permute-start.9 = (bf16[384,128]{1,0:T(8,128)(2,1)S(1)}, bf16[384,128]{1,0:T(8,128)(2,1)S(1)}, u32[]{:S(2)}, u32[]{:S(2)}) collective-permute-start(bf16[384,128]{1,0:T(8,128)(2,1)S(1)} %copy-done.7), channel_id=1, source_target_pairs={{0,8},{1,9},{2,10},{3,11},{4,12},{5,13},{6,14},{7,15},{8,0},{9,1},... | collective-permute-start | bytes 294920 | tf_op jit(solution)/shard_map/ppermute | solution.py:777
  90.6 19.9 %collective-permute-start.10 = (bf16[384,128]{1,0:T(8,128)(2,1)S(1)}, bf16[384,128]{1,0:T(8,128)(2,1)S(1)}, u32[]{:S(2)}, u32[]{:S(2)}) collective-permute-start(bf16[384,128]{1,0:T(8,128)(2,1)S(1)} %copy-done.6), channel_id=1, source_target_pairs={{0,9},{1,8},{2,11},{3,10},{4,13},{5,12},{6,15},{7,14},{8,1},{9,0},... | collective-permute-start | bytes 294920 | tf_op jit(solution)/shard_map/ppermute | solution.py:777
  91.4 21.4 %collective-permute-start.11 = (bf16[384,128]{1,0:T(8,128)(2,1)S(1)}, bf16[384,128]{1,0:T(8,128)(2,1)S(1)}, u32[]{:S(2)}, u32[]{:S(2)}) collective-permute-start(bf16[384,128]{1,0:T(8,128)(2,1)S(1)} %copy-done.5), channel_id=1, source_target_pairs={{0,10},{1,11},{2,8},{3,9},{4,14},{5,15},{6,12},{7,13},{8,2},{9,3},... | collective-permute-start | bytes 294920 | tf_op jit(solution)/shard_map/ppermute | solution.py:777
  94.4 21.7 %collective-permute-start.12 = (bf16[384,128]{1,0:T(8,128)(2,1)S(1)}, bf16[384,128]{1,0:T(8,128)(2,1)S(1)}, u32[]{:S(2)}, u32[]{:S(2)}) collective-permute-start(bf16[384,128]{1,0:T(8,128)(2,1)S(1)} %copy-done.4), channel_id=1, source_target_pairs={{0,11},{1,10},{2,9},{3,8},{4,15},{5,14},{6,13},{7,12},{8,3},{9,2},... | collective-permute-start | bytes 294920 | tf_op jit(solution)/shard_map/ppermute | solution.py:777
  94.7 22.3 %collective-permute-start.13 = (bf16[384,128]{1,0:T(8,128)(2,1)S(1)}, bf16[384,128]{1,0:T(8,128)(2,1)S(1)}, u32[]{:S(2)}, u32[]{:S(2)}) collective-permute-start(bf16[384,128]{1,0:T(8,128)(2,1)S(1)} %copy-done.3), channel_id=1, source_target_pairs={{0,12},{1,13},{2,14},{3,15},{4,8},{5,9},{6,10},{7,11},{8,4},{9,5},... | collective-permute-start | bytes 294920 | tf_op jit(solution)/shard_map/ppermute | solution.py:777
  107.7 17.3 %collective-permute-start.14 = (bf16[384,128]{1,0:T(8,128)(2,1)S(1)}, bf16[384,128]{1,0:T(8,128)(2,1)S(1)}, u32[]{:S(2)}, u32[]{:S(2)}) collective-permute-start(bf16[384,128]{1,0:T(8,128)(2,1)S(1)} %copy-done.2), channel_id=1, source_target_pairs={{0,13},{1,12},{2,15},{3,14},{4,9},{5,8},{6,11},{7,10},{8,5},{9,4},... | collective-permute-start | bytes 294920 | tf_op jit(solution)/shard_map/ppermute | solution.py:777
  110.4 17.5 %collective-permute-start.15 = (bf16[384,128]{1,0:T(8,128)(2,1)S(1)}, bf16[384,128]{1,0:T(8,128)(2,1)S(1)}, u32[]{:S(2)}, u32[]{:S(2)}) collective-permute-start(bf16[384,128]{1,0:T(8,128)(2,1)S(1)} %copy-done.1), channel_id=1, source_target_pairs={{0,14},{1,15},{2,12},{3,13},{4,10},{5,11},{6,8},{7,9},{8,6},{9,7},... | collective-permute-start | bytes 294920 | tf_op jit(solution)/shard_map/ppermute | solution.py:777
  112.8 17.3 %collective-permute-start.16 = (bf16[384,128]{1,0:T(8,128)(2,1)S(1)}, bf16[384,128]{1,0:T(8,128)(2,1)S(1)}, u32[]{:S(2)}, u32[]{:S(2)}) collective-permute-start(bf16[384,128]{1,0:T(8,128)(2,1)S(1)} %copy-done), channel_id=1, source_target_pairs={{0,15},{1,14},{2,13},{3,12},{4,11},{5,10},{6,9},{7,8},{8,7},{9,6},... | collective-permute-start | bytes 294920 | tf_op jit(solution)/shard_map/ppermute | solution.py:777

commit v28 on v27

--- a/solution.py
+++ b/solution.py
@@ -796,8 +796,6 @@
     far, (obs, prec, *raw_fields) = far[:half], far[half:]
     near = swap_near(near, slabs)
     far = [exchange(piece, half + x, slabs) for x, piece in enumerate(far)]
-    raw_near = raw_states(near, RAW, lines, far)
-    across = exchange(raw_near, half, slabs)
     grads = []
     numbers = [spread, anneal, step_size]
     for group in GRADIENTS:
@@ -808,6 +806,8 @@
         slopes, rows = gradient_pieces(arrays, tuple(views), obs, prec, [] if grads else numbers)
         grads.append(in_hbm(slopes))
         numbers = numbers if len(grads) > 1 else rows
+    raw_near = raw_states(near, RAW, lines, [*far, numbers])
+    across = exchange(raw_near, half, slabs)
     grams = swap(gram_pieces(near, far, lines, grads[:1], [raw_near]))
     views = tuple((0, k, lines + TILE) for k in range(half))
     raw_grads = in_hbm(gradient_pieces([near], views, *raw_fields, [])[0])

time: 131 us -> 127 us (0.969)
  waiting for transfers between devices: 71.8 us -> 65.4 us
  starting transfers between devices: 31 us -> 33.6 us
    ppermute x17, waiting for transfers between devices: 71.8 us -> 64.9 us  [exchange(): return lax.ppermute(piece, 'slab', [(i, i ^ k) for i in range(slabs)])]
    ppermute x17, starting transfers between devices: 16.3 us -> 18.3 us  [exchange(): return lax.ppermute(piece, 'slab', [(i, i ^ k) for i in range(slabs)])]
  transfers between devices with their start and end apart: 20 -> 20, of which waited for: 14 -> 15; matrix products, arithmetic and copies ran while one was open for 0% -> 0% of each run, Pallas kernels for 12% -> 13%
where the time goes in v28:
time: 127 us
  waiting for transfers between devices  65.4 us (51%)
  starting transfers between devices  33.6 us (26%)
  Pallas kernels  25.9 us (20%)
  between operations  2.13 us (2%)
    ppermute x17, waiting for transfers between devices, exchange(): return lax.ppermute(piece, 'slab', [(i, i ^ k) for i in range(slabs)])  64.9 us
    ppermute x17, starting transfers between devices, exchange(): return lax.ppermute(piece, 'slab', [(i, i ^ k) for i in range(slabs)])  18.3 us
    all_to_all x2, starting transfers between devices, swap_near(): lax.all_to_all(pieces, 'slab', 0, 0, axis_index_groups=groups, tiled=True)  9.54 us
    pallas_call x4, Pallas kernels, gradient_pieces(): call(functools.partial(gradient_pieces_body, views, len(arrays), len(numb...  9.06 us
    all_to_all x1, starting transfers between devices, swap(): lax.all_to_all(slabs, 'slab', split_axis=0, concat_axis=0, tiled=True)  5.75 us
    pallas_call x4, Pallas kernels, join_pieces(): call(functools.partial(join_pieces_body, pieces, slabs // 2, raw, NCELL /...  5.54 us
    pallas_call x1, Pallas kernels, update_pieces(): call(functools.partial(update_pieces_body, half, raw, lines, groups), 'up...  5.25 us
    pallas_call x1, Pallas kernels, split_pieces(): call(functools.partial(split_pieces_body, slabs, raw, lines, len(fields))...  3.55 us
  transfers between devices with their start and end apart: 20, of which 15 were waited for; matrix products, arithmetic and copies ran while one was open for 0% of the time, Pallas kernels for 13%

profile of v28, /device:TPU:9, one launch (start us, length us, event | category | flops | bytes accessed | tf_op | source)
XLA Modules:
  0.0 127.1 jit_solution(7234873750724570527)
XLA Ops:
  0.0 3.6 %split_pieces.1 = (bf16[8,672,128]{2,1,0:T(8,128)(2,1)}, bf16[528,128]{1,0:T(8,128)(2,1)S(1)}, bf16[528,128]{1,0:T(8,128)(2,1)S(1)}, bf16[528,128]{1,0:T(8,128)(...) custom-call(bf16[1,1048576]{1,0:T(2,128)(2,1)} %row_ref.1, ...), custom_call_target="tpu_custom_call" | custom-call | bytes 7372800 | tf_op jit(solution)/shard_map/split_pieces/pallas_call | solution.py:431
  3.6 4.6 %all-to-all-start = ((bf16[8,672,128]{2,1,0:T(8,128)(2,1)}), bf16[8,672,128]{2,1,0:T(8,128)(2,1)S(1)}, u32[]{:S(2)}, u32[]{:S(2)}) async-start(bf16[8,672,128]{2,1,0:T(8,128)(2,1)} %get-tuple-element.32), calls=%async_computation | async-start | bytes 2752512 | tf_op jit(solution)/shard_map/all_to_all | solution.py:782
  8.1 2.3 %collective-permute-start = (bf16[528,128]{1,0:T(8,128)(2,1)S(1)}, bf16[528,128]{1,0:T(8,128)(2,1)S(1)}, u32[]{:S(2)}, u32[]{:S(2)}) collective-permute-start(bf16[528,128]{1,0:T(8,128)(2,1)S(1)} %get-tuple-element.33), channel_id=1, source_target_pairs={{0,8},{1,9},{2,10},{3,11},{4,12},{5,13},{6,14},{7,15},{8,0},{9,1},... | collective-permute-start | bytes 405512 | tf_op jit(solution)/shard_map/ppermute | solution.py:777
  10.5 0.6 collective-permute-start.1
  11.0 3.2 %collective-permute-start.2 = (bf16[528,128]{1,0:T(8,128)(2,1)S(1)}, bf16[528,128]{1,0:T(8,128)(2,1)S(1)}, u32[]{:S(2)}, u32[]{:S(2)}) collective-permute-start(bf16[528,128]{1,0:T(8,128)(2,1)S(1)} %get-tuple-element.35), channel_id=1, source_target_pairs={{0,10},{1,11},{2,8},{3,9},{4,14},{5,15},{6,12},{7,13},{8,2},{9,3},... | collective-permute-start | bytes 405512 | tf_op jit(solution)/shard_map/ppermute | solution.py:777
  14.2 0.3 collective-permute-start.3
  14.5 1.0 collective-permute-start.4
  15.5 13.5 %collective-permute-done.refs_0_ = bf16[528,128]{1,0:T(8,128)(2,1)S(1)} collective-permute-done((bf16[528,128]{1,0:T(8,128)(2,1)S(1)}, bf16[528,128]{1,0:T(8,128)(2,1)S(1)}, u32[]{:S(2)}, u32[]{:S(2)}) %collective-permute-start) | collective-permute-done | bytes 135200 | tf_op jit(solution)/shard_map/ppermute | solution.py:777
  29.1 0.0 collective-permute-start.5
  29.1 3.6 %collective-permute-done.1.refs_1_ = bf16[528,128]{1,0:T(8,128)(2,1)S(1)} collective-permute-done((bf16[528,128]{1,0:T(8,128)(2,1)S(1)}, bf16[528,128]{1,0:T(8,128)(2,1)S(1)}, u32[]{:S(2)}, u32[]{:S(2)}) %collective-permute-start.1) | collective-permute-done | bytes 135200 | tf_op jit(solution)/shard_map/ppermute | solution.py:777
  32.7 0.3 collective-permute-start.6
  33.0 2.8 %collective-permute-done.2.refs_2_ = bf16[528,128]{1,0:T(8,128)(2,1)S(1)} collective-permute-done((bf16[528,128]{1,0:T(8,128)(2,1)S(1)}, bf16[528,128]{1,0:T(8,128)(2,1)S(1)}, u32[]{:S(2)}, u32[]{:S(2)}) %collective-permute-start.2) | collective-permute-done | bytes 135200 | tf_op jit(solution)/shard_map/ppermute | solution.py:777
  35.8 0.0 collective-permute-start.7
  37.8 1.7 %collective-permute-done.3.refs_3_ = bf16[528,128]{1,0:T(8,128)(2,1)S(1)} collective-permute-done((bf16[528,128]{1,0:T(8,128)(2,1)}, bf16[528,128]{1,0:T(8,128)(2,1)S(1)}, u32[]{:S(2)}, u32[]{:S(2)}) %collective-permute-start.3) | collective-permute-done | bytes 135200 | tf_op jit(solution)/shard_map/ppermute | solution.py:777
  39.4 1.8 %gradient_pieces.4 = (bf16[4,512,128]{2,1,0:T(8,128)(2,1)}, f32[8,128]{1,0:T(8,128)S(1)}) custom-call(bf16[528,128]{1,0:T(8,128)(2,1)S(1)} %collective-permute-done.refs_0_, bf16[528,128]{1,0:T(8,128)(2,1)S(1)} %collective-permute-done.1.refs_1_, bf16[528,128]{1,0:T(8,128)(2,1)S(1)} %collective-permute-done.2.refs_2_, ...), custom_call_target="tpu_custom_call" | custom-call | flops 7864320 | bytes 2097152 | tf_op jit(solution)/shard_map/gradient_pieces/pallas_call | solution.py:595
  41.2 6.7 %collective-permute-done.4.refs_4_.refs_0_ = bf16[528,128]{1,0:T(8,128)(2,1)S(1)} collective-permute-done((bf16[528,128]{1,0:T(8,128)(2,1)S(1)}, bf16[528,128]{1,0:T(8,128)(2,1)S(1)}, u32[]{:S(2)}, u32[]{:S(2)}) %collective-permute-start.4) | collective-permute-done | bytes 135200 | tf_op jit(solution)/shard_map/ppermute | solution.py:777
  47.9 4.7 %collective-permute-done.5.refs_5_.refs_1_ = bf16[528,128]{1,0:T(8,128)(2,1)S(1)} collective-permute-done((bf16[528,128]{1,0:T(8,128)(2,1)S(1)}, bf16[528,128]{1,0:T(8,128)(2,1)S(1)}, u32[]{:S(2)}, u32[]{:S(2)}) %collective-permute-start.5) | collective-permute-done | bytes 135200 | tf_op jit(solution)/shard_map/ppermute | solution.py:777
  52.7 3.8 %collective-permute-done.6.refs_6_.refs_2_ = bf16[528,128]{1,0:T(8,128)(2,1)S(1)} collective-permute-done((bf16[528,128]{1,0:T(8,128)(2,1)S(1)}, bf16[528,128]{1,0:T(8,128)(2,1)S(1)}, u32[]{:S(2)}, u32[]{:S(2)}) %collective-permute-start.6) | collective-permute-done | bytes 135200 | tf_op jit(solution)/shard_map/ppermute | solution.py:777
  56.5 2.9 %collective-permute-done.7.refs_7_.refs_3_ = bf16[528,128]{1,0:T(8,128)(2,1)S(1)} collective-permute-done((bf16[528,128]{1,0:T(8,128)(2,1)S(1)}, bf16[528,128]{1,0:T(8,128)(2,1)S(1)}, u32[]{:S(2)}, u32[]{:S(2)}) %collective-permute-start.7) | collective-permute-done | bytes 135200 | tf_op jit(solution)/shard_map/ppermute | solution.py:777
  59.4 0.1 collective-permute-start.8
  59.5 2.5 %gram_pieces.1 = f32[16,8,128]{2,1,0:T(8,128)} custom-call(bf16[8,672,128]{2,1,0:T(8,128)(2,1)S(1)} %all-to-all-done.near_ref.refs_0_, bf16[528,128]{1,0:T(8,128)(2,1)S(1)} %collective-permute-done.refs_0_, bf16[528,128]{1,0:T(8,128)(2,1)S(1)} %collective-permute-done.1.refs_1_, bf16[528,128]{1,0:T(8,128)(2,1)S(1)} %collective-permute-done.2.refs_2_, ...), custom_call_target="tpu_custom_call" | custom-call | flops 536870912 | bytes 2097152 | tf_op jit(solution)/shard_map/gram_pieces/pallas_call | solution.py:522
  61.9 5.7 %all-to-all-start.1 = ((f32[16,8,128]{2,1,0:T(8,128)}), f32[16,8,128]{2,1,0:T(8,128)S(1)}, u32[]{:S(2)}, u32[]{:S(2)}) async-start(f32[16,8,128]{2,1,0:T(8,128)} %gram_pieces.1), calls=%async_computation.1 | async-start | bytes 131072 | tf_op jit(solution)/shard_map/all_to_all | solution.py:365
  67.7 2.4 %gradient_pieces.6 = (bf16[4,512,128]{2,1,0:T(8,128)(2,1)}, f32[8,128]{1,0:T(8,128)}) custom-call(bf16[528,128]{1,0:T(8,128)(2,1)S(1)} %collective-permute-done.4.refs_4_.refs_0_, bf16[528,128]{1,0:T(8,128)(2,1)S(1)} %collective-permute-done.5.refs_5_.refs_1_, bf16[528,128]{1,0:T(8,128)(2,1)S(1)} %collective-permute-done.6.refs_6_.refs_2_, ...), custom_call_target="tpu_custom_call" | custom-call | flops 7864320 | bytes 2097152 | tf_op jit(solution)/shard_map/gradient_pieces/pallas_call | solution.py:595
  70.1 1.7 %gradient_pieces.5 = (bf16[8,128,128]{2,1,0:T(8,128)(2,1)}, f32[8,128]{1,0:T(8,128)}) custom-call(bf16[8,672,128]{2,1,0:T(8,128)(2,1)S(1)} %all-to-all-done.near_ref.refs_0_, bf16[128,128]{1,0:T(8,128)(2,1)S(1)} %get-tuple-element.44.refs_1_.refs_9_, bf16[128,128]{1,0:T(8,128)(2,1)S(1)} %get-tuple-element.45.refs_2_.refs_10_), custom_call_target="tpu_custom_call" | custom-call | flops 3932160 | bytes 1048576 | tf_op jit(solution)/shard_map/gradient_pieces/pallas_call | solution.py:595
  71.8 3.2 %gradient_pieces.7 = (bf16[8,512,128]{2,1,0:T(8,128)(2,1)}, f32[8,128]{1,0:T(8,128)}) custom-call(bf16[8,672,128]{2,1,0:T(8,128)(2,1)S(1)} %all-to-all-done.near_ref.refs_0_, bf16[512,128]{1,0:T(8,128)(2,1)S(1)} %get-tuple-element.41.refs_4_.refs_1_, bf16[512,128]{1,0:T(8,128)(2,1)S(1)} %get-tuple-element.42.refs_5_.refs_2_), custom_call_target="tpu_custom_call" | custom-call | flops 15728640 | bytes 4194304 | tf_op jit(solution)/shard_map/gradient_pieces/pallas_call | solution.py:595
  75.0 0.5 all-to-all-done.1.refs_12_
  75.5 0.0 collective-permute-done.8.refs_8_
  75.5 5.2 %update_pieces.1 = (bf16[8,640,128]{2,1,0:T(8,128)(2,1)}, bf16[384,128]{1,0:T(8,128)(2,1)}, bf16[384,128]{1,0:T(8,128)(2,1)}, bf16[384,128]{1,0:T(8,128)(2,1)}, ...) custom-call(bf16[8,672,128]{2,1,0:T(8,128)(2,1)S(1)} %all-to-all-don, ...), custom_call_target="tpu_custom_call" | custom-call | flops 1073741824 | bytes 6291456 | tf_op jit(solution)/shard_map/update_pieces/pallas_call | solution.py:755
  80.8 5.0 %all-to-all-start.2 = ((bf16[8,640,128]{2,1,0:T(8,128)(2,1)}), bf16[8,640,128]{2,1,0:T(8,128)(2,1)S(1)}, u32[]{:S(2)}, u32[]{:S(2)}) async-start(bf16[8,640,128]{2,1,0:T(8,128)(2,1)} %get-tuple-element.50), calls=%async_computation.2 | async-start | bytes 2621440 | tf_op jit(solution)/shard_map/all_to_all | solution.py:782
  85.8 1.0 collective-permute-start.9
  86.8 1.9 %collective-permute-start.10 = (bf16[384,128]{1,0:T(8,128)(2,1)S(1)}, bf16[384,128]{1,0:T(8,128)(2,1)S(1)}, u32[]{:S(2)}, u32[]{:S(2)}) collective-permute-start(bf16[384,128]{1,0:T(8,128)(2,1)S(1)} %copy-done.6), channel_id=1, source_target_pairs={{0,9},{1,8},{2,11},{3,10},{4,13},{5,12},{6,15},{7,14},{8,1},{9,0},... | collective-permute-start | bytes 294920 | tf_op jit(solution)/shard_map/ppermute | solution.py:777
  88.7 1.9 %collective-permute-start.11 = (bf16[384,128]{1,0:T(8,128)(2,1)S(1)}, bf16[384,128]{1,0:T(8,128)(2,1)S(1)}, u32[]{:S(2)}, u32[]{:S(2)}) collective-permute-start(bf16[384,128]{1,0:T(8,128)(2,1)S(1)} %copy-done.5), channel_id=1, source_target_pairs={{0,10},{1,11},{2,8},{3,9},{4,14},{5,15},{6,12},{7,13},{8,2},{9,3},... | collective-permute-start | bytes 294920 | tf_op jit(solution)/shard_map/ppermute | solution.py:777
  90.6 1.4 %collective-permute-start.12 = (bf16[384,128]{1,0:T(8,128)(2,1)S(1)}, bf16[384,128]{1,0:T(8,128)(2,1)S(1)}, u32[]{:S(2)}, u32[]{:S(2)}) collective-permute-start(bf16[384,128]{1,0:T(8,128)(2,1)S(1)} %copy-done.4), channel_id=1, source_target_pairs={{0,11},{1,10},{2,9},{3,8},{4,15},{5,14},{6,13},{7,12},{8,3},{9,2},... | collective-permute-start | bytes 294920 | tf_op jit(solution)/shard_map/ppermute | solution.py:777
  92.0 0.0 collective-permute-start.13
  92.0 11.9 %collective-permute-done.9.refs_1_ = bf16[384,128]{1,0:T(8,128)(2,1)S(1)} collective-permute-done((bf16[384,128]{1,0:T(8,128)(2,1)S(1)}, bf16[384,128]{1,0:T(8,128)(2,1)S(1)}, u32[]{:S(2)}, u32[]{:S(2)}) %collective-permute-start.9) | collective-permute-done | bytes 98336 | tf_op jit(solution)/shard_map/ppermute | solution.py:777
  103.9 1.3 %collective-permute-start.14 = (bf16[384,128]{1,0:T(8,128)(2,1)S(1)}, bf16[384,128]{1,0:T(8,128)(2,1)S(1)}, u32[]{:S(2)}, u32[]{:S(2)}) collective-permute-start(bf16[384,128]{1,0:T(8,128)(2,1)S(1)} %copy-done.2), channel_id=1, source_target_pairs={{0,13},{1,12},{2,15},{3,14},{4,9},{5,8},{6,11},{7,10},{8,5},{9,4},... | collective-permute-start | bytes 294920 | tf_op jit(solution)/shard_map/ppermute | solution.py:777
  105.2 1.5 %collective-permute-done.10.refs_2_ = bf16[384,128]{1,0:T(8,128)(2,1)S(1)} collective-permute-done((bf16[384,128]{1,0:T(8,128)(2,1)S(1)}, bf16[384,128]{1,0:T(8,128)(2,1)S(1)}, u32[]{:S(2)}, u32[]{:S(2)}) %collective-permute-start.10) | collective-permute-done | bytes 98336 | tf_op jit(solution)/shard_map/ppermute | solution.py:777
  106.7 1.6 %collective-permute-start.15 = (bf16[384,128]{1,0:T(8,128)(2,1)S(1)}, bf16[384,128]{1,0:T(8,128)(2,1)S(1)}, u32[]{:S(2)}, u32[]{:S(2)}) collective-permute-start(bf16[384,128]{1,0:T(8,128)(2,1)S(1)} %copy-done.1), channel_id=1, source_target_pairs={{0,14},{1,15},{2,12},{3,13},{4,10},{5,11},{6,8},{7,9},{8,6},{9,7},... | collective-permute-start | bytes 294920 | tf_op jit(solution)/shard_map/ppermute | solution.py:777
  108.3 0.7 collective-permute-done.11.refs_3_
  109.0 1.4 %collective-permute-start.16 = (bf16[384,128]{1,0:T(8,128)(2,1)S(1)}, bf16[384,128]{1,0:T(8,128)(2,1)S(1)}, u32[]{:S(2)}, u32[]{:S(2)}) collective-permute-start(bf16[384,128]{1,0:T(8,128)(2,1)S(1)} %copy-done), channel_id=1, source_target_pairs={{0,15},{1,14},{2,13},{3,12},{4,11},{5,10},{6,9},{7,8},{8,7},{9,6},... | collective-permute-start | bytes 294920 | tf_op jit(solution)/shard_map/ppermute | solution.py:777
  110.4 3.0 %join_pieces.4.refs_0_ = bf16[1,1048576]{1,0:T(2,128)(2,1)} custom-call(bf16[8,640,128]{2,1,0:T(8,128)(2,1)S(1)} %all-to-all-done.2.refs_0_), custom_call_target="tpu_custom_call" | custom-call | bytes 3932160 | tf_op jit(solution)/shard_map/join_pieces/pallas_call | solution.py:467
  113.4 0.0 collective-permute-done.12.refs_4_
  113.4 1.0 join_pieces.5.refs_0_
  114.4 6.8 %collective-permute-done.14.refs_2_ = bf16[384,128]{1,0:T(8,128)(2,1)S(1)} collective-permute-done((bf16[384,128]{1,0:T(8,128)(2,1)S(1)}, bf16[384,128]{1,0:T(8,128)(2,1)S(1)}, u32[]{:S(2)}, u32[]{:S(2)}) %collective-permute-start.14) | collective-permute-done | bytes 98336 | tf_op jit(solution)/shard_map/ppermute | solution.py:777
  121.2 0.8 join_pieces.6.refs_0_
  122.0 2.2 %collective-permute-done.15.refs_1_ = bf16[384,128]{1,0:T(8,128)(2,1)S(1)} collective-permute-done((bf16[384,128]{1,0:T(8,128)(2,1)S(1)}, bf16[384,128]{1,0:T(8,128)(2,1)S(1)}, u32[]{:S(2)}, u32[]{:S(2)}) %collective-permute-start.15) | collective-permute-done | bytes 98336 | tf_op jit(solution)/shard_map/ppermute | solution.py:777
  124.2 2.1 %collective-permute-done.16.refs_2_ = bf16[384,128]{1,0:T(8,128)(2,1)S(1)} collective-permute-done((bf16[384,128]{1,0:T(8,128)(2,1)S(1)}, bf16[384,128]{1,0:T(8,128)(2,1)S(1)}, u32[]{:S(2)}, u32[]{:S(2)}) %collective-permute-start.16) | collective-permute-done | bytes 98336 | tf_op jit(solution)/shard_map/ppermute | solution.py:777
  126.3 0.8 join_pieces.7
  (20 shorter events, 0.1 us)
Async XLA Ops:
  3.6 55.8 %all-to-all-start = ((bf16[8,672,128]{2,1,0:T(8,128)(2,1)}), bf16[8,672,128]{2,1,0:T(8,128)(2,1)S(1)}, u32[]{:S(2)}, u32[]{:S(2)}) async-start(bf16[8,672,128]{2,1,0:T(8,128)(2,1)} %get-tuple-element.32), calls=%async_computation | async-start | bytes 2752512 | tf_op jit(solution)/shard_map/all_to_all | solution.py:782
  8.1 20.9 %collective-permute-start = (bf16[528,128]{1,0:T(8,128)(2,1)S(1)}, bf16[528,128]{1,0:T(8,128)(2,1)S(1)}, u32[]{:S(2)}, u32[]{:S(2)}) collective-permute-start(bf16[528,128]{1,0:T(8,128)(2,1)S(1)} %get-tuple-element.33), channel_id=1, source_target_pairs={{0,8},{1,9},{2,10},{3,11},{4,12},{5,13},{6,14},{7,15},{8,0},{9,1},... | collective-permute-start | bytes 405512 | tf_op jit(solution)/shard_map/ppermute | solution.py:777
  10.5 22.2 %collective-permute-start.1 = (bf16[528,128]{1,0:T(8,128)(2,1)S(1)}, bf16[528,128]{1,0:T(8,128)(2,1)S(1)}, u32[]{:S(2)}, u32[]{:S(2)}) collective-permute-start(bf16[528,128]{1,0:T(8,128)(2,1)S(1)} %get-tuple-element.34), channel_id=1, source_target_pairs={{0,9},{1,8},{2,11},{3,10},{4,13},{5,12},{6,15},{7,14},{8,1},{9,0},... | collective-permute-start | bytes 405512 | tf_op jit(solution)/shard_map/ppermute | solution.py:777
  11.0 24.8 %collective-permute-start.2 = (bf16[528,128]{1,0:T(8,128)(2,1)S(1)}, bf16[528,128]{1,0:T(8,128)(2,1)S(1)}, u32[]{:S(2)}, u32[]{:S(2)}) collective-permute-start(bf16[528,128]{1,0:T(8,128)(2,1)S(1)} %get-tuple-element.35), channel_id=1, source_target_pairs={{0,10},{1,11},{2,8},{3,9},{4,14},{5,15},{6,12},{7,13},{8,2},{9,3},... | collective-permute-start | bytes 405512 | tf_op jit(solution)/shard_map/ppermute | solution.py:777
  14.2 25.2 %collective-permute-start.3 = (bf16[528,128]{1,0:T(8,128)(2,1)}, bf16[528,128]{1,0:T(8,128)(2,1)S(1)}, u32[]{:S(2)}, u32[]{:S(2)}) collective-permute-start(bf16[528,128]{1,0:T(8,128)(2,1)} %get-tuple-element.36), channel_id=1, source_target_pairs={{0,11},{1,10},{2,9},{3,8},{4,15},{5,14},{6,13},{7,12},{8,3},{9,2},... | collective-permute-start | bytes 405512 | tf_op jit(solution)/shard_map/ppermute | solution.py:777
  14.5 33.4 %collective-permute-start.4 = (bf16[528,128]{1,0:T(8,128)(2,1)S(1)}, bf16[528,128]{1,0:T(8,128)(2,1)S(1)}, u32[]{:S(2)}, u32[]{:S(2)}) collective-permute-start(bf16[528,128]{1,0:T(8,128)(2,1)S(1)} %get-tuple-element.37), channel_id=1, source_target_pairs={{0,12},{1,13},{2,14},{3,15},{4,8},{5,9},{6,10},{7,11},{8,4},{9,5},... | collective-permute-start | bytes 405512 | tf_op jit(solution)/shard_map/ppermute | solution.py:777
  29.1 23.6 %collective-permute-start.5 = (bf16[528,128]{1,0:T(8,128)(2,1)S(1)}, bf16[528,128]{1,0:T(8,128)(2,1)S(1)}, u32[]{:S(2)}, u32[]{:S(2)}) collective-permute-start(bf16[528,128]{1,0:T(8,128)(2,1)S(1)} %get-tuple-element.38), channel_id=1, source_target_pairs={{0,13},{1,12},{2,15},{3,14},{4,9},{5,8},{6,11},{7,10},{8,5},{9,4},... | collective-permute-start | bytes 405512 | tf_op jit(solution)/shard_map/ppermute | solution.py:777
  32.7 23.8 %collective-permute-start.6 = (bf16[528,128]{1,0:T(8,128)(2,1)S(1)}, bf16[528,128]{1,0:T(8,128)(2,1)S(1)}, u32[]{:S(2)}, u32[]{:S(2)}) collective-permute-start(bf16[528,128]{1,0:T(8,128)(2,1)S(1)} %get-tuple-element.39), channel_id=1, source_target_pairs={{0,14},{1,15},{2,12},{3,13},{4,10},{5,11},{6,8},{7,9},{8,6},{9,7},... | collective-permute-start | bytes 405512 | tf_op jit(solution)/shard_map/ppermute | solution.py:777
  35.8 23.5 %collective-permute-start.7 = (bf16[528,128]{1,0:T(8,128)(2,1)S(1)}, bf16[528,128]{1,0:T(8,128)(2,1)S(1)}, u32[]{:S(2)}, u32[]{:S(2)}) collective-permute-start(bf16[528,128]{1,0:T(8,128)(2,1)S(1)} %get-tuple-element.40), channel_id=1, source_target_pairs={{0,15},{1,14},{2,13},{3,12},{4,11},{5,10},{6,9},{7,8},{8,7},{9,6},... | collective-permute-start | bytes 405512 | tf_op jit(solution)/shard_map/ppermute | solution.py:777
  59.4 16.1 %collective-permute-start.8 = (bf16[8,144,128]{2,1,0:T(8,128)(2,1)S(1)}, bf16[8,144,128]{2,1,0:T(8,128)(2,1)S(1)}, u32[]{:S(2)}, u32[]{:S(2)}) collective-permute-start(bf16[8,144,128]{2,1,0:T(8,128)(2,1)S(1)} %raw_states.1.refs_9_), channel_id=1, source_target_pairs={{0,8},{1,9},{2,10},{3,11},{4,12},{5,13},{6,14},{7,15},{8,0},{9,1},... | collective-permute-start | bytes 884744 | tf_op jit(solution)/shard_map/ppermute | solution.py:777
  61.9 13.6 %all-to-all-start.1 = ((f32[16,8,128]{2,1,0:T(8,128)}), f32[16,8,128]{2,1,0:T(8,128)S(1)}, u32[]{:S(2)}, u32[]{:S(2)}) async-start(f32[16,8,128]{2,1,0:T(8,128)} %gram_pieces.1), calls=%async_computation.1 | async-start | bytes 131072 | tf_op jit(solution)/shard_map/all_to_all | solution.py:365
  80.7 5.0 %copy-start.7 = (bf16[384,128]{1,0:T(8,128)(2,1)S(1)}, bf16[384,128]{1,0:T(8,128)(2,1)}, u32[]{:S(2)}) copy-start(bf16[384,128]{1,0:T(8,128)(2,1)} %get-tuple-element.51) | copy-start | bytes 294916
  80.7 6.0 %copy-start.6 = (bf16[384,128]{1,0:T(8,128)(2,1)S(1)}, bf16[384,128]{1,0:T(8,128)(2,1)}, u32[]{:S(2)}) copy-start(bf16[384,128]{1,0:T(8,128)(2,1)} %get-tuple-element.52) | copy-start | bytes 294916
  80.8 7.9 %copy-start.5 = (bf16[384,128]{1,0:T(8,128)(2,1)S(1)}, bf16[384,128]{1,0:T(8,128)(2,1)}, u32[]{:S(2)}) copy-start(bf16[384,128]{1,0:T(8,128)(2,1)} %get-tuple-element.53) | copy-start | bytes 294916
  80.8 9.8 %copy-start.4 = (bf16[384,128]{1,0:T(8,128)(2,1)S(1)}, bf16[384,128]{1,0:T(8,128)(2,1)}, u32[]{:S(2)}) copy-start(bf16[384,128]{1,0:T(8,128)(2,1)} %get-tuple-element.54) | copy-start | bytes 294916
  80.8 11.2 %copy-start.3 = (bf16[384,128]{1,0:T(8,128)(2,1)S(1)}, bf16[384,128]{1,0:T(8,128)(2,1)}, u32[]{:S(2)}) copy-start(bf16[384,128]{1,0:T(8,128)(2,1)} %get-tuple-element.55) | copy-start | bytes 294916
  80.8 23.1 %copy-start.2 = (bf16[384,128]{1,0:T(8,128)(2,1)S(1)}, bf16[384,128]{1,0:T(8,128)(2,1)}, u32[]{:S(2)}) copy-start(bf16[384,128]{1,0:T(8,128)(2,1)} %get-tuple-element.56) | copy-start | bytes 294916
  80.8 25.9 %copy-start.1 = (bf16[384,128]{1,0:T(8,128)(2,1)S(1)}, bf16[384,128]{1,0:T(8,128)(2,1)}, u32[]{:S(2)}) copy-start(bf16[384,128]{1,0:T(8,128)(2,1)} %get-tuple-element.57) | copy-start | bytes 294916
  80.8 28.2 %copy-start = (bf16[384,128]{1,0:T(8,128)(2,1)S(1)}, bf16[384,128]{1,0:T(8,128)(2,1)}, u32[]{:S(2)}) copy-start(bf16[384,128]{1,0:T(8,128)(2,1)} %get-tuple-element.58) | copy-start | bytes 294916
  80.8 29.6 %all-to-all-start.2 = ((bf16[8,640,128]{2,1,0:T(8,128)(2,1)}), bf16[8,640,128]{2,1,0:T(8,128)(2,1)S(1)}, u32[]{:S(2)}, u32[]{:S(2)}) async-start(bf16[8,640,128]{2,1,0:T(8,128)(2,1)} %get-tuple-element.50), calls=%async_computation.2 | async-start | bytes 2621440 | tf_op jit(solution)/shard_map/all_to_all | solution.py:782
  85.8 18.1 %collective-permute-start.9 = (bf16[384,128]{1,0:T(8,128)(2,1)S(1)}, bf16[384,128]{1,0:T(8,128)(2,1)S(1)}, u32[]{:S(2)}, u32[]{:S(2)}) collective-permute-start(bf16[384,128]{1,0:T(8,128)(2,1)S(1)} %copy-done.7), channel_id=1, source_target_pairs={{0,8},{1,9},{2,10},{3,11},{4,12},{5,13},{6,14},{7,15},{8,0},{9,1},... | collective-permute-start | bytes 294920 | tf_op jit(solution)/shard_map/ppermute | solution.py:777
  86.8 19.9 %collective-permute-start.10 = (bf16[384,128]{1,0:T(8,128)(2,1)S(1)}, bf16[384,128]{1,0:T(8,128)(2,1)S(1)}, u32[]{:S(2)}, u32[]{:S(2)}) collective-permute-start(bf16[384,128]{1,0:T(8,128)(2,1)S(1)} %copy-done.6), channel_id=1, source_target_pairs={{0,9},{1,8},{2,11},{3,10},{4,13},{5,12},{6,15},{7,14},{8,1},{9,0},... | collective-permute-start | bytes 294920 | tf_op jit(solution)/shard_map/ppermute | solution.py:777
  88.7 20.3 %collective-permute-start.11 = (bf16[384,128]{1,0:T(8,128)(2,1)S(1)}, bf16[384,128]{1,0:T(8,128)(2,1)S(1)}, u32[]{:S(2)}, u32[]{:S(2)}) collective-permute-start(bf16[384,128]{1,0:T(8,128)(2,1)S(1)} %copy-done.5), channel_id=1, source_target_pairs={{0,10},{1,11},{2,8},{3,9},{4,14},{5,15},{6,12},{7,13},{8,2},{9,3},... | collective-permute-start | bytes 294920 | tf_op jit(solution)/shard_map/ppermute | solution.py:777
  90.6 22.8 %collective-permute-start.12 = (bf16[384,128]{1,0:T(8,128)(2,1)S(1)}, bf16[384,128]{1,0:T(8,128)(2,1)S(1)}, u32[]{:S(2)}, u32[]{:S(2)}) collective-permute-start(bf16[384,128]{1,0:T(8,128)(2,1)S(1)} %copy-done.4), channel_id=1, source_target_pairs={{0,11},{1,10},{2,9},{3,8},{4,15},{5,14},{6,13},{7,12},{8,3},{9,2},... | collective-permute-start | bytes 294920 | tf_op jit(solution)/shard_map/ppermute | solution.py:777
  92.0 22.4 %collective-permute-start.13 = (bf16[384,128]{1,0:T(8,128)(2,1)S(1)}, bf16[384,128]{1,0:T(8,128)(2,1)S(1)}, u32[]{:S(2)}, u32[]{:S(2)}) collective-permute-start(bf16[384,128]{1,0:T(8,128)(2,1)S(1)} %copy-done.3), channel_id=1, source_target_pairs={{0,12},{1,13},{2,14},{3,15},{4,8},{5,9},{6,10},{7,11},{8,4},{9,5},... | collective-permute-start | bytes 294920 | tf_op jit(solution)/shard_map/ppermute | solution.py:777
  103.9 17.3 %collective-permute-start.14 = (bf16[384,128]{1,0:T(8,128)(2,1)S(1)}, bf16[384,128]{1,0:T(8,128)(2,1)S(1)}, u32[]{:S(2)}, u32[]{:S(2)}) collective-permute-start(bf16[384,128]{1,0:T(8,128)(2,1)S(1)} %copy-done.2), channel_id=1, source_target_pairs={{0,13},{1,12},{2,15},{3,14},{4,9},{5,8},{6,11},{7,10},{8,5},{9,4},... | collective-permute-start | bytes 294920 | tf_op jit(solution)/shard_map/ppermute | solution.py:777
  106.7 17.5 %collective-permute-start.15 = (bf16[384,128]{1,0:T(8,128)(2,1)S(1)}, bf16[384,128]{1,0:T(8,128)(2,1)S(1)}, u32[]{:S(2)}, u32[]{:S(2)}) collective-permute-start(bf16[384,128]{1,0:T(8,128)(2,1)S(1)} %copy-done.1), channel_id=1, source_target_pairs={{0,14},{1,15},{2,12},{3,13},{4,10},{5,11},{6,8},{7,9},{8,6},{9,7},... | collective-permute-start | bytes 294920 | tf_op jit(solution)/shard_map/ppermute | solution.py:777
  109.0 17.3 %collective-permute-start.16 = (bf16[384,128]{1,0:T(8,128)(2,1)S(1)}, bf16[384,128]{1,0:T(8,128)(2,1)S(1)}, u32[]{:S(2)}, u32[]{:S(2)}) collective-permute-start(bf16[384,128]{1,0:T(8,128)(2,1)S(1)} %copy-done), channel_id=1, source_target_pairs={{0,15},{1,14},{2,13},{3,12},{4,11},{5,10},{6,9},{7,8},{8,7},{9,6},... | collective-permute-start | bytes 294920 | tf_op jit(solution)/shard_map/ppermute | solution.py:777
